TPU v7x, 32 devices: a whole 2x2x4 slice. The times are simulated.
32 devices in a mesh: groups: 2 (over x), latent: 16 (over z, y, core).
Axes of the slice: x: 2, y: 2, z: 4, core: 2. Of those that a mesh axis runs over, the one named last changes fastest.
Arguments:
- x_rows: bfloat16 [32768, 3584], P(('groups', 'latent')), parts along dimension 0, may hold values from -6 to 6
- out_grad: bfloat16 [32768, 3584], P(('groups', 'latent')), parts along dimension 0, may hold values from -0.046875 to 0.046875
- enc_coef: bfloat16 [32768, 512], P(('groups', 'latent')), parts along dimension 0, may hold values from -0.0625 to 0.0625
- latent_act: bfloat16 [32768, 512], P(('groups', 'latent')), parts along dimension 0, may hold values from 0 to 1
- enc_w: float32 [1024, 3584], P(('groups', 'latent')), parts along dimension 0, may hold values from -0.036 to 0.036
- enc_m: float32 [1024, 3584], P(('groups', 'latent')), parts along dimension 0, may hold values from -0.18 to 0.18
- enc_v: float32 [1024, 3584], P(('groups', 'latent')), parts along dimension 0, may hold values from 0.0005 to 0.05
- dec_w: float32 [1024, 3584], P(('groups', 'latent')), parts along dimension 0, may hold values from -0.036 to 0.036
- dec_m: float32 [1024, 3584], P(('groups', 'latent')), parts along dimension 0, may hold values from -0.18 to 0.18
- dec_v: float32 [1024, 3584], P(('groups', 'latent')), parts along dimension 0, may hold values from 0.0005 to 0.05
- dead_order: int32 [32, 32], P(('groups', 'latent')), parts along dimension 0, may hold values from 0 to 31, each once within a row
- pick_rows: int32 [32, 16, 2], P(('groups', 'latent')), parts along dimension 0, may hold values from 0 to 1023
- send_count: int32 [32, 16], P(('groups', 'latent')), parts along dimension 0, may hold values from 0 to 2, as said below
Outputs:
- enc_w_out: float32 [1024, 3584], P(('groups', 'latent')), parts along dimension 0
- enc_m_out: float32 [1024, 3584], P(('groups', 'latent')), parts along dimension 0
- enc_v_out: float32 [1024, 3584], P(('groups', 'latent')), parts along dimension 0
- dec_w_out: float32 [1024, 3584], P(('groups', 'latent')), parts along dimension 0
- dec_m_out: float32 [1024, 3584], P(('groups', 'latent')), parts along dimension 0
- dec_v_out: float32 [1024, 3584], P(('groups', 'latent')), parts along dimension 0
- enc_full: bfloat16 [1024, 3584], P('groups'), parts along dimension 0
- dec_full: bfloat16 [1024, 3584], P('groups'), parts along dimension 0
There are 2 independent parts, one for each index of `groups`. A program takes and returns all parts, laid end to end along the dimension named above; each array names one. Nothing has to cross between parts.
Inputs may be any that keep to these rules, and one draw needn't show every extreme that they name: `send_count`: column d counts the rows that owner d receives; each column sums to at most 32, and some column reaches 32 in every draw.
All inputs are finite; a program needn't handle non-finite values.
Results may differ from a plain program's by a relative error of at most 0.015.
Values may be sent and summed in bfloat16 or wider, within the bound.
No kernel may reach another device: no remote copies, remote signals or barrier semaphores. Data moves between devices by JAX's collectives and lax.ppermute only.
A program may use at most 128 MiB of HBM per device.

v0:
```python
import jax
import jax.numpy as jnp
from jax import lax
from jax.sharding import PartitionSpec as P

beta_one = 0.9
beta_two = 0.99
first_fix = 1.0 - 0.9**4
second_fix = 1.0 - 0.99**4
learn_rate = 0.02
adam_eps = 1e-08
reset_gain = 0.01
norm_eps = 1e-06


def adam_update(weight, moment, second, gradient):
    moment_new = beta_one * moment + (1.0 - beta_one) * gradient
    second_new = beta_two * second + (1.0 - beta_two) * gradient * gradient
    weight_new = weight - learn_rate * (moment_new / first_fix) / (
        jnp.sqrt(second_new / second_fix) + adam_eps
    )
    return (weight_new, moment_new, second_new)


def reset_shard(arrived, arrived_counts, dead_list, states):
    enc_weight, enc_moment, enc_second, dec_weight, dec_moment, dec_second = states
    sources = arrived_counts.shape[0]
    per_source = arrived.shape[0] // sources
    latents = enc_weight.shape[0]
    offsets = jnp.cumsum(arrived_counts) - arrived_counts
    within = jnp.tile(jnp.arange(per_source), sources)
    slot_rank = jnp.repeat(offsets, per_source) + within
    slot_live = within < jnp.repeat(arrived_counts, per_source)
    dead_total = jnp.sum(arrived_counts)
    positions = jnp.arange(latents)
    in_use = positions < dead_total
    chooser = (
        (slot_rank[None, :] == positions[:, None]) & slot_live[None, :] & in_use[:, None]
    ).astype(jnp.float32)
    fresh_rows = jnp.dot(chooser, arrived.astype(jnp.float32), precision=lax.Precision.HIGHEST)
    placing = ((dead_list[:, None] == positions[None, :]) & in_use[:, None]).astype(jnp.float32)
    is_reset = (jnp.sum(placing, axis=0) > 0.5)[:, None]
    placed = jnp.dot(placing.T, fresh_rows, precision=lax.Precision.HIGHEST)
    enc_fresh = (
        reset_gain * placed * lax.rsqrt(jnp.mean(placed * placed, axis=1, keepdims=True) + norm_eps)
    )
    enc_weight = jnp.where(is_reset, enc_fresh, enc_weight)
    enc_moment = jnp.where(is_reset, 0.0, enc_moment)
    enc_second = jnp.where(is_reset, 0.0, enc_second)
    dec_weight = jnp.where(is_reset, placed, dec_weight)
    dec_moment = jnp.where(is_reset, 0.0, dec_moment)
    dec_second = jnp.where(is_reset, 0.0, dec_second)
    dec_weight = dec_weight * lax.rsqrt(
        jnp.mean(dec_weight * dec_weight, axis=1, keepdims=True) + norm_eps
    )
    return (enc_weight, enc_moment, enc_second, dec_weight, dec_moment, dec_second)


def shards(
    x_rows,
    out_grad,
    enc_coef,
    latent_act,
    enc_w,
    enc_m,
    enc_v,
    dec_w,
    dec_m,
    dec_v,
    dead_order,
    pick_rows,
    send_count,
):
    width = x_rows.shape[1]
    contraction = (((0,), (0,)), ((), ()))
    enc_grad = lax.psum_scatter(
        lax.dot_general(enc_coef, x_rows, contraction, preferred_element_type=jnp.float32).astype(
            jnp.bfloat16
        ),
        "latent",
        scatter_dimension=0,
        tiled=True,
    ).astype(jnp.float32)
    dec_grad = lax.psum_scatter(
        lax.dot_general(
            latent_act, out_grad, contraction, preferred_element_type=jnp.float32
        ).astype(jnp.bfloat16),
        "latent",
        scatter_dimension=0,
        tiled=True,
    ).astype(jnp.float32)
    enc_new = adam_update(enc_w, enc_m, enc_v, enc_grad)
    dec_new = adam_update(dec_w, dec_m, dec_v, dec_grad)
    chosen = x_rows[pick_rows[0]]
    arrived = lax.all_to_all(chosen, "latent", split_axis=0, concat_axis=0, tiled=True)
    arrived_counts = lax.all_to_all(
        send_count[0], "latent", split_axis=0, concat_axis=0, tiled=True
    )
    results = reset_shard(
        arrived.reshape(-1, width), arrived_counts, dead_order[0], enc_new + dec_new
    )
    enc_out, enc_mo, enc_vo, dec_out, dec_mo, dec_vo = results
    enc_full, dec_full = (
        lax.all_gather(enc_out.astype(jnp.bfloat16), "latent", axis=0, tiled=True),
        lax.all_gather(dec_out.astype(jnp.bfloat16), "latent", axis=0, tiled=True),
    )
    return (enc_out, enc_mo, enc_vo, dec_out, dec_mo, dec_vo, enc_full, dec_full)


def solution(mesh):
    placed = (
        P(("groups", "latent"), None),
        P(("groups", "latent"), None),
        P(("groups", "latent"), None),
        P(("groups", "latent"), None),
        P(("groups", "latent"), None),
        P(("groups", "latent"), None),
        P(("groups", "latent"), None),
        P(("groups", "latent"), None),
        P(("groups", "latent"), None),
        P(("groups", "latent"), None),
        P(("groups", "latent"), None),
        P(("groups", "latent"), None, None),
        P(("groups", "latent"), None),
    )
    return jax.shard_map(
        shards,
        mesh=mesh,
        in_specs=placed,
        out_specs=(
            P(("groups", "latent"), None),
            P(("groups", "latent"), None),
            P(("groups", "latent"), None),
            P(("groups", "latent"), None),
            P(("groups", "latent"), None),
            P(("groups", "latent"), None),
            P("groups", None),
            P("groups", None),
        ),
        check_vma=False,
    )
```

profile of v0, /device:TPU:0, one launch (start us, length us, event | category | flops | bytes accessed | tf_op | source)
XLA Modules:
  0.0 274.5 jit_solution(11499733368809448646)
XLA Ops:
  7.2 1.2 copy-done
  8.4 8.5 %convolution_convert_fusion = bf16[512,3584]{1,0:T(8,128)(2,1)} fusion(bf16[1024,512]{1,0:T(8,128)(2,1)S(1)} %copy-done, bf16[1024,3584]{1,0:T(8,128)(2,1)} %param.14), kind=kOutput, calls=%fused_computation.1 | convolution fusion | flops 3759931392 | bytes 12058624 | tf_op jit(solution)/shard_map/dot_general | solution.py:85
  17.1 8.5 %convolution_convert_fusion.1 = bf16[512,3584]{1,0:T(8,128)(2,1)} fusion(bf16[1024,512]{1,0:T(8,128)(2,1)S(1)} %copy-done.8, bf16[1024,3584]{1,0:T(8,128)(2,1)} %param.13), kind=kOutput, calls=%fused_computation.2 | convolution fusion | flops 3759931392 | bytes 12058624 | tf_op jit(solution)/shard_map/dot_general | solution.py:77
  25.6 0.7 copy.31
  26.3 7.4 %all-to-all-start = ((s32[16,1,1]{2,1,0:T(1,128)}), s32[16,1,1]{2,1,0:T(1,128)S(1)}, u32[]{:S(2)}, u32[]{:S(2)}) async-start(s32[16,1,1]{2,1,0:T(1,128)} %copy.31), calls=%async_computation | async-start | bytes 16384 | tf_op jit(solution)/shard_map/all_to_all | solution.py:96
  33.7 0.1 copy.33
  33.8 0.1 reshape.128
  33.9 5.2 %gather_fusion = bf16[32,3584]{1,0:T(8,128)(2,1)S(1)} fusion(bf16[1024,3584]{1,0:T(8,128)(2,1)} %param.13, s32[1024]{0:T(1024)S(1)} %pad_clamp_fusion), kind=kCustom, calls=%fused_computation | custom fusion | bytes 458880 | tf_op jit(solution)/shard_map/gather | solution.py:94
  39.2 0.8 reshape.127
  40.0 0.1 all-to-all-done
  40.1 5.9 %all-to-all-start.1 = ((bf16[16,2,3584]{2,1,0:T(2,128)(2,1)}), bf16[16,2,3584]{2,1,0:T(2,128)(2,1)S(1)}, u32[]{:S(2)}, u32[]{:S(2)}) async-start(bf16[16,2,3584]{2,1,0:T(2,128)(2,1)} %reshape.127), calls=%async_computation.1 | async-start | bytes 458752 | tf_op jit(solution)/shard_map/all_to_all | solution.py:95
  46.0 0.0 all-gather.3.cloned.1.call-start
  46.0 0.9 fusion.20
  47.0 0.1 iota_compare_fusion.2
  47.0 0.1 lt.36
  47.2 0.1 reduce.1
  47.3 0.1 iota_add_fusion
  47.4 0.1 add.62
  47.5 0.7 iota_compare_fusion.3
  48.1 0.1 convert_reduce_fusion
  48.2 10.1 %all-to-all-done.1 = bf16[16,2,3584]{2,1,0:T(2,128)(2,1)S(1)} async-done(((bf16[16,2,3584]{2,1,0:T(2,128)(2,1)}), bf16[16,2,3584]{2,1,0:T(2,128)(2,1)S(1)}, u32[]{:S(2)}, u32[]{:S(2)}) %all-to-all-start.1) | async-done | bytes 229408 | tf_op jit(solution)/shard_map/all_to_all | solution.py:95
  58.4 0.1 reshape.125
  58.5 0.3 fusion.13
  58.7 0.6 multiply_reduce_fusion.1
  59.3 30.9 %reduce-scatter.5.cloned.1.call-done = bf16[32,3584]{1,0:T(8,128)(2,1)} async-done(((bf16[512,3584]{1,0:T(8,128)(2,1)}), bf16[32,3584]{1,0:T(8,128)(2,1)}) %reduce-scatter.5.cloned.1.call-update) | async-done | bytes 229392 | tf_op jit(solution)/shard_map/reduce_scatter | solution.py:84
  90.2 72.4 %reduce-scatter.3.cloned.1.call-done = bf16[32,3584]{1,0:T(8,128)(2,1)} async-done(((bf16[512,3584]{1,0:T(8,128)(2,1)}), bf16[32,3584]{1,0:T(8,128)(2,1)}) %reduce-scatter.3.cloned.1.call-update) | async-done | bytes 229392 | tf_op jit(solution)/shard_map/reduce_scatter | solution.py:76
  162.6 3.5 %fusion.22 = (bf16[32,3584]{1,0:T(8,128)(2,1)}, f32[32,3584]{1,0:T(8,128)}, f32[32,3584]{1,0:T(8,128)}, f32[32,3584]{1,0:T(8,128)}, f32[32,3584]{1,0:T(8,128)}, ...) fusion(f32[32,3584]{1,0:T(8,128)S(1)} %copy-done.2, f32[32,3584]{1,0:T(8,128)S(1)} %copy-done.3, ...), kind=kLoop, calls=%fused_computation.43 | loop fusion | flops 4128736 | bytes 6652192 | tf_op jit(solution)/shard_map/convert_element_type | solution.py:104
  166.2 1.0 fusion.21
  167.2 45.4 %all-gather.3.cloned.1.call-done = bf16[512,3584]{1,0:T(8,128)(2,1)} async-done(((bf16[32,3584]{1,0:T(8,128)(2,1)}), bf16[512,3584]{1,0:T(8,128)(2,1)}) %all-gather.3.cloned.1.call-update) | async-done | bytes 3670032 | tf_op jit(solution)/shard_map/all_gather | solution.py:104
  212.5 49.3 %all-gather.5.cloned.1.call-done = bf16[512,3584]{1,0:T(8,128)(2,1)} async-done(((bf16[32,3584]{1,0:T(8,128)(2,1)}), bf16[512,3584]{1,0:T(8,128)(2,1)}) %all-gather.5.cloned.1.call-update) | async-done | bytes 3670032 | tf_op jit(solution)/shard_map/all_gather | solution.py:105
  261.8 4.3 %copy.36 = bf16[512,3584]{1,0:T(8,128)(2,1)} copy(bf16[512,3584]{1,0:T(8,128)(2,1)} %all-gather.3.cloned.1.call-done) | data formatting | bytes 7340032
  266.1 1.8 copy.37
  (31 shorter events, 0.3 us)
Async XLA Ops:
  7.2 1.2 copy-start
  7.2 9.9 %copy-start.8 = (bf16[1024,512]{1,0:T(8,128)(2,1)S(1)}, bf16[1024,512]{1,0:T(8,128)(2,1)}, u32[]{:S(2)}) copy-start(bf16[1024,512]{1,0:T(8,128)(2,1)} %param.15) | copy-start | bytes 3145732
  7.2 83.0 %reduce-scatter.5.cloned.1.call-start = ((), (), s32[]{:S(2)}) async-start(), calls=%async_computation.5 | async-start | bytes 3899392 | tf_op jit(solution)/shard_map/reduce_scatter | solution.py:84
  17.0 8.7 %copy-start.7 = (s32[1,16]{1,0:T(1,128)S(1)}, s32[1,16]{1,0:T(1,128)}, u32[]{:S(2)}) copy-start(s32[1,16]{1,0:T(1,128)} %param.25) | copy-start | bytes 196
  17.0 16.7 %copy-start.5 = (s32[1,16,2]{1,2,0:T(2,128)S(1)}, s32[1,16,2]{1,2,0:T(2,128)}, u32[]{:S(2)}) copy-start(s32[1,16,2]{1,2,0:T(2,128)} %param.24) | copy-start | bytes 388
  17.0 31.1 %copy-start.6 = (s32[1,32]{1,0:T(1,128)S(1)}, s32[1,32]{1,0:T(1,128)}, u32[]{:S(2)}) copy-start(s32[1,32]{1,0:T(1,128)} %param.23) | copy-start | bytes 388
  17.0 145.6 %reduce-scatter.3.cloned.1.call-start = ((), (), s32[]{:S(2)}) async-start(), calls=%async_computation.4 | async-start | bytes 3899392 | tf_op jit(solution)/shard_map/reduce_scatter | solution.py:76
  25.6 137.0 %copy-start.2 = (f32[32,3584]{1,0:T(8,128)S(1)}, f32[32,3584]{1,0:T(8,128)}, u32[]{:S(2)}) copy-start(f32[32,3584]{1,0:T(8,128)} %param.17) | copy-start | bytes 1376260
  25.6 137.0 %copy-start.3 = (f32[32,3584]{1,0:T(8,128)S(1)}, f32[32,3584]{1,0:T(8,128)}, u32[]{:S(2)}) copy-start(f32[32,3584]{1,0:T(8,128)} %param.19) | copy-start | bytes 1376260
  25.6 137.0 %copy-start.4 = (f32[32,3584]{1,0:T(8,128)S(1)}, f32[32,3584]{1,0:T(8,128)}, u32[]{:S(2)}) copy-start(f32[32,3584]{1,0:T(8,128)} %param.18) | copy-start | bytes 1376260
  26.3 13.7 %all-to-all-start = ((s32[16,1,1]{2,1,0:T(1,128)}), s32[16,1,1]{2,1,0:T(1,128)S(1)}, u32[]{:S(2)}, u32[]{:S(2)}) async-start(s32[16,1,1]{2,1,0:T(1,128)} %copy.31), calls=%async_computation | async-start | bytes 16384 | tf_op jit(solution)/shard_map/all_to_all | solution.py:96
  40.1 18.3 %all-to-all-start.1 = ((bf16[16,2,3584]{2,1,0:T(2,128)(2,1)}), bf16[16,2,3584]{2,1,0:T(2,128)(2,1)S(1)}, u32[]{:S(2)}, u32[]{:S(2)}) async-start(bf16[16,2,3584]{2,1,0:T(2,128)(2,1)} %reshape.127), calls=%async_computation.1 | async-start | bytes 458752 | tf_op jit(solution)/shard_map/all_to_all | solution.py:95
  46.0 166.5 %all-gather.3.cloned.1.call-start = ((), (), s32[]{:S(2)}) async-start(), calls=%async_computation.6 | async-start | bytes 3899392 | tf_op jit(solution)/shard_map/all_gather | solution.py:104
  166.1 95.7 %all-gather.5.cloned.1.call-start = ((), (), s32[]{:S(2)}) async-start(), calls=%async_computation.7 | async-start | bytes 3899392 | tf_op jit(solution)/shard_map/all_gather | solution.py:105
  261.8 4.3 %copy-start.1 = (bf16[512,3584]{1,0:T(8,128)(2,1)S(1)}, bf16[512,3584]{1,0:T(8,128)(2,1)}, u32[]{:S(2)}) copy-start(bf16[512,3584]{1,0:T(8,128)(2,1)} %all-gather.5.cloned.1.call-done) | copy-start | bytes 11010052
Sparse Core Ops, SparseCore 0:
  17.1 73.0 reduce-scatter.4
  95.1 67.4 reduce-scatter.2
  166.2 46.2 all-gather.2
  215.2 46.5 all-gather.4
where the time goes:
time: 275 us; the launch traced here: 274 us
  waiting for transfers between devices  208 us (76%)
  matrix products  17.9 us (7%)
  local copies, waits for them, and re-layouts  14.4 us (5%)
  between operations  13.9 us (5%)
  starting transfers between devices  13.5 us (5%)
  other arithmetic  6.48 us (2%)
    reduce_scatter x1, waiting for transfers between devices, shards(): lax.psum_scatter(lax.dot_general(enc_coef, x_rows, contraction, preferred...  72.4 us
    all_gather x1, waiting for transfers between devices, shards(): lax.all_gather(dec_out.astype(jnp.bfloat16), 'latent', axis=0, tiled=True)  49.3 us
    all_gather x1, waiting for transfers between devices, shards(): lax.all_gather(enc_out.astype(jnp.bfloat16), 'latent', axis=0, tiled=True)  45.4 us
    reduce_scatter x1, waiting for transfers between devices, shards(): lax.psum_scatter(lax.dot_general(latent_act, out_grad, contraction, prefe...  30.9 us
    all_to_all x1, waiting for transfers between devices, shards(): lax.all_to_all(chosen, 'latent', split_axis=0, concat_axis=0, tiled=True)  10.1 us
    dot_general x1, matrix products, shards(): lax.dot_general(latent_act, out_grad, contraction, preferred_element_type...  8.54 us
    dot_general x1, matrix products, shards(): lax.dot_general(enc_coef, x_rows, contraction, preferred_element_type=jnp...  8.54 us
    all_to_all x1, starting transfers between devices, shards(): lax.all_to_all(send_count[0], 'latent', split_axis=0, concat_axis=0, tile...  7.39 us
  transfers between devices with their start and end apart: 6, of which 6 were waited for; matrix products, arithmetic and copies ran while one was open for 7% of the time, Pallas kernels for 0%

commit v1 on v0

--- a/solution.py
+++ b/solution.py
@@ -1,6 +1,10 @@
+import functools
+
 import jax
 import jax.numpy as jnp
 from jax import lax
+from jax.experimental import pallas as pl
+from jax.experimental.pallas import tpu as pltpu
 from jax.sharding import PartitionSpec as P
 
 beta_one = 0.9
@@ -56,6 +60,84 @@
     return (enc_weight, enc_moment, enc_second, dec_weight, dec_moment, dec_second)
 
 
+def swap(value, bits, size):
+    return lax.ppermute(value, "latent", [(i, i ^ bits) for i in range(size)])
+
+
+def relative_rows(coef, owners, rows):
+    latents = coef.shape[1]
+    wanted = (owners[:, None] * rows + jnp.arange(rows)[None, :]).reshape(-1)
+    pick = (wanted[:, None] == jnp.arange(latents)[None, :]).astype(coef.dtype)
+    return lax.dot_general(
+        pick, coef, (((1,), (1,)), ((), ())), preferred_element_type=jnp.float32
+    ).astype(coef.dtype)
+
+
+def owned_gradient(left, right, rows, size):
+    depth = size // 4
+    half, quarter = depth * 2 * rows, depth * rows
+
+    def part(begin, count):
+        return jnp.dot(
+            left[begin : begin + count], right, preferred_element_type=jnp.float32
+        )
+
+    from_core = swap(part(0, half).astype(jnp.bfloat16), 1, size)
+    to_y = part(half, quarter) + from_core[:quarter].astype(jnp.float32)
+    from_y = swap(to_y.astype(jnp.bfloat16), 2, size)
+    mine = (
+        part(half + quarter, quarter)
+        + from_core[quarter:].astype(jnp.float32)
+    ).astype(jnp.bfloat16)
+    total = mine.astype(jnp.float32) + from_y.astype(jnp.float32)
+    sent = total.astype(jnp.bfloat16)
+    gradient = total[:rows]
+    for k in range(1, depth):
+        gradient = gradient + swap(sent[k * rows : (k + 1) * rows], 4 * k, size).astype(
+            jnp.float32
+        )
+    return gradient
+
+
+def place_kernel(plan, rows, *refs):
+    pieces, whole, sems = refs[: len(plan)], refs[len(plan)], refs[len(plan) + 1]
+    me = lax.axis_index("latent")
+    copies = []
+    for piece, keys in zip(pieces, plan):
+        for i, key in enumerate(keys):
+            start = pl.multiple_of((me ^ key) * rows, rows)
+            copies.append(
+                pltpu.make_async_copy(
+                    piece.at[pl.ds(i * rows, rows)],
+                    whole.at[pl.ds(start, rows)],
+                    sems.at[len(copies)],
+                )
+            )
+    for copy in copies:
+        copy.start()
+    for copy in copies:
+        copy.wait()
+
+
+def gathered(block, size):
+    rows, width = block.shape
+    depth = size // 4
+    z_keys = [4 * k for k in range(1, depth)]
+    near = jnp.concatenate([swap(block, key, size) for key in z_keys], axis=0)
+    pieces = [(block, [0]), (near, z_keys)]
+    pieces += [(swap(value, 2, size), [key ^ 2 for key in keys]) for value, keys in pieces]
+    pieces += [(swap(value, 1, size), [key ^ 1 for key in keys]) for value, keys in pieces]
+    plan = [keys for _, keys in pieces]
+    return pl.pallas_call(
+        functools.partial(place_kernel, plan, rows),
+        out_shape=jax.ShapeDtypeStruct((size * rows, width), block.dtype),
+        in_specs=[pl.BlockSpec(memory_space=pl.ANY)] * len(pieces),
+        out_specs=pl.BlockSpec(memory_space=pl.ANY),
+        scratch_shapes=[pltpu.SemaphoreType.DMA((size,))],
+        name="place",
+    )(*[value for value, _ in pieces])
+
+
 def shards(
     x_rows,
     out_grad,
@@ -72,23 +154,17 @@
     send_count,
 ):
     width = x_rows.shape[1]
-    contraction = (((0,), (0,)), ((), ()))
-    enc_grad = lax.psum_scatter(
-        lax.dot_general(enc_coef, x_rows, contraction, preferred_element_type=jnp.float32).astype(
-            jnp.bfloat16
-        ),
-        "latent",
-        scatter_dimension=0,
-        tiled=True,
-    ).astype(jnp.float32)
-    dec_grad = lax.psum_scatter(
-        lax.dot_general(
-            latent_act, out_grad, contraction, preferred_element_type=jnp.float32
-        ).astype(jnp.bfloat16),
-        "latent",
-        scatter_dimension=0,
-        tiled=True,
-    ).astype(jnp.float32)
+    rows = enc_w.shape[0]
+    size = lax.axis_size("latent")
+    depth = size // 4
+    me = lax.axis_index("latent")
+    keys = jnp.array(
+        [4 * kz + 2 * ky + kc for kc in (1, 0) for ky in (1, 0) for kz in range(depth)],
+        jnp.int32,
+    )
+    owners = me ^ keys
+    enc_grad = owned_gradient(relative_rows(enc_coef, owners, rows), x_rows, rows, size)
+    dec_grad = owned_gradient(relative_rows(latent_act, owners, rows), out_grad, rows, size)
     enc_new = adam_update(enc_w, enc_m, enc_v, enc_grad)
     dec_new = adam_update(dec_w, dec_m, dec_v, dec_grad)
     chosen = x_rows[pick_rows[0]]
@@ -100,42 +176,18 @@
         arrived.reshape(-1, width), arrived_counts, dead_order[0], enc_new + dec_new
     )
     enc_out, enc_mo, enc_vo, dec_out, dec_mo, dec_vo = results
-    enc_full, dec_full = (
-        lax.all_gather(enc_out.astype(jnp.bfloat16), "latent", axis=0, tiled=True),
-        lax.all_gather(dec_out.astype(jnp.bfloat16), "latent", axis=0, tiled=True),
-    )
+    enc_full = gathered(enc_out.astype(jnp.bfloat16), size)
+    dec_full = gathered(dec_out.astype(jnp.bfloat16), size)
     return (enc_out, enc_mo, enc_vo, dec_out, dec_mo, dec_vo, enc_full, dec_full)
 
 
 def solution(mesh):
-    placed = (
-        P(("groups", "latent"), None),
-        P(("groups", "latent"), None),
-        P(("groups", "latent"), None),
-        P(("groups", "latent"), None),
-        P(("groups", "latent"), None),
-        P(("groups", "latent"), None),
-        P(("groups", "latent"), None),
-        P(("groups", "latent"), None),
-        P(("groups", "latent"), None),
-        P(("groups", "latent"), None),
-        P(("groups", "latent"), None),
-        P(("groups", "latent"), None, None),
-        P(("groups", "latent"), None),
-    )
+    split = P(("groups", "latent"), None)
+    placed = (split,) * 11 + (P(("groups", "latent"), None, None), split)
     return jax.shard_map(
         shards,
         mesh=mesh,
         in_specs=placed,
-        out_specs=(
-            P(("groups", "latent"), None),
-            P(("groups", "latent"), None),
-            P(("groups", "latent"), None),
-            P(("groups", "latent"), None),
-            P(("groups", "latent"), None),
-            P(("groups", "latent"), None),
-            P("groups", None),
-            P("groups", None),
-        ),
+        out_specs=(split,) * 6 + (P("groups", None),) * 2,
         check_vma=False,
     )

time: 275 us -> 432 us (1.57)
  Pallas kernels: 0 us -> 225 us
  waiting for transfers between devices: 208 us -> 126 us
  starting transfers between devices: 13.5 us -> 33.6 us
  between operations: 13.9 us -> 1.34 us
  matrix products: 17.9 us -> 27 us
  local copies, waits for them, and re-layouts: 14.4 us -> 8.03 us
    pallas_call x0 -> x2, Pallas kernels: none -> 225 us  [gathered(): pl.pallas_call(functools.partial(place_kernel, plan, rows), out_shape=jax...]
    ppermute x0 -> x28, waiting for transfers between devices: none -> 119 us  [swap(): return lax.ppermute(value, 'latent', [(i, i ^ bits) for i in range(size)])]
    reduce_scatter x2 -> x0, waiting for transfers between devices: 103 us -> none  [the longest x1 72.4 us: shards(): lax.psum_scatter(lax.dot_general(enc_coef, x_rows, contraction, preferred...]
    all_gather x2 -> x0, waiting for transfers between devices: 94.7 us -> none  [the longest x1 49.3 us: shards(): lax.all_gather(dec_out.astype(jnp.bfloat16), 'latent', axis=0, tiled=True)]
    ppermute x0 -> x28, starting transfers between devices: none -> 20.2 us  [swap(): return lax.ppermute(value, 'latent', [(i, i ^ bits) for i in range(size)])]
    dot_general x2 -> x8, matrix products: 17.1 us -> 26.1 us  [the longest x6 24.6 us: part(): jnp.dot(left[begin:begin + count], right, preferred_element_type=jnp.floa...]
    unnamed x20 -> x56, local copies, waits for them, and re-layouts: 7.3 us -> 0.24 us
  transfers between devices with their start and end apart: 6 -> 30, of which waited for: 6 -> 13; matrix products, arithmetic and copies ran while one was open for 7% -> 10% of each run, Pallas kernels for 0% -> 26%
where the time goes in v1:
time: 432 us; the launch traced here: 431 us
  Pallas kernels  225 us (52%)
  waiting for transfers between devices  126 us (29%)
  starting transfers between devices  33.6 us (8%)
  matrix products  27 us (6%)
  other arithmetic  10.5 us (2%)
  local copies, waits for them, and re-layouts  8.03 us (2%)
    pallas_call x2, Pallas kernels, gathered(): pl.pallas_call(functools.partial(place_kernel, plan, rows), out_shape=jax...  225 us
    ppermute x28, waiting for transfers between devices, swap(): return lax.ppermute(value, 'latent', [(i, i ^ bits) for i in range(size)])  119 us
    dot_general x6, matrix products, part(): jnp.dot(left[begin:begin + count], right, preferred_element_type=jnp.floa...  24.6 us
    ppermute x28, starting transfers between devices, swap(): return lax.ppermute(value, 'latent', [(i, i ^ bits) for i in range(size)])  20.2 us
  transfers between devices with their start and end apart: 30, of which 13 were waited for; matrix products, arithmetic and copies ran while one was open for 10% of the time, Pallas kernels for 26%

profile of v1, /device:TPU:0, one launch (start us, length us, event | category | flops | bytes accessed | tf_op | source)
XLA Modules:
  0.0 431.2 jit_solution(15865579404255899678)
XLA Ops:
  0.6 1.4 copy.32
  2.1 7.4 %all-to-all-start = ((s32[16,1,1]{2,1,0:T(1,128)}), s32[16,1,1]{2,1,0:T(1,128)S(1)}, u32[]{:S(2)}, u32[]{:S(2)}) async-start(s32[16,1,1]{2,1,0:T(1,128)} %copy.32), calls=%async_computation | async-start | bytes 16384 | tf_op jit(solution)/shard_map/all_to_all | solution.py:172
  11.1 7.4 %convolution_convert_fusion = bf16[256,3584]{1,0:T(8,128)(2,1)} fusion(bf16[1024,3584]{1,0:T(8,128)(2,1)} %param.15, bf16[512,1024]{1,0:T(8,128)(2,1)S(1)} %convolution_convert_fusion.2), kind=kOutput, calls=%fused_computation.1 | convolution fusion | flops 1879965696 | bytes 9699328 | tf_op jit(solution)/shard_map/dot_general | solution.py:81
  19.7 3.3 convolution_convert_fusion.1
  24.5 5.5 %fusion.14 = f32[128,3584]{1,0:T(8,128)} fusion(bf16[1024,3584]{1,0:T(8,128)(2,1)} %param.15, bf16[512,1024]{1,0:T(8,128)(2,1)} %copy-done.10), kind=kOutput, calls=%fused_computation.34 | convolution fusion | flops 939524096 | bytes 9437184 | tf_op jit(solution)/shard_map/dot_general | solution.py:81
  30.0 4.9 %gather_fusion = bf16[32,3584]{1,0:T(8,128)(2,1)S(1)} fusion(bf16[1024,3584]{1,0:T(8,128)(2,1)} %param.14, s32[1024]{0:T(1024)S(1)} %pad_clamp_fusion), kind=kCustom, calls=%fused_computation | custom fusion | bytes 458880 | tf_op jit(solution)/shard_map/gather | solution.py:170
  35.8 6.0 %all-to-all-start.1 = ((bf16[16,2,3584]{2,1,0:T(2,128)(2,1)}), bf16[16,2,3584]{2,1,0:T(2,128)(2,1)S(1)}, u32[]{:S(2)}, u32[]{:S(2)}) async-start(bf16[16,2,3584]{2,1,0:T(2,128)(2,1)} %reshape.143), calls=%async_computation.1 | async-start | bytes 458752 | tf_op jit(solution)/shard_map/all_to_all | solution.py:171
  44.0 7.3 %all-to-all-done.1 = bf16[16,2,3584]{2,1,0:T(2,128)(2,1)S(1)} async-done(((bf16[16,2,3584]{2,1,0:T(2,128)(2,1)}), bf16[16,2,3584]{2,1,0:T(2,128)(2,1)S(1)}, u32[]{:S(2)}, u32[]{:S(2)}) %all-to-all-start.1) | async-done | bytes 229408 | tf_op jit(solution)/shard_map/all_to_all | solution.py:171
  51.7 4.6 %add_convert_fusion = bf16[128,3584]{1,0:T(8,128)(2,1)S(1)} fusion(bf16[256,3584]{1,0:T(8,128)(2,1)} %collective-permute-done.5, bf16[1024,3584]{1,0:T(8,128)(2,1)} %param.15, bf16[512,1024]{1,0:T(8,128)(2,1)} %copy-done.10), kind=kOutput, calls=%fused_computation.4 | convolution fusion | flops 940900352 | bytes 9437184 | tf_op jit(solution)/shard_map/dot_general | solution.py:81
  57.1 2.6 add_convert_fusion.2
  59.6 2.1 collective-permute-start.1
  61.7 17.9 %collective-permute-done.6 = bf16[128,3584]{1,0:T(8,128)(2,1)S(1)} collective-permute-done((bf16[128,3584]{1,0:T(8,128)(2,1)S(1)}, bf16[128,3584]{1,0:T(8,128)(2,1)S(1)}, u32[]{:S(2)}, u32[]{:S(2)}) %collective-permute-start.6) | collective-permute-done | bytes 917536 | tf_op jit(solution)/shard_map/ppermute | solution.py:64
  79.7 1.5 fusion.39
  81.3 2.4 collective-permute-start.9
  84.8 13.4 %collective-permute-done.1 = bf16[128,3584]{1,0:T(8,128)(2,1)S(1)} collective-permute-done((bf16[128,3584]{1,0:T(8,128)(2,1)S(1)}, bf16[128,3584]{1,0:T(8,128)(2,1)S(1)}, u32[]{:S(2)}, u32[]{:S(2)}) %collective-permute-start.1) | collective-permute-done | bytes 917536 | tf_op jit(solution)/shard_map/ppermute | solution.py:64
  98.2 1.5 fusion.40
  100.3 1.6 collective-permute-start.4
  104.3 8.6 %collective-permute-done.2 = bf16[32,3584]{1,0:T(8,128)(2,1)S(1)} collective-permute-done((bf16[32,3584]{1,0:T(8,128)(2,1)S(1)}, bf16[32,3584]{1,0:T(8,128)(2,1)S(1)}, u32[]{:S(2)}, u32[]{:S(2)}) %collective-permute-start.2) | collective-permute-done | bytes 229408 | tf_op jit(solution)/shard_map/ppermute | solution.py:64
  113.4 9.0 %collective-permute-done.3 = bf16[32,3584]{1,0:T(8,128)(2,1)S(1)} collective-permute-done((bf16[32,3584]{1,0:T(8,128)(2,1)S(1)}, bf16[32,3584]{1,0:T(8,128)(2,1)S(1)}, u32[]{:S(2)}, u32[]{:S(2)}) %collective-permute-start.3) | collective-permute-done | bytes 229408 | tf_op jit(solution)/shard_map/ppermute | solution.py:64
  122.4 1.8 multiply_reduce_fusion
  125.1 1.8 collective-permute-start.21
  126.9 1.7 collective-permute-start.20
  128.6 1.8 collective-permute-start.12
  131.0 7.6 %collective-permute-done.19 = bf16[32,3584]{1,0:T(8,128)(2,1)S(1)} collective-permute-done((bf16[32,3584]{1,0:T(8,128)(2,1)S(1)}, bf16[32,3584]{1,0:T(8,128)(2,1)S(1)}, u32[]{:S(2)}, u32[]{:S(2)}) %collective-permute-start.19) | collective-permute-done | bytes 229408 | tf_op jit(solution)/shard_map/ppermute | solution.py:64
  138.6 20.3 %collective-permute-done.20 = bf16[32,3584]{1,0:T(8,128)(2,1)S(1)} collective-permute-done((bf16[32,3584]{1,0:T(8,128)(2,1)S(1)}, bf16[32,3584]{1,0:T(8,128)(2,1)S(1)}, u32[]{:S(2)}, u32[]{:S(2)}) %collective-permute-start.20) | collective-permute-done | bytes 229408 | tf_op jit(solution)/shard_map/ppermute | solution.py:64
  159.8 6.3 %collective-permute-done.11 = bf16[32,3584]{1,0:T(8,128)(2,1)S(1)} collective-permute-done((bf16[32,3584]{1,0:T(8,128)(2,1)S(1)}, bf16[32,3584]{1,0:T(8,128)(2,1)S(1)}, u32[]{:S(2)}, u32[]{:S(2)}) %collective-permute-start.11) | collective-permute-done | bytes 229408 | tf_op jit(solution)/shard_map/ppermute | solution.py:64
  166.3 1.6 collective-permute-start.14
  169.9 27.2 %collective-permute-done.22.refs_2_ = bf16[32,3584]{1,0:T(8,128)(2,1)S(1)} collective-permute-done((bf16[32,3584]{1,0:T(8,128)(2,1)S(1)}, bf16[32,3584]{1,0:T(8,128)(2,1)S(1)}, u32[]{:S(2)}, u32[]{:S(2)}) %collective-permute-start.22) | collective-permute-done | bytes 229408 | tf_op jit(solution)/shard_map/ppermute | solution.py:64
  197.0 4.6 %collective-permute-done.13.refs_2_ = bf16[32,3584]{1,0:T(8,128)(2,1)} collective-permute-done((bf16[32,3584]{1,0:T(8,128)(2,1)S(1)}, bf16[32,3584]{1,0:T(8,128)(2,1)}, u32[]{:S(2)}, u32[]{:S(2)}) %collective-permute-start.13) | collective-permute-done | bytes 229408 | tf_op jit(solution)/shard_map/ppermute | solution.py:64
  203.9 2.3 collective-permute-done.27.refs_7_
  206.2 112.4 %place.3 = bf16[512,3584]{1,0:T(8,128)(2,1)} custom-call(bf16[32,3584]{1,0:T(8,128)(2,1)} %copy-done.8, bf16[96,3584]{1,0:T(8,128)(2,1)} %copy-done.5, bf16[32,3584]{1,0:T(8,128)(2,1)} %copy-done.17, bf16[96,3584]{1,0:T(8,128)(2,1)} %copy-done.12, bf16[32,3584]{1,0:T(8,128)(2,1)} %copy-done.16, bf16[96,3584]{1,0:T(8,128)(2,1)} %copy-done.11, ...), custom_call_target="tpu_custom_call" | custom-call | tf_op jit(solution)/shard_map/place/pallas_call | solution.py:131
  318.6 112.4 %place.2 = bf16[512,3584]{1,0:T(8,128)(2,1)} custom-call(bf16[32,3584]{1,0:T(8,128)(2,1)} %copy-done.7, bf16[96,3584]{1,0:T(8,128)(2,1)} %copy-done.6, bf16[32,3584]{1,0:T(8,128)(2,1)} %collective-permute-done.13.refs_2_, bf16[96,3584]{1,0:T(8,128)(2,1)} %collective-permute-done.14.refs_3_, bf16[32,3584]{1,0:T(8,128)(2,1)} %collective-permute-done.15.refs_4_, ...), custom_call_target="tpu_custom_call" | custom-call | tf_op jit(solution)/shard_map/place/pallas_call | solution.py:131
  (132 shorter events, 19.6 us)
Async XLA Ops:
  2.1 33.7 %all-to-all-start = ((s32[16,1,1]{2,1,0:T(1,128)}), s32[16,1,1]{2,1,0:T(1,128)S(1)}, u32[]{:S(2)}, u32[]{:S(2)}) async-start(s32[16,1,1]{2,1,0:T(1,128)} %copy.32), calls=%async_computation | async-start | bytes 16384 | tf_op jit(solution)/shard_map/all_to_all | solution.py:172
  18.5 33.2 %collective-permute-start.5 = (bf16[256,3584]{1,0:T(8,128)(2,1)}, bf16[256,3584]{1,0:T(8,128)(2,1)}, u32[]{:S(2)}, u32[]{:S(2)}) collective-permute-start(bf16[256,3584]{1,0:T(8,128)(2,1)} %convolution_convert_fusion), channel_id=1, source_target_pairs={{0,1},{1,0},{2,3},{3,2},{4,5},{5,4},{6,7},{7,6},{8,9},{9,8},{10,11... | collective-permute-start | bytes 5505032 | tf_op jit(solution)/shard_map/ppermute | solution.py:64
  23.0 34.0 %collective-permute-start = (bf16[256,3584]{1,0:T(8,128)(2,1)}, bf16[256,3584]{1,0:T(8,128)(2,1)}, u32[]{:S(2)}, u32[]{:S(2)}) collective-permute-start(bf16[256,3584]{1,0:T(8,128)(2,1)} %convolution_convert_fusion.1), channel_id=1, source_target_pairs={{0,1},{1,0},{2,3},{3,2},{4,5},{5,4},{6,7},{7,6},{8,9},{9,8},{10,11... | collective-permute-start | bytes 5505032 | tf_op jit(solution)/shard_map/ppermute | solution.py:64
  35.8 15.5 %all-to-all-start.1 = ((bf16[16,2,3584]{2,1,0:T(2,128)(2,1)}), bf16[16,2,3584]{2,1,0:T(2,128)(2,1)S(1)}, u32[]{:S(2)}, u32[]{:S(2)}) async-start(bf16[16,2,3584]{2,1,0:T(2,128)(2,1)} %reshape.143), calls=%async_computation.1 | async-start | bytes 458752 | tf_op jit(solution)/shard_map/all_to_all | solution.py:171
  56.3 23.3 %collective-permute-start.6 = (bf16[128,3584]{1,0:T(8,128)(2,1)S(1)}, bf16[128,3584]{1,0:T(8,128)(2,1)S(1)}, u32[]{:S(2)}, u32[]{:S(2)}) collective-permute-start(bf16[128,3584]{1,0:T(8,128)(2,1)S(1)} %add_convert_fusion), channel_id=1, source_target_pairs={{0,2},{1,3},{2,0},{3,1},{4,6},{5,7},{6,4},{7,5},{8,10},{9,11},{10,... | collective-permute-start | bytes 2752520 | tf_op jit(solution)/shard_map/ppermute | solution.py:64
  59.6 38.5 %collective-permute-start.1 = (bf16[128,3584]{1,0:T(8,128)(2,1)S(1)}, bf16[128,3584]{1,0:T(8,128)(2,1)S(1)}, u32[]{:S(2)}, u32[]{:S(2)}) collective-permute-start(bf16[128,3584]{1,0:T(8,128)(2,1)S(1)} %add_convert_fusion.2), channel_id=1, source_target_pairs={{0,2},{1,3},{2,0},{3,1},{4,6},{5,7},{6,4},{7,5},{8,10},{9,11},{10,... | collective-permute-start | bytes 2752520 | tf_op jit(solution)/shard_map/ppermute | solution.py:64
  81.2 20.7 %collective-permute-start.7 = (bf16[32,3584]{1,0:T(8,128)(2,1)S(1)}, bf16[32,3584]{1,0:T(8,128)(2,1)S(1)}, u32[]{:S(2)}, u32[]{:S(2)}) collective-permute-start(bf16[32,3584]{1,0:T(8,128)(2,1)S(1)} %get-tuple-element.24), channel_id=1, source_target_pairs={{0,4},{1,5},{2,6},{3,7},{4,0},{5,1},{6,2},{7,3},{8,12},{9,13},{10,... | collective-permute-start | bytes 688136 | tf_op jit(solution)/shard_map/ppermute | solution.py:64
  81.3 22.1 %collective-permute-start.9 = (bf16[32,3584]{1,0:T(8,128)(2,1)S(1)}, bf16[32,3584]{1,0:T(8,128)(2,1)S(1)}, u32[]{:S(2)}, u32[]{:S(2)}) collective-permute-start(bf16[32,3584]{1,0:T(8,128)(2,1)S(1)} %get-tuple-element.25), channel_id=1, source_target_pairs={{0,12},{1,13},{2,14},{3,15},{4,8},{5,9},{6,10},{7,11},{8,4},{9,5},... | collective-permute-start | bytes 688136 | tf_op jit(solution)/shard_map/ppermute | solution.py:64
  83.6 19.7 %collective-permute-start.8 = (bf16[32,3584]{1,0:T(8,128)(2,1)S(1)}, bf16[32,3584]{1,0:T(8,128)(2,1)S(1)}, u32[]{:S(2)}, u32[]{:S(2)}) collective-permute-start(bf16[32,3584]{1,0:T(8,128)(2,1)S(1)} %get-tuple-element.26), channel_id=1, source_target_pairs={{0,8},{1,9},{2,10},{3,11},{4,12},{5,13},{6,14},{7,15},{8,0},{9,1},... | collective-permute-start | bytes 688136 | tf_op jit(solution)/shard_map/ppermute | solution.py:64
  99.8 13.1 %collective-permute-start.2 = (bf16[32,3584]{1,0:T(8,128)(2,1)S(1)}, bf16[32,3584]{1,0:T(8,128)(2,1)S(1)}, u32[]{:S(2)}, u32[]{:S(2)}) collective-permute-start(bf16[32,3584]{1,0:T(8,128)(2,1)S(1)} %get-tuple-element.27), channel_id=1, source_target_pairs={{0,4},{1,5},{2,6},{3,7},{4,0},{5,1},{6,2},{7,3},{8,12},{9,13},{10,... | collective-permute-start | bytes 688136 | tf_op jit(solution)/shard_map/ppermute | solution.py:64
  100.3 13.0 %collective-permute-start.4 = (bf16[32,3584]{1,0:T(8,128)(2,1)S(1)}, bf16[32,3584]{1,0:T(8,128)(2,1)S(1)}, u32[]{:S(2)}, u32[]{:S(2)}) collective-permute-start(bf16[32,3584]{1,0:T(8,128)(2,1)S(1)} %get-tuple-element.28), channel_id=1, source_target_pairs={{0,12},{1,13},{2,14},{3,15},{4,8},{5,9},{6,10},{7,11},{8,4},{9,5},... | collective-permute-start | bytes 688136 | tf_op jit(solution)/shard_map/ppermute | solution.py:64
  101.9 20.4 %collective-permute-start.3 = (bf16[32,3584]{1,0:T(8,128)(2,1)S(1)}, bf16[32,3584]{1,0:T(8,128)(2,1)S(1)}, u32[]{:S(2)}, u32[]{:S(2)}) collective-permute-start(bf16[32,3584]{1,0:T(8,128)(2,1)S(1)} %get-tuple-element.29), channel_id=1, source_target_pairs={{0,8},{1,9},{2,10},{3,11},{4,12},{5,13},{6,14},{7,15},{8,0},{9,1},... | collective-permute-start | bytes 688136 | tf_op jit(solution)/shard_map/ppermute | solution.py:64
  125.1 78.7 %copy-start.8 = (bf16[32,3584]{1,0:T(8,128)(2,1)}, bf16[32,3584]{1,0:T(8,128)(2,1)S(1)}, u32[]{:S(2)}) copy-start(bf16[32,3584]{1,0:T(8,128)(2,1)S(1)} %get-tuple-element.10.refs_0_) | copy-start | bytes 688132
  125.1 13.4 %collective-permute-start.19 = (bf16[32,3584]{1,0:T(8,128)(2,1)S(1)}, bf16[32,3584]{1,0:T(8,128)(2,1)S(1)}, u32[]{:S(2)}, u32[]{:S(2)}) collective-permute-start(bf16[32,3584]{1,0:T(8,128)(2,1)S(1)} %get-tuple-element.10.refs_0_), channel_id=1, source_target_pairs={{0,4},{1,5},{2,6},{3,7},{4,0},{5,1},{6,2},{7,3},{8,12},{9,13},{10,... | collective-permute-start | bytes 688136 | tf_op jit(solution)/shard_map/ppermute | solution.py:64
  125.1 33.8 %collective-permute-start.21 = (bf16[32,3584]{1,0:T(8,128)(2,1)S(1)}, bf16[32,3584]{1,0:T(8,128)(2,1)S(1)}, u32[]{:S(2)}, u32[]{:S(2)}) collective-permute-start(bf16[32,3584]{1,0:T(8,128)(2,1)S(1)} %get-tuple-element.10.refs_0_), channel_id=1, source_target_pairs={{0,12},{1,13},{2,14},{3,15},{4,8},{5,9},{6,10},{7,11},{8,4},{9,5},... | collective-permute-start | bytes 688136 | tf_op jit(solution)/shard_map/ppermute | solution.py:64
  126.9 32.0 %collective-permute-start.20 = (bf16[32,3584]{1,0:T(8,128)(2,1)S(1)}, bf16[32,3584]{1,0:T(8,128)(2,1)S(1)}, u32[]{:S(2)}, u32[]{:S(2)}) collective-permute-start(bf16[32,3584]{1,0:T(8,128)(2,1)S(1)} %get-tuple-element.10.refs_0_), channel_id=1, source_target_pairs={{0,8},{1,9},{2,10},{3,11},{4,12},{5,13},{6,14},{7,15},{8,0},{9,1},... | collective-permute-start | bytes 688136 | tf_op jit(solution)/shard_map/ppermute | solution.py:64
  128.6 37.6 %collective-permute-start.12 = (bf16[32,3584]{1,0:T(8,128)(2,1)S(1)}, bf16[32,3584]{1,0:T(8,128)(2,1)S(1)}, u32[]{:S(2)}, u32[]{:S(2)}) collective-permute-start(bf16[32,3584]{1,0:T(8,128)(2,1)S(1)} %get-tuple-element.30.refs_0_), channel_id=1, source_target_pairs={{0,12},{1,13},{2,14},{3,15},{4,8},{5,9},{6,10},{7,11},{8,4},{9,5},... | collective-permute-start | bytes 688136 | tf_op jit(solution)/shard_map/ppermute | solution.py:64
  130.4 35.8 %collective-permute-start.11 = (bf16[32,3584]{1,0:T(8,128)(2,1)S(1)}, bf16[32,3584]{1,0:T(8,128)(2,1)S(1)}, u32[]{:S(2)}, u32[]{:S(2)}) collective-permute-start(bf16[32,3584]{1,0:T(8,128)(2,1)S(1)} %get-tuple-element.30.refs_0_), channel_id=1, source_target_pairs={{0,8},{1,9},{2,10},{3,11},{4,12},{5,13},{6,14},{7,15},{8,0},{9,1},... | collective-permute-start | bytes 688136 | tf_op jit(solution)/shard_map/ppermute | solution.py:64
  138.5 21.3 %collective-permute-start.10 = (bf16[32,3584]{1,0:T(8,128)(2,1)S(1)}, bf16[32,3584]{1,0:T(8,128)(2,1)S(1)}, u32[]{:S(2)}, u32[]{:S(2)}) collective-permute-start(bf16[32,3584]{1,0:T(8,128)(2,1)S(1)} %get-tuple-element.30.refs_0_), channel_id=1, source_target_pairs={{0,4},{1,5},{2,6},{3,7},{4,0},{5,1},{6,2},{7,3},{8,12},{9,13},{10,... | collective-permute-start | bytes 688136 | tf_op jit(solution)/shard_map/ppermute | solution.py:64
  159.0 43.1 %collective-permute-start.25 = (bf16[96,3584]{1,0:T(8,128)(2,1)S(1)}, bf16[96,3584]{1,0:T(8,128)(2,1)S(1)}, u32[]{:S(2)}, u32[]{:S(2)}) collective-permute-start(bf16[96,3584]{1,0:T(8,128)(2,1)S(1)} %constant_dynamic-update-slice_fusion.3.refs_1_), channel_id=1, source_target_pairs={{0,1},{1,0},{2,3},{3,2},{4,5},{5,4},{6,7},{7,6},{8,9},{9,8},{10,11... | collective-permute-start | bytes 2064392 | tf_op jit(solution)/shard_map/ppermute | solution.py:64
  159.1 43.1 %collective-permute-start.23 = (bf16[96,3584]{1,0:T(8,128)(2,1)S(1)}, bf16[96,3584]{1,0:T(8,128)(2,1)S(1)}, u32[]{:S(2)}, u32[]{:S(2)}) collective-permute-start(bf16[96,3584]{1,0:T(8,128)(2,1)S(1)} %constant_dynamic-update-slice_fusion.3.refs_1_), channel_id=1, source_target_pairs={{0,2},{1,3},{2,0},{3,1},{4,6},{5,7},{6,4},{7,5},{8,10},{9,11},{10,... | collective-permute-start | bytes 2064392 | tf_op jit(solution)/shard_map/ppermute | solution.py:64
  166.2 152.4 %copy-start.6 = (bf16[96,3584]{1,0:T(8,128)(2,1)}, bf16[96,3584]{1,0:T(8,128)(2,1)S(1)}, u32[]{:S(2)}) copy-start(bf16[96,3584]{1,0:T(8,128)(2,1)S(1)} %constant_dynamic-update-slice_fusion.refs_1_) | copy-start | bytes 2064388
  166.3 36.4 %collective-permute-start.14 = (bf16[96,3584]{1,0:T(8,128)(2,1)S(1)}, bf16[96,3584]{1,0:T(8,128)(2,1)}, u32[]{:S(2)}, u32[]{:S(2)}) collective-permute-start(bf16[96,3584]{1,0:T(8,128)(2,1)S(1)} %constant_dynamic-update-slice_fusion.refs_1_), channel_id=1, source_target_pairs={{0,2},{1,3},{2,0},{3,1},{4,6},{5,7},{6,4},{7,5},{8,10},{9,11},{10,... | collective-permute-start | bytes 2064392 | tf_op jit(solution)/shard_map/ppermute | solution.py:64
  167.8 1.5 collective-permute-start.24
  167.8 29.2 %collective-permute-start.22 = (bf16[32,3584]{1,0:T(8,128)(2,1)S(1)}, bf16[32,3584]{1,0:T(8,128)(2,1)S(1)}, u32[]{:S(2)}, u32[]{:S(2)}) collective-permute-start(bf16[32,3584]{1,0:T(8,128)(2,1)S(1)} %get-tuple-element.10.refs_0_), channel_id=1, source_target_pairs={{0,2},{1,3},{2,0},{3,1},{4,6},{5,7},{6,4},{7,5},{8,10},{9,11},{10,... | collective-permute-start | bytes 688136 | tf_op jit(solution)/shard_map/ppermute | solution.py:64
  169.3 32.3 %collective-permute-start.13 = (bf16[32,3584]{1,0:T(8,128)(2,1)S(1)}, bf16[32,3584]{1,0:T(8,128)(2,1)}, u32[]{:S(2)}, u32[]{:S(2)}) collective-permute-start(bf16[32,3584]{1,0:T(8,128)(2,1)S(1)} %get-tuple-element.30.refs_0_), channel_id=1, source_target_pairs={{0,2},{1,3},{2,0},{3,1},{4,6},{5,7},{6,4},{7,5},{8,10},{9,11},{10,... | collective-permute-start | bytes 688136 | tf_op jit(solution)/shard_map/ppermute | solution.py:64
  197.0 4.6 %collective-permute-start.26 = (bf16[32,3584]{1,0:T(8,128)(2,1)S(1)}, bf16[32,3584]{1,0:T(8,128)(2,1)S(1)}, u32[]{:S(2)}, u32[]{:S(2)}) collective-permute-start(bf16[32,3584]{1,0:T(8,128)(2,1)S(1)} %collective-permute-done.22.refs_2_), channel_id=1, source_target_pairs={{0,1},{1,0},{2,3},{3,2},{4,5},{5,4},{6,7},{7,6},{8,9},{9,8},{10,11... | collective-permute-start | bytes 688136 | tf_op jit(solution)/shard_map/ppermute | solution.py:64
  201.6 117.0 %collective-permute-start.15 = (bf16[32,3584]{1,0:T(8,128)(2,1)S(1)}, bf16[32,3584]{1,0:T(8,128)(2,1)}, u32[]{:S(2)}, u32[]{:S(2)}) collective-permute-start(bf16[32,3584]{1,0:T(8,128)(2,1)S(1)} %get-tuple-element.30.refs_0_), channel_id=1, source_target_pairs={{0,1},{1,0},{2,3},{3,2},{4,5},{5,4},{6,7},{7,6},{8,9},{9,8},{10,11... | collective-permute-start | bytes 688136 | tf_op jit(solution)/shard_map/ppermute | solution.py:64
  201.6 117.0 %collective-permute-start.16 = (bf16[96,3584]{1,0:T(8,128)(2,1)S(1)}, bf16[96,3584]{1,0:T(8,128)(2,1)}, u32[]{:S(2)}, u32[]{:S(2)}) collective-permute-start(bf16[96,3584]{1,0:T(8,128)(2,1)S(1)} %constant_dynamic-update-slice_fusion.refs_1_), channel_id=1, source_target_pairs={{0,1},{1,0},{2,3},{3,2},{4,5},{5,4},{6,7},{7,6},{8,9},{9,8},{10,11... | collective-permute-start | bytes 2064392 | tf_op jit(solution)/shard_map/ppermute | solution.py:64
  202.1 116.5 %collective-permute-start.17 = (bf16[32,3584]{1,0:T(8,128)(2,1)}, bf16[32,3584]{1,0:T(8,128)(2,1)}, u32[]{:S(2)}, u32[]{:S(2)}) collective-permute-start(bf16[32,3584]{1,0:T(8,128)(2,1)} %collective-permute-done.13.refs_2_), channel_id=1, source_target_pairs={{0,1},{1,0},{2,3},{3,2},{4,5},{5,4},{6,7},{7,6},{8,9},{9,8},{10,11... | collective-permute-start | bytes 688136 | tf_op jit(solution)/shard_map/ppermute | solution.py:64
  202.2 4.0 collective-permute-start.27
  202.6 116.0 %collective-permute-start.18 = (bf16[96,3584]{1,0:T(8,128)(2,1)}, bf16[96,3584]{1,0:T(8,128)(2,1)}, u32[]{:S(2)}, u32[]{:S(2)}) collective-permute-start(bf16[96,3584]{1,0:T(8,128)(2,1)} %collective-permute-done.14.refs_3_), channel_id=1, source_target_pairs={{0,1},{1,0},{2,3},{3,2},{4,5},{5,4},{6,7},{7,6},{8,9},{9,8},{10,11... | collective-permute-start | bytes 2064392 | tf_op jit(solution)/shard_map/ppermute | solution.py:64
  (24 other events, 402.3 us)

commit v2 on v1

v2 whole, which is shorter than its diff:
```python
import functools

import jax
import jax.numpy as jnp
from jax import lax
from jax.experimental import pallas as pl
from jax.experimental.pallas import tpu as pltpu
from jax.sharding import PartitionSpec as P

beta_one = 0.9
beta_two = 0.99
first_fix = 1.0 - 0.9**4
second_fix = 1.0 - 0.99**4
learn_rate = 0.02
adam_eps = 1e-08
reset_gain = 0.01
norm_eps = 1e-06

KEPT = -1
ABSENT = -2


def adam_update(weight, moment, second, gradient):
    moment_new = beta_one * moment + (1.0 - beta_one) * gradient
    second_new = beta_two * second + (1.0 - beta_two) * gradient * gradient
    weight_new = weight - learn_rate * (moment_new / first_fix) / (
        jnp.sqrt(second_new / second_fix) + adam_eps
    )
    return (weight_new, moment_new, second_new)


def inverse_rms(value):
    return lax.rsqrt(jnp.mean(value * value, axis=1, keepdims=True) + norm_eps)


def swap(value, bits, size):
    return lax.ppermute(value, "latent", [(i, i ^ bits) for i in range(size)])


def cost(flops, moved):
    return pl.CostEstimate(flops=int(flops), bytes_accessed=int(moved), transcendentals=0)


def slot_key(slot, depth):
    core = 1 - slot // (2 * depth)
    y = 1 - (slot // depth) % 2
    return 4 * (slot % depth) + 2 * y + core


def gather_table(row, size):
    table = row
    step = 1
    while step < size:
        near = [table]
        for k in range(1, 4 if step * 2 < size else 2):
            near.append(swap(table, step * k, size))
        table = jnp.concatenate(near, axis=0)
        step *= len(near)
    return table


def ordered_coef(coef, wanted):
    latents = coef.shape[1]
    columns = lax.broadcasted_iota(jnp.int32, (latents, latents), 1)
    pick = (wanted == columns).astype(coef.dtype)
    return lax.dot_general(
        pick, coef, (((1,), (1,)), ((), ())), preferred_element_type=jnp.float32
    ).astype(coef.dtype)


def slot_rows(size, rows):
    row = lax.broadcasted_iota(jnp.int32, (size * rows, 1), 0)
    return slot_key(row // rows, size // 4), row % rows


def order_kernel(size, rows, coef_ref, out_ref):
    key, local = slot_rows(size, rows)
    owner = lax.axis_index("latent") ^ key
    out_ref[...] = ordered_coef(coef_ref[...], owner * rows + local)


def select_kernel(size, rows, table_ref, picks_ref, coef_ref, out_ref, code_ref):
    me = lax.axis_index("latent")
    cap = picks_ref.shape[0]
    key, local = slot_rows(size, rows)
    counts = table_ref[:, :size]
    order = table_ref[:, size:]
    source = me ^ lax.broadcasted_iota(jnp.int32, (size, 1), 0)
    before = jnp.sum(jnp.where(source < me, counts, 0), axis=0, keepdims=True)
    total = jnp.sum(counts, axis=0, keepdims=True)
    owners = lax.broadcasted_iota(jnp.int32, (size, size), 1) == source

    def by_key(row):
        return jnp.sum(jnp.where(owners, row, 0), axis=1, keepdims=True)

    begin, here = by_key(before), by_key(counts[:1])
    place = lax.broadcasted_iota(jnp.int32, (size, rows), 1)
    token = jnp.full((size, rows), ABSENT, jnp.int32)
    for c in range(cap):
        own = (place == begin + c) & (here > c)
        token = jnp.where(own, by_key(picks_ref[c : c + 1]), token)
    token = jnp.where(place < by_key(total), token, KEPT)
    spread = (lax.broadcasted_iota(jnp.int32, (size * rows, size), 1) == key).astype(jnp.float32)

    def by_row(table):
        return jnp.dot(
            spread, table.astype(jnp.float32), precision=lax.Precision.HIGHEST
        )

    is_latent = by_row(order) == local.astype(jnp.float32)
    code = jnp.sum(jnp.where(is_latent, by_row(token), 0.0), axis=1, keepdims=True)
    code = (code + jnp.where(code < 0, -0.5, 0.5)).astype(jnp.int32)
    code_ref[...] = code
    ordered = ordered_coef(coef_ref[...], (me ^ key) * rows + local)
    tokens = lax.broadcasted_iota(jnp.int32, ordered.shape, 1)
    out_ref[...] = jnp.where(code == KEPT, ordered, (tokens == code).astype(ordered.dtype))


def order_call(coef, size, rows):
    tokens, latents = coef.shape
    return pl.pallas_call(
        functools.partial(order_kernel, size, rows),
        out_shape=jax.ShapeDtypeStruct((latents, tokens), coef.dtype),
        cost_estimate=cost(2 * latents * latents * tokens, 4 * latents * tokens),
        name="order",
    )(coef)


def select_call(table, picks, coef, size, rows):
    tokens, latents = coef.shape
    return pl.pallas_call(
        functools.partial(select_kernel, size, rows),
        out_shape=(
            jax.ShapeDtypeStruct((latents, tokens), coef.dtype),
            jax.ShapeDtypeStruct((latents, 1), jnp.int32),
        ),
        cost_estimate=cost(4 * latents * latents * tokens, 4 * latents * tokens),
        name="select",
    )(table, picks, coef)


def product_kernel(left_ref, right_ref, sent_ref, kept_ref):
    half = sent_ref.shape[0]
    right = right_ref[...]
    for ref, begin in ((sent_ref, 0), (kept_ref, half)):
        ref[...] = jnp.dot(
            left_ref[begin : begin + half], right, preferred_element_type=jnp.float32
        ).astype(ref.dtype)


def product(left, right, begin, width):
    latents, tokens = left.shape
    tile = 256
    half = latents // 2
    out = jax.ShapeDtypeStruct((half, width), left.dtype)
    return pl.pallas_call(
        product_kernel,
        grid=(width // tile,),
        in_specs=[
            pl.BlockSpec((latents, tokens), lambda j: (0, 0)),
            pl.BlockSpec((tokens, tile), lambda j: (0, j + begin // tile)),
        ],
        out_specs=(pl.BlockSpec((half, tile), lambda j: (0, j)),) * 2,
        out_shape=(out, out),
        cost_estimate=cost(
            2 * latents * tokens * width, 2 * (latents * tokens + (latents + tokens) * width)
        ),
        name="product",
    )(left, right)


def chunk_parts(left, right, begin, width, rows, size):
    depth = size // 4
    quarter = depth * rows
    sent, kept = product(left, right, begin, width)
    from_core = swap(sent, 1, size)
    wide = jnp.float32
    to_y = (kept[:quarter].astype(wide) + from_core[:quarter].astype(wide)).astype(kept.dtype)
    from_y = swap(to_y, 2, size)
    total = (
        kept[quarter:].astype(wide) + from_core[quarter:].astype(wide) + from_y.astype(wide)
    ).astype(kept.dtype)
    parts = [total[k * rows : (k + 1) * rows] for k in range(depth)]
    return [parts[0]] + [swap(parts[k], 4 * k, size) for k in range(1, depth)]


def read_gradient(refs, depth):
    sums = []
    for begin in range(0, len(refs), depth):
        total = refs[begin][...].astype(jnp.float32)
        for ref in refs[begin + 1 : begin + depth]:
            total = total + ref[...].astype(jnp.float32)
        sums.append(total)
    return jnp.concatenate(sums, axis=1)


def enc_kernel(depth, code_ref, w_ref, m_ref, v_ref, *refs):
    parts, (w_out, m_out, v_out, block, fresh) = refs[:-5], refs[-5:]
    gradient = read_gradient(parts, depth)
    reset = code_ref[...] != KEPT
    w, m, v = adam_update(w_ref[...], m_ref[...], v_ref[...], gradient)
    w = jnp.where(reset, reset_gain * gradient * inverse_rms(gradient), w)
    w_out[...] = w
    m_out[...] = jnp.where(reset, 0.0, m)
    v_out[...] = jnp.where(reset, 0.0, v)
    block[...] = w.astype(block.dtype)
    fresh[...] = gradient.astype(fresh.dtype)


def dec_kernel(depth, code_ref, w_ref, m_ref, v_ref, fresh_ref, *refs):
    parts, (w_out, m_out, v_out, block) = refs[:-4], refs[-4:]
    reset = code_ref[...] != KEPT
    w, m, v = adam_update(w_ref[...], m_ref[...], v_ref[...], read_gradient(parts, depth))
    w = jnp.where(reset, fresh_ref[...].astype(jnp.float32), w)
    w = w * inverse_rms(w)
    w_out[...] = w
    m_out[...] = jnp.where(reset, 0.0, m)
    v_out[...] = jnp.where(reset, 0.0, v)
    block[...] = w.astype(block.dtype)


def update(kernel, code, states, fresh, parts, size, extra, name):
    rows, width = states[0].shape
    depth = size // 4
    tile = 16
    own_slot = 3 * depth

    def row_block(columns):
        return pl.BlockSpec((tile, columns), lambda i: (i, 0))

    code_spec = pl.BlockSpec((tile, 1), lambda i: (i + own_slot * rows // tile, 0))
    operands = list(states) + list(fresh) + list(parts)
    wide = jax.ShapeDtypeStruct((rows, width), jnp.float32)
    narrow = jax.ShapeDtypeStruct((rows, width), jnp.bfloat16)
    return pl.pallas_call(
        functools.partial(kernel, depth),
        grid=(rows // tile,),
        in_specs=[code_spec] + [row_block(value.shape[1]) for value in operands],
        out_specs=(row_block(width),) * (3 + extra),
        out_shape=(wide,) * 3 + (narrow,) * extra,
        cost_estimate=cost(40 * rows * width, 40 * rows * width),
        name=name,
    )(code, *operands)


def place_kernel(keys, rows, *refs):
    count = len(keys)
    whole, stage, sems_in, sems_out = refs[-4:]
    pieces = refs[:count]
    me = lax.axis_index("latent")
    first = [
        pltpu.make_async_copy(piece, stage.at[i], sems_in.at[i])
        for i, piece in enumerate(pieces)
    ]
    second = []
    for i, key in enumerate(keys):
        start = pl.multiple_of((me ^ key) * rows, rows)
        second.append(
            pltpu.make_async_copy(stage.at[i], whole.at[pl.ds(start, rows)], sems_out.at[i])
        )
    for copy in first:
        copy.start()
    for before, after in zip(first, second):
        before.wait()
        after.start()
    for copy in second:
        copy.wait()


def place(pieces, size, prior=None):
    keys = [key for key, _ in pieces]
    blocks = [block for _, block in pieces]
    rows, width = blocks[0].shape
    dtype = blocks[0].dtype
    count = len(keys)
    operands = blocks + ([] if prior is None else [prior])
    return pl.pallas_call(
        functools.partial(place_kernel, keys, rows),
        out_shape=jax.ShapeDtypeStruct((size * rows, width), dtype),
        in_specs=[pl.BlockSpec(memory_space=pl.ANY)] * len(operands),
        out_specs=pl.BlockSpec(memory_space=pl.ANY),
        scratch_shapes=[
            pltpu.VMEM((count, rows, width), dtype),
            pltpu.SemaphoreType.DMA((count,)),
            pltpu.SemaphoreType.DMA((count,)),
        ],
        input_output_aliases={} if prior is None else {count: 0},
        cost_estimate=cost(0, 4 * count * rows * width),
        name="place",
    )(*operands)


def gathered(block, size):
    depth = size // 4
    near = [(0, block)] + [(4 * k, swap(block, 4 * k, size)) for k in range(1, depth)]
    near += [(key ^ 2, swap(value, 2, size)) for key, value in near]
    far = [(key ^ 1, swap(value, 1, size)) for key, value in near]
    return place(far, size, place(near, size))


def shards(
    x_rows,
    out_grad,
    enc_coef,
    latent_act,
    enc_w,
    enc_m,
    enc_v,
    dec_w,
    dec_m,
    dec_v,
    dead_order,
    pick_rows,
    send_count,
):
    width = x_rows.shape[1]
    rows = enc_w.shape[0]
    size = lax.axis_size("latent")
    half = width // 2
    table = gather_table(jnp.concatenate([send_count, dead_order], axis=1), size)
    dec_left = order_call(latent_act, size, rows)
    dec_parts = chunk_parts(dec_left, out_grad, 0, half, rows, size)
    enc_left, code = select_call(table, pick_rows[0].T, enc_coef, size, rows)
    enc_parts = chunk_parts(enc_left, x_rows, 0, half, rows, size)
    enc_parts += chunk_parts(enc_left, x_rows, half, half, rows, size)
    dec_parts += chunk_parts(dec_left, out_grad, half, half, rows, size)
    enc_out, enc_mo, enc_vo, enc_block, fresh = update(
        enc_kernel, code, (enc_w, enc_m, enc_v), (), enc_parts, size, 2, "enc_update"
    )
    enc_full = gathered(enc_block, size)
    dec_out, dec_mo, dec_vo, dec_block = update(
        dec_kernel, code, (dec_w, dec_m, dec_v), (fresh,), dec_parts, size, 1, "dec_update"
    )
    dec_full = gathered(dec_block, size)
    return (enc_out, enc_mo, enc_vo, dec_out, dec_mo, dec_vo, enc_full, dec_full)


def solution(mesh):
    split = P(("groups", "latent"), None)
    placed = (split,) * 11 + (P(("groups", "latent"), None, None), split)
    return jax.shard_map(
        shards,
        mesh=mesh,
        in_specs=placed,
        out_specs=(split,) * 6 + (P("groups", None),) * 2,
        check_vma=False,
    )
```

time: 432 us -> 203 us (0.47)
  Pallas kernels: 225 us -> 52.1 us
  waiting for transfers between devices: 126 us -> 86.2 us
  matrix products: 27 us -> 0 us
  starting transfers between devices: 33.6 us -> 51.2 us
  other arithmetic: 10.5 us -> 5.54 us
    pallas_call x2 -> x12, Pallas kernels: 225 us -> 52.1 us  [the longest x4 29.7 us: product(): pl.pallas_call(product_kernel, grid=(width // tile,), in_specs=[pl.BlockS...]
    ppermute x28 -> x56, waiting for transfers between devices: 119 us -> 86.2 us  [swap(): return lax.ppermute(value, 'latent', [(i, i ^ bits) for i in range(size)])]
    ppermute x28 -> x56, starting transfers between devices: 20.2 us -> 51.2 us  [swap(): return lax.ppermute(value, 'latent', [(i, i ^ bits) for i in range(size)])]
    dot_general x10 -> x0, matrix products: 27 us -> none  [the longest x6 24.6 us: part(): jnp.dot(left[begin:begin + count], right, preferred_element_type=jnp.floa...]
    all_to_all x2 -> x0, starting transfers between devices: 13.4 us -> none  [the longest x1 7.39 us: shards(): lax.all_to_all(send_count[0], 'latent', split_axis=0, concat_axis=0, tile...]
    all_to_all x2 -> x0, waiting for transfers between devices: 7.31 us -> none  [the longest x1 7.31 us: shards(): lax.all_to_all(chosen, 'latent', split_axis=0, concat_axis=0, tiled=True)]
    gather x2 -> x0, local copies, waits for them, and re-layouts: 5.72 us -> none  [shards(): chosen = x_rows[pick_rows[0]]]
  transfers between devices with their start and end apart: 30 -> 56, of which waited for: 13 -> 18; matrix products, arithmetic and copies ran while one was open for 10% -> 5% of each run, Pallas kernels for 26% -> 19%
where the time goes in v2:
time: 203 us; the launch traced here: 202 us
  waiting for transfers between devices  86.2 us (42%)
  Pallas kernels  52.1 us (26%)
  starting transfers between devices  51.2 us (25%)
  other arithmetic  5.54 us (3%)
  local copies, waits for them, and re-layouts  5.48 us (3%)
    ppermute x56, waiting for transfers between devices, swap(): return lax.ppermute(value, 'latent', [(i, i ^ bits) for i in range(size)])  86.2 us
    ppermute x56, starting transfers between devices, swap(): return lax.ppermute(value, 'latent', [(i, i ^ bits) for i in range(size)])  51.2 us
    pallas_call x4, Pallas kernels, product(): pl.pallas_call(product_kernel, grid=(width // tile,), in_specs=[pl.BlockS...  29.7 us
    pallas_call x4, Pallas kernels, place(): pl.pallas_call(functools.partial(place_kernel, keys, rows), out_shape=jax...  9.64 us
    pallas_call x2, Pallas kernels, update(): pl.pallas_call(functools.partial(kernel, depth), grid=(rows // tile,), in...  6.17 us
  transfers between devices with their start and end apart: 56, of which 18 were waited for; matrix products, arithmetic and copies ran while one was open for 5% of the time, Pallas kernels for 19%

profile of v2, /device:TPU:0, one launch (start us, length us, event | category | flops | bytes accessed | tf_op | source)
XLA Modules:
  0.0 201.7 jit_solution(16257365131415605489)
XLA Ops:
  0.6 3.0 %order.1.left_ref = bf16[512,1024]{1,0:T(8,128)(2,1)} custom-call(bf16[1024,512]{1,0:T(8,128)(2,1)} %coef_ref.3), custom_call_target="tpu_custom_call" | custom-call | flops 536870912 | bytes 2097152 | tf_op jit(solution)/shard_map/order/pallas_call | solution.py:121
  3.6 7.4 %product.6 = (bf16[256,1792]{1,0:T(8,128)(2,1)}, bf16[256,1792]{1,0:T(8,128)(2,1)}) custom-call(bf16[512,1024]{1,0:T(8,128)(2,1)} %order.1.left_ref, bf16[1024,3584]{1,0:T(8,128)(2,1)} %right_ref.7), custom_call_target="tpu_custom_call" | custom-call | flops 1879048192 | bytes 6553600 | tf_op jit(solution)/shard_map/product/pallas_call | solution.py:156
  11.6 2.6 %collective-permute-start.2 = (s32[1,48]{1,0:T(1,128)S(1)}, s32[1,48]{1,0:T(1,128)S(1)}, u32[]{:S(2)}, u32[]{:S(2)}) collective-permute-start(s32[1,48]{1,0:T(1,128)S(1)} %pad_add_fusion.1), channel_id=1, source_target_pairs={{0,3},{1,2},{2,1},{3,0},{4,7},{5,6},{6,5},{7,4},{8,11},{9,10},{10,... | collective-permute-start | bytes 584 | tf_op jit(solution)/shard_map/ppermute | solution.py:37
  17.8 3.6 %collective-permute-start.5 = (s32[4,48]{1,0:T(4,128)S(1)}, s32[4,48]{1,0:T(4,128)S(1)}, u32[]{:S(2)}, u32[]{:S(2)}) collective-permute-start(s32[4,48]{1,0:T(4,128)S(1)} %pad_add_fusion), channel_id=1, source_target_pairs={{0,12},{1,13},{2,14},{3,15},{4,8},{5,9},{6,10},{7,11},{8,4},{9,5},... | collective-permute-start | bytes 2312 | tf_op jit(solution)/shard_map/ppermute | solution.py:37
  22.2 7.4 %product.7 = (bf16[256,1792]{1,0:T(8,128)(2,1)}, bf16[256,1792]{1,0:T(8,128)(2,1)}) custom-call(bf16[512,1024]{1,0:T(8,128)(2,1)} %order.1.left_ref, bf16[1024,3584]{1,0:T(8,128)(2,1)} %right_ref.7), custom_call_target="tpu_custom_call" | custom-call | flops 1879048192 | bytes 6553600 | tf_op jit(solution)/shard_map/product/pallas_call | solution.py:156
  30.9 3.6 %select.1 = (bf16[512,1024]{1,0:T(8,128)(2,1)}, s32[512,1]{1,0:T(8,128)}) custom-call(s32[16,48]{1,0:T(8,128)} %concatenate.12.table_ref, s32[2,16]{1,0:T(2,128)} %bitcast.3, bf16[1024,512]{1,0:T(8,128)(2,1)} %coef_ref.2), custom_call_target="tpu_custom_call" | custom-call | flops 1073741824 | bytes 2097152 | tf_op jit(solution)/shard_map/select/pallas_call | solution.py:131
  34.5 7.4 %product.4 = (bf16[256,1792]{1,0:T(8,128)(2,1)}, bf16[256,1792]{1,0:T(8,128)(2,1)}) custom-call(bf16[512,1024]{1,0:T(8,128)(2,1)} %get-tuple-element.28.left_ref, bf16[1024,3584]{1,0:T(8,128)(2,1)} %right_ref.5), custom_call_target="tpu_custom_call" | custom-call | flops 1879048192 | bytes 6553600 | tf_op jit(solution)/shard_map/product/pallas_call | solution.py:156
  42.4 7.5 %product.5 = (bf16[256,1792]{1,0:T(8,128)(2,1)}, bf16[256,1792]{1,0:T(8,128)(2,1)}) custom-call(bf16[512,1024]{1,0:T(8,128)(2,1)} %get-tuple-element.28.left_ref, bf16[1024,3584]{1,0:T(8,128)(2,1)} %right_ref.5), custom_call_target="tpu_custom_call" | custom-call | flops 1879048192 | bytes 6553600 | tf_op jit(solution)/shard_map/product/pallas_call | solution.py:156
  57.1 6.5 %collective-permute-done.17 = bf16[128,1792]{1,0:T(8,128)(2,1)S(1)} collective-permute-done((bf16[128,1792]{1,0:T(8,128)(2,1)S(1)}, bf16[128,1792]{1,0:T(8,128)(2,1)S(1)}, u32[]{:S(2)}, u32[]{:S(2)}) %collective-permute-start.17) | collective-permute-done | bytes 458784 | tf_op jit(solution)/shard_map/ppermute | solution.py:37
  64.4 3.6 %collective-permute-start.20 = (bf16[32,1792]{1,0:T(8,128)(2,1)S(1)}, bf16[32,1792]{1,0:T(8,128)(2,1)S(1)}, u32[]{:S(2)}, u32[]{:S(2)}) collective-permute-start(bf16[32,1792]{1,0:T(8,128)(2,1)S(1)} %get-tuple-element.50), channel_id=1, source_target_pairs={{0,12},{1,13},{2,14},{3,15},{4,8},{5,9},{6,10},{7,11},{8,4},{9,5},... | collective-permute-start | bytes 344072 | tf_op jit(solution)/shard_map/ppermute | solution.py:37
  68.0 5.4 %collective-permute-done.22 = bf16[128,1792]{1,0:T(8,128)(2,1)S(1)} collective-permute-done((bf16[128,1792]{1,0:T(8,128)(2,1)S(1)}, bf16[128,1792]{1,0:T(8,128)(2,1)S(1)}, u32[]{:S(2)}, u32[]{:S(2)}) %collective-permute-start.22) | collective-permute-done | bytes 458784 | tf_op jit(solution)/shard_map/ppermute | solution.py:37
  74.6 8.6 %collective-permute-done.7 = bf16[128,1792]{1,0:T(8,128)(2,1)S(1)} collective-permute-done((bf16[128,1792]{1,0:T(8,128)(2,1)S(1)}, bf16[128,1792]{1,0:T(8,128)(2,1)S(1)}, u32[]{:S(2)}, u32[]{:S(2)}) %collective-permute-start.7) | collective-permute-done | bytes 458784 | tf_op jit(solution)/shard_map/ppermute | solution.py:37
  85.1 3.6 %collective-permute-start.10 = (bf16[32,1792]{1,0:T(8,128)(2,1)S(1)}, bf16[32,1792]{1,0:T(8,128)(2,1)S(1)}, u32[]{:S(2)}, u32[]{:S(2)}) collective-permute-start(bf16[32,1792]{1,0:T(8,128)(2,1)S(1)} %get-tuple-element.58), channel_id=1, source_target_pairs={{0,12},{1,13},{2,14},{3,15},{4,8},{5,9},{6,10},{7,11},{8,4},{9,5},... | collective-permute-start | bytes 344072 | tf_op jit(solution)/shard_map/ppermute | solution.py:37
  89.5 3.0 %collective-permute-done.12 = bf16[128,1792]{1,0:T(8,128)(2,1)S(1)} collective-permute-done((bf16[128,1792]{1,0:T(8,128)(2,1)S(1)}, bf16[128,1792]{1,0:T(8,128)(2,1)S(1)}, u32[]{:S(2)}, u32[]{:S(2)}) %collective-permute-start.12) | collective-permute-done | bytes 458784 | tf_op jit(solution)/shard_map/ppermute | solution.py:37
  93.3 3.6 %collective-permute-start.15 = (bf16[32,1792]{1,0:T(8,128)(2,1)S(1)}, bf16[32,1792]{1,0:T(8,128)(2,1)S(1)}, u32[]{:S(2)}, u32[]{:S(2)}) collective-permute-start(bf16[32,1792]{1,0:T(8,128)(2,1)S(1)} %get-tuple-element.54), channel_id=1, source_target_pairs={{0,12},{1,13},{2,14},{3,15},{4,8},{5,9},{6,10},{7,11},{8,4},{9,5},... | collective-permute-start | bytes 344072 | tf_op jit(solution)/shard_map/ppermute | solution.py:37
  98.4 4.0 %collective-permute-done.9.refs_2_ = bf16[32,1792]{1,0:T(8,128)(2,1)S(1)} collective-permute-done((bf16[32,1792]{1,0:T(8,128)(2,1)S(1)}, bf16[32,1792]{1,0:T(8,128)(2,1)S(1)}, u32[]{:S(2)}, u32[]{:S(2)}) %collective-permute-start.9) | collective-permute-done | bytes 114720 | tf_op jit(solution)/shard_map/ppermute | solution.py:37
  102.6 4.2 %collective-permute-start.25 = (bf16[32,1792]{1,0:T(8,128)(2,1)S(1)}, bf16[32,1792]{1,0:T(8,128)(2,1)S(1)}, u32[]{:S(2)}, u32[]{:S(2)}) collective-permute-start(bf16[32,1792]{1,0:T(8,128)(2,1)S(1)} %get-tuple-element.46), channel_id=1, source_target_pairs={{0,12},{1,13},{2,14},{3,15},{4,8},{5,9},{6,10},{7,11},{8,4},{9,5},... | collective-permute-start | bytes 344072 | tf_op jit(solution)/shard_map/ppermute | solution.py:37
  106.8 7.4 %collective-permute-done.14.refs_6_ = bf16[32,1792]{1,0:T(8,128)(2,1)S(1)} collective-permute-done((bf16[32,1792]{1,0:T(8,128)(2,1)S(1)}, bf16[32,1792]{1,0:T(8,128)(2,1)S(1)}, u32[]{:S(2)}, u32[]{:S(2)}) %collective-permute-start.14) | collective-permute-done | bytes 114720 | tf_op jit(solution)/shard_map/ppermute | solution.py:37
  114.2 3.1 %collective-permute-start.23 = (bf16[32,1792]{1,0:T(8,128)(2,1)S(1)}, bf16[32,1792]{1,0:T(8,128)(2,1)S(1)}, u32[]{:S(2)}, u32[]{:S(2)}) collective-permute-start(bf16[32,1792]{1,0:T(8,128)(2,1)S(1)} %get-tuple-element.48), channel_id=1, source_target_pairs={{0,4},{1,5},{2,6},{3,7},{4,0},{5,1},{6,2},{7,3},{8,12},{9,13},{10,... | collective-permute-start | bytes 344072 | tf_op jit(solution)/shard_map/ppermute | solution.py:37
  117.4 3.1 %enc_update.1 = (f32[32,3584]{1,0:T(8,128)}, f32[32,3584]{1,0:T(8,128)}, f32[32,3584]{1,0:T(8,128)}, bf16[32,3584]{1,0:T(8,128)(2,1)}, bf16[32,3584]{1,0:T(8,128)(2,1)}) custom-call(s32[512,1]{1,0:T(8,128)} %get-tuple-element.27.code_ref, f32[32,3584]{1,0:T(8,128)} %w_ref.2, f32[32,3584]{1,0:T(8,128)} %m_ref.2, f32[32,3584]{1,0:T(8,128)} %v_ref.2, ...), custom_call_target="tpu_custom_call" | custom-call | flops 4587520 | bytes 4587520 | tf_op jit(solution)/shard_map/enc_update/pallas_call | solution.py:235
  124.1 7.2 %collective-permute-done.24.refs_6_ = bf16[32,1792]{1,0:T(8,128)(2,1)S(1)} collective-permute-done((bf16[32,1792]{1,0:T(8,128)(2,1)S(1)}, bf16[32,1792]{1,0:T(8,128)(2,1)S(1)}, u32[]{:S(2)}, u32[]{:S(2)}) %collective-permute-start.24) | collective-permute-done | bytes 114720 | tf_op jit(solution)/shard_map/ppermute | solution.py:37
  132.1 3.1 %dec_update.1 = (f32[32,3584]{1,0:T(8,128)}, f32[32,3584]{1,0:T(8,128)}, f32[32,3584]{1,0:T(8,128)}, bf16[32,3584]{1,0:T(8,128)(2,1)}) custom-call(s32[512,1]{1,0:T(8,128)} %get-tuple-element.27.code_ref, f32[32,3584]{1,0:T(8,128)} %w_ref.3, f32[32,3584]{1,0:T(8,128)} %m_ref.3, f32[32,3584]{1,0:T(8,128)} %v_ref.3, ...), custom_call_target="tpu_custom_call" | custom-call | flops 4587520 | bytes 4587520 | tf_op jit(solution)/shard_map/dec_update/pallas_call | solution.py:235
  136.9 10.6 %collective-permute-done.29.refs_2_ = bf16[32,3584]{1,0:T(8,128)(2,1)} collective-permute-done((bf16[32,3584]{1,0:T(8,128)(2,1)}, bf16[32,3584]{1,0:T(8,128)(2,1)}, u32[]{:S(2)}, u32[]{:S(2)}) %collective-permute-start.29) | collective-permute-done | bytes 229408 | tf_op jit(solution)/shard_map/ppermute | solution.py:37
  147.5 3.3 %collective-permute-start.42 = (bf16[32,3584]{1,0:T(8,128)(2,1)}, bf16[32,3584]{1,0:T(8,128)(2,1)S(1)}, u32[]{:S(2)}, u32[]{:S(2)}) collective-permute-start(bf16[32,3584]{1,0:T(8,128)(2,1)} %get-tuple-element.45.refs_0_), channel_id=1, source_target_pairs={{0,4},{1,5},{2,6},{3,7},{4,0},{5,1},{6,2},{7,3},{8,12},{9,13},{10,... | collective-permute-start | bytes 688136 | tf_op jit(solution)/shard_map/ppermute | solution.py:37
  151.3 2.9 %collective-permute-start.39 = (bf16[32,3584]{1,0:T(8,128)(2,1)S(1)}, bf16[32,3584]{1,0:T(8,128)(2,1)}, u32[]{:S(2)}, u32[]{:S(2)}) collective-permute-start(bf16[32,3584]{1,0:T(8,128)(2,1)S(1)} %collective-permute-done.31.refs_3_), channel_id=1, source_target_pairs={{0,2},{1,3},{2,0},{3,1},{4,6},{5,7},{6,4},{7,5},{8,10},{9,11},{10,... | collective-permute-start | bytes 688136 | tf_op jit(solution)/shard_map/ppermute | solution.py:37
  154.3 6.9 %collective-permute-done.44.refs_2_ = bf16[32,3584]{1,0:T(8,128)(2,1)S(1)} collective-permute-done((bf16[32,3584]{1,0:T(8,128)(2,1)}, bf16[32,3584]{1,0:T(8,128)(2,1)S(1)}, u32[]{:S(2)}, u32[]{:S(2)}) %collective-permute-start.44) | collective-permute-done | bytes 229408 | tf_op jit(solution)/shard_map/ppermute | solution.py:37
  164.3 5.7 %collective-permute-done.37.refs_6_ = bf16[32,3584]{1,0:T(8,128)(2,1)} collective-permute-done((bf16[32,3584]{1,0:T(8,128)(2,1)}, bf16[32,3584]{1,0:T(8,128)(2,1)}, u32[]{:S(2)}, u32[]{:S(2)}) %collective-permute-start.37) | collective-permute-done | bytes 229408 | tf_op jit(solution)/shard_map/ppermute | solution.py:37
  170.6 4.2 %collective-permute-done.35.refs_5_ = bf16[32,3584]{1,0:T(8,128)(2,1)} collective-permute-done((bf16[32,3584]{1,0:T(8,128)(2,1)}, bf16[32,3584]{1,0:T(8,128)(2,1)}, u32[]{:S(2)}, u32[]{:S(2)}) %collective-permute-start.35) | collective-permute-done | bytes 229408 | tf_op jit(solution)/shard_map/ppermute | solution.py:37
  175.6 4.1 %collective-permute-done.54.refs_7_ = bf16[32,3584]{1,0:T(8,128)(2,1)S(1)} collective-permute-done((bf16[32,3584]{1,0:T(8,128)(2,1)S(1)}, bf16[32,3584]{1,0:T(8,128)(2,1)S(1)}, u32[]{:S(2)}, u32[]{:S(2)}) %collective-permute-start.54) | collective-permute-done | bytes 229408 | tf_op jit(solution)/shard_map/ppermute | solution.py:37
  180.2 4.4 %collective-permute-done.52.refs_6_ = bf16[32,3584]{1,0:T(8,128)(2,1)S(1)} collective-permute-done((bf16[32,3584]{1,0:T(8,128)(2,1)S(1)}, bf16[32,3584]{1,0:T(8,128)(2,1)S(1)}, u32[]{:S(2)}, u32[]{:S(2)}) %collective-permute-start.52) | collective-permute-done | bytes 229408 | tf_op jit(solution)/shard_map/ppermute | solution.py:37
  184.6 4.5 %collective-permute-done.50.refs_5_ = bf16[32,3584]{1,0:T(8,128)(2,1)S(1)} collective-permute-done((bf16[32,3584]{1,0:T(8,128)(2,1)S(1)}, bf16[32,3584]{1,0:T(8,128)(2,1)S(1)}, u32[]{:S(2)}, u32[]{:S(2)}) %collective-permute-start.50) | collective-permute-done | bytes 229408 | tf_op jit(solution)/shard_map/ppermute | solution.py:37
  195.9 2.4 %place.7 = bf16[512,3584]{1,0:T(8,128)(2,1)} custom-call(bf16[32,3584]{1,0:T(8,128)(2,1)} %copy-done.7, bf16[32,3584]{1,0:T(8,128)(2,1)} %copy-done.12, bf16[32,3584]{1,0:T(8,128)(2,1)} %copy-done.10, bf16[32,3584]{1,0:T(8,128)(2,1)} %copy-done.9, bf16[32,3584]{1,0:T(8,128)(2,1)} %copy-done.8, ...), custom_call_target="tpu_custom_call", output_to_operand_aliasing={{}: (8, {})} | custom-call | bytes 3670016 | tf_op jit(solution)/shard_map/place/pallas_call | solution.py:277
  (191 shorter events, 42.6 us)
Async XLA Ops:
  11.0 39.0 %collective-permute-start.16 = (bf16[256,1792]{1,0:T(8,128)(2,1)}, bf16[256,1792]{1,0:T(8,128)(2,1)S(1)}, u32[]{:S(2)}, u32[]{:S(2)}) collective-permute-start(bf16[256,1792]{1,0:T(8,128)(2,1)} %get-tuple-element.38), channel_id=1, source_target_pairs={{0,1},{1,0},{2,3},{3,2},{4,5},{5,4},{6,7},{7,6},{8,9},{9,8},{10,11... | collective-permute-start | bytes 2752520 | tf_op jit(solution)/shard_map/ppermute | solution.py:37
  29.6 20.9 %collective-permute-start.21 = (bf16[256,1792]{1,0:T(8,128)(2,1)}, bf16[256,1792]{1,0:T(8,128)(2,1)}, u32[]{:S(2)}, u32[]{:S(2)}) collective-permute-start(bf16[256,1792]{1,0:T(8,128)(2,1)} %get-tuple-element.40), channel_id=1, source_target_pairs={{0,1},{1,0},{2,3},{3,2},{4,5},{5,4},{6,7},{7,6},{8,9},{9,8},{10,11... | collective-permute-start | bytes 2752520 | tf_op jit(solution)/shard_map/ppermute | solution.py:37
  50.1 13.4 %collective-permute-start.17 = (bf16[128,1792]{1,0:T(8,128)(2,1)S(1)}, bf16[128,1792]{1,0:T(8,128)(2,1)S(1)}, u32[]{:S(2)}, u32[]{:S(2)}) collective-permute-start(bf16[128,1792]{1,0:T(8,128)(2,1)S(1)} %add_convert_fusion.3), channel_id=1, source_target_pairs={{0,2},{1,3},{2,0},{3,1},{4,6},{5,7},{6,4},{7,5},{8,10},{9,11},{10,... | collective-permute-start | bytes 1376264 | tf_op jit(solution)/shard_map/ppermute | solution.py:37
  51.7 21.7 %collective-permute-start.22 = (bf16[128,1792]{1,0:T(8,128)(2,1)S(1)}, bf16[128,1792]{1,0:T(8,128)(2,1)S(1)}, u32[]{:S(2)}, u32[]{:S(2)}) collective-permute-start(bf16[128,1792]{1,0:T(8,128)(2,1)S(1)} %add_convert_fusion.1), channel_id=1, source_target_pairs={{0,2},{1,3},{2,0},{3,1},{4,6},{5,7},{6,4},{7,5},{8,10},{9,11},{10,... | collective-permute-start | bytes 1376264 | tf_op jit(solution)/shard_map/ppermute | solution.py:37
  54.8 28.4 %collective-permute-start.7 = (bf16[128,1792]{1,0:T(8,128)(2,1)S(1)}, bf16[128,1792]{1,0:T(8,128)(2,1)S(1)}, u32[]{:S(2)}, u32[]{:S(2)}) collective-permute-start(bf16[128,1792]{1,0:T(8,128)(2,1)S(1)} %add_convert_fusion.7), channel_id=1, source_target_pairs={{0,2},{1,3},{2,0},{3,1},{4,6},{5,7},{6,4},{7,5},{8,10},{9,11},{10,... | collective-permute-start | bytes 1376264 | tf_op jit(solution)/shard_map/ppermute | solution.py:37
  55.3 37.2 %collective-permute-start.12 = (bf16[128,1792]{1,0:T(8,128)(2,1)S(1)}, bf16[128,1792]{1,0:T(8,128)(2,1)S(1)}, u32[]{:S(2)}, u32[]{:S(2)}) collective-permute-start(bf16[128,1792]{1,0:T(8,128)(2,1)S(1)} %add_convert_fusion.5), channel_id=1, source_target_pairs={{0,2},{1,3},{2,0},{3,1},{4,6},{5,7},{6,4},{7,5},{8,10},{9,11},{10,... | collective-permute-start | bytes 1376264 | tf_op jit(solution)/shard_map/ppermute | solution.py:37
  64.4 32.5 %collective-permute-start.20 = (bf16[32,1792]{1,0:T(8,128)(2,1)S(1)}, bf16[32,1792]{1,0:T(8,128)(2,1)S(1)}, u32[]{:S(2)}, u32[]{:S(2)}) collective-permute-start(bf16[32,1792]{1,0:T(8,128)(2,1)S(1)} %get-tuple-element.50), channel_id=1, source_target_pairs={{0,12},{1,13},{2,14},{3,15},{4,8},{5,9},{6,10},{7,11},{8,4},{9,5},... | collective-permute-start | bytes 344072 | tf_op jit(solution)/shard_map/ppermute | solution.py:37
  88.7 13.7 %collective-permute-start.9 = (bf16[32,1792]{1,0:T(8,128)(2,1)S(1)}, bf16[32,1792]{1,0:T(8,128)(2,1)S(1)}, u32[]{:S(2)}, u32[]{:S(2)}) collective-permute-start(bf16[32,1792]{1,0:T(8,128)(2,1)S(1)} %get-tuple-element.59), channel_id=1, source_target_pairs={{0,8},{1,9},{2,10},{3,11},{4,12},{5,13},{6,14},{7,15},{8,0},{9,1},... | collective-permute-start | bytes 344072 | tf_op jit(solution)/shard_map/ppermute | solution.py:37
  88.7 13.7 %collective-permute-start.8 = (bf16[32,1792]{1,0:T(8,128)(2,1)S(1)}, bf16[32,1792]{1,0:T(8,128)(2,1)S(1)}, u32[]{:S(2)}, u32[]{:S(2)}) collective-permute-start(bf16[32,1792]{1,0:T(8,128)(2,1)S(1)} %get-tuple-element.60), channel_id=1, source_target_pairs={{0,4},{1,5},{2,6},{3,7},{4,0},{5,1},{6,2},{7,3},{8,12},{9,13},{10,... | collective-permute-start | bytes 344072 | tf_op jit(solution)/shard_map/ppermute | solution.py:37
  96.9 17.3 %collective-permute-start.14 = (bf16[32,1792]{1,0:T(8,128)(2,1)S(1)}, bf16[32,1792]{1,0:T(8,128)(2,1)S(1)}, u32[]{:S(2)}, u32[]{:S(2)}) collective-permute-start(bf16[32,1792]{1,0:T(8,128)(2,1)S(1)} %get-tuple-element.55), channel_id=1, source_target_pairs={{0,8},{1,9},{2,10},{3,11},{4,12},{5,13},{6,14},{7,15},{8,0},{9,1},... | collective-permute-start | bytes 344072 | tf_op jit(solution)/shard_map/ppermute | solution.py:37
  97.0 17.2 %collective-permute-start.13 = (bf16[32,1792]{1,0:T(8,128)(2,1)S(1)}, bf16[32,1792]{1,0:T(8,128)(2,1)S(1)}, u32[]{:S(2)}, u32[]{:S(2)}) collective-permute-start(bf16[32,1792]{1,0:T(8,128)(2,1)S(1)} %get-tuple-element.56), channel_id=1, source_target_pairs={{0,4},{1,5},{2,6},{3,7},{4,0},{5,1},{6,2},{7,3},{8,12},{9,13},{10,... | collective-permute-start | bytes 344072 | tf_op jit(solution)/shard_map/ppermute | solution.py:37
  102.4 18.1 %collective-permute-start.19 = (bf16[32,1792]{1,0:T(8,128)(2,1)S(1)}, bf16[32,1792]{1,0:T(8,128)(2,1)S(1)}, u32[]{:S(2)}, u32[]{:S(2)}) collective-permute-start(bf16[32,1792]{1,0:T(8,128)(2,1)S(1)} %get-tuple-element.51), channel_id=1, source_target_pairs={{0,8},{1,9},{2,10},{3,11},{4,12},{5,13},{6,14},{7,15},{8,0},{9,1},... | collective-permute-start | bytes 344072 | tf_op jit(solution)/shard_map/ppermute | solution.py:37
  102.4 18.6 %collective-permute-start.18 = (bf16[32,1792]{1,0:T(8,128)(2,1)S(1)}, bf16[32,1792]{1,0:T(8,128)(2,1)S(1)}, u32[]{:S(2)}, u32[]{:S(2)}) collective-permute-start(bf16[32,1792]{1,0:T(8,128)(2,1)S(1)} %get-tuple-element.52), channel_id=1, source_target_pairs={{0,4},{1,5},{2,6},{3,7},{4,0},{5,1},{6,2},{7,3},{8,12},{9,13},{10,... | collective-permute-start | bytes 344072 | tf_op jit(solution)/shard_map/ppermute | solution.py:37
  102.6 19.7 %collective-permute-start.25 = (bf16[32,1792]{1,0:T(8,128)(2,1)S(1)}, bf16[32,1792]{1,0:T(8,128)(2,1)S(1)}, u32[]{:S(2)}, u32[]{:S(2)}) collective-permute-start(bf16[32,1792]{1,0:T(8,128)(2,1)S(1)} %get-tuple-element.46), channel_id=1, source_target_pairs={{0,12},{1,13},{2,14},{3,15},{4,8},{5,9},{6,10},{7,11},{8,4},{9,5},... | collective-permute-start | bytes 344072 | tf_op jit(solution)/shard_map/ppermute | solution.py:37
  114.2 17.2 %collective-permute-start.24 = (bf16[32,1792]{1,0:T(8,128)(2,1)S(1)}, bf16[32,1792]{1,0:T(8,128)(2,1)S(1)}, u32[]{:S(2)}, u32[]{:S(2)}) collective-permute-start(bf16[32,1792]{1,0:T(8,128)(2,1)S(1)} %get-tuple-element.47), channel_id=1, source_target_pairs={{0,8},{1,9},{2,10},{3,11},{4,12},{5,13},{6,14},{7,15},{8,0},{9,1},... | collective-permute-start | bytes 344072 | tf_op jit(solution)/shard_map/ppermute | solution.py:37
  114.2 17.2 %collective-permute-start.23 = (bf16[32,1792]{1,0:T(8,128)(2,1)S(1)}, bf16[32,1792]{1,0:T(8,128)(2,1)S(1)}, u32[]{:S(2)}, u32[]{:S(2)}) collective-permute-start(bf16[32,1792]{1,0:T(8,128)(2,1)S(1)} %get-tuple-element.48), channel_id=1, source_target_pairs={{0,4},{1,5},{2,6},{3,7},{4,0},{5,1},{6,2},{7,3},{8,12},{9,13},{10,... | collective-permute-start | bytes 344072 | tf_op jit(solution)/shard_map/ppermute | solution.py:37
  120.5 14.7 %collective-permute-start.33 = (bf16[32,3584]{1,0:T(8,128)(2,1)}, bf16[32,3584]{1,0:T(8,128)(2,1)S(1)}, u32[]{:S(2)}, u32[]{:S(2)}) collective-permute-start(bf16[32,3584]{1,0:T(8,128)(2,1)} %get-tuple-element.44.refs_0_), channel_id=1, source_target_pairs={{0,2},{1,3},{2,0},{3,1},{4,6},{5,7},{6,4},{7,5},{8,10},{9,11},{10,... | collective-permute-start | bytes 688136 | tf_op jit(solution)/shard_map/ppermute | solution.py:37
  121.1 14.2 %collective-permute-start.31 = (bf16[32,3584]{1,0:T(8,128)(2,1)}, bf16[32,3584]{1,0:T(8,128)(2,1)S(1)}, u32[]{:S(2)}, u32[]{:S(2)}) collective-permute-start(bf16[32,3584]{1,0:T(8,128)(2,1)} %get-tuple-element.44.refs_0_), channel_id=1, source_target_pairs={{0,12},{1,13},{2,14},{3,15},{4,8},{5,9},{6,10},{7,11},{8,4},{9,5},... | collective-permute-start | bytes 688136 | tf_op jit(solution)/shard_map/ppermute | solution.py:37
  122.3 25.2 %collective-permute-start.29 = (bf16[32,3584]{1,0:T(8,128)(2,1)}, bf16[32,3584]{1,0:T(8,128)(2,1)}, u32[]{:S(2)}, u32[]{:S(2)}) collective-permute-start(bf16[32,3584]{1,0:T(8,128)(2,1)} %get-tuple-element.44.refs_0_), channel_id=1, source_target_pairs={{0,8},{1,9},{2,10},{3,11},{4,12},{5,13},{6,14},{7,15},{8,0},{9,1},... | collective-permute-start | bytes 688136 | tf_op jit(solution)/shard_map/ppermute | solution.py:37
  131.4 16.2 %collective-permute-start.27 = (bf16[32,3584]{1,0:T(8,128)(2,1)}, bf16[32,3584]{1,0:T(8,128)(2,1)}, u32[]{:S(2)}, u32[]{:S(2)}) collective-permute-start(bf16[32,3584]{1,0:T(8,128)(2,1)} %get-tuple-element.44.refs_0_), channel_id=1, source_target_pairs={{0,4},{1,5},{2,6},{3,7},{4,0},{5,1},{6,2},{7,3},{8,12},{9,13},{10,... | collective-permute-start | bytes 688136 | tf_op jit(solution)/shard_map/ppermute | solution.py:37
  131.4 19.4 %collective-permute-start.26 = (bf16[32,3584]{1,0:T(8,128)(2,1)}, bf16[32,3584]{1,0:T(8,128)(2,1)S(1)}, u32[]{:S(2)}, u32[]{:S(2)}) collective-permute-start(bf16[32,3584]{1,0:T(8,128)(2,1)} %get-tuple-element.44.refs_0_), channel_id=1, source_target_pairs={{0,1},{1,0},{2,3},{3,2},{4,5},{5,4},{6,7},{7,6},{8,9},{9,8},{10,11... | collective-permute-start | bytes 688136 | tf_op jit(solution)/shard_map/ppermute | solution.py:37
  135.2 15.6 %collective-permute-start.48 = (bf16[32,3584]{1,0:T(8,128)(2,1)}, bf16[32,3584]{1,0:T(8,128)(2,1)S(1)}, u32[]{:S(2)}, u32[]{:S(2)}) collective-permute-start(bf16[32,3584]{1,0:T(8,128)(2,1)} %get-tuple-element.45.refs_0_), channel_id=1, source_target_pairs={{0,2},{1,3},{2,0},{3,1},{4,6},{5,7},{6,4},{7,5},{8,10},{9,11},{10,... | collective-permute-start | bytes 688136 | tf_op jit(solution)/shard_map/ppermute | solution.py:37
  135.3 16.1 %collective-permute-start.46 = (bf16[32,3584]{1,0:T(8,128)(2,1)}, bf16[32,3584]{1,0:T(8,128)(2,1)S(1)}, u32[]{:S(2)}, u32[]{:S(2)}) collective-permute-start(bf16[32,3584]{1,0:T(8,128)(2,1)} %get-tuple-element.45.refs_0_), channel_id=1, source_target_pairs={{0,12},{1,13},{2,14},{3,15},{4,8},{5,9},{6,10},{7,11},{8,4},{9,5},... | collective-permute-start | bytes 688136 | tf_op jit(solution)/shard_map/ppermute | solution.py:37
  147.5 13.7 %collective-permute-start.44 = (bf16[32,3584]{1,0:T(8,128)(2,1)}, bf16[32,3584]{1,0:T(8,128)(2,1)S(1)}, u32[]{:S(2)}, u32[]{:S(2)}) collective-permute-start(bf16[32,3584]{1,0:T(8,128)(2,1)} %get-tuple-element.45.refs_0_), channel_id=1, source_target_pairs={{0,8},{1,9},{2,10},{3,11},{4,12},{5,13},{6,14},{7,15},{8,0},{9,1},... | collective-permute-start | bytes 688136 | tf_op jit(solution)/shard_map/ppermute | solution.py:37
  147.5 13.6 %collective-permute-start.42 = (bf16[32,3584]{1,0:T(8,128)(2,1)}, bf16[32,3584]{1,0:T(8,128)(2,1)S(1)}, u32[]{:S(2)}, u32[]{:S(2)}) collective-permute-start(bf16[32,3584]{1,0:T(8,128)(2,1)} %get-tuple-element.45.refs_0_), channel_id=1, source_target_pairs={{0,4},{1,5},{2,6},{3,7},{4,0},{5,1},{6,2},{7,3},{8,12},{9,13},{10,... | collective-permute-start | bytes 688136 | tf_op jit(solution)/shard_map/ppermute | solution.py:37
  150.8 12.5 %collective-permute-start.34 = (bf16[32,3584]{1,0:T(8,128)(2,1)S(1)}, bf16[32,3584]{1,0:T(8,128)(2,1)S(1)}, u32[]{:S(2)}, u32[]{:S(2)}) collective-permute-start(bf16[32,3584]{1,0:T(8,128)(2,1)S(1)} %collective-permute-done.33.refs_4_), channel_id=1, source_target_pairs={{0,1},{1,0},{2,3},{3,2},{4,5},{5,4},{6,7},{7,6},{8,9},{9,8},{10,11... | collective-permute-start | bytes 688136 | tf_op jit(solution)/shard_map/ppermute | solution.py:37
  161.9 13.0 %collective-permute-start.35 = (bf16[32,3584]{1,0:T(8,128)(2,1)}, bf16[32,3584]{1,0:T(8,128)(2,1)}, u32[]{:S(2)}, u32[]{:S(2)}) collective-permute-start(bf16[32,3584]{1,0:T(8,128)(2,1)} %collective-permute-done.27.refs_1_), channel_id=1, source_target_pairs={{0,2},{1,3},{2,0},{3,1},{4,6},{5,7},{6,4},{7,5},{8,10},{9,11},{10,... | collective-permute-start | bytes 688136 | tf_op jit(solution)/shard_map/ppermute | solution.py:37
  163.4 16.3 %collective-permute-start.54 = (bf16[32,3584]{1,0:T(8,128)(2,1)S(1)}, bf16[32,3584]{1,0:T(8,128)(2,1)S(1)}, u32[]{:S(2)}, u32[]{:S(2)}) collective-permute-start(bf16[32,3584]{1,0:T(8,128)(2,1)S(1)} %collective-permute-done.46.refs_3_), channel_id=1, source_target_pairs={{0,2},{1,3},{2,0},{3,1},{4,6},{5,7},{6,4},{7,5},{8,10},{9,11},{10,... | collective-permute-start | bytes 688136 | tf_op jit(solution)/shard_map/ppermute | solution.py:37
  164.1 15.6 %collective-permute-start.47 = (bf16[32,3584]{1,0:T(8,128)(2,1)S(1)}, bf16[32,3584]{1,0:T(8,128)(2,1)S(1)}, u32[]{:S(2)}, u32[]{:S(2)}) collective-permute-start(bf16[32,3584]{1,0:T(8,128)(2,1)S(1)} %collective-permute-done.46.refs_3_), channel_id=1, source_target_pairs={{0,1},{1,0},{2,3},{3,2},{4,5},{5,4},{6,7},{7,6},{8,9},{9,8},{10,11... | collective-permute-start | bytes 688136 | tf_op jit(solution)/shard_map/ppermute | solution.py:37
  170.0 14.6 %collective-permute-start.52 = (bf16[32,3584]{1,0:T(8,128)(2,1)S(1)}, bf16[32,3584]{1,0:T(8,128)(2,1)S(1)}, u32[]{:S(2)}, u32[]{:S(2)}) collective-permute-start(bf16[32,3584]{1,0:T(8,128)(2,1)S(1)} %collective-permute-done.44.refs_2_), channel_id=1, source_target_pairs={{0,2},{1,3},{2,0},{3,1},{4,6},{5,7},{6,4},{7,5},{8,10},{9,11},{10,... | collective-permute-start | bytes 688136 | tf_op jit(solution)/shard_map/ppermute | solution.py:37
  174.9 14.2 %collective-permute-start.50 = (bf16[32,3584]{1,0:T(8,128)(2,1)S(1)}, bf16[32,3584]{1,0:T(8,128)(2,1)S(1)}, u32[]{:S(2)}, u32[]{:S(2)}) collective-permute-start(bf16[32,3584]{1,0:T(8,128)(2,1)S(1)} %collective-permute-done.42.refs_1_), channel_id=1, source_target_pairs={{0,2},{1,3},{2,0},{3,1},{4,6},{5,7},{6,4},{7,5},{8,10},{9,11},{10,... | collective-permute-start | bytes 688136 | tf_op jit(solution)/shard_map/ppermute | solution.py:37
  175.6 13.5 %collective-permute-start.45 = (bf16[32,3584]{1,0:T(8,128)(2,1)S(1)}, bf16[32,3584]{1,0:T(8,128)(2,1)S(1)}, u32[]{:S(2)}, u32[]{:S(2)}) collective-permute-start(bf16[32,3584]{1,0:T(8,128)(2,1)S(1)} %collective-permute-done.44.refs_2_), channel_id=1, source_target_pairs={{0,1},{1,0},{2,3},{3,2},{4,5},{5,4},{6,7},{7,6},{8,9},{9,8},{10,11... | collective-permute-start | bytes 688136 | tf_op jit(solution)/shard_map/ppermute | solution.py:37
  (66 other events, 822.2 us)

commit v3 on v2

v3 whole, which is shorter than its diff:
```python
import functools

import jax
import jax.numpy as jnp
from jax import lax
from jax.experimental import pallas as pl
from jax.experimental.pallas import tpu as pltpu
from jax.sharding import PartitionSpec as P

beta_one = 0.9
beta_two = 0.99
first_fix = 1.0 - 0.9**4
second_fix = 1.0 - 0.99**4
learn_rate = 0.02
adam_eps = 1e-08
reset_gain = 0.01
norm_eps = 1e-06

KEPT = -1
ABSENT = -2


def adam_update(weight, moment, second, gradient):
    moment_new = beta_one * moment + (1.0 - beta_one) * gradient
    second_new = beta_two * second + (1.0 - beta_two) * gradient * gradient
    weight_new = weight - learn_rate * (moment_new / first_fix) / (
        jnp.sqrt(second_new / second_fix) + adam_eps
    )
    return (weight_new, moment_new, second_new)


def inverse_rms(value):
    return lax.rsqrt(jnp.mean(value * value, axis=1, keepdims=True) + norm_eps)


def swap(value, bits, size):
    return lax.ppermute(value, "latent", [(i, i ^ bits) for i in range(size)])


def cost(flops, moved):
    return pl.CostEstimate(flops=int(flops), bytes_accessed=int(moved), transcendentals=0)


def chip_at(position, chips):
    return jnp.where(position < chips // 2, 2 * position, 2 * (chips - 1 - position) + 1)


def position_of(chip, chips):
    return jnp.where(chip % 2 == 0, chip // 2, chips - 1 - chip // 2)


def owner_at(offset, other_core, size):
    me = lax.axis_index("latent")
    chips = size // 2
    position = lax.rem(position_of(me // 2, chips) + offset + chips, chips)
    return 2 * chip_at(position, chips) + ((me % 2) ^ other_core)


def shift(value, step, size):
    chips = size // 2
    ring = [2 * q for q in range(chips // 2)] + [2 * q + 1 for q in reversed(range(chips // 2))]
    pairs = [
        (2 * ring[p] + core, 2 * ring[(p + step) % chips] + core)
        for p in range(chips)
        for core in range(2)
    ]
    return lax.ppermute(value, "latent", pairs)


def slot_offset(slot, chips):
    far = chips // 2 - slot // 2
    return jnp.where(slot % 2 == 0, far, 1 - far)


def gather_table(row, size):
    table = row
    step = 1
    while step < size:
        near = [table]
        for k in range(1, 4 if step * 2 < size else 2):
            near.append(swap(table, step * k, size))
        table = jnp.concatenate(near, axis=0)
        step *= len(near)
    return table


def ordered_coef(coef, wanted):
    latents = coef.shape[1]
    columns = lax.broadcasted_iota(jnp.int32, (latents, latents), 1)
    pick = (wanted == columns).astype(coef.dtype)
    return lax.dot_general(
        pick, coef, (((1,), (1,)), ((), ())), preferred_element_type=jnp.float32
    ).astype(coef.dtype)


def slot_rows(size, rows):
    chips = size // 2
    row = lax.broadcasted_iota(jnp.int32, (size * rows, 1), 0)
    block = row // rows
    group, inside = block // chips, block % chips
    slot = group * (chips // 2) + inside % (chips // 2)
    other_core = 1 - inside // (chips // 2)
    return owner_at(slot_offset(slot, chips), other_core, size), row % rows


def order_kernel(size, rows, coef_ref, out_ref):
    owner, local = slot_rows(size, rows)
    out_ref[...] = ordered_coef(coef_ref[...], owner * rows + local)


def select_kernel(size, rows, table_ref, picks_ref, coef_ref, out_ref, code_ref):
    me = lax.axis_index("latent")
    cap = picks_ref.shape[0]
    owner, local = slot_rows(size, rows)
    counts = table_ref[:, :size]
    order = table_ref[:, size:]
    source = me ^ lax.broadcasted_iota(jnp.int32, (size, 1), 0)
    before = jnp.sum(jnp.where(source < me, counts, 0), axis=0, keepdims=True)
    total = jnp.sum(counts, axis=0, keepdims=True)
    owners = lax.broadcasted_iota(jnp.int32, (size, size), 1) == source

    def by_key(row):
        return jnp.sum(jnp.where(owners, row, 0), axis=1, keepdims=True)

    begin, here = by_key(before), by_key(counts[:1])
    place = lax.broadcasted_iota(jnp.int32, (size, rows), 1)
    token = jnp.full((size, rows), ABSENT, jnp.int32)
    for c in range(cap):
        own = (place == begin + c) & (here > c)
        token = jnp.where(own, by_key(picks_ref[c : c + 1]), token)
    token = jnp.where(place < by_key(total), token, KEPT)
    spread = (lax.broadcasted_iota(jnp.int32, (size * rows, size), 1) == (owner ^ me)).astype(jnp.float32)

    def by_row(table):
        return jnp.dot(
            spread, table.astype(jnp.float32), precision=lax.Precision.HIGHEST
        )

    is_latent = by_row(order) == local.astype(jnp.float32)
    code = jnp.sum(jnp.where(is_latent, by_row(token), 0.0), axis=1, keepdims=True)
    code = (code + jnp.where(code < 0, -0.5, 0.5)).astype(jnp.int32)
    code_ref[...] = code
    ordered = ordered_coef(coef_ref[...], owner * rows + local)
    tokens = lax.broadcasted_iota(jnp.int32, ordered.shape, 1)
    out_ref[...] = jnp.where(code == KEPT, ordered, (tokens == code).astype(ordered.dtype))


def order_call(coef, size, rows):
    tokens, latents = coef.shape
    return pl.pallas_call(
        functools.partial(order_kernel, size, rows),
        out_shape=jax.ShapeDtypeStruct((latents, tokens), coef.dtype),
        cost_estimate=cost(2 * latents * latents * tokens, 4 * latents * tokens),
        name="order",
    )(coef)


def select_call(table, picks, coef, size, rows):
    tokens, latents = coef.shape
    return pl.pallas_call(
        functools.partial(select_kernel, size, rows),
        out_shape=(
            jax.ShapeDtypeStruct((latents, tokens), coef.dtype),
            jax.ShapeDtypeStruct((latents, 1), jnp.int32),
        ),
        cost_estimate=cost(4 * latents * latents * tokens, 4 * latents * tokens),
        name="select",
    )(table, picks, coef)


def product_kernel(left_ref, right_ref, sent_ref, kept_ref):
    half = sent_ref.shape[0]
    out = jnp.dot(left_ref[...], right_ref[...], preferred_element_type=jnp.float32)
    sent_ref[...] = out[:half].astype(sent_ref.dtype)
    kept_ref[...] = out[half:].astype(kept_ref.dtype)


def product(left, right, group):
    latents, tokens = left.shape
    width = right.shape[1]
    tile = 896
    half = latents // 4
    out = jax.ShapeDtypeStruct((half, width), left.dtype)
    return pl.pallas_call(
        product_kernel,
        grid=(width // tile,),
        in_specs=[
            pl.BlockSpec((2 * half, tokens), lambda j: (group, 0)),
            pl.BlockSpec((tokens, tile), lambda j: (0, j)),
        ],
        out_specs=(pl.BlockSpec((half, tile), lambda j: (0, j)),) * 2,
        out_shape=(out, out),
        cost_estimate=cost(
            latents * tokens * width, 2 * tokens * width + latents * (tokens + width)
        ),
        name="product",
    )(left, right)


def owned_parts(left, right, rows, size):
    chips = size // 2
    slots = chips // 2
    kept, from_core = [], []
    for group in range(2):
        sent, own = product(left, right, group)
        kept.append(own)
        from_core.append(swap(sent, 1, size))

    def term(slot):
        begin = slot % slots * rows
        return sum(
            half[slot // slots][begin : begin + rows].astype(jnp.float32)
            for half in (kept, from_core)
        )

    def travel(first, step):
        moving = term(first).astype(jnp.bfloat16)
        for slot in range(first + 2, chips - 1, 2):
            came = shift(moving, step, size).astype(jnp.float32)
            moving = (came + term(slot)).astype(jnp.bfloat16)
        return shift(moving, step, size)

    return [kept[1], from_core[1], travel(0, 1), travel(1, -1)]


def read_gradient(refs):
    return sum(ref[...].astype(jnp.float32) for ref in refs)


def enc_kernel(code_ref, w_ref, m_ref, v_ref, *refs):
    parts, (w_out, m_out, v_out, block, fresh) = refs[:-5], refs[-5:]
    gradient = read_gradient(parts)
    reset = code_ref[...] != KEPT
    w, m, v = adam_update(w_ref[...], m_ref[...], v_ref[...], gradient)
    w = jnp.where(reset, reset_gain * gradient * inverse_rms(gradient), w)
    w_out[...] = w
    m_out[...] = jnp.where(reset, 0.0, m)
    v_out[...] = jnp.where(reset, 0.0, v)
    block[...] = w.astype(block.dtype)
    fresh[...] = gradient.astype(fresh.dtype)


def dec_kernel(code_ref, w_ref, m_ref, v_ref, fresh_ref, *refs):
    parts, (w_out, m_out, v_out, block) = refs[:-4], refs[-4:]
    reset = code_ref[...] != KEPT
    w, m, v = adam_update(w_ref[...], m_ref[...], v_ref[...], read_gradient(parts))
    w = jnp.where(reset, fresh_ref[...].astype(jnp.float32), w)
    w = w * inverse_rms(w)
    w_out[...] = w
    m_out[...] = jnp.where(reset, 0.0, m)
    v_out[...] = jnp.where(reset, 0.0, v)
    block[...] = w.astype(block.dtype)


def update(kernel, code, states, fresh, parts, extra, name):
    rows, width = states[0].shape
    tile = 16

    def last_rows(value):
        skipped = (value.shape[0] - rows) // tile
        return pl.BlockSpec((tile, value.shape[1]), lambda i: (i + skipped, 0))

    operands = [code] + list(states) + list(fresh) + list(parts)
    out_spec = pl.BlockSpec((tile, width), lambda i: (i, 0))
    wide = jax.ShapeDtypeStruct((rows, width), jnp.float32)
    narrow = jax.ShapeDtypeStruct((rows, width), jnp.bfloat16)
    return pl.pallas_call(
        kernel,
        grid=(rows // tile,),
        in_specs=[last_rows(value) for value in operands],
        out_specs=(out_spec,) * (3 + extra),
        out_shape=(wide,) * 3 + (narrow,) * extra,
        cost_estimate=cost(40 * rows * width, 40 * rows * width),
        name=name,
    )(*operands)


def place_kernel(owners, size, rows, *refs):
    count = len(owners)
    pieces, (whole, sems) = refs[:count], refs[-2:]
    copies = []
    for i, (offset, other_core) in enumerate(owners):
        start = pl.multiple_of(owner_at(offset, other_core, size) * rows, rows)
        copies.append(
            pltpu.make_async_copy(pieces[i], whole.at[pl.ds(start, rows)], sems.at[i])
        )
    for copy in copies:
        copy.start()
    for copy in copies:
        copy.wait()


def place(pieces, other_core, size, prior=None):
    owners = [(offset, other_core) for offset, _ in pieces]
    blocks = [block for _, block in pieces]
    rows, width = blocks[0].shape
    dtype = blocks[0].dtype
    count = len(blocks)
    in_specs = [pl.BlockSpec(memory_space=pltpu.VMEM)] * count
    if prior is not None:
        in_specs.append(pl.BlockSpec(memory_space=pl.ANY))
    return pl.pallas_call(
        functools.partial(place_kernel, owners, size, rows),
        out_shape=jax.ShapeDtypeStruct((size * rows, width), dtype),
        in_specs=in_specs,
        out_specs=pl.BlockSpec(memory_space=pl.ANY),
        scratch_shapes=[pltpu.SemaphoreType.DMA((count,))],
        input_output_aliases={} if prior is None else {count: 0},
        cost_estimate=cost(0, 4 * count * rows * width),
        name="place",
    )(*blocks, *([] if prior is None else [prior]))


def gathered(block, size):
    chips = size // 2
    near = [(0, block)]
    for step, hops in ((1, chips // 2), (-1, (chips - 1) // 2)):
        moving = block
        for hop in range(1, hops + 1):
            moving = shift(moving, step, size)
            near.append((-step * hop, moving))
    far = [(offset, swap(value, 1, size)) for offset, value in near]
    return place(far, 1, size, place(near, 0, size))


def shards(
    x_rows,
    out_grad,
    enc_coef,
    latent_act,
    enc_w,
    enc_m,
    enc_v,
    dec_w,
    dec_m,
    dec_v,
    dead_order,
    pick_rows,
    send_count,
):
    rows = enc_w.shape[0]
    size = lax.axis_size("latent")
    table = gather_table(jnp.concatenate([send_count, dead_order], axis=1), size)
    dec_parts = owned_parts(order_call(latent_act, size, rows), out_grad, rows, size)
    enc_left, code = select_call(table, pick_rows[0].T, enc_coef, size, rows)
    enc_parts = owned_parts(enc_left, x_rows, rows, size)
    enc_out, enc_mo, enc_vo, enc_block, fresh = update(
        enc_kernel, code, (enc_w, enc_m, enc_v), (), enc_parts, 2, "enc_update"
    )
    enc_full = gathered(enc_block, size)
    dec_out, dec_mo, dec_vo, dec_block = update(
        dec_kernel, code, (dec_w, dec_m, dec_v), (fresh,), dec_parts, 1, "dec_update"
    )
    dec_full = gathered(dec_block, size)
    return (enc_out, enc_mo, enc_vo, dec_out, dec_mo, dec_vo, enc_full, dec_full)


def solution(mesh):
    split = P(("groups", "latent"), None)
    placed = (split,) * 11 + (P(("groups", "latent"), None, None), split)
    return jax.shard_map(
        shards,
        mesh=mesh,
        in_specs=placed,
        out_specs=(split,) * 6 + (P("groups", None),) * 2,
        check_vma=False,
    )
```

time: 203 us -> 159 us (0.78)
  waiting for transfers between devices: 86.2 us -> 57.4 us
  starting transfers between devices: 51.2 us -> 39.3 us
    ppermute x56 -> x26, waiting for transfers between devices: 86.2 us -> 6.62 us  [swap(): return lax.ppermute(value, 'latent', [(i, i ^ bits) for i in range(size)])]
    ppermute x0 -> x28, waiting for transfers between devices: none -> 50.8 us  [shift(): return lax.ppermute(value, 'latent', pairs)]
    ppermute x56 -> x26, starting transfers between devices: 51.2 us -> 10.9 us  [swap(): return lax.ppermute(value, 'latent', [(i, i ^ bits) for i in range(size)])]
    ppermute x0 -> x28, starting transfers between devices: none -> 28.4 us  [shift(): return lax.ppermute(value, 'latent', pairs)]
    pallas_call x4, Pallas kernels: 29.7 us -> 25.4 us  [product(): pl.pallas_call(product_kernel, grid=(width // tile,), in_specs=[pl.BlockS...]
    slice x4 -> x0, local copies, waits for them, and re-layouts: 2.7 us -> none  [chunk_parts(): parts = [total[k * rows:(k + 1) * rows] for k in range(depth)]]
  transfers between devices with their start and end apart: 56 -> 54, of which waited for: 18 -> 20; matrix products, arithmetic and copies ran while one was open for 5% -> 3% of each run, Pallas kernels for 19% -> 23%
where the time goes in v3:
time: 159 us
  waiting for transfers between devices  57.4 us (36%)
  Pallas kernels  50.3 us (32%)
  starting transfers between devices  39.3 us (25%)
  other arithmetic  6.83 us (4%)
  local copies, waits for them, and re-layouts  3.62 us (2%)
    ppermute x28, waiting for transfers between devices, shift(): return lax.ppermute(value, 'latent', pairs)  50.8 us
    ppermute x28, starting transfers between devices, shift(): return lax.ppermute(value, 'latent', pairs)  28.4 us
    pallas_call x4, Pallas kernels, product(): pl.pallas_call(product_kernel, grid=(width // tile,), in_specs=[pl.BlockS...  25.4 us
    pallas_call x4, Pallas kernels, place(): pl.pallas_call(functools.partial(place_kernel, owners, size, rows), out_s...  11.4 us
    ppermute x26, starting transfers between devices, swap(): return lax.ppermute(value, 'latent', [(i, i ^ bits) for i in range(size)])  10.9 us
    ppermute x26, waiting for transfers between devices, swap(): return lax.ppermute(value, 'latent', [(i, i ^ bits) for i in range(size)])  6.62 us
    pallas_call x2, Pallas kernels, update(): pl.pallas_call(kernel, grid=(rows // tile,), in_specs=[last_rows(value) f...  6.3 us
    pallas_call x1, Pallas kernels, select_call(): pl.pallas_call(functools.partial(select_kernel, size, rows), out_shape=(j...  3.97 us
  transfers between devices with their start and end apart: 54, of which 20 were waited for; matrix products, arithmetic and copies ran while one was open for 3% of the time, Pallas kernels for 23%

profile of v3, /device:TPU:0, one launch (start us, length us, event | category | flops | bytes accessed | tf_op | source)
XLA Modules:
  0.0 158.6 jit_solution(16615081263297889667)
XLA Ops:
  1.4 2.4 %collective-permute-start.2 = (s32[1,48]{1,0:T(1,128)S(1)}, s32[1,48]{1,0:T(1,128)S(1)}, u32[]{:S(2)}, u32[]{:S(2)}) collective-permute-start(s32[1,48]{1,0:T(1,128)S(1)} %pad_add_fusion.1), channel_id=1, source_target_pairs={{0,3},{1,2},{2,1},{3,0},{4,7},{5,6},{6,5},{7,4},{8,11},{9,10},{10,... | collective-permute-start | bytes 584 | tf_op jit(solution)/shard_map/ppermute | solution.py:37
  5.1 2.2 %collective-permute-done.1 = s32[1,48]{1,0:T(1,128)S(1)} collective-permute-done((s32[1,48]{1,0:T(1,128)S(1)}, s32[1,48]{1,0:T(1,128)S(1)}, u32[]{:S(2)}, u32[]{:S(2)}) %collective-permute-start.1) | collective-permute-done | bytes 224 | tf_op jit(solution)/shard_map/ppermute | solution.py:37
  8.1 3.6 %collective-permute-start.5 = (s32[4,48]{1,0:T(4,128)S(1)}, s32[4,48]{1,0:T(4,128)S(1)}, u32[]{:S(2)}, u32[]{:S(2)}) collective-permute-start(s32[4,48]{1,0:T(4,128)S(1)} %pad_add_fusion), channel_id=1, source_target_pairs={{0,12},{1,13},{2,14},{3,15},{4,8},{5,9},{6,10},{7,11},{8,4},{9,5},... | collective-permute-start | bytes 2312 | tf_op jit(solution)/shard_map/ppermute | solution.py:37
  13.5 2.7 %collective-permute-done.4 = s32[4,48]{1,0:T(4,128)S(1)} collective-permute-done((s32[4,48]{1,0:T(4,128)S(1)}, s32[4,48]{1,0:T(4,128)S(1)}, u32[]{:S(2)}, u32[]{:S(2)}) %collective-permute-start.4) | collective-permute-done | bytes 800 | tf_op jit(solution)/shard_map/ppermute | solution.py:37
  17.4 4.0 %select.1 = (bf16[512,1024]{1,0:T(8,128)(2,1)}, s32[512,1]{1,0:T(8,128)}) custom-call(s32[16,48]{1,0:T(8,128)} %concatenate.12.table_ref, s32[2,16]{1,0:T(2,128)} %bitcast.3, bf16[1024,512]{1,0:T(8,128)(2,1)} %coef_ref.2), custom_call_target="tpu_custom_call" | custom-call | flops 1073741824 | bytes 2097152 | tf_op jit(solution)/shard_map/select/pallas_call | solution.py:160
  21.4 6.3 %product.5 = (bf16[128,3584]{1,0:T(8,128)(2,1)}, bf16[128,3584]{1,0:T(8,128)(2,1)}) custom-call(bf16[512,1024]{1,0:T(8,128)(2,1)} %get-tuple-element.28.left_ref, bf16[1024,3584]{1,0:T(8,128)(2,1)} %right_ref.5), custom_call_target="tpu_custom_call" | custom-call | flops 1879048192 | bytes 9699328 | tf_op jit(solution)/shard_map/product/pallas_call | solution.py:184
  27.7 3.3 %order.1.left_ref = bf16[512,1024]{1,0:T(8,128)(2,1)} custom-call(bf16[1024,512]{1,0:T(8,128)(2,1)} %coef_ref.3), custom_call_target="tpu_custom_call" | custom-call | flops 536870912 | bytes 2097152 | tf_op jit(solution)/shard_map/order/pallas_call | solution.py:150
  31.0 6.3 %product.6 = (bf16[128,3584]{1,0:T(8,128)(2,1)}, bf16[128,3584]{1,0:T(8,128)(2,1)}) custom-call(bf16[512,1024]{1,0:T(8,128)(2,1)} %order.1.left_ref, bf16[1024,3584]{1,0:T(8,128)(2,1)} %right_ref.7), custom_call_target="tpu_custom_call" | custom-call | flops 1879048192 | bytes 9699328 | tf_op jit(solution)/shard_map/product/pallas_call | solution.py:184
  37.8 6.3 %product.7 = (bf16[128,3584]{1,0:T(8,128)(2,1)}, bf16[128,3584]{1,0:T(8,128)(2,1)}) custom-call(bf16[512,1024]{1,0:T(8,128)(2,1)} %order.1.left_ref, bf16[1024,3584]{1,0:T(8,128)(2,1)} %right_ref.7), custom_call_target="tpu_custom_call" | custom-call | flops 1879048192 | bytes 9699328 | tf_op jit(solution)/shard_map/product/pallas_call | solution.py:184
  44.2 6.4 %product.4 = (bf16[128,3584]{1,0:T(8,128)(2,1)}, bf16[128,3584]{1,0:T(8,128)(2,1)}) custom-call(bf16[512,1024]{1,0:T(8,128)(2,1)} %get-tuple-element.28.left_ref, bf16[1024,3584]{1,0:T(8,128)(2,1)} %right_ref.5), custom_call_target="tpu_custom_call" | custom-call | flops 1879048192 | bytes 9699328 | tf_op jit(solution)/shard_map/product/pallas_call | solution.py:184
  56.2 4.6 %collective-permute-done.12 = bf16[32,3584]{1,0:T(8,128)(2,1)S(1)} collective-permute-done((bf16[32,3584]{1,0:T(8,128)(2,1)S(1)}, bf16[32,3584]{1,0:T(8,128)(2,1)S(1)}, u32[]{:S(2)}, u32[]{:S(2)}) %collective-permute-start.12) | collective-permute-done | bytes 229408 | tf_op jit(solution)/shard_map/ppermute | solution.py:67
  62.5 2.1 %collective-permute-start.9 = (bf16[32,3584]{1,0:T(8,128)(2,1)S(1)}, bf16[32,3584]{1,0:T(8,128)(2,1)S(1)}, u32[]{:S(2)}, u32[]{:S(2)}) collective-permute-start(bf16[32,3584]{1,0:T(8,128)(2,1)S(1)} %get-tuple-element.55), channel_id=1, source_target_pairs={{0,4},{1,5},{4,8},{5,9},{8,12},{9,13},{12,14},{13,15},{14,10},{15,... | collective-permute-start | bytes 688136 | tf_op jit(solution)/shard_map/ppermute | solution.py:67
  64.9 4.4 %collective-permute-done.17 = bf16[32,3584]{1,0:T(8,128)(2,1)S(1)} collective-permute-done((bf16[32,3584]{1,0:T(8,128)(2,1)S(1)}, bf16[32,3584]{1,0:T(8,128)(2,1)S(1)}, u32[]{:S(2)}, u32[]{:S(2)}) %collective-permute-start.17) | collective-permute-done | bytes 229408 | tf_op jit(solution)/shard_map/ppermute | solution.py:67
  74.9 4.8 %collective-permute-done.18 = bf16[32,3584]{1,0:T(8,128)(2,1)S(1)} collective-permute-done((bf16[32,3584]{1,0:T(8,128)(2,1)S(1)}, bf16[32,3584]{1,0:T(8,128)(2,1)S(1)}, u32[]{:S(2)}, u32[]{:S(2)}) %collective-permute-start.18) | collective-permute-done | bytes 229408 | tf_op jit(solution)/shard_map/ppermute | solution.py:67
  79.8 1.5 collective-permute-start.19
  81.3 3.3 %collective-permute-done.10 = bf16[32,3584]{1,0:T(8,128)(2,1)S(1)} collective-permute-done((bf16[32,3584]{1,0:T(8,128)(2,1)S(1)}, bf16[32,3584]{1,0:T(8,128)(2,1)S(1)}, u32[]{:S(2)}, u32[]{:S(2)}) %collective-permute-start.10) | collective-permute-done | bytes 229408 | tf_op jit(solution)/shard_map/ppermute | solution.py:67
  86.9 2.7 %collective-permute-done.19 = bf16[32,3584]{1,0:T(8,128)(2,1)S(1)} collective-permute-done((bf16[32,3584]{1,0:T(8,128)(2,1)S(1)}, bf16[32,3584]{1,0:T(8,128)(2,1)S(1)}, u32[]{:S(2)}, u32[]{:S(2)}) %collective-permute-start.19) | collective-permute-done | bytes 229408 | tf_op jit(solution)/shard_map/ppermute | solution.py:67
  91.8 2.0 %collective-permute-done.11.refs_2_ = bf16[32,3584]{1,0:T(8,128)(2,1)S(1)} collective-permute-done((bf16[32,3584]{1,0:T(8,128)(2,1)S(1)}, bf16[32,3584]{1,0:T(8,128)(2,1)S(1)}, u32[]{:S(2)}, u32[]{:S(2)}) %collective-permute-start.11) | collective-permute-done | bytes 229408 | tf_op jit(solution)/shard_map/ppermute | solution.py:67
  94.5 3.1 %enc_update.1 = (f32[32,3584]{1,0:T(8,128)}, f32[32,3584]{1,0:T(8,128)}, f32[32,3584]{1,0:T(8,128)}, bf16[32,3584]{1,0:T(8,128)(2,1)}, bf16[32,3584]{1,0:T(8,128)(2,1)}) custom-call(s32[512,1]{1,0:T(8,128)} %get-tuple-element.27.code_ref, f32[32,3584]{1,0:T(8,128)} %w_ref.2, f32[32,3584]{1,0:T(8,128)} %m_ref.2, f32[32,3584]{1,0:T(8,128)} %v_ref.2, ...), custom_call_target="tpu_custom_call" | custom-call | flops 4587520 | bytes 4587520 | tf_op jit(solution)/shard_map/enc_update/pallas_call | solution.py:267
  100.5 3.2 %dec_update.1 = (f32[32,3584]{1,0:T(8,128)}, f32[32,3584]{1,0:T(8,128)}, f32[32,3584]{1,0:T(8,128)}, bf16[32,3584]{1,0:T(8,128)(2,1)}) custom-call(s32[512,1]{1,0:T(8,128)} %get-tuple-element.27.code_ref, f32[32,3584]{1,0:T(8,128)} %w_ref.3, f32[32,3584]{1,0:T(8,128)} %m_ref.3, f32[32,3584]{1,0:T(8,128)} %v_ref.3, ...), custom_call_target="tpu_custom_call" | custom-call | flops 4587520 | bytes 4587520 | tf_op jit(solution)/shard_map/dec_update/pallas_call | solution.py:267
  106.6 5.7 %collective-permute-done.48.refs_5_ = bf16[32,3584]{1,0:T(8,128)(2,1)S(1)} collective-permute-done((bf16[32,3584]{1,0:T(8,128)(2,1)}, bf16[32,3584]{1,0:T(8,128)(2,1)S(1)}, u32[]{:S(2)}, u32[]{:S(2)}) %collective-permute-start.48) | collective-permute-done | bytes 229408 | tf_op jit(solution)/shard_map/ppermute | solution.py:67
  114.9 2.0 %collective-permute-done.35.refs_6_ = bf16[32,3584]{1,0:T(8,128)(2,1)} collective-permute-done((bf16[32,3584]{1,0:T(8,128)(2,1)S(1)}, bf16[32,3584]{1,0:T(8,128)(2,1)}, u32[]{:S(2)}, u32[]{:S(2)}) %collective-permute-start.35) | collective-permute-done | bytes 229408 | tf_op jit(solution)/shard_map/ppermute | solution.py:67
  117.6 3.4 %collective-permute-done.27.refs_2_ = bf16[32,3584]{1,0:T(8,128)(2,1)} collective-permute-done((bf16[32,3584]{1,0:T(8,128)(2,1)S(1)}, bf16[32,3584]{1,0:T(8,128)(2,1)}, u32[]{:S(2)}, u32[]{:S(2)}) %collective-permute-start.27) | collective-permute-done | bytes 229408 | tf_op jit(solution)/shard_map/ppermute | solution.py:67
  121.0 3.1 %collective-permute-done.42.refs_2_ = bf16[32,3584]{1,0:T(8,128)(2,1)S(1)} collective-permute-done((bf16[32,3584]{1,0:T(8,128)(2,1)S(1)}, bf16[32,3584]{1,0:T(8,128)(2,1)S(1)}, u32[]{:S(2)}, u32[]{:S(2)}) %collective-permute-start.42) | collective-permute-done | bytes 229408 | tf_op jit(solution)/shard_map/ppermute | solution.py:67
  128.3 4.4 %collective-permute-done.44.refs_3_ = bf16[32,3584]{1,0:T(8,128)(2,1)S(1)} collective-permute-done((bf16[32,3584]{1,0:T(8,128)(2,1)S(1)}, bf16[32,3584]{1,0:T(8,128)(2,1)S(1)}, u32[]{:S(2)}, u32[]{:S(2)}) %collective-permute-start.44) | collective-permute-done | bytes 229408 | tf_op jit(solution)/shard_map/ppermute | solution.py:67
  133.8 3.8 %collective-permute-done.29.refs_3_ = bf16[32,3584]{1,0:T(8,128)(2,1)} collective-permute-done((bf16[32,3584]{1,0:T(8,128)(2,1)}, bf16[32,3584]{1,0:T(8,128)(2,1)}, u32[]{:S(2)}, u32[]{:S(2)}) %collective-permute-start.29) | collective-permute-done | bytes 229408 | tf_op jit(solution)/shard_map/ppermute | solution.py:67
  139.2 3.1 %collective-permute-done.46.refs_4_ = bf16[32,3584]{1,0:T(8,128)(2,1)S(1)} collective-permute-done((bf16[32,3584]{1,0:T(8,128)(2,1)S(1)}, bf16[32,3584]{1,0:T(8,128)(2,1)S(1)}, u32[]{:S(2)}, u32[]{:S(2)}) %collective-permute-start.46) | collective-permute-done | bytes 229408 | tf_op jit(solution)/shard_map/ppermute | solution.py:67
  142.9 2.0 %collective-permute-done.31.refs_4_ = bf16[32,3584]{1,0:T(8,128)(2,1)} collective-permute-done((bf16[32,3584]{1,0:T(8,128)(2,1)}, bf16[32,3584]{1,0:T(8,128)(2,1)}, u32[]{:S(2)}, u32[]{:S(2)}) %collective-permute-start.31) | collective-permute-done | bytes 229408 | tf_op jit(solution)/shard_map/ppermute | solution.py:67
  146.2 2.8 %place.6.refs_8_ = bf16[512,3584]{1,0:T(8,128)(2,1)} custom-call(bf16[32,3584]{1,0:T(8,128)(2,1)} %get-tuple-element.45.refs_0_, bf16[32,3584]{1,0:T(8,128)(2,1)} %copy-done.26, bf16[32,3584]{1,0:T(8,128)(2,1)} %copy-done.27, bf16[32,3584]{1,0:T(8,128)(2,1)} %copy-done.29, bf16[32,3584]{1,0:T(8,128)(2,1)} %copy-done.31, bf16[32,3584]{1,0:T(8,128)(2,1)} %copy-done.25, ...), custom_call_target="tpu_custom_call" | custom-call | bytes 3670016 | tf_op jit(solution)/shard_map/place/pallas_call | solution.py:302
  149.0 2.8 %place.4.refs_8_ = bf16[512,3584]{1,0:T(8,128)(2,1)} custom-call(bf16[32,3584]{1,0:T(8,128)(2,1)} %get-tuple-element.44.refs_0_, bf16[32,3584]{1,0:T(8,128)(2,1)} %copy-done.24, bf16[32,3584]{1,0:T(8,128)(2,1)} %collective-permute-done.27.refs_2_, bf16[32,3584]{1,0:T(8,128)(2,1)} %collective-permute-done.29.refs_3_, ...), custom_call_target="tpu_custom_call" | custom-call | bytes 3670016 | tf_op jit(solution)/shard_map/place/pallas_call | solution.py:302
  152.0 2.8 %place.7 = bf16[512,3584]{1,0:T(8,128)(2,1)} custom-call(bf16[32,3584]{1,0:T(8,128)(2,1)} %copy-done.8, bf16[32,3584]{1,0:T(8,128)(2,1)} %copy-done.11, bf16[32,3584]{1,0:T(8,128)(2,1)} %copy-done.13, bf16[32,3584]{1,0:T(8,128)(2,1)} %copy-done.18, bf16[32,3584]{1,0:T(8,128)(2,1)} %copy-done.20, ...), custom_call_target="tpu_custom_call", output_to_operand_aliasing={{}: (8, {})} | custom-call | bytes 3670016 | tf_op jit(solution)/shard_map/place/pallas_call | solution.py:302
  155.8 2.8 %place.5 = bf16[512,3584]{1,0:T(8,128)(2,1)} custom-call(bf16[32,3584]{1,0:T(8,128)(2,1)} %copy-done.6, bf16[32,3584]{1,0:T(8,128)(2,1)} %copy-done.9, bf16[32,3584]{1,0:T(8,128)(2,1)} %copy-done.15, bf16[32,3584]{1,0:T(8,128)(2,1)} %copy-done.17, bf16[32,3584]{1,0:T(8,128)(2,1)} %collective-permute-done.32.refs_4_, ...), custom_call_target="tpu_custom_call", output_to_operand_aliasing={{}: (8, {})} | custom-call | bytes 3670016 | tf_op jit(solution)/shard_map/place/pallas_call | solution.py:302
  (167 shorter events, 43.2 us)
Async XLA Ops:
  27.7 23.3 %collective-permute-start.7 = (bf16[128,3584]{1,0:T(8,128)(2,1)}, bf16[128,3584]{1,0:T(8,128)(2,1)}, u32[]{:S(2)}, u32[]{:S(2)}) collective-permute-start(bf16[128,3584]{1,0:T(8,128)(2,1)} %get-tuple-element.32), channel_id=1, source_target_pairs={{0,1},{1,0},{2,3},{3,2},{4,5},{5,4},{6,7},{7,6},{8,9},{9,8},{10,11... | collective-permute-start | bytes 2752520 | tf_op jit(solution)/shard_map/ppermute | solution.py:37
  37.3 37.6 %collective-permute-start.15 = (bf16[128,3584]{1,0:T(8,128)(2,1)}, bf16[128,3584]{1,0:T(8,128)(2,1)S(1)}, u32[]{:S(2)}, u32[]{:S(2)}) collective-permute-start(bf16[128,3584]{1,0:T(8,128)(2,1)} %get-tuple-element.38), channel_id=1, source_target_pairs={{0,1},{1,0},{2,3},{3,2},{4,5},{5,4},{6,7},{7,6},{8,9},{9,8},{10,11... | collective-permute-start | bytes 2752520 | tf_op jit(solution)/shard_map/ppermute | solution.py:37
  44.2 10.2 %collective-permute-start.16 = (bf16[128,3584]{1,0:T(8,128)(2,1)}, bf16[128,3584]{1,0:T(8,128)(2,1)}, u32[]{:S(2)}, u32[]{:S(2)}) collective-permute-start(bf16[128,3584]{1,0:T(8,128)(2,1)} %get-tuple-element.40), channel_id=1, source_target_pairs={{0,1},{1,0},{2,3},{3,2},{4,5},{5,4},{6,7},{7,6},{8,9},{9,8},{10,11... | collective-permute-start | bytes 2752520 | tf_op jit(solution)/shard_map/ppermute | solution.py:37
  50.6 22.0 %collective-permute-start.6 = (bf16[128,3584]{1,0:T(8,128)(2,1)}, bf16[128,3584]{1,0:T(8,128)(2,1)S(1)}, u32[]{:S(2)}, u32[]{:S(2)}) collective-permute-start(bf16[128,3584]{1,0:T(8,128)(2,1)} %get-tuple-element.30), channel_id=1, source_target_pairs={{0,1},{1,0},{2,3},{3,2},{4,5},{5,4},{6,7},{7,6},{8,9},{9,8},{10,11... | collective-permute-start | bytes 2752520 | tf_op jit(solution)/shard_map/ppermute | solution.py:37
  55.5 9.4 %collective-permute-start.21 = (bf16[32,3584]{1,0:T(8,128)(2,1)S(1)}, bf16[32,3584]{1,0:T(8,128)(2,1)S(1)}, u32[]{:S(2)}, u32[]{:S(2)}) collective-permute-start(bf16[32,3584]{1,0:T(8,128)(2,1)S(1)} %get-tuple-element.50), channel_id=1, source_target_pairs={{0,2},{1,3},{4,0},{5,1},{8,4},{9,5},{12,8},{13,9},{14,12},{15,13},... | collective-permute-start | bytes 688136 | tf_op jit(solution)/shard_map/ppermute | solution.py:67
  62.5 11.7 %collective-permute-start.9 = (bf16[32,3584]{1,0:T(8,128)(2,1)S(1)}, bf16[32,3584]{1,0:T(8,128)(2,1)S(1)}, u32[]{:S(2)}, u32[]{:S(2)}) collective-permute-start(bf16[32,3584]{1,0:T(8,128)(2,1)S(1)} %get-tuple-element.55), channel_id=1, source_target_pairs={{0,4},{1,5},{4,8},{5,9},{8,12},{9,13},{12,14},{13,15},{14,10},{15,... | collective-permute-start | bytes 688136 | tf_op jit(solution)/shard_map/ppermute | solution.py:67
  70.5 16.4 %collective-permute-start.22 = (bf16[32,3584]{1,0:T(8,128)(2,1)S(1)}, bf16[32,3584]{1,0:T(8,128)(2,1)S(1)}, u32[]{:S(2)}, u32[]{:S(2)}) collective-permute-start(bf16[32,3584]{1,0:T(8,128)(2,1)S(1)} %get-tuple-element.48), channel_id=1, source_target_pairs={{0,2},{1,3},{4,0},{5,1},{8,4},{9,5},{12,8},{13,9},{14,12},{15,13},... | collective-permute-start | bytes 688136 | tf_op jit(solution)/shard_map/ppermute | solution.py:67
  71.2 8.5 %collective-permute-start.18 = (bf16[32,3584]{1,0:T(8,128)(2,1)S(1)}, bf16[32,3584]{1,0:T(8,128)(2,1)S(1)}, u32[]{:S(2)}, u32[]{:S(2)}) collective-permute-start(bf16[32,3584]{1,0:T(8,128)(2,1)S(1)} %get-tuple-element.49), channel_id=1, source_target_pairs={{0,4},{1,5},{4,8},{5,9},{8,12},{9,13},{12,14},{13,15},{14,10},{15,... | collective-permute-start | bytes 688136 | tf_op jit(solution)/shard_map/ppermute | solution.py:67
  72.6 8.7 %collective-permute-start.13 = (bf16[32,3584]{1,0:T(8,128)(2,1)S(1)}, bf16[32,3584]{1,0:T(8,128)(2,1)S(1)}, u32[]{:S(2)}, u32[]{:S(2)}) collective-permute-start(bf16[32,3584]{1,0:T(8,128)(2,1)S(1)} %get-tuple-element.54), channel_id=1, source_target_pairs={{0,2},{1,3},{4,0},{5,1},{8,4},{9,5},{12,8},{13,9},{14,12},{15,13},... | collective-permute-start | bytes 688136 | tf_op jit(solution)/shard_map/ppermute | solution.py:67
  74.3 10.3 %collective-permute-start.10 = (bf16[32,3584]{1,0:T(8,128)(2,1)S(1)}, bf16[32,3584]{1,0:T(8,128)(2,1)S(1)}, u32[]{:S(2)}, u32[]{:S(2)}) collective-permute-start(bf16[32,3584]{1,0:T(8,128)(2,1)S(1)} %add_convert_fusion.11), channel_id=1, source_target_pairs={{0,4},{1,5},{4,8},{5,9},{8,12},{9,13},{12,14},{13,15},{14,10},{15,... | collective-permute-start | bytes 688136 | tf_op jit(solution)/shard_map/ppermute | solution.py:67
  79.8 9.7 %collective-permute-start.19 = (bf16[32,3584]{1,0:T(8,128)(2,1)S(1)}, bf16[32,3584]{1,0:T(8,128)(2,1)S(1)}, u32[]{:S(2)}, u32[]{:S(2)}) collective-permute-start(bf16[32,3584]{1,0:T(8,128)(2,1)S(1)} %add_convert_fusion.4), channel_id=1, source_target_pairs={{0,4},{1,5},{4,8},{5,9},{8,12},{9,13},{12,14},{13,15},{14,10},{15,... | collective-permute-start | bytes 688136 | tf_op jit(solution)/shard_map/ppermute | solution.py:67
  89.7 10.0 %collective-permute-start.23 = (bf16[32,3584]{1,0:T(8,128)(2,1)S(1)}, bf16[32,3584]{1,0:T(8,128)(2,1)S(1)}, u32[]{:S(2)}, u32[]{:S(2)}) collective-permute-start(bf16[32,3584]{1,0:T(8,128)(2,1)S(1)} %get-tuple-element.46), channel_id=1, source_target_pairs={{0,2},{1,3},{4,0},{5,1},{8,4},{9,5},{12,8},{13,9},{14,12},{15,13},... | collective-permute-start | bytes 688136 | tf_op jit(solution)/shard_map/ppermute | solution.py:67
  90.3 9.4 %collective-permute-start.20 = (bf16[32,3584]{1,0:T(8,128)(2,1)S(1)}, bf16[32,3584]{1,0:T(8,128)(2,1)S(1)}, u32[]{:S(2)}, u32[]{:S(2)}) collective-permute-start(bf16[32,3584]{1,0:T(8,128)(2,1)S(1)} %get-tuple-element.47), channel_id=1, source_target_pairs={{0,4},{1,5},{4,8},{5,9},{8,12},{9,13},{12,14},{13,15},{14,10},{15,... | collective-permute-start | bytes 688136 | tf_op jit(solution)/shard_map/ppermute | solution.py:67
  103.7 8.7 %collective-permute-start.48 = (bf16[32,3584]{1,0:T(8,128)(2,1)}, bf16[32,3584]{1,0:T(8,128)(2,1)S(1)}, u32[]{:S(2)}, u32[]{:S(2)}) collective-permute-start(bf16[32,3584]{1,0:T(8,128)(2,1)} %get-tuple-element.45.refs_0_), channel_id=1, source_target_pairs={{0,2},{1,3},{4,0},{5,1},{8,4},{9,5},{12,8},{13,9},{14,12},{15,13},... | collective-permute-start | bytes 688136 | tf_op jit(solution)/shard_map/ppermute | solution.py:67
  104.3 9.2 %collective-permute-start.40 = (bf16[32,3584]{1,0:T(8,128)(2,1)}, bf16[32,3584]{1,0:T(8,128)(2,1)S(1)}, u32[]{:S(2)}, u32[]{:S(2)}) collective-permute-start(bf16[32,3584]{1,0:T(8,128)(2,1)} %get-tuple-element.45.refs_0_), channel_id=1, source_target_pairs={{0,4},{1,5},{4,8},{5,9},{8,12},{9,13},{12,14},{13,15},{14,10},{15,... | collective-permute-start | bytes 688136 | tf_op jit(solution)/shard_map/ppermute | solution.py:67
  105.8 9.2 %collective-permute-start.39 = (bf16[32,3584]{1,0:T(8,128)(2,1)}, bf16[32,3584]{1,0:T(8,128)(2,1)S(1)}, u32[]{:S(2)}, u32[]{:S(2)}) collective-permute-start(bf16[32,3584]{1,0:T(8,128)(2,1)} %get-tuple-element.45.refs_0_), channel_id=1, source_target_pairs={{0,1},{1,0},{2,3},{3,2},{4,5},{5,4},{6,7},{7,6},{8,9},{9,8},{10,11... | collective-permute-start | bytes 688136 | tf_op jit(solution)/shard_map/ppermute | solution.py:37
  105.8 11.2 %collective-permute-start.35 = (bf16[32,3584]{1,0:T(8,128)(2,1)S(1)}, bf16[32,3584]{1,0:T(8,128)(2,1)}, u32[]{:S(2)}, u32[]{:S(2)}) collective-permute-start(bf16[32,3584]{1,0:T(8,128)(2,1)S(1)} %collective-permute-done.33.refs_5_), channel_id=1, source_target_pairs={{0,2},{1,3},{4,0},{5,1},{8,4},{9,5},{12,8},{13,9},{14,12},{15,13},... | collective-permute-start | bytes 688136 | tf_op jit(solution)/shard_map/ppermute | solution.py:67
  106.4 11.1 %collective-permute-start.34 = (bf16[32,3584]{1,0:T(8,128)(2,1)S(1)}, bf16[32,3584]{1,0:T(8,128)(2,1)S(1)}, u32[]{:S(2)}, u32[]{:S(2)}) collective-permute-start(bf16[32,3584]{1,0:T(8,128)(2,1)S(1)} %collective-permute-done.33.refs_5_), channel_id=1, source_target_pairs={{0,1},{1,0},{2,3},{3,2},{4,5},{5,4},{6,7},{7,6},{8,9},{9,8},{10,11... | collective-permute-start | bytes 688136 | tf_op jit(solution)/shard_map/ppermute | solution.py:37
  112.3 8.6 %collective-permute-start.27 = (bf16[32,3584]{1,0:T(8,128)(2,1)S(1)}, bf16[32,3584]{1,0:T(8,128)(2,1)}, u32[]{:S(2)}, u32[]{:S(2)}) collective-permute-start(bf16[32,3584]{1,0:T(8,128)(2,1)S(1)} %collective-permute-done.25.refs_1_), channel_id=1, source_target_pairs={{0,4},{1,5},{4,8},{5,9},{8,12},{9,13},{12,14},{13,15},{14,10},{15,... | collective-permute-start | bytes 688136 | tf_op jit(solution)/shard_map/ppermute | solution.py:67
  113.5 10.6 %collective-permute-start.42 = (bf16[32,3584]{1,0:T(8,128)(2,1)S(1)}, bf16[32,3584]{1,0:T(8,128)(2,1)S(1)}, u32[]{:S(2)}, u32[]{:S(2)}) collective-permute-start(bf16[32,3584]{1,0:T(8,128)(2,1)S(1)} %collective-permute-done.40.refs_1_), channel_id=1, source_target_pairs={{0,4},{1,5},{4,8},{5,9},{8,12},{9,13},{12,14},{13,15},{14,10},{15,... | collective-permute-start | bytes 688136 | tf_op jit(solution)/shard_map/ppermute | solution.py:67
  114.9 10.3 %collective-permute-start.26 = (bf16[32,3584]{1,0:T(8,128)(2,1)S(1)}, bf16[32,3584]{1,0:T(8,128)(2,1)S(1)}, u32[]{:S(2)}, u32[]{:S(2)}) collective-permute-start(bf16[32,3584]{1,0:T(8,128)(2,1)S(1)} %collective-permute-done.25.refs_1_), channel_id=1, source_target_pairs={{0,1},{1,0},{2,3},{3,2},{4,5},{5,4},{6,7},{7,6},{8,9},{9,8},{10,11... | collective-permute-start | bytes 688136 | tf_op jit(solution)/shard_map/ppermute | solution.py:37
  117.0 9.2 %collective-permute-start.50 = (bf16[32,3584]{1,0:T(8,128)(2,1)S(1)}, bf16[32,3584]{1,0:T(8,128)(2,1)S(1)}, u32[]{:S(2)}, u32[]{:S(2)}) collective-permute-start(bf16[32,3584]{1,0:T(8,128)(2,1)S(1)} %collective-permute-done.48.refs_5_), channel_id=1, source_target_pairs={{0,2},{1,3},{4,0},{5,1},{8,4},{9,5},{12,8},{13,9},{14,12},{15,13},... | collective-permute-start | bytes 688136 | tf_op jit(solution)/shard_map/ppermute | solution.py:67
  117.6 9.7 %collective-permute-start.49 = (bf16[32,3584]{1,0:T(8,128)(2,1)S(1)}, bf16[32,3584]{1,0:T(8,128)(2,1)S(1)}, u32[]{:S(2)}, u32[]{:S(2)}) collective-permute-start(bf16[32,3584]{1,0:T(8,128)(2,1)S(1)} %collective-permute-done.48.refs_5_), channel_id=1, source_target_pairs={{0,1},{1,0},{2,3},{3,2},{4,5},{5,4},{6,7},{7,6},{8,9},{9,8},{10,11... | collective-permute-start | bytes 688136 | tf_op jit(solution)/shard_map/ppermute | solution.py:37
  126.2 11.5 %collective-permute-start.29 = (bf16[32,3584]{1,0:T(8,128)(2,1)}, bf16[32,3584]{1,0:T(8,128)(2,1)}, u32[]{:S(2)}, u32[]{:S(2)}) collective-permute-start(bf16[32,3584]{1,0:T(8,128)(2,1)} %collective-permute-done.27.refs_2_), channel_id=1, source_target_pairs={{0,4},{1,5},{4,8},{5,9},{8,12},{9,13},{12,14},{13,15},{14,10},{15,... | collective-permute-start | bytes 688136 | tf_op jit(solution)/shard_map/ppermute | solution.py:67
  127.3 11.4 %collective-permute-start.52 = (bf16[32,3584]{1,0:T(8,128)(2,1)S(1)}, bf16[32,3584]{1,0:T(8,128)(2,1)S(1)}, u32[]{:S(2)}, u32[]{:S(2)}) collective-permute-start(bf16[32,3584]{1,0:T(8,128)(2,1)S(1)} %collective-permute-done.50.refs_6_), channel_id=1, source_target_pairs={{0,2},{1,3},{4,0},{5,1},{8,4},{9,5},{12,8},{13,9},{14,12},{15,13},... | collective-permute-start | bytes 688136 | tf_op jit(solution)/shard_map/ppermute | solution.py:67
  128.2 10.5 %collective-permute-start.51 = (bf16[32,3584]{1,0:T(8,128)(2,1)S(1)}, bf16[32,3584]{1,0:T(8,128)(2,1)S(1)}, u32[]{:S(2)}, u32[]{:S(2)}) collective-permute-start(bf16[32,3584]{1,0:T(8,128)(2,1)S(1)} %collective-permute-done.50.refs_6_), channel_id=1, source_target_pairs={{0,1},{1,0},{2,3},{3,2},{4,5},{5,4},{6,7},{7,6},{8,9},{9,8},{10,11... | collective-permute-start | bytes 688136 | tf_op jit(solution)/shard_map/ppermute | solution.py:37
  132.7 9.7 %collective-permute-start.46 = (bf16[32,3584]{1,0:T(8,128)(2,1)S(1)}, bf16[32,3584]{1,0:T(8,128)(2,1)S(1)}, u32[]{:S(2)}, u32[]{:S(2)}) collective-permute-start(bf16[32,3584]{1,0:T(8,128)(2,1)S(1)} %collective-permute-done.44.refs_3_), channel_id=1, source_target_pairs={{0,4},{1,5},{4,8},{5,9},{8,12},{9,13},{12,14},{13,15},{14,10},{15,... | collective-permute-start | bytes 688136 | tf_op jit(solution)/shard_map/ppermute | solution.py:67
  142.4 12.5 %collective-permute-start.36 = (bf16[32,3584]{1,0:T(8,128)(2,1)}, bf16[32,3584]{1,0:T(8,128)(2,1)S(1)}, u32[]{:S(2)}, u32[]{:S(2)}) collective-permute-start(bf16[32,3584]{1,0:T(8,128)(2,1)} %collective-permute-done.35.refs_6_), channel_id=1, source_target_pairs={{0,1},{1,0},{2,3},{3,2},{4,5},{5,4},{6,7},{7,6},{8,9},{9,8},{10,11... | collective-permute-start | bytes 688136 | tf_op jit(solution)/shard_map/ppermute | solution.py:37
  144.9 9.9 %collective-permute-start.28 = (bf16[32,3584]{1,0:T(8,128)(2,1)}, bf16[32,3584]{1,0:T(8,128)(2,1)S(1)}, u32[]{:S(2)}, u32[]{:S(2)}) collective-permute-start(bf16[32,3584]{1,0:T(8,128)(2,1)} %collective-permute-done.27.refs_2_), channel_id=1, source_target_pairs={{0,1},{1,0},{2,3},{3,2},{4,5},{5,4},{6,7},{7,6},{8,9},{9,8},{10,11... | collective-permute-start | bytes 688136 | tf_op jit(solution)/shard_map/ppermute | solution.py:37
  144.9 10.0 %collective-permute-start.30 = (bf16[32,3584]{1,0:T(8,128)(2,1)}, bf16[32,3584]{1,0:T(8,128)(2,1)S(1)}, u32[]{:S(2)}, u32[]{:S(2)}) collective-permute-start(bf16[32,3584]{1,0:T(8,128)(2,1)} %collective-permute-done.29.refs_3_), channel_id=1, source_target_pairs={{0,1},{1,0},{2,3},{3,2},{4,5},{5,4},{6,7},{7,6},{8,9},{9,8},{10,11... | collective-permute-start | bytes 688136 | tf_op jit(solution)/shard_map/ppermute | solution.py:37
  145.5 9.4 %collective-permute-start.38 = (bf16[32,3584]{1,0:T(8,128)(2,1)}, bf16[32,3584]{1,0:T(8,128)(2,1)S(1)}, u32[]{:S(2)}, u32[]{:S(2)}) collective-permute-start(bf16[32,3584]{1,0:T(8,128)(2,1)} %collective-permute-done.37.refs_7_), channel_id=1, source_target_pairs={{0,1},{1,0},{2,3},{3,2},{4,5},{5,4},{6,7},{7,6},{8,9},{9,8},{10,11... | collective-permute-start | bytes 688136 | tf_op jit(solution)/shard_map/ppermute | solution.py:37
  145.6 9.3 %collective-permute-start.32 = (bf16[32,3584]{1,0:T(8,128)(2,1)}, bf16[32,3584]{1,0:T(8,128)(2,1)}, u32[]{:S(2)}, u32[]{:S(2)}) collective-permute-start(bf16[32,3584]{1,0:T(8,128)(2,1)} %collective-permute-done.31.refs_4_), channel_id=1, source_target_pairs={{0,1},{1,0},{2,3},{3,2},{4,5},{5,4},{6,7},{7,6},{8,9},{9,8},{10,11... | collective-permute-start | bytes 688136 | tf_op jit(solution)/shard_map/ppermute | solution.py:37
  (56 other events, 667.7 us)

commit v4 on v3

v4 whole, which is shorter than its diff:
```python
import functools

import jax
import jax.numpy as jnp
from jax import lax
from jax.experimental import pallas as pl
from jax.experimental.pallas import tpu as pltpu
from jax.sharding import PartitionSpec as P

beta_one = 0.9
beta_two = 0.99
first_fix = 1.0 - 0.9**4
second_fix = 1.0 - 0.99**4
learn_rate = 0.02
adam_eps = 1e-08
reset_gain = 0.01
norm_eps = 1e-06

KEPT = -1
ABSENT = -2


def adam_update(weight, moment, second, gradient):
    moment_new = beta_one * moment + (1.0 - beta_one) * gradient
    second_new = beta_two * second + (1.0 - beta_two) * gradient * gradient
    weight_new = weight - learn_rate * (moment_new / first_fix) / (
        jnp.sqrt(second_new / second_fix) + adam_eps
    )
    return (weight_new, moment_new, second_new)


def inverse_rms(value):
    return lax.rsqrt(jnp.mean(value * value, axis=1, keepdims=True) + norm_eps)


def swap(value, bits, size):
    return lax.ppermute(value, "latent", [(i, i ^ bits) for i in range(size)])


def after(value, *others):
    return lax.optimization_barrier((value,) + others)[0]


def params(mebibytes):
    return pltpu.CompilerParams(vmem_limit_bytes=mebibytes * 2**20)


def cost(flops, moved):
    return pl.CostEstimate(flops=int(flops), bytes_accessed=int(moved), transcendentals=0)


def chip_at(position, chips):
    return jnp.where(position < chips // 2, 2 * position, 2 * (chips - 1 - position) + 1)


def position_of(chip, chips):
    return jnp.where(chip % 2 == 0, chip // 2, chips - 1 - chip // 2)


def owner_at(offset, other_core, size):
    me = lax.axis_index("latent")
    chips = size // 2
    position = lax.rem(position_of(me // 2, chips) + offset + chips, chips)
    return 2 * chip_at(position, chips) + ((me % 2) ^ other_core)


def shift(value, step, size):
    chips = size // 2
    ring = [2 * q for q in range(chips // 2)] + [2 * q + 1 for q in reversed(range(chips // 2))]
    pairs = [
        (2 * ring[p] + core, 2 * ring[(p + step) % chips] + core)
        for p in range(chips)
        for core in range(2)
    ]
    return lax.ppermute(value, "latent", pairs)


def gather_table(row, size, late):
    pieces, step = [row], 1
    while step < size:
        if step > 1:
            pieces = [jnp.concatenate([after(piece, late) for piece in pieces], axis=0)]
        pieces += [swap(pieces[0], step * k, size) for k in range(1, min(4, size // step))]
        step *= len(pieces)
    return pieces


def ordered_rows(size, rows, by_latent, by_slot):
    chips = size // 2
    for block in range(size):
        group, inside = block // chips, block % chips
        slot = group * (chips // 2) + inside % (chips // 2)
        far = chips // 2 - slot // 2
        offset = far if slot % 2 == 0 else 1 - far
        owner = owner_at(offset, 1 - inside // (chips // 2), size)
        begin = pl.multiple_of(owner * rows, rows)
        by_slot[block * rows : (block + 1) * rows] = by_latent[pl.ds(begin, rows)]


def row_codes(size, rows, table, picks_ref):
    me = lax.axis_index("latent")
    counts = table[:, :size]
    order = table[:, size:]
    source = me ^ lax.broadcasted_iota(jnp.int32, (size, 1), 0)
    before = jnp.sum(jnp.where(source < me, counts, 0), axis=0, keepdims=True)
    total = jnp.sum(counts, axis=0, keepdims=True)
    owners = lax.broadcasted_iota(jnp.int32, (size, size), 1) == source

    def by_key(row):
        return jnp.sum(jnp.where(owners, row, 0), axis=1, keepdims=True)

    begin, here = by_key(before), by_key(counts[:1])
    place = lax.broadcasted_iota(jnp.int32, (size, rows), 1)
    token = jnp.full((size, rows), ABSENT, jnp.int32)
    for c in range(picks_ref.shape[0]):
        own = (place == begin + c) & (here > c)
        token = jnp.where(own, by_key(picks_ref[c : c + 1]), token)
    token = jnp.where(place < by_key(total), token, KEPT)
    latent = lax.broadcasted_iota(jnp.int32, (size * rows, 1), 0)
    keys = lax.broadcasted_iota(jnp.int32, (size * rows, size), 1)
    spread = (keys == (me ^ (latent // rows))).astype(jnp.float32)

    def by_row(values):
        return jnp.dot(spread, values.astype(jnp.float32), precision=lax.Precision.HIGHEST)

    is_latent = by_row(order) == (latent % rows).astype(jnp.float32)
    code = jnp.sum(jnp.where(is_latent, by_row(token), 0.0), axis=1, keepdims=True)
    return (code + jnp.where(code < 0, -0.5, 0.5)).astype(jnp.int32)


def multiply(by_slot, right_ref, outs):
    out = jnp.dot(by_slot[...], right_ref[...], preferred_element_type=jnp.float32)
    part = outs[0].shape[0]
    for i, ref in enumerate(outs):
        ref[...] = out[i * part : (i + 1) * part].astype(ref.dtype)


def product_kernel(size, rows, coef_ref, right_ref, *refs):
    outs, (by_latent, by_slot) = refs[:4], refs[4:]

    @pl.when(pl.program_id(0) == 0)
    def _():
        by_latent[...] = coef_ref[...].T
        ordered_rows(size, rows, by_latent, by_slot)

    multiply(by_slot, right_ref, outs)


def select_kernel(size, rows, count, coef_ref, right_ref, picks_ref, *refs):
    pieces, refs = refs[:count], refs[count:]
    outs, own_code, (by_latent, by_slot, table, codes) = refs[:4], refs[4], refs[5:]

    @pl.when(pl.program_id(0) == 0)
    def _():
        height = size // count
        for i, piece in enumerate(pieces):
            table[i * height : (i + 1) * height] = piece[...]
        code = row_codes(size, rows, table[...], picks_ref)
        codes[...] = code
        own_code[...] = codes[pl.ds(pl.multiple_of(lax.axis_index("latent") * rows, rows), rows)]
        tokens = lax.broadcasted_iota(jnp.int32, by_latent.shape, 1)
        by_latent[...] = jnp.where(
            code == KEPT, coef_ref[...].T, (tokens == code).astype(by_latent.dtype)
        )
        ordered_rows(size, rows, by_latent, by_slot)

    multiply(by_slot, right_ref, outs)


def product(coef, right, size, rows, picks=None, table=()):
    tokens, latents = coef.shape
    width = right.shape[1]
    tile = 512
    part = latents // 4
    fixed = lambda j: (0, 0)
    in_specs = [pl.BlockSpec((tokens, latents), fixed), pl.BlockSpec((tokens, tile), lambda j: (0, j))]
    out_specs = [pl.BlockSpec((part, tile), lambda j: (0, j))] * 4
    out_shape = [jax.ShapeDtypeStruct((part, width), coef.dtype)] * 4
    scratch = [pltpu.VMEM((latents, tokens), coef.dtype)] * 2
    kernel = functools.partial(product_kernel, size, rows)
    operands = [coef, right]
    if picks is not None:
        kernel = functools.partial(select_kernel, size, rows, len(table))
        operands += [picks] + list(table)
        in_specs += [pl.BlockSpec(value.shape, fixed) for value in operands[2:]]
        out_specs.append(pl.BlockSpec((rows, 1), fixed))
        out_shape.append(jax.ShapeDtypeStruct((rows, 1), jnp.int32))
        scratch += [
            pltpu.VMEM((size, table[0].shape[1]), jnp.int32),
            pltpu.VMEM((latents, 1), jnp.int32),
        ]
    return pl.pallas_call(
        kernel,
        grid=(width // tile,),
        in_specs=in_specs,
        out_specs=out_specs,
        out_shape=out_shape,
        scratch_shapes=scratch,
        compiler_params=params(24),
        cost_estimate=cost(
            2 * latents * tokens * width, 2 * (tokens * width + latents * (tokens + width))
        ),
        name="product" if picks is None else "select_product",
    )(*operands)


def term(kept, from_core, slot, rows):
    slots = kept[0].shape[0] // rows
    group, begin = slot // slots, slot % slots * rows
    pair = (kept[group], from_core[group])
    return sum(value[begin : begin + rows].astype(jnp.float32) for value in pair)


def read_gradient(refs):
    return sum(ref[...].astype(jnp.float32) for ref in refs)


def enc_kernel(code_ref, w_ref, m_ref, v_ref, *refs):
    parts, (w_out, m_out, v_out, block, fresh) = refs[:-5], refs[-5:]
    gradient = read_gradient(parts)
    reset = code_ref[...] != KEPT
    w, m, v = adam_update(w_ref[...], m_ref[...], v_ref[...], gradient)
    w = jnp.where(reset, reset_gain * gradient * inverse_rms(gradient), w)
    w_out[...] = w
    m_out[...] = jnp.where(reset, 0.0, m)
    v_out[...] = jnp.where(reset, 0.0, v)
    block[...] = w.astype(block.dtype)
    fresh[...] = gradient.astype(fresh.dtype)


def dec_kernel(code_ref, w_ref, m_ref, v_ref, fresh_ref, *refs):
    parts, (w_out, m_out, v_out, block) = refs[:-4], refs[-4:]
    reset = code_ref[...] != KEPT
    w, m, v = adam_update(w_ref[...], m_ref[...], v_ref[...], read_gradient(parts))
    w = jnp.where(reset, fresh_ref[...].astype(jnp.float32), w)
    w = w * inverse_rms(w)
    w_out[...] = w
    m_out[...] = jnp.where(reset, 0.0, m)
    v_out[...] = jnp.where(reset, 0.0, v)
    block[...] = w.astype(block.dtype)


def update(kernel, code, states, fresh, parts, extra, name):
    rows, width = states[0].shape
    tile = 16

    def last_rows(value):
        skipped = (value.shape[0] - rows) // tile
        return pl.BlockSpec((tile, value.shape[1]), lambda i: (i + skipped, 0))

    operands = [code] + list(states) + list(fresh) + list(parts)
    out_spec = pl.BlockSpec((tile, width), lambda i: (i, 0))
    wide = jax.ShapeDtypeStruct((rows, width), jnp.float32)
    narrow = jax.ShapeDtypeStruct((rows, width), jnp.bfloat16)
    return pl.pallas_call(
        kernel,
        grid=(rows // tile,),
        in_specs=[last_rows(value) for value in operands],
        out_specs=(out_spec,) * (3 + extra),
        out_shape=(wide,) * 3 + (narrow,) * extra,
        cost_estimate=cost(40 * rows * width, 40 * rows * width),
        compiler_params=params(12),
        name=name,
    )(*operands)


def place_kernel(plan, size, rows, wholes, count, *refs):
    pieces, refs = refs[:count], refs[count:]
    outs, (stage, sems_in, sems_out, sems_pack) = refs[wholes:-4], refs[-4:]
    coming, going = [], []
    for i, (piece, block, whole, offset, other_core, pack) in enumerate(plan):
        source = pieces[piece].at[pl.ds(block * rows, rows)]
        coming.append(pltpu.make_async_copy(source, stage.at[i], sems_in.at[i]))
        start = pl.multiple_of(owner_at(offset, other_core, size) * rows, rows)
        target = outs[whole].at[pl.ds(start, rows)]
        copies = [pltpu.make_async_copy(stage.at[i], target, sems_out.at[i])]
        if pack is not None:
            target = outs[2].at[pl.ds(pack * rows, rows)]
            copies.append(pltpu.make_async_copy(stage.at[i], target, sems_pack.at[pack]))
        going.append(copies)
    for copy in coming:
        copy.start()
    for copy, copies in zip(coming, going):
        copy.wait()
        for later in reversed(copies):
            later.start()
    for copies in going:
        for copy in copies:
            copy.wait()


def place(near, far, wholes, size, rows, pack=True):
    operands = [block for _, _, block in near] + [value for value, _ in far]
    plan = []
    for i, (whole, offset, _) in enumerate(near):
        plan.append((i, 0, whole, offset, 0, i if pack else None))
    for i, (_, places) in enumerate(far):
        for block, (whole, offset) in enumerate(places):
            plan.append((len(near) + i, block, whole, offset, 1, None))
    width, dtype = operands[0].shape[1], operands[0].dtype
    out_shape = [jax.ShapeDtypeStruct((size * rows, width), dtype)] * 2
    packed = len(near) if pack else 0
    if packed:
        out_shape.append(jax.ShapeDtypeStruct((packed * rows, width), dtype))
    first = wholes is None
    count = len(operands)
    if not first:
        operands += list(wholes)
    anywhere = pl.BlockSpec(memory_space=pl.ANY)
    out = pl.pallas_call(
        functools.partial(place_kernel, plan, size, rows, 0 if first else 2, count),
        out_shape=out_shape,
        in_specs=[anywhere] * len(operands),
        out_specs=[anywhere] * len(out_shape),
        scratch_shapes=[
            pltpu.VMEM((len(plan), rows, width), dtype),
            pltpu.SemaphoreType.DMA((len(plan),)),
            pltpu.SemaphoreType.DMA((len(plan),)),
            pltpu.SemaphoreType.DMA((max(packed, 1),)),
        ],
        input_output_aliases={} if first else {count: 0, count + 1: 1},
        compiler_params=params(10),
        cost_estimate=cost(0, 4 * len(plan) * rows * width),
        name="place",
    )(*operands)
    return (out[:2], out[2]) if packed else (out, None)


def gathered(blocks, size, rows):
    chips = size // 2
    left_hops = (chips - 1) // 2
    moving = [[block, block] for block in blocks]
    near = [(whole, 0, block) for whole, block in enumerate(blocks)]
    wholes, far = None, []
    for hop in range(1, chips // 2 + 1):
        sides = ((1, -hop), (-1, hop))[: 1 + (hop <= left_hops)]
        for whole in range(2):
            moving[whole] = [shift(moving[whole][i], step, size) for i, (step, _) in enumerate(sides)]
        held = [value for _, _, value in near]
        held, moving[0] = lax.optimization_barrier((held, moving[0]))
        near = [(whole, offset, value) for (whole, offset, _), value in zip(near, held)]
        wholes, packed = place(near, far[:-1], wholes, size, rows)
        moving[1] = after(moving[1], packed)
        far = far[-1:] + [(swap(packed, 1, size), [(whole, offset) for whole, offset, _ in near])]
        near = [
            (whole, offset, moving[whole][i])
            for whole in range(2)
            for i, (_, offset) in enumerate(sides)
        ]
    last_far = [(swap(value, 1, size), [(whole, offset)]) for whole, offset, value in near]
    wholes, _ = place(near, far, wholes, size, rows, pack=False)
    wholes, _ = place([], last_far, wholes, size, rows, pack=False)
    return wholes


def shards(
    x_rows,
    out_grad,
    enc_coef,
    latent_act,
    enc_w,
    enc_m,
    enc_v,
    dec_w,
    dec_m,
    dec_v,
    dead_order,
    pick_rows,
    send_count,
):
    rows = enc_w.shape[0]
    size = lax.axis_size("latent")
    chips = size // 2
    own = jnp.concatenate([send_count, dead_order], axis=1)
    dec = product(after(latent_act, own), out_grad, size, rows)
    table = gather_table(own, size, dec[0])
    dec_core = [swap(dec[0], 1, size), swap(dec[2], 1, size)]
    dec_kept = [dec[1], dec[3]]

    def advance(moving, step, kept, from_core, slot):
        came = shift(moving, step, size).astype(jnp.float32)
        return (came + term(kept, from_core, slot, rows)).astype(jnp.bfloat16)

    def begin(kept, from_core):
        return [term(kept, from_core, slot, rows).astype(jnp.bfloat16) for slot in range(2)]

    dec_moving = begin(after(dec_kept, table[0]), dec_core)
    *enc, code = product(
        after(enc_coef, *dec_moving), x_rows, size, rows, pick_rows[0].T, table
    )
    enc_core = [swap(enc[0], 1, size), swap(enc[2], 1, size)]
    enc_kept = [enc[1], enc[3]]
    dec_kept = after(dec_kept, enc[0])
    enc_moving = begin(enc_kept, enc_core)
    for slot in range(2, chips - 1):
        side = slot % 2
        step = 1 - 2 * side
        dec_moving[side] = advance(dec_moving[side], step, dec_kept, dec_core, slot)
        enc_moving[side] = advance(enc_moving[side], step, enc_kept, enc_core, slot)
    dec_parts, enc_parts = (
        [kept[1], from_core[1], shift(moving[0], 1, size), shift(moving[1], -1, size)]
        for kept, from_core, moving in (
            (dec_kept, dec_core, dec_moving),
            (enc_kept, enc_core, enc_moving),
        )
    )
    enc_out, enc_mo, enc_vo, enc_block, fresh = update(
        enc_kernel, code, (enc_w, enc_m, enc_v), (), enc_parts, 2, "enc_update"
    )
    dec_out, dec_mo, dec_vo, dec_block = update(
        dec_kernel, code, (dec_w, dec_m, dec_v), (fresh,), dec_parts, 1, "dec_update"
    )
    enc_full, dec_full = gathered((enc_block, dec_block), size, rows)
    return (enc_out, enc_mo, enc_vo, dec_out, dec_mo, dec_vo, enc_full, dec_full)


def solution(mesh):
    split = P(("groups", "latent"), None)
    placed = (split,) * 11 + (P(("groups", "latent"), None, None), split)
    return jax.shard_map(
        shards,
        mesh=mesh,
        in_specs=placed,
        out_specs=(split,) * 6 + (P("groups", None),) * 2,
        check_vma=False,
    )
```

time: 159 us -> 141 us (0.89)
  Pallas kernels: 50.3 us -> 36.4 us
  other arithmetic: 6.83 us -> 1.83 us
  waiting for transfers between devices: 57.4 us -> 59.5 us
  starting transfers between devices: 39.3 us -> 37.3 us
    pallas_call x10 -> x8, Pallas kernels: 44 us -> 32.9 us  [the longest x6 19.6 us: place(): pl.pallas_call(functools.partial(place_kernel, plan, size, rows, 0 if fir...]
    convert_element_type x8, other arithmetic: 5.33 us -> 1.07 us  [the longest x6 0.84 us: advance(): return (came + term(kept, from_core, slot, rows)).astype(jnp.bfloat16)]
    ppermute x26 -> x16, waiting for transfers between devices: 6.62 us -> 10.5 us  [swap(): return lax.ppermute(value, 'latent', [(i, i ^ bits) for i in range(size)])]
    pallas_call x2, Pallas kernels: 6.3 us -> 3.49 us  [update(): pl.pallas_call(kernel, grid=(rows // tile,), in_specs=[last_rows(value) f...]
    ppermute x26 -> x16, starting transfers between devices: 10.9 us -> 8.62 us  [swap(): return lax.ppermute(value, 'latent', [(i, i ^ bits) for i in range(size)])]
    unnamed x68 -> x22, local copies, waits for them, and re-layouts: 2.4 us -> 4.36 us
    ppermute x28, waiting for transfers between devices: 50.8 us -> 49.1 us  [shift(): return lax.ppermute(value, 'latent', pairs)]
  transfers between devices with their start and end apart: 54 -> 44, of which waited for: 20 -> 27; matrix products, arithmetic and copies ran while one was open for 3% -> 1% of each run, Pallas kernels for 23% -> 13%
where the time goes in v4:
time: 141 us; the launch traced here: 140 us
  waiting for transfers between devices  59.5 us (42%)
  starting transfers between devices  37.3 us (26%)
  Pallas kernels  36.4 us (26%)
  local copies, waits for them, and re-layouts  4.36 us (3%)
  other arithmetic  1.83 us (1%)
    ppermute x28, waiting for transfers between devices, shift(): return lax.ppermute(value, 'latent', pairs)  49.1 us
    ppermute x28, starting transfers between devices, shift(): return lax.ppermute(value, 'latent', pairs)  28.6 us
    pallas_call x6, Pallas kernels, place(): pl.pallas_call(functools.partial(place_kernel, plan, size, rows, 0 if fir...  19.6 us
    pallas_call x2, Pallas kernels, product(): pl.pallas_call(kernel, grid=(width // tile,), in_specs=in_specs, out_spec...  13.3 us
    ppermute x16, waiting for transfers between devices, swap(): return lax.ppermute(value, 'latent', [(i, i ^ bits) for i in range(size)])  10.5 us
    ppermute x16, starting transfers between devices, swap(): return lax.ppermute(value, 'latent', [(i, i ^ bits) for i in range(size)])  8.62 us
    unnamed x22, local copies, waits for them, and re-layouts  4.36 us
    pallas_call x2, Pallas kernels, update(): pl.pallas_call(kernel, grid=(rows // tile,), in_specs=[last_rows(value) f...  3.49 us
  transfers between devices with their start and end apart: 44, of which 27 were waited for; matrix products, arithmetic and copies ran while one was open for 1% of the time, Pallas kernels for 13%

profile of v4, /device:TPU:0, one launch (start us, length us, event | category | flops | bytes accessed | tf_op | source)
XLA Modules:
  0.0 140.3 jit_solution(4232771004340277303)
XLA Ops:
  1.4 3.1 %copy-done.6 = bf16[1024,3584]{1,0:T(8,128)(2,1)S(1)} copy-done((bf16[1024,3584]{1,0:T(8,128)(2,1)S(1)}, bf16[1024,3584]{1,0:T(8,128)(2,1)}, u32[]{:S(2)}) %copy-start.6) | copy-done | bytes 7340056
  5.7 6.3 %product.1 = (bf16[128,3584]{1,0:T(8,128)(2,1)S(1)}, bf16[128,3584]{1,0:T(8,128)(2,1)S(1)}, bf16[128,3584]{1,0:T(8,128)(2,1)S(1)}, bf16[128,3584]{1,0:T(8,128)(2,1)S(1)}) custom-call(bf16[1024,512]{1,0:T(8,128)(2,1)S(1)} %copy-done.8, bf16[1024,3584]{1,0:T(8,128)(2,1)S(1)} %copy-done.6), custom_call_target="tpu_custom_call" | custom-call | flops 3758096384 | bytes 12058624 | tf_op jit(solution)/shard_map/product/pallas_call | solution.py:192
  12.6 2.9 %collective-permute-start.1 = (s32[1,48]{1,0:T(1,128)S(1)}, s32[1,48]{1,0:T(1,128)S(1)}, u32[]{:S(2)}, u32[]{:S(2)}) collective-permute-start(s32[1,48]{1,0:T(1,128)S(1)} %pad_add_fusion.1), channel_id=1, source_target_pairs={{0,2},{1,3},{2,0},{3,1},{4,6},{5,7},{6,4},{7,5},{8,10},{9,11},{10,... | collective-permute-start | bytes 584 | tf_op jit(solution)/shard_map/ppermute | solution.py:37
  20.2 2.6 %collective-permute-start.5 = (s32[4,48]{1,0:T(4,128)S(1)}, s32[4,48]{1,0:T(4,128)S(1)}, u32[]{:S(2)}, u32[]{:S(2)}) collective-permute-start(s32[4,48]{1,0:T(4,128)S(1)} %pad_add_fusion.refs_0_), channel_id=1, source_target_pairs={{0,8},{1,9},{2,10},{3,11},{4,12},{5,13},{6,14},{7,15},{8,0},{9,1},... | collective-permute-start | bytes 2312 | tf_op jit(solution)/shard_map/ppermute | solution.py:37
  24.7 3.5 %collective-permute-done.6.refs_3_ = s32[4,48]{1,0:T(4,128)S(1)} collective-permute-done((s32[4,48]{1,0:T(4,128)S(1)}, s32[4,48]{1,0:T(4,128)S(1)}, u32[]{:S(2)}, u32[]{:S(2)}) %collective-permute-start.6) | collective-permute-done | bytes 800 | tf_op jit(solution)/shard_map/ppermute | solution.py:37
  28.2 7.0 %select_product.1 = (bf16[128,3584]{1,0:T(8,128)(2,1)S(1)}, bf16[128,3584]{1,0:T(8,128)(2,1)S(1)}, bf16[128,3584]{1,0:T(8,128)(2,1)S(1)}, bf16[128,3584]{1,0:T(8,128)(2,1)S(1)}, s32[32,1]{1,0:T(8,128)S(1)}) custom-call(bf16[1024,512]{1,0:T(8,128)(2,1)S(1)} %copy-done.9, bf16[1024,3584]{1,0:T(8,128)(2,1)S(1)} %copy-done.7, s32[2,16]{1,0:T(2,128)S(1)} %bitcast.3, ...), custom_call_target="tpu_custom_call" | custom-call | flops 3758096384 | bytes 12058624 | tf_op jit(solution)/shard_map/select_product/pallas_call | solution.py:192
  35.3 2.5 %collective-permute-done.8 = bf16[128,3584]{1,0:T(8,128)(2,1)S(1)} collective-permute-done((bf16[128,3584]{1,0:T(8,128)(2,1)S(1)}, bf16[128,3584]{1,0:T(8,128)(2,1)S(1)}, u32[]{:S(2)}, u32[]{:S(2)}) %collective-permute-start.8) | collective-permute-done | bytes 917536 | tf_op jit(solution)/shard_map/ppermute | solution.py:37
  39.9 2.0 %collective-permute-start.21 = (bf16[32,3584]{1,0:T(8,128)(2,1)S(1)}, bf16[32,3584]{1,0:T(8,128)(2,1)S(1)}, u32[]{:S(2)}, u32[]{:S(2)}) collective-permute-start(bf16[32,3584]{1,0:T(8,128)(2,1)S(1)} %get-tuple-element.160), channel_id=1, source_target_pairs={{0,2},{1,3},{4,0},{5,1},{8,4},{9,5},{12,8},{13,9},{14,12},{15,13},... | collective-permute-start | bytes 688136 | tf_op jit(solution)/shard_map/ppermute | solution.py:75
  41.9 4.4 %collective-permute-done.13 = bf16[32,3584]{1,0:T(8,128)(2,1)S(1)} collective-permute-done((bf16[32,3584]{1,0:T(8,128)(2,1)S(1)}, bf16[32,3584]{1,0:T(8,128)(2,1)S(1)}, u32[]{:S(2)}, u32[]{:S(2)}) %collective-permute-start.13) | collective-permute-done | bytes 229408 | tf_op jit(solution)/shard_map/ppermute | solution.py:75
  48.7 3.1 %collective-permute-done.17 = bf16[32,3584]{1,0:T(8,128)(2,1)S(1)} collective-permute-done((bf16[32,3584]{1,0:T(8,128)(2,1)S(1)}, bf16[32,3584]{1,0:T(8,128)(2,1)S(1)}, u32[]{:S(2)}, u32[]{:S(2)}) %collective-permute-start.17) | collective-permute-done | bytes 229408 | tf_op jit(solution)/shard_map/ppermute | solution.py:75
  51.9 1.6 %collective-permute-start.18 = (bf16[32,3584]{1,0:T(8,128)(2,1)S(1)}, bf16[32,3584]{1,0:T(8,128)(2,1)S(1)}, u32[]{:S(2)}, u32[]{:S(2)}) collective-permute-start(bf16[32,3584]{1,0:T(8,128)(2,1)S(1)} %get-tuple-element.153), channel_id=1, source_target_pairs={{0,4},{1,5},{4,8},{5,9},{8,12},{9,13},{12,14},{13,15},{14,10},{15,... | collective-permute-start | bytes 688136 | tf_op jit(solution)/shard_map/ppermute | solution.py:75
  54.1 2.5 %collective-permute-done.10 = bf16[32,3584]{1,0:T(8,128)(2,1)S(1)} collective-permute-done((bf16[32,3584]{1,0:T(8,128)(2,1)S(1)}, bf16[32,3584]{1,0:T(8,128)(2,1)S(1)}, u32[]{:S(2)}, u32[]{:S(2)}) %collective-permute-start.10) | collective-permute-done | bytes 229408 | tf_op jit(solution)/shard_map/ppermute | solution.py:75
  56.7 1.7 %collective-permute-start.11 = (bf16[32,3584]{1,0:T(8,128)(2,1)S(1)}, bf16[32,3584]{1,0:T(8,128)(2,1)S(1)}, u32[]{:S(2)}, u32[]{:S(2)}) collective-permute-start(bf16[32,3584]{1,0:T(8,128)(2,1)S(1)} %add_convert_fusion.9), channel_id=1, source_target_pairs={{0,4},{1,5},{4,8},{5,9},{8,12},{9,13},{12,14},{13,15},{14,10},{15,... | collective-permute-start | bytes 688136 | tf_op jit(solution)/shard_map/ppermute | solution.py:75
  58.4 3.2 %collective-permute-done.18 = bf16[32,3584]{1,0:T(8,128)(2,1)S(1)} collective-permute-done((bf16[32,3584]{1,0:T(8,128)(2,1)S(1)}, bf16[32,3584]{1,0:T(8,128)(2,1)S(1)}, u32[]{:S(2)}, u32[]{:S(2)}) %collective-permute-start.18) | collective-permute-done | bytes 229408 | tf_op jit(solution)/shard_map/ppermute | solution.py:75
  61.7 1.6 %collective-permute-start.19 = (bf16[32,3584]{1,0:T(8,128)(2,1)S(1)}, bf16[32,3584]{1,0:T(8,128)(2,1)S(1)}, u32[]{:S(2)}, u32[]{:S(2)}) collective-permute-start(bf16[32,3584]{1,0:T(8,128)(2,1)S(1)} %add_convert_fusion.3), channel_id=1, source_target_pairs={{0,4},{1,5},{4,8},{5,9},{8,12},{9,13},{12,14},{13,15},{14,10},{15,... | collective-permute-start | bytes 688136 | tf_op jit(solution)/shard_map/ppermute | solution.py:75
  63.5 2.9 %collective-permute-done.11 = bf16[32,3584]{1,0:T(8,128)(2,1)S(1)} collective-permute-done((bf16[32,3584]{1,0:T(8,128)(2,1)S(1)}, bf16[32,3584]{1,0:T(8,128)(2,1)S(1)}, u32[]{:S(2)}, u32[]{:S(2)}) %collective-permute-start.11) | collective-permute-done | bytes 229408 | tf_op jit(solution)/shard_map/ppermute | solution.py:75
  66.6 1.6 %collective-permute-start.12 = (bf16[32,3584]{1,0:T(8,128)(2,1)S(1)}, bf16[32,3584]{1,0:T(8,128)(2,1)S(1)}, u32[]{:S(2)}, u32[]{:S(2)}) collective-permute-start(bf16[32,3584]{1,0:T(8,128)(2,1)S(1)} %get-tuple-element.155), channel_id=1, source_target_pairs={{0,4},{1,5},{4,8},{5,9},{8,12},{9,13},{12,14},{13,15},{14,10},{15,... | collective-permute-start | bytes 688136 | tf_op jit(solution)/shard_map/ppermute | solution.py:75
  68.7 2.7 %collective-permute-done.19 = bf16[32,3584]{1,0:T(8,128)(2,1)S(1)} collective-permute-done((bf16[32,3584]{1,0:T(8,128)(2,1)S(1)}, bf16[32,3584]{1,0:T(8,128)(2,1)S(1)}, u32[]{:S(2)}, u32[]{:S(2)}) %collective-permute-start.19) | collective-permute-done | bytes 229408 | tf_op jit(solution)/shard_map/ppermute | solution.py:75
  71.5 1.7 %collective-permute-start.20 = (bf16[32,3584]{1,0:T(8,128)(2,1)S(1)}, bf16[32,3584]{1,0:T(8,128)(2,1)S(1)}, u32[]{:S(2)}, u32[]{:S(2)}) collective-permute-start(bf16[32,3584]{1,0:T(8,128)(2,1)S(1)} %get-tuple-element.151), channel_id=1, source_target_pairs={{0,4},{1,5},{4,8},{5,9},{8,12},{9,13},{12,14},{13,15},{14,10},{15,... | collective-permute-start | bytes 688136 | tf_op jit(solution)/shard_map/ppermute | solution.py:75
  73.6 2.7 %collective-permute-done.12.refs_2_ = bf16[32,3584]{1,0:T(8,128)(2,1)S(1)} collective-permute-done((bf16[32,3584]{1,0:T(8,128)(2,1)S(1)}, bf16[32,3584]{1,0:T(8,128)(2,1)S(1)}, u32[]{:S(2)}, u32[]{:S(2)}) %collective-permute-start.12) | collective-permute-done | bytes 229408 | tf_op jit(solution)/shard_map/ppermute | solution.py:75
  76.3 1.8 %enc_update.1 = (f32[32,3584]{1,0:T(8,128)}, f32[32,3584]{1,0:T(8,128)}, f32[32,3584]{1,0:T(8,128)}, bf16[32,3584]{1,0:T(8,128)(2,1)S(1)}, bf16[32,3584]{1,0:T(8,128)(2,1)S(1)}) custom-call(s32[32,1]{1,0:T(8,128)S(1)} %get-tuple-element.89.code_ref, f32[32,3584]{1,0:T(8,128)S(1)} %copy-done, f32[32,3584]{1,0:T(8,128)S(1)} %copy-done.1, ...), custom_call_target="tpu_custom_call" | custom-call | flops 4587520 | bytes 4587520 | tf_op jit(solution)/shard_map/enc_update/pallas_call | solution.py:255
  81.2 1.7 %dec_update.1 = (f32[32,3584]{1,0:T(8,128)}, f32[32,3584]{1,0:T(8,128)}, f32[32,3584]{1,0:T(8,128)}, bf16[32,3584]{1,0:T(8,128)(2,1)S(1)}) custom-call(s32[32,1]{1,0:T(8,128)S(1)} %get-tuple-element.89.code_ref, f32[32,3584]{1,0:T(8,128)S(1)} %copy-done.3, f32[32,3584]{1,0:T(8,128)S(1)} %copy-done.4, f32[32,3584]{1,0:T(8,128)S(1)} %copy-done.5, ...), custom_call_target="tpu_custom_call" | custom-call | flops 4587520 | bytes 4587520 | tf_op jit(solution)/shard_map/dec_update/pallas_call | solution.py:255
  88.6 1.9 %place.6 = (bf16[512,3584]{1,0:T(8,128)(2,1)}, bf16[512,3584]{1,0:T(8,128)(2,1)}, bf16[64,3584]{1,0:T(8,128)(2,1)S(1)}) custom-call(bf16[32,3584]{1,0:T(8,128)(2,1)S(1)} %get-tuple-element.108.refs_0_, bf16[32,3584]{1,0:T(8,128)(2,1)S(1)} %get-tuple-element.109.refs_1_), custom_call_target="tpu_custom_call" | custom-call | bytes 917504 | tf_op jit(solution)/shard_map/place/pallas_call | solution.py:310
  93.1 1.9 %collective-permute-done.28.refs_0_ = bf16[32,3584]{1,0:T(8,128)(2,1)S(1)} collective-permute-done((bf16[32,3584]{1,0:T(8,128)(2,1)S(1)}, bf16[32,3584]{1,0:T(8,128)(2,1)S(1)}, u32[]{:S(2)}, u32[]{:S(2)}) %collective-permute-start.28) | collective-permute-done | bytes 229408 | tf_op jit(solution)/shard_map/ppermute | solution.py:75
  95.5 3.1 %place.7 = (bf16[512,3584]{1,0:T(8,128)(2,1)}, bf16[512,3584]{1,0:T(8,128)(2,1)}, bf16[128,3584]{1,0:T(8,128)(2,1)S(1)}) custom-call(bf16[32,3584]{1,0:T(8,128)(2,1)S(1)} %collective-permute-done.24.refs_0_, bf16[32,3584]{1,0:T(8,128)(2,1)S(1)} %collective-permute-done.25.refs_1_, ...), custom_call_target="tpu_custom_call", output_to_operand_aliasing={{0}: (4, {}), {1}: (5, {})} | custom-call | bytes 1835008 | tf_op jit(solution)/shard_map/place/pallas_call | solution.py:310
  101.9 5.3 %collective-permute-done.30.refs_2_ = bf16[32,3584]{1,0:T(8,128)(2,1)S(1)} collective-permute-done((bf16[32,3584]{1,0:T(8,128)(2,1)S(1)}, bf16[32,3584]{1,0:T(8,128)(2,1)S(1)}, u32[]{:S(2)}, u32[]{:S(2)}) %collective-permute-start.30) | collective-permute-done | bytes 229408 | tf_op jit(solution)/shard_map/ppermute | solution.py:75
  109.2 2.9 %collective-permute-done.32.refs_0_ = bf16[32,3584]{1,0:T(8,128)(2,1)S(1)} collective-permute-done((bf16[32,3584]{1,0:T(8,128)(2,1)S(1)}, bf16[32,3584]{1,0:T(8,128)(2,1)S(1)}, u32[]{:S(2)}, u32[]{:S(2)}) %collective-permute-start.32) | collective-permute-done | bytes 229408 | tf_op jit(solution)/shard_map/ppermute | solution.py:75
  114.8 3.9 %place.8 = (bf16[512,3584]{1,0:T(8,128)(2,1)}, bf16[512,3584]{1,0:T(8,128)(2,1)}, bf16[128,3584]{1,0:T(8,128)(2,1)S(1)}) custom-call(bf16[32,3584]{1,0:T(8,128)(2,1)S(1)} %collective-permute-done.28.refs_0_, bf16[32,3584]{1,0:T(8,128)(2,1)S(1)} %collective-permute-done.29.refs_1_, ...), custom_call_target="tpu_custom_call", output_to_operand_aliasing={{0}: (5, {}), {1}: (6, {})} | custom-call | bytes 2752512 | tf_op jit(solution)/shard_map/place/pallas_call | solution.py:310
  118.9 2.6 %collective-permute-done.37.refs_0_ = bf16[32,3584]{1,0:T(8,128)(2,1)S(1)} collective-permute-done((bf16[32,3584]{1,0:T(8,128)(2,1)S(1)}, bf16[32,3584]{1,0:T(8,128)(2,1)S(1)}, u32[]{:S(2)}, u32[]{:S(2)}) %collective-permute-start.37) | collective-permute-done | bytes 229408 | tf_op jit(solution)/shard_map/ppermute | solution.py:75
  121.5 4.7 %place.9 = (bf16[512,3584]{1,0:T(8,128)(2,1)}, bf16[512,3584]{1,0:T(8,128)(2,1)}, bf16[128,3584]{1,0:T(8,128)(2,1)S(1)}) custom-call(bf16[32,3584]{1,0:T(8,128)(2,1)S(1)} %collective-permute-done.32.refs_0_, bf16[32,3584]{1,0:T(8,128)(2,1)S(1)} %collective-permute-done.33.refs_1_, ...), custom_call_target="tpu_custom_call", output_to_operand_aliasing={{0}: (5, {}), {1}: (6, {})} | custom-call | bytes 3670016 | tf_op jit(solution)/shard_map/place/pallas_call | solution.py:310
  127.4 6.9 %collective-permute-done.39.refs_1_ = bf16[32,3584]{1,0:T(8,128)(2,1)S(1)} collective-permute-done((bf16[32,3584]{1,0:T(8,128)(2,1)S(1)}, bf16[32,3584]{1,0:T(8,128)(2,1)S(1)}, u32[]{:S(2)}, u32[]{:S(2)}) %collective-permute-start.39) | collective-permute-done | bytes 229408 | tf_op jit(solution)/shard_map/ppermute | solution.py:75
  134.3 4.6 %place.10 = (bf16[512,3584]{1,0:T(8,128)(2,1)}, bf16[512,3584]{1,0:T(8,128)(2,1)}) custom-call(bf16[32,3584]{1,0:T(8,128)(2,1)S(1)} %collective-permute-done.37.refs_0_, bf16[32,3584]{1,0:T(8,128)(2,1)S(1)} %collective-permute-done.39.refs_1_, bf16[128,3584]{1,0:T(8,128)(2,1)S(1)} %collective-permute-done.42.refs_2_, ...), custom_call_target="tpu_custom_call", output_to_operand_aliasing={{0}: (4, {}), {1}: (5, {})} | custom-call | bytes 4587520 | tf_op jit(solution)/shard_map/place/pallas_call | solution.py:310
  (98 shorter events, 38.7 us)
Async XLA Ops:
  12.0 11.0 %collective-permute-start.3 = (bf16[128,3584]{1,0:T(8,128)(2,1)S(1)}, bf16[128,3584]{1,0:T(8,128)(2,1)S(1)}, u32[]{:S(2)}, u32[]{:S(2)}) collective-permute-start(bf16[128,3584]{1,0:T(8,128)(2,1)S(1)} %get-tuple-element.82), channel_id=1, source_target_pairs={{0,1},{1,0},{2,3},{3,2},{4,5},{5,4},{6,7},{7,6},{8,9},{9,8},{10,11... | collective-permute-start | bytes 2752520 | tf_op jit(solution)/shard_map/ppermute | solution.py:37
  37.8 8.5 %collective-permute-start.13 = (bf16[32,3584]{1,0:T(8,128)(2,1)S(1)}, bf16[32,3584]{1,0:T(8,128)(2,1)S(1)}, u32[]{:S(2)}, u32[]{:S(2)}) collective-permute-start(bf16[32,3584]{1,0:T(8,128)(2,1)S(1)} %get-tuple-element.158), channel_id=1, source_target_pairs={{0,2},{1,3},{4,0},{5,1},{8,4},{9,5},{12,8},{13,9},{14,12},{15,13},... | collective-permute-start | bytes 688136 | tf_op jit(solution)/shard_map/ppermute | solution.py:75
  38.5 8.5 %collective-permute-start.9 = (bf16[32,3584]{1,0:T(8,128)(2,1)S(1)}, bf16[32,3584]{1,0:T(8,128)(2,1)S(1)}, u32[]{:S(2)}, u32[]{:S(2)}) collective-permute-start(bf16[32,3584]{1,0:T(8,128)(2,1)S(1)} %get-tuple-element.159), channel_id=1, source_target_pairs={{0,4},{1,5},{4,8},{5,9},{8,12},{9,13},{12,14},{13,15},{14,10},{15,... | collective-permute-start | bytes 688136 | tf_op jit(solution)/shard_map/ppermute | solution.py:75
  39.9 18.5 %collective-permute-start.16 = (bf16[128,3584]{1,0:T(8,128)(2,1)S(1)}, bf16[128,3584]{1,0:T(8,128)(2,1)S(1)}, u32[]{:S(2)}, u32[]{:S(2)}) collective-permute-start(bf16[128,3584]{1,0:T(8,128)(2,1)S(1)} %get-tuple-element.99), channel_id=1, source_target_pairs={{0,1},{1,0},{2,3},{3,2},{4,5},{5,4},{6,7},{7,6},{8,9},{9,8},{10,11... | collective-permute-start | bytes 2752520 | tf_op jit(solution)/shard_map/ppermute | solution.py:37
  39.9 11.8 %collective-permute-start.17 = (bf16[32,3584]{1,0:T(8,128)(2,1)S(1)}, bf16[32,3584]{1,0:T(8,128)(2,1)S(1)}, u32[]{:S(2)}, u32[]{:S(2)}) collective-permute-start(bf16[32,3584]{1,0:T(8,128)(2,1)S(1)} %get-tuple-element.161), channel_id=1, source_target_pairs={{0,4},{1,5},{4,8},{5,9},{8,12},{9,13},{12,14},{13,15},{14,10},{15,... | collective-permute-start | bytes 688136 | tf_op jit(solution)/shard_map/ppermute | solution.py:75
  39.9 11.8 %collective-permute-start.21 = (bf16[32,3584]{1,0:T(8,128)(2,1)S(1)}, bf16[32,3584]{1,0:T(8,128)(2,1)S(1)}, u32[]{:S(2)}, u32[]{:S(2)}) collective-permute-start(bf16[32,3584]{1,0:T(8,128)(2,1)S(1)} %get-tuple-element.160), channel_id=1, source_target_pairs={{0,2},{1,3},{4,0},{5,1},{8,4},{9,5},{12,8},{13,9},{14,12},{15,13},... | collective-permute-start | bytes 688136 | tf_op jit(solution)/shard_map/ppermute | solution.py:75
  46.3 7.6 %collective-permute-start.7 = (bf16[128,3584]{1,0:T(8,128)(2,1)S(1)}, bf16[128,3584]{1,0:T(8,128)(2,1)S(1)}, u32[]{:S(2)}, u32[]{:S(2)}) collective-permute-start(bf16[128,3584]{1,0:T(8,128)(2,1)S(1)} %get-tuple-element.91), channel_id=1, source_target_pairs={{0,1},{1,0},{2,3},{3,2},{4,5},{5,4},{6,7},{7,6},{8,9},{9,8},{10,11... | collective-permute-start | bytes 2752520 | tf_op jit(solution)/shard_map/ppermute | solution.py:37
  47.2 9.5 %collective-permute-start.10 = (bf16[32,3584]{1,0:T(8,128)(2,1)S(1)}, bf16[32,3584]{1,0:T(8,128)(2,1)S(1)}, u32[]{:S(2)}, u32[]{:S(2)}) collective-permute-start(bf16[32,3584]{1,0:T(8,128)(2,1)S(1)} %get-tuple-element.157), channel_id=1, source_target_pairs={{0,4},{1,5},{4,8},{5,9},{8,12},{9,13},{12,14},{13,15},{14,10},{15,... | collective-permute-start | bytes 688136 | tf_op jit(solution)/shard_map/ppermute | solution.py:75
  51.9 9.7 %collective-permute-start.18 = (bf16[32,3584]{1,0:T(8,128)(2,1)S(1)}, bf16[32,3584]{1,0:T(8,128)(2,1)S(1)}, u32[]{:S(2)}, u32[]{:S(2)}) collective-permute-start(bf16[32,3584]{1,0:T(8,128)(2,1)S(1)} %get-tuple-element.153), channel_id=1, source_target_pairs={{0,4},{1,5},{4,8},{5,9},{8,12},{9,13},{12,14},{13,15},{14,10},{15,... | collective-permute-start | bytes 688136 | tf_op jit(solution)/shard_map/ppermute | solution.py:75
  53.5 15.2 %collective-permute-start.22 = (bf16[32,3584]{1,0:T(8,128)(2,1)S(1)}, bf16[32,3584]{1,0:T(8,128)(2,1)S(1)}, u32[]{:S(2)}, u32[]{:S(2)}) collective-permute-start(bf16[32,3584]{1,0:T(8,128)(2,1)S(1)} %get-tuple-element.152), channel_id=1, source_target_pairs={{0,2},{1,3},{4,0},{5,1},{8,4},{9,5},{12,8},{13,9},{14,12},{15,13},... | collective-permute-start | bytes 688136 | tf_op jit(solution)/shard_map/ppermute | solution.py:75
  54.0 9.6 %collective-permute-start.14 = (bf16[32,3584]{1,0:T(8,128)(2,1)S(1)}, bf16[32,3584]{1,0:T(8,128)(2,1)S(1)}, u32[]{:S(2)}, u32[]{:S(2)}) collective-permute-start(bf16[32,3584]{1,0:T(8,128)(2,1)S(1)} %get-tuple-element.156), channel_id=1, source_target_pairs={{0,2},{1,3},{4,0},{5,1},{8,4},{9,5},{12,8},{13,9},{14,12},{15,13},... | collective-permute-start | bytes 688136 | tf_op jit(solution)/shard_map/ppermute | solution.py:75
  56.7 9.7 %collective-permute-start.11 = (bf16[32,3584]{1,0:T(8,128)(2,1)S(1)}, bf16[32,3584]{1,0:T(8,128)(2,1)S(1)}, u32[]{:S(2)}, u32[]{:S(2)}) collective-permute-start(bf16[32,3584]{1,0:T(8,128)(2,1)S(1)} %add_convert_fusion.9), channel_id=1, source_target_pairs={{0,4},{1,5},{4,8},{5,9},{8,12},{9,13},{12,14},{13,15},{14,10},{15,... | collective-permute-start | bytes 688136 | tf_op jit(solution)/shard_map/ppermute | solution.py:75
  61.7 9.7 %collective-permute-start.19 = (bf16[32,3584]{1,0:T(8,128)(2,1)S(1)}, bf16[32,3584]{1,0:T(8,128)(2,1)S(1)}, u32[]{:S(2)}, u32[]{:S(2)}) collective-permute-start(bf16[32,3584]{1,0:T(8,128)(2,1)S(1)} %add_convert_fusion.3), channel_id=1, source_target_pairs={{0,4},{1,5},{4,8},{5,9},{8,12},{9,13},{12,14},{13,15},{14,10},{15,... | collective-permute-start | bytes 688136 | tf_op jit(solution)/shard_map/ppermute | solution.py:75
  66.6 9.7 %collective-permute-start.12 = (bf16[32,3584]{1,0:T(8,128)(2,1)S(1)}, bf16[32,3584]{1,0:T(8,128)(2,1)S(1)}, u32[]{:S(2)}, u32[]{:S(2)}) collective-permute-start(bf16[32,3584]{1,0:T(8,128)(2,1)S(1)} %get-tuple-element.155), channel_id=1, source_target_pairs={{0,4},{1,5},{4,8},{5,9},{8,12},{9,13},{12,14},{13,15},{14,10},{15,... | collective-permute-start | bytes 688136 | tf_op jit(solution)/shard_map/ppermute | solution.py:75
  68.3 8.0 %collective-permute-start.15 = (bf16[32,3584]{1,0:T(8,128)(2,1)S(1)}, bf16[32,3584]{1,0:T(8,128)(2,1)S(1)}, u32[]{:S(2)}, u32[]{:S(2)}) collective-permute-start(bf16[32,3584]{1,0:T(8,128)(2,1)S(1)} %get-tuple-element.154), channel_id=1, source_target_pairs={{0,2},{1,3},{4,0},{5,1},{8,4},{9,5},{12,8},{13,9},{14,12},{15,13},... | collective-permute-start | bytes 688136 | tf_op jit(solution)/shard_map/ppermute | solution.py:75
  71.5 9.7 %collective-permute-start.20 = (bf16[32,3584]{1,0:T(8,128)(2,1)S(1)}, bf16[32,3584]{1,0:T(8,128)(2,1)S(1)}, u32[]{:S(2)}, u32[]{:S(2)}) collective-permute-start(bf16[32,3584]{1,0:T(8,128)(2,1)S(1)} %get-tuple-element.151), channel_id=1, source_target_pairs={{0,4},{1,5},{4,8},{5,9},{8,12},{9,13},{12,14},{13,15},{14,10},{15,... | collective-permute-start | bytes 688136 | tf_op jit(solution)/shard_map/ppermute | solution.py:75
  73.2 8.0 %collective-permute-start.23 = (bf16[32,3584]{1,0:T(8,128)(2,1)S(1)}, bf16[32,3584]{1,0:T(8,128)(2,1)S(1)}, u32[]{:S(2)}, u32[]{:S(2)}) collective-permute-start(bf16[32,3584]{1,0:T(8,128)(2,1)S(1)} %get-tuple-element.150), channel_id=1, source_target_pairs={{0,2},{1,3},{4,0},{5,1},{8,4},{9,5},{12,8},{13,9},{14,12},{15,13},... | collective-permute-start | bytes 688136 | tf_op jit(solution)/shard_map/ppermute | solution.py:75
  78.1 8.4 %collective-permute-start.24 = (bf16[32,3584]{1,0:T(8,128)(2,1)S(1)}, bf16[32,3584]{1,0:T(8,128)(2,1)S(1)}, u32[]{:S(2)}, u32[]{:S(2)}) collective-permute-start(bf16[32,3584]{1,0:T(8,128)(2,1)S(1)} %get-tuple-element.108.refs_0_), channel_id=1, source_target_pairs={{0,4},{1,5},{4,8},{5,9},{8,12},{9,13},{12,14},{13,15},{14,10},{15,... | collective-permute-start | bytes 688136 | tf_op jit(solution)/shard_map/ppermute | solution.py:75
  83.0 8.5 %collective-permute-start.26 = (bf16[32,3584]{1,0:T(8,128)(2,1)S(1)}, bf16[32,3584]{1,0:T(8,128)(2,1)S(1)}, u32[]{:S(2)}, u32[]{:S(2)}) collective-permute-start(bf16[32,3584]{1,0:T(8,128)(2,1)S(1)} %get-tuple-element.109.refs_1_), channel_id=1, source_target_pairs={{0,4},{1,5},{4,8},{5,9},{8,12},{9,13},{12,14},{13,15},{14,10},{15,... | collective-permute-start | bytes 688136 | tf_op jit(solution)/shard_map/ppermute | solution.py:75
  84.6 8.5 %collective-permute-start.27 = (bf16[32,3584]{1,0:T(8,128)(2,1)S(1)}, bf16[32,3584]{1,0:T(8,128)(2,1)S(1)}, u32[]{:S(2)}, u32[]{:S(2)}) collective-permute-start(bf16[32,3584]{1,0:T(8,128)(2,1)S(1)} %get-tuple-element.109.refs_1_), channel_id=1, source_target_pairs={{0,2},{1,3},{4,0},{5,1},{8,4},{9,5},{12,8},{13,9},{14,12},{15,13},... | collective-permute-start | bytes 688136 | tf_op jit(solution)/shard_map/ppermute | solution.py:75
  86.6 8.4 %collective-permute-start.28 = (bf16[32,3584]{1,0:T(8,128)(2,1)S(1)}, bf16[32,3584]{1,0:T(8,128)(2,1)S(1)}, u32[]{:S(2)}, u32[]{:S(2)}) collective-permute-start(bf16[32,3584]{1,0:T(8,128)(2,1)S(1)} %collective-permute-done.24.refs_0_), channel_id=1, source_target_pairs={{0,4},{1,5},{4,8},{5,9},{8,12},{9,13},{12,14},{13,15},{14,10},{15,... | collective-permute-start | bytes 688136 | tf_op jit(solution)/shard_map/ppermute | solution.py:75
  98.7 22.8 %collective-permute-start.40 = (bf16[128,3584]{1,0:T(8,128)(2,1)S(1)}, bf16[128,3584]{1,0:T(8,128)(2,1)S(1)}, u32[]{:S(2)}, u32[]{:S(2)}) collective-permute-start(bf16[128,3584]{1,0:T(8,128)(2,1)S(1)} %get-tuple-element.121), channel_id=1, source_target_pairs={{0,1},{1,0},{2,3},{3,2},{4,5},{5,4},{6,7},{7,6},{8,9},{9,8},{10,11... | collective-permute-start | bytes 2752520 | tf_op jit(solution)/shard_map/ppermute | solution.py:37
  98.7 8.5 %collective-permute-start.30 = (bf16[32,3584]{1,0:T(8,128)(2,1)S(1)}, bf16[32,3584]{1,0:T(8,128)(2,1)S(1)}, u32[]{:S(2)}, u32[]{:S(2)}) collective-permute-start(bf16[32,3584]{1,0:T(8,128)(2,1)S(1)} %collective-permute-done.26.refs_2_), channel_id=1, source_target_pairs={{0,4},{1,5},{4,8},{5,9},{8,12},{9,13},{12,14},{13,15},{14,10},{15,... | collective-permute-start | bytes 688136 | tf_op jit(solution)/shard_map/ppermute | solution.py:75
  99.7 15.1 %collective-permute-start.36 = (bf16[64,3584]{1,0:T(8,128)(2,1)S(1)}, bf16[64,3584]{1,0:T(8,128)(2,1)S(1)}, u32[]{:S(2)}, u32[]{:S(2)}) collective-permute-start(bf16[64,3584]{1,0:T(8,128)(2,1)S(1)} %get-tuple-element.110), channel_id=1, source_target_pairs={{0,1},{1,0},{2,3},{3,2},{4,5},{5,4},{6,7},{7,6},{8,9},{9,8},{10,11... | collective-permute-start | bytes 1376264 | tf_op jit(solution)/shard_map/ppermute | solution.py:37
  99.9 7.9 %collective-permute-start.31 = (bf16[32,3584]{1,0:T(8,128)(2,1)S(1)}, bf16[32,3584]{1,0:T(8,128)(2,1)S(1)}, u32[]{:S(2)}, u32[]{:S(2)}) collective-permute-start(bf16[32,3584]{1,0:T(8,128)(2,1)S(1)} %collective-permute-done.27.refs_3_), channel_id=1, source_target_pairs={{0,2},{1,3},{4,0},{5,1},{8,4},{9,5},{12,8},{13,9},{14,12},{15,13},... | collective-permute-start | bytes 688136 | tf_op jit(solution)/shard_map/ppermute | solution.py:75
  101.0 11.1 %collective-permute-start.32 = (bf16[32,3584]{1,0:T(8,128)(2,1)S(1)}, bf16[32,3584]{1,0:T(8,128)(2,1)S(1)}, u32[]{:S(2)}, u32[]{:S(2)}) collective-permute-start(bf16[32,3584]{1,0:T(8,128)(2,1)S(1)} %collective-permute-done.28.refs_0_), channel_id=1, source_target_pairs={{0,4},{1,5},{4,8},{5,9},{8,12},{9,13},{12,14},{13,15},{14,10},{15,... | collective-permute-start | bytes 688136 | tf_op jit(solution)/shard_map/ppermute | solution.py:75
  107.7 11.1 %collective-permute-start.34 = (bf16[32,3584]{1,0:T(8,128)(2,1)S(1)}, bf16[32,3584]{1,0:T(8,128)(2,1)S(1)}, u32[]{:S(2)}, u32[]{:S(2)}) collective-permute-start(bf16[32,3584]{1,0:T(8,128)(2,1)S(1)} %collective-permute-done.30.refs_2_), channel_id=1, source_target_pairs={{0,4},{1,5},{4,8},{5,9},{8,12},{9,13},{12,14},{13,15},{14,10},{15,... | collective-permute-start | bytes 688136 | tf_op jit(solution)/shard_map/ppermute | solution.py:75
  113.9 7.6 %collective-permute-start.37 = (bf16[32,3584]{1,0:T(8,128)(2,1)S(1)}, bf16[32,3584]{1,0:T(8,128)(2,1)S(1)}, u32[]{:S(2)}, u32[]{:S(2)}) collective-permute-start(bf16[32,3584]{1,0:T(8,128)(2,1)S(1)} %collective-permute-done.32.refs_0_), channel_id=1, source_target_pairs={{0,4},{1,5},{4,8},{5,9},{8,12},{9,13},{12,14},{13,15},{14,10},{15,... | collective-permute-start | bytes 688136 | tf_op jit(solution)/shard_map/ppermute | solution.py:75
  118.8 15.5 %collective-permute-start.42 = (bf16[128,3584]{1,0:T(8,128)(2,1)S(1)}, bf16[128,3584]{1,0:T(8,128)(2,1)S(1)}, u32[]{:S(2)}, u32[]{:S(2)}) collective-permute-start(bf16[128,3584]{1,0:T(8,128)(2,1)S(1)} %get-tuple-element.132), channel_id=1, source_target_pairs={{0,1},{1,0},{2,3},{3,2},{4,5},{5,4},{6,7},{7,6},{8,9},{9,8},{10,11... | collective-permute-start | bytes 2752520 | tf_op jit(solution)/shard_map/ppermute | solution.py:37
  126.2 8.1 %collective-permute-start.43 = (bf16[128,3584]{1,0:T(8,128)(2,1)S(1)}, bf16[128,3584]{1,0:T(8,128)(2,1)S(1)}, u32[]{:S(2)}, u32[]{:S(2)}) collective-permute-start(bf16[128,3584]{1,0:T(8,128)(2,1)S(1)} %get-tuple-element.142), channel_id=1, source_target_pairs={{0,1},{1,0},{2,3},{3,2},{4,5},{5,4},{6,7},{7,6},{8,9},{9,8},{10,11... | collective-permute-start | bytes 2752520 | tf_op jit(solution)/shard_map/ppermute | solution.py:37
  126.3 8.0 %collective-permute-start.39 = (bf16[32,3584]{1,0:T(8,128)(2,1)S(1)}, bf16[32,3584]{1,0:T(8,128)(2,1)S(1)}, u32[]{:S(2)}, u32[]{:S(2)}) collective-permute-start(bf16[32,3584]{1,0:T(8,128)(2,1)S(1)} %collective-permute-done.34.refs_2_), channel_id=1, source_target_pairs={{0,4},{1,5},{4,8},{5,9},{8,12},{9,13},{12,14},{13,15},{14,10},{15,... | collective-permute-start | bytes 688136 | tf_op jit(solution)/shard_map/ppermute | solution.py:75
  127.3 11.6 %collective-permute-start.38 = (bf16[32,3584]{1,0:T(8,128)(2,1)S(1)}, bf16[32,3584]{1,0:T(8,128)(2,1)S(1)}, u32[]{:S(2)}, u32[]{:S(2)}) collective-permute-start(bf16[32,3584]{1,0:T(8,128)(2,1)S(1)} %collective-permute-done.37.refs_0_), channel_id=1, source_target_pairs={{0,1},{1,0},{2,3},{3,2},{4,5},{5,4},{6,7},{7,6},{8,9},{9,8},{10,11... | collective-permute-start | bytes 688136 | tf_op jit(solution)/shard_map/ppermute | solution.py:37
  (23 other events, 277.7 us)

commit v5 on v4

--- a/solution.py
+++ b/solution.py
@@ -75,14 +75,16 @@
     return lax.ppermute(value, "latent", pairs)
 
 
-def gather_table(row, size, late):
-    pieces, step = [row], 1
+def gather_table(row, size):
+    stages, step = [], 1
+    pieces = [row]
     while step < size:
         if step > 1:
-            pieces = [jnp.concatenate([after(piece, late) for piece in pieces], axis=0)]
+            pieces = [jnp.concatenate(pieces, axis=0)]
         pieces += [swap(pieces[0], step * k, size) for k in range(1, min(4, size // step))]
+        stages.append(pieces)
         step *= len(pieces)
-    return pieces
+    return stages
 
 
 def ordered_rows(size, rows, by_latent, by_slot):
@@ -167,7 +169,7 @@
     multiply(by_slot, right_ref, outs)
 
 
-def product(coef, right, size, rows, picks=None, table=()):
+def product(coef, right, size, rows, vmem, picks=None, table=()):
     tokens, latents = coef.shape
     width = right.shape[1]
     tile = 512
@@ -196,7 +198,7 @@
         out_specs=out_specs,
         out_shape=out_shape,
         scratch_shapes=scratch,
-        compiler_params=params(24),
+        compiler_params=params(vmem),
         cost_estimate=cost(
             2 * latents * tokens * width, 2 * (tokens * width + latents * (tokens + width))
         ),
@@ -228,8 +230,8 @@
     fresh[...] = gradient.astype(fresh.dtype)
 
 
-def dec_kernel(code_ref, w_ref, m_ref, v_ref, fresh_ref, *refs):
-    parts, (w_out, m_out, v_out, block) = refs[:-4], refs[-4:]
+def dec_kernel(code_ref, w_ref, m_ref, v_ref, fresh_ref, enc_block, *refs):
+    parts, (w_out, m_out, v_out, blocks) = refs[:-4], refs[-4:]
     reset = code_ref[...] != KEPT
     w, m, v = adam_update(w_ref[...], m_ref[...], v_ref[...], read_gradient(parts))
     w = jnp.where(reset, fresh_ref[...].astype(jnp.float32), w)
@@ -237,10 +239,11 @@
     w_out[...] = w
     m_out[...] = jnp.where(reset, 0.0, m)
     v_out[...] = jnp.where(reset, 0.0, v)
-    block[...] = w.astype(block.dtype)
-
-
-def update(kernel, code, states, fresh, parts, extra, name):
+    blocks[0] = enc_block[...]
+    blocks[1] = w.astype(blocks.dtype)
+
+
+def update(kernel, code, states, others, parts, last_shapes, name):
     rows, width = states[0].shape
     tile = 16
 
@@ -248,109 +251,82 @@
         skipped = (value.shape[0] - rows) // tile
         return pl.BlockSpec((tile, value.shape[1]), lambda i: (i + skipped, 0))
 
-    operands = [code] + list(states) + list(fresh) + list(parts)
-    out_spec = pl.BlockSpec((tile, width), lambda i: (i, 0))
-    wide = jax.ShapeDtypeStruct((rows, width), jnp.float32)
-    narrow = jax.ShapeDtypeStruct((rows, width), jnp.bfloat16)
+    operands = [code] + list(states) + list(others) + list(parts)
+    out_shape = [jax.ShapeDtypeStruct((rows, width), jnp.float32)] * 3
+    out_specs = [pl.BlockSpec((tile, width), lambda i: (i, 0))] * 3
+    for pair in last_shapes:
+        lead = (2,) if pair else ()
+        out_shape.append(jax.ShapeDtypeStruct(lead + (rows, width), jnp.bfloat16))
+        out_specs.append(
+            pl.BlockSpec(lead + (tile, width), lambda i, pair=pair: (0, i, 0) if pair else (i, 0))
+        )
     return pl.pallas_call(
         kernel,
         grid=(rows // tile,),
         in_specs=[last_rows(value) for value in operands],
-        out_specs=(out_spec,) * (3 + extra),
-        out_shape=(wide,) * 3 + (narrow,) * extra,
+        out_specs=out_specs,
+        out_shape=out_shape,
         cost_estimate=cost(40 * rows * width, 40 * rows * width),
         compiler_params=params(12),
         name=name,
     )(*operands)
 
 
-def place_kernel(plan, size, rows, wholes, count, *refs):
-    pieces, refs = refs[:count], refs[count:]
-    outs, (stage, sems_in, sems_out, sems_pack) = refs[wholes:-4], refs[-4:]
-    coming, going = [], []
-    for i, (piece, block, whole, offset, other_core, pack) in enumerate(plan):
-        source = pieces[piece].at[pl.ds(block * rows, rows)]
-        coming.append(pltpu.make_async_copy(source, stage.at[i], sems_in.at[i]))
+def place_kernel(plan, size, rows, count, *refs):
+    pieces, outs, sems = refs[:count], refs[-3:-1], refs[-1]
+    copies = []
+    for i, (offset, other_core, column) in enumerate(plan):
         start = pl.multiple_of(owner_at(offset, other_core, size) * rows, rows)
-        target = outs[whole].at[pl.ds(start, rows)]
-        copies = [pltpu.make_async_copy(stage.at[i], target, sems_out.at[i])]
-        if pack is not None:
-            target = outs[2].at[pl.ds(pack * rows, rows)]
-            copies.append(pltpu.make_async_copy(stage.at[i], target, sems_pack.at[pack]))
-        going.append(copies)
-    for copy in coming:
+        for whole, out in enumerate(outs):
+            source = pieces[i].at[pl.ds(whole * rows, rows)]
+            target = out.at[pl.ds(start, rows), pl.ds(column, pieces[i].shape[1])]
+            copies.append(pltpu.make_async_copy(source, target, sems.at[i, whole]))
+    for copy in copies:
         copy.start()
-    for copy, copies in zip(coming, going):
+    for copy in copies:
         copy.wait()
-        for later in reversed(copies):
-            later.start()
-    for copies in going:
-        for copy in copies:
-            copy.wait()
-
-
-def place(near, far, wholes, size, rows, pack=True):
-    operands = [block for _, _, block in near] + [value for value, _ in far]
-    plan = []
-    for i, (whole, offset, _) in enumerate(near):
-        plan.append((i, 0, whole, offset, 0, i if pack else None))
-    for i, (_, places) in enumerate(far):
-        for block, (whole, offset) in enumerate(places):
-            plan.append((len(near) + i, block, whole, offset, 1, None))
-    width, dtype = operands[0].shape[1], operands[0].dtype
-    out_shape = [jax.ShapeDtypeStruct((size * rows, width), dtype)] * 2
-    packed = len(near) if pack else 0
-    if packed:
-        out_shape.append(jax.ShapeDtypeStruct((packed * rows, width), dtype))
+
+
+def place(pieces, wholes, size, rows, width):
+    operands = [value for _, _, _, value in pieces]
+    plan = [piece[:3] for piece in pieces]
+    count = len(operands)
     first = wholes is None
-    count = len(operands)
     if not first:
         operands += list(wholes)
     anywhere = pl.BlockSpec(memory_space=pl.ANY)
-    out = pl.pallas_call(
-        functools.partial(place_kernel, plan, size, rows, 0 if first else 2, count),
-        out_shape=out_shape,
+    return pl.pallas_call(
+        functools.partial(place_kernel, plan, size, rows, count),
+        out_shape=[jax.ShapeDtypeStruct((size * rows, width), operands[0].dtype)] * 2,
         in_specs=[anywhere] * len(operands),
-        out_specs=[anywhere] * len(out_shape),
-        scratch_shapes=[
-            pltpu.VMEM((len(plan), rows, width), dtype),
-            pltpu.SemaphoreType.DMA((len(plan),)),
-            pltpu.SemaphoreType.DMA((len(plan),)),
-            pltpu.SemaphoreType.DMA((max(packed, 1),)),
-        ],
+        out_specs=[anywhere] * 2,
+        scratch_shapes=[pltpu.SemaphoreType.DMA((count, 2))],
         input_output_aliases={} if first else {count: 0, count + 1: 1},
-        compiler_params=params(10),
-        cost_estimate=cost(0, 4 * len(plan) * rows * width),
+        compiler_params=params(4),
+        cost_estimate=cost(0, 8 * count * rows * width),
         name="place",
     )(*operands)
-    return (out[:2], out[2]) if packed else (out, None)
-
-
-def gathered(blocks, size, rows):
+
+
+def gathered(block, size, rows):
     chips = size // 2
-    left_hops = (chips - 1) // 2
-    moving = [[block, block] for block in blocks]
-    near = [(whole, 0, block) for whole, block in enumerate(blocks)]
-    wholes, far = None, []
-    for hop in range(1, chips // 2 + 1):
-        sides = ((1, -hop), (-1, hop))[: 1 + (hop <= left_hops)]
-        for whole in range(2):
-            moving[whole] = [shift(moving[whole][i], step, size) for i, (step, _) in enumerate(sides)]
-        held = [value for _, _, value in near]
-        held, moving[0] = lax.optimization_barrier((held, moving[0]))
-        near = [(whole, offset, value) for (whole, offset, _), value in zip(near, held)]
-        wholes, packed = place(near, far[:-1], wholes, size, rows)
-        moving[1] = after(moving[1], packed)
-        far = far[-1:] + [(swap(packed, 1, size), [(whole, offset) for whole, offset, _ in near])]
-        near = [
-            (whole, offset, moving[whole][i])
-            for whole in range(2)
-            for i, (_, offset) in enumerate(sides)
-        ]
-    last_far = [(swap(value, 1, size), [(whole, offset)]) for whole, offset, value in near]
-    wholes, _ = place(near, far, wholes, size, rows, pack=False)
-    wholes, _ = place([], last_far, wholes, size, rows, pack=False)
-    return wholes
+    width = block.shape[1]
+    half = width // 2
+    hops = chips // 2
+    right = left = block
+    near, far, wholes = [(0, 0, 0, block)], [], None
+    for hop in range(1, hops + 1):
+        if hop == hops:
+            right, left = right[:, :half], left[:, half:]
+        right, left = shift(right, 1, size), shift(left, -1, size)
+        sent = [(offset, 1, column, swap(value, 1, size)) for offset, _, column, value in near]
+        wholes = place(near + far, wholes, size, rows, width)
+        far = sent
+        right, left, wholes = lax.optimization_barrier((right, left, wholes))
+        near = [(-hop, 0, 0, right), (hop, 0, half if hop == hops else 0, left)]
+    sent = [(offset, 1, column, swap(value, 1, size)) for offset, _, column, value in near]
+    wholes = place(near + far, wholes, size, rows, width)
+    return place(sent, wholes, size, rows, width)
 
 
 def shards(
@@ -368,49 +344,64 @@
     pick_rows,
     send_count,
 ):
-    rows = enc_w.shape[0]
+    rows, width = enc_w.shape
+    half = width // 2
     size = lax.axis_size("latent")
     chips = size // 2
-    own = jnp.concatenate([send_count, dead_order], axis=1)
-    dec = product(after(latent_act, own), out_grad, size, rows)
-    table = gather_table(own, size, dec[0])
-    dec_core = [swap(dec[0], 1, size), swap(dec[2], 1, size)]
-    dec_kept = [dec[1], dec[3]]
-
-    def advance(moving, step, kept, from_core, slot):
-        came = shift(moving, step, size).astype(jnp.float32)
-        return (came + term(kept, from_core, slot, rows)).astype(jnp.bfloat16)
+    stages = gather_table(jnp.concatenate([send_count, dead_order], axis=1), size)
+    table = stages[-1]
+    dec = product(latent_act, out_grad, size, rows, 56)
+    dec_far = after(dec[0], *stages[0])
+    dec_kept, dec_core = [dec[1], dec[3]], [swap(dec_far, 1, size), swap(dec[2], 1, size)]
 
     def begin(kept, from_core):
-        return [term(kept, from_core, slot, rows).astype(jnp.bfloat16) for slot in range(2)]
-
-    dec_moving = begin(after(dec_kept, table[0]), dec_core)
+        far = term(kept, from_core, 0, rows).astype(jnp.bfloat16)
+        return [far[:, :half], far[:, half:]]
+
+    def travel(moving):
+        return [shift(moving[0], 1, size), shift(moving[1], -1, size)]
+
+    def advance(came, kept, from_core, hop):
+        moving = []
+        for side, value in enumerate(came):
+            value = value.astype(jnp.float32)
+            if value.shape[1] < width:
+                pads = ((0, 0, 0), (0, half, 0) if side == 0 else (half, 0, 0))
+                value = lax.pad(value, jnp.float32(0), pads)
+            value = value + term(kept, from_core, 2 * hop - side, rows)
+            moving.append(value.astype(jnp.bfloat16))
+        return moving
+
+    dec_moving = begin(dec_kept, dec_core)
     *enc, code = product(
-        after(enc_coef, *dec_moving), x_rows, size, rows, pick_rows[0].T, table
+        after(enc_coef, *dec_moving), x_rows, size, rows, 24, pick_rows[0].T, table
     )
-    enc_core = [swap(enc[0], 1, size), swap(enc[2], 1, size)]
-    enc_kept = [enc[1], enc[3]]
-    dec_kept = after(dec_kept, enc[0])
-    enc_moving = begin(enc_kept, enc_core)
-    for slot in range(2, chips - 1):
-        side = slot % 2
-        step = 1 - 2 * side
-        dec_moving[side] = advance(dec_moving[side], step, dec_kept, dec_core, slot)
-        enc_moving[side] = advance(enc_moving[side], step, enc_kept, enc_core, slot)
-    dec_parts, enc_parts = (
-        [kept[1], from_core[1], shift(moving[0], 1, size), shift(moving[1], -1, size)]
-        for kept, from_core, moving in (
-            (dec_kept, dec_core, dec_moving),
-            (enc_kept, enc_core, enc_moving),
-        )
+    dec_came = travel(dec_moving)
+    enc_far, enc_near = after((enc[0], enc[2]), *dec_came)
+    enc_kept, enc_core = [enc[1], enc[3]], [swap(enc_far, 1, size), swap(enc_near, 1, size)]
+    enc_came = travel(begin(enc_kept, enc_core))
+    for hop in range(1, chips // 2):
+        dec_came = travel(advance(dec_came, dec_kept, dec_core, hop))
+        enc_came = travel(advance(enc_came, enc_kept, enc_core, hop))
+    enc_out, enc_mo, enc_vo, enc_block, fresh = update(
+        enc_kernel,
+        code,
+        (enc_w, enc_m, enc_v),
+        (),
+        [enc_kept[1], enc_core[1]] + enc_came,
+        (False, False),
+        "enc_update",
     )
-    enc_out, enc_mo, enc_vo, enc_block, fresh = update(
-        enc_kernel, code, (enc_w, enc_m, enc_v), (), enc_parts, 2, "enc_update"
+    dec_out, dec_mo, dec_vo, blocks = update(
+        dec_kernel,
+        code,
+        (dec_w, dec_m, dec_v),
+        (fresh, enc_block),
+        [dec_kept[1], dec_core[1]] + dec_came,
+        (True,),
+        "dec_update",
     )
-    dec_out, dec_mo, dec_vo, dec_block = update(
-        dec_kernel, code, (dec_w, dec_m, dec_v), (fresh,), dec_parts, 1, "dec_update"
-    )
-    enc_full, dec_full = gathered((enc_block, dec_block), size, rows)
+    enc_full, dec_full = gathered(blocks.reshape(2 * rows, width), size, rows)
     return (enc_out, enc_mo, enc_vo, dec_out, dec_mo, dec_vo, enc_full, dec_full)
 
 

time: 141 us -> 124 us (0.88)
  Pallas kernels: 36.4 us -> 26.4 us
  local copies, waits for them, and re-layouts: 4.36 us -> 1.36 us
  starting transfers between devices: 37.3 us -> 34.5 us
  waiting for transfers between devices: 59.5 us -> 57.8 us
    pallas_call x6, Pallas kernels: 19.6 us -> 6.39 us  [place(): pl.pallas_call(functools.partial(place_kernel, plan, size, rows, count),...]
    ppermute x16 -> x19, waiting for transfers between devices: 10.5 us -> 3.34 us  [swap(): return lax.ppermute(value, 'latent', [(i, i ^ bits) for i in range(size)])]
    ppermute x28 -> x24, waiting for transfers between devices: 49.1 us -> 54.4 us  [shift(): return lax.ppermute(value, 'latent', pairs)]
    ppermute x28 -> x24, starting transfers between devices: 28.6 us -> 24.3 us  [shift(): return lax.ppermute(value, 'latent', pairs)]
    pallas_call x2, Pallas kernels: 13.3 us -> 16.5 us  [product(): pl.pallas_call(kernel, grid=(width // tile,), in_specs=in_specs, out_spec...]
    unnamed x22 -> x30, local copies, waits for them, and re-layouts: 4.36 us -> 1.29 us
    ppermute x16 -> x19, starting transfers between devices: 8.62 us -> 10.2 us  [swap(): return lax.ppermute(value, 'latent', [(i, i ^ bits) for i in range(size)])]
  transfers between devices with their start and end apart: 44 -> 43, of which waited for: 27 -> 21; matrix products, arithmetic and copies ran while one was open for 1% -> 2% of each run, Pallas kernels for 13% -> 19%
where the time goes in v5:
time: 124 us
  waiting for transfers between devices  57.8 us (47%)
  starting transfers between devices  34.5 us (28%)
  Pallas kernels  26.4 us (21%)
  other arithmetic  2.98 us (2%)
  local copies, waits for them, and re-layouts  1.36 us (1%)
    ppermute x24, waiting for transfers between devices, shift(): return lax.ppermute(value, 'latent', pairs)  54.4 us
    ppermute x24, starting transfers between devices, shift(): return lax.ppermute(value, 'latent', pairs)  24.3 us
    pallas_call x2, Pallas kernels, product(): pl.pallas_call(kernel, grid=(width // tile,), in_specs=in_specs, out_spec...  16.5 us
    ppermute x19, starting transfers between devices, swap(): return lax.ppermute(value, 'latent', [(i, i ^ bits) for i in range(size)])  10.2 us
    pallas_call x6, Pallas kernels, place(): pl.pallas_call(functools.partial(place_kernel, plan, size, rows, count),...  6.39 us
    pallas_call x2, Pallas kernels, update(): pl.pallas_call(kernel, grid=(rows // tile,), in_specs=[last_rows(value) f...  3.51 us
    ppermute x19, waiting for transfers between devices, swap(): return lax.ppermute(value, 'latent', [(i, i ^ bits) for i in range(size)])  3.34 us
  transfers between devices with their start and end apart: 43, of which 21 were waited for; matrix products, arithmetic and copies ran while one was open for 2% of the time, Pallas kernels for 19%

profile of v5, /device:TPU:0, one launch (start us, length us, event | category | flops | bytes accessed | tf_op | source)
XLA Modules:
  0.0 124.0 jit_solution(17683746372447096967)
XLA Ops:
  1.6 2.5 %collective-permute-start.2 = (s32[1,48]{1,0:T(1,128)S(1)}, s32[1,48]{1,0:T(1,128)S(1)}, u32[]{:S(2)}, u32[]{:S(2)}) collective-permute-start(s32[1,48]{1,0:T(1,128)S(1)} %pad_add_fusion.1), channel_id=1, source_target_pairs={{0,3},{1,2},{2,1},{3,0},{4,7},{5,6},{6,5},{7,4},{8,11},{9,10},{10,... | collective-permute-start | bytes 584 | tf_op jit(solution)/shard_map/ppermute | solution.py:37
  4.7 9.5 %product.1 = (bf16[128,3584]{1,0:T(8,128)(2,1)}, bf16[128,3584]{1,0:T(8,128)(2,1)}, bf16[128,3584]{1,0:T(8,128)(2,1)}, bf16[128,3584]{1,0:T(8,128)(2,1)}) custom-call(bf16[1024,512]{1,0:T(8,128)(2,1)} %coef_ref.1, bf16[1024,3584]{1,0:T(8,128)(2,1)} %right_ref.2), custom_call_target="tpu_custom_call" | custom-call | flops 3758096384 | bytes 12058624 | tf_op jit(solution)/shard_map/product/pallas_call | solution.py:194
  14.9 3.6 %collective-permute-start.6 = (s32[4,48]{1,0:T(4,128)S(1)}, s32[4,48]{1,0:T(4,128)S(1)}, u32[]{:S(2)}, u32[]{:S(2)}) collective-permute-start(s32[4,48]{1,0:T(4,128)S(1)} %pad_add_fusion.refs_0_), channel_id=1, source_target_pairs={{0,12},{1,13},{2,14},{3,15},{4,8},{5,9},{6,10},{7,11},{8,4},{9,5},... | collective-permute-start | bytes 2312 | tf_op jit(solution)/shard_map/ppermute | solution.py:37
  20.3 1.4 %collective-permute-start.8 = (bf16[32,1792]{1,0:T(8,128)(2,1)S(1)}, bf16[32,1792]{1,0:T(8,128)(2,1)S(1)}, u32[]{:S(2)}, u32[]{:S(2)}) collective-permute-start(bf16[32,1792]{1,0:T(8,128)(2,1)S(1)} %get-tuple-element.118), channel_id=1, source_target_pairs={{0,2},{1,3},{4,0},{5,1},{8,4},{9,5},{12,8},{13,9},{14,12},{15,13},... | collective-permute-start | bytes 344072 | tf_op jit(solution)/shard_map/ppermute | solution.py:75
  24.3 7.0 %select_product.1 = (bf16[128,3584]{1,0:T(8,128)(2,1)S(1)}, bf16[128,3584]{1,0:T(8,128)(2,1)S(1)}, bf16[128,3584]{1,0:T(8,128)(2,1)S(1)}, bf16[128,3584]{1,0:T(8,128)(2,1)S(1)}, s32[32,1]{1,0:T(8,128)S(1)}) custom-call(bf16[1024,512]{1,0:T(8,128)(2,1)S(1)} %copy-done.7, bf16[1024,3584]{1,0:T(8,128)(2,1)S(1)} %bitcast.9, s32[2,16]{1,0:T(2,128)S(1)} %bitcast.10, ...), custom_call_target="tpu_custom_call" | custom-call | flops 3758096384 | bytes 12058624 | tf_op jit(solution)/shard_map/select_product/pallas_call | solution.py:194
  31.4 2.5 %collective-permute-done.10 = bf16[128,3584]{1,0:T(8,128)(2,1)S(1)} collective-permute-done((bf16[128,3584]{1,0:T(8,128)(2,1)S(1)}, bf16[128,3584]{1,0:T(8,128)(2,1)S(1)}, u32[]{:S(2)}, u32[]{:S(2)}) %collective-permute-start.10) | collective-permute-done | bytes 917536 | tf_op jit(solution)/shard_map/ppermute | solution.py:37
  34.0 1.3 %collective-permute-start.15 = (bf16[32,1792]{1,0:T(8,128)(2,1)S(1)}, bf16[32,1792]{1,0:T(8,128)(2,1)S(1)}, u32[]{:S(2)}, u32[]{:S(2)}) collective-permute-start(bf16[32,1792]{1,0:T(8,128)(2,1)S(1)} %get-tuple-element.116), channel_id=1, source_target_pairs={{0,2},{1,3},{4,0},{5,1},{8,4},{9,5},{12,8},{13,9},{14,12},{15,13},... | collective-permute-start | bytes 344072 | tf_op jit(solution)/shard_map/ppermute | solution.py:75
  36.1 3.2 %collective-permute-done.15 = bf16[32,1792]{1,0:T(8,128)(2,1)S(1)} collective-permute-done((bf16[32,1792]{1,0:T(8,128)(2,1)S(1)}, bf16[32,1792]{1,0:T(8,128)(2,1)S(1)}, u32[]{:S(2)}, u32[]{:S(2)}) %collective-permute-start.15) | collective-permute-done | bytes 114720 | tf_op jit(solution)/shard_map/ppermute | solution.py:75
  39.3 1.3 %collective-permute-start.16 = (bf16[32,3584]{1,0:T(8,128)(2,1)S(1)}, bf16[32,3584]{1,0:T(8,128)(2,1)S(1)}, u32[]{:S(2)}, u32[]{:S(2)}) collective-permute-start(bf16[32,3584]{1,0:T(8,128)(2,1)S(1)} %add_convert_fusion.8), channel_id=1, source_target_pairs={{0,2},{1,3},{4,0},{5,1},{8,4},{9,5},{12,8},{13,9},{14,12},{15,13},... | collective-permute-start | bytes 688136 | tf_op jit(solution)/shard_map/ppermute | solution.py:75
  41.4 6.5 %collective-permute-done.16 = bf16[32,3584]{1,0:T(8,128)(2,1)S(1)} collective-permute-done((bf16[32,3584]{1,0:T(8,128)(2,1)S(1)}, bf16[32,3584]{1,0:T(8,128)(2,1)S(1)}, u32[]{:S(2)}, u32[]{:S(2)}) %collective-permute-start.16) | collective-permute-done | bytes 229408 | tf_op jit(solution)/shard_map/ppermute | solution.py:75
  48.9 2.2 %collective-permute-done.23 = bf16[32,3584]{1,0:T(8,128)(2,1)S(1)} collective-permute-done((bf16[32,3584]{1,0:T(8,128)(2,1)S(1)}, bf16[32,3584]{1,0:T(8,128)(2,1)S(1)}, u32[]{:S(2)}, u32[]{:S(2)}) %collective-permute-start.23) | collective-permute-done | bytes 229408 | tf_op jit(solution)/shard_map/ppermute | solution.py:75
  51.2 1.3 %collective-permute-start.24 = (bf16[32,3584]{1,0:T(8,128)(2,1)S(1)}, bf16[32,3584]{1,0:T(8,128)(2,1)S(1)}, u32[]{:S(2)}, u32[]{:S(2)}) collective-permute-start(bf16[32,3584]{1,0:T(8,128)(2,1)S(1)} %get-tuple-element.110), channel_id=1, source_target_pairs={{0,2},{1,3},{4,0},{5,1},{8,4},{9,5},{12,8},{13,9},{14,12},{15,13},... | collective-permute-start | bytes 688136 | tf_op jit(solution)/shard_map/ppermute | solution.py:75
  53.3 1.3 %collective-permute-start.17 = (bf16[32,3584]{1,0:T(8,128)(2,1)S(1)}, bf16[32,3584]{1,0:T(8,128)(2,1)S(1)}, u32[]{:S(2)}, u32[]{:S(2)}) collective-permute-start(bf16[32,3584]{1,0:T(8,128)(2,1)S(1)} %get-tuple-element.114), channel_id=1, source_target_pairs={{0,2},{1,3},{4,0},{5,1},{8,4},{9,5},{12,8},{13,9},{14,12},{15,13},... | collective-permute-start | bytes 688136 | tf_op jit(solution)/shard_map/ppermute | solution.py:75
  55.9 5.2 %collective-permute-done.20 = bf16[32,3584]{1,0:T(8,128)(2,1)S(1)} collective-permute-done((bf16[32,3584]{1,0:T(8,128)(2,1)S(1)}, bf16[32,3584]{1,0:T(8,128)(2,1)S(1)}, u32[]{:S(2)}, u32[]{:S(2)}) %collective-permute-start.20) | collective-permute-done | bytes 229408 | tf_op jit(solution)/shard_map/ppermute | solution.py:75
  62.1 3.9 %collective-permute-done.13 = bf16[32,3584]{1,0:T(8,128)(2,1)S(1)} collective-permute-done((bf16[32,3584]{1,0:T(8,128)(2,1)S(1)}, bf16[32,3584]{1,0:T(8,128)(2,1)S(1)}, u32[]{:S(2)}, u32[]{:S(2)}) %collective-permute-start.13) | collective-permute-done | bytes 229408 | tf_op jit(solution)/shard_map/ppermute | solution.py:75
  66.9 1.4 %collective-permute-start.14 = (bf16[32,3584]{1,0:T(8,128)(2,1)S(1)}, bf16[32,3584]{1,0:T(8,128)(2,1)S(1)}, u32[]{:S(2)}, u32[]{:S(2)}) collective-permute-start(bf16[32,3584]{1,0:T(8,128)(2,1)S(1)} %get-tuple-element.113), channel_id=1, source_target_pairs={{0,4},{1,5},{4,8},{5,9},{8,12},{9,13},{12,14},{13,15},{14,10},{15,... | collective-permute-start | bytes 688136 | tf_op jit(solution)/shard_map/ppermute | solution.py:75
  68.3 2.7 %collective-permute-done.21 = bf16[32,3584]{1,0:T(8,128)(2,1)S(1)} collective-permute-done((bf16[32,3584]{1,0:T(8,128)(2,1)S(1)}, bf16[32,3584]{1,0:T(8,128)(2,1)S(1)}, u32[]{:S(2)}, u32[]{:S(2)}) %collective-permute-start.21) | collective-permute-done | bytes 229408 | tf_op jit(solution)/shard_map/ppermute | solution.py:75
  71.8 1.4 %collective-permute-start.22 = (bf16[32,3584]{1,0:T(8,128)(2,1)S(1)}, bf16[32,3584]{1,0:T(8,128)(2,1)S(1)}, u32[]{:S(2)}, u32[]{:S(2)}) collective-permute-start(bf16[32,3584]{1,0:T(8,128)(2,1)S(1)} %get-tuple-element.109), channel_id=1, source_target_pairs={{0,4},{1,5},{4,8},{5,9},{8,12},{9,13},{12,14},{13,15},{14,10},{15,... | collective-permute-start | bytes 688136 | tf_op jit(solution)/shard_map/ppermute | solution.py:75
  73.2 1.5 %collective-permute-done.18.refs_3_ = bf16[32,3584]{1,0:T(8,128)(2,1)S(1)} collective-permute-done((bf16[32,3584]{1,0:T(8,128)(2,1)S(1)}, bf16[32,3584]{1,0:T(8,128)(2,1)S(1)}, u32[]{:S(2)}, u32[]{:S(2)}) %collective-permute-start.18) | collective-permute-done | bytes 229408 | tf_op jit(solution)/shard_map/ppermute | solution.py:75
  75.9 1.8 %enc_update.1 = (f32[32,3584]{1,0:T(8,128)}, f32[32,3584]{1,0:T(8,128)}, f32[32,3584]{1,0:T(8,128)}, bf16[32,3584]{1,0:T(8,128)(2,1)S(1)}, bf16[32,3584]{1,0:T(8,128)(2,1)S(1)}) custom-call(s32[32,1]{1,0:T(8,128)S(1)} %get-tuple-element.62.code_ref, f32[32,3584]{1,0:T(8,128)S(1)} %copy-done.1, f32[32,3584]{1,0:T(8,128)S(1)} %copy-done.2, ...), custom_call_target="tpu_custom_call" | custom-call | flops 4587520 | bytes 4587520 | tf_op jit(solution)/shard_map/enc_update/pallas_call | solution.py:263
  78.7 1.8 %dec_update.1 = (f32[32,3584]{1,0:T(8,128)}, f32[32,3584]{1,0:T(8,128)}, f32[32,3584]{1,0:T(8,128)}, bf16[2,32,3584]{2,1,0:T(8,128)(2,1)S(1)}) custom-call(s32[32,1]{1,0:T(8,128)S(1)} %get-tuple-element.62.code_ref, f32[32,3584]{1,0:T(8,128)S(1)} %copy-done.4, f32[32,3584]{1,0:T(8,128)S(1)} %copy-done.5, f32[32,3584]{1,0:T(8,128)S(1)} %copy-done.6, ...), custom_call_target="tpu_custom_call" | custom-call | flops 4587520 | bytes 4587520 | tf_op jit(solution)/shard_map/dec_update/pallas_call | solution.py:263
  83.3 7.7 %collective-permute-done.27.refs_1_ = bf16[64,3584]{1,0:T(8,128)(2,1)S(1)} collective-permute-done((bf16[64,3584]{1,0:T(8,128)(2,1)S(1)}, bf16[64,3584]{1,0:T(8,128)(2,1)S(1)}, u32[]{:S(2)}, u32[]{:S(2)}) %collective-permute-start.27) | collective-permute-done | bytes 458784 | tf_op jit(solution)/shard_map/ppermute | solution.py:75
  91.0 1.5 %collective-permute-done.26.refs_0_ = bf16[64,3584]{1,0:T(8,128)(2,1)S(1)} collective-permute-done((bf16[64,3584]{1,0:T(8,128)(2,1)S(1)}, bf16[64,3584]{1,0:T(8,128)(2,1)S(1)}, u32[]{:S(2)}, u32[]{:S(2)}) %collective-permute-start.26) | collective-permute-done | bytes 458784 | tf_op jit(solution)/shard_map/ppermute | solution.py:75
  92.8 1.7 %collective-permute-start.29 = (bf16[64,3584]{1,0:T(8,128)(2,1)S(1)}, bf16[64,3584]{1,0:T(8,128)(2,1)S(1)}, u32[]{:S(2)}, u32[]{:S(2)}) collective-permute-start(bf16[64,3584]{1,0:T(8,128)(2,1)S(1)} %collective-permute-done.27.refs_1_), channel_id=1, source_target_pairs={{0,2},{1,3},{4,0},{5,1},{8,4},{9,5},{12,8},{13,9},{14,12},{15,13},... | collective-permute-start | bytes 1376264 | tf_op jit(solution)/shard_map/ppermute | solution.py:75
  96.1 6.5 %collective-permute-done.28.refs_0_ = bf16[64,3584]{1,0:T(8,128)(2,1)S(1)} collective-permute-done((bf16[64,3584]{1,0:T(8,128)(2,1)S(1)}, bf16[64,3584]{1,0:T(8,128)(2,1)S(1)}, u32[]{:S(2)}, u32[]{:S(2)}) %collective-permute-start.28) | collective-permute-done | bytes 458784 | tf_op jit(solution)/shard_map/ppermute | solution.py:75
  102.6 1.3 %collective-permute-start.31 = (bf16[64,3584]{1,0:T(8,128)(2,1)S(1)}, bf16[64,3584]{1,0:T(8,128)(2,1)S(1)}, u32[]{:S(2)}, u32[]{:S(2)}) collective-permute-start(bf16[64,3584]{1,0:T(8,128)(2,1)S(1)} %collective-permute-done.28.refs_0_), channel_id=1, source_target_pairs={{0,4},{1,5},{4,8},{5,9},{8,12},{9,13},{12,14},{13,15},{14,10},{15,... | collective-permute-start | bytes 1376264 | tf_op jit(solution)/shard_map/ppermute | solution.py:75
  105.2 1.3 %place.8 = (bf16[512,3584]{1,0:T(8,128)(2,1)}, bf16[512,3584]{1,0:T(8,128)(2,1)}) custom-call(bf16[64,3584]{1,0:T(8,128)(2,1)S(1)} %collective-permute-done.28.refs_0_, bf16[64,3584]{1,0:T(8,128)(2,1)S(1)} %collective-permute-done.29.refs_1_, bf16[64,3584]{1,0:T(8,128)(2,1)S(1)} %collective-permute-done.33.refs_2_, ...), custom_call_target="tpu_custom_call", output_to_operand_aliasing={{0}: (4, {}), {1}: (5, {})} | custom-call | bytes 3670016 | tf_op jit(solution)/shard_map/place/pallas_call | solution.py:298
  106.5 5.8 %collective-permute-done.31.refs_0_ = bf16[64,3584]{1,0:T(8,128)(2,1)S(1)} collective-permute-done((bf16[64,3584]{1,0:T(8,128)(2,1)S(1)}, bf16[64,3584]{1,0:T(8,128)(2,1)S(1)}, u32[]{:S(2)}, u32[]{:S(2)}) %collective-permute-start.31) | collective-permute-done | bytes 458784 | tf_op jit(solution)/shard_map/ppermute | solution.py:75
  112.3 2.2 %collective-permute-done.32.refs_1_ = bf16[64,3584]{1,0:T(8,128)(2,1)S(1)} collective-permute-done((bf16[64,3584]{1,0:T(8,128)(2,1)S(1)}, bf16[64,3584]{1,0:T(8,128)(2,1)S(1)}, u32[]{:S(2)}, u32[]{:S(2)}) %collective-permute-start.32) | collective-permute-done | bytes 458784 | tf_op jit(solution)/shard_map/ppermute | solution.py:75
  115.3 1.3 %collective-permute-start.35 = (bf16[64,1792]{1,0:T(8,128)(2,1)S(1)}, bf16[64,1792]{1,0:T(8,128)(2,1)S(1)}, u32[]{:S(2)}, u32[]{:S(2)}) collective-permute-start(bf16[64,1792]{1,0:T(8,128)(2,1)S(1)} %slice.134), channel_id=1, source_target_pairs={{0,4},{1,5},{4,8},{5,9},{8,12},{9,13},{12,14},{13,15},{14,10},{15,... | collective-permute-start | bytes 688136 | tf_op jit(solution)/shard_map/ppermute | solution.py:75
  117.2 1.3 %place.9 = (bf16[512,3584]{1,0:T(8,128)(2,1)}, bf16[512,3584]{1,0:T(8,128)(2,1)}) custom-call(bf16[64,3584]{1,0:T(8,128)(2,1)S(1)} %collective-permute-done.31.refs_0_, bf16[64,3584]{1,0:T(8,128)(2,1)S(1)} %collective-permute-done.32.refs_1_, bf16[64,3584]{1,0:T(8,128)(2,1)S(1)} %collective-permute-done.37.refs_2_, ...), custom_call_target="tpu_custom_call", output_to_operand_aliasing={{0}: (4, {}), {1}: (5, {})} | custom-call | bytes 3670016 | tf_op jit(solution)/shard_map/place/pallas_call | solution.py:298
  118.5 2.2 %collective-permute-done.36.refs_1_ = bf16[64,1792]{1,0:T(8,128)(2,1)S(1)} collective-permute-done((bf16[64,1792]{1,0:T(8,128)(2,1)S(1)}, bf16[64,1792]{1,0:T(8,128)(2,1)S(1)}, u32[]{:S(2)}, u32[]{:S(2)}) %collective-permute-start.36) | collective-permute-done | bytes 229408 | tf_op jit(solution)/shard_map/ppermute | solution.py:75
  (111 shorter events, 27.1 us)
Async XLA Ops:
  1.6 12.7 %collective-permute-start.2 = (s32[1,48]{1,0:T(1,128)S(1)}, s32[1,48]{1,0:T(1,128)S(1)}, u32[]{:S(2)}, u32[]{:S(2)}) collective-permute-start(s32[1,48]{1,0:T(1,128)S(1)} %pad_add_fusion.1), channel_id=1, source_target_pairs={{0,3},{1,2},{2,1},{3,0},{4,7},{5,6},{6,5},{7,4},{8,11},{9,10},{10,... | collective-permute-start | bytes 584 | tf_op jit(solution)/shard_map/ppermute | solution.py:37
  4.0 10.2 %collective-permute-start.1 = (s32[1,48]{1,0:T(1,128)S(1)}, s32[1,48]{1,0:T(1,128)S(1)}, u32[]{:S(2)}, u32[]{:S(2)}) collective-permute-start(s32[1,48]{1,0:T(1,128)S(1)} %pad_add_fusion.1), channel_id=1, source_target_pairs={{0,2},{1,3},{2,0},{3,1},{4,6},{5,7},{6,4},{7,5},{8,10},{9,11},{10,... | collective-permute-start | bytes 584 | tf_op jit(solution)/shard_map/ppermute | solution.py:37
  4.7 9.6 %collective-permute-start = (s32[1,48]{1,0:T(1,128)S(1)}, s32[1,48]{1,0:T(1,128)S(1)}, u32[]{:S(2)}, u32[]{:S(2)}) collective-permute-start(s32[1,48]{1,0:T(1,128)S(1)} %pad_add_fusion.1), channel_id=1, source_target_pairs={{0,1},{1,0},{2,3},{3,2},{4,5},{5,4},{6,7},{7,6},{8,9},{9,8},{10,11... | collective-permute-start | bytes 584 | tf_op jit(solution)/shard_map/ppermute | solution.py:37
  14.9 7.5 %collective-permute-start.6 = (s32[4,48]{1,0:T(4,128)S(1)}, s32[4,48]{1,0:T(4,128)S(1)}, u32[]{:S(2)}, u32[]{:S(2)}) collective-permute-start(s32[4,48]{1,0:T(4,128)S(1)} %pad_add_fusion.refs_0_), channel_id=1, source_target_pairs={{0,12},{1,13},{2,14},{3,15},{4,8},{5,9},{6,10},{7,11},{8,4},{9,5},... | collective-permute-start | bytes 2312 | tf_op jit(solution)/shard_map/ppermute | solution.py:37
  20.3 11.0 %collective-permute-start.8 = (bf16[32,1792]{1,0:T(8,128)(2,1)S(1)}, bf16[32,1792]{1,0:T(8,128)(2,1)S(1)}, u32[]{:S(2)}, u32[]{:S(2)}) collective-permute-start(bf16[32,1792]{1,0:T(8,128)(2,1)S(1)} %get-tuple-element.118), channel_id=1, source_target_pairs={{0,2},{1,3},{4,0},{5,1},{8,4},{9,5},{12,8},{13,9},{14,12},{15,13},... | collective-permute-start | bytes 344072 | tf_op jit(solution)/shard_map/ppermute | solution.py:75
  21.7 9.6 %collective-permute-start.7 = (bf16[32,1792]{1,0:T(8,128)(2,1)S(1)}, bf16[32,1792]{1,0:T(8,128)(2,1)S(1)}, u32[]{:S(2)}, u32[]{:S(2)}) collective-permute-start(bf16[32,1792]{1,0:T(8,128)(2,1)S(1)} %get-tuple-element.119), channel_id=1, source_target_pairs={{0,4},{1,5},{4,8},{5,9},{8,12},{9,13},{12,14},{13,15},{14,10},{15,... | collective-permute-start | bytes 344072 | tf_op jit(solution)/shard_map/ppermute | solution.py:75
  35.3 20.6 %collective-permute-start.19 = (bf16[128,3584]{1,0:T(8,128)(2,1)S(1)}, bf16[128,3584]{1,0:T(8,128)(2,1)S(1)}, u32[]{:S(2)}, u32[]{:S(2)}) collective-permute-start(bf16[128,3584]{1,0:T(8,128)(2,1)S(1)} %copy-done.12), channel_id=1, source_target_pairs={{0,1},{1,0},{2,3},{3,2},{4,5},{5,4},{6,7},{7,6},{8,9},{9,8},{10,11... | collective-permute-start | bytes 2752520 | tf_op jit(solution)/shard_map/ppermute | solution.py:37
  35.3 6.1 %collective-permute-start.11 = (bf16[32,1792]{1,0:T(8,128)(2,1)S(1)}, bf16[32,1792]{1,0:T(8,128)(2,1)S(1)}, u32[]{:S(2)}, u32[]{:S(2)}) collective-permute-start(bf16[32,1792]{1,0:T(8,128)(2,1)S(1)} %get-tuple-element.117), channel_id=1, source_target_pairs={{0,4},{1,5},{4,8},{5,9},{8,12},{9,13},{12,14},{13,15},{14,10},{15,... | collective-permute-start | bytes 344072 | tf_op jit(solution)/shard_map/ppermute | solution.py:75
  39.3 8.6 %collective-permute-start.16 = (bf16[32,3584]{1,0:T(8,128)(2,1)S(1)}, bf16[32,3584]{1,0:T(8,128)(2,1)S(1)}, u32[]{:S(2)}, u32[]{:S(2)}) collective-permute-start(bf16[32,3584]{1,0:T(8,128)(2,1)S(1)} %add_convert_fusion.8), channel_id=1, source_target_pairs={{0,2},{1,3},{4,0},{5,1},{8,4},{9,5},{12,8},{13,9},{14,12},{15,13},... | collective-permute-start | bytes 688136 | tf_op jit(solution)/shard_map/ppermute | solution.py:75
  40.7 10.4 %collective-permute-start.23 = (bf16[32,3584]{1,0:T(8,128)(2,1)S(1)}, bf16[32,3584]{1,0:T(8,128)(2,1)S(1)}, u32[]{:S(2)}, u32[]{:S(2)}) collective-permute-start(bf16[32,3584]{1,0:T(8,128)(2,1)S(1)} %add_convert_fusion.2), channel_id=1, source_target_pairs={{0,2},{1,3},{4,0},{5,1},{8,4},{9,5},{12,8},{13,9},{14,12},{15,13},... | collective-permute-start | bytes 688136 | tf_op jit(solution)/shard_map/ppermute | solution.py:75
  41.4 11.9 %collective-permute-start.9 = (bf16[128,3584]{1,0:T(8,128)(2,1)S(1)}, bf16[128,3584]{1,0:T(8,128)(2,1)S(1)}, u32[]{:S(2)}, u32[]{:S(2)}) collective-permute-start(bf16[128,3584]{1,0:T(8,128)(2,1)S(1)} %get-tuple-element.66), channel_id=1, source_target_pairs={{0,1},{1,0},{2,3},{3,2},{4,5},{5,4},{6,7},{7,6},{8,9},{9,8},{10,11... | collective-permute-start | bytes 2752520 | tf_op jit(solution)/shard_map/ppermute | solution.py:37
  48.1 6.9 %collective-permute-start.12 = (bf16[32,3584]{1,0:T(8,128)(2,1)S(1)}, bf16[32,3584]{1,0:T(8,128)(2,1)S(1)}, u32[]{:S(2)}, u32[]{:S(2)}) collective-permute-start(bf16[32,3584]{1,0:T(8,128)(2,1)S(1)} %get-tuple-element.115), channel_id=1, source_target_pairs={{0,4},{1,5},{4,8},{5,9},{8,12},{9,13},{12,14},{13,15},{14,10},{15,... | collective-permute-start | bytes 688136 | tf_op jit(solution)/shard_map/ppermute | solution.py:75
  51.2 17.0 %collective-permute-start.24 = (bf16[32,3584]{1,0:T(8,128)(2,1)S(1)}, bf16[32,3584]{1,0:T(8,128)(2,1)S(1)}, u32[]{:S(2)}, u32[]{:S(2)}) collective-permute-start(bf16[32,3584]{1,0:T(8,128)(2,1)S(1)} %get-tuple-element.110), channel_id=1, source_target_pairs={{0,2},{1,3},{4,0},{5,1},{8,4},{9,5},{12,8},{13,9},{14,12},{15,13},... | collective-permute-start | bytes 688136 | tf_op jit(solution)/shard_map/ppermute | solution.py:75
  52.6 8.5 %collective-permute-start.20 = (bf16[32,3584]{1,0:T(8,128)(2,1)S(1)}, bf16[32,3584]{1,0:T(8,128)(2,1)S(1)}, u32[]{:S(2)}, u32[]{:S(2)}) collective-permute-start(bf16[32,3584]{1,0:T(8,128)(2,1)S(1)} %get-tuple-element.111), channel_id=1, source_target_pairs={{0,4},{1,5},{4,8},{5,9},{8,12},{9,13},{12,14},{13,15},{14,10},{15,... | collective-permute-start | bytes 688136 | tf_op jit(solution)/shard_map/ppermute | solution.py:75
  53.3 8.8 %collective-permute-start.17 = (bf16[32,3584]{1,0:T(8,128)(2,1)S(1)}, bf16[32,3584]{1,0:T(8,128)(2,1)S(1)}, u32[]{:S(2)}, u32[]{:S(2)}) collective-permute-start(bf16[32,3584]{1,0:T(8,128)(2,1)S(1)} %get-tuple-element.114), channel_id=1, source_target_pairs={{0,2},{1,3},{4,0},{5,1},{8,4},{9,5},{12,8},{13,9},{14,12},{15,13},... | collective-permute-start | bytes 688136 | tf_op jit(solution)/shard_map/ppermute | solution.py:75
  55.1 11.0 %collective-permute-start.13 = (bf16[32,3584]{1,0:T(8,128)(2,1)S(1)}, bf16[32,3584]{1,0:T(8,128)(2,1)S(1)}, u32[]{:S(2)}, u32[]{:S(2)}) collective-permute-start(bf16[32,3584]{1,0:T(8,128)(2,1)S(1)} %add_convert_fusion.10), channel_id=1, source_target_pairs={{0,4},{1,5},{4,8},{5,9},{8,12},{9,13},{12,14},{13,15},{14,10},{15,... | collective-permute-start | bytes 688136 | tf_op jit(solution)/shard_map/ppermute | solution.py:75
  61.2 9.7 %collective-permute-start.21 = (bf16[32,3584]{1,0:T(8,128)(2,1)S(1)}, bf16[32,3584]{1,0:T(8,128)(2,1)S(1)}, u32[]{:S(2)}, u32[]{:S(2)}) collective-permute-start(bf16[32,3584]{1,0:T(8,128)(2,1)S(1)} %add_convert_fusion.4), channel_id=1, source_target_pairs={{0,4},{1,5},{4,8},{5,9},{8,12},{9,13},{12,14},{13,15},{14,10},{15,... | collective-permute-start | bytes 688136 | tf_op jit(solution)/shard_map/ppermute | solution.py:75
  66.2 8.5 %collective-permute-start.18 = (bf16[32,3584]{1,0:T(8,128)(2,1)S(1)}, bf16[32,3584]{1,0:T(8,128)(2,1)S(1)}, u32[]{:S(2)}, u32[]{:S(2)}) collective-permute-start(bf16[32,3584]{1,0:T(8,128)(2,1)S(1)} %get-tuple-element.112), channel_id=1, source_target_pairs={{0,2},{1,3},{4,0},{5,1},{8,4},{9,5},{12,8},{13,9},{14,12},{15,13},... | collective-permute-start | bytes 688136 | tf_op jit(solution)/shard_map/ppermute | solution.py:75
  66.9 8.9 %collective-permute-start.14 = (bf16[32,3584]{1,0:T(8,128)(2,1)S(1)}, bf16[32,3584]{1,0:T(8,128)(2,1)S(1)}, u32[]{:S(2)}, u32[]{:S(2)}) collective-permute-start(bf16[32,3584]{1,0:T(8,128)(2,1)S(1)} %get-tuple-element.113), channel_id=1, source_target_pairs={{0,4},{1,5},{4,8},{5,9},{8,12},{9,13},{12,14},{13,15},{14,10},{15,... | collective-permute-start | bytes 688136 | tf_op jit(solution)/shard_map/ppermute | solution.py:75
  71.1 6.5 %collective-permute-start.25 = (bf16[32,3584]{1,0:T(8,128)(2,1)S(1)}, bf16[32,3584]{1,0:T(8,128)(2,1)S(1)}, u32[]{:S(2)}, u32[]{:S(2)}) collective-permute-start(bf16[32,3584]{1,0:T(8,128)(2,1)S(1)} %get-tuple-element.108), channel_id=1, source_target_pairs={{0,2},{1,3},{4,0},{5,1},{8,4},{9,5},{12,8},{13,9},{14,12},{15,13},... | collective-permute-start | bytes 688136 | tf_op jit(solution)/shard_map/ppermute | solution.py:75
  71.8 6.9 %collective-permute-start.22 = (bf16[32,3584]{1,0:T(8,128)(2,1)S(1)}, bf16[32,3584]{1,0:T(8,128)(2,1)S(1)}, u32[]{:S(2)}, u32[]{:S(2)}) collective-permute-start(bf16[32,3584]{1,0:T(8,128)(2,1)S(1)} %get-tuple-element.109), channel_id=1, source_target_pairs={{0,4},{1,5},{4,8},{5,9},{8,12},{9,13},{12,14},{13,15},{14,10},{15,... | collective-permute-start | bytes 688136 | tf_op jit(solution)/shard_map/ppermute | solution.py:75
  80.5 10.5 %collective-permute-start.27 = (bf16[64,3584]{1,0:T(8,128)(2,1)S(1)}, bf16[64,3584]{1,0:T(8,128)(2,1)S(1)}, u32[]{:S(2)}, u32[]{:S(2)}) collective-permute-start(bf16[64,3584]{1,0:T(8,128)(2,1)S(1)} %bitcast.4), channel_id=1, source_target_pairs={{0,2},{1,3},{4,0},{5,1},{8,4},{9,5},{12,8},{13,9},{14,12},{15,13},... | collective-permute-start | bytes 1376264 | tf_op jit(solution)/shard_map/ppermute | solution.py:75
  81.8 10.7 %collective-permute-start.26 = (bf16[64,3584]{1,0:T(8,128)(2,1)S(1)}, bf16[64,3584]{1,0:T(8,128)(2,1)S(1)}, u32[]{:S(2)}, u32[]{:S(2)}) collective-permute-start(bf16[64,3584]{1,0:T(8,128)(2,1)S(1)} %bitcast.5), channel_id=1, source_target_pairs={{0,4},{1,5},{4,8},{5,9},{8,12},{9,13},{12,14},{13,15},{14,10},{15,... | collective-permute-start | bytes 1376264 | tf_op jit(solution)/shard_map/ppermute | solution.py:75
  82.5 12.5 %collective-permute-start.30 = (bf16[64,3584]{1,0:T(8,128)(2,1)S(1)}, bf16[64,3584]{1,0:T(8,128)(2,1)S(1)}, u32[]{:S(2)}, u32[]{:S(2)}) collective-permute-start(bf16[64,3584]{1,0:T(8,128)(2,1)S(1)} %bitcast.6), channel_id=1, source_target_pairs={{0,1},{1,0},{2,3},{3,2},{4,5},{5,4},{6,7},{7,6},{8,9},{9,8},{10,11... | collective-permute-start | bytes 1376264 | tf_op jit(solution)/shard_map/ppermute | solution.py:37
  92.5 10.2 %collective-permute-start.28 = (bf16[64,3584]{1,0:T(8,128)(2,1)S(1)}, bf16[64,3584]{1,0:T(8,128)(2,1)S(1)}, u32[]{:S(2)}, u32[]{:S(2)}) collective-permute-start(bf16[64,3584]{1,0:T(8,128)(2,1)S(1)} %collective-permute-done.26.refs_0_), channel_id=1, source_target_pairs={{0,4},{1,5},{4,8},{5,9},{8,12},{9,13},{12,14},{13,15},{14,10},{15,... | collective-permute-start | bytes 1376264 | tf_op jit(solution)/shard_map/ppermute | solution.py:75
  92.8 9.9 %collective-permute-start.29 = (bf16[64,3584]{1,0:T(8,128)(2,1)S(1)}, bf16[64,3584]{1,0:T(8,128)(2,1)S(1)}, u32[]{:S(2)}, u32[]{:S(2)}) collective-permute-start(bf16[64,3584]{1,0:T(8,128)(2,1)S(1)} %collective-permute-done.27.refs_1_), channel_id=1, source_target_pairs={{0,2},{1,3},{4,0},{5,1},{8,4},{9,5},{12,8},{13,9},{14,12},{15,13},... | collective-permute-start | bytes 1376264 | tf_op jit(solution)/shard_map/ppermute | solution.py:75
  94.5 10.2 %collective-permute-start.33 = (bf16[64,3584]{1,0:T(8,128)(2,1)S(1)}, bf16[64,3584]{1,0:T(8,128)(2,1)S(1)}, u32[]{:S(2)}, u32[]{:S(2)}) collective-permute-start(bf16[64,3584]{1,0:T(8,128)(2,1)S(1)} %collective-permute-done.26.refs_0_), channel_id=1, source_target_pairs={{0,1},{1,0},{2,3},{3,2},{4,5},{5,4},{6,7},{7,6},{8,9},{9,8},{10,11... | collective-permute-start | bytes 1376264 | tf_op jit(solution)/shard_map/ppermute | solution.py:37
  94.5 10.7 %collective-permute-start.34 = (bf16[64,3584]{1,0:T(8,128)(2,1)S(1)}, bf16[64,3584]{1,0:T(8,128)(2,1)S(1)}, u32[]{:S(2)}, u32[]{:S(2)}) collective-permute-start(bf16[64,3584]{1,0:T(8,128)(2,1)S(1)} %collective-permute-done.27.refs_1_), channel_id=1, source_target_pairs={{0,1},{1,0},{2,3},{3,2},{4,5},{5,4},{6,7},{7,6},{8,9},{9,8},{10,11... | collective-permute-start | bytes 1376264 | tf_op jit(solution)/shard_map/ppermute | solution.py:37
  102.6 9.7 %collective-permute-start.31 = (bf16[64,3584]{1,0:T(8,128)(2,1)S(1)}, bf16[64,3584]{1,0:T(8,128)(2,1)S(1)}, u32[]{:S(2)}, u32[]{:S(2)}) collective-permute-start(bf16[64,3584]{1,0:T(8,128)(2,1)S(1)} %collective-permute-done.28.refs_0_), channel_id=1, source_target_pairs={{0,4},{1,5},{4,8},{5,9},{8,12},{9,13},{12,14},{13,15},{14,10},{15,... | collective-permute-start | bytes 1376264 | tf_op jit(solution)/shard_map/ppermute | solution.py:75
  103.9 10.6 %collective-permute-start.32 = (bf16[64,3584]{1,0:T(8,128)(2,1)S(1)}, bf16[64,3584]{1,0:T(8,128)(2,1)S(1)}, u32[]{:S(2)}, u32[]{:S(2)}) collective-permute-start(bf16[64,3584]{1,0:T(8,128)(2,1)S(1)} %collective-permute-done.29.refs_1_), channel_id=1, source_target_pairs={{0,2},{1,3},{4,0},{5,1},{8,4},{9,5},{12,8},{13,9},{14,12},{15,13},... | collective-permute-start | bytes 1376264 | tf_op jit(solution)/shard_map/ppermute | solution.py:75
  104.7 12.0 %collective-permute-start.37 = (bf16[64,3584]{1,0:T(8,128)(2,1)S(1)}, bf16[64,3584]{1,0:T(8,128)(2,1)S(1)}, u32[]{:S(2)}, u32[]{:S(2)}) collective-permute-start(bf16[64,3584]{1,0:T(8,128)(2,1)S(1)} %collective-permute-done.28.refs_0_), channel_id=1, source_target_pairs={{0,1},{1,0},{2,3},{3,2},{4,5},{5,4},{6,7},{7,6},{8,9},{9,8},{10,11... | collective-permute-start | bytes 1376264 | tf_op jit(solution)/shard_map/ppermute | solution.py:37
  104.7 12.5 %collective-permute-start.38 = (bf16[64,3584]{1,0:T(8,128)(2,1)S(1)}, bf16[64,3584]{1,0:T(8,128)(2,1)S(1)}, u32[]{:S(2)}, u32[]{:S(2)}) collective-permute-start(bf16[64,3584]{1,0:T(8,128)(2,1)S(1)} %collective-permute-done.29.refs_1_), channel_id=1, source_target_pairs={{0,1},{1,0},{2,3},{3,2},{4,5},{5,4},{6,7},{7,6},{8,9},{9,8},{10,11... | collective-permute-start | bytes 1376264 | tf_op jit(solution)/shard_map/ppermute | solution.py:37
  (26 other events, 334.3 us)

commit v6 on v5

--- a/solution.py
+++ b/solution.py
@@ -39,6 +39,10 @@
 
 def after(value, *others):
     return lax.optimization_barrier((value,) + others)[0]
+
+
+def tied(*values):
+    return lax.optimization_barrier(values)
 
 
 def params(mebibytes):
@@ -87,7 +91,7 @@
     return stages
 
 
-def ordered_rows(size, rows, by_latent, by_slot):
+def ordered_rows(size, rows, by_latent, groups):
     chips = size // 2
     for block in range(size):
         group, inside = block // chips, block % chips
@@ -96,7 +100,7 @@
         offset = far if slot % 2 == 0 else 1 - far
         owner = owner_at(offset, 1 - inside // (chips // 2), size)
         begin = pl.multiple_of(owner * rows, rows)
-        by_slot[block * rows : (block + 1) * rows] = by_latent[pl.ds(begin, rows)]
+        groups[group][inside * rows : (inside + 1) * rows] = by_latent[pl.ds(begin, rows)]
 
 
 def row_codes(size, rows, table, picks_ref):
@@ -130,27 +134,27 @@
     return (code + jnp.where(code < 0, -0.5, 0.5)).astype(jnp.int32)
 
 
-def multiply(by_slot, right_ref, outs):
-    out = jnp.dot(by_slot[...], right_ref[...], preferred_element_type=jnp.float32)
+def multiply(left_ref, right_ref, outs):
+    out = jnp.dot(left_ref[...], right_ref[...], preferred_element_type=jnp.float32)
     part = outs[0].shape[0]
     for i, ref in enumerate(outs):
         ref[...] = out[i * part : (i + 1) * part].astype(ref.dtype)
 
 
-def product_kernel(size, rows, coef_ref, right_ref, *refs):
-    outs, (by_latent, by_slot) = refs[:4], refs[4:]
+def far_kernel(size, rows, coef_ref, right_ref, *refs):
+    outs, near_left, (by_latent, left) = refs[:2], refs[2], refs[3:]
 
     @pl.when(pl.program_id(0) == 0)
     def _():
         by_latent[...] = coef_ref[...].T
-        ordered_rows(size, rows, by_latent, by_slot)
-
-    multiply(by_slot, right_ref, outs)
-
-
-def select_kernel(size, rows, count, coef_ref, right_ref, picks_ref, *refs):
+        ordered_rows(size, rows, by_latent, (left, near_left))
+
+    multiply(left, right_ref, outs)
+
+
+def select_far_kernel(size, rows, count, coef_ref, right_ref, picks_ref, *refs):
     pieces, refs = refs[:count], refs[count:]
-    outs, own_code, (by_latent, by_slot, table, codes) = refs[:4], refs[4], refs[5:]
+    outs, near_left, own_code, (by_latent, left, table, codes) = refs[:2], refs[2], refs[3], refs[4:]
 
     @pl.when(pl.program_id(0) == 0)
     def _():
@@ -164,46 +168,59 @@
         by_latent[...] = jnp.where(
             code == KEPT, coef_ref[...].T, (tokens == code).astype(by_latent.dtype)
         )
-        ordered_rows(size, rows, by_latent, by_slot)
-
-    multiply(by_slot, right_ref, outs)
-
-
-def product(coef, right, size, rows, vmem, picks=None, table=()):
-    tokens, latents = coef.shape
-    width = right.shape[1]
+        ordered_rows(size, rows, by_latent, (left, near_left))
+
+    multiply(left, right_ref, outs)
+
+
+def near_kernel(left_ref, right_ref, *outs):
+    multiply(left_ref, right_ref, outs)
+
+
+def product(kernel, left, right, others, out_more, scratch, name):
+    tokens, width = right.shape
     tile = 512
-    part = latents // 4
+    part = left.size // tokens // (4 if out_more else 2)
     fixed = lambda j: (0, 0)
-    in_specs = [pl.BlockSpec((tokens, latents), fixed), pl.BlockSpec((tokens, tile), lambda j: (0, j))]
-    out_specs = [pl.BlockSpec((part, tile), lambda j: (0, j))] * 4
-    out_shape = [jax.ShapeDtypeStruct((part, width), coef.dtype)] * 4
-    scratch = [pltpu.VMEM((latents, tokens), coef.dtype)] * 2
-    kernel = functools.partial(product_kernel, size, rows)
-    operands = [coef, right]
-    if picks is not None:
-        kernel = functools.partial(select_kernel, size, rows, len(table))
-        operands += [picks] + list(table)
-        in_specs += [pl.BlockSpec(value.shape, fixed) for value in operands[2:]]
-        out_specs.append(pl.BlockSpec((rows, 1), fixed))
-        out_shape.append(jax.ShapeDtypeStruct((rows, 1), jnp.int32))
-        scratch += [
-            pltpu.VMEM((size, table[0].shape[1]), jnp.int32),
-            pltpu.VMEM((latents, 1), jnp.int32),
-        ]
+    in_specs = [pl.BlockSpec(left.shape, fixed), pl.BlockSpec((tokens, tile), lambda j: (0, j))]
     return pl.pallas_call(
         kernel,
         grid=(width // tile,),
-        in_specs=in_specs,
-        out_specs=out_specs,
-        out_shape=out_shape,
+        in_specs=in_specs + [pl.BlockSpec(value.shape, fixed) for value in others],
+        out_specs=[pl.BlockSpec((part, tile), lambda j: (0, j))] * 2
+        + [pl.BlockSpec(value.shape, fixed) for value in out_more],
+        out_shape=[jax.ShapeDtypeStruct((part, width), left.dtype)] * 2 + list(out_more),
         scratch_shapes=scratch,
-        compiler_params=params(vmem),
+        compiler_params=params(20),
         cost_estimate=cost(
-            2 * latents * tokens * width, 2 * (tokens * width + latents * (tokens + width))
+            4 * part * tokens * width, 2 * (tokens * width + 2 * part * (tokens + width))
         ),
-        name="product" if picks is None else "select_product",
-    )(*operands)
+        name=name,
+    )(left, right, *others)
+
+
+def far_product(coef, right, size, rows, picks=None, table=()):
+    tokens, latents = coef.shape
+    near_left = jax.ShapeDtypeStruct((latents // 2, tokens), coef.dtype)
+    scratch = [
+        pltpu.VMEM((latents, tokens), coef.dtype),
+        pltpu.VMEM((latents // 2, tokens), coef.dtype),
+    ]
+    if picks is None:
+        kernel = functools.partial(far_kernel, size, rows)
+        return product(kernel, coef, right, [], [near_left], scratch, "far_product")
+    kernel = functools.partial(select_far_kernel, size, rows, len(table))
+    scratch += [
+        pltpu.VMEM((size, table[0].shape[1]), jnp.int32),
+        pltpu.VMEM((latents, 1), jnp.int32),
+    ]
+    code = jax.ShapeDtypeStruct((rows, 1), jnp.int32)
+    others = [picks] + list(table)
+    return product(kernel, coef, right, others, [near_left, code], scratch, "select_far_product")
+
+
+def near_product(left, right):
+    return product(near_kernel, left, right, [], [], [], "near_product")
 
 
 def term(kept, from_core, slot, rows):
@@ -350,9 +367,9 @@
     chips = size // 2
     stages = gather_table(jnp.concatenate([send_count, dead_order], axis=1), size)
     table = stages[-1]
-    dec = product(latent_act, out_grad, size, rows, 56)
-    dec_far = after(dec[0], *stages[0])
-    dec_kept, dec_core = [dec[1], dec[3]], [swap(dec_far, 1, size), swap(dec[2], 1, size)]
+    dec_sent, dec_kept, dec_left = far_product(latent_act, out_grad, size, rows)
+    dec_sent = after(dec_sent, *stages[0])
+    dec_kept, dec_core = [dec_kept], [swap(dec_sent, 1, size)]
 
     def begin(kept, from_core):
         far = term(kept, from_core, 0, rows).astype(jnp.bfloat16)
@@ -372,17 +389,33 @@
             moving.append(value.astype(jnp.bfloat16))
         return moving
 
-    dec_moving = begin(dec_kept, dec_core)
-    *enc, code = product(
-        after(enc_coef, *dec_moving), x_rows, size, rows, 24, pick_rows[0].T, table
-    )
+    dec_moving = begin(dec_kept, after(dec_core, table[0]))
+    enc_sent, enc_kept, enc_left, code = far_product(
+        after(enc_coef, *dec_moving), x_rows, size, rows, pick_rows[0].T, table
+    )
+    dec_came, enc_sent = tied(travel(dec_moving), enc_sent)
+    enc_kept, enc_core = [enc_kept], [swap(enc_sent, 1, size)]
+    dec_moving = advance(dec_came, dec_kept, dec_core, 1)
     dec_came = travel(dec_moving)
-    enc_far, enc_near = after((enc[0], enc[2]), *dec_came)
-    enc_kept, enc_core = [enc[1], enc[3]], [swap(enc_far, 1, size), swap(enc_near, 1, size)]
-    enc_came = travel(begin(enc_kept, enc_core))
-    for hop in range(1, chips // 2):
-        dec_came = travel(advance(dec_came, dec_kept, dec_core, hop))
-        enc_came = travel(advance(enc_came, enc_kept, enc_core, hop))
+    dec_sent, kept = near_product(after(dec_left, enc_sent, *dec_moving), out_grad)
+    dec_kept.append(kept)
+    enc_moving, dec_came, dec_sent = tied(
+        begin(after(enc_kept, dec_sent), enc_core), dec_came, dec_sent
+    )
+    dec_core.append(swap(dec_sent, 1, size))
+    enc_sent, kept = near_product(after(enc_left, dec_sent), x_rows)
+    enc_kept.append(kept)
+    enc_came, enc_sent = tied(travel(enc_moving), enc_sent)
+    enc_core.append(swap(enc_sent, 1, size))
+    dec_came = after(dec_came, enc_sent)
+    for hop in range(2, chips // 2 + 1):
+        if hop < chips // 2:
+            dec_moving = advance(dec_came, dec_kept, dec_core, hop)
+            dec_came = travel(dec_moving)
+            enc_came = after(enc_came, *dec_moving)
+        enc_moving = advance(enc_came, enc_kept, enc_core, hop - 1)
+        enc_came = travel(enc_moving)
+        dec_came = after(dec_came, *enc_moving)
     enc_out, enc_mo, enc_vo, enc_block, fresh = update(
         enc_kernel,
         code,

time: 124 us -> 123 us (level)
  waiting for transfers between devices: 57.8 us -> 53.7 us
  local copies, waits for them, and re-layouts: 1.36 us -> 4.43 us
    unnamed x30 -> x28, local copies, waits for them, and re-layouts: 1.29 us -> 4.36 us
    ppermute x24, waiting for transfers between devices: 54.4 us -> 51.9 us  [shift(): return lax.ppermute(value, 'latent', pairs)]
    ppermute x19, waiting for transfers between devices: 3.34 us -> 1.74 us  [swap(): return lax.ppermute(value, 'latent', [(i, i ^ bits) for i in range(size)])]
    pallas_call x2 -> x4, Pallas kernels: 16.5 us -> 16.6 us  [product(): pl.pallas_call(kernel, grid=(width // tile,), in_specs=in_specs + [pl.Blo...]
  transfers between devices with their start and end apart: 43 -> 43, of which waited for: 21 -> 21; matrix products, arithmetic and copies ran while one was open for 2% -> 1% of each run, Pallas kernels for 19% -> 18%
where the time goes in v6:
time: 123 us
  waiting for transfers between devices  53.7 us (44%)
  starting transfers between devices  35 us (28%)
  Pallas kernels  26.5 us (22%)
  local copies, waits for them, and re-layouts  4.43 us (4%)
  other arithmetic  1.95 us (2%)
    ppermute x24, waiting for transfers between devices, shift(): return lax.ppermute(value, 'latent', pairs)  51.9 us
    ppermute x24, starting transfers between devices, shift(): return lax.ppermute(value, 'latent', pairs)  24.8 us
    pallas_call x4, Pallas kernels, product(): pl.pallas_call(kernel, grid=(width // tile,), in_specs=in_specs + [pl.Blo...  16.6 us
    ppermute x19, starting transfers between devices, swap(): return lax.ppermute(value, 'latent', [(i, i ^ bits) for i in range(size)])  10.2 us
    pallas_call x6, Pallas kernels, place(): pl.pallas_call(functools.partial(place_kernel, plan, size, rows, count),...  6.39 us
    unnamed x28, local copies, waits for them, and re-layouts  4.36 us
    pallas_call x2, Pallas kernels, update(): pl.pallas_call(kernel, grid=(rows // tile,), in_specs=[last_rows(value) f...  3.51 us
  transfers between devices with their start and end apart: 43, of which 21 were waited for; matrix products, arithmetic and copies ran while one was open for 1% of the time, Pallas kernels for 18%

profile of v6, /device:TPU:0, one launch (start us, length us, event | category | flops | bytes accessed | tf_op | source)
XLA Modules:
  0.0 122.6 jit_solution(11631305632962678767)
XLA Ops:
  1.4 2.4 %collective-permute-start.2 = (s32[1,48]{1,0:T(1,128)S(1)}, s32[1,48]{1,0:T(1,128)S(1)}, u32[]{:S(2)}, u32[]{:S(2)}) collective-permute-start(s32[1,48]{1,0:T(1,128)S(1)} %pad_add_fusion.1), channel_id=1, source_target_pairs={{0,3},{1,2},{2,1},{3,0},{4,7},{5,6},{6,5},{7,4},{8,11},{9,10},{10,... | collective-permute-start | bytes 584 | tf_op jit(solution)/shard_map/ppermute | solution.py:37
  4.5 3.1 %copy-done.1 = bf16[1024,3584]{1,0:T(8,128)(2,1)S(1)} copy-done((bf16[1024,3584]{1,0:T(8,128)(2,1)S(1)}, bf16[1024,3584]{1,0:T(8,128)(2,1)}, u32[]{:S(2)}) %copy-start.1) | copy-done | bytes 7340056
  8.8 4.2 %far_product.1 = (bf16[128,3584]{1,0:T(8,128)(2,1)S(1)}, bf16[128,3584]{1,0:T(8,128)(2,1)S(1)}, bf16[256,1024]{1,0:T(8,128)(2,1)S(1)}) custom-call(bf16[1024,512]{1,0:T(8,128)(2,1)S(1)} %copy-done.4, bf16[1024,3584]{1,0:T(8,128)(2,1)S(1)} %copy-done.1), custom_call_target="tpu_custom_call" | custom-call | flops 1879048192 | bytes 9699328 | tf_op jit(solution)/shard_map/far_product/pallas_call | solution.py:186
  13.7 3.6 %collective-permute-start.6 = (s32[4,48]{1,0:T(4,128)S(1)}, s32[4,48]{1,0:T(4,128)S(1)}, u32[]{:S(2)}, u32[]{:S(2)}) collective-permute-start(s32[4,48]{1,0:T(4,128)S(1)} %pad_add_fusion.refs_0_), channel_id=1, source_target_pairs={{0,12},{1,13},{2,14},{3,15},{4,8},{5,9},{6,10},{7,11},{8,4},{9,5},... | collective-permute-start | bytes 2312 | tf_op jit(solution)/shard_map/ppermute | solution.py:37
  18.2 1.6 %collective-permute-start.8 = (bf16[32,1792]{1,0:T(8,128)(2,1)S(1)}, bf16[32,1792]{1,0:T(8,128)(2,1)S(1)}, u32[]{:S(2)}, u32[]{:S(2)}) collective-permute-start(bf16[32,1792]{1,0:T(8,128)(2,1)S(1)} %get-tuple-element.172), channel_id=1, source_target_pairs={{0,2},{1,3},{4,0},{5,1},{8,4},{9,5},{12,8},{13,9},{14,12},{15,13},... | collective-permute-start | bytes 344072 | tf_op jit(solution)/shard_map/ppermute | solution.py:79
  20.3 1.6 %collective-permute-done.5.refs_2_ = s32[4,48]{1,0:T(4,128)S(1)} collective-permute-done((s32[4,48]{1,0:T(4,128)S(1)}, s32[4,48]{1,0:T(4,128)S(1)}, u32[]{:S(2)}, u32[]{:S(2)}) %collective-permute-start.5) | collective-permute-done | bytes 800 | tf_op jit(solution)/shard_map/ppermute | solution.py:37
  21.8 4.9 %select_far_product.1 = (bf16[128,3584]{1,0:T(8,128)(2,1)S(1)}, bf16[128,3584]{1,0:T(8,128)(2,1)S(1)}, bf16[256,1024]{1,0:T(8,128)(2,1)S(1)}, s32[32,1]{1,0:T(8,128)S(1)}) custom-call(bf16[1024,512]{1,0:T(8,128)(2,1)S(1)} %copy-done.3, bf16[1024,3584]{1,0:T(8,128)(2,1)S(1)} %copy-done, s32[2,16]{1,0:T(2,128)S(1)} %bitcast.8, ...), custom_call_target="tpu_custom_call" | custom-call | flops 1879048192 | bytes 9699328 | tf_op jit(solution)/shard_map/select_far_product/pallas_call | solution.py:186
  27.1 1.7 %collective-permute-start.11 = (bf16[32,3584]{1,0:T(8,128)(2,1)S(1)}, bf16[32,3584]{1,0:T(8,128)(2,1)S(1)}, u32[]{:S(2)}, u32[]{:S(2)}) collective-permute-start(bf16[32,3584]{1,0:T(8,128)(2,1)S(1)} %get-tuple-element.168), channel_id=1, source_target_pairs={{0,2},{1,3},{4,0},{5,1},{8,4},{9,5},{12,8},{13,9},{14,12},{15,13},... | collective-permute-start | bytes 688136 | tf_op jit(solution)/shard_map/ppermute | solution.py:79
  29.1 3.8 %near_product.2 = (bf16[128,3584]{1,0:T(8,128)(2,1)S(1)}, bf16[128,3584]{1,0:T(8,128)(2,1)S(1)}) custom-call(bf16[256,1024]{1,0:T(8,128)(2,1)S(1)} %get-tuple-element.98.left_ref, bf16[1024,3584]{1,0:T(8,128)(2,1)S(1)} %copy-done.2), custom_call_target="tpu_custom_call" | custom-call | flops 1879048192 | bytes 9699328 | tf_op jit(solution)/shard_map/near_product/pallas_call | solution.py:186
  33.0 2.1 %collective-permute-done.11 = bf16[32,3584]{1,0:T(8,128)(2,1)S(1)} collective-permute-done((bf16[32,3584]{1,0:T(8,128)(2,1)S(1)}, bf16[32,3584]{1,0:T(8,128)(2,1)S(1)}, u32[]{:S(2)}, u32[]{:S(2)}) %collective-permute-start.11) | collective-permute-done | bytes 229408 | tf_op jit(solution)/shard_map/ppermute | solution.py:79
  36.9 1.6 %collective-permute-start.13 = (bf16[32,1792]{1,0:T(8,128)(2,1)S(1)}, bf16[32,1792]{1,0:T(8,128)(2,1)S(1)}, u32[]{:S(2)}, u32[]{:S(2)}) collective-permute-start(bf16[32,1792]{1,0:T(8,128)(2,1)S(1)} %get-tuple-element.105), channel_id=1, source_target_pairs={{0,2},{1,3},{4,0},{5,1},{8,4},{9,5},{12,8},{13,9},{14,12},{15,13},... | collective-permute-start | bytes 344072 | tf_op jit(solution)/shard_map/ppermute | solution.py:79
  38.5 3.7 %near_product.3 = (bf16[128,3584]{1,0:T(8,128)(2,1)S(1)}, bf16[128,3584]{1,0:T(8,128)(2,1)S(1)}) custom-call(bf16[256,1024]{1,0:T(8,128)(2,1)S(1)} %get-tuple-element.102.left_ref, bf16[1024,3584]{1,0:T(8,128)(2,1)S(1)} %copy-done), custom_call_target="tpu_custom_call" | custom-call | flops 1879048192 | bytes 9699328 | tf_op jit(solution)/shard_map/near_product/pallas_call | solution.py:186
  42.4 1.5 %collective-permute-start.19 = (bf16[32,3584]{1,0:T(8,128)(2,1)S(1)}, bf16[32,3584]{1,0:T(8,128)(2,1)S(1)}, u32[]{:S(2)}, u32[]{:S(2)}) collective-permute-start(bf16[32,3584]{1,0:T(8,128)(2,1)S(1)} %add_convert_fusion.8), channel_id=1, source_target_pairs={{0,2},{1,3},{4,0},{5,1},{8,4},{9,5},{12,8},{13,9},{14,12},{15,13},... | collective-permute-start | bytes 688136 | tf_op jit(solution)/shard_map/ppermute | solution.py:79
  46.9 4.0 %collective-permute-done.19 = bf16[32,3584]{1,0:T(8,128)(2,1)S(1)} collective-permute-done((bf16[32,3584]{1,0:T(8,128)(2,1)S(1)}, bf16[32,3584]{1,0:T(8,128)(2,1)S(1)}, u32[]{:S(2)}, u32[]{:S(2)}) %collective-permute-start.19) | collective-permute-done | bytes 229408 | tf_op jit(solution)/shard_map/ppermute | solution.py:79
  50.8 1.7 %collective-permute-done.18 = bf16[32,3584]{1,0:T(8,128)(2,1)S(1)} collective-permute-done((bf16[32,3584]{1,0:T(8,128)(2,1)S(1)}, bf16[32,3584]{1,0:T(8,128)(2,1)S(1)}, u32[]{:S(2)}, u32[]{:S(2)}) %collective-permute-start.18) | collective-permute-done | bytes 229408 | tf_op jit(solution)/shard_map/ppermute | solution.py:79
  52.7 2.7 %collective-permute-done.17 = bf16[32,3584]{1,0:T(8,128)(2,1)S(1)} collective-permute-done((bf16[32,3584]{1,0:T(8,128)(2,1)S(1)}, bf16[32,3584]{1,0:T(8,128)(2,1)S(1)}, u32[]{:S(2)}, u32[]{:S(2)}) %collective-permute-start.17) | collective-permute-done | bytes 229408 | tf_op jit(solution)/shard_map/ppermute | solution.py:79
  61.1 4.3 %collective-permute-done.22 = bf16[32,3584]{1,0:T(8,128)(2,1)S(1)} collective-permute-done((bf16[32,3584]{1,0:T(8,128)(2,1)S(1)}, bf16[32,3584]{1,0:T(8,128)(2,1)S(1)}, u32[]{:S(2)}, u32[]{:S(2)}) %collective-permute-start.22) | collective-permute-done | bytes 229408 | tf_op jit(solution)/shard_map/ppermute | solution.py:79
  66.7 1.5 %collective-permute-start.23 = (bf16[32,3584]{1,0:T(8,128)(2,1)S(1)}, bf16[32,3584]{1,0:T(8,128)(2,1)S(1)}, u32[]{:S(2)}, u32[]{:S(2)}) collective-permute-start(bf16[32,3584]{1,0:T(8,128)(2,1)S(1)} %get-tuple-element.162), channel_id=1, source_target_pairs={{0,2},{1,3},{4,0},{5,1},{8,4},{9,5},{12,8},{13,9},{14,12},{15,13},... | collective-permute-start | bytes 688136 | tf_op jit(solution)/shard_map/ppermute | solution.py:79
  68.8 1.5 %collective-permute-done.25.refs_3_ = bf16[32,3584]{1,0:T(8,128)(2,1)S(1)} collective-permute-done((bf16[32,3584]{1,0:T(8,128)(2,1)S(1)}, bf16[32,3584]{1,0:T(8,128)(2,1)S(1)}, u32[]{:S(2)}, u32[]{:S(2)}) %collective-permute-start.25) | collective-permute-done | bytes 229408 | tf_op jit(solution)/shard_map/ppermute | solution.py:79
  71.5 2.2 %collective-permute-done.23.refs_3_ = bf16[32,3584]{1,0:T(8,128)(2,1)S(1)} collective-permute-done((bf16[32,3584]{1,0:T(8,128)(2,1)S(1)}, bf16[32,3584]{1,0:T(8,128)(2,1)S(1)}, u32[]{:S(2)}, u32[]{:S(2)}) %collective-permute-start.23) | collective-permute-done | bytes 229408 | tf_op jit(solution)/shard_map/ppermute | solution.py:79
  74.5 1.8 %enc_update.1 = (f32[32,3584]{1,0:T(8,128)}, f32[32,3584]{1,0:T(8,128)}, f32[32,3584]{1,0:T(8,128)}, bf16[32,3584]{1,0:T(8,128)(2,1)S(1)}, bf16[32,3584]{1,0:T(8,128)(2,1)S(1)}) custom-call(s32[32,1]{1,0:T(8,128)S(1)} %get-tuple-element.90.code_ref, f32[32,3584]{1,0:T(8,128)S(1)} %copy-done.5, f32[32,3584]{1,0:T(8,128)S(1)} %copy-done.6, ...), custom_call_target="tpu_custom_call" | custom-call | flops 4587520 | bytes 4587520 | tf_op jit(solution)/shard_map/enc_update/pallas_call | solution.py:280
  76.2 1.8 %dec_update.1 = (f32[32,3584]{1,0:T(8,128)}, f32[32,3584]{1,0:T(8,128)}, f32[32,3584]{1,0:T(8,128)}, bf16[2,32,3584]{2,1,0:T(8,128)(2,1)S(1)}) custom-call(s32[32,1]{1,0:T(8,128)S(1)} %get-tuple-element.90.code_ref, f32[32,3584]{1,0:T(8,128)S(1)} %copy-done.8, f32[32,3584]{1,0:T(8,128)S(1)} %copy-done.9, f32[32,3584]{1,0:T(8,128)S(1)} %copy-done.10, ...), custom_call_target="tpu_custom_call" | custom-call | flops 4587520 | bytes 4587520 | tf_op jit(solution)/shard_map/dec_update/pallas_call | solution.py:280
  80.8 7.4 %collective-permute-done.27.refs_1_ = bf16[64,3584]{1,0:T(8,128)(2,1)S(1)} collective-permute-done((bf16[64,3584]{1,0:T(8,128)(2,1)S(1)}, bf16[64,3584]{1,0:T(8,128)(2,1)S(1)}, u32[]{:S(2)}, u32[]{:S(2)}) %collective-permute-start.27) | collective-permute-done | bytes 458784 | tf_op jit(solution)/shard_map/ppermute | solution.py:79
  88.2 2.0 %collective-permute-done.26.refs_0_ = bf16[64,3584]{1,0:T(8,128)(2,1)S(1)} collective-permute-done((bf16[64,3584]{1,0:T(8,128)(2,1)S(1)}, bf16[64,3584]{1,0:T(8,128)(2,1)S(1)}, u32[]{:S(2)}, u32[]{:S(2)}) %collective-permute-start.26) | collective-permute-done | bytes 458784 | tf_op jit(solution)/shard_map/ppermute | solution.py:79
  90.5 1.7 %collective-permute-start.29 = (bf16[64,3584]{1,0:T(8,128)(2,1)S(1)}, bf16[64,3584]{1,0:T(8,128)(2,1)S(1)}, u32[]{:S(2)}, u32[]{:S(2)}) collective-permute-start(bf16[64,3584]{1,0:T(8,128)(2,1)S(1)} %collective-permute-done.27.refs_1_), channel_id=1, source_target_pairs={{0,2},{1,3},{4,0},{5,1},{8,4},{9,5},{12,8},{13,9},{14,12},{15,13},... | collective-permute-start | bytes 1376264 | tf_op jit(solution)/shard_map/ppermute | solution.py:79
  93.8 7.0 %collective-permute-done.28.refs_0_ = bf16[64,3584]{1,0:T(8,128)(2,1)S(1)} collective-permute-done((bf16[64,3584]{1,0:T(8,128)(2,1)S(1)}, bf16[64,3584]{1,0:T(8,128)(2,1)S(1)}, u32[]{:S(2)}, u32[]{:S(2)}) %collective-permute-start.28) | collective-permute-done | bytes 458784 | tf_op jit(solution)/shard_map/ppermute | solution.py:79
  101.4 1.5 %collective-permute-start.32 = (bf16[64,3584]{1,0:T(8,128)(2,1)S(1)}, bf16[64,3584]{1,0:T(8,128)(2,1)S(1)}, u32[]{:S(2)}, u32[]{:S(2)}) collective-permute-start(bf16[64,3584]{1,0:T(8,128)(2,1)S(1)} %collective-permute-done.29.refs_1_), channel_id=1, source_target_pairs={{0,2},{1,3},{4,0},{5,1},{8,4},{9,5},{12,8},{13,9},{14,12},{15,13},... | collective-permute-start | bytes 1376264 | tf_op jit(solution)/shard_map/ppermute | solution.py:79
  104.7 5.8 %collective-permute-done.31.refs_0_ = bf16[64,3584]{1,0:T(8,128)(2,1)S(1)} collective-permute-done((bf16[64,3584]{1,0:T(8,128)(2,1)S(1)}, bf16[64,3584]{1,0:T(8,128)(2,1)S(1)}, u32[]{:S(2)}, u32[]{:S(2)}) %collective-permute-start.31) | collective-permute-done | bytes 458784 | tf_op jit(solution)/shard_map/ppermute | solution.py:79
  110.5 1.6 %collective-permute-done.32.refs_1_ = bf16[64,3584]{1,0:T(8,128)(2,1)S(1)} collective-permute-done((bf16[64,3584]{1,0:T(8,128)(2,1)S(1)}, bf16[64,3584]{1,0:T(8,128)(2,1)S(1)}, u32[]{:S(2)}, u32[]{:S(2)}) %collective-permute-start.32) | collective-permute-done | bytes 458784 | tf_op jit(solution)/shard_map/ppermute | solution.py:79
  112.2 1.8 %collective-permute-start.36 = (bf16[64,1792]{1,0:T(8,128)(2,1)S(1)}, bf16[64,1792]{1,0:T(8,128)(2,1)S(1)}, u32[]{:S(2)}, u32[]{:S(2)}) collective-permute-start(bf16[64,1792]{1,0:T(8,128)(2,1)S(1)} %slice.135), channel_id=1, source_target_pairs={{0,2},{1,3},{4,0},{5,1},{8,4},{9,5},{12,8},{13,9},{14,12},{15,13},... | collective-permute-start | bytes 688136 | tf_op jit(solution)/shard_map/ppermute | solution.py:79
  116.0 2.2 %collective-permute-done.36.refs_1_ = bf16[64,1792]{1,0:T(8,128)(2,1)S(1)} collective-permute-done((bf16[64,1792]{1,0:T(8,128)(2,1)S(1)}, bf16[64,1792]{1,0:T(8,128)(2,1)S(1)}, u32[]{:S(2)}, u32[]{:S(2)}) %collective-permute-start.36) | collective-permute-done | bytes 229408 | tf_op jit(solution)/shard_map/ppermute | solution.py:79
  118.2 1.7 %collective-permute-done.35.refs_0_ = bf16[64,1792]{1,0:T(8,128)(2,1)S(1)} collective-permute-done((bf16[64,1792]{1,0:T(8,128)(2,1)S(1)}, bf16[64,1792]{1,0:T(8,128)(2,1)S(1)}, u32[]{:S(2)}, u32[]{:S(2)}) %collective-permute-start.35) | collective-permute-done | bytes 229408 | tf_op jit(solution)/shard_map/ppermute | solution.py:79
  (110 shorter events, 31.7 us)
Async XLA Ops:
  1.4 11.6 %collective-permute-start.2 = (s32[1,48]{1,0:T(1,128)S(1)}, s32[1,48]{1,0:T(1,128)S(1)}, u32[]{:S(2)}, u32[]{:S(2)}) collective-permute-start(s32[1,48]{1,0:T(1,128)S(1)} %pad_add_fusion.1), channel_id=1, source_target_pairs={{0,3},{1,2},{2,1},{3,0},{4,7},{5,6},{6,5},{7,4},{8,11},{9,10},{10,... | collective-permute-start | bytes 584 | tf_op jit(solution)/shard_map/ppermute | solution.py:37
  3.9 9.2 %collective-permute-start.1 = (s32[1,48]{1,0:T(1,128)S(1)}, s32[1,48]{1,0:T(1,128)S(1)}, u32[]{:S(2)}, u32[]{:S(2)}) collective-permute-start(s32[1,48]{1,0:T(1,128)S(1)} %pad_add_fusion.1), channel_id=1, source_target_pairs={{0,2},{1,3},{2,0},{3,1},{4,6},{5,7},{6,4},{7,5},{8,10},{9,11},{10,... | collective-permute-start | bytes 584 | tf_op jit(solution)/shard_map/ppermute | solution.py:37
  4.5 8.6 %collective-permute-start = (s32[1,48]{1,0:T(1,128)S(1)}, s32[1,48]{1,0:T(1,128)S(1)}, u32[]{:S(2)}, u32[]{:S(2)}) collective-permute-start(s32[1,48]{1,0:T(1,128)S(1)} %pad_add_fusion.1), channel_id=1, source_target_pairs={{0,1},{1,0},{2,3},{3,2},{4,5},{5,4},{6,7},{7,6},{8,9},{9,8},{10,11... | collective-permute-start | bytes 584 | tf_op jit(solution)/shard_map/ppermute | solution.py:37
  13.7 6.6 %collective-permute-start.6 = (s32[4,48]{1,0:T(4,128)S(1)}, s32[4,48]{1,0:T(4,128)S(1)}, u32[]{:S(2)}, u32[]{:S(2)}) collective-permute-start(s32[4,48]{1,0:T(4,128)S(1)} %pad_add_fusion.refs_0_), channel_id=1, source_target_pairs={{0,12},{1,13},{2,14},{3,15},{4,8},{5,9},{6,10},{7,11},{8,4},{9,5},... | collective-permute-start | bytes 2312 | tf_op jit(solution)/shard_map/ppermute | solution.py:37
  18.2 8.6 %collective-permute-start.8 = (bf16[32,1792]{1,0:T(8,128)(2,1)S(1)}, bf16[32,1792]{1,0:T(8,128)(2,1)S(1)}, u32[]{:S(2)}, u32[]{:S(2)}) collective-permute-start(bf16[32,1792]{1,0:T(8,128)(2,1)S(1)} %get-tuple-element.172), channel_id=1, source_target_pairs={{0,2},{1,3},{4,0},{5,1},{8,4},{9,5},{12,8},{13,9},{14,12},{15,13},... | collective-permute-start | bytes 344072 | tf_op jit(solution)/shard_map/ppermute | solution.py:79
  19.8 7.1 %collective-permute-start.7 = (bf16[32,1792]{1,0:T(8,128)(2,1)S(1)}, bf16[32,1792]{1,0:T(8,128)(2,1)S(1)}, u32[]{:S(2)}, u32[]{:S(2)}) collective-permute-start(bf16[32,1792]{1,0:T(8,128)(2,1)S(1)} %get-tuple-element.173), channel_id=1, source_target_pairs={{0,4},{1,5},{4,8},{5,9},{8,12},{9,13},{12,14},{13,15},{14,10},{15,... | collective-permute-start | bytes 344072 | tf_op jit(solution)/shard_map/ppermute | solution.py:79
  27.1 8.1 %collective-permute-start.11 = (bf16[32,3584]{1,0:T(8,128)(2,1)S(1)}, bf16[32,3584]{1,0:T(8,128)(2,1)S(1)}, u32[]{:S(2)}, u32[]{:S(2)}) collective-permute-start(bf16[32,3584]{1,0:T(8,128)(2,1)S(1)} %get-tuple-element.168), channel_id=1, source_target_pairs={{0,2},{1,3},{4,0},{5,1},{8,4},{9,5},{12,8},{13,9},{14,12},{15,13},... | collective-permute-start | bytes 688136 | tf_op jit(solution)/shard_map/ppermute | solution.py:79
  28.7 7.7 %collective-permute-start.10 = (bf16[32,3584]{1,0:T(8,128)(2,1)S(1)}, bf16[32,3584]{1,0:T(8,128)(2,1)S(1)}, u32[]{:S(2)}, u32[]{:S(2)}) collective-permute-start(bf16[32,3584]{1,0:T(8,128)(2,1)S(1)} %get-tuple-element.169), channel_id=1, source_target_pairs={{0,4},{1,5},{4,8},{5,9},{8,12},{9,13},{12,14},{13,15},{14,10},{15,... | collective-permute-start | bytes 688136 | tf_op jit(solution)/shard_map/ppermute | solution.py:79
  36.4 7.5 %collective-permute-start.15 = (bf16[128,3584]{1,0:T(8,128)(2,1)S(1)}, bf16[128,3584]{1,0:T(8,128)(2,1)S(1)}, u32[]{:S(2)}, u32[]{:S(2)}) collective-permute-start(bf16[128,3584]{1,0:T(8,128)(2,1)S(1)} %get-tuple-element.101), channel_id=1, source_target_pairs={{0,1},{1,0},{2,3},{3,2},{4,5},{5,4},{6,7},{7,6},{8,9},{9,8},{10,11... | collective-permute-start | bytes 2752520 | tf_op jit(solution)/shard_map/ppermute | solution.py:37
  42.2 15.7 %collective-permute-start.14 = (bf16[128,3584]{1,0:T(8,128)(2,1)S(1)}, bf16[128,3584]{1,0:T(8,128)(2,1)S(1)}, u32[]{:S(2)}, u32[]{:S(2)}) collective-permute-start(bf16[128,3584]{1,0:T(8,128)(2,1)S(1)} %get-tuple-element.107), channel_id=1, source_target_pairs={{0,1},{1,0},{2,3},{3,2},{4,5},{5,4},{6,7},{7,6},{8,9},{9,8},{10,11... | collective-permute-start | bytes 2752520 | tf_op jit(solution)/shard_map/ppermute | solution.py:37
  42.4 8.5 %collective-permute-start.19 = (bf16[32,3584]{1,0:T(8,128)(2,1)S(1)}, bf16[32,3584]{1,0:T(8,128)(2,1)S(1)}, u32[]{:S(2)}, u32[]{:S(2)}) collective-permute-start(bf16[32,3584]{1,0:T(8,128)(2,1)S(1)} %add_convert_fusion.8), channel_id=1, source_target_pairs={{0,2},{1,3},{4,0},{5,1},{8,4},{9,5},{12,8},{13,9},{14,12},{15,13},... | collective-permute-start | bytes 688136 | tf_op jit(solution)/shard_map/ppermute | solution.py:79
  44.0 8.5 %collective-permute-start.18 = (bf16[32,3584]{1,0:T(8,128)(2,1)S(1)}, bf16[32,3584]{1,0:T(8,128)(2,1)S(1)}, u32[]{:S(2)}, u32[]{:S(2)}) collective-permute-start(bf16[32,3584]{1,0:T(8,128)(2,1)S(1)} %add_convert_fusion.9), channel_id=1, source_target_pairs={{0,4},{1,5},{4,8},{5,9},{8,12},{9,13},{12,14},{13,15},{14,10},{15,... | collective-permute-start | bytes 688136 | tf_op jit(solution)/shard_map/ppermute | solution.py:79
  44.8 10.6 %collective-permute-start.17 = (bf16[32,3584]{1,0:T(8,128)(2,1)S(1)}, bf16[32,3584]{1,0:T(8,128)(2,1)S(1)}, u32[]{:S(2)}, u32[]{:S(2)}) collective-permute-start(bf16[32,3584]{1,0:T(8,128)(2,1)S(1)} %get-tuple-element.166), channel_id=1, source_target_pairs={{0,2},{1,3},{4,0},{5,1},{8,4},{9,5},{12,8},{13,9},{14,12},{15,13},... | collective-permute-start | bytes 688136 | tf_op jit(solution)/shard_map/ppermute | solution.py:79
  46.3 10.4 %collective-permute-start.16 = (bf16[32,3584]{1,0:T(8,128)(2,1)S(1)}, bf16[32,3584]{1,0:T(8,128)(2,1)S(1)}, u32[]{:S(2)}, u32[]{:S(2)}) collective-permute-start(bf16[32,3584]{1,0:T(8,128)(2,1)S(1)} %get-tuple-element.167), channel_id=1, source_target_pairs={{0,4},{1,5},{4,8},{5,9},{8,12},{9,13},{12,14},{13,15},{14,10},{15,... | collective-permute-start | bytes 688136 | tf_op jit(solution)/shard_map/ppermute | solution.py:79
  56.8 8.6 %collective-permute-start.22 = (bf16[32,3584]{1,0:T(8,128)(2,1)S(1)}, bf16[32,3584]{1,0:T(8,128)(2,1)S(1)}, u32[]{:S(2)}, u32[]{:S(2)}) collective-permute-start(bf16[32,3584]{1,0:T(8,128)(2,1)S(1)} %add_convert_fusion.1), channel_id=1, source_target_pairs={{0,2},{1,3},{4,0},{5,1},{8,4},{9,5},{12,8},{13,9},{14,12},{15,13},... | collective-permute-start | bytes 688136 | tf_op jit(solution)/shard_map/ppermute | solution.py:79
  58.0 8.6 %collective-permute-start.20 = (bf16[32,3584]{1,0:T(8,128)(2,1)S(1)}, bf16[32,3584]{1,0:T(8,128)(2,1)S(1)}, u32[]{:S(2)}, u32[]{:S(2)}) collective-permute-start(bf16[32,3584]{1,0:T(8,128)(2,1)S(1)} %add_convert_fusion.3), channel_id=1, source_target_pairs={{0,4},{1,5},{4,8},{5,9},{8,12},{9,13},{12,14},{13,15},{14,10},{15,... | collective-permute-start | bytes 688136 | tf_op jit(solution)/shard_map/ppermute | solution.py:79
  59.0 11.3 %collective-permute-start.25 = (bf16[32,3584]{1,0:T(8,128)(2,1)S(1)}, bf16[32,3584]{1,0:T(8,128)(2,1)S(1)}, u32[]{:S(2)}, u32[]{:S(2)}) collective-permute-start(bf16[32,3584]{1,0:T(8,128)(2,1)S(1)} %get-tuple-element.164), channel_id=1, source_target_pairs={{0,2},{1,3},{4,0},{5,1},{8,4},{9,5},{12,8},{13,9},{14,12},{15,13},... | collective-permute-start | bytes 688136 | tf_op jit(solution)/shard_map/ppermute | solution.py:79
  60.0 11.4 %collective-permute-start.24 = (bf16[32,3584]{1,0:T(8,128)(2,1)S(1)}, bf16[32,3584]{1,0:T(8,128)(2,1)S(1)}, u32[]{:S(2)}, u32[]{:S(2)}) collective-permute-start(bf16[32,3584]{1,0:T(8,128)(2,1)S(1)} %get-tuple-element.165), channel_id=1, source_target_pairs={{0,4},{1,5},{4,8},{5,9},{8,12},{9,13},{12,14},{13,15},{14,10},{15,... | collective-permute-start | bytes 688136 | tf_op jit(solution)/shard_map/ppermute | solution.py:79
  66.7 6.9 %collective-permute-start.23 = (bf16[32,3584]{1,0:T(8,128)(2,1)S(1)}, bf16[32,3584]{1,0:T(8,128)(2,1)S(1)}, u32[]{:S(2)}, u32[]{:S(2)}) collective-permute-start(bf16[32,3584]{1,0:T(8,128)(2,1)S(1)} %get-tuple-element.162), channel_id=1, source_target_pairs={{0,2},{1,3},{4,0},{5,1},{8,4},{9,5},{12,8},{13,9},{14,12},{15,13},... | collective-permute-start | bytes 688136 | tf_op jit(solution)/shard_map/ppermute | solution.py:79
  78.0 10.2 %collective-permute-start.27 = (bf16[64,3584]{1,0:T(8,128)(2,1)S(1)}, bf16[64,3584]{1,0:T(8,128)(2,1)S(1)}, u32[]{:S(2)}, u32[]{:S(2)}) collective-permute-start(bf16[64,3584]{1,0:T(8,128)(2,1)S(1)} %bitcast.4), channel_id=1, source_target_pairs={{0,2},{1,3},{4,0},{5,1},{8,4},{9,5},{12,8},{13,9},{14,12},{15,13},... | collective-permute-start | bytes 1376264 | tf_op jit(solution)/shard_map/ppermute | solution.py:79
  79.5 10.7 %collective-permute-start.26 = (bf16[64,3584]{1,0:T(8,128)(2,1)S(1)}, bf16[64,3584]{1,0:T(8,128)(2,1)S(1)}, u32[]{:S(2)}, u32[]{:S(2)}) collective-permute-start(bf16[64,3584]{1,0:T(8,128)(2,1)S(1)} %bitcast.5), channel_id=1, source_target_pairs={{0,4},{1,5},{4,8},{5,9},{8,12},{9,13},{12,14},{13,15},{14,10},{15,... | collective-permute-start | bytes 1376264 | tf_op jit(solution)/shard_map/ppermute | solution.py:79
  80.0 12.7 %collective-permute-start.30 = (bf16[64,3584]{1,0:T(8,128)(2,1)S(1)}, bf16[64,3584]{1,0:T(8,128)(2,1)S(1)}, u32[]{:S(2)}, u32[]{:S(2)}) collective-permute-start(bf16[64,3584]{1,0:T(8,128)(2,1)S(1)} %bitcast.6), channel_id=1, source_target_pairs={{0,1},{1,0},{2,3},{3,2},{4,5},{5,4},{6,7},{7,6},{8,9},{9,8},{10,11... | collective-permute-start | bytes 1376264 | tf_op jit(solution)/shard_map/ppermute | solution.py:37
  90.2 10.7 %collective-permute-start.28 = (bf16[64,3584]{1,0:T(8,128)(2,1)S(1)}, bf16[64,3584]{1,0:T(8,128)(2,1)S(1)}, u32[]{:S(2)}, u32[]{:S(2)}) collective-permute-start(bf16[64,3584]{1,0:T(8,128)(2,1)S(1)} %collective-permute-done.26.refs_0_), channel_id=1, source_target_pairs={{0,4},{1,5},{4,8},{5,9},{8,12},{9,13},{12,14},{13,15},{14,10},{15,... | collective-permute-start | bytes 1376264 | tf_op jit(solution)/shard_map/ppermute | solution.py:79
  90.5 10.4 %collective-permute-start.29 = (bf16[64,3584]{1,0:T(8,128)(2,1)S(1)}, bf16[64,3584]{1,0:T(8,128)(2,1)S(1)}, u32[]{:S(2)}, u32[]{:S(2)}) collective-permute-start(bf16[64,3584]{1,0:T(8,128)(2,1)S(1)} %collective-permute-done.27.refs_1_), channel_id=1, source_target_pairs={{0,2},{1,3},{4,0},{5,1},{8,4},{9,5},{12,8},{13,9},{14,12},{15,13},... | collective-permute-start | bytes 1376264 | tf_op jit(solution)/shard_map/ppermute | solution.py:79
  92.2 10.7 %collective-permute-start.33 = (bf16[64,3584]{1,0:T(8,128)(2,1)S(1)}, bf16[64,3584]{1,0:T(8,128)(2,1)S(1)}, u32[]{:S(2)}, u32[]{:S(2)}) collective-permute-start(bf16[64,3584]{1,0:T(8,128)(2,1)S(1)} %collective-permute-done.26.refs_0_), channel_id=1, source_target_pairs={{0,1},{1,0},{2,3},{3,2},{4,5},{5,4},{6,7},{7,6},{8,9},{9,8},{10,11... | collective-permute-start | bytes 1376264 | tf_op jit(solution)/shard_map/ppermute | solution.py:37
  92.2 11.2 %collective-permute-start.34 = (bf16[64,3584]{1,0:T(8,128)(2,1)S(1)}, bf16[64,3584]{1,0:T(8,128)(2,1)S(1)}, u32[]{:S(2)}, u32[]{:S(2)}) collective-permute-start(bf16[64,3584]{1,0:T(8,128)(2,1)S(1)} %collective-permute-done.27.refs_1_), channel_id=1, source_target_pairs={{0,1},{1,0},{2,3},{3,2},{4,5},{5,4},{6,7},{7,6},{8,9},{9,8},{10,11... | collective-permute-start | bytes 1376264 | tf_op jit(solution)/shard_map/ppermute | solution.py:37
  100.9 9.6 %collective-permute-start.31 = (bf16[64,3584]{1,0:T(8,128)(2,1)S(1)}, bf16[64,3584]{1,0:T(8,128)(2,1)S(1)}, u32[]{:S(2)}, u32[]{:S(2)}) collective-permute-start(bf16[64,3584]{1,0:T(8,128)(2,1)S(1)} %collective-permute-done.28.refs_0_), channel_id=1, source_target_pairs={{0,4},{1,5},{4,8},{5,9},{8,12},{9,13},{12,14},{13,15},{14,10},{15,... | collective-permute-start | bytes 1376264 | tf_op jit(solution)/shard_map/ppermute | solution.py:79
  101.4 10.8 %collective-permute-start.32 = (bf16[64,3584]{1,0:T(8,128)(2,1)S(1)}, bf16[64,3584]{1,0:T(8,128)(2,1)S(1)}, u32[]{:S(2)}, u32[]{:S(2)}) collective-permute-start(bf16[64,3584]{1,0:T(8,128)(2,1)S(1)} %collective-permute-done.29.refs_1_), channel_id=1, source_target_pairs={{0,2},{1,3},{4,0},{5,1},{8,4},{9,5},{12,8},{13,9},{14,12},{15,13},... | collective-permute-start | bytes 1376264 | tf_op jit(solution)/shard_map/ppermute | solution.py:79
  102.9 11.3 %collective-permute-start.37 = (bf16[64,3584]{1,0:T(8,128)(2,1)S(1)}, bf16[64,3584]{1,0:T(8,128)(2,1)S(1)}, u32[]{:S(2)}, u32[]{:S(2)}) collective-permute-start(bf16[64,3584]{1,0:T(8,128)(2,1)S(1)} %collective-permute-done.28.refs_0_), channel_id=1, source_target_pairs={{0,1},{1,0},{2,3},{3,2},{4,5},{5,4},{6,7},{7,6},{8,9},{9,8},{10,11... | collective-permute-start | bytes 1376264 | tf_op jit(solution)/shard_map/ppermute | solution.py:37
  102.9 11.8 %collective-permute-start.38 = (bf16[64,3584]{1,0:T(8,128)(2,1)S(1)}, bf16[64,3584]{1,0:T(8,128)(2,1)S(1)}, u32[]{:S(2)}, u32[]{:S(2)}) collective-permute-start(bf16[64,3584]{1,0:T(8,128)(2,1)S(1)} %collective-permute-done.29.refs_1_), channel_id=1, source_target_pairs={{0,1},{1,0},{2,3},{3,2},{4,5},{5,4},{6,7},{7,6},{8,9},{9,8},{10,11... | collective-permute-start | bytes 1376264 | tf_op jit(solution)/shard_map/ppermute | solution.py:37
  114.2 6.2 %collective-permute-start.41 = (bf16[64,3584]{1,0:T(8,128)(2,1)S(1)}, bf16[64,3584]{1,0:T(8,128)(2,1)S(1)}, u32[]{:S(2)}, u32[]{:S(2)}) collective-permute-start(bf16[64,3584]{1,0:T(8,128)(2,1)S(1)} %collective-permute-done.31.refs_0_), channel_id=1, source_target_pairs={{0,1},{1,0},{2,3},{3,2},{4,5},{5,4},{6,7},{7,6},{8,9},{9,8},{10,11... | collective-permute-start | bytes 1376264 | tf_op jit(solution)/shard_map/ppermute | solution.py:37
  114.2 6.2 %collective-permute-start.42 = (bf16[64,3584]{1,0:T(8,128)(2,1)S(1)}, bf16[64,3584]{1,0:T(8,128)(2,1)S(1)}, u32[]{:S(2)}, u32[]{:S(2)}) collective-permute-start(bf16[64,3584]{1,0:T(8,128)(2,1)S(1)} %collective-permute-done.32.refs_1_), channel_id=1, source_target_pairs={{0,1},{1,0},{2,3},{3,2},{4,5},{5,4},{6,7},{7,6},{8,9},{9,8},{10,11... | collective-permute-start | bytes 1376264 | tf_op jit(solution)/shard_map/ppermute | solution.py:37
  (25 other events, 286.8 us)

commit v7 on v5

--- a/solution.py
+++ b/solution.py
@@ -39,6 +39,10 @@
 
 def after(value, *others):
     return lax.optimization_barrier((value,) + others)[0]
+
+
+def tied(*values):
+    return lax.optimization_barrier(values)
 
 
 def params(mebibytes):
@@ -130,80 +134,103 @@
     return (code + jnp.where(code < 0, -0.5, 0.5)).astype(jnp.int32)
 
 
-def multiply(by_slot, right_ref, outs):
-    out = jnp.dot(by_slot[...], right_ref[...], preferred_element_type=jnp.float32)
+def product_kernel(size, rows, count, coef_ref, right_hbm, *refs):
+    if count:
+        picks_ref, pieces, refs = refs[0], refs[1 : count + 1], refs[count + 1 :]
+        outs, own_code, table, codes = refs[:4], refs[4], refs[-2], refs[-1]
+        refs = refs[5:-2]
+    else:
+        outs, refs = refs[:4], refs[4:]
+    right, by_latent, left, total, stage, sems_in, sems_out = refs
+    tokens, width = right.shape
     part = outs[0].shape[0]
-    for i, ref in enumerate(outs):
-        ref[...] = out[i * part : (i + 1) * part].astype(ref.dtype)
-
-
-def product_kernel(size, rows, coef_ref, right_ref, *refs):
-    outs, (by_latent, by_slot) = refs[:4], refs[4:]
-
-    @pl.when(pl.program_id(0) == 0)
-    def _():
-        by_latent[...] = coef_ref[...].T
-        ordered_rows(size, rows, by_latent, by_slot)
-
-    multiply(by_slot, right_ref, outs)
-
-
-def select_kernel(size, rows, count, coef_ref, right_ref, picks_ref, *refs):
-    pieces, refs = refs[:count], refs[count:]
-    outs, own_code, (by_latent, by_slot, table, codes) = refs[:4], refs[4], refs[5:]
-
-    @pl.when(pl.program_id(0) == 0)
-    def _():
-        height = size // count
+    reads, passes, tile = 8, 2, 512
+    height, depth = tokens // reads, tokens // passes
+
+    def read(i):
+        span = pl.ds(i * height, height)
+        return pltpu.make_async_copy(right_hbm.at[span], right.at[span], sems_in.at[i])
+
+    def write(i, group):
+        columns = pl.ds(pl.multiple_of(i * tile, tile), tile)
+        return pltpu.make_async_copy(
+            stage.at[pl.ds(group * part, part), columns],
+            outs[group].at[:, columns],
+            sems_out.at[i, group],
+        )
+
+    for i in range(reads):
+        read(i).start()
+    if count:
+        piece_rows = size // count
         for i, piece in enumerate(pieces):
-            table[i * height : (i + 1) * height] = piece[...]
+            table[i * piece_rows : (i + 1) * piece_rows] = piece[...]
         code = row_codes(size, rows, table[...], picks_ref)
         codes[...] = code
         own_code[...] = codes[pl.ds(pl.multiple_of(lax.axis_index("latent") * rows, rows), rows)]
-        tokens = lax.broadcasted_iota(jnp.int32, by_latent.shape, 1)
-        by_latent[...] = jnp.where(
-            code == KEPT, coef_ref[...].T, (tokens == code).astype(by_latent.dtype)
-        )
-        ordered_rows(size, rows, by_latent, by_slot)
-
-    multiply(by_slot, right_ref, outs)
-
-
-def product(coef, right, size, rows, vmem, picks=None, table=()):
+        chosen = lax.broadcasted_iota(jnp.int32, by_latent.shape, 1) == code
+        by_latent[...] = jnp.where(code == KEPT, coef_ref[...].T, chosen.astype(by_latent.dtype))
+    else:
+        by_latent[...] = coef_ref[...].T
+    ordered_rows(size, rows, by_latent, left)
+    for step in range(passes):
+        for i in range(step * reads // passes, (step + 1) * reads // passes):
+            read(i).wait()
+        span = slice(step * depth, (step + 1) * depth)
+
+        @pl.loop(0, width // tile)
+        def _(i):
+            columns = pl.ds(pl.multiple_of(i * tile, tile), tile)
+            out = jnp.dot(left[:, span], right[span, columns], preferred_element_type=jnp.float32)
+            if step > 0:
+                out = out + total[:, columns]
+            if step < passes - 1:
+                total[:, columns] = out
+            else:
+                stage[:, columns] = out.astype(stage.dtype)
+                for group in range(4):
+                    write(i, group).start()
+
+    @pl.loop(0, width // tile)
+    def _(i):
+        for group in range(4):
+            write(i, group).wait()
+
+
+def product(coef, right, size, rows, picks=None, table=()):
     tokens, latents = coef.shape
     width = right.shape[1]
-    tile = 512
     part = latents // 4
-    fixed = lambda j: (0, 0)
-    in_specs = [pl.BlockSpec((tokens, latents), fixed), pl.BlockSpec((tokens, tile), lambda j: (0, j))]
-    out_specs = [pl.BlockSpec((part, tile), lambda j: (0, j))] * 4
+    vmem, anywhere = (pl.BlockSpec(memory_space=space) for space in (pltpu.VMEM, pl.ANY))
+    others = [] if picks is None else [picks] + list(table)
     out_shape = [jax.ShapeDtypeStruct((part, width), coef.dtype)] * 4
-    scratch = [pltpu.VMEM((latents, tokens), coef.dtype)] * 2
-    kernel = functools.partial(product_kernel, size, rows)
-    operands = [coef, right]
-    if picks is not None:
-        kernel = functools.partial(select_kernel, size, rows, len(table))
-        operands += [picks] + list(table)
-        in_specs += [pl.BlockSpec(value.shape, fixed) for value in operands[2:]]
-        out_specs.append(pl.BlockSpec((rows, 1), fixed))
+    scratch = [
+        pltpu.VMEM((tokens, width), coef.dtype),
+        pltpu.VMEM((latents, tokens), coef.dtype),
+        pltpu.VMEM((latents, tokens), coef.dtype),
+        pltpu.VMEM((latents, width), jnp.float32),
+        pltpu.VMEM((latents, width), coef.dtype),
+        pltpu.SemaphoreType.DMA((8,)),
+        pltpu.SemaphoreType.DMA((width // 512, 4)),
+    ]
+    if others:
         out_shape.append(jax.ShapeDtypeStruct((rows, 1), jnp.int32))
         scratch += [
             pltpu.VMEM((size, table[0].shape[1]), jnp.int32),
             pltpu.VMEM((latents, 1), jnp.int32),
         ]
     return pl.pallas_call(
-        kernel,
-        grid=(width // tile,),
-        in_specs=in_specs,
-        out_specs=out_specs,
+        functools.partial(product_kernel, size, rows, len(table)),
+        in_specs=[vmem, anywhere] + [vmem] * len(others),
+        out_specs=[anywhere] * 4 + [vmem] * (len(out_shape) - 4),
         out_shape=out_shape,
         scratch_shapes=scratch,
-        compiler_params=params(vmem),
+        compiler_params=params(56),
         cost_estimate=cost(
             2 * latents * tokens * width, 2 * (tokens * width + latents * (tokens + width))
         ),
-        name="product" if picks is None else "select_product",
-    )(*operands)
+        name="select_product" if others else "product",
+    )(coef, right, *others)
 
 
 def term(kept, from_core, slot, rows):
@@ -350,10 +377,6 @@
     chips = size // 2
     stages = gather_table(jnp.concatenate([send_count, dead_order], axis=1), size)
     table = stages[-1]
-    dec = product(latent_act, out_grad, size, rows, 56)
-    dec_far = after(dec[0], *stages[0])
-    dec_kept, dec_core = [dec[1], dec[3]], [swap(dec_far, 1, size), swap(dec[2], 1, size)]
-
     def begin(kept, from_core):
         far = term(kept, from_core, 0, rows).astype(jnp.bfloat16)
         return [far[:, :half], far[:, half:]]
@@ -372,17 +395,28 @@
             moving.append(value.astype(jnp.bfloat16))
         return moving
 
-    dec_moving = begin(dec_kept, dec_core)
+    dec = product(latent_act, out_grad, size, rows)
+    dec_far = after(dec[0], *stages[0])
+    dec_kept, dec_core = [dec[1], dec[3]], [swap(dec_far, 1, size), swap(dec[2], 1, size)]
+    dec_moving = begin(dec_kept, after(dec_core, table[0]))
     *enc, code = product(
-        after(enc_coef, *dec_moving), x_rows, size, rows, 24, pick_rows[0].T, table
+        after(enc_coef, *dec_moving), x_rows, size, rows, pick_rows[0].T, table
     )
+    dec_came, enc_far = tied(travel(dec_moving), enc[0])
+    enc_kept, enc_core = [enc[1], enc[3]], [swap(enc_far, 1, size), swap(enc[2], 1, size)]
+    dec_moving = advance(dec_came, dec_kept, dec_core, 1)
     dec_came = travel(dec_moving)
-    enc_far, enc_near = after((enc[0], enc[2]), *dec_came)
-    enc_kept, enc_core = [enc[1], enc[3]], [swap(enc_far, 1, size), swap(enc_near, 1, size)]
-    enc_came = travel(begin(enc_kept, enc_core))
+    enc_moving = begin(enc_kept, after(enc_core, *dec_moving))
+    enc_came = travel(enc_moving)
+    dec_came = after(dec_came, *enc_moving)
     for hop in range(1, chips // 2):
-        dec_came = travel(advance(dec_came, dec_kept, dec_core, hop))
-        enc_came = travel(advance(enc_came, enc_kept, enc_core, hop))
+        if hop + 1 < chips // 2:
+            dec_moving = advance(dec_came, dec_kept, dec_core, hop + 1)
+            dec_came = travel(dec_moving)
+            enc_came = after(enc_came, *dec_moving)
+        enc_moving = advance(enc_came, enc_kept, enc_core, hop)
+        enc_came = travel(enc_moving)
+        dec_came = after(dec_came, *enc_moving)
     enc_out, enc_mo, enc_vo, enc_block, fresh = update(
         enc_kernel,
         code,

time: 124 us -> 125 us (level)
  waiting for transfers between devices: 57.8 us -> 51 us
  Pallas kernels: 26.4 us -> 32.7 us
    pallas_call x2, Pallas kernels: 16.5 us -> 22.8 us  [product(): pl.pallas_call(functools.partial(product_kernel, size, rows, len(table)),...]
    ppermute x24, waiting for transfers between devices: 54.4 us -> 48.8 us  [shift(): return lax.ppermute(value, 'latent', pairs)]
  transfers between devices with their start and end apart: 43 -> 43, of which waited for: 21 -> 23; matrix products, arithmetic and copies ran while one was open for 2% -> 2% of each run, Pallas kernels for 19% -> 23%
where the time goes in v7:
time: 125 us
  waiting for transfers between devices  51 us (41%)
  starting transfers between devices  35.7 us (29%)
  Pallas kernels  32.7 us (26%)
  other arithmetic  3.76 us (3%)
    ppermute x24, waiting for transfers between devices, shift(): return lax.ppermute(value, 'latent', pairs)  48.8 us
    ppermute x24, starting transfers between devices, shift(): return lax.ppermute(value, 'latent', pairs)  24.8 us
    pallas_call x2, Pallas kernels, product(): pl.pallas_call(functools.partial(product_kernel, size, rows, len(table)),...  22.8 us
    ppermute x19, starting transfers between devices, swap(): return lax.ppermute(value, 'latent', [(i, i ^ bits) for i in range(size)])  10.9 us
    pallas_call x6, Pallas kernels, place(): pl.pallas_call(functools.partial(place_kernel, plan, size, rows, count),...  6.39 us
    pallas_call x2, Pallas kernels, update(): pl.pallas_call(kernel, grid=(rows // tile,), in_specs=[last_rows(value) f...  3.51 us
  transfers between devices with their start and end apart: 43, of which 23 were waited for; matrix products, arithmetic and copies ran while one was open for 2% of the time, Pallas kernels for 23%

profile of v7, /device:TPU:0, one launch (start us, length us, event | category | flops | bytes accessed | tf_op | source)
XLA Modules:
  0.0 124.8 jit_solution(220256031760354639)
XLA Ops:
  1.4 2.4 %collective-permute-start.2 = (s32[1,48]{1,0:T(1,128)S(1)}, s32[1,48]{1,0:T(1,128)S(1)}, u32[]{:S(2)}, u32[]{:S(2)}) collective-permute-start(s32[1,48]{1,0:T(1,128)S(1)} %pad_add_fusion.1), channel_id=1, source_target_pairs={{0,3},{1,2},{2,1},{3,0},{4,7},{5,6},{6,5},{7,4},{8,11},{9,10},{10,... | collective-permute-start | bytes 584 | tf_op jit(solution)/shard_map/ppermute | solution.py:37
  4.5 10.6 %product.1 = (bf16[128,3584]{1,0:T(8,128)(2,1)}, bf16[128,3584]{1,0:T(8,128)(2,1)}, bf16[128,3584]{1,0:T(8,128)(2,1)}, bf16[128,3584]{1,0:T(8,128)(2,1)}) custom-call(bf16[1024,512]{1,0:T(8,128)(2,1)} %coef_ref.1, bf16[1024,3584]{1,0:T(8,128)(2,1)} %right_hbm.2), custom_call_target="tpu_custom_call" | custom-call | flops 3758096384 | bytes 12058624 | tf_op jit(solution)/shard_map/product/pallas_call | solution.py:222
  15.8 3.8 %collective-permute-start.7 = (s32[4,48]{1,0:T(4,128)S(1)}, s32[4,48]{1,0:T(4,128)S(1)}, u32[]{:S(2)}, u32[]{:S(2)}) collective-permute-start(s32[4,48]{1,0:T(4,128)S(1)} %pad_add_fusion.refs_1_), channel_id=1, source_target_pairs={{0,12},{1,13},{2,14},{3,15},{4,8},{5,9},{6,10},{7,11},{8,4},{9,5},... | collective-permute-start | bytes 2312 | tf_op jit(solution)/shard_map/ppermute | solution.py:37
  21.3 1.7 %collective-permute-start.10 = (bf16[32,1792]{1,0:T(8,128)(2,1)S(1)}, bf16[32,1792]{1,0:T(8,128)(2,1)S(1)}, u32[]{:S(2)}, u32[]{:S(2)}) collective-permute-start(bf16[32,1792]{1,0:T(8,128)(2,1)S(1)} %get-tuple-element.148), channel_id=1, source_target_pairs={{0,2},{1,3},{4,0},{5,1},{8,4},{9,5},{12,8},{13,9},{14,12},{15,13},... | collective-permute-start | bytes 344072 | tf_op jit(solution)/shard_map/ppermute | solution.py:79
  24.8 12.2 %select_product.1 = (bf16[128,3584]{1,0:T(8,128)(2,1)}, bf16[128,3584]{1,0:T(8,128)(2,1)}, bf16[128,3584]{1,0:T(8,128)(2,1)}, bf16[128,3584]{1,0:T(8,128)(2,1)}, s32[32,1]{1,0:T(8,128)}) custom-call(bf16[1024,512]{1,0:T(8,128)(2,1)} %coef_ref.2, bf16[1024,3584]{1,0:T(8,128)(2,1)} %right_hbm.3, s32[2,16]{1,0:T(2,128)} %bitcast.8, s32[4,48]{1,0:T(4,128)} %copy-done.11, ...), custom_call_target="tpu_custom_call" | custom-call | flops 3758096384 | bytes 12058624 | tf_op jit(solution)/shard_map/select_product/pallas_call | solution.py:222
  37.8 1.5 %collective-permute-start.15 = (bf16[32,3584]{1,0:T(8,128)(2,1)S(1)}, bf16[32,3584]{1,0:T(8,128)(2,1)S(1)}, u32[]{:S(2)}, u32[]{:S(2)}) collective-permute-start(bf16[32,3584]{1,0:T(8,128)(2,1)S(1)} %get-tuple-element.144), channel_id=1, source_target_pairs={{0,2},{1,3},{4,0},{5,1},{8,4},{9,5},{12,8},{13,9},{14,12},{15,13},... | collective-permute-start | bytes 688136 | tf_op jit(solution)/shard_map/ppermute | solution.py:79
  42.1 1.5 %collective-permute-start.13 = (bf16[32,1792]{1,0:T(8,128)(2,1)S(1)}, bf16[32,1792]{1,0:T(8,128)(2,1)S(1)}, u32[]{:S(2)}, u32[]{:S(2)}) collective-permute-start(bf16[32,1792]{1,0:T(8,128)(2,1)S(1)} %get-tuple-element.146), channel_id=1, source_target_pairs={{0,2},{1,3},{4,0},{5,1},{8,4},{9,5},{12,8},{13,9},{14,12},{15,13},... | collective-permute-start | bytes 344072 | tf_op jit(solution)/shard_map/ppermute | solution.py:79
  44.2 1.7 %collective-permute-done.15 = bf16[32,3584]{1,0:T(8,128)(2,1)S(1)} collective-permute-done((bf16[32,3584]{1,0:T(8,128)(2,1)S(1)}, bf16[32,3584]{1,0:T(8,128)(2,1)S(1)}, u32[]{:S(2)}, u32[]{:S(2)}) %collective-permute-start.15) | collective-permute-done | bytes 229408 | tf_op jit(solution)/shard_map/ppermute | solution.py:79
  47.9 1.5 %collective-permute-start.19 = (bf16[32,3584]{1,0:T(8,128)(2,1)S(1)}, bf16[32,3584]{1,0:T(8,128)(2,1)S(1)}, u32[]{:S(2)}, u32[]{:S(2)}) collective-permute-start(bf16[32,3584]{1,0:T(8,128)(2,1)S(1)} %add_convert_fusion.8), channel_id=1, source_target_pairs={{0,2},{1,3},{4,0},{5,1},{8,4},{9,5},{12,8},{13,9},{14,12},{15,13},... | collective-permute-start | bytes 688136 | tf_op jit(solution)/shard_map/ppermute | solution.py:79
  50.5 1.3 %collective-permute-start.16 = (bf16[32,3584]{1,0:T(8,128)(2,1)S(1)}, bf16[32,3584]{1,0:T(8,128)(2,1)S(1)}, u32[]{:S(2)}, u32[]{:S(2)}) collective-permute-start(bf16[32,3584]{1,0:T(8,128)(2,1)S(1)} %get-tuple-element.143), channel_id=1, source_target_pairs={{0,4},{1,5},{4,8},{5,9},{8,12},{9,13},{12,14},{13,15},{14,10},{15,... | collective-permute-start | bytes 688136 | tf_op jit(solution)/shard_map/ppermute | solution.py:79
  51.8 3.9 %collective-permute-done.18 = bf16[32,3584]{1,0:T(8,128)(2,1)S(1)} collective-permute-done((bf16[32,3584]{1,0:T(8,128)(2,1)S(1)}, bf16[32,3584]{1,0:T(8,128)(2,1)S(1)}, u32[]{:S(2)}, u32[]{:S(2)}) %collective-permute-start.18) | collective-permute-done | bytes 229408 | tf_op jit(solution)/shard_map/ppermute | solution.py:79
  56.4 2.3 %collective-permute-done.17 = bf16[32,3584]{1,0:T(8,128)(2,1)S(1)} collective-permute-done((bf16[32,3584]{1,0:T(8,128)(2,1)S(1)}, bf16[32,3584]{1,0:T(8,128)(2,1)S(1)}, u32[]{:S(2)}, u32[]{:S(2)}) %collective-permute-start.17) | collective-permute-done | bytes 229408 | tf_op jit(solution)/shard_map/ppermute | solution.py:79
  59.9 1.3 %collective-permute-start.22 = (bf16[32,3584]{1,0:T(8,128)(2,1)S(1)}, bf16[32,3584]{1,0:T(8,128)(2,1)S(1)}, u32[]{:S(2)}, u32[]{:S(2)}) collective-permute-start(bf16[32,3584]{1,0:T(8,128)(2,1)S(1)} %add_convert_fusion.1), channel_id=1, source_target_pairs={{0,2},{1,3},{4,0},{5,1},{8,4},{9,5},{12,8},{13,9},{14,12},{15,13},... | collective-permute-start | bytes 688136 | tf_op jit(solution)/shard_map/ppermute | solution.py:79
  63.2 4.2 %collective-permute-done.20 = bf16[32,3584]{1,0:T(8,128)(2,1)S(1)} collective-permute-done((bf16[32,3584]{1,0:T(8,128)(2,1)S(1)}, bf16[32,3584]{1,0:T(8,128)(2,1)S(1)}, u32[]{:S(2)}, u32[]{:S(2)}) %collective-permute-start.20) | collective-permute-done | bytes 229408 | tf_op jit(solution)/shard_map/ppermute | solution.py:79
  68.7 1.3 %collective-permute-start.23 = (bf16[32,3584]{1,0:T(8,128)(2,1)S(1)}, bf16[32,3584]{1,0:T(8,128)(2,1)S(1)}, u32[]{:S(2)}, u32[]{:S(2)}) collective-permute-start(bf16[32,3584]{1,0:T(8,128)(2,1)S(1)} %get-tuple-element.138), channel_id=1, source_target_pairs={{0,2},{1,3},{4,0},{5,1},{8,4},{9,5},{12,8},{13,9},{14,12},{15,13},... | collective-permute-start | bytes 688136 | tf_op jit(solution)/shard_map/ppermute | solution.py:79
  70.7 2.3 %collective-permute-done.25.refs_3_ = bf16[32,3584]{1,0:T(8,128)(2,1)S(1)} collective-permute-done((bf16[32,3584]{1,0:T(8,128)(2,1)S(1)}, bf16[32,3584]{1,0:T(8,128)(2,1)S(1)}, u32[]{:S(2)}, u32[]{:S(2)}) %collective-permute-start.25) | collective-permute-done | bytes 229408 | tf_op jit(solution)/shard_map/ppermute | solution.py:79
  73.1 2.5 %collective-permute-done.23.refs_3_ = bf16[32,3584]{1,0:T(8,128)(2,1)S(1)} collective-permute-done((bf16[32,3584]{1,0:T(8,128)(2,1)S(1)}, bf16[32,3584]{1,0:T(8,128)(2,1)S(1)}, u32[]{:S(2)}, u32[]{:S(2)}) %collective-permute-start.23) | collective-permute-done | bytes 229408 | tf_op jit(solution)/shard_map/ppermute | solution.py:79
  76.0 1.8 %enc_update.1 = (f32[32,3584]{1,0:T(8,128)}, f32[32,3584]{1,0:T(8,128)}, f32[32,3584]{1,0:T(8,128)}, bf16[32,3584]{1,0:T(8,128)(2,1)S(1)}, bf16[32,3584]{1,0:T(8,128)(2,1)S(1)}) custom-call(s32[32,1]{1,0:T(8,128)S(1)} %copy-done.8, f32[32,3584]{1,0:T(8,128)S(1)} %copy-done.2, f32[32,3584]{1,0:T(8,128)S(1)} %copy-done.3, f32[32,3584]{1,0:T(8,128)S(1)} %copy-done.4, ...), custom_call_target="tpu_custom_call" | custom-call | flops 4587520 | bytes 4587520 | tf_op jit(solution)/shard_map/enc_update/pallas_call | solution.py:290
  77.8 1.8 %dec_update.1 = (f32[32,3584]{1,0:T(8,128)}, f32[32,3584]{1,0:T(8,128)}, f32[32,3584]{1,0:T(8,128)}, bf16[2,32,3584]{2,1,0:T(8,128)(2,1)S(1)}) custom-call(s32[32,1]{1,0:T(8,128)S(1)} %copy-done.8, f32[32,3584]{1,0:T(8,128)S(1)} %copy-done.5, f32[32,3584]{1,0:T(8,128)S(1)} %copy-done.6, f32[32,3584]{1,0:T(8,128)S(1)} %copy-done.7, ...), custom_call_target="tpu_custom_call" | custom-call | flops 4587520 | bytes 4587520 | tf_op jit(solution)/shard_map/dec_update/pallas_call | solution.py:290
  82.3 6.7 %collective-permute-done.27.refs_1_ = bf16[64,3584]{1,0:T(8,128)(2,1)S(1)} collective-permute-done((bf16[64,3584]{1,0:T(8,128)(2,1)S(1)}, bf16[64,3584]{1,0:T(8,128)(2,1)S(1)}, u32[]{:S(2)}, u32[]{:S(2)}) %collective-permute-start.27) | collective-permute-done | bytes 458784 | tf_op jit(solution)/shard_map/ppermute | solution.py:79
  89.0 1.7 %collective-permute-done.26.refs_0_ = bf16[64,3584]{1,0:T(8,128)(2,1)S(1)} collective-permute-done((bf16[64,3584]{1,0:T(8,128)(2,1)S(1)}, bf16[64,3584]{1,0:T(8,128)(2,1)S(1)}, u32[]{:S(2)}, u32[]{:S(2)}) %collective-permute-start.26) | collective-permute-done | bytes 458784 | tf_op jit(solution)/shard_map/ppermute | solution.py:79
  90.7 1.5 %collective-permute-start.28 = (bf16[64,3584]{1,0:T(8,128)(2,1)S(1)}, bf16[64,3584]{1,0:T(8,128)(2,1)S(1)}, u32[]{:S(2)}, u32[]{:S(2)}) collective-permute-start(bf16[64,3584]{1,0:T(8,128)(2,1)S(1)} %collective-permute-done.26.refs_0_), channel_id=1, source_target_pairs={{0,4},{1,5},{4,8},{5,9},{8,12},{9,13},{12,14},{13,15},{14,10},{15,... | collective-permute-start | bytes 1376264 | tf_op jit(solution)/shard_map/ppermute | solution.py:79
  94.4 6.8 %collective-permute-done.28.refs_0_ = bf16[64,3584]{1,0:T(8,128)(2,1)S(1)} collective-permute-done((bf16[64,3584]{1,0:T(8,128)(2,1)S(1)}, bf16[64,3584]{1,0:T(8,128)(2,1)S(1)}, u32[]{:S(2)}, u32[]{:S(2)}) %collective-permute-start.28) | collective-permute-done | bytes 458784 | tf_op jit(solution)/shard_map/ppermute | solution.py:79
  101.2 1.8 %collective-permute-done.29.refs_1_ = bf16[64,3584]{1,0:T(8,128)(2,1)S(1)} collective-permute-done((bf16[64,3584]{1,0:T(8,128)(2,1)S(1)}, bf16[64,3584]{1,0:T(8,128)(2,1)S(1)}, u32[]{:S(2)}, u32[]{:S(2)}) %collective-permute-start.29) | collective-permute-done | bytes 458784 | tf_op jit(solution)/shard_map/ppermute | solution.py:79
  103.6 1.5 %collective-permute-start.32 = (bf16[64,3584]{1,0:T(8,128)(2,1)S(1)}, bf16[64,3584]{1,0:T(8,128)(2,1)S(1)}, u32[]{:S(2)}, u32[]{:S(2)}) collective-permute-start(bf16[64,3584]{1,0:T(8,128)(2,1)S(1)} %collective-permute-done.29.refs_1_), channel_id=1, source_target_pairs={{0,2},{1,3},{4,0},{5,1},{8,4},{9,5},{12,8},{13,9},{14,12},{15,13},... | collective-permute-start | bytes 1376264 | tf_op jit(solution)/shard_map/ppermute | solution.py:79
  105.6 1.3 %place.8 = (bf16[512,3584]{1,0:T(8,128)(2,1)}, bf16[512,3584]{1,0:T(8,128)(2,1)}) custom-call(bf16[64,3584]{1,0:T(8,128)(2,1)S(1)} %collective-permute-done.28.refs_0_, bf16[64,3584]{1,0:T(8,128)(2,1)S(1)} %collective-permute-done.29.refs_1_, bf16[64,3584]{1,0:T(8,128)(2,1)S(1)} %collective-permute-done.33.refs_2_, ...), custom_call_target="tpu_custom_call", output_to_operand_aliasing={{0}: (4, {}), {1}: (5, {})} | custom-call | bytes 3670016 | tf_op jit(solution)/shard_map/place/pallas_call | solution.py:325
  106.9 6.1 %collective-permute-done.31.refs_0_ = bf16[64,3584]{1,0:T(8,128)(2,1)S(1)} collective-permute-done((bf16[64,3584]{1,0:T(8,128)(2,1)S(1)}, bf16[64,3584]{1,0:T(8,128)(2,1)S(1)}, u32[]{:S(2)}, u32[]{:S(2)}) %collective-permute-start.31) | collective-permute-done | bytes 458784 | tf_op jit(solution)/shard_map/ppermute | solution.py:79
  113.0 1.4 %collective-permute-done.32.refs_1_ = bf16[64,3584]{1,0:T(8,128)(2,1)S(1)} collective-permute-done((bf16[64,3584]{1,0:T(8,128)(2,1)S(1)}, bf16[64,3584]{1,0:T(8,128)(2,1)S(1)}, u32[]{:S(2)}, u32[]{:S(2)}) %collective-permute-start.32) | collective-permute-done | bytes 458784 | tf_op jit(solution)/shard_map/ppermute | solution.py:79
  114.4 1.7 %collective-permute-start.36 = (bf16[64,1792]{1,0:T(8,128)(2,1)S(1)}, bf16[64,1792]{1,0:T(8,128)(2,1)S(1)}, u32[]{:S(2)}, u32[]{:S(2)}) collective-permute-start(bf16[64,1792]{1,0:T(8,128)(2,1)S(1)} %slice.135), channel_id=1, source_target_pairs={{0,2},{1,3},{4,0},{5,1},{8,4},{9,5},{12,8},{13,9},{14,12},{15,13},... | collective-permute-start | bytes 688136 | tf_op jit(solution)/shard_map/ppermute | solution.py:79
  117.0 1.3 %place.9 = (bf16[512,3584]{1,0:T(8,128)(2,1)}, bf16[512,3584]{1,0:T(8,128)(2,1)}) custom-call(bf16[64,3584]{1,0:T(8,128)(2,1)S(1)} %collective-permute-done.31.refs_0_, bf16[64,3584]{1,0:T(8,128)(2,1)S(1)} %collective-permute-done.32.refs_1_, bf16[64,3584]{1,0:T(8,128)(2,1)S(1)} %collective-permute-done.37.refs_2_, ...), custom_call_target="tpu_custom_call", output_to_operand_aliasing={{0}: (4, {}), {1}: (5, {})} | custom-call | bytes 3670016 | tf_op jit(solution)/shard_map/place/pallas_call | solution.py:325
  118.3 2.2 %collective-permute-done.36.refs_1_ = bf16[64,1792]{1,0:T(8,128)(2,1)S(1)} collective-permute-done((bf16[64,1792]{1,0:T(8,128)(2,1)S(1)}, bf16[64,1792]{1,0:T(8,128)(2,1)S(1)}, u32[]{:S(2)}, u32[]{:S(2)}) %collective-permute-start.36) | collective-permute-done | bytes 229408 | tf_op jit(solution)/shard_map/ppermute | solution.py:79
  120.5 1.6 %collective-permute-done.35.refs_0_ = bf16[64,1792]{1,0:T(8,128)(2,1)S(1)} collective-permute-done((bf16[64,1792]{1,0:T(8,128)(2,1)S(1)}, bf16[64,1792]{1,0:T(8,128)(2,1)S(1)}, u32[]{:S(2)}, u32[]{:S(2)}) %collective-permute-start.35) | collective-permute-done | bytes 229408 | tf_op jit(solution)/shard_map/ppermute | solution.py:79
  (114 shorter events, 28.8 us)
Async XLA Ops:
  1.4 14.2 %collective-permute-start.2 = (s32[1,48]{1,0:T(1,128)S(1)}, s32[1,48]{1,0:T(1,128)S(1)}, u32[]{:S(2)}, u32[]{:S(2)}) collective-permute-start(s32[1,48]{1,0:T(1,128)S(1)} %pad_add_fusion.1), channel_id=1, source_target_pairs={{0,3},{1,2},{2,1},{3,0},{4,7},{5,6},{6,5},{7,4},{8,11},{9,10},{10,... | collective-permute-start | bytes 584 | tf_op jit(solution)/shard_map/ppermute | solution.py:37
  3.8 11.8 %collective-permute-start.1 = (s32[1,48]{1,0:T(1,128)S(1)}, s32[1,48]{1,0:T(1,128)S(1)}, u32[]{:S(2)}, u32[]{:S(2)}) collective-permute-start(s32[1,48]{1,0:T(1,128)S(1)} %pad_add_fusion.1), channel_id=1, source_target_pairs={{0,2},{1,3},{2,0},{3,1},{4,6},{5,7},{6,4},{7,5},{8,10},{9,11},{10,... | collective-permute-start | bytes 584 | tf_op jit(solution)/shard_map/ppermute | solution.py:37
  4.4 11.2 %collective-permute-start = (s32[1,48]{1,0:T(1,128)S(1)}, s32[1,48]{1,0:T(1,128)S(1)}, u32[]{:S(2)}, u32[]{:S(2)}) collective-permute-start(s32[1,48]{1,0:T(1,128)S(1)} %pad_add_fusion.1), channel_id=1, source_target_pairs={{0,1},{1,0},{2,3},{3,2},{4,5},{5,4},{6,7},{7,6},{8,9},{9,8},{10,11... | collective-permute-start | bytes 584 | tf_op jit(solution)/shard_map/ppermute | solution.py:37
  15.8 7.6 %collective-permute-start.7 = (s32[4,48]{1,0:T(4,128)S(1)}, s32[4,48]{1,0:T(4,128)S(1)}, u32[]{:S(2)}, u32[]{:S(2)}) collective-permute-start(s32[4,48]{1,0:T(4,128)S(1)} %pad_add_fusion.refs_1_), channel_id=1, source_target_pairs={{0,12},{1,13},{2,14},{3,15},{4,8},{5,9},{6,10},{7,11},{8,4},{9,5},... | collective-permute-start | bytes 2312 | tf_op jit(solution)/shard_map/ppermute | solution.py:37
  21.3 15.8 %collective-permute-start.10 = (bf16[32,1792]{1,0:T(8,128)(2,1)S(1)}, bf16[32,1792]{1,0:T(8,128)(2,1)S(1)}, u32[]{:S(2)}, u32[]{:S(2)}) collective-permute-start(bf16[32,1792]{1,0:T(8,128)(2,1)S(1)} %get-tuple-element.148), channel_id=1, source_target_pairs={{0,2},{1,3},{4,0},{5,1},{8,4},{9,5},{12,8},{13,9},{14,12},{15,13},... | collective-permute-start | bytes 344072 | tf_op jit(solution)/shard_map/ppermute | solution.py:79
  23.0 14.1 %collective-permute-start.9 = (bf16[32,1792]{1,0:T(8,128)(2,1)S(1)}, bf16[32,1792]{1,0:T(8,128)(2,1)S(1)}, u32[]{:S(2)}, u32[]{:S(2)}) collective-permute-start(bf16[32,1792]{1,0:T(8,128)(2,1)S(1)} %get-tuple-element.149), channel_id=1, source_target_pairs={{0,4},{1,5},{4,8},{5,9},{8,12},{9,13},{12,14},{13,15},{14,10},{15,... | collective-permute-start | bytes 344072 | tf_op jit(solution)/shard_map/ppermute | solution.py:79
  37.8 8.0 %collective-permute-start.15 = (bf16[32,3584]{1,0:T(8,128)(2,1)S(1)}, bf16[32,3584]{1,0:T(8,128)(2,1)S(1)}, u32[]{:S(2)}, u32[]{:S(2)}) collective-permute-start(bf16[32,3584]{1,0:T(8,128)(2,1)S(1)} %get-tuple-element.144), channel_id=1, source_target_pairs={{0,2},{1,3},{4,0},{5,1},{8,4},{9,5},{12,8},{13,9},{14,12},{15,13},... | collective-permute-start | bytes 688136 | tf_op jit(solution)/shard_map/ppermute | solution.py:79
  39.3 7.7 %collective-permute-start.14 = (bf16[32,3584]{1,0:T(8,128)(2,1)S(1)}, bf16[32,3584]{1,0:T(8,128)(2,1)S(1)}, u32[]{:S(2)}, u32[]{:S(2)}) collective-permute-start(bf16[32,3584]{1,0:T(8,128)(2,1)S(1)} %get-tuple-element.145), channel_id=1, source_target_pairs={{0,4},{1,5},{4,8},{5,9},{8,12},{9,13},{12,14},{13,15},{14,10},{15,... | collective-permute-start | bytes 688136 | tf_op jit(solution)/shard_map/ppermute | solution.py:79
  42.1 7.3 %collective-permute-start.13 = (bf16[32,1792]{1,0:T(8,128)(2,1)S(1)}, bf16[32,1792]{1,0:T(8,128)(2,1)S(1)}, u32[]{:S(2)}, u32[]{:S(2)}) collective-permute-start(bf16[32,1792]{1,0:T(8,128)(2,1)S(1)} %get-tuple-element.146), channel_id=1, source_target_pairs={{0,2},{1,3},{4,0},{5,1},{8,4},{9,5},{12,8},{13,9},{14,12},{15,13},... | collective-permute-start | bytes 344072 | tf_op jit(solution)/shard_map/ppermute | solution.py:79
  47.1 8.6 %collective-permute-start.18 = (bf16[32,3584]{1,0:T(8,128)(2,1)S(1)}, bf16[32,3584]{1,0:T(8,128)(2,1)S(1)}, u32[]{:S(2)}, u32[]{:S(2)}) collective-permute-start(bf16[32,3584]{1,0:T(8,128)(2,1)S(1)} %add_convert_fusion.9), channel_id=1, source_target_pairs={{0,4},{1,5},{4,8},{5,9},{8,12},{9,13},{12,14},{13,15},{14,10},{15,... | collective-permute-start | bytes 688136 | tf_op jit(solution)/shard_map/ppermute | solution.py:79
  47.9 8.3 %collective-permute-start.19 = (bf16[32,3584]{1,0:T(8,128)(2,1)S(1)}, bf16[32,3584]{1,0:T(8,128)(2,1)S(1)}, u32[]{:S(2)}, u32[]{:S(2)}) collective-permute-start(bf16[32,3584]{1,0:T(8,128)(2,1)S(1)} %add_convert_fusion.8), channel_id=1, source_target_pairs={{0,2},{1,3},{4,0},{5,1},{8,4},{9,5},{12,8},{13,9},{14,12},{15,13},... | collective-permute-start | bytes 688136 | tf_op jit(solution)/shard_map/ppermute | solution.py:79
  49.8 8.9 %collective-permute-start.17 = (bf16[32,3584]{1,0:T(8,128)(2,1)S(1)}, bf16[32,3584]{1,0:T(8,128)(2,1)S(1)}, u32[]{:S(2)}, u32[]{:S(2)}) collective-permute-start(bf16[32,3584]{1,0:T(8,128)(2,1)S(1)} %get-tuple-element.142), channel_id=1, source_target_pairs={{0,2},{1,3},{4,0},{5,1},{8,4},{9,5},{12,8},{13,9},{14,12},{15,13},... | collective-permute-start | bytes 688136 | tf_op jit(solution)/shard_map/ppermute | solution.py:79
  50.5 8.3 %collective-permute-start.16 = (bf16[32,3584]{1,0:T(8,128)(2,1)S(1)}, bf16[32,3584]{1,0:T(8,128)(2,1)S(1)}, u32[]{:S(2)}, u32[]{:S(2)}) collective-permute-start(bf16[32,3584]{1,0:T(8,128)(2,1)S(1)} %get-tuple-element.143), channel_id=1, source_target_pairs={{0,4},{1,5},{4,8},{5,9},{8,12},{9,13},{12,14},{13,15},{14,10},{15,... | collective-permute-start | bytes 688136 | tf_op jit(solution)/shard_map/ppermute | solution.py:79
  59.0 8.4 %collective-permute-start.20 = (bf16[32,3584]{1,0:T(8,128)(2,1)S(1)}, bf16[32,3584]{1,0:T(8,128)(2,1)S(1)}, u32[]{:S(2)}, u32[]{:S(2)}) collective-permute-start(bf16[32,3584]{1,0:T(8,128)(2,1)S(1)} %add_convert_fusion.3), channel_id=1, source_target_pairs={{0,4},{1,5},{4,8},{5,9},{8,12},{9,13},{12,14},{13,15},{14,10},{15,... | collective-permute-start | bytes 688136 | tf_op jit(solution)/shard_map/ppermute | solution.py:79
  59.9 8.6 %collective-permute-start.22 = (bf16[32,3584]{1,0:T(8,128)(2,1)S(1)}, bf16[32,3584]{1,0:T(8,128)(2,1)S(1)}, u32[]{:S(2)}, u32[]{:S(2)}) collective-permute-start(bf16[32,3584]{1,0:T(8,128)(2,1)S(1)} %add_convert_fusion.1), channel_id=1, source_target_pairs={{0,2},{1,3},{4,0},{5,1},{8,4},{9,5},{12,8},{13,9},{14,12},{15,13},... | collective-permute-start | bytes 688136 | tf_op jit(solution)/shard_map/ppermute | solution.py:79
  61.2 11.9 %collective-permute-start.25 = (bf16[32,3584]{1,0:T(8,128)(2,1)S(1)}, bf16[32,3584]{1,0:T(8,128)(2,1)S(1)}, u32[]{:S(2)}, u32[]{:S(2)}) collective-permute-start(bf16[32,3584]{1,0:T(8,128)(2,1)S(1)} %get-tuple-element.140), channel_id=1, source_target_pairs={{0,2},{1,3},{4,0},{5,1},{8,4},{9,5},{12,8},{13,9},{14,12},{15,13},... | collective-permute-start | bytes 688136 | tf_op jit(solution)/shard_map/ppermute | solution.py:79
  62.3 10.8 %collective-permute-start.24 = (bf16[32,3584]{1,0:T(8,128)(2,1)S(1)}, bf16[32,3584]{1,0:T(8,128)(2,1)S(1)}, u32[]{:S(2)}, u32[]{:S(2)}) collective-permute-start(bf16[32,3584]{1,0:T(8,128)(2,1)S(1)} %get-tuple-element.141), channel_id=1, source_target_pairs={{0,4},{1,5},{4,8},{5,9},{8,12},{9,13},{12,14},{13,15},{14,10},{15,... | collective-permute-start | bytes 688136 | tf_op jit(solution)/shard_map/ppermute | solution.py:79
  68.7 6.9 %collective-permute-start.23 = (bf16[32,3584]{1,0:T(8,128)(2,1)S(1)}, bf16[32,3584]{1,0:T(8,128)(2,1)S(1)}, u32[]{:S(2)}, u32[]{:S(2)}) collective-permute-start(bf16[32,3584]{1,0:T(8,128)(2,1)S(1)} %get-tuple-element.138), channel_id=1, source_target_pairs={{0,2},{1,3},{4,0},{5,1},{8,4},{9,5},{12,8},{13,9},{14,12},{15,13},... | collective-permute-start | bytes 688136 | tf_op jit(solution)/shard_map/ppermute | solution.py:79
  79.5 9.5 %collective-permute-start.27 = (bf16[64,3584]{1,0:T(8,128)(2,1)S(1)}, bf16[64,3584]{1,0:T(8,128)(2,1)S(1)}, u32[]{:S(2)}, u32[]{:S(2)}) collective-permute-start(bf16[64,3584]{1,0:T(8,128)(2,1)S(1)} %bitcast.4), channel_id=1, source_target_pairs={{0,2},{1,3},{4,0},{5,1},{8,4},{9,5},{12,8},{13,9},{14,12},{15,13},... | collective-permute-start | bytes 1376264 | tf_op jit(solution)/shard_map/ppermute | solution.py:79
  80.6 10.1 %collective-permute-start.26 = (bf16[64,3584]{1,0:T(8,128)(2,1)S(1)}, bf16[64,3584]{1,0:T(8,128)(2,1)S(1)}, u32[]{:S(2)}, u32[]{:S(2)}) collective-permute-start(bf16[64,3584]{1,0:T(8,128)(2,1)S(1)} %bitcast.5), channel_id=1, source_target_pairs={{0,4},{1,5},{4,8},{5,9},{8,12},{9,13},{12,14},{13,15},{14,10},{15,... | collective-permute-start | bytes 1376264 | tf_op jit(solution)/shard_map/ppermute | solution.py:79
  81.5 11.7 %collective-permute-start.30 = (bf16[64,3584]{1,0:T(8,128)(2,1)S(1)}, bf16[64,3584]{1,0:T(8,128)(2,1)S(1)}, u32[]{:S(2)}, u32[]{:S(2)}) collective-permute-start(bf16[64,3584]{1,0:T(8,128)(2,1)S(1)} %bitcast.6), channel_id=1, source_target_pairs={{0,1},{1,0},{2,3},{3,2},{4,5},{5,4},{6,7},{7,6},{8,9},{9,8},{10,11... | collective-permute-start | bytes 1376264 | tf_op jit(solution)/shard_map/ppermute | solution.py:37
  90.7 10.5 %collective-permute-start.28 = (bf16[64,3584]{1,0:T(8,128)(2,1)S(1)}, bf16[64,3584]{1,0:T(8,128)(2,1)S(1)}, u32[]{:S(2)}, u32[]{:S(2)}) collective-permute-start(bf16[64,3584]{1,0:T(8,128)(2,1)S(1)} %collective-permute-done.26.refs_0_), channel_id=1, source_target_pairs={{0,4},{1,5},{4,8},{5,9},{8,12},{9,13},{12,14},{13,15},{14,10},{15,... | collective-permute-start | bytes 1376264 | tf_op jit(solution)/shard_map/ppermute | solution.py:79
  92.2 10.8 %collective-permute-start.29 = (bf16[64,3584]{1,0:T(8,128)(2,1)S(1)}, bf16[64,3584]{1,0:T(8,128)(2,1)S(1)}, u32[]{:S(2)}, u32[]{:S(2)}) collective-permute-start(bf16[64,3584]{1,0:T(8,128)(2,1)S(1)} %collective-permute-done.27.refs_1_), channel_id=1, source_target_pairs={{0,2},{1,3},{4,0},{5,1},{8,4},{9,5},{12,8},{13,9},{14,12},{15,13},... | collective-permute-start | bytes 1376264 | tf_op jit(solution)/shard_map/ppermute | solution.py:79
  92.8 12.3 %collective-permute-start.33 = (bf16[64,3584]{1,0:T(8,128)(2,1)S(1)}, bf16[64,3584]{1,0:T(8,128)(2,1)S(1)}, u32[]{:S(2)}, u32[]{:S(2)}) collective-permute-start(bf16[64,3584]{1,0:T(8,128)(2,1)S(1)} %collective-permute-done.26.refs_0_), channel_id=1, source_target_pairs={{0,1},{1,0},{2,3},{3,2},{4,5},{5,4},{6,7},{7,6},{8,9},{9,8},{10,11... | collective-permute-start | bytes 1376264 | tf_op jit(solution)/shard_map/ppermute | solution.py:37
  92.8 12.8 %collective-permute-start.34 = (bf16[64,3584]{1,0:T(8,128)(2,1)S(1)}, bf16[64,3584]{1,0:T(8,128)(2,1)S(1)}, u32[]{:S(2)}, u32[]{:S(2)}) collective-permute-start(bf16[64,3584]{1,0:T(8,128)(2,1)S(1)} %collective-permute-done.27.refs_1_), channel_id=1, source_target_pairs={{0,1},{1,0},{2,3},{3,2},{4,5},{5,4},{6,7},{7,6},{8,9},{9,8},{10,11... | collective-permute-start | bytes 1376264 | tf_op jit(solution)/shard_map/ppermute | solution.py:37
  103.1 9.9 %collective-permute-start.31 = (bf16[64,3584]{1,0:T(8,128)(2,1)S(1)}, bf16[64,3584]{1,0:T(8,128)(2,1)S(1)}, u32[]{:S(2)}, u32[]{:S(2)}) collective-permute-start(bf16[64,3584]{1,0:T(8,128)(2,1)S(1)} %collective-permute-done.28.refs_0_), channel_id=1, source_target_pairs={{0,4},{1,5},{4,8},{5,9},{8,12},{9,13},{12,14},{13,15},{14,10},{15,... | collective-permute-start | bytes 1376264 | tf_op jit(solution)/shard_map/ppermute | solution.py:79
  103.6 10.8 %collective-permute-start.32 = (bf16[64,3584]{1,0:T(8,128)(2,1)S(1)}, bf16[64,3584]{1,0:T(8,128)(2,1)S(1)}, u32[]{:S(2)}, u32[]{:S(2)}) collective-permute-start(bf16[64,3584]{1,0:T(8,128)(2,1)S(1)} %collective-permute-done.29.refs_1_), channel_id=1, source_target_pairs={{0,2},{1,3},{4,0},{5,1},{8,4},{9,5},{12,8},{13,9},{14,12},{15,13},... | collective-permute-start | bytes 1376264 | tf_op jit(solution)/shard_map/ppermute | solution.py:79
  105.1 11.4 %collective-permute-start.37 = (bf16[64,3584]{1,0:T(8,128)(2,1)S(1)}, bf16[64,3584]{1,0:T(8,128)(2,1)S(1)}, u32[]{:S(2)}, u32[]{:S(2)}) collective-permute-start(bf16[64,3584]{1,0:T(8,128)(2,1)S(1)} %collective-permute-done.28.refs_0_), channel_id=1, source_target_pairs={{0,1},{1,0},{2,3},{3,2},{4,5},{5,4},{6,7},{7,6},{8,9},{9,8},{10,11... | collective-permute-start | bytes 1376264 | tf_op jit(solution)/shard_map/ppermute | solution.py:37
  105.1 11.9 %collective-permute-start.38 = (bf16[64,3584]{1,0:T(8,128)(2,1)S(1)}, bf16[64,3584]{1,0:T(8,128)(2,1)S(1)}, u32[]{:S(2)}, u32[]{:S(2)}) collective-permute-start(bf16[64,3584]{1,0:T(8,128)(2,1)S(1)} %collective-permute-done.29.refs_1_), channel_id=1, source_target_pairs={{0,1},{1,0},{2,3},{3,2},{4,5},{5,4},{6,7},{7,6},{8,9},{9,8},{10,11... | collective-permute-start | bytes 1376264 | tf_op jit(solution)/shard_map/ppermute | solution.py:37
  114.4 6.1 %collective-permute-start.36 = (bf16[64,1792]{1,0:T(8,128)(2,1)S(1)}, bf16[64,1792]{1,0:T(8,128)(2,1)S(1)}, u32[]{:S(2)}, u32[]{:S(2)}) collective-permute-start(bf16[64,1792]{1,0:T(8,128)(2,1)S(1)} %slice.135), channel_id=1, source_target_pairs={{0,2},{1,3},{4,0},{5,1},{8,4},{9,5},{12,8},{13,9},{14,12},{15,13},... | collective-permute-start | bytes 688136 | tf_op jit(solution)/shard_map/ppermute | solution.py:79
  116.5 6.1 %collective-permute-start.41 = (bf16[64,3584]{1,0:T(8,128)(2,1)S(1)}, bf16[64,3584]{1,0:T(8,128)(2,1)S(1)}, u32[]{:S(2)}, u32[]{:S(2)}) collective-permute-start(bf16[64,3584]{1,0:T(8,128)(2,1)S(1)} %collective-permute-done.31.refs_0_), channel_id=1, source_target_pairs={{0,1},{1,0},{2,3},{3,2},{4,5},{5,4},{6,7},{7,6},{8,9},{9,8},{10,11... | collective-permute-start | bytes 1376264 | tf_op jit(solution)/shard_map/ppermute | solution.py:37
  116.5 6.1 %collective-permute-start.42 = (bf16[64,3584]{1,0:T(8,128)(2,1)S(1)}, bf16[64,3584]{1,0:T(8,128)(2,1)S(1)}, u32[]{:S(2)}, u32[]{:S(2)}) collective-permute-start(bf16[64,3584]{1,0:T(8,128)(2,1)S(1)} %collective-permute-done.32.refs_1_), channel_id=1, source_target_pairs={{0,1},{1,0},{2,3},{3,2},{4,5},{5,4},{6,7},{7,6},{8,9},{9,8},{10,11... | collective-permute-start | bytes 1376264 | tf_op jit(solution)/shard_map/ppermute | solution.py:37
  (28 other events, 325.0 us)

commit v8 on v5

--- a/solution.py
+++ b/solution.py
@@ -39,6 +39,10 @@
 
 def after(value, *others):
     return lax.optimization_barrier((value,) + others)[0]
+
+
+def tied(*values):
+    return lax.optimization_barrier(values)
 
 
 def params(mebibytes):
@@ -137,15 +141,67 @@
         ref[...] = out[i * part : (i + 1) * part].astype(ref.dtype)
 
 
-def product_kernel(size, rows, coef_ref, right_ref, *refs):
-    outs, (by_latent, by_slot) = refs[:4], refs[4:]
-
-    @pl.when(pl.program_id(0) == 0)
-    def _():
-        by_latent[...] = coef_ref[...].T
-        ordered_rows(size, rows, by_latent, by_slot)
-
-    multiply(by_slot, right_ref, outs)
+def stream_kernel(size, rows, coef_ref, right_hbm, *refs):
+    outs, (right, by_latent, by_slot, stage, sems_in, sems_out) = refs[:4], refs[4:]
+    tokens, width = right.shape
+    part = outs[0].shape[0]
+    pieces, cuts = sems_in.shape
+    tile, height = width // pieces, tokens // cuts
+    reads, writes = [], []
+    for i in range(pieces):
+        columns = pl.ds(i * tile, tile)
+        reads.append([])
+        for cut in range(cuts):
+            span = pl.ds(cut * height, height)
+            reads[i].append(
+                pltpu.make_async_copy(
+                    right_hbm.at[span, columns], right.at[span, columns], sems_in.at[i, cut]
+                )
+            )
+        for group, out in enumerate(outs):
+            source = stage.at[pl.ds(group * part, part), columns]
+            writes.append(pltpu.make_async_copy(source, out.at[:, columns], sems_out.at[i, group]))
+    for read in sum(reads, []):
+        read.start()
+    by_latent[...] = coef_ref[...].T
+    ordered_rows(size, rows, by_latent, by_slot)
+    for i in range(pieces):
+        for read in reads[i]:
+            read.wait()
+        columns = slice(i * tile, (i + 1) * tile)
+        out = jnp.dot(by_slot[...], right[:, columns], preferred_element_type=jnp.float32)
+        stage[:, columns] = out.astype(stage.dtype)
+        for write in writes[4 * i : 4 * i + 4]:
+            write.start()
+    for write in writes:
+        write.wait()
+
+
+def stream_product(coef, right, size, rows):
+    tokens, latents = coef.shape
+    width = right.shape[1]
+    part = latents // 4
+    pieces, cuts = 4, 4
+    anywhere = pl.BlockSpec(memory_space=pl.ANY)
+    return pl.pallas_call(
+        functools.partial(stream_kernel, size, rows),
+        in_specs=[pl.BlockSpec(memory_space=pltpu.VMEM), anywhere],
+        out_specs=[anywhere] * 4,
+        out_shape=[jax.ShapeDtypeStruct((part, width), coef.dtype)] * 4,
+        scratch_shapes=[
+            pltpu.VMEM((tokens, width), coef.dtype),
+            pltpu.VMEM((latents, tokens), coef.dtype),
+            pltpu.VMEM((latents, tokens), coef.dtype),
+            pltpu.VMEM((latents, width), coef.dtype),
+            pltpu.SemaphoreType.DMA((pieces, cuts)),
+            pltpu.SemaphoreType.DMA((pieces, 4)),
+        ],
+        compiler_params=params(56),
+        cost_estimate=cost(
+            2 * latents * tokens * width, 2 * (tokens * width + latents * (tokens + width))
+        ),
+        name="product",
+    )(coef, right)
 
 
 def select_kernel(size, rows, count, coef_ref, right_ref, picks_ref, *refs):
@@ -169,40 +225,34 @@
     multiply(by_slot, right_ref, outs)
 
 
-def product(coef, right, size, rows, vmem, picks=None, table=()):
+def select_product(coef, right, size, rows, picks, table):
     tokens, latents = coef.shape
     width = right.shape[1]
     tile = 512
     part = latents // 4
     fixed = lambda j: (0, 0)
-    in_specs = [pl.BlockSpec((tokens, latents), fixed), pl.BlockSpec((tokens, tile), lambda j: (0, j))]
-    out_specs = [pl.BlockSpec((part, tile), lambda j: (0, j))] * 4
-    out_shape = [jax.ShapeDtypeStruct((part, width), coef.dtype)] * 4
-    scratch = [pltpu.VMEM((latents, tokens), coef.dtype)] * 2
-    kernel = functools.partial(product_kernel, size, rows)
-    operands = [coef, right]
-    if picks is not None:
-        kernel = functools.partial(select_kernel, size, rows, len(table))
-        operands += [picks] + list(table)
-        in_specs += [pl.BlockSpec(value.shape, fixed) for value in operands[2:]]
-        out_specs.append(pl.BlockSpec((rows, 1), fixed))
-        out_shape.append(jax.ShapeDtypeStruct((rows, 1), jnp.int32))
-        scratch += [
+    operands = [coef, right, picks] + list(table)
+    in_specs = [pl.BlockSpec(value.shape, fixed) for value in operands]
+    in_specs[1] = pl.BlockSpec((tokens, tile), lambda j: (0, j))
+    return pl.pallas_call(
+        functools.partial(select_kernel, size, rows, len(table)),
+        grid=(width // tile,),
+        in_specs=in_specs,
+        out_specs=[pl.BlockSpec((part, tile), lambda j: (0, j))] * 4
+        + [pl.BlockSpec((rows, 1), fixed)],
+        out_shape=[jax.ShapeDtypeStruct((part, width), coef.dtype)] * 4
+        + [jax.ShapeDtypeStruct((rows, 1), jnp.int32)],
+        scratch_shapes=[
+            pltpu.VMEM((latents, tokens), coef.dtype),
+            pltpu.VMEM((latents, tokens), coef.dtype),
             pltpu.VMEM((size, table[0].shape[1]), jnp.int32),
             pltpu.VMEM((latents, 1), jnp.int32),
-        ]
-    return pl.pallas_call(
-        kernel,
-        grid=(width // tile,),
-        in_specs=in_specs,
-        out_specs=out_specs,
-        out_shape=out_shape,
-        scratch_shapes=scratch,
-        compiler_params=params(vmem),
+        ],
+        compiler_params=params(24),
         cost_estimate=cost(
             2 * latents * tokens * width, 2 * (tokens * width + latents * (tokens + width))
         ),
-        name="product" if picks is None else "select_product",
+        name="select_product",
     )(*operands)
 
 
@@ -350,10 +400,6 @@
     chips = size // 2
     stages = gather_table(jnp.concatenate([send_count, dead_order], axis=1), size)
     table = stages[-1]
-    dec = product(latent_act, out_grad, size, rows, 56)
-    dec_far = after(dec[0], *stages[0])
-    dec_kept, dec_core = [dec[1], dec[3]], [swap(dec_far, 1, size), swap(dec[2], 1, size)]
-
     def begin(kept, from_core):
         far = term(kept, from_core, 0, rows).astype(jnp.bfloat16)
         return [far[:, :half], far[:, half:]]
@@ -372,17 +418,28 @@
             moving.append(value.astype(jnp.bfloat16))
         return moving
 
-    dec_moving = begin(dec_kept, dec_core)
-    *enc, code = product(
-        after(enc_coef, *dec_moving), x_rows, size, rows, 24, pick_rows[0].T, table
+    dec = stream_product(latent_act, out_grad, size, rows)
+    dec_far = after(dec[0], *stages[0])
+    dec_kept, dec_core = [dec[1], dec[3]], [swap(dec_far, 1, size), swap(after(dec[2], table[0]), 1, size)]
+    dec_moving = begin(dec_kept, after(dec_core, table[0]))
+    *enc, code = select_product(
+        after(enc_coef, *dec_moving), x_rows, size, rows, pick_rows[0].T, table
     )
+    dec_came, enc_far = tied(travel(dec_moving), enc[0])
+    enc_kept, enc_core = [enc[1], enc[3]], [swap(enc_far, 1, size), swap(enc[2], 1, size)]
+    dec_moving = advance(dec_came, dec_kept, dec_core, 1)
     dec_came = travel(dec_moving)
-    enc_far, enc_near = after((enc[0], enc[2]), *dec_came)
-    enc_kept, enc_core = [enc[1], enc[3]], [swap(enc_far, 1, size), swap(enc_near, 1, size)]
-    enc_came = travel(begin(enc_kept, enc_core))
+    enc_moving = begin(enc_kept, after(enc_core, *dec_moving))
+    enc_came = travel(enc_moving)
+    dec_came = after(dec_came, *enc_moving)
     for hop in range(1, chips // 2):
-        dec_came = travel(advance(dec_came, dec_kept, dec_core, hop))
-        enc_came = travel(advance(enc_came, enc_kept, enc_core, hop))
+        if hop + 1 < chips // 2:
+            dec_moving = advance(dec_came, dec_kept, dec_core, hop + 1)
+            dec_came = travel(dec_moving)
+            enc_came = after(enc_came, *dec_moving)
+        enc_moving = advance(enc_came, enc_kept, enc_core, hop)
+        enc_came = travel(enc_moving)
+        dec_came = after(dec_came, *enc_moving)
     enc_out, enc_mo, enc_vo, enc_block, fresh = update(
         enc_kernel,
         code,

time: 124 us -> 119 us (0.960)
  waiting for transfers between devices: 57.8 us -> 52.4 us
    ppermute x24, waiting for transfers between devices: 54.4 us -> 50.3 us  [shift(): return lax.ppermute(value, 'latent', pairs)]
    ppermute x19, waiting for transfers between devices: 3.34 us -> 2.1 us  [swap(): return lax.ppermute(value, 'latent', [(i, i ^ bits) for i in range(size)])]
  transfers between devices with their start and end apart: 43 -> 43, of which waited for: 21 -> 21; matrix products, arithmetic and copies ran while one was open for 2% -> 2% of each run, Pallas kernels for 19% -> 18%
where the time goes in v8:
time: 119 us
  waiting for transfers between devices  52.4 us (44%)
  starting transfers between devices  35.5 us (30%)
  Pallas kernels  25.8 us (22%)
  other arithmetic  2.98 us (3%)
  local copies, waits for them, and re-layouts  1.35 us (1%)
    ppermute x24, waiting for transfers between devices, shift(): return lax.ppermute(value, 'latent', pairs)  50.3 us
    ppermute x24, starting transfers between devices, shift(): return lax.ppermute(value, 'latent', pairs)  24.8 us
    ppermute x19, starting transfers between devices, swap(): return lax.ppermute(value, 'latent', [(i, i ^ bits) for i in range(size)])  10.7 us
    pallas_call x1, Pallas kernels, stream_product(): pl.pallas_call(functools.partial(stream_kernel, size, rows), in_specs=[pl...  8.92 us
    pallas_call x1, Pallas kernels, select_product(): pl.pallas_call(functools.partial(select_kernel, size, rows, len(table)),...  6.98 us
    pallas_call x6, Pallas kernels, place(): pl.pallas_call(functools.partial(place_kernel, plan, size, rows, count),...  6.39 us
    pallas_call x2, Pallas kernels, update(): pl.pallas_call(kernel, grid=(rows // tile,), in_specs=[last_rows(value) f...  3.53 us
  transfers between devices with their start and end apart: 43, of which 21 were waited for; matrix products, arithmetic and copies ran while one was open for 2% of the time, Pallas kernels for 18%

profile of v8, /device:TPU:0, one launch (start us, length us, event | category | flops | bytes accessed | tf_op | source)
XLA Modules:
  0.0 119.0 jit_solution(3539445207812647074)
XLA Ops:
  1.6 2.5 %collective-permute-start.2 = (s32[1,48]{1,0:T(1,128)S(1)}, s32[1,48]{1,0:T(1,128)S(1)}, u32[]{:S(2)}, u32[]{:S(2)}) collective-permute-start(s32[1,48]{1,0:T(1,128)S(1)} %pad_add_fusion.1), channel_id=1, source_target_pairs={{0,3},{1,2},{2,1},{3,0},{4,7},{5,6},{6,5},{7,4},{8,11},{9,10},{10,... | collective-permute-start | bytes 584 | tf_op jit(solution)/shard_map/ppermute | solution.py:37
  4.7 8.9 %product.1 = (bf16[128,3584]{1,0:T(8,128)(2,1)}, bf16[128,3584]{1,0:T(8,128)(2,1)}, bf16[128,3584]{1,0:T(8,128)(2,1)}, bf16[128,3584]{1,0:T(8,128)(2,1)}) custom-call(bf16[1024,512]{1,0:T(8,128)(2,1)} %coef_ref.1, bf16[1024,3584]{1,0:T(8,128)(2,1)} %right_hbm.1), custom_call_target="tpu_custom_call" | custom-call | flops 3758096384 | bytes 12058624 | tf_op jit(solution)/shard_map/product/pallas_call | solution.py:186
  14.3 3.8 %collective-permute-start.7 = (s32[4,48]{1,0:T(4,128)S(1)}, s32[4,48]{1,0:T(4,128)S(1)}, u32[]{:S(2)}, u32[]{:S(2)}) collective-permute-start(s32[4,48]{1,0:T(4,128)S(1)} %pad_add_fusion.refs_0_), channel_id=1, source_target_pairs={{0,12},{1,13},{2,14},{3,15},{4,8},{5,9},{6,10},{7,11},{8,4},{9,5},... | collective-permute-start | bytes 2312 | tf_op jit(solution)/shard_map/ppermute | solution.py:37
  19.7 1.8 %collective-permute-start.10 = (bf16[32,1792]{1,0:T(8,128)(2,1)S(1)}, bf16[32,1792]{1,0:T(8,128)(2,1)S(1)}, u32[]{:S(2)}, u32[]{:S(2)}) collective-permute-start(bf16[32,1792]{1,0:T(8,128)(2,1)S(1)} %get-tuple-element.150), channel_id=1, source_target_pairs={{0,2},{1,3},{4,0},{5,1},{8,4},{9,5},{12,8},{13,9},{14,12},{15,13},... | collective-permute-start | bytes 344072 | tf_op jit(solution)/shard_map/ppermute | solution.py:79
  22.7 1.2 %copy-done.7 = bf16[1024,512]{1,0:T(8,128)(2,1)S(1)} copy-done((bf16[1024,512]{1,0:T(8,128)(2,1)S(1)}, bf16[1024,512]{1,0:T(8,128)(2,1)}, u32[]{:S(2)}) %copy-start.7) | copy-done | bytes 1048600
  23.9 7.0 %select_product.1 = (bf16[128,3584]{1,0:T(8,128)(2,1)S(1)}, bf16[128,3584]{1,0:T(8,128)(2,1)S(1)}, bf16[128,3584]{1,0:T(8,128)(2,1)S(1)}, bf16[128,3584]{1,0:T(8,128)(2,1)S(1)}, s32[32,1]{1,0:T(8,128)S(1)}) custom-call(bf16[1024,512]{1,0:T(8,128)(2,1)S(1)} %copy-done.7, bf16[1024,3584]{1,0:T(8,128)(2,1)S(1)} %bitcast.9, s32[2,16]{1,0:T(2,128)S(1)} %bitcast.10, ...), custom_call_target="tpu_custom_call" | custom-call | flops 3758096384 | bytes 12058624 | tf_op jit(solution)/shard_map/select_product/pallas_call | solution.py:237
  31.7 1.5 %collective-permute-start.15 = (bf16[32,3584]{1,0:T(8,128)(2,1)S(1)}, bf16[32,3584]{1,0:T(8,128)(2,1)S(1)}, u32[]{:S(2)}, u32[]{:S(2)}) collective-permute-start(bf16[32,3584]{1,0:T(8,128)(2,1)S(1)} %get-tuple-element.146), channel_id=1, source_target_pairs={{0,2},{1,3},{4,0},{5,1},{8,4},{9,5},{12,8},{13,9},{14,12},{15,13},... | collective-permute-start | bytes 688136 | tf_op jit(solution)/shard_map/ppermute | solution.py:79
  34.9 1.5 %collective-permute-start.13 = (bf16[32,1792]{1,0:T(8,128)(2,1)S(1)}, bf16[32,1792]{1,0:T(8,128)(2,1)S(1)}, u32[]{:S(2)}, u32[]{:S(2)}) collective-permute-start(bf16[32,1792]{1,0:T(8,128)(2,1)S(1)} %get-tuple-element.148), channel_id=1, source_target_pairs={{0,2},{1,3},{4,0},{5,1},{8,4},{9,5},{12,8},{13,9},{14,12},{15,13},... | collective-permute-start | bytes 344072 | tf_op jit(solution)/shard_map/ppermute | solution.py:79
  36.9 3.2 %collective-permute-done.15 = bf16[32,3584]{1,0:T(8,128)(2,1)S(1)} collective-permute-done((bf16[32,3584]{1,0:T(8,128)(2,1)S(1)}, bf16[32,3584]{1,0:T(8,128)(2,1)S(1)}, u32[]{:S(2)}, u32[]{:S(2)}) %collective-permute-start.15) | collective-permute-done | bytes 229408 | tf_op jit(solution)/shard_map/ppermute | solution.py:79
  40.2 1.5 %collective-permute-done.14 = bf16[32,3584]{1,0:T(8,128)(2,1)S(1)} collective-permute-done((bf16[32,3584]{1,0:T(8,128)(2,1)S(1)}, bf16[32,3584]{1,0:T(8,128)(2,1)S(1)}, u32[]{:S(2)}, u32[]{:S(2)}) %collective-permute-start.14) | collective-permute-done | bytes 229408 | tf_op jit(solution)/shard_map/ppermute | solution.py:79
  42.5 1.5 %collective-permute-start.19 = (bf16[32,3584]{1,0:T(8,128)(2,1)S(1)}, bf16[32,3584]{1,0:T(8,128)(2,1)S(1)}, u32[]{:S(2)}, u32[]{:S(2)}) collective-permute-start(bf16[32,3584]{1,0:T(8,128)(2,1)S(1)} %add_convert_fusion.8), channel_id=1, source_target_pairs={{0,2},{1,3},{4,0},{5,1},{8,4},{9,5},{12,8},{13,9},{14,12},{15,13},... | collective-permute-start | bytes 688136 | tf_op jit(solution)/shard_map/ppermute | solution.py:79
  44.8 1.4 %collective-permute-start.16 = (bf16[32,3584]{1,0:T(8,128)(2,1)S(1)}, bf16[32,3584]{1,0:T(8,128)(2,1)S(1)}, u32[]{:S(2)}, u32[]{:S(2)}) collective-permute-start(bf16[32,3584]{1,0:T(8,128)(2,1)S(1)} %get-tuple-element.145), channel_id=1, source_target_pairs={{0,4},{1,5},{4,8},{5,9},{8,12},{9,13},{12,14},{13,15},{14,10},{15,... | collective-permute-start | bytes 688136 | tf_op jit(solution)/shard_map/ppermute | solution.py:79
  46.2 4.1 %collective-permute-done.18 = bf16[32,3584]{1,0:T(8,128)(2,1)S(1)} collective-permute-done((bf16[32,3584]{1,0:T(8,128)(2,1)S(1)}, bf16[32,3584]{1,0:T(8,128)(2,1)S(1)}, u32[]{:S(2)}, u32[]{:S(2)}) %collective-permute-start.18) | collective-permute-done | bytes 229408 | tf_op jit(solution)/shard_map/ppermute | solution.py:79
  50.5 2.0 %collective-permute-done.17 = bf16[32,3584]{1,0:T(8,128)(2,1)S(1)} collective-permute-done((bf16[32,3584]{1,0:T(8,128)(2,1)S(1)}, bf16[32,3584]{1,0:T(8,128)(2,1)S(1)}, u32[]{:S(2)}, u32[]{:S(2)}) %collective-permute-start.17) | collective-permute-done | bytes 229408 | tf_op jit(solution)/shard_map/ppermute | solution.py:79
  53.8 1.2 %collective-permute-start.22 = (bf16[32,3584]{1,0:T(8,128)(2,1)S(1)}, bf16[32,3584]{1,0:T(8,128)(2,1)S(1)}, u32[]{:S(2)}, u32[]{:S(2)}) collective-permute-start(bf16[32,3584]{1,0:T(8,128)(2,1)S(1)} %add_convert_fusion.1), channel_id=1, source_target_pairs={{0,2},{1,3},{4,0},{5,1},{8,4},{9,5},{12,8},{13,9},{14,12},{15,13},... | collective-permute-start | bytes 688136 | tf_op jit(solution)/shard_map/ppermute | solution.py:79
  57.1 4.2 %collective-permute-done.20 = bf16[32,3584]{1,0:T(8,128)(2,1)S(1)} collective-permute-done((bf16[32,3584]{1,0:T(8,128)(2,1)S(1)}, bf16[32,3584]{1,0:T(8,128)(2,1)S(1)}, u32[]{:S(2)}, u32[]{:S(2)}) %collective-permute-start.20) | collective-permute-done | bytes 229408 | tf_op jit(solution)/shard_map/ppermute | solution.py:79
  62.6 1.2 %collective-permute-start.23 = (bf16[32,3584]{1,0:T(8,128)(2,1)S(1)}, bf16[32,3584]{1,0:T(8,128)(2,1)S(1)}, u32[]{:S(2)}, u32[]{:S(2)}) collective-permute-start(bf16[32,3584]{1,0:T(8,128)(2,1)S(1)} %get-tuple-element.140), channel_id=1, source_target_pairs={{0,2},{1,3},{4,0},{5,1},{8,4},{9,5},{12,8},{13,9},{14,12},{15,13},... | collective-permute-start | bytes 688136 | tf_op jit(solution)/shard_map/ppermute | solution.py:79
  64.7 1.6 %collective-permute-done.25.refs_3_ = bf16[32,3584]{1,0:T(8,128)(2,1)S(1)} collective-permute-done((bf16[32,3584]{1,0:T(8,128)(2,1)S(1)}, bf16[32,3584]{1,0:T(8,128)(2,1)S(1)}, u32[]{:S(2)}, u32[]{:S(2)}) %collective-permute-start.25) | collective-permute-done | bytes 229408 | tf_op jit(solution)/shard_map/ppermute | solution.py:79
  66.2 2.5 %collective-permute-done.23.refs_3_ = bf16[32,3584]{1,0:T(8,128)(2,1)S(1)} collective-permute-done((bf16[32,3584]{1,0:T(8,128)(2,1)S(1)}, bf16[32,3584]{1,0:T(8,128)(2,1)S(1)}, u32[]{:S(2)}, u32[]{:S(2)}) %collective-permute-start.23) | collective-permute-done | bytes 229408 | tf_op jit(solution)/shard_map/ppermute | solution.py:79
  69.9 1.8 %enc_update.1 = (f32[32,3584]{1,0:T(8,128)}, f32[32,3584]{1,0:T(8,128)}, f32[32,3584]{1,0:T(8,128)}, bf16[32,3584]{1,0:T(8,128)(2,1)S(1)}, bf16[32,3584]{1,0:T(8,128)(2,1)S(1)}) custom-call(s32[32,1]{1,0:T(8,128)S(1)} %get-tuple-element.81.code_ref, f32[32,3584]{1,0:T(8,128)S(1)} %copy-done.1, f32[32,3584]{1,0:T(8,128)S(1)} %copy-done.2, ...), custom_call_target="tpu_custom_call" | custom-call | flops 4587520 | bytes 4587520 | tf_op jit(solution)/shard_map/enc_update/pallas_call | solution.py:313
  71.6 1.8 %dec_update.1 = (f32[32,3584]{1,0:T(8,128)}, f32[32,3584]{1,0:T(8,128)}, f32[32,3584]{1,0:T(8,128)}, bf16[2,32,3584]{2,1,0:T(8,128)(2,1)S(1)}) custom-call(s32[32,1]{1,0:T(8,128)S(1)} %get-tuple-element.81.code_ref, f32[32,3584]{1,0:T(8,128)S(1)} %copy-done.4, f32[32,3584]{1,0:T(8,128)S(1)} %copy-done.5, f32[32,3584]{1,0:T(8,128)S(1)} %copy-done.6, ...), custom_call_target="tpu_custom_call" | custom-call | flops 4587520 | bytes 4587520 | tf_op jit(solution)/shard_map/dec_update/pallas_call | solution.py:313
  76.2 6.5 %collective-permute-done.27.refs_1_ = bf16[64,3584]{1,0:T(8,128)(2,1)S(1)} collective-permute-done((bf16[64,3584]{1,0:T(8,128)(2,1)S(1)}, bf16[64,3584]{1,0:T(8,128)(2,1)S(1)}, u32[]{:S(2)}, u32[]{:S(2)}) %collective-permute-start.27) | collective-permute-done | bytes 458784 | tf_op jit(solution)/shard_map/ppermute | solution.py:79
  82.7 2.5 %collective-permute-done.26.refs_0_ = bf16[64,3584]{1,0:T(8,128)(2,1)S(1)} collective-permute-done((bf16[64,3584]{1,0:T(8,128)(2,1)S(1)}, bf16[64,3584]{1,0:T(8,128)(2,1)S(1)}, u32[]{:S(2)}, u32[]{:S(2)}) %collective-permute-start.26) | collective-permute-done | bytes 458784 | tf_op jit(solution)/shard_map/ppermute | solution.py:79
  85.2 1.2 %collective-permute-start.28 = (bf16[64,3584]{1,0:T(8,128)(2,1)S(1)}, bf16[64,3584]{1,0:T(8,128)(2,1)S(1)}, u32[]{:S(2)}, u32[]{:S(2)}) collective-permute-start(bf16[64,3584]{1,0:T(8,128)(2,1)S(1)} %collective-permute-done.26.refs_0_), channel_id=1, source_target_pairs={{0,4},{1,5},{4,8},{5,9},{8,12},{9,13},{12,14},{13,15},{14,10},{15,... | collective-permute-start | bytes 1376264 | tf_op jit(solution)/shard_map/ppermute | solution.py:79
  88.9 6.7 %collective-permute-done.28.refs_0_ = bf16[64,3584]{1,0:T(8,128)(2,1)S(1)} collective-permute-done((bf16[64,3584]{1,0:T(8,128)(2,1)S(1)}, bf16[64,3584]{1,0:T(8,128)(2,1)S(1)}, u32[]{:S(2)}, u32[]{:S(2)}) %collective-permute-start.28) | collective-permute-done | bytes 458784 | tf_op jit(solution)/shard_map/ppermute | solution.py:79
  95.6 1.7 %collective-permute-done.29.refs_1_ = bf16[64,3584]{1,0:T(8,128)(2,1)S(1)} collective-permute-done((bf16[64,3584]{1,0:T(8,128)(2,1)S(1)}, bf16[64,3584]{1,0:T(8,128)(2,1)S(1)}, u32[]{:S(2)}, u32[]{:S(2)}) %collective-permute-start.29) | collective-permute-done | bytes 458784 | tf_op jit(solution)/shard_map/ppermute | solution.py:79
  97.3 1.2 collective-permute-start.31
  99.9 1.3 %place.8 = (bf16[512,3584]{1,0:T(8,128)(2,1)}, bf16[512,3584]{1,0:T(8,128)(2,1)}) custom-call(bf16[64,3584]{1,0:T(8,128)(2,1)S(1)} %collective-permute-done.28.refs_0_, bf16[64,3584]{1,0:T(8,128)(2,1)S(1)} %collective-permute-done.29.refs_1_, bf16[64,3584]{1,0:T(8,128)(2,1)S(1)} %collective-permute-done.33.refs_2_, ...), custom_call_target="tpu_custom_call", output_to_operand_aliasing={{0}: (4, {}), {1}: (5, {})} | custom-call | bytes 3670016 | tf_op jit(solution)/shard_map/place/pallas_call | solution.py:348
  101.2 5.8 %collective-permute-done.31.refs_0_ = bf16[64,3584]{1,0:T(8,128)(2,1)S(1)} collective-permute-done((bf16[64,3584]{1,0:T(8,128)(2,1)S(1)}, bf16[64,3584]{1,0:T(8,128)(2,1)S(1)}, u32[]{:S(2)}, u32[]{:S(2)}) %collective-permute-start.31) | collective-permute-done | bytes 458784 | tf_op jit(solution)/shard_map/ppermute | solution.py:79
  106.9 2.5 %collective-permute-done.32.refs_1_ = bf16[64,3584]{1,0:T(8,128)(2,1)S(1)} collective-permute-done((bf16[64,3584]{1,0:T(8,128)(2,1)S(1)}, bf16[64,3584]{1,0:T(8,128)(2,1)S(1)}, u32[]{:S(2)}, u32[]{:S(2)}) %collective-permute-start.32) | collective-permute-done | bytes 458784 | tf_op jit(solution)/shard_map/ppermute | solution.py:79
  112.1 1.3 %place.9 = (bf16[512,3584]{1,0:T(8,128)(2,1)}, bf16[512,3584]{1,0:T(8,128)(2,1)}) custom-call(bf16[64,3584]{1,0:T(8,128)(2,1)S(1)} %collective-permute-done.31.refs_0_, bf16[64,3584]{1,0:T(8,128)(2,1)S(1)} %collective-permute-done.32.refs_1_, bf16[64,3584]{1,0:T(8,128)(2,1)S(1)} %collective-permute-done.37.refs_2_, ...), custom_call_target="tpu_custom_call", output_to_operand_aliasing={{0}: (4, {}), {1}: (5, {})} | custom-call | bytes 3670016 | tf_op jit(solution)/shard_map/place/pallas_call | solution.py:348
  113.4 2.2 %collective-permute-done.36.refs_1_ = bf16[64,1792]{1,0:T(8,128)(2,1)S(1)} collective-permute-done((bf16[64,1792]{1,0:T(8,128)(2,1)S(1)}, bf16[64,1792]{1,0:T(8,128)(2,1)S(1)}, u32[]{:S(2)}, u32[]{:S(2)}) %collective-permute-start.36) | collective-permute-done | bytes 229408 | tf_op jit(solution)/shard_map/ppermute | solution.py:79
  (109 shorter events, 29.3 us)
Async XLA Ops:
  1.6 12.1 %collective-permute-start.2 = (s32[1,48]{1,0:T(1,128)S(1)}, s32[1,48]{1,0:T(1,128)S(1)}, u32[]{:S(2)}, u32[]{:S(2)}) collective-permute-start(s32[1,48]{1,0:T(1,128)S(1)} %pad_add_fusion.1), channel_id=1, source_target_pairs={{0,3},{1,2},{2,1},{3,0},{4,7},{5,6},{6,5},{7,4},{8,11},{9,10},{10,... | collective-permute-start | bytes 584 | tf_op jit(solution)/shard_map/ppermute | solution.py:37
  4.0 9.6 %collective-permute-start.1 = (s32[1,48]{1,0:T(1,128)S(1)}, s32[1,48]{1,0:T(1,128)S(1)}, u32[]{:S(2)}, u32[]{:S(2)}) collective-permute-start(s32[1,48]{1,0:T(1,128)S(1)} %pad_add_fusion.1), channel_id=1, source_target_pairs={{0,2},{1,3},{2,0},{3,1},{4,6},{5,7},{6,4},{7,5},{8,10},{9,11},{10,... | collective-permute-start | bytes 584 | tf_op jit(solution)/shard_map/ppermute | solution.py:37
  4.7 9.0 %collective-permute-start = (s32[1,48]{1,0:T(1,128)S(1)}, s32[1,48]{1,0:T(1,128)S(1)}, u32[]{:S(2)}, u32[]{:S(2)}) collective-permute-start(s32[1,48]{1,0:T(1,128)S(1)} %pad_add_fusion.1), channel_id=1, source_target_pairs={{0,1},{1,0},{2,3},{3,2},{4,5},{5,4},{6,7},{7,6},{8,9},{9,8},{10,11... | collective-permute-start | bytes 584 | tf_op jit(solution)/shard_map/ppermute | solution.py:37
  14.3 7.5 %collective-permute-start.7 = (s32[4,48]{1,0:T(4,128)S(1)}, s32[4,48]{1,0:T(4,128)S(1)}, u32[]{:S(2)}, u32[]{:S(2)}) collective-permute-start(s32[4,48]{1,0:T(4,128)S(1)} %pad_add_fusion.refs_0_), channel_id=1, source_target_pairs={{0,12},{1,13},{2,14},{3,15},{4,8},{5,9},{6,10},{7,11},{8,4},{9,5},... | collective-permute-start | bytes 2312 | tf_op jit(solution)/shard_map/ppermute | solution.py:37
  19.7 11.3 %collective-permute-start.10 = (bf16[32,1792]{1,0:T(8,128)(2,1)S(1)}, bf16[32,1792]{1,0:T(8,128)(2,1)S(1)}, u32[]{:S(2)}, u32[]{:S(2)}) collective-permute-start(bf16[32,1792]{1,0:T(8,128)(2,1)S(1)} %get-tuple-element.150), channel_id=1, source_target_pairs={{0,2},{1,3},{4,0},{5,1},{8,4},{9,5},{12,8},{13,9},{14,12},{15,13},... | collective-permute-start | bytes 344072 | tf_op jit(solution)/shard_map/ppermute | solution.py:79
  21.5 9.5 %collective-permute-start.9 = (bf16[32,1792]{1,0:T(8,128)(2,1)S(1)}, bf16[32,1792]{1,0:T(8,128)(2,1)S(1)}, u32[]{:S(2)}, u32[]{:S(2)}) collective-permute-start(bf16[32,1792]{1,0:T(8,128)(2,1)S(1)} %get-tuple-element.151), channel_id=1, source_target_pairs={{0,4},{1,5},{4,8},{5,9},{8,12},{9,13},{12,14},{13,15},{14,10},{15,... | collective-permute-start | bytes 344072 | tf_op jit(solution)/shard_map/ppermute | solution.py:79
  31.7 8.5 %collective-permute-start.15 = (bf16[32,3584]{1,0:T(8,128)(2,1)S(1)}, bf16[32,3584]{1,0:T(8,128)(2,1)S(1)}, u32[]{:S(2)}, u32[]{:S(2)}) collective-permute-start(bf16[32,3584]{1,0:T(8,128)(2,1)S(1)} %get-tuple-element.146), channel_id=1, source_target_pairs={{0,2},{1,3},{4,0},{5,1},{8,4},{9,5},{12,8},{13,9},{14,12},{15,13},... | collective-permute-start | bytes 688136 | tf_op jit(solution)/shard_map/ppermute | solution.py:79
  33.1 8.5 %collective-permute-start.14 = (bf16[32,3584]{1,0:T(8,128)(2,1)S(1)}, bf16[32,3584]{1,0:T(8,128)(2,1)S(1)}, u32[]{:S(2)}, u32[]{:S(2)}) collective-permute-start(bf16[32,3584]{1,0:T(8,128)(2,1)S(1)} %get-tuple-element.147), channel_id=1, source_target_pairs={{0,4},{1,5},{4,8},{5,9},{8,12},{9,13},{12,14},{13,15},{14,10},{15,... | collective-permute-start | bytes 688136 | tf_op jit(solution)/shard_map/ppermute | solution.py:79
  34.9 9.1 %collective-permute-start.13 = (bf16[32,1792]{1,0:T(8,128)(2,1)S(1)}, bf16[32,1792]{1,0:T(8,128)(2,1)S(1)}, u32[]{:S(2)}, u32[]{:S(2)}) collective-permute-start(bf16[32,1792]{1,0:T(8,128)(2,1)S(1)} %get-tuple-element.148), channel_id=1, source_target_pairs={{0,2},{1,3},{4,0},{5,1},{8,4},{9,5},{12,8},{13,9},{14,12},{15,13},... | collective-permute-start | bytes 344072 | tf_op jit(solution)/shard_map/ppermute | solution.py:79
  36.3 7.6 %collective-permute-start.12 = (bf16[32,1792]{1,0:T(8,128)(2,1)S(1)}, bf16[32,1792]{1,0:T(8,128)(2,1)S(1)}, u32[]{:S(2)}, u32[]{:S(2)}) collective-permute-start(bf16[32,1792]{1,0:T(8,128)(2,1)S(1)} %get-tuple-element.149), channel_id=1, source_target_pairs={{0,4},{1,5},{4,8},{5,9},{8,12},{9,13},{12,14},{13,15},{14,10},{15,... | collective-permute-start | bytes 344072 | tf_op jit(solution)/shard_map/ppermute | solution.py:79
  41.7 8.5 %collective-permute-start.18 = (bf16[32,3584]{1,0:T(8,128)(2,1)S(1)}, bf16[32,3584]{1,0:T(8,128)(2,1)S(1)}, u32[]{:S(2)}, u32[]{:S(2)}) collective-permute-start(bf16[32,3584]{1,0:T(8,128)(2,1)S(1)} %add_convert_fusion.9), channel_id=1, source_target_pairs={{0,4},{1,5},{4,8},{5,9},{8,12},{9,13},{12,14},{13,15},{14,10},{15,... | collective-permute-start | bytes 688136 | tf_op jit(solution)/shard_map/ppermute | solution.py:79
  42.5 7.8 %collective-permute-start.19 = (bf16[32,3584]{1,0:T(8,128)(2,1)S(1)}, bf16[32,3584]{1,0:T(8,128)(2,1)S(1)}, u32[]{:S(2)}, u32[]{:S(2)}) collective-permute-start(bf16[32,3584]{1,0:T(8,128)(2,1)S(1)} %add_convert_fusion.8), channel_id=1, source_target_pairs={{0,2},{1,3},{4,0},{5,1},{8,4},{9,5},{12,8},{13,9},{14,12},{15,13},... | collective-permute-start | bytes 688136 | tf_op jit(solution)/shard_map/ppermute | solution.py:79
  44.1 8.3 %collective-permute-start.17 = (bf16[32,3584]{1,0:T(8,128)(2,1)S(1)}, bf16[32,3584]{1,0:T(8,128)(2,1)S(1)}, u32[]{:S(2)}, u32[]{:S(2)}) collective-permute-start(bf16[32,3584]{1,0:T(8,128)(2,1)S(1)} %get-tuple-element.144), channel_id=1, source_target_pairs={{0,2},{1,3},{4,0},{5,1},{8,4},{9,5},{12,8},{13,9},{14,12},{15,13},... | collective-permute-start | bytes 688136 | tf_op jit(solution)/shard_map/ppermute | solution.py:79
  44.8 7.9 %collective-permute-start.16 = (bf16[32,3584]{1,0:T(8,128)(2,1)S(1)}, bf16[32,3584]{1,0:T(8,128)(2,1)S(1)}, u32[]{:S(2)}, u32[]{:S(2)}) collective-permute-start(bf16[32,3584]{1,0:T(8,128)(2,1)S(1)} %get-tuple-element.145), channel_id=1, source_target_pairs={{0,4},{1,5},{4,8},{5,9},{8,12},{9,13},{12,14},{13,15},{14,10},{15,... | collective-permute-start | bytes 688136 | tf_op jit(solution)/shard_map/ppermute | solution.py:79
  52.8 8.4 %collective-permute-start.20 = (bf16[32,3584]{1,0:T(8,128)(2,1)S(1)}, bf16[32,3584]{1,0:T(8,128)(2,1)S(1)}, u32[]{:S(2)}, u32[]{:S(2)}) collective-permute-start(bf16[32,3584]{1,0:T(8,128)(2,1)S(1)} %add_convert_fusion.3), channel_id=1, source_target_pairs={{0,4},{1,5},{4,8},{5,9},{8,12},{9,13},{12,14},{13,15},{14,10},{15,... | collective-permute-start | bytes 688136 | tf_op jit(solution)/shard_map/ppermute | solution.py:79
  53.8 8.6 %collective-permute-start.22 = (bf16[32,3584]{1,0:T(8,128)(2,1)S(1)}, bf16[32,3584]{1,0:T(8,128)(2,1)S(1)}, u32[]{:S(2)}, u32[]{:S(2)}) collective-permute-start(bf16[32,3584]{1,0:T(8,128)(2,1)S(1)} %add_convert_fusion.1), channel_id=1, source_target_pairs={{0,2},{1,3},{4,0},{5,1},{8,4},{9,5},{12,8},{13,9},{14,12},{15,13},... | collective-permute-start | bytes 688136 | tf_op jit(solution)/shard_map/ppermute | solution.py:79
  55.1 11.2 %collective-permute-start.25 = (bf16[32,3584]{1,0:T(8,128)(2,1)S(1)}, bf16[32,3584]{1,0:T(8,128)(2,1)S(1)}, u32[]{:S(2)}, u32[]{:S(2)}) collective-permute-start(bf16[32,3584]{1,0:T(8,128)(2,1)S(1)} %get-tuple-element.142), channel_id=1, source_target_pairs={{0,2},{1,3},{4,0},{5,1},{8,4},{9,5},{12,8},{13,9},{14,12},{15,13},... | collective-permute-start | bytes 688136 | tf_op jit(solution)/shard_map/ppermute | solution.py:79
  56.2 10.0 %collective-permute-start.24 = (bf16[32,3584]{1,0:T(8,128)(2,1)S(1)}, bf16[32,3584]{1,0:T(8,128)(2,1)S(1)}, u32[]{:S(2)}, u32[]{:S(2)}) collective-permute-start(bf16[32,3584]{1,0:T(8,128)(2,1)S(1)} %get-tuple-element.143), channel_id=1, source_target_pairs={{0,4},{1,5},{4,8},{5,9},{8,12},{9,13},{12,14},{13,15},{14,10},{15,... | collective-permute-start | bytes 688136 | tf_op jit(solution)/shard_map/ppermute | solution.py:79
  62.6 6.1 %collective-permute-start.23 = (bf16[32,3584]{1,0:T(8,128)(2,1)S(1)}, bf16[32,3584]{1,0:T(8,128)(2,1)S(1)}, u32[]{:S(2)}, u32[]{:S(2)}) collective-permute-start(bf16[32,3584]{1,0:T(8,128)(2,1)S(1)} %get-tuple-element.140), channel_id=1, source_target_pairs={{0,2},{1,3},{4,0},{5,1},{8,4},{9,5},{12,8},{13,9},{14,12},{15,13},... | collective-permute-start | bytes 688136 | tf_op jit(solution)/shard_map/ppermute | solution.py:79
  73.4 9.3 %collective-permute-start.27 = (bf16[64,3584]{1,0:T(8,128)(2,1)S(1)}, bf16[64,3584]{1,0:T(8,128)(2,1)S(1)}, u32[]{:S(2)}, u32[]{:S(2)}) collective-permute-start(bf16[64,3584]{1,0:T(8,128)(2,1)S(1)} %bitcast.4), channel_id=1, source_target_pairs={{0,2},{1,3},{4,0},{5,1},{8,4},{9,5},{12,8},{13,9},{14,12},{15,13},... | collective-permute-start | bytes 1376264 | tf_op jit(solution)/shard_map/ppermute | solution.py:79
  74.6 10.7 %collective-permute-start.26 = (bf16[64,3584]{1,0:T(8,128)(2,1)S(1)}, bf16[64,3584]{1,0:T(8,128)(2,1)S(1)}, u32[]{:S(2)}, u32[]{:S(2)}) collective-permute-start(bf16[64,3584]{1,0:T(8,128)(2,1)S(1)} %bitcast.5), channel_id=1, source_target_pairs={{0,4},{1,5},{4,8},{5,9},{8,12},{9,13},{12,14},{13,15},{14,10},{15,... | collective-permute-start | bytes 1376264 | tf_op jit(solution)/shard_map/ppermute | solution.py:79
  75.4 12.4 %collective-permute-start.30 = (bf16[64,3584]{1,0:T(8,128)(2,1)S(1)}, bf16[64,3584]{1,0:T(8,128)(2,1)S(1)}, u32[]{:S(2)}, u32[]{:S(2)}) collective-permute-start(bf16[64,3584]{1,0:T(8,128)(2,1)S(1)} %bitcast.6), channel_id=1, source_target_pairs={{0,1},{1,0},{2,3},{3,2},{4,5},{5,4},{6,7},{7,6},{8,9},{9,8},{10,11... | collective-permute-start | bytes 1376264 | tf_op jit(solution)/shard_map/ppermute | solution.py:37
  85.2 10.4 %collective-permute-start.28 = (bf16[64,3584]{1,0:T(8,128)(2,1)S(1)}, bf16[64,3584]{1,0:T(8,128)(2,1)S(1)}, u32[]{:S(2)}, u32[]{:S(2)}) collective-permute-start(bf16[64,3584]{1,0:T(8,128)(2,1)S(1)} %collective-permute-done.26.refs_0_), channel_id=1, source_target_pairs={{0,4},{1,5},{4,8},{5,9},{8,12},{9,13},{12,14},{13,15},{14,10},{15,... | collective-permute-start | bytes 1376264 | tf_op jit(solution)/shard_map/ppermute | solution.py:79
  86.5 10.8 %collective-permute-start.29 = (bf16[64,3584]{1,0:T(8,128)(2,1)S(1)}, bf16[64,3584]{1,0:T(8,128)(2,1)S(1)}, u32[]{:S(2)}, u32[]{:S(2)}) collective-permute-start(bf16[64,3584]{1,0:T(8,128)(2,1)S(1)} %collective-permute-done.27.refs_1_), channel_id=1, source_target_pairs={{0,2},{1,3},{4,0},{5,1},{8,4},{9,5},{12,8},{13,9},{14,12},{15,13},... | collective-permute-start | bytes 1376264 | tf_op jit(solution)/shard_map/ppermute | solution.py:79
  87.3 12.1 %collective-permute-start.33 = (bf16[64,3584]{1,0:T(8,128)(2,1)S(1)}, bf16[64,3584]{1,0:T(8,128)(2,1)S(1)}, u32[]{:S(2)}, u32[]{:S(2)}) collective-permute-start(bf16[64,3584]{1,0:T(8,128)(2,1)S(1)} %collective-permute-done.26.refs_0_), channel_id=1, source_target_pairs={{0,1},{1,0},{2,3},{3,2},{4,5},{5,4},{6,7},{7,6},{8,9},{9,8},{10,11... | collective-permute-start | bytes 1376264 | tf_op jit(solution)/shard_map/ppermute | solution.py:37
  87.3 12.6 %collective-permute-start.34 = (bf16[64,3584]{1,0:T(8,128)(2,1)S(1)}, bf16[64,3584]{1,0:T(8,128)(2,1)S(1)}, u32[]{:S(2)}, u32[]{:S(2)}) collective-permute-start(bf16[64,3584]{1,0:T(8,128)(2,1)S(1)} %collective-permute-done.27.refs_1_), channel_id=1, source_target_pairs={{0,1},{1,0},{2,3},{3,2},{4,5},{5,4},{6,7},{7,6},{8,9},{9,8},{10,11... | collective-permute-start | bytes 1376264 | tf_op jit(solution)/shard_map/ppermute | solution.py:37
  97.3 9.6 %collective-permute-start.31 = (bf16[64,3584]{1,0:T(8,128)(2,1)S(1)}, bf16[64,3584]{1,0:T(8,128)(2,1)S(1)}, u32[]{:S(2)}, u32[]{:S(2)}) collective-permute-start(bf16[64,3584]{1,0:T(8,128)(2,1)S(1)} %collective-permute-done.28.refs_0_), channel_id=1, source_target_pairs={{0,4},{1,5},{4,8},{5,9},{8,12},{9,13},{12,14},{13,15},{14,10},{15,... | collective-permute-start | bytes 1376264 | tf_op jit(solution)/shard_map/ppermute | solution.py:79
  98.5 10.9 %collective-permute-start.32 = (bf16[64,3584]{1,0:T(8,128)(2,1)S(1)}, bf16[64,3584]{1,0:T(8,128)(2,1)S(1)}, u32[]{:S(2)}, u32[]{:S(2)}) collective-permute-start(bf16[64,3584]{1,0:T(8,128)(2,1)S(1)} %collective-permute-done.29.refs_1_), channel_id=1, source_target_pairs={{0,2},{1,3},{4,0},{5,1},{8,4},{9,5},{12,8},{13,9},{14,12},{15,13},... | collective-permute-start | bytes 1376264 | tf_op jit(solution)/shard_map/ppermute | solution.py:79
  99.3 12.2 %collective-permute-start.37 = (bf16[64,3584]{1,0:T(8,128)(2,1)S(1)}, bf16[64,3584]{1,0:T(8,128)(2,1)S(1)}, u32[]{:S(2)}, u32[]{:S(2)}) collective-permute-start(bf16[64,3584]{1,0:T(8,128)(2,1)S(1)} %collective-permute-done.28.refs_0_), channel_id=1, source_target_pairs={{0,1},{1,0},{2,3},{3,2},{4,5},{5,4},{6,7},{7,6},{8,9},{9,8},{10,11... | collective-permute-start | bytes 1376264 | tf_op jit(solution)/shard_map/ppermute | solution.py:37
  99.3 12.7 %collective-permute-start.38 = (bf16[64,3584]{1,0:T(8,128)(2,1)S(1)}, bf16[64,3584]{1,0:T(8,128)(2,1)S(1)}, u32[]{:S(2)}, u32[]{:S(2)}) collective-permute-start(bf16[64,3584]{1,0:T(8,128)(2,1)S(1)} %collective-permute-done.29.refs_1_), channel_id=1, source_target_pairs={{0,1},{1,0},{2,3},{3,2},{4,5},{5,4},{6,7},{7,6},{8,9},{9,8},{10,11... | collective-permute-start | bytes 1376264 | tf_op jit(solution)/shard_map/ppermute | solution.py:37
  109.5 6.1 %collective-permute-start.36 = (bf16[64,1792]{1,0:T(8,128)(2,1)S(1)}, bf16[64,1792]{1,0:T(8,128)(2,1)S(1)}, u32[]{:S(2)}, u32[]{:S(2)}) collective-permute-start(bf16[64,1792]{1,0:T(8,128)(2,1)S(1)} %slice.135), channel_id=1, source_target_pairs={{0,2},{1,3},{4,0},{5,1},{8,4},{9,5},{12,8},{13,9},{14,12},{15,13},... | collective-permute-start | bytes 688136 | tf_op jit(solution)/shard_map/ppermute | solution.py:79
  110.4 6.0 %collective-permute-start.35 = (bf16[64,1792]{1,0:T(8,128)(2,1)S(1)}, bf16[64,1792]{1,0:T(8,128)(2,1)S(1)}, u32[]{:S(2)}, u32[]{:S(2)}) collective-permute-start(bf16[64,1792]{1,0:T(8,128)(2,1)S(1)} %slice.134), channel_id=1, source_target_pairs={{0,4},{1,5},{4,8},{5,9},{8,12},{9,13},{12,14},{13,15},{14,10},{15,... | collective-permute-start | bytes 688136 | tf_op jit(solution)/shard_map/ppermute | solution.py:79
  (25 other events, 299.2 us)

commit v9 on v8

--- a/solution.py
+++ b/solution.py
@@ -196,7 +196,7 @@
             pltpu.SemaphoreType.DMA((pieces, cuts)),
             pltpu.SemaphoreType.DMA((pieces, 4)),
         ],
-        compiler_params=params(56),
+        compiler_params=params(50),
         cost_estimate=cost(
             2 * latents * tokens * width, 2 * (tokens * width + latents * (tokens + width))
         ),
@@ -372,7 +372,8 @@
         sent = [(offset, 1, column, swap(value, 1, size)) for offset, _, column, value in near]
         wholes = place(near + far, wholes, size, rows, width)
         far = sent
-        right, left, wholes = lax.optimization_barrier((right, left, wholes))
+        right, wholes = tied(right, wholes)
+        left = after(left, right)
         near = [(-hop, 0, 0, right), (hop, 0, half if hop == hops else 0, left)]
     sent = [(offset, 1, column, swap(value, 1, size)) for offset, _, column, value in near]
     wholes = place(near + far, wholes, size, rows, width)
@@ -407,16 +408,17 @@
     def travel(moving):
         return [shift(moving[0], 1, size), shift(moving[1], -1, size)]
 
-    def advance(came, kept, from_core, hop):
-        moving = []
+    def advance(came, kept, from_core, hop, order):
+        following = []
         for side, value in enumerate(came):
-            value = value.astype(jnp.float32)
+            value = after(value, order).astype(jnp.float32)
             if value.shape[1] < width:
                 pads = ((0, 0, 0), (0, half, 0) if side == 0 else (half, 0, 0))
                 value = lax.pad(value, jnp.float32(0), pads)
             value = value + term(kept, from_core, 2 * hop - side, rows)
-            moving.append(value.astype(jnp.bfloat16))
-        return moving
+            order = value.astype(jnp.bfloat16)
+            following.append(shift(order, 1 - 2 * side, size))
+        return following, order
 
     dec = stream_product(latent_act, out_grad, size, rows)
     dec_far = after(dec[0], *stages[0])
@@ -427,19 +429,15 @@
     )
     dec_came, enc_far = tied(travel(dec_moving), enc[0])
     enc_kept, enc_core = [enc[1], enc[3]], [swap(enc_far, 1, size), swap(enc[2], 1, size)]
-    dec_moving = advance(dec_came, dec_kept, dec_core, 1)
-    dec_came = travel(dec_moving)
-    enc_moving = begin(enc_kept, after(enc_core, *dec_moving))
-    enc_came = travel(enc_moving)
-    dec_came = after(dec_came, *enc_moving)
+    dec_came, order = advance(dec_came, dec_kept, dec_core, 1, enc[0])
+    enc_moving = begin(enc_kept, after(enc_core, order))
+    enc_came, order = travel(enc_moving), enc_moving[1]
     for hop in range(1, chips // 2):
         if hop + 1 < chips // 2:
-            dec_moving = advance(dec_came, dec_kept, dec_core, hop + 1)
-            dec_came = travel(dec_moving)
-            enc_came = after(enc_came, *dec_moving)
-        enc_moving = advance(enc_came, enc_kept, enc_core, hop)
-        enc_came = travel(enc_moving)
-        dec_came = after(dec_came, *enc_moving)
+            dec_came, order = advance(dec_came, dec_kept, dec_core, hop + 1, order)
+        else:
+            dec_came, order = tied(dec_came, order)
+        enc_came, order = advance(enc_came, enc_kept, enc_core, hop, order)
     enc_out, enc_mo, enc_vo, enc_block, fresh = update(
         enc_kernel,
         code,

time: 119 us -> 118 us (level)
  local copies, waits for them, and re-layouts: 1.35 us -> 0.12 us
    ppermute x24, starting transfers between devices: 24.8 us -> 26.1 us  [shift(): return lax.ppermute(value, 'latent', pairs)]
    unnamed x28 -> x24, local copies, waits for them, and re-layouts: 1.28 us -> 0.06 us
  transfers between devices with their start and end apart: 43 -> 43, of which waited for: 21 -> 17; matrix products, arithmetic and copies ran while one was open for 2% -> 1% of each run, Pallas kernels for 18% -> 18%
where the time goes in v9:
time: 118 us; the launch traced here: 117 us
  waiting for transfers between devices  52.5 us (44%)
  starting transfers between devices  36.4 us (31%)
  Pallas kernels  25.3 us (21%)
  other arithmetic  2.07 us (2%)
    ppermute x24, waiting for transfers between devices, shift(): return lax.ppermute(value, 'latent', pairs)  49.3 us
    ppermute x24, starting transfers between devices, shift(): return lax.ppermute(value, 'latent', pairs)  26.1 us
    ppermute x19, starting transfers between devices, swap(): return lax.ppermute(value, 'latent', [(i, i ^ bits) for i in range(size)])  10.2 us
    pallas_call x1, Pallas kernels, stream_product(): pl.pallas_call(functools.partial(stream_kernel, size, rows), in_specs=[pl...  8.36 us
    pallas_call x1, Pallas kernels, select_product(): pl.pallas_call(functools.partial(select_kernel, size, rows, len(table)),...  7.01 us
    pallas_call x6, Pallas kernels, place(): pl.pallas_call(functools.partial(place_kernel, plan, size, rows, count),...  6.43 us
    pallas_call x2, Pallas kernels, update(): pl.pallas_call(kernel, grid=(rows // tile,), in_specs=[last_rows(value) f...  3.52 us
    ppermute x19, waiting for transfers between devices, swap(): return lax.ppermute(value, 'latent', [(i, i ^ bits) for i in range(size)])  3.13 us
  transfers between devices with their start and end apart: 43, of which 17 were waited for; matrix products, arithmetic and copies ran while one was open for 1% of the time, Pallas kernels for 18%

profile of v9, /device:TPU:0, one launch (start us, length us, event | category | flops | bytes accessed | tf_op | source)
XLA Modules:
  0.0 117.3 jit_solution(3579793225949535837)
XLA Ops:
  1.6 2.5 %collective-permute-start.2 = (s32[1,48]{1,0:T(1,128)S(1)}, s32[1,48]{1,0:T(1,128)S(1)}, u32[]{:S(2)}, u32[]{:S(2)}) collective-permute-start(s32[1,48]{1,0:T(1,128)S(1)} %pad_add_fusion.1), channel_id=1, source_target_pairs={{0,3},{1,2},{2,1},{3,0},{4,7},{5,6},{6,5},{7,4},{8,11},{9,10},{10,... | collective-permute-start | bytes 584 | tf_op jit(solution)/shard_map/ppermute | solution.py:37
  4.7 8.4 %product.1 = (bf16[128,3584]{1,0:T(8,128)(2,1)S(1)}, bf16[128,3584]{1,0:T(8,128)(2,1)S(1)}, bf16[128,3584]{1,0:T(8,128)(2,1)S(1)}, bf16[128,3584]{1,0:T(8,128)(2,1)S(1)}) custom-call(bf16[1024,512]{1,0:T(8,128)(2,1)} %coef_ref.1, bf16[1024,3584]{1,0:T(8,128)(2,1)} %right_hbm.1), custom_call_target="tpu_custom_call" | custom-call | flops 3758096384 | bytes 12058624 | tf_op jit(solution)/shard_map/product/pallas_call | solution.py:186
  13.8 3.8 %collective-permute-start.7 = (s32[4,48]{1,0:T(4,128)S(1)}, s32[4,48]{1,0:T(4,128)S(1)}, u32[]{:S(2)}, u32[]{:S(2)}) collective-permute-start(s32[4,48]{1,0:T(4,128)S(1)} %pad_add_fusion.refs_0_), channel_id=1, source_target_pairs={{0,12},{1,13},{2,14},{3,15},{4,8},{5,9},{6,10},{7,11},{8,4},{9,5},... | collective-permute-start | bytes 2312 | tf_op jit(solution)/shard_map/ppermute | solution.py:37
  18.3 1.8 %collective-permute-start.10 = (bf16[32,1792]{1,0:T(8,128)(2,1)S(1)}, bf16[32,1792]{1,0:T(8,128)(2,1)S(1)}, u32[]{:S(2)}, u32[]{:S(2)}) collective-permute-start(bf16[32,1792]{1,0:T(8,128)(2,1)S(1)} %get-tuple-element.144), channel_id=1, source_target_pairs={{0,2},{1,3},{4,0},{5,1},{8,4},{9,5},{12,8},{13,9},{14,12},{15,13},... | collective-permute-start | bytes 344072 | tf_op jit(solution)/shard_map/ppermute | solution.py:79
  20.3 1.8 %collective-permute-done.6.refs_2_ = s32[4,48]{1,0:T(4,128)S(1)} collective-permute-done((s32[4,48]{1,0:T(4,128)S(1)}, s32[4,48]{1,0:T(4,128)S(1)}, u32[]{:S(2)}, u32[]{:S(2)}) %collective-permute-start.6) | collective-permute-done | bytes 800 | tf_op jit(solution)/shard_map/ppermute | solution.py:37
  22.2 7.0 %select_product.1 = (bf16[128,3584]{1,0:T(8,128)(2,1)S(1)}, bf16[128,3584]{1,0:T(8,128)(2,1)S(1)}, bf16[128,3584]{1,0:T(8,128)(2,1)S(1)}, bf16[128,3584]{1,0:T(8,128)(2,1)S(1)}, s32[32,1]{1,0:T(8,128)S(1)}) custom-call(bf16[1024,512]{1,0:T(8,128)(2,1)S(1)} %copy-done.6, bf16[1024,3584]{1,0:T(8,128)(2,1)S(1)} %bitcast.9, s32[2,16]{1,0:T(2,128)S(1)} %bitcast.10, ...), custom_call_target="tpu_custom_call" | custom-call | flops 3758096384 | bytes 12058624 | tf_op jit(solution)/shard_map/select_product/pallas_call | solution.py:237
  30.0 2.1 %collective-permute-start.13 = (bf16[32,3584]{1,0:T(8,128)(2,1)S(1)}, bf16[32,3584]{1,0:T(8,128)(2,1)S(1)}, u32[]{:S(2)}, u32[]{:S(2)}) collective-permute-start(bf16[32,3584]{1,0:T(8,128)(2,1)S(1)} %add_convert_fusion.11), channel_id=1, source_target_pairs={{0,2},{1,3},{4,0},{5,1},{8,4},{9,5},{12,8},{13,9},{14,12},{15,13},... | collective-permute-start | bytes 688136 | tf_op jit(solution)/shard_map/ppermute | solution.py:79
  33.1 1.6 %collective-permute-start.18 = (bf16[32,1792]{1,0:T(8,128)(2,1)S(1)}, bf16[32,1792]{1,0:T(8,128)(2,1)S(1)}, u32[]{:S(2)}, u32[]{:S(2)}) collective-permute-start(bf16[32,1792]{1,0:T(8,128)(2,1)S(1)} %get-tuple-element.142), channel_id=1, source_target_pairs={{0,2},{1,3},{4,0},{5,1},{8,4},{9,5},{12,8},{13,9},{14,12},{15,13},... | collective-permute-start | bytes 344072 | tf_op jit(solution)/shard_map/ppermute | solution.py:79
  34.7 2.8 %collective-permute-done.14 = bf16[32,3584]{1,0:T(8,128)(2,1)S(1)} collective-permute-done((bf16[32,3584]{1,0:T(8,128)(2,1)S(1)}, bf16[32,3584]{1,0:T(8,128)(2,1)S(1)}, u32[]{:S(2)}, u32[]{:S(2)}) %collective-permute-start.14) | collective-permute-done | bytes 229408 | tf_op jit(solution)/shard_map/ppermute | solution.py:79
  39.0 2.1 %collective-permute-start.12 = (bf16[32,1792]{1,0:T(8,128)(2,1)S(1)}, bf16[32,1792]{1,0:T(8,128)(2,1)S(1)}, u32[]{:S(2)}, u32[]{:S(2)}) collective-permute-start(bf16[32,1792]{1,0:T(8,128)(2,1)S(1)} %get-tuple-element.143), channel_id=1, source_target_pairs={{0,4},{1,5},{4,8},{5,9},{8,12},{9,13},{12,14},{13,15},{14,10},{15,... | collective-permute-start | bytes 344072 | tf_op jit(solution)/shard_map/ppermute | solution.py:79
  41.2 5.6 %collective-permute-done.12 = bf16[32,1792]{1,0:T(8,128)(2,1)S(1)} collective-permute-done((bf16[32,1792]{1,0:T(8,128)(2,1)S(1)}, bf16[32,1792]{1,0:T(8,128)(2,1)S(1)}, u32[]{:S(2)}, u32[]{:S(2)}) %collective-permute-start.12) | collective-permute-done | bytes 114720 | tf_op jit(solution)/shard_map/ppermute | solution.py:79
  47.7 1.5 %collective-permute-start.21 = (bf16[32,3584]{1,0:T(8,128)(2,1)S(1)}, bf16[32,3584]{1,0:T(8,128)(2,1)S(1)}, u32[]{:S(2)}, u32[]{:S(2)}) collective-permute-start(bf16[32,3584]{1,0:T(8,128)(2,1)S(1)} %add_convert_fusion.6), channel_id=1, source_target_pairs={{0,2},{1,3},{4,0},{5,1},{8,4},{9,5},{12,8},{13,9},{14,12},{15,13},... | collective-permute-start | bytes 688136 | tf_op jit(solution)/shard_map/ppermute | solution.py:79
  50.0 1.5 %collective-permute-start.25 = (bf16[32,3584]{1,0:T(8,128)(2,1)S(1)}, bf16[32,3584]{1,0:T(8,128)(2,1)S(1)}, u32[]{:S(2)}, u32[]{:S(2)}) collective-permute-start(bf16[32,3584]{1,0:T(8,128)(2,1)S(1)} %add_convert_fusion.4), channel_id=1, source_target_pairs={{0,2},{1,3},{4,0},{5,1},{8,4},{9,5},{12,8},{13,9},{14,12},{15,13},... | collective-permute-start | bytes 688136 | tf_op jit(solution)/shard_map/ppermute | solution.py:79
  51.5 4.1 %collective-permute-done.15 = bf16[32,3584]{1,0:T(8,128)(2,1)S(1)} collective-permute-done((bf16[32,3584]{1,0:T(8,128)(2,1)S(1)}, bf16[32,3584]{1,0:T(8,128)(2,1)S(1)}, u32[]{:S(2)}, u32[]{:S(2)}) %collective-permute-start.15) | collective-permute-done | bytes 229408 | tf_op jit(solution)/shard_map/ppermute | solution.py:79
  56.4 1.5 %collective-permute-start.22 = (bf16[32,3584]{1,0:T(8,128)(2,1)S(1)}, bf16[32,3584]{1,0:T(8,128)(2,1)S(1)}, u32[]{:S(2)}, u32[]{:S(2)}) collective-permute-start(bf16[32,3584]{1,0:T(8,128)(2,1)S(1)} %add_convert_fusion.1), channel_id=1, source_target_pairs={{0,2},{1,3},{4,0},{5,1},{8,4},{9,5},{12,8},{13,9},{14,12},{15,13},... | collective-permute-start | bytes 688136 | tf_op jit(solution)/shard_map/ppermute | solution.py:79
  57.9 4.8 %collective-permute-done.19 = bf16[32,3584]{1,0:T(8,128)(2,1)S(1)} collective-permute-done((bf16[32,3584]{1,0:T(8,128)(2,1)S(1)}, bf16[32,3584]{1,0:T(8,128)(2,1)S(1)}, u32[]{:S(2)}, u32[]{:S(2)}) %collective-permute-start.19) | collective-permute-done | bytes 229408 | tf_op jit(solution)/shard_map/ppermute | solution.py:79
  63.6 1.2 %collective-permute-start.23 = (bf16[32,3584]{1,0:T(8,128)(2,1)S(1)}, bf16[32,3584]{1,0:T(8,128)(2,1)S(1)}, u32[]{:S(2)}, u32[]{:S(2)}) collective-permute-start(bf16[32,3584]{1,0:T(8,128)(2,1)S(1)} %add_convert_fusion), channel_id=1, source_target_pairs={{0,2},{1,3},{4,0},{5,1},{8,4},{9,5},{12,8},{13,9},{14,12},{15,13},... | collective-permute-start | bytes 688136 | tf_op jit(solution)/shard_map/ppermute | solution.py:79
  65.6 4.0 %collective-permute-done.23.refs_3_ = bf16[32,3584]{1,0:T(8,128)(2,1)S(1)} collective-permute-done((bf16[32,3584]{1,0:T(8,128)(2,1)S(1)}, bf16[32,3584]{1,0:T(8,128)(2,1)S(1)}, u32[]{:S(2)}, u32[]{:S(2)}) %collective-permute-start.23) | collective-permute-done | bytes 229408 | tf_op jit(solution)/shard_map/ppermute | solution.py:79
  70.8 1.8 %enc_update.1 = (f32[32,3584]{1,0:T(8,128)}, f32[32,3584]{1,0:T(8,128)}, f32[32,3584]{1,0:T(8,128)}, bf16[32,3584]{1,0:T(8,128)(2,1)S(1)}, bf16[32,3584]{1,0:T(8,128)(2,1)S(1)}) custom-call(s32[32,1]{1,0:T(8,128)S(1)} %get-tuple-element.82.code_ref, f32[32,3584]{1,0:T(8,128)S(1)} %copy-done, f32[32,3584]{1,0:T(8,128)S(1)} %copy-done.1, ...), custom_call_target="tpu_custom_call" | custom-call | flops 4587520 | bytes 4587520 | tf_op jit(solution)/shard_map/enc_update/pallas_call | solution.py:313
  72.6 1.8 %dec_update.1 = (f32[32,3584]{1,0:T(8,128)}, f32[32,3584]{1,0:T(8,128)}, f32[32,3584]{1,0:T(8,128)}, bf16[2,32,3584]{2,1,0:T(8,128)(2,1)S(1)}) custom-call(s32[32,1]{1,0:T(8,128)S(1)} %get-tuple-element.82.code_ref, f32[32,3584]{1,0:T(8,128)S(1)} %copy-done.3, f32[32,3584]{1,0:T(8,128)S(1)} %copy-done.4, f32[32,3584]{1,0:T(8,128)S(1)} %copy-done.5, ...), custom_call_target="tpu_custom_call" | custom-call | flops 4587520 | bytes 4587520 | tf_op jit(solution)/shard_map/dec_update/pallas_call | solution.py:313
  77.1 7.8 %collective-permute-done.26.refs_0_ = bf16[64,3584]{1,0:T(8,128)(2,1)S(1)} collective-permute-done((bf16[64,3584]{1,0:T(8,128)(2,1)S(1)}, bf16[64,3584]{1,0:T(8,128)(2,1)S(1)}, u32[]{:S(2)}, u32[]{:S(2)}) %collective-permute-start.26) | collective-permute-done | bytes 458784 | tf_op jit(solution)/shard_map/ppermute | solution.py:79
  85.0 1.2 collective-permute-start.27
  88.9 6.3 %collective-permute-done.27.refs_0_ = bf16[64,3584]{1,0:T(8,128)(2,1)S(1)} collective-permute-done((bf16[64,3584]{1,0:T(8,128)(2,1)S(1)}, bf16[64,3584]{1,0:T(8,128)(2,1)S(1)}, u32[]{:S(2)}, u32[]{:S(2)}) %collective-permute-start.27) | collective-permute-done | bytes 458784 | tf_op jit(solution)/shard_map/ppermute | solution.py:79
  95.2 1.4 %collective-permute-start.30 = (bf16[64,3584]{1,0:T(8,128)(2,1)S(1)}, bf16[64,3584]{1,0:T(8,128)(2,1)S(1)}, u32[]{:S(2)}, u32[]{:S(2)}) collective-permute-start(bf16[64,3584]{1,0:T(8,128)(2,1)S(1)} %collective-permute-done.27.refs_0_), channel_id=1, source_target_pairs={{0,4},{1,5},{4,8},{5,9},{8,12},{9,13},{12,14},{13,15},{14,10},{15,... | collective-permute-start | bytes 1376264 | tf_op jit(solution)/shard_map/ppermute | solution.py:79
  96.8 1.3 %collective-permute-start.35 = (bf16[64,3584]{1,0:T(8,128)(2,1)S(1)}, bf16[64,3584]{1,0:T(8,128)(2,1)S(1)}, u32[]{:S(2)}, u32[]{:S(2)}) collective-permute-start(bf16[64,3584]{1,0:T(8,128)(2,1)S(1)} %collective-permute-done.31.refs_1_), channel_id=1, source_target_pairs={{0,2},{1,3},{4,0},{5,1},{8,4},{9,5},{12,8},{13,9},{14,12},{15,13},... | collective-permute-start | bytes 1376264 | tf_op jit(solution)/shard_map/ppermute | solution.py:79
  98.6 1.3 %place.8 = (bf16[512,3584]{1,0:T(8,128)(2,1)}, bf16[512,3584]{1,0:T(8,128)(2,1)}) custom-call(bf16[64,3584]{1,0:T(8,128)(2,1)S(1)} %collective-permute-done.27.refs_0_, bf16[64,3584]{1,0:T(8,128)(2,1)S(1)} %collective-permute-done.31.refs_1_, bf16[64,3584]{1,0:T(8,128)(2,1)S(1)} %collective-permute-done.32.refs_2_, ...), custom_call_target="tpu_custom_call", output_to_operand_aliasing={{0}: (4, {}), {1}: (5, {})} | custom-call | bytes 3670016 | tf_op jit(solution)/shard_map/place/pallas_call | solution.py:348
  99.9 4.8 %collective-permute-done.30.refs_0_ = bf16[64,3584]{1,0:T(8,128)(2,1)S(1)} collective-permute-done((bf16[64,3584]{1,0:T(8,128)(2,1)S(1)}, bf16[64,3584]{1,0:T(8,128)(2,1)S(1)}, u32[]{:S(2)}, u32[]{:S(2)}) %collective-permute-start.30) | collective-permute-done | bytes 458784 | tf_op jit(solution)/shard_map/ppermute | solution.py:79
  104.8 2.1 %collective-permute-start.34 = (bf16[64,1792]{1,0:T(8,128)(2,1)S(1)}, bf16[64,1792]{1,0:T(8,128)(2,1)S(1)}, u32[]{:S(2)}, u32[]{:S(2)}) collective-permute-start(bf16[64,1792]{1,0:T(8,128)(2,1)S(1)} %slice.134), channel_id=1, source_target_pairs={{0,4},{1,5},{4,8},{5,9},{8,12},{9,13},{12,14},{13,15},{14,10},{15,... | collective-permute-start | bytes 688136 | tf_op jit(solution)/shard_map/ppermute | solution.py:79
  107.8 1.3 %place.9 = (bf16[512,3584]{1,0:T(8,128)(2,1)}, bf16[512,3584]{1,0:T(8,128)(2,1)}) custom-call(bf16[64,3584]{1,0:T(8,128)(2,1)S(1)} %collective-permute-done.30.refs_0_, bf16[64,3584]{1,0:T(8,128)(2,1)S(1)} %collective-permute-done.35.refs_1_, bf16[64,3584]{1,0:T(8,128)(2,1)S(1)} %collective-permute-done.36.refs_2_, ...), custom_call_target="tpu_custom_call", output_to_operand_aliasing={{0}: (4, {}), {1}: (5, {})} | custom-call | bytes 3670016 | tf_op jit(solution)/shard_map/place/pallas_call | solution.py:348
  109.1 2.1 %collective-permute-done.34.refs_0_ = bf16[64,1792]{1,0:T(8,128)(2,1)S(1)} collective-permute-done((bf16[64,1792]{1,0:T(8,128)(2,1)S(1)}, bf16[64,1792]{1,0:T(8,128)(2,1)S(1)}, u32[]{:S(2)}, u32[]{:S(2)}) %collective-permute-start.34) | collective-permute-done | bytes 229408 | tf_op jit(solution)/shard_map/ppermute | solution.py:79
  111.2 3.9 %collective-permute-done.39.refs_1_ = bf16[64,1792]{1,0:T(8,128)(2,1)S(1)} collective-permute-done((bf16[64,1792]{1,0:T(8,128)(2,1)S(1)}, bf16[64,1792]{1,0:T(8,128)(2,1)S(1)}, u32[]{:S(2)}, u32[]{:S(2)}) %collective-permute-start.39) | collective-permute-done | bytes 229408 | tf_op jit(solution)/shard_map/ppermute | solution.py:79
  115.1 1.2 place.10
  (109 shorter events, 20.3 us)
Async XLA Ops:
  1.6 11.5 %collective-permute-start.2 = (s32[1,48]{1,0:T(1,128)S(1)}, s32[1,48]{1,0:T(1,128)S(1)}, u32[]{:S(2)}, u32[]{:S(2)}) collective-permute-start(s32[1,48]{1,0:T(1,128)S(1)} %pad_add_fusion.1), channel_id=1, source_target_pairs={{0,3},{1,2},{2,1},{3,0},{4,7},{5,6},{6,5},{7,4},{8,11},{9,10},{10,... | collective-permute-start | bytes 584 | tf_op jit(solution)/shard_map/ppermute | solution.py:37
  4.0 9.1 %collective-permute-start.1 = (s32[1,48]{1,0:T(1,128)S(1)}, s32[1,48]{1,0:T(1,128)S(1)}, u32[]{:S(2)}, u32[]{:S(2)}) collective-permute-start(s32[1,48]{1,0:T(1,128)S(1)} %pad_add_fusion.1), channel_id=1, source_target_pairs={{0,2},{1,3},{2,0},{3,1},{4,6},{5,7},{6,4},{7,5},{8,10},{9,11},{10,... | collective-permute-start | bytes 584 | tf_op jit(solution)/shard_map/ppermute | solution.py:37
  4.7 8.4 %collective-permute-start = (s32[1,48]{1,0:T(1,128)S(1)}, s32[1,48]{1,0:T(1,128)S(1)}, u32[]{:S(2)}, u32[]{:S(2)}) collective-permute-start(s32[1,48]{1,0:T(1,128)S(1)} %pad_add_fusion.1), channel_id=1, source_target_pairs={{0,1},{1,0},{2,3},{3,2},{4,5},{5,4},{6,7},{7,6},{8,9},{9,8},{10,11... | collective-permute-start | bytes 584 | tf_op jit(solution)/shard_map/ppermute | solution.py:37
  13.8 6.6 %collective-permute-start.7 = (s32[4,48]{1,0:T(4,128)S(1)}, s32[4,48]{1,0:T(4,128)S(1)}, u32[]{:S(2)}, u32[]{:S(2)}) collective-permute-start(s32[4,48]{1,0:T(4,128)S(1)} %pad_add_fusion.refs_0_), channel_id=1, source_target_pairs={{0,12},{1,13},{2,14},{3,15},{4,8},{5,9},{6,10},{7,11},{8,4},{9,5},... | collective-permute-start | bytes 2312 | tf_op jit(solution)/shard_map/ppermute | solution.py:37
  18.3 11.0 %collective-permute-start.10 = (bf16[32,1792]{1,0:T(8,128)(2,1)S(1)}, bf16[32,1792]{1,0:T(8,128)(2,1)S(1)}, u32[]{:S(2)}, u32[]{:S(2)}) collective-permute-start(bf16[32,1792]{1,0:T(8,128)(2,1)S(1)} %get-tuple-element.144), channel_id=1, source_target_pairs={{0,2},{1,3},{4,0},{5,1},{8,4},{9,5},{12,8},{13,9},{14,12},{15,13},... | collective-permute-start | bytes 344072 | tf_op jit(solution)/shard_map/ppermute | solution.py:79
  20.0 9.3 %collective-permute-start.9 = (bf16[32,1792]{1,0:T(8,128)(2,1)S(1)}, bf16[32,1792]{1,0:T(8,128)(2,1)S(1)}, u32[]{:S(2)}, u32[]{:S(2)}) collective-permute-start(bf16[32,1792]{1,0:T(8,128)(2,1)S(1)} %get-tuple-element.145), channel_id=1, source_target_pairs={{0,4},{1,5},{4,8},{5,9},{8,12},{9,13},{12,14},{13,15},{14,10},{15,... | collective-permute-start | bytes 344072 | tf_op jit(solution)/shard_map/ppermute | solution.py:79
  29.9 7.7 %collective-permute-start.14 = (bf16[32,3584]{1,0:T(8,128)(2,1)S(1)}, bf16[32,3584]{1,0:T(8,128)(2,1)S(1)}, u32[]{:S(2)}, u32[]{:S(2)}) collective-permute-start(bf16[32,3584]{1,0:T(8,128)(2,1)S(1)} %add_convert_fusion.12), channel_id=1, source_target_pairs={{0,4},{1,5},{4,8},{5,9},{8,12},{9,13},{12,14},{13,15},{14,10},{15,... | collective-permute-start | bytes 688136 | tf_op jit(solution)/shard_map/ppermute | solution.py:79
  30.0 9.0 %collective-permute-start.13 = (bf16[32,3584]{1,0:T(8,128)(2,1)S(1)}, bf16[32,3584]{1,0:T(8,128)(2,1)S(1)}, u32[]{:S(2)}, u32[]{:S(2)}) collective-permute-start(bf16[32,3584]{1,0:T(8,128)(2,1)S(1)} %add_convert_fusion.11), channel_id=1, source_target_pairs={{0,2},{1,3},{4,0},{5,1},{8,4},{9,5},{12,8},{13,9},{14,12},{15,13},... | collective-permute-start | bytes 688136 | tf_op jit(solution)/shard_map/ppermute | solution.py:79
  33.1 14.5 %collective-permute-start.18 = (bf16[32,1792]{1,0:T(8,128)(2,1)S(1)}, bf16[32,1792]{1,0:T(8,128)(2,1)S(1)}, u32[]{:S(2)}, u32[]{:S(2)}) collective-permute-start(bf16[32,1792]{1,0:T(8,128)(2,1)S(1)} %get-tuple-element.142), channel_id=1, source_target_pairs={{0,2},{1,3},{4,0},{5,1},{8,4},{9,5},{12,8},{13,9},{14,12},{15,13},... | collective-permute-start | bytes 344072 | tf_op jit(solution)/shard_map/ppermute | solution.py:79
  37.6 11.6 %collective-permute-start.17 = (bf16[32,3584]{1,0:T(8,128)(2,1)S(1)}, bf16[32,3584]{1,0:T(8,128)(2,1)S(1)}, u32[]{:S(2)}, u32[]{:S(2)}) collective-permute-start(bf16[32,3584]{1,0:T(8,128)(2,1)S(1)} %add_convert_fusion.9), channel_id=1, source_target_pairs={{0,4},{1,5},{4,8},{5,9},{8,12},{9,13},{12,14},{13,15},{14,10},{15,... | collective-permute-start | bytes 688136 | tf_op jit(solution)/shard_map/ppermute | solution.py:79
  39.0 7.9 %collective-permute-start.12 = (bf16[32,1792]{1,0:T(8,128)(2,1)S(1)}, bf16[32,1792]{1,0:T(8,128)(2,1)S(1)}, u32[]{:S(2)}, u32[]{:S(2)}) collective-permute-start(bf16[32,1792]{1,0:T(8,128)(2,1)S(1)} %get-tuple-element.143), channel_id=1, source_target_pairs={{0,4},{1,5},{4,8},{5,9},{8,12},{9,13},{12,14},{13,15},{14,10},{15,... | collective-permute-start | bytes 344072 | tf_op jit(solution)/shard_map/ppermute | solution.py:79
  41.2 8.7 %collective-permute-start.16 = (bf16[32,3584]{1,0:T(8,128)(2,1)S(1)}, bf16[32,3584]{1,0:T(8,128)(2,1)S(1)}, u32[]{:S(2)}, u32[]{:S(2)}) collective-permute-start(bf16[32,3584]{1,0:T(8,128)(2,1)S(1)} %add_convert_fusion.8), channel_id=1, source_target_pairs={{0,2},{1,3},{4,0},{5,1},{8,4},{9,5},{12,8},{13,9},{14,12},{15,13},... | collective-permute-start | bytes 688136 | tf_op jit(solution)/shard_map/ppermute | solution.py:79
  47.0 8.6 %collective-permute-start.15 = (bf16[32,3584]{1,0:T(8,128)(2,1)S(1)}, bf16[32,3584]{1,0:T(8,128)(2,1)S(1)}, u32[]{:S(2)}, u32[]{:S(2)}) collective-permute-start(bf16[32,3584]{1,0:T(8,128)(2,1)S(1)} %add_convert_fusion.7), channel_id=1, source_target_pairs={{0,4},{1,5},{4,8},{5,9},{8,12},{9,13},{12,14},{13,15},{14,10},{15,... | collective-permute-start | bytes 688136 | tf_op jit(solution)/shard_map/ppermute | solution.py:79
  47.7 8.6 %collective-permute-start.21 = (bf16[32,3584]{1,0:T(8,128)(2,1)S(1)}, bf16[32,3584]{1,0:T(8,128)(2,1)S(1)}, u32[]{:S(2)}, u32[]{:S(2)}) collective-permute-start(bf16[32,3584]{1,0:T(8,128)(2,1)S(1)} %add_convert_fusion.6), channel_id=1, source_target_pairs={{0,2},{1,3},{4,0},{5,1},{8,4},{9,5},{12,8},{13,9},{14,12},{15,13},... | collective-permute-start | bytes 688136 | tf_op jit(solution)/shard_map/ppermute | solution.py:79
  49.3 16.4 %collective-permute-start.24 = (bf16[32,3584]{1,0:T(8,128)(2,1)S(1)}, bf16[32,3584]{1,0:T(8,128)(2,1)S(1)}, u32[]{:S(2)}, u32[]{:S(2)}) collective-permute-start(bf16[32,3584]{1,0:T(8,128)(2,1)S(1)} %add_convert_fusion.5), channel_id=1, source_target_pairs={{0,4},{1,5},{4,8},{5,9},{8,12},{9,13},{12,14},{13,15},{14,10},{15,... | collective-permute-start | bytes 688136 | tf_op jit(solution)/shard_map/ppermute | solution.py:79
  50.0 15.6 %collective-permute-start.25 = (bf16[32,3584]{1,0:T(8,128)(2,1)S(1)}, bf16[32,3584]{1,0:T(8,128)(2,1)S(1)}, u32[]{:S(2)}, u32[]{:S(2)}) collective-permute-start(bf16[32,3584]{1,0:T(8,128)(2,1)S(1)} %add_convert_fusion.4), channel_id=1, source_target_pairs={{0,2},{1,3},{4,0},{5,1},{8,4},{9,5},{12,8},{13,9},{14,12},{15,13},... | collective-permute-start | bytes 688136 | tf_op jit(solution)/shard_map/ppermute | solution.py:79
  55.6 7.0 %collective-permute-start.19 = (bf16[32,3584]{1,0:T(8,128)(2,1)S(1)}, bf16[32,3584]{1,0:T(8,128)(2,1)S(1)}, u32[]{:S(2)}, u32[]{:S(2)}) collective-permute-start(bf16[32,3584]{1,0:T(8,128)(2,1)S(1)} %add_convert_fusion.3), channel_id=1, source_target_pairs={{0,4},{1,5},{4,8},{5,9},{8,12},{9,13},{12,14},{13,15},{14,10},{15,... | collective-permute-start | bytes 688136 | tf_op jit(solution)/shard_map/ppermute | solution.py:79
  56.4 7.1 %collective-permute-start.22 = (bf16[32,3584]{1,0:T(8,128)(2,1)S(1)}, bf16[32,3584]{1,0:T(8,128)(2,1)S(1)}, u32[]{:S(2)}, u32[]{:S(2)}) collective-permute-start(bf16[32,3584]{1,0:T(8,128)(2,1)S(1)} %add_convert_fusion.1), channel_id=1, source_target_pairs={{0,2},{1,3},{4,0},{5,1},{8,4},{9,5},{12,8},{13,9},{14,12},{15,13},... | collective-permute-start | bytes 688136 | tf_op jit(solution)/shard_map/ppermute | solution.py:79
  74.3 10.6 %collective-permute-start.26 = (bf16[64,3584]{1,0:T(8,128)(2,1)S(1)}, bf16[64,3584]{1,0:T(8,128)(2,1)S(1)}, u32[]{:S(2)}, u32[]{:S(2)}) collective-permute-start(bf16[64,3584]{1,0:T(8,128)(2,1)S(1)} %bitcast.4), channel_id=1, source_target_pairs={{0,4},{1,5},{4,8},{5,9},{8,12},{9,13},{12,14},{13,15},{14,10},{15,... | collective-permute-start | bytes 1376264 | tf_op jit(solution)/shard_map/ppermute | solution.py:79
  75.2 10.9 %collective-permute-start.28 = (bf16[64,3584]{1,0:T(8,128)(2,1)S(1)}, bf16[64,3584]{1,0:T(8,128)(2,1)S(1)}, u32[]{:S(2)}, u32[]{:S(2)}) collective-permute-start(bf16[64,3584]{1,0:T(8,128)(2,1)S(1)} %bitcast.5), channel_id=1, source_target_pairs={{0,2},{1,3},{4,0},{5,1},{8,4},{9,5},{12,8},{13,9},{14,12},{15,13},... | collective-permute-start | bytes 1376264 | tf_op jit(solution)/shard_map/ppermute | solution.py:79
  76.3 11.4 %collective-permute-start.29 = (bf16[64,3584]{1,0:T(8,128)(2,1)S(1)}, bf16[64,3584]{1,0:T(8,128)(2,1)S(1)}, u32[]{:S(2)}, u32[]{:S(2)}) collective-permute-start(bf16[64,3584]{1,0:T(8,128)(2,1)S(1)} %bitcast.6), channel_id=1, source_target_pairs={{0,1},{1,0},{2,3},{3,2},{4,5},{5,4},{6,7},{7,6},{8,9},{9,8},{10,11... | collective-permute-start | bytes 1376264 | tf_op jit(solution)/shard_map/ppermute | solution.py:37
  85.0 10.3 %collective-permute-start.27 = (bf16[64,3584]{1,0:T(8,128)(2,1)S(1)}, bf16[64,3584]{1,0:T(8,128)(2,1)S(1)}, u32[]{:S(2)}, u32[]{:S(2)}) collective-permute-start(bf16[64,3584]{1,0:T(8,128)(2,1)S(1)} %collective-permute-done.26.refs_0_), channel_id=1, source_target_pairs={{0,4},{1,5},{4,8},{5,9},{8,12},{9,13},{12,14},{13,15},{14,10},{15,... | collective-permute-start | bytes 1376264 | tf_op jit(solution)/shard_map/ppermute | solution.py:79
  86.1 10.7 %collective-permute-start.31 = (bf16[64,3584]{1,0:T(8,128)(2,1)S(1)}, bf16[64,3584]{1,0:T(8,128)(2,1)S(1)}, u32[]{:S(2)}, u32[]{:S(2)}) collective-permute-start(bf16[64,3584]{1,0:T(8,128)(2,1)S(1)} %collective-permute-done.28.refs_1_), channel_id=1, source_target_pairs={{0,2},{1,3},{4,0},{5,1},{8,4},{9,5},{12,8},{13,9},{14,12},{15,13},... | collective-permute-start | bytes 1376264 | tf_op jit(solution)/shard_map/ppermute | solution.py:79
  87.3 10.8 %collective-permute-start.33 = (bf16[64,3584]{1,0:T(8,128)(2,1)S(1)}, bf16[64,3584]{1,0:T(8,128)(2,1)S(1)}, u32[]{:S(2)}, u32[]{:S(2)}) collective-permute-start(bf16[64,3584]{1,0:T(8,128)(2,1)S(1)} %collective-permute-done.28.refs_1_), channel_id=1, source_target_pairs={{0,1},{1,0},{2,3},{3,2},{4,5},{5,4},{6,7},{7,6},{8,9},{9,8},{10,11... | collective-permute-start | bytes 1376264 | tf_op jit(solution)/shard_map/ppermute | solution.py:37
  87.3 11.4 %collective-permute-start.32 = (bf16[64,3584]{1,0:T(8,128)(2,1)S(1)}, bf16[64,3584]{1,0:T(8,128)(2,1)S(1)}, u32[]{:S(2)}, u32[]{:S(2)}) collective-permute-start(bf16[64,3584]{1,0:T(8,128)(2,1)S(1)} %collective-permute-done.26.refs_0_), channel_id=1, source_target_pairs={{0,1},{1,0},{2,3},{3,2},{4,5},{5,4},{6,7},{7,6},{8,9},{9,8},{10,11... | collective-permute-start | bytes 1376264 | tf_op jit(solution)/shard_map/ppermute | solution.py:37
  95.2 9.5 %collective-permute-start.30 = (bf16[64,3584]{1,0:T(8,128)(2,1)S(1)}, bf16[64,3584]{1,0:T(8,128)(2,1)S(1)}, u32[]{:S(2)}, u32[]{:S(2)}) collective-permute-start(bf16[64,3584]{1,0:T(8,128)(2,1)S(1)} %collective-permute-done.27.refs_0_), channel_id=1, source_target_pairs={{0,4},{1,5},{4,8},{5,9},{8,12},{9,13},{12,14},{13,15},{14,10},{15,... | collective-permute-start | bytes 1376264 | tf_op jit(solution)/shard_map/ppermute | solution.py:79
  96.8 10.1 %collective-permute-start.35 = (bf16[64,3584]{1,0:T(8,128)(2,1)S(1)}, bf16[64,3584]{1,0:T(8,128)(2,1)S(1)}, u32[]{:S(2)}, u32[]{:S(2)}) collective-permute-start(bf16[64,3584]{1,0:T(8,128)(2,1)S(1)} %collective-permute-done.31.refs_1_), channel_id=1, source_target_pairs={{0,2},{1,3},{4,0},{5,1},{8,4},{9,5},{12,8},{13,9},{14,12},{15,13},... | collective-permute-start | bytes 1376264 | tf_op jit(solution)/shard_map/ppermute | solution.py:79
  98.1 9.4 %collective-permute-start.37 = (bf16[64,3584]{1,0:T(8,128)(2,1)S(1)}, bf16[64,3584]{1,0:T(8,128)(2,1)S(1)}, u32[]{:S(2)}, u32[]{:S(2)}) collective-permute-start(bf16[64,3584]{1,0:T(8,128)(2,1)S(1)} %collective-permute-done.31.refs_1_), channel_id=1, source_target_pairs={{0,1},{1,0},{2,3},{3,2},{4,5},{5,4},{6,7},{7,6},{8,9},{9,8},{10,11... | collective-permute-start | bytes 1376264 | tf_op jit(solution)/shard_map/ppermute | solution.py:37
  98.1 9.7 %collective-permute-start.36 = (bf16[64,3584]{1,0:T(8,128)(2,1)S(1)}, bf16[64,3584]{1,0:T(8,128)(2,1)S(1)}, u32[]{:S(2)}, u32[]{:S(2)}) collective-permute-start(bf16[64,3584]{1,0:T(8,128)(2,1)S(1)} %collective-permute-done.27.refs_0_), channel_id=1, source_target_pairs={{0,1},{1,0},{2,3},{3,2},{4,5},{5,4},{6,7},{7,6},{8,9},{9,8},{10,11... | collective-permute-start | bytes 1376264 | tf_op jit(solution)/shard_map/ppermute | solution.py:37
  106.9 8.2 %collective-permute-start.42 = (bf16[64,3584]{1,0:T(8,128)(2,1)S(1)}, bf16[64,3584]{1,0:T(8,128)(2,1)S(1)}, u32[]{:S(2)}, u32[]{:S(2)}) collective-permute-start(bf16[64,3584]{1,0:T(8,128)(2,1)S(1)} %collective-permute-done.35.refs_1_), channel_id=1, source_target_pairs={{0,1},{1,0},{2,3},{3,2},{4,5},{5,4},{6,7},{7,6},{8,9},{9,8},{10,11... | collective-permute-start | bytes 1376264 | tf_op jit(solution)/shard_map/ppermute | solution.py:37
  107.0 8.1 %collective-permute-start.41 = (bf16[64,3584]{1,0:T(8,128)(2,1)S(1)}, bf16[64,3584]{1,0:T(8,128)(2,1)S(1)}, u32[]{:S(2)}, u32[]{:S(2)}) collective-permute-start(bf16[64,3584]{1,0:T(8,128)(2,1)S(1)} %collective-permute-done.30.refs_0_), channel_id=1, source_target_pairs={{0,1},{1,0},{2,3},{3,2},{4,5},{5,4},{6,7},{7,6},{8,9},{9,8},{10,11... | collective-permute-start | bytes 1376264 | tf_op jit(solution)/shard_map/ppermute | solution.py:37
  107.5 7.6 %collective-permute-start.39 = (bf16[64,1792]{1,0:T(8,128)(2,1)S(1)}, bf16[64,1792]{1,0:T(8,128)(2,1)S(1)}, u32[]{:S(2)}, u32[]{:S(2)}) collective-permute-start(bf16[64,1792]{1,0:T(8,128)(2,1)S(1)} %slice.135), channel_id=1, source_target_pairs={{0,2},{1,3},{4,0},{5,1},{8,4},{9,5},{12,8},{13,9},{14,12},{15,13},... | collective-permute-start | bytes 688136 | tf_op jit(solution)/shard_map/ppermute | solution.py:79
  (23 other events, 296.7 us)

commit v10 on v9

--- a/solution.py
+++ b/solution.py
@@ -91,7 +91,7 @@
     return stages
 
 
-def ordered_rows(size, rows, by_latent, by_slot):
+def ordered_rows(size, rows, by_latent, groups):
     chips = size // 2
     for block in range(size):
         group, inside = block // chips, block % chips
@@ -100,7 +100,7 @@
         offset = far if slot % 2 == 0 else 1 - far
         owner = owner_at(offset, 1 - inside // (chips // 2), size)
         begin = pl.multiple_of(owner * rows, rows)
-        by_slot[block * rows : (block + 1) * rows] = by_latent[pl.ds(begin, rows)]
+        groups[group][inside * rows : (inside + 1) * rows] = by_latent[pl.ds(begin, rows)]
 
 
 def row_codes(size, rows, table, picks_ref):
@@ -132,13 +132,6 @@
     is_latent = by_row(order) == (latent % rows).astype(jnp.float32)
     code = jnp.sum(jnp.where(is_latent, by_row(token), 0.0), axis=1, keepdims=True)
     return (code + jnp.where(code < 0, -0.5, 0.5)).astype(jnp.int32)
-
-
-def multiply(by_slot, right_ref, outs):
-    out = jnp.dot(by_slot[...], right_ref[...], preferred_element_type=jnp.float32)
-    part = outs[0].shape[0]
-    for i, ref in enumerate(outs):
-        ref[...] = out[i * part : (i + 1) * part].astype(ref.dtype)
 
 
 def stream_kernel(size, rows, coef_ref, right_hbm, *refs):
@@ -164,7 +157,10 @@
     for read in sum(reads, []):
         read.start()
     by_latent[...] = coef_ref[...].T
-    ordered_rows(size, rows, by_latent, by_slot)
+    far_rows = by_slot.shape[0] // 2
+    ordered_rows(
+        size, rows, by_latent, (by_slot.at[pl.ds(0, far_rows)], by_slot.at[pl.ds(far_rows, far_rows)])
+    )
     for i in range(pieces):
         for read in reads[i]:
             read.wait()
@@ -204,9 +200,16 @@
     )(coef, right)
 
 
-def select_kernel(size, rows, count, coef_ref, right_ref, picks_ref, *refs):
+def multiply(left_ref, right_ref, outs):
+    out = jnp.dot(left_ref[...], right_ref[...], preferred_element_type=jnp.float32)
+    part = outs[0].shape[0]
+    for i, ref in enumerate(outs):
+        ref[...] = out[i * part : (i + 1) * part].astype(ref.dtype)
+
+
+def select_far_kernel(size, rows, count, coef_ref, right_ref, picks_ref, *refs):
     pieces, refs = refs[:count], refs[count:]
-    outs, own_code, (by_latent, by_slot, table, codes) = refs[:4], refs[4], refs[5:]
+    outs, near_left, own_code, (by_latent, left, table, codes) = refs[:2], refs[2], refs[3], refs[4:]
 
     @pl.when(pl.program_id(0) == 0)
     def _():
@@ -220,40 +223,54 @@
         by_latent[...] = jnp.where(
             code == KEPT, coef_ref[...].T, (tokens == code).astype(by_latent.dtype)
         )
-        ordered_rows(size, rows, by_latent, by_slot)
-
-    multiply(by_slot, right_ref, outs)
-
-
-def select_product(coef, right, size, rows, picks, table):
+        ordered_rows(size, rows, by_latent, (left, near_left))
+
+    multiply(left, right_ref, outs)
+
+
+def near_kernel(left_ref, right_ref, *outs):
+    multiply(left_ref, right_ref, outs)
+
+
+def product(kernel, left, right, others, out_more, scratch, name):
+    tokens, width = right.shape
+    tile = 512
+    part = left.size // tokens // (4 if out_more else 2)
+    fixed = lambda j: (0, 0)
+    in_specs = [pl.BlockSpec(left.shape, fixed), pl.BlockSpec((tokens, tile), lambda j: (0, j))]
+    return pl.pallas_call(
+        kernel,
+        grid=(width // tile,),
+        in_specs=in_specs + [pl.BlockSpec(value.shape, fixed) for value in others],
+        out_specs=[pl.BlockSpec((part, tile), lambda j: (0, j))] * 2
+        + [pl.BlockSpec(value.shape, fixed) for value in out_more],
+        out_shape=[jax.ShapeDtypeStruct((part, width), left.dtype)] * 2 + list(out_more),
+        scratch_shapes=scratch,
+        compiler_params=params(20),
+        cost_estimate=cost(
+            4 * part * tokens * width, 2 * (tokens * width + 2 * part * (tokens + width))
+        ),
+        name=name,
+    )(left, right, *others)
+
+
+def far_product(coef, right, size, rows, picks, table):
     tokens, latents = coef.shape
-    width = right.shape[1]
-    tile = 512
-    part = latents // 4
-    fixed = lambda j: (0, 0)
-    operands = [coef, right, picks] + list(table)
-    in_specs = [pl.BlockSpec(value.shape, fixed) for value in operands]
-    in_specs[1] = pl.BlockSpec((tokens, tile), lambda j: (0, j))
-    return pl.pallas_call(
-        functools.partial(select_kernel, size, rows, len(table)),
-        grid=(width // tile,),
-        in_specs=in_specs,
-        out_specs=[pl.BlockSpec((part, tile), lambda j: (0, j))] * 4
-        + [pl.BlockSpec((rows, 1), fixed)],
-        out_shape=[jax.ShapeDtypeStruct((part, width), coef.dtype)] * 4
-        + [jax.ShapeDtypeStruct((rows, 1), jnp.int32)],
-        scratch_shapes=[
-            pltpu.VMEM((latents, tokens), coef.dtype),
-            pltpu.VMEM((latents, tokens), coef.dtype),
-            pltpu.VMEM((size, table[0].shape[1]), jnp.int32),
-            pltpu.VMEM((latents, 1), jnp.int32),
-        ],
-        compiler_params=params(24),
-        cost_estimate=cost(
-            2 * latents * tokens * width, 2 * (tokens * width + latents * (tokens + width))
-        ),
-        name="select_product",
-    )(*operands)
+    near_left = jax.ShapeDtypeStruct((latents // 2, tokens), coef.dtype)
+    code = jax.ShapeDtypeStruct((rows, 1), jnp.int32)
+    scratch = [
+        pltpu.VMEM((latents, tokens), coef.dtype),
+        pltpu.VMEM((latents // 2, tokens), coef.dtype),
+        pltpu.VMEM((size, table[0].shape[1]), jnp.int32),
+        pltpu.VMEM((latents, 1), jnp.int32),
+    ]
+    kernel = functools.partial(select_far_kernel, size, rows, len(table))
+    others = [picks] + list(table)
+    return product(kernel, coef, right, others, [near_left, code], scratch, "far_product")
+
+
+def near_product(left, right):
+    return product(near_kernel, left, right, [], [], [], "near_product")
 
 
 def term(kept, from_core, slot, rows):
@@ -409,34 +426,37 @@
         return [shift(moving[0], 1, size), shift(moving[1], -1, size)]
 
     def advance(came, kept, from_core, hop, order):
-        following = []
-        for side, value in enumerate(came):
-            value = after(value, order).astype(jnp.float32)
+        moving = []
+        for side, value in enumerate(after(came, order)):
+            value = value.astype(jnp.float32)
             if value.shape[1] < width:
                 pads = ((0, 0, 0), (0, half, 0) if side == 0 else (half, 0, 0))
                 value = lax.pad(value, jnp.float32(0), pads)
             value = value + term(kept, from_core, 2 * hop - side, rows)
-            order = value.astype(jnp.bfloat16)
-            following.append(shift(order, 1 - 2 * side, size))
-        return following, order
+            moving.append(value.astype(jnp.bfloat16))
+        return travel(moving), moving
 
     dec = stream_product(latent_act, out_grad, size, rows)
     dec_far = after(dec[0], *stages[0])
     dec_kept, dec_core = [dec[1], dec[3]], [swap(dec_far, 1, size), swap(after(dec[2], table[0]), 1, size)]
     dec_moving = begin(dec_kept, after(dec_core, table[0]))
-    *enc, code = select_product(
+    enc_sent, kept, enc_left, code = far_product(
         after(enc_coef, *dec_moving), x_rows, size, rows, pick_rows[0].T, table
     )
-    dec_came, enc_far = tied(travel(dec_moving), enc[0])
-    enc_kept, enc_core = [enc[1], enc[3]], [swap(enc_far, 1, size), swap(enc[2], 1, size)]
-    dec_came, order = advance(dec_came, dec_kept, dec_core, 1, enc[0])
+    dec_came, enc_sent = tied(travel(dec_moving), enc_sent)
+    enc_kept, enc_core = [kept], [swap(enc_sent, 1, size)]
+    dec_came, order = advance(dec_came, dec_kept, dec_core, 1, enc_sent)
     enc_moving = begin(enc_kept, after(enc_core, order))
-    enc_came, order = travel(enc_moving), enc_moving[1]
+    enc_sent, kept = near_product(after(enc_left, *enc_moving), x_rows)
+    enc_came, enc_sent = tied(travel(enc_moving), enc_sent)
+    enc_kept.append(kept)
+    enc_core.append(swap(enc_sent, 1, size))
+    order = enc_sent
     for hop in range(1, chips // 2):
         if hop + 1 < chips // 2:
             dec_came, order = advance(dec_came, dec_kept, dec_core, hop + 1, order)
         else:
-            dec_came, order = tied(dec_came, order)
+            order = (order, dec_came)
         enc_came, order = advance(enc_came, enc_kept, enc_core, hop, order)
     enc_out, enc_mo, enc_vo, enc_block, fresh = update(
         enc_kernel,

time: 118 us -> 118 us (level)
  starting transfers between devices: 36.4 us -> 34.6 us
  Pallas kernels: 25.3 us -> 27 us
    pallas_call x1 -> x2, Pallas kernels: 7.01 us -> 8.7 us  [product(): pl.pallas_call(kernel, grid=(width // tile,), in_specs=in_specs + [pl.Blo...]
    ppermute x24, starting transfers between devices: 26.1 us -> 24.9 us  [shift(): return lax.ppermute(value, 'latent', pairs)]
  transfers between devices with their start and end apart: 43 -> 43, of which waited for: 17 -> 16; matrix products, arithmetic and copies ran while one was open for 1% -> 1% of each run, Pallas kernels for 18% -> 19%
where the time goes in v10:
time: 118 us; the launch traced here: 117 us
  waiting for transfers between devices  52.6 us (45%)
  starting transfers between devices  34.6 us (29%)
  Pallas kernels  27 us (23%)
  other arithmetic  2.06 us (2%)
    ppermute x24, waiting for transfers between devices, shift(): return lax.ppermute(value, 'latent', pairs)  50.2 us
    ppermute x24, starting transfers between devices, shift(): return lax.ppermute(value, 'latent', pairs)  24.9 us
    ppermute x19, starting transfers between devices, swap(): return lax.ppermute(value, 'latent', [(i, i ^ bits) for i in range(size)])  9.76 us
    pallas_call x2, Pallas kernels, product(): pl.pallas_call(kernel, grid=(width // tile,), in_specs=in_specs + [pl.Blo...  8.7 us
    pallas_call x1, Pallas kernels, stream_product(): pl.pallas_call(functools.partial(stream_kernel, size, rows), in_specs=[pl...  8.36 us
    pallas_call x6, Pallas kernels, place(): pl.pallas_call(functools.partial(place_kernel, plan, size, rows, count),...  6.43 us
    pallas_call x2, Pallas kernels, update(): pl.pallas_call(kernel, grid=(rows // tile,), in_specs=[last_rows(value) f...  3.51 us
    ppermute x19, waiting for transfers between devices, swap(): return lax.ppermute(value, 'latent', [(i, i ^ bits) for i in range(size)])  2.37 us
  transfers between devices with their start and end apart: 43, of which 16 were waited for; matrix products, arithmetic and copies ran while one was open for 1% of the time, Pallas kernels for 19%

profile of v10, /device:TPU:0, one launch (start us, length us, event | category | flops | bytes accessed | tf_op | source)
XLA Modules:
  0.0 117.4 jit_solution(15059762142513951594)
XLA Ops:
  1.6 2.5 %collective-permute-start.2 = (s32[1,48]{1,0:T(1,128)S(1)}, s32[1,48]{1,0:T(1,128)S(1)}, u32[]{:S(2)}, u32[]{:S(2)}) collective-permute-start(s32[1,48]{1,0:T(1,128)S(1)} %pad_add_fusion.1), channel_id=1, source_target_pairs={{0,3},{1,2},{2,1},{3,0},{4,7},{5,6},{6,5},{7,4},{8,11},{9,10},{10,... | collective-permute-start | bytes 584 | tf_op jit(solution)/shard_map/ppermute | solution.py:37
  4.7 8.4 %product.1 = (bf16[128,3584]{1,0:T(8,128)(2,1)S(1)}, bf16[128,3584]{1,0:T(8,128)(2,1)S(1)}, bf16[128,3584]{1,0:T(8,128)(2,1)S(1)}, bf16[128,3584]{1,0:T(8,128)(2,1)S(1)}) custom-call(bf16[1024,512]{1,0:T(8,128)(2,1)} %coef_ref.1, bf16[1024,3584]{1,0:T(8,128)(2,1)} %right_hbm.1), custom_call_target="tpu_custom_call" | custom-call | flops 3758096384 | bytes 12058624 | tf_op jit(solution)/shard_map/product/pallas_call | solution.py:182
  13.8 3.8 %collective-permute-start.7 = (s32[4,48]{1,0:T(4,128)S(1)}, s32[4,48]{1,0:T(4,128)S(1)}, u32[]{:S(2)}, u32[]{:S(2)}) collective-permute-start(s32[4,48]{1,0:T(4,128)S(1)} %pad_add_fusion.refs_0_), channel_id=1, source_target_pairs={{0,12},{1,13},{2,14},{3,15},{4,8},{5,9},{6,10},{7,11},{8,4},{9,5},... | collective-permute-start | bytes 2312 | tf_op jit(solution)/shard_map/ppermute | solution.py:37
  18.3 1.8 %collective-permute-start.9 = (bf16[32,1792]{1,0:T(8,128)(2,1)S(1)}, bf16[32,1792]{1,0:T(8,128)(2,1)S(1)}, u32[]{:S(2)}, u32[]{:S(2)}) collective-permute-start(bf16[32,1792]{1,0:T(8,128)(2,1)S(1)} %get-tuple-element.162), channel_id=1, source_target_pairs={{0,2},{1,3},{4,0},{5,1},{8,4},{9,5},{12,8},{13,9},{14,12},{15,13},... | collective-permute-start | bytes 344072 | tf_op jit(solution)/shard_map/ppermute | solution.py:79
  20.3 1.8 %collective-permute-done.6.refs_2_ = s32[4,48]{1,0:T(4,128)S(1)} collective-permute-done((s32[4,48]{1,0:T(4,128)S(1)}, s32[4,48]{1,0:T(4,128)S(1)}, u32[]{:S(2)}, u32[]{:S(2)}) %collective-permute-start.6) | collective-permute-done | bytes 800 | tf_op jit(solution)/shard_map/ppermute | solution.py:37
  22.2 4.9 %far_product.1 = (bf16[128,3584]{1,0:T(8,128)(2,1)S(1)}, bf16[128,3584]{1,0:T(8,128)(2,1)S(1)}, bf16[256,1024]{1,0:T(8,128)(2,1)S(1)}, s32[32,1]{1,0:T(8,128)S(1)}) custom-call(bf16[1024,512]{1,0:T(8,128)(2,1)S(1)} %copy-done, bf16[1024,3584]{1,0:T(8,128)(2,1)S(1)} %bitcast.5, s32[2,16]{1,0:T(2,128)S(1)} %bitcast.10, s32[4,48]{1,0:T(4,128)S(1)} %pad_add_fusion.refs_0_, ...), custom_call_target="tpu_custom_call" | custom-call | flops 1879048192 | bytes 9699328 | tf_op jit(solution)/shard_map/far_product/pallas_call | solution.py:241
  27.4 1.6 %collective-permute-start.15 = (bf16[32,3584]{1,0:T(8,128)(2,1)S(1)}, bf16[32,3584]{1,0:T(8,128)(2,1)S(1)}, u32[]{:S(2)}, u32[]{:S(2)}) collective-permute-start(bf16[32,3584]{1,0:T(8,128)(2,1)S(1)} %get-tuple-element.158), channel_id=1, source_target_pairs={{0,2},{1,3},{4,0},{5,1},{8,4},{9,5},{12,8},{13,9},{14,12},{15,13},... | collective-permute-start | bytes 688136 | tf_op jit(solution)/shard_map/ppermute | solution.py:79
  29.8 1.6 %collective-permute-start.12 = (bf16[32,1792]{1,0:T(8,128)(2,1)S(1)}, bf16[32,1792]{1,0:T(8,128)(2,1)S(1)}, u32[]{:S(2)}, u32[]{:S(2)}) collective-permute-start(bf16[32,1792]{1,0:T(8,128)(2,1)S(1)} %get-tuple-element.160), channel_id=1, source_target_pairs={{0,2},{1,3},{4,0},{5,1},{8,4},{9,5},{12,8},{13,9},{14,12},{15,13},... | collective-permute-start | bytes 344072 | tf_op jit(solution)/shard_map/ppermute | solution.py:79
  31.9 3.8 %near_product.1 = (bf16[128,3584]{1,0:T(8,128)(2,1)S(1)}, bf16[128,3584]{1,0:T(8,128)(2,1)S(1)}) custom-call(bf16[256,1024]{1,0:T(8,128)(2,1)S(1)} %get-tuple-element.98.left_ref, bf16[1024,3584]{1,0:T(8,128)(2,1)S(1)} %bitcast.5), custom_call_target="tpu_custom_call" | custom-call | flops 1879048192 | bytes 9699328 | tf_op jit(solution)/shard_map/near_product/pallas_call | solution.py:241
  35.6 2.3 %collective-permute-done.12 = bf16[32,1792]{1,0:T(8,128)(2,1)S(1)} collective-permute-done((bf16[32,1792]{1,0:T(8,128)(2,1)S(1)}, bf16[32,1792]{1,0:T(8,128)(2,1)S(1)}, u32[]{:S(2)}, u32[]{:S(2)}) %collective-permute-start.12) | collective-permute-done | bytes 114720 | tf_op jit(solution)/shard_map/ppermute | solution.py:79
  39.9 1.6 %collective-permute-start.19 = (bf16[32,3584]{1,0:T(8,128)(2,1)S(1)}, bf16[32,3584]{1,0:T(8,128)(2,1)S(1)}, u32[]{:S(2)}, u32[]{:S(2)}) collective-permute-start(bf16[32,3584]{1,0:T(8,128)(2,1)S(1)} %add_convert_fusion.8), channel_id=1, source_target_pairs={{0,2},{1,3},{4,0},{5,1},{8,4},{9,5},{12,8},{13,9},{14,12},{15,13},... | collective-permute-start | bytes 688136 | tf_op jit(solution)/shard_map/ppermute | solution.py:79
  42.4 1.3 %collective-permute-start.16 = (bf16[32,3584]{1,0:T(8,128)(2,1)S(1)}, bf16[32,3584]{1,0:T(8,128)(2,1)S(1)}, u32[]{:S(2)}, u32[]{:S(2)}) collective-permute-start(bf16[32,3584]{1,0:T(8,128)(2,1)S(1)} %get-tuple-element.157), channel_id=1, source_target_pairs={{0,4},{1,5},{4,8},{5,9},{8,12},{9,13},{12,14},{13,15},{14,10},{15,... | collective-permute-start | bytes 688136 | tf_op jit(solution)/shard_map/ppermute | solution.py:79
  43.7 4.0 %collective-permute-done.18 = bf16[32,3584]{1,0:T(8,128)(2,1)S(1)} collective-permute-done((bf16[32,3584]{1,0:T(8,128)(2,1)S(1)}, bf16[32,3584]{1,0:T(8,128)(2,1)S(1)}, u32[]{:S(2)}, u32[]{:S(2)}) %collective-permute-start.18) | collective-permute-done | bytes 229408 | tf_op jit(solution)/shard_map/ppermute | solution.py:79
  48.6 1.6 %collective-permute-start.23 = (bf16[32,3584]{1,0:T(8,128)(2,1)S(1)}, bf16[32,3584]{1,0:T(8,128)(2,1)S(1)}, u32[]{:S(2)}, u32[]{:S(2)}) collective-permute-start(bf16[32,3584]{1,0:T(8,128)(2,1)S(1)} %get-tuple-element.154), channel_id=1, source_target_pairs={{0,2},{1,3},{4,0},{5,1},{8,4},{9,5},{12,8},{13,9},{14,12},{15,13},... | collective-permute-start | bytes 688136 | tf_op jit(solution)/shard_map/ppermute | solution.py:79
  50.7 2.7 %collective-permute-done.17 = bf16[32,3584]{1,0:T(8,128)(2,1)S(1)} collective-permute-done((bf16[32,3584]{1,0:T(8,128)(2,1)S(1)}, bf16[32,3584]{1,0:T(8,128)(2,1)S(1)}, u32[]{:S(2)}, u32[]{:S(2)}) %collective-permute-start.17) | collective-permute-done | bytes 229408 | tf_op jit(solution)/shard_map/ppermute | solution.py:79
  53.4 1.6 %collective-permute-start.21 = (bf16[32,3584]{1,0:T(8,128)(2,1)S(1)}, bf16[32,3584]{1,0:T(8,128)(2,1)S(1)}, u32[]{:S(2)}, u32[]{:S(2)}) collective-permute-start(bf16[32,3584]{1,0:T(8,128)(2,1)S(1)} %add_convert_fusion.2), channel_id=1, source_target_pairs={{0,2},{1,3},{4,0},{5,1},{8,4},{9,5},{12,8},{13,9},{14,12},{15,13},... | collective-permute-start | bytes 688136 | tf_op jit(solution)/shard_map/ppermute | solution.py:79
  55.7 6.8 %collective-permute-done.21 = bf16[32,3584]{1,0:T(8,128)(2,1)S(1)} collective-permute-done((bf16[32,3584]{1,0:T(8,128)(2,1)S(1)}, bf16[32,3584]{1,0:T(8,128)(2,1)S(1)}, u32[]{:S(2)}, u32[]{:S(2)}) %collective-permute-start.21) | collective-permute-done | bytes 229408 | tf_op jit(solution)/shard_map/ppermute | solution.py:79
  62.6 1.6 %collective-permute-start.25 = (bf16[32,3584]{1,0:T(8,128)(2,1)S(1)}, bf16[32,3584]{1,0:T(8,128)(2,1)S(1)}, u32[]{:S(2)}, u32[]{:S(2)}) collective-permute-start(bf16[32,3584]{1,0:T(8,128)(2,1)S(1)} %get-tuple-element.152), channel_id=1, source_target_pairs={{0,2},{1,3},{4,0},{5,1},{8,4},{9,5},{12,8},{13,9},{14,12},{15,13},... | collective-permute-start | bytes 688136 | tf_op jit(solution)/shard_map/ppermute | solution.py:79
  64.7 4.9 %collective-permute-done.25.refs_3_ = bf16[32,3584]{1,0:T(8,128)(2,1)S(1)} collective-permute-done((bf16[32,3584]{1,0:T(8,128)(2,1)S(1)}, bf16[32,3584]{1,0:T(8,128)(2,1)S(1)}, u32[]{:S(2)}, u32[]{:S(2)}) %collective-permute-start.25) | collective-permute-done | bytes 229408 | tf_op jit(solution)/shard_map/ppermute | solution.py:79
  70.9 1.8 %enc_update.1 = (f32[32,3584]{1,0:T(8,128)}, f32[32,3584]{1,0:T(8,128)}, f32[32,3584]{1,0:T(8,128)}, bf16[32,3584]{1,0:T(8,128)(2,1)S(1)}, bf16[32,3584]{1,0:T(8,128)(2,1)S(1)}) custom-call(s32[32,1]{1,0:T(8,128)S(1)} %get-tuple-element.88.code_ref, f32[32,3584]{1,0:T(8,128)S(1)} %copy-done.1, f32[32,3584]{1,0:T(8,128)S(1)} %copy-done.2, ...), custom_call_target="tpu_custom_call" | custom-call | flops 4587520 | bytes 4587520 | tf_op jit(solution)/shard_map/enc_update/pallas_call | solution.py:330
  72.6 1.8 %dec_update.1 = (f32[32,3584]{1,0:T(8,128)}, f32[32,3584]{1,0:T(8,128)}, f32[32,3584]{1,0:T(8,128)}, bf16[2,32,3584]{2,1,0:T(8,128)(2,1)S(1)}) custom-call(s32[32,1]{1,0:T(8,128)S(1)} %get-tuple-element.88.code_ref, f32[32,3584]{1,0:T(8,128)S(1)} %copy-done.4, f32[32,3584]{1,0:T(8,128)S(1)} %copy-done.5, f32[32,3584]{1,0:T(8,128)S(1)} %copy-done.6, ...), custom_call_target="tpu_custom_call" | custom-call | flops 4587520 | bytes 4587520 | tf_op jit(solution)/shard_map/dec_update/pallas_call | solution.py:330
  74.9 1.5 %collective-permute-start.28 = (bf16[64,3584]{1,0:T(8,128)(2,1)S(1)}, bf16[64,3584]{1,0:T(8,128)(2,1)S(1)}, u32[]{:S(2)}, u32[]{:S(2)}) collective-permute-start(bf16[64,3584]{1,0:T(8,128)(2,1)S(1)} %bitcast.7), channel_id=1, source_target_pairs={{0,2},{1,3},{4,0},{5,1},{8,4},{9,5},{12,8},{13,9},{14,12},{15,13},... | collective-permute-start | bytes 1376264 | tf_op jit(solution)/shard_map/ppermute | solution.py:79
  77.2 7.9 %collective-permute-done.26.refs_0_ = bf16[64,3584]{1,0:T(8,128)(2,1)S(1)} collective-permute-done((bf16[64,3584]{1,0:T(8,128)(2,1)S(1)}, bf16[64,3584]{1,0:T(8,128)(2,1)S(1)}, u32[]{:S(2)}, u32[]{:S(2)}) %collective-permute-start.26) | collective-permute-done | bytes 458784 | tf_op jit(solution)/shard_map/ppermute | solution.py:79
  85.6 1.5 %collective-permute-start.31 = (bf16[64,3584]{1,0:T(8,128)(2,1)S(1)}, bf16[64,3584]{1,0:T(8,128)(2,1)S(1)}, u32[]{:S(2)}, u32[]{:S(2)}) collective-permute-start(bf16[64,3584]{1,0:T(8,128)(2,1)S(1)} %collective-permute-done.28.refs_1_), channel_id=1, source_target_pairs={{0,2},{1,3},{4,0},{5,1},{8,4},{9,5},{12,8},{13,9},{14,12},{15,13},... | collective-permute-start | bytes 1376264 | tf_op jit(solution)/shard_map/ppermute | solution.py:79
  88.7 7.0 %collective-permute-done.27.refs_0_ = bf16[64,3584]{1,0:T(8,128)(2,1)S(1)} collective-permute-done((bf16[64,3584]{1,0:T(8,128)(2,1)S(1)}, bf16[64,3584]{1,0:T(8,128)(2,1)S(1)}, u32[]{:S(2)}, u32[]{:S(2)}) %collective-permute-start.27) | collective-permute-done | bytes 458784 | tf_op jit(solution)/shard_map/ppermute | solution.py:79
  96.3 1.5 %collective-permute-start.35 = (bf16[64,3584]{1,0:T(8,128)(2,1)S(1)}, bf16[64,3584]{1,0:T(8,128)(2,1)S(1)}, u32[]{:S(2)}, u32[]{:S(2)}) collective-permute-start(bf16[64,3584]{1,0:T(8,128)(2,1)S(1)} %collective-permute-done.31.refs_1_), channel_id=1, source_target_pairs={{0,2},{1,3},{4,0},{5,1},{8,4},{9,5},{12,8},{13,9},{14,12},{15,13},... | collective-permute-start | bytes 1376264 | tf_op jit(solution)/shard_map/ppermute | solution.py:79
  98.3 1.3 %place.8 = (bf16[512,3584]{1,0:T(8,128)(2,1)}, bf16[512,3584]{1,0:T(8,128)(2,1)}) custom-call(bf16[64,3584]{1,0:T(8,128)(2,1)S(1)} %collective-permute-done.27.refs_0_, bf16[64,3584]{1,0:T(8,128)(2,1)S(1)} %collective-permute-done.31.refs_1_, bf16[64,3584]{1,0:T(8,128)(2,1)S(1)} %collective-permute-done.32.refs_2_, ...), custom_call_target="tpu_custom_call", output_to_operand_aliasing={{0}: (4, {}), {1}: (5, {})} | custom-call | bytes 3670016 | tf_op jit(solution)/shard_map/place/pallas_call | solution.py:365
  99.6 6.8 %collective-permute-done.30.refs_0_ = bf16[64,3584]{1,0:T(8,128)(2,1)S(1)} collective-permute-done((bf16[64,3584]{1,0:T(8,128)(2,1)S(1)}, bf16[64,3584]{1,0:T(8,128)(2,1)S(1)}, u32[]{:S(2)}, u32[]{:S(2)}) %collective-permute-start.30) | collective-permute-done | bytes 458784 | tf_op jit(solution)/shard_map/ppermute | solution.py:79
  107.6 1.5 %collective-permute-start.39 = (bf16[64,1792]{1,0:T(8,128)(2,1)S(1)}, bf16[64,1792]{1,0:T(8,128)(2,1)S(1)}, u32[]{:S(2)}, u32[]{:S(2)}) collective-permute-start(bf16[64,1792]{1,0:T(8,128)(2,1)S(1)} %slice.135), channel_id=1, source_target_pairs={{0,2},{1,3},{4,0},{5,1},{8,4},{9,5},{12,8},{13,9},{14,12},{15,13},... | collective-permute-start | bytes 688136 | tf_op jit(solution)/shard_map/ppermute | solution.py:79
  109.1 1.3 %place.9 = (bf16[512,3584]{1,0:T(8,128)(2,1)}, bf16[512,3584]{1,0:T(8,128)(2,1)}) custom-call(bf16[64,3584]{1,0:T(8,128)(2,1)S(1)} %collective-permute-done.30.refs_0_, bf16[64,3584]{1,0:T(8,128)(2,1)S(1)} %collective-permute-done.35.refs_1_, bf16[64,3584]{1,0:T(8,128)(2,1)S(1)} %collective-permute-done.36.refs_2_, ...), custom_call_target="tpu_custom_call", output_to_operand_aliasing={{0}: (4, {}), {1}: (5, {})} | custom-call | bytes 3670016 | tf_op jit(solution)/shard_map/place/pallas_call | solution.py:365
  110.4 2.1 %collective-permute-done.34.refs_0_ = bf16[64,1792]{1,0:T(8,128)(2,1)S(1)} collective-permute-done((bf16[64,1792]{1,0:T(8,128)(2,1)S(1)}, bf16[64,1792]{1,0:T(8,128)(2,1)S(1)}, u32[]{:S(2)}, u32[]{:S(2)}) %collective-permute-start.34) | collective-permute-done | bytes 229408 | tf_op jit(solution)/shard_map/ppermute | solution.py:79
  112.5 2.7 %collective-permute-done.39.refs_1_ = bf16[64,1792]{1,0:T(8,128)(2,1)S(1)} collective-permute-done((bf16[64,1792]{1,0:T(8,128)(2,1)S(1)}, bf16[64,1792]{1,0:T(8,128)(2,1)S(1)}, u32[]{:S(2)}, u32[]{:S(2)}) %collective-permute-start.39) | collective-permute-done | bytes 229408 | tf_op jit(solution)/shard_map/ppermute | solution.py:79
  (106 shorter events, 19.7 us)
Async XLA Ops:
  1.6 11.5 %collective-permute-start.2 = (s32[1,48]{1,0:T(1,128)S(1)}, s32[1,48]{1,0:T(1,128)S(1)}, u32[]{:S(2)}, u32[]{:S(2)}) collective-permute-start(s32[1,48]{1,0:T(1,128)S(1)} %pad_add_fusion.1), channel_id=1, source_target_pairs={{0,3},{1,2},{2,1},{3,0},{4,7},{5,6},{6,5},{7,4},{8,11},{9,10},{10,... | collective-permute-start | bytes 584 | tf_op jit(solution)/shard_map/ppermute | solution.py:37
  4.0 9.1 %collective-permute-start.1 = (s32[1,48]{1,0:T(1,128)S(1)}, s32[1,48]{1,0:T(1,128)S(1)}, u32[]{:S(2)}, u32[]{:S(2)}) collective-permute-start(s32[1,48]{1,0:T(1,128)S(1)} %pad_add_fusion.1), channel_id=1, source_target_pairs={{0,2},{1,3},{2,0},{3,1},{4,6},{5,7},{6,4},{7,5},{8,10},{9,11},{10,... | collective-permute-start | bytes 584 | tf_op jit(solution)/shard_map/ppermute | solution.py:37
  4.7 8.4 %collective-permute-start = (s32[1,48]{1,0:T(1,128)S(1)}, s32[1,48]{1,0:T(1,128)S(1)}, u32[]{:S(2)}, u32[]{:S(2)}) collective-permute-start(s32[1,48]{1,0:T(1,128)S(1)} %pad_add_fusion.1), channel_id=1, source_target_pairs={{0,1},{1,0},{2,3},{3,2},{4,5},{5,4},{6,7},{7,6},{8,9},{9,8},{10,11... | collective-permute-start | bytes 584 | tf_op jit(solution)/shard_map/ppermute | solution.py:37
  18.3 8.9 %collective-permute-start.9 = (bf16[32,1792]{1,0:T(8,128)(2,1)S(1)}, bf16[32,1792]{1,0:T(8,128)(2,1)S(1)}, u32[]{:S(2)}, u32[]{:S(2)}) collective-permute-start(bf16[32,1792]{1,0:T(8,128)(2,1)S(1)} %get-tuple-element.162), channel_id=1, source_target_pairs={{0,2},{1,3},{4,0},{5,1},{8,4},{9,5},{12,8},{13,9},{14,12},{15,13},... | collective-permute-start | bytes 344072 | tf_op jit(solution)/shard_map/ppermute | solution.py:79
  20.0 7.1 %collective-permute-start.8 = (bf16[32,1792]{1,0:T(8,128)(2,1)S(1)}, bf16[32,1792]{1,0:T(8,128)(2,1)S(1)}, u32[]{:S(2)}, u32[]{:S(2)}) collective-permute-start(bf16[32,1792]{1,0:T(8,128)(2,1)S(1)} %get-tuple-element.163), channel_id=1, source_target_pairs={{0,4},{1,5},{4,8},{5,9},{8,12},{9,13},{12,14},{13,15},{14,10},{15,... | collective-permute-start | bytes 344072 | tf_op jit(solution)/shard_map/ppermute | solution.py:79
  27.4 11.8 %collective-permute-start.15 = (bf16[32,3584]{1,0:T(8,128)(2,1)S(1)}, bf16[32,3584]{1,0:T(8,128)(2,1)S(1)}, u32[]{:S(2)}, u32[]{:S(2)}) collective-permute-start(bf16[32,3584]{1,0:T(8,128)(2,1)S(1)} %get-tuple-element.158), channel_id=1, source_target_pairs={{0,2},{1,3},{4,0},{5,1},{8,4},{9,5},{12,8},{13,9},{14,12},{15,13},... | collective-permute-start | bytes 688136 | tf_op jit(solution)/shard_map/ppermute | solution.py:79
  28.9 10.2 %collective-permute-start.14 = (bf16[32,3584]{1,0:T(8,128)(2,1)S(1)}, bf16[32,3584]{1,0:T(8,128)(2,1)S(1)}, u32[]{:S(2)}, u32[]{:S(2)}) collective-permute-start(bf16[32,3584]{1,0:T(8,128)(2,1)S(1)} %get-tuple-element.159), channel_id=1, source_target_pairs={{0,4},{1,5},{4,8},{5,9},{8,12},{9,13},{12,14},{13,15},{14,10},{15,... | collective-permute-start | bytes 688136 | tf_op jit(solution)/shard_map/ppermute | solution.py:79
  29.8 8.1 %collective-permute-start.12 = (bf16[32,1792]{1,0:T(8,128)(2,1)S(1)}, bf16[32,1792]{1,0:T(8,128)(2,1)S(1)}, u32[]{:S(2)}, u32[]{:S(2)}) collective-permute-start(bf16[32,1792]{1,0:T(8,128)(2,1)S(1)} %get-tuple-element.160), channel_id=1, source_target_pairs={{0,2},{1,3},{4,0},{5,1},{8,4},{9,5},{12,8},{13,9},{14,12},{15,13},... | collective-permute-start | bytes 344072 | tf_op jit(solution)/shard_map/ppermute | solution.py:79
  31.3 7.8 %collective-permute-start.11 = (bf16[32,1792]{1,0:T(8,128)(2,1)S(1)}, bf16[32,1792]{1,0:T(8,128)(2,1)S(1)}, u32[]{:S(2)}, u32[]{:S(2)}) collective-permute-start(bf16[32,1792]{1,0:T(8,128)(2,1)S(1)} %get-tuple-element.161), channel_id=1, source_target_pairs={{0,4},{1,5},{4,8},{5,9},{8,12},{9,13},{12,14},{13,15},{14,10},{15,... | collective-permute-start | bytes 344072 | tf_op jit(solution)/shard_map/ppermute | solution.py:79
  39.1 15.9 %collective-permute-start.13 = (bf16[128,3584]{1,0:T(8,128)(2,1)S(1)}, bf16[128,3584]{1,0:T(8,128)(2,1)S(1)}, u32[]{:S(2)}, u32[]{:S(2)}) collective-permute-start(bf16[128,3584]{1,0:T(8,128)(2,1)S(1)} %get-tuple-element.101), channel_id=1, source_target_pairs={{0,1},{1,0},{2,3},{3,2},{4,5},{5,4},{6,7},{7,6},{8,9},{9,8},{10,11... | collective-permute-start | bytes 2752520 | tf_op jit(solution)/shard_map/ppermute | solution.py:37
  39.2 8.5 %collective-permute-start.18 = (bf16[32,3584]{1,0:T(8,128)(2,1)S(1)}, bf16[32,3584]{1,0:T(8,128)(2,1)S(1)}, u32[]{:S(2)}, u32[]{:S(2)}) collective-permute-start(bf16[32,3584]{1,0:T(8,128)(2,1)S(1)} %add_convert_fusion.9), channel_id=1, source_target_pairs={{0,4},{1,5},{4,8},{5,9},{8,12},{9,13},{12,14},{13,15},{14,10},{15,... | collective-permute-start | bytes 688136 | tf_op jit(solution)/shard_map/ppermute | solution.py:79
  39.9 8.5 %collective-permute-start.19 = (bf16[32,3584]{1,0:T(8,128)(2,1)S(1)}, bf16[32,3584]{1,0:T(8,128)(2,1)S(1)}, u32[]{:S(2)}, u32[]{:S(2)}) collective-permute-start(bf16[32,3584]{1,0:T(8,128)(2,1)S(1)} %add_convert_fusion.8), channel_id=1, source_target_pairs={{0,2},{1,3},{4,0},{5,1},{8,4},{9,5},{12,8},{13,9},{14,12},{15,13},... | collective-permute-start | bytes 688136 | tf_op jit(solution)/shard_map/ppermute | solution.py:79
  41.6 11.7 %collective-permute-start.17 = (bf16[32,3584]{1,0:T(8,128)(2,1)S(1)}, bf16[32,3584]{1,0:T(8,128)(2,1)S(1)}, u32[]{:S(2)}, u32[]{:S(2)}) collective-permute-start(bf16[32,3584]{1,0:T(8,128)(2,1)S(1)} %get-tuple-element.156), channel_id=1, source_target_pairs={{0,2},{1,3},{4,0},{5,1},{8,4},{9,5},{12,8},{13,9},{14,12},{15,13},... | collective-permute-start | bytes 688136 | tf_op jit(solution)/shard_map/ppermute | solution.py:79
  42.4 10.9 %collective-permute-start.16 = (bf16[32,3584]{1,0:T(8,128)(2,1)S(1)}, bf16[32,3584]{1,0:T(8,128)(2,1)S(1)}, u32[]{:S(2)}, u32[]{:S(2)}) collective-permute-start(bf16[32,3584]{1,0:T(8,128)(2,1)S(1)} %get-tuple-element.157), channel_id=1, source_target_pairs={{0,4},{1,5},{4,8},{5,9},{8,12},{9,13},{12,14},{13,15},{14,10},{15,... | collective-permute-start | bytes 688136 | tf_op jit(solution)/shard_map/ppermute | solution.py:79
  48.6 13.9 %collective-permute-start.23 = (bf16[32,3584]{1,0:T(8,128)(2,1)S(1)}, bf16[32,3584]{1,0:T(8,128)(2,1)S(1)}, u32[]{:S(2)}, u32[]{:S(2)}) collective-permute-start(bf16[32,3584]{1,0:T(8,128)(2,1)S(1)} %get-tuple-element.154), channel_id=1, source_target_pairs={{0,2},{1,3},{4,0},{5,1},{8,4},{9,5},{12,8},{13,9},{14,12},{15,13},... | collective-permute-start | bytes 688136 | tf_op jit(solution)/shard_map/ppermute | solution.py:79
  50.2 12.3 %collective-permute-start.22 = (bf16[32,3584]{1,0:T(8,128)(2,1)S(1)}, bf16[32,3584]{1,0:T(8,128)(2,1)S(1)}, u32[]{:S(2)}, u32[]{:S(2)}) collective-permute-start(bf16[32,3584]{1,0:T(8,128)(2,1)S(1)} %get-tuple-element.155), channel_id=1, source_target_pairs={{0,4},{1,5},{4,8},{5,9},{8,12},{9,13},{12,14},{13,15},{14,10},{15,... | collective-permute-start | bytes 688136 | tf_op jit(solution)/shard_map/ppermute | solution.py:79
  53.4 9.0 %collective-permute-start.21 = (bf16[32,3584]{1,0:T(8,128)(2,1)S(1)}, bf16[32,3584]{1,0:T(8,128)(2,1)S(1)}, u32[]{:S(2)}, u32[]{:S(2)}) collective-permute-start(bf16[32,3584]{1,0:T(8,128)(2,1)S(1)} %add_convert_fusion.2), channel_id=1, source_target_pairs={{0,2},{1,3},{4,0},{5,1},{8,4},{9,5},{12,8},{13,9},{14,12},{15,13},... | collective-permute-start | bytes 688136 | tf_op jit(solution)/shard_map/ppermute | solution.py:79
  55.1 7.4 %collective-permute-start.20 = (bf16[32,3584]{1,0:T(8,128)(2,1)S(1)}, bf16[32,3584]{1,0:T(8,128)(2,1)S(1)}, u32[]{:S(2)}, u32[]{:S(2)}) collective-permute-start(bf16[32,3584]{1,0:T(8,128)(2,1)S(1)} %add_convert_fusion.3), channel_id=1, source_target_pairs={{0,4},{1,5},{4,8},{5,9},{8,12},{9,13},{12,14},{13,15},{14,10},{15,... | collective-permute-start | bytes 688136 | tf_op jit(solution)/shard_map/ppermute | solution.py:79
  74.4 10.7 %collective-permute-start.26 = (bf16[64,3584]{1,0:T(8,128)(2,1)S(1)}, bf16[64,3584]{1,0:T(8,128)(2,1)S(1)}, u32[]{:S(2)}, u32[]{:S(2)}) collective-permute-start(bf16[64,3584]{1,0:T(8,128)(2,1)S(1)} %bitcast.6), channel_id=1, source_target_pairs={{0,4},{1,5},{4,8},{5,9},{8,12},{9,13},{12,14},{13,15},{14,10},{15,... | collective-permute-start | bytes 1376264 | tf_op jit(solution)/shard_map/ppermute | solution.py:79
  74.9 10.7 %collective-permute-start.28 = (bf16[64,3584]{1,0:T(8,128)(2,1)S(1)}, bf16[64,3584]{1,0:T(8,128)(2,1)S(1)}, u32[]{:S(2)}, u32[]{:S(2)}) collective-permute-start(bf16[64,3584]{1,0:T(8,128)(2,1)S(1)} %bitcast.7), channel_id=1, source_target_pairs={{0,2},{1,3},{4,0},{5,1},{8,4},{9,5},{12,8},{13,9},{14,12},{15,13},... | collective-permute-start | bytes 1376264 | tf_op jit(solution)/shard_map/ppermute | solution.py:79
  76.4 11.2 %collective-permute-start.29 = (bf16[64,3584]{1,0:T(8,128)(2,1)S(1)}, bf16[64,3584]{1,0:T(8,128)(2,1)S(1)}, u32[]{:S(2)}, u32[]{:S(2)}) collective-permute-start(bf16[64,3584]{1,0:T(8,128)(2,1)S(1)} %bitcast.8), channel_id=1, source_target_pairs={{0,1},{1,0},{2,3},{3,2},{4,5},{5,4},{6,7},{7,6},{8,9},{9,8},{10,11... | collective-permute-start | bytes 1376264 | tf_op jit(solution)/shard_map/ppermute | solution.py:37
  85.1 10.7 %collective-permute-start.27 = (bf16[64,3584]{1,0:T(8,128)(2,1)S(1)}, bf16[64,3584]{1,0:T(8,128)(2,1)S(1)}, u32[]{:S(2)}, u32[]{:S(2)}) collective-permute-start(bf16[64,3584]{1,0:T(8,128)(2,1)S(1)} %collective-permute-done.26.refs_0_), channel_id=1, source_target_pairs={{0,4},{1,5},{4,8},{5,9},{8,12},{9,13},{12,14},{13,15},{14,10},{15,... | collective-permute-start | bytes 1376264 | tf_op jit(solution)/shard_map/ppermute | solution.py:79
  85.6 10.7 %collective-permute-start.31 = (bf16[64,3584]{1,0:T(8,128)(2,1)S(1)}, bf16[64,3584]{1,0:T(8,128)(2,1)S(1)}, u32[]{:S(2)}, u32[]{:S(2)}) collective-permute-start(bf16[64,3584]{1,0:T(8,128)(2,1)S(1)} %collective-permute-done.28.refs_1_), channel_id=1, source_target_pairs={{0,2},{1,3},{4,0},{5,1},{8,4},{9,5},{12,8},{13,9},{14,12},{15,13},... | collective-permute-start | bytes 1376264 | tf_op jit(solution)/shard_map/ppermute | solution.py:79
  87.1 10.7 %collective-permute-start.33 = (bf16[64,3584]{1,0:T(8,128)(2,1)S(1)}, bf16[64,3584]{1,0:T(8,128)(2,1)S(1)}, u32[]{:S(2)}, u32[]{:S(2)}) collective-permute-start(bf16[64,3584]{1,0:T(8,128)(2,1)S(1)} %collective-permute-done.28.refs_1_), channel_id=1, source_target_pairs={{0,1},{1,0},{2,3},{3,2},{4,5},{5,4},{6,7},{7,6},{8,9},{9,8},{10,11... | collective-permute-start | bytes 1376264 | tf_op jit(solution)/shard_map/ppermute | solution.py:37
  87.1 11.2 %collective-permute-start.32 = (bf16[64,3584]{1,0:T(8,128)(2,1)S(1)}, bf16[64,3584]{1,0:T(8,128)(2,1)S(1)}, u32[]{:S(2)}, u32[]{:S(2)}) collective-permute-start(bf16[64,3584]{1,0:T(8,128)(2,1)S(1)} %collective-permute-done.26.refs_0_), channel_id=1, source_target_pairs={{0,1},{1,0},{2,3},{3,2},{4,5},{5,4},{6,7},{7,6},{8,9},{9,8},{10,11... | collective-permute-start | bytes 1376264 | tf_op jit(solution)/shard_map/ppermute | solution.py:37
  95.8 10.6 %collective-permute-start.30 = (bf16[64,3584]{1,0:T(8,128)(2,1)S(1)}, bf16[64,3584]{1,0:T(8,128)(2,1)S(1)}, u32[]{:S(2)}, u32[]{:S(2)}) collective-permute-start(bf16[64,3584]{1,0:T(8,128)(2,1)S(1)} %collective-permute-done.27.refs_0_), channel_id=1, source_target_pairs={{0,4},{1,5},{4,8},{5,9},{8,12},{9,13},{12,14},{13,15},{14,10},{15,... | collective-permute-start | bytes 1376264 | tf_op jit(solution)/shard_map/ppermute | solution.py:79
  96.3 10.7 %collective-permute-start.35 = (bf16[64,3584]{1,0:T(8,128)(2,1)S(1)}, bf16[64,3584]{1,0:T(8,128)(2,1)S(1)}, u32[]{:S(2)}, u32[]{:S(2)}) collective-permute-start(bf16[64,3584]{1,0:T(8,128)(2,1)S(1)} %collective-permute-done.31.refs_1_), channel_id=1, source_target_pairs={{0,2},{1,3},{4,0},{5,1},{8,4},{9,5},{12,8},{13,9},{14,12},{15,13},... | collective-permute-start | bytes 1376264 | tf_op jit(solution)/shard_map/ppermute | solution.py:79
  97.8 9.8 %collective-permute-start.37 = (bf16[64,3584]{1,0:T(8,128)(2,1)S(1)}, bf16[64,3584]{1,0:T(8,128)(2,1)S(1)}, u32[]{:S(2)}, u32[]{:S(2)}) collective-permute-start(bf16[64,3584]{1,0:T(8,128)(2,1)S(1)} %collective-permute-done.31.refs_1_), channel_id=1, source_target_pairs={{0,1},{1,0},{2,3},{3,2},{4,5},{5,4},{6,7},{7,6},{8,9},{9,8},{10,11... | collective-permute-start | bytes 1376264 | tf_op jit(solution)/shard_map/ppermute | solution.py:37
  97.8 11.3 %collective-permute-start.36 = (bf16[64,3584]{1,0:T(8,128)(2,1)S(1)}, bf16[64,3584]{1,0:T(8,128)(2,1)S(1)}, u32[]{:S(2)}, u32[]{:S(2)}) collective-permute-start(bf16[64,3584]{1,0:T(8,128)(2,1)S(1)} %collective-permute-done.27.refs_0_), channel_id=1, source_target_pairs={{0,1},{1,0},{2,3},{3,2},{4,5},{5,4},{6,7},{7,6},{8,9},{9,8},{10,11... | collective-permute-start | bytes 1376264 | tf_op jit(solution)/shard_map/ppermute | solution.py:37
  107.0 8.2 %collective-permute-start.42 = (bf16[64,3584]{1,0:T(8,128)(2,1)S(1)}, bf16[64,3584]{1,0:T(8,128)(2,1)S(1)}, u32[]{:S(2)}, u32[]{:S(2)}) collective-permute-start(bf16[64,3584]{1,0:T(8,128)(2,1)S(1)} %collective-permute-done.35.refs_1_), channel_id=1, source_target_pairs={{0,1},{1,0},{2,3},{3,2},{4,5},{5,4},{6,7},{7,6},{8,9},{9,8},{10,11... | collective-permute-start | bytes 1376264 | tf_op jit(solution)/shard_map/ppermute | solution.py:37
  107.1 8.1 %collective-permute-start.41 = (bf16[64,3584]{1,0:T(8,128)(2,1)S(1)}, bf16[64,3584]{1,0:T(8,128)(2,1)S(1)}, u32[]{:S(2)}, u32[]{:S(2)}) collective-permute-start(bf16[64,3584]{1,0:T(8,128)(2,1)S(1)} %collective-permute-done.30.refs_0_), channel_id=1, source_target_pairs={{0,1},{1,0},{2,3},{3,2},{4,5},{5,4},{6,7},{7,6},{8,9},{9,8},{10,11... | collective-permute-start | bytes 1376264 | tf_op jit(solution)/shard_map/ppermute | solution.py:37
  107.6 7.6 %collective-permute-start.39 = (bf16[64,1792]{1,0:T(8,128)(2,1)S(1)}, bf16[64,1792]{1,0:T(8,128)(2,1)S(1)}, u32[]{:S(2)}, u32[]{:S(2)}) collective-permute-start(bf16[64,1792]{1,0:T(8,128)(2,1)S(1)} %slice.135), channel_id=1, source_target_pairs={{0,2},{1,3},{4,0},{5,1},{8,4},{9,5},{12,8},{13,9},{14,12},{15,13},... | collective-permute-start | bytes 688136 | tf_op jit(solution)/shard_map/ppermute | solution.py:79
  (23 other events, 319.5 us)

commit v11 on v10

--- a/solution.py
+++ b/solution.py
@@ -280,63 +280,59 @@
     return sum(value[begin : begin + rows].astype(jnp.float32) for value in pair)
 
 
-def read_gradient(refs):
-    return sum(ref[...].astype(jnp.float32) for ref in refs)
-
-
-def enc_kernel(code_ref, w_ref, m_ref, v_ref, *refs):
-    parts, (w_out, m_out, v_out, block, fresh) = refs[:-5], refs[-5:]
-    gradient = read_gradient(parts)
-    reset = code_ref[...] != KEPT
-    w, m, v = adam_update(w_ref[...], m_ref[...], v_ref[...], gradient)
-    w = jnp.where(reset, reset_gain * gradient * inverse_rms(gradient), w)
-    w_out[...] = w
-    m_out[...] = jnp.where(reset, 0.0, m)
-    v_out[...] = jnp.where(reset, 0.0, v)
-    block[...] = w.astype(block.dtype)
-    fresh[...] = gradient.astype(fresh.dtype)
-
-
-def dec_kernel(code_ref, w_ref, m_ref, v_ref, fresh_ref, enc_block, *refs):
-    parts, (w_out, m_out, v_out, blocks) = refs[:-4], refs[-4:]
-    reset = code_ref[...] != KEPT
-    w, m, v = adam_update(w_ref[...], m_ref[...], v_ref[...], read_gradient(parts))
-    w = jnp.where(reset, fresh_ref[...].astype(jnp.float32), w)
-    w = w * inverse_rms(w)
-    w_out[...] = w
-    m_out[...] = jnp.where(reset, 0.0, m)
-    v_out[...] = jnp.where(reset, 0.0, v)
-    blocks[0] = enc_block[...]
-    blocks[1] = w.astype(blocks.dtype)
-
-
-def update(kernel, code, states, others, parts, last_shapes, name):
+def updated(refs):
+    code, states, terms = refs[0], refs[1:7], refs[7:15]
+    reset = code[...] != KEPT
+    enc_grad, dec_grad = (
+        sum(ref[...].astype(jnp.float32) for ref in half) for half in (terms[:4], terms[4:])
+    )
+    enc = adam_update(*(ref[...] for ref in states[:3]), enc_grad)
+    dec = adam_update(*(ref[...] for ref in states[3:]), dec_grad)
+    enc_w = jnp.where(reset, reset_gain * enc_grad * inverse_rms(enc_grad), enc[0])
+    dec_w = jnp.where(reset, enc_grad, dec[0])
+    dec_w = dec_w * inverse_rms(dec_w)
+    moments = [jnp.where(reset, 0.0, value) for value in enc[1:] + dec[1:]]
+    return [enc_w] + moments[:2] + [dec_w] + moments[2:]
+
+
+def blocks_kernel(*refs):
+    results, blocks = updated(refs), refs[-1]
+    blocks[0] = results[0].astype(blocks.dtype)
+    blocks[1] = results[3].astype(blocks.dtype)
+
+
+def states_kernel(*refs):
+    for ref, value in zip(refs[-6:], updated(refs)):
+        ref[...] = value
+
+
+def update(code, states, enc_parts, dec_parts, came, blocks_only):
     rows, width = states[0].shape
     tile = 16
 
-    def last_rows(value):
-        skipped = (value.shape[0] - rows) // tile
-        return pl.BlockSpec((tile, value.shape[1]), lambda i: (i + skipped, 0))
-
-    operands = [code] + list(states) + list(others) + list(parts)
-    out_shape = [jax.ShapeDtypeStruct((rows, width), jnp.float32)] * 3
-    out_specs = [pl.BlockSpec((tile, width), lambda i: (i, 0))] * 3
-    for pair in last_shapes:
-        lead = (2,) if pair else ()
-        out_shape.append(jax.ShapeDtypeStruct(lead + (rows, width), jnp.bfloat16))
-        out_specs.append(
-            pl.BlockSpec(lead + (tile, width), lambda i, pair=pair: (0, i, 0) if pair else (i, 0))
-        )
+    def row_tile(value, skipped):
+        return pl.BlockSpec((tile, value.shape[1]), lambda i: (i + skipped // tile, 0))
+
+    operands = [(value, 0) for value in [code] + list(states)]
+    for parts, first in ((enc_parts, 0), (dec_parts, rows)):
+        operands += [(value, value.shape[0] - rows) for value in parts]
+        operands += [(value, first) for value in came]
+    if blocks_only:
+        out_shape = [jax.ShapeDtypeStruct((2, rows, width), jnp.bfloat16)]
+        out_specs = [pl.BlockSpec((2, tile, width), lambda i: (0, i, 0))]
+    else:
+        out_shape = [jax.ShapeDtypeStruct((rows, width), jnp.float32)] * 6
+        out_specs = [pl.BlockSpec((tile, width), lambda i: (i, 0))] * 6
     return pl.pallas_call(
-        kernel,
+        blocks_kernel if blocks_only else states_kernel,
         grid=(rows // tile,),
-        in_specs=[last_rows(value) for value in operands],
+        in_specs=[row_tile(*operand) for operand in operands],
         out_specs=out_specs,
         out_shape=out_shape,
-        cost_estimate=cost(40 * rows * width, 40 * rows * width),
-        compiler_params=params(12),
-        name=name,
-    )(*operands)
+        cost_estimate=cost(10 * rows * width, 10 * rows * width),
+        compiler_params=params(20),
+        name="blocks" if blocks_only else "states",
+    )(*(value for value, _ in operands))
 
 
 def place_kernel(plan, size, rows, count, *refs):
@@ -375,13 +371,13 @@
     )(*operands)
 
 
-def gathered(block, size, rows):
+def gathered(block, order, size, rows):
     chips = size // 2
     width = block.shape[1]
     half = width // 2
     hops = chips // 2
     right = left = block
-    near, far, wholes = [(0, 0, 0, block)], [], None
+    near, far, wholes = [(0, 0, 0, after(block, order))], [], None
     for hop in range(1, hops + 1):
         if hop == hops:
             right, left = right[:, :half], left[:, half:]
@@ -393,8 +389,8 @@
         left = after(left, right)
         near = [(-hop, 0, 0, right), (hop, 0, half if hop == hops else 0, left)]
     sent = [(offset, 1, column, swap(value, 1, size)) for offset, _, column, value in near]
-    wholes = place(near + far, wholes, size, rows, width)
-    return place(sent, wholes, size, rows, width)
+    wholes = place(near, wholes, size, rows, width)
+    return place(far + sent, wholes, size, rows, width)
 
 
 def shards(
@@ -418,66 +414,43 @@
     chips = size // 2
     stages = gather_table(jnp.concatenate([send_count, dead_order], axis=1), size)
     table = stages[-1]
-    def begin(kept, from_core):
-        far = term(kept, from_core, 0, rows).astype(jnp.bfloat16)
-        return [far[:, :half], far[:, half:]]
+    dec = stream_product(latent_act, out_grad, size, rows)
+    dec_far = after(dec[0], *stages[0])
+    dec_kept = [dec[1], dec[3]]
+    dec_core = [swap(dec_far, 1, size), swap(after(dec[2], table[0]), 1, size)]
+    enc_sent, kept, enc_left, code = far_product(
+        enc_coef, x_rows, size, rows, pick_rows[0].T, table
+    )
+    enc_kept, enc_core = [kept], [swap(enc_sent, 1, size)]
+
+    def both(slot):
+        terms = [term(*pair, slot, rows) for pair in ((enc_kept, enc_core), (dec_kept, dec_core))]
+        return jnp.concatenate(terms, axis=0)
 
     def travel(moving):
         return [shift(moving[0], 1, size), shift(moving[1], -1, size)]
 
-    def advance(came, kept, from_core, hop, order):
+    far = both(0).astype(jnp.bfloat16)
+    moving = [far[:, :half], far[:, half:]]
+    enc_sent, kept = near_product(after(enc_left, *moving), x_rows)
+    came, enc_sent = tied(travel(moving), enc_sent)
+    enc_kept.append(kept)
+    enc_core.append(swap(enc_sent, 1, size))
+    for hop in range(1, chips // 2):
         moving = []
-        for side, value in enumerate(after(came, order)):
+        for side, value in enumerate(came):
             value = value.astype(jnp.float32)
             if value.shape[1] < width:
                 pads = ((0, 0, 0), (0, half, 0) if side == 0 else (half, 0, 0))
                 value = lax.pad(value, jnp.float32(0), pads)
-            value = value + term(kept, from_core, 2 * hop - side, rows)
-            moving.append(value.astype(jnp.bfloat16))
-        return travel(moving), moving
-
-    dec = stream_product(latent_act, out_grad, size, rows)
-    dec_far = after(dec[0], *stages[0])
-    dec_kept, dec_core = [dec[1], dec[3]], [swap(dec_far, 1, size), swap(after(dec[2], table[0]), 1, size)]
-    dec_moving = begin(dec_kept, after(dec_core, table[0]))
-    enc_sent, kept, enc_left, code = far_product(
-        after(enc_coef, *dec_moving), x_rows, size, rows, pick_rows[0].T, table
-    )
-    dec_came, enc_sent = tied(travel(dec_moving), enc_sent)
-    enc_kept, enc_core = [kept], [swap(enc_sent, 1, size)]
-    dec_came, order = advance(dec_came, dec_kept, dec_core, 1, enc_sent)
-    enc_moving = begin(enc_kept, after(enc_core, order))
-    enc_sent, kept = near_product(after(enc_left, *enc_moving), x_rows)
-    enc_came, enc_sent = tied(travel(enc_moving), enc_sent)
-    enc_kept.append(kept)
-    enc_core.append(swap(enc_sent, 1, size))
-    order = enc_sent
-    for hop in range(1, chips // 2):
-        if hop + 1 < chips // 2:
-            dec_came, order = advance(dec_came, dec_kept, dec_core, hop + 1, order)
-        else:
-            order = (order, dec_came)
-        enc_came, order = advance(enc_came, enc_kept, enc_core, hop, order)
-    enc_out, enc_mo, enc_vo, enc_block, fresh = update(
-        enc_kernel,
-        code,
-        (enc_w, enc_m, enc_v),
-        (),
-        [enc_kept[1], enc_core[1]] + enc_came,
-        (False, False),
-        "enc_update",
-    )
-    dec_out, dec_mo, dec_vo, blocks = update(
-        dec_kernel,
-        code,
-        (dec_w, dec_m, dec_v),
-        (fresh, enc_block),
-        [dec_kept[1], dec_core[1]] + dec_came,
-        (True,),
-        "dec_update",
-    )
-    enc_full, dec_full = gathered(blocks.reshape(2 * rows, width), size, rows)
-    return (enc_out, enc_mo, enc_vo, dec_out, dec_mo, dec_vo, enc_full, dec_full)
+            moving.append((value + both(2 * hop - side)).astype(jnp.bfloat16))
+        came = travel(moving)
+    states = (enc_w, enc_m, enc_v, dec_w, dec_m, dec_v)
+    parts = ([enc_kept[1], enc_core[1]], [dec_kept[1], dec_core[1]], came)
+    (blocks,) = update(code, states, *parts, True)
+    results = update(code, after(states, blocks), *parts, False)
+    enc_full, dec_full = gathered(blocks.reshape(2 * rows, width), results[0], size, rows)
+    return (*results, enc_full, dec_full)
 
 
 def solution(mesh):

time: 118 us -> 113 us (0.958)
  starting transfers between devices: 34.6 us -> 26.6 us
  waiting for transfers between devices: 52.6 us -> 55.4 us
    ppermute x24 -> x16, starting transfers between devices: 24.9 us -> 16.7 us  [shift(): return lax.ppermute(value, 'latent', pairs)]
    ppermute x19, waiting for transfers between devices: 2.37 us -> 6.48 us  [swap(): return lax.ppermute(value, 'latent', [(i, i ^ bits) for i in range(size)])]
    ppermute x24 -> x16, waiting for transfers between devices: 50.2 us -> 48.9 us  [shift(): return lax.ppermute(value, 'latent', pairs)]
  transfers between devices with their start and end apart: 43 -> 35, of which waited for: 16 -> 18; matrix products, arithmetic and copies ran while one was open for 1% -> 1% of each run, Pallas kernels for 19% -> 22%
where the time goes in v11:
time: 113 us
  waiting for transfers between devices  55.4 us (49%)
  Pallas kernels  27.7 us (25%)
  starting transfers between devices  26.6 us (24%)
  other arithmetic  2.16 us (2%)
    ppermute x16, waiting for transfers between devices, shift(): return lax.ppermute(value, 'latent', pairs)  48.9 us
    ppermute x16, starting transfers between devices, shift(): return lax.ppermute(value, 'latent', pairs)  16.7 us
    ppermute x19, starting transfers between devices, swap(): return lax.ppermute(value, 'latent', [(i, i ^ bits) for i in range(size)])  9.86 us
    pallas_call x2, Pallas kernels, product(): pl.pallas_call(kernel, grid=(width // tile,), in_specs=in_specs + [pl.Blo...  8.71 us
    pallas_call x1, Pallas kernels, stream_product(): pl.pallas_call(functools.partial(stream_kernel, size, rows), in_specs=[pl...  8.36 us
    ppermute x19, waiting for transfers between devices, swap(): return lax.ppermute(value, 'latent', [(i, i ^ bits) for i in range(size)])  6.48 us
    pallas_call x6, Pallas kernels, place(): pl.pallas_call(functools.partial(place_kernel, plan, size, rows, count),...  6.39 us
    pallas_call x2, Pallas kernels, update(): pl.pallas_call(blocks_kernel if blocks_only else states_kernel, grid=(row...  4.19 us
  transfers between devices with their start and end apart: 35, of which 18 were waited for; matrix products, arithmetic and copies ran while one was open for 1% of the time, Pallas kernels for 22%

profile of v11, /device:TPU:0, one launch (start us, length us, event | category | flops | bytes accessed | tf_op | source)
XLA Modules:
  0.0 112.9 jit_solution(277229974777434824)
XLA Ops:
  1.6 2.5 %collective-permute-start.2 = (s32[1,48]{1,0:T(1,128)S(1)}, s32[1,48]{1,0:T(1,128)S(1)}, u32[]{:S(2)}, u32[]{:S(2)}) collective-permute-start(s32[1,48]{1,0:T(1,128)S(1)} %pad_add_fusion.1), channel_id=1, source_target_pairs={{0,3},{1,2},{2,1},{3,0},{4,7},{5,6},{6,5},{7,4},{8,11},{9,10},{10,... | collective-permute-start | bytes 584 | tf_op jit(solution)/shard_map/ppermute | solution.py:37
  4.7 8.4 %product.1 = (bf16[128,3584]{1,0:T(8,128)(2,1)S(1)}, bf16[128,3584]{1,0:T(8,128)(2,1)S(1)}, bf16[128,3584]{1,0:T(8,128)(2,1)S(1)}, bf16[128,3584]{1,0:T(8,128)(2,1)S(1)}) custom-call(bf16[1024,512]{1,0:T(8,128)(2,1)} %coef_ref.3, bf16[1024,3584]{1,0:T(8,128)(2,1)} %right_hbm.1), custom_call_target="tpu_custom_call" | custom-call | flops 3758096384 | bytes 12058624 | tf_op jit(solution)/shard_map/product/pallas_call | solution.py:182
  13.7 3.6 %collective-permute-start.5 = (s32[4,48]{1,0:T(4,128)S(1)}, s32[4,48]{1,0:T(4,128)S(1)}, u32[]{:S(2)}, u32[]{:S(2)}) collective-permute-start(s32[4,48]{1,0:T(4,128)S(1)} %pad_add_fusion.refs_0_), channel_id=1, source_target_pairs={{0,12},{1,13},{2,14},{3,15},{4,8},{5,9},{6,10},{7,11},{8,4},{9,5},... | collective-permute-start | bytes 2312 | tf_op jit(solution)/shard_map/ppermute | solution.py:37
  18.1 1.0 collective-permute-done.5.refs_3_
  19.1 2.7 %collective-permute-done.4.refs_2_ = s32[4,48]{1,0:T(4,128)S(1)} collective-permute-done((s32[4,48]{1,0:T(4,128)S(1)}, s32[4,48]{1,0:T(4,128)S(1)}, u32[]{:S(2)}, u32[]{:S(2)}) %collective-permute-start.4) | collective-permute-done | bytes 800 | tf_op jit(solution)/shard_map/ppermute | solution.py:37
  21.9 4.9 %far_product.1 = (bf16[128,3584]{1,0:T(8,128)(2,1)S(1)}, bf16[128,3584]{1,0:T(8,128)(2,1)S(1)}, bf16[256,1024]{1,0:T(8,128)(2,1)S(1)}, s32[32,1]{1,0:T(8,128)S(1)}) custom-call(bf16[1024,512]{1,0:T(8,128)(2,1)S(1)} %copy-done.6, bf16[1024,3584]{1,0:T(8,128)(2,1)S(1)} %bitcast.5, s32[2,16]{1,0:T(2,128)S(1)} %bitcast.10, s32[4,48]{1,0:T(4,128)S(1)} %pad_add_fusion.refs_0_, ...), custom_call_target="tpu_custom_call" | custom-call | flops 1879048192 | bytes 9699328 | tf_op jit(solution)/shard_map/far_product/pallas_call | solution.py:241
  27.1 2.2 %collective-permute-done.6 = bf16[128,3584]{1,0:T(8,128)(2,1)S(1)} collective-permute-done((bf16[128,3584]{1,0:T(8,128)(2,1)S(1)}, bf16[128,3584]{1,0:T(8,128)(2,1)S(1)}, u32[]{:S(2)}, u32[]{:S(2)}) %collective-permute-start.6) | collective-permute-done | bytes 917536 | tf_op jit(solution)/shard_map/ppermute | solution.py:37
  29.6 1.4 %collective-permute-start.9 = (bf16[64,1792]{1,0:T(8,128)(2,1)S(1)}, bf16[64,1792]{1,0:T(8,128)(2,1)S(1)}, u32[]{:S(2)}, u32[]{:S(2)}) collective-permute-start(bf16[64,1792]{1,0:T(8,128)(2,1)S(1)} %get-tuple-element.136), channel_id=1, source_target_pairs={{0,2},{1,3},{4,0},{5,1},{8,4},{9,5},{12,8},{13,9},{14,12},{15,13},... | collective-permute-start | bytes 688136 | tf_op jit(solution)/shard_map/ppermute | solution.py:79
  31.8 3.8 %near_product.1 = (bf16[128,3584]{1,0:T(8,128)(2,1)S(1)}, bf16[128,3584]{1,0:T(8,128)(2,1)S(1)}) custom-call(bf16[256,1024]{1,0:T(8,128)(2,1)S(1)} %get-tuple-element.72.left_ref, bf16[1024,3584]{1,0:T(8,128)(2,1)S(1)} %bitcast.5), custom_call_target="tpu_custom_call" | custom-call | flops 1879048192 | bytes 9699328 | tf_op jit(solution)/shard_map/near_product/pallas_call | solution.py:241
  35.6 1.6 %collective-permute-done.9 = bf16[64,1792]{1,0:T(8,128)(2,1)S(1)} collective-permute-done((bf16[64,1792]{1,0:T(8,128)(2,1)S(1)}, bf16[64,1792]{1,0:T(8,128)(2,1)S(1)}, u32[]{:S(2)}, u32[]{:S(2)}) %collective-permute-start.9) | collective-permute-done | bytes 229408 | tf_op jit(solution)/shard_map/ppermute | solution.py:79
  37.3 1.1 collective-permute-done.8
  39.4 1.2 %collective-permute-start.11 = (bf16[64,3584]{1,0:T(8,128)(2,1)S(1)}, bf16[64,3584]{1,0:T(8,128)(2,1)S(1)}, u32[]{:S(2)}, u32[]{:S(2)}) collective-permute-start(bf16[64,3584]{1,0:T(8,128)(2,1)S(1)} %fusion), channel_id=1, source_target_pairs={{0,4},{1,5},{4,8},{5,9},{8,12},{9,13},{12,14},{13,15},{14,10},{15,... | collective-permute-start | bytes 1376264 | tf_op jit(solution)/shard_map/ppermute | solution.py:79
  40.7 9.3 %collective-permute-done.15 = bf16[64,3584]{1,0:T(8,128)(2,1)S(1)} collective-permute-done((bf16[64,3584]{1,0:T(8,128)(2,1)S(1)}, bf16[64,3584]{1,0:T(8,128)(2,1)S(1)}, u32[]{:S(2)}, u32[]{:S(2)}) %collective-permute-start.15) | collective-permute-done | bytes 458784 | tf_op jit(solution)/shard_map/ppermute | solution.py:79
  50.0 1.2 %collective-permute-start.16 = (bf16[64,3584]{1,0:T(8,128)(2,1)S(1)}, bf16[64,3584]{1,0:T(8,128)(2,1)S(1)}, u32[]{:S(2)}, u32[]{:S(2)}) collective-permute-start(bf16[64,3584]{1,0:T(8,128)(2,1)S(1)} %fusion.4), channel_id=1, source_target_pairs={{0,2},{1,3},{4,0},{5,1},{8,4},{9,5},{12,8},{13,9},{14,12},{15,13},... | collective-permute-start | bytes 1376264 | tf_op jit(solution)/shard_map/ppermute | solution.py:79
  52.5 8.2 %collective-permute-done.16 = bf16[64,3584]{1,0:T(8,128)(2,1)S(1)} collective-permute-done((bf16[64,3584]{1,0:T(8,128)(2,1)S(1)}, bf16[64,3584]{1,0:T(8,128)(2,1)S(1)}, u32[]{:S(2)}, u32[]{:S(2)}) %collective-permute-start.16) | collective-permute-done | bytes 458784 | tf_op jit(solution)/shard_map/ppermute | solution.py:79
  60.7 1.5 %collective-permute-start.17 = (bf16[64,3584]{1,0:T(8,128)(2,1)S(1)}, bf16[64,3584]{1,0:T(8,128)(2,1)S(1)}, u32[]{:S(2)}, u32[]{:S(2)}) collective-permute-start(bf16[64,3584]{1,0:T(8,128)(2,1)S(1)} %fusion.5), channel_id=1, source_target_pairs={{0,2},{1,3},{4,0},{5,1},{8,4},{9,5},{12,8},{13,9},{14,12},{15,13},... | collective-permute-start | bytes 1376264 | tf_op jit(solution)/shard_map/ppermute | solution.py:79
  63.0 7.4 %collective-permute-done.17.refs_10_.refs_14_ = bf16[64,3584]{1,0:T(8,128)(2,1)S(1)} collective-permute-done((bf16[64,3584]{1,0:T(8,128)(2,1)S(1)}, bf16[64,3584]{1,0:T(8,128)(2,1)S(1)}, u32[]{:S(2)}, u32[]{:S(2)}) %collective-permute-start.17) | collective-permute-done | bytes 458784 | tf_op jit(solution)/shard_map/ppermute | solution.py:79
  70.4 1.6 %collective-permute-done.14.refs_9_.refs_13_ = bf16[64,3584]{1,0:T(8,128)(2,1)S(1)} collective-permute-done((bf16[64,3584]{1,0:T(8,128)(2,1)S(1)}, bf16[64,3584]{1,0:T(8,128)(2,1)S(1)}, u32[]{:S(2)}, u32[]{:S(2)}) %collective-permute-start.14) | collective-permute-done | bytes 458784 | tf_op jit(solution)/shard_map/ppermute | solution.py:79
  72.0 1.6 %blocks.1 = bf16[2,32,3584]{2,1,0:T(8,128)(2,1)S(1)} custom-call(s32[32,1]{1,0:T(8,128)S(1)} %get-tuple-element.65.refs_0_, f32[32,3584]{1,0:T(8,128)S(1)} %copy-done, f32[32,3584]{1,0:T(8,128)S(1)} %copy-done.1, f32[32,3584]{1,0:T(8,128)S(1)} %copy-done.2, f32[32,3584]{1,0:T(8,128)S(1)} %copy-done.3, f32[32,3584]{1,0:T(8,128)S(1)} %copy-done.4, ...), custom_call_target="tpu_custom_call" | custom-call | flops 1146880 | bytes 1146880 | tf_op jit(solution)/shard_map/blocks/pallas_call | solution.py:326
  74.2 1.5 %collective-permute-start.20 = (bf16[64,3584]{1,0:T(8,128)(2,1)S(1)}, bf16[64,3584]{1,0:T(8,128)(2,1)S(1)}, u32[]{:S(2)}, u32[]{:S(2)}) collective-permute-start(bf16[64,3584]{1,0:T(8,128)(2,1)S(1)} %bitcast.7), channel_id=1, source_target_pairs={{0,2},{1,3},{4,0},{5,1},{8,4},{9,5},{12,8},{13,9},{14,12},{15,13},... | collective-permute-start | bytes 1376264 | tf_op jit(solution)/shard_map/ppermute | solution.py:79
  75.7 2.6 %states.1 = (f32[32,3584]{1,0:T(8,128)}, f32[32,3584]{1,0:T(8,128)}, f32[32,3584]{1,0:T(8,128)}, f32[32,3584]{1,0:T(8,128)}, f32[32,3584]{1,0:T(8,128)}, /*index=5*/f32[32,3584]{1,0:T(8,128)}) custom-call(s32[32,1]{1,0:T(8,128)S(1)} %get-tuple-element.65.refs_0_, f32[32,3584]{1,0:T(8,128)S(1)} %copy-done, f32[32,3584]{1,0:T(8,128)S(1)} %copy-done.1, ...), custom_call_target="tpu_custom_call" | custom-call | flops 1146880 | bytes 1146880 | tf_op jit(solution)/shard_map/states/pallas_call | solution.py:326
  79.1 3.4 %collective-permute-done.18.refs_0_ = bf16[64,3584]{1,0:T(8,128)(2,1)S(1)} collective-permute-done((bf16[64,3584]{1,0:T(8,128)(2,1)S(1)}, bf16[64,3584]{1,0:T(8,128)(2,1)S(1)}, u32[]{:S(2)}, u32[]{:S(2)}) %collective-permute-start.18) | collective-permute-done | bytes 458784 | tf_op jit(solution)/shard_map/ppermute | solution.py:79
  82.8 1.7 %collective-permute-start.23 = (bf16[64,3584]{1,0:T(8,128)(2,1)S(1)}, bf16[64,3584]{1,0:T(8,128)(2,1)S(1)}, u32[]{:S(2)}, u32[]{:S(2)}) collective-permute-start(bf16[64,3584]{1,0:T(8,128)(2,1)S(1)} %collective-permute-done.20.refs_1_), channel_id=1, source_target_pairs={{0,2},{1,3},{4,0},{5,1},{8,4},{9,5},{12,8},{13,9},{14,12},{15,13},... | collective-permute-start | bytes 1376264 | tf_op jit(solution)/shard_map/ppermute | solution.py:79
  85.0 1.1 place.7
  86.2 7.0 %collective-permute-done.19.refs_0_ = bf16[64,3584]{1,0:T(8,128)(2,1)S(1)} collective-permute-done((bf16[64,3584]{1,0:T(8,128)(2,1)S(1)}, bf16[64,3584]{1,0:T(8,128)(2,1)S(1)}, u32[]{:S(2)}, u32[]{:S(2)}) %collective-permute-start.19) | collective-permute-done | bytes 458784 | tf_op jit(solution)/shard_map/ppermute | solution.py:79
  93.5 1.7 %collective-permute-start.27 = (bf16[64,3584]{1,0:T(8,128)(2,1)S(1)}, bf16[64,3584]{1,0:T(8,128)(2,1)S(1)}, u32[]{:S(2)}, u32[]{:S(2)}) collective-permute-start(bf16[64,3584]{1,0:T(8,128)(2,1)S(1)} %collective-permute-done.23.refs_1_), channel_id=1, source_target_pairs={{0,2},{1,3},{4,0},{5,1},{8,4},{9,5},{12,8},{13,9},{14,12},{15,13},... | collective-permute-start | bytes 1376264 | tf_op jit(solution)/shard_map/ppermute | solution.py:79
  95.7 1.3 %place.8 = (bf16[512,3584]{1,0:T(8,128)(2,1)}, bf16[512,3584]{1,0:T(8,128)(2,1)}) custom-call(bf16[64,3584]{1,0:T(8,128)(2,1)S(1)} %collective-permute-done.19.refs_0_, bf16[64,3584]{1,0:T(8,128)(2,1)S(1)} %collective-permute-done.23.refs_1_, bf16[64,3584]{1,0:T(8,128)(2,1)S(1)} %collective-permute-done.24.refs_2_, ...), custom_call_target="tpu_custom_call", output_to_operand_aliasing={{0}: (4, {}), {1}: (5, {})} | custom-call | bytes 3670016 | tf_op jit(solution)/shard_map/place/pallas_call | solution.py:361
  97.0 6.8 %collective-permute-done.22.refs_0_ = bf16[64,3584]{1,0:T(8,128)(2,1)S(1)} collective-permute-done((bf16[64,3584]{1,0:T(8,128)(2,1)S(1)}, bf16[64,3584]{1,0:T(8,128)(2,1)S(1)}, u32[]{:S(2)}, u32[]{:S(2)}) %collective-permute-start.22) | collective-permute-done | bytes 458784 | tf_op jit(solution)/shard_map/ppermute | solution.py:79
  104.2 1.8 %collective-permute-start.33 = (bf16[64,1792]{1,0:T(8,128)(2,1)S(1)}, bf16[64,1792]{1,0:T(8,128)(2,1)S(1)}, u32[]{:S(2)}, u32[]{:S(2)}) collective-permute-start(bf16[64,1792]{1,0:T(8,128)(2,1)S(1)} %slice.127), channel_id=1, source_target_pairs={{0,2},{1,3},{4,0},{5,1},{8,4},{9,5},{12,8},{13,9},{14,12},{15,13},... | collective-permute-start | bytes 688136 | tf_op jit(solution)/shard_map/ppermute | solution.py:79
  106.5 1.3 %place.9 = (bf16[512,3584]{1,0:T(8,128)(2,1)}, bf16[512,3584]{1,0:T(8,128)(2,1)}) custom-call(bf16[64,3584]{1,0:T(8,128)(2,1)S(1)} %collective-permute-done.22.refs_0_, bf16[64,3584]{1,0:T(8,128)(2,1)S(1)} %collective-permute-done.27.refs_1_, bf16[64,3584]{1,0:T(8,128)(2,1)S(1)} %collective-permute-done.30.refs_2_, ...), custom_call_target="tpu_custom_call", output_to_operand_aliasing={{0}: (4, {}), {1}: (5, {})} | custom-call | bytes 3670016 | tf_op jit(solution)/shard_map/place/pallas_call | solution.py:361
  107.8 2.1 %collective-permute-done.29.refs_0_ = bf16[64,1792]{1,0:T(8,128)(2,1)S(1)} collective-permute-done((bf16[64,1792]{1,0:T(8,128)(2,1)S(1)}, bf16[64,1792]{1,0:T(8,128)(2,1)S(1)}, u32[]{:S(2)}, u32[]{:S(2)}) %collective-permute-start.29) | collective-permute-done | bytes 229408 | tf_op jit(solution)/shard_map/ppermute | solution.py:79
  111.7 1.1 %place.11 = (bf16[512,3584]{1,0:T(8,128)(2,1)}, bf16[512,3584]{1,0:T(8,128)(2,1)}) custom-call(bf16[64,3584]{1,0:T(8,128)(2,1)S(1)} %collective-permute-done.26.refs_0_, bf16[64,3584]{1,0:T(8,128)(2,1)S(1)} %collective-permute-done.28.refs_1_, bf16[64,1792]{1,0:T(8,128)(2,1)S(1)} %collective-permute-done.32.refs_2_, ...), custom_call_target="tpu_custom_call", output_to_operand_aliasing={{0}: (4, {}), {1}: (5, {})} | custom-call | bytes 3670016 | tf_op jit(solution)/shard_map/place/pallas_call | solution.py:361
  (89 shorter events, 13.3 us)
Async XLA Ops:
  1.6 11.5 %collective-permute-start.2 = (s32[1,48]{1,0:T(1,128)S(1)}, s32[1,48]{1,0:T(1,128)S(1)}, u32[]{:S(2)}, u32[]{:S(2)}) collective-permute-start(s32[1,48]{1,0:T(1,128)S(1)} %pad_add_fusion.1), channel_id=1, source_target_pairs={{0,3},{1,2},{2,1},{3,0},{4,7},{5,6},{6,5},{7,4},{8,11},{9,10},{10,... | collective-permute-start | bytes 584 | tf_op jit(solution)/shard_map/ppermute | solution.py:37
  4.0 9.1 %collective-permute-start.1 = (s32[1,48]{1,0:T(1,128)S(1)}, s32[1,48]{1,0:T(1,128)S(1)}, u32[]{:S(2)}, u32[]{:S(2)}) collective-permute-start(s32[1,48]{1,0:T(1,128)S(1)} %pad_add_fusion.1), channel_id=1, source_target_pairs={{0,2},{1,3},{2,0},{3,1},{4,6},{5,7},{6,4},{7,5},{8,10},{9,11},{10,... | collective-permute-start | bytes 584 | tf_op jit(solution)/shard_map/ppermute | solution.py:37
  4.7 8.4 %collective-permute-start = (s32[1,48]{1,0:T(1,128)S(1)}, s32[1,48]{1,0:T(1,128)S(1)}, u32[]{:S(2)}, u32[]{:S(2)}) collective-permute-start(s32[1,48]{1,0:T(1,128)S(1)} %pad_add_fusion.1), channel_id=1, source_target_pairs={{0,1},{1,0},{2,3},{3,2},{4,5},{5,4},{6,7},{7,6},{8,9},{9,8},{10,11... | collective-permute-start | bytes 584 | tf_op jit(solution)/shard_map/ppermute | solution.py:37
  13.1 13.8 %collective-permute-start.7 = (bf16[128,3584]{1,0:T(8,128)(2,1)S(1)}, bf16[128,3584]{1,0:T(8,128)(2,1)S(1)}, u32[]{:S(2)}, u32[]{:S(2)}) collective-permute-start(bf16[128,3584]{1,0:T(8,128)(2,1)S(1)} %get-tuple-element.71), channel_id=1, source_target_pairs={{0,1},{1,0},{2,3},{3,2},{4,5},{5,4},{6,7},{7,6},{8,9},{9,8},{10,11... | collective-permute-start | bytes 2752520 | tf_op jit(solution)/shard_map/ppermute | solution.py:37
  13.7 5.4 %collective-permute-start.5 = (s32[4,48]{1,0:T(4,128)S(1)}, s32[4,48]{1,0:T(4,128)S(1)}, u32[]{:S(2)}, u32[]{:S(2)}) collective-permute-start(s32[4,48]{1,0:T(4,128)S(1)} %pad_add_fusion.refs_0_), channel_id=1, source_target_pairs={{0,12},{1,13},{2,14},{3,15},{4,8},{5,9},{6,10},{7,11},{8,4},{9,5},... | collective-permute-start | bytes 2312 | tf_op jit(solution)/shard_map/ppermute | solution.py:37
  17.3 4.5 %collective-permute-start.4 = (s32[4,48]{1,0:T(4,128)S(1)}, s32[4,48]{1,0:T(4,128)S(1)}, u32[]{:S(2)}, u32[]{:S(2)}) collective-permute-start(s32[4,48]{1,0:T(4,128)S(1)} %pad_add_fusion.refs_0_), channel_id=1, source_target_pairs={{0,8},{1,9},{2,10},{3,11},{4,12},{5,13},{6,14},{7,15},{8,0},{9,1},... | collective-permute-start | bytes 2312 | tf_op jit(solution)/shard_map/ppermute | solution.py:37
  17.4 4.5 %collective-permute-start.3 = (s32[4,48]{1,0:T(4,128)S(1)}, s32[4,48]{1,0:T(4,128)S(1)}, u32[]{:S(2)}, u32[]{:S(2)}) collective-permute-start(s32[4,48]{1,0:T(4,128)S(1)} %pad_add_fusion.refs_0_), channel_id=1, source_target_pairs={{0,4},{1,5},{2,6},{3,7},{4,0},{5,1},{6,2},{7,3},{8,12},{9,13},{10,... | collective-permute-start | bytes 2312 | tf_op jit(solution)/shard_map/ppermute | solution.py:37
  18.1 13.5 %collective-permute-start.12 = (bf16[128,3584]{1,0:T(8,128)(2,1)S(1)}, bf16[128,3584]{1,0:T(8,128)(2,1)S(1)}, u32[]{:S(2)}, u32[]{:S(2)}) collective-permute-start(bf16[128,3584]{1,0:T(8,128)(2,1)S(1)} %get-tuple-element.79), channel_id=1, source_target_pairs={{0,1},{1,0},{2,3},{3,2},{4,5},{5,4},{6,7},{7,6},{8,9},{9,8},{10,11... | collective-permute-start | bytes 2752520 | tf_op jit(solution)/shard_map/ppermute | solution.py:37
  29.6 7.7 %collective-permute-start.9 = (bf16[64,1792]{1,0:T(8,128)(2,1)S(1)}, bf16[64,1792]{1,0:T(8,128)(2,1)S(1)}, u32[]{:S(2)}, u32[]{:S(2)}) collective-permute-start(bf16[64,1792]{1,0:T(8,128)(2,1)S(1)} %get-tuple-element.136), channel_id=1, source_target_pairs={{0,2},{1,3},{4,0},{5,1},{8,4},{9,5},{12,8},{13,9},{14,12},{15,13},... | collective-permute-start | bytes 688136 | tf_op jit(solution)/shard_map/ppermute | solution.py:79
  31.0 7.4 %collective-permute-start.8 = (bf16[64,1792]{1,0:T(8,128)(2,1)S(1)}, bf16[64,1792]{1,0:T(8,128)(2,1)S(1)}, u32[]{:S(2)}, u32[]{:S(2)}) collective-permute-start(bf16[64,1792]{1,0:T(8,128)(2,1)S(1)} %get-tuple-element.137), channel_id=1, source_target_pairs={{0,4},{1,5},{4,8},{5,9},{8,12},{9,13},{12,14},{13,15},{14,10},{15,... | collective-permute-start | bytes 688136 | tf_op jit(solution)/shard_map/ppermute | solution.py:79
  38.5 11.5 %collective-permute-start.15 = (bf16[64,3584]{1,0:T(8,128)(2,1)S(1)}, bf16[64,3584]{1,0:T(8,128)(2,1)S(1)}, u32[]{:S(2)}, u32[]{:S(2)}) collective-permute-start(bf16[64,3584]{1,0:T(8,128)(2,1)S(1)} %fusion.3), channel_id=1, source_target_pairs={{0,2},{1,3},{4,0},{5,1},{8,4},{9,5},{12,8},{13,9},{14,12},{15,13},... | collective-permute-start | bytes 1376264 | tf_op jit(solution)/shard_map/ppermute | solution.py:79
  39.4 12.0 %collective-permute-start.11 = (bf16[64,3584]{1,0:T(8,128)(2,1)S(1)}, bf16[64,3584]{1,0:T(8,128)(2,1)S(1)}, u32[]{:S(2)}, u32[]{:S(2)}) collective-permute-start(bf16[64,3584]{1,0:T(8,128)(2,1)S(1)} %fusion), channel_id=1, source_target_pairs={{0,4},{1,5},{4,8},{5,9},{8,12},{9,13},{12,14},{13,15},{14,10},{15,... | collective-permute-start | bytes 1376264 | tf_op jit(solution)/shard_map/ppermute | solution.py:79
  40.7 10.6 %collective-permute-start.10 = (bf16[128,3584]{1,0:T(8,128)(2,1)S(1)}, bf16[128,3584]{1,0:T(8,128)(2,1)S(1)}, u32[]{:S(2)}, u32[]{:S(2)}) collective-permute-start(bf16[128,3584]{1,0:T(8,128)(2,1)S(1)} %get-tuple-element.75), channel_id=1, source_target_pairs={{0,1},{1,0},{2,3},{3,2},{4,5},{5,4},{6,7},{7,6},{8,9},{9,8},{10,11... | collective-permute-start | bytes 2752520 | tf_op jit(solution)/shard_map/ppermute | solution.py:37
  50.0 10.6 %collective-permute-start.16 = (bf16[64,3584]{1,0:T(8,128)(2,1)S(1)}, bf16[64,3584]{1,0:T(8,128)(2,1)S(1)}, u32[]{:S(2)}, u32[]{:S(2)}) collective-permute-start(bf16[64,3584]{1,0:T(8,128)(2,1)S(1)} %fusion.4), channel_id=1, source_target_pairs={{0,2},{1,3},{4,0},{5,1},{8,4},{9,5},{12,8},{13,9},{14,12},{15,13},... | collective-permute-start | bytes 1376264 | tf_op jit(solution)/shard_map/ppermute | solution.py:79
  51.5 10.6 %collective-permute-start.13 = (bf16[64,3584]{1,0:T(8,128)(2,1)S(1)}, bf16[64,3584]{1,0:T(8,128)(2,1)S(1)}, u32[]{:S(2)}, u32[]{:S(2)}) collective-permute-start(bf16[64,3584]{1,0:T(8,128)(2,1)S(1)} %fusion.1), channel_id=1, source_target_pairs={{0,4},{1,5},{4,8},{5,9},{8,12},{9,13},{12,14},{13,15},{14,10},{15,... | collective-permute-start | bytes 1376264 | tf_op jit(solution)/shard_map/ppermute | solution.py:79
  60.7 9.7 %collective-permute-start.17 = (bf16[64,3584]{1,0:T(8,128)(2,1)S(1)}, bf16[64,3584]{1,0:T(8,128)(2,1)S(1)}, u32[]{:S(2)}, u32[]{:S(2)}) collective-permute-start(bf16[64,3584]{1,0:T(8,128)(2,1)S(1)} %fusion.5), channel_id=1, source_target_pairs={{0,2},{1,3},{4,0},{5,1},{8,4},{9,5},{12,8},{13,9},{14,12},{15,13},... | collective-permute-start | bytes 1376264 | tf_op jit(solution)/shard_map/ppermute | solution.py:79
  62.3 9.7 %collective-permute-start.14 = (bf16[64,3584]{1,0:T(8,128)(2,1)S(1)}, bf16[64,3584]{1,0:T(8,128)(2,1)S(1)}, u32[]{:S(2)}, u32[]{:S(2)}) collective-permute-start(bf16[64,3584]{1,0:T(8,128)(2,1)S(1)} %fusion.2), channel_id=1, source_target_pairs={{0,4},{1,5},{4,8},{5,9},{8,12},{9,13},{12,14},{13,15},{14,10},{15,... | collective-permute-start | bytes 1376264 | tf_op jit(solution)/shard_map/ppermute | solution.py:79
  73.6 8.9 %collective-permute-start.18 = (bf16[64,3584]{1,0:T(8,128)(2,1)S(1)}, bf16[64,3584]{1,0:T(8,128)(2,1)S(1)}, u32[]{:S(2)}, u32[]{:S(2)}) collective-permute-start(bf16[64,3584]{1,0:T(8,128)(2,1)S(1)} %bitcast.6), channel_id=1, source_target_pairs={{0,4},{1,5},{4,8},{5,9},{8,12},{9,13},{12,14},{13,15},{14,10},{15,... | collective-permute-start | bytes 1376264 | tf_op jit(solution)/shard_map/ppermute | solution.py:79
  74.2 8.6 %collective-permute-start.20 = (bf16[64,3584]{1,0:T(8,128)(2,1)S(1)}, bf16[64,3584]{1,0:T(8,128)(2,1)S(1)}, u32[]{:S(2)}, u32[]{:S(2)}) collective-permute-start(bf16[64,3584]{1,0:T(8,128)(2,1)S(1)} %bitcast.7), channel_id=1, source_target_pairs={{0,2},{1,3},{4,0},{5,1},{8,4},{9,5},{12,8},{13,9},{14,12},{15,13},... | collective-permute-start | bytes 1376264 | tf_op jit(solution)/shard_map/ppermute | solution.py:79
  78.3 6.8 %collective-permute-start.21 = (bf16[64,3584]{1,0:T(8,128)(2,1)S(1)}, bf16[64,3584]{1,0:T(8,128)(2,1)S(1)}, u32[]{:S(2)}, u32[]{:S(2)}) collective-permute-start(bf16[64,3584]{1,0:T(8,128)(2,1)S(1)} %bitcast.8), channel_id=1, source_target_pairs={{0,1},{1,0},{2,3},{3,2},{4,5},{5,4},{6,7},{7,6},{8,9},{9,8},{10,11... | collective-permute-start | bytes 1376264 | tf_op jit(solution)/shard_map/ppermute | solution.py:37
  82.5 10.7 %collective-permute-start.19 = (bf16[64,3584]{1,0:T(8,128)(2,1)S(1)}, bf16[64,3584]{1,0:T(8,128)(2,1)S(1)}, u32[]{:S(2)}, u32[]{:S(2)}) collective-permute-start(bf16[64,3584]{1,0:T(8,128)(2,1)S(1)} %collective-permute-done.18.refs_0_), channel_id=1, source_target_pairs={{0,4},{1,5},{4,8},{5,9},{8,12},{9,13},{12,14},{13,15},{14,10},{15,... | collective-permute-start | bytes 1376264 | tf_op jit(solution)/shard_map/ppermute | solution.py:79
  82.8 10.7 %collective-permute-start.23 = (bf16[64,3584]{1,0:T(8,128)(2,1)S(1)}, bf16[64,3584]{1,0:T(8,128)(2,1)S(1)}, u32[]{:S(2)}, u32[]{:S(2)}) collective-permute-start(bf16[64,3584]{1,0:T(8,128)(2,1)S(1)} %collective-permute-done.20.refs_1_), channel_id=1, source_target_pairs={{0,2},{1,3},{4,0},{5,1},{8,4},{9,5},{12,8},{13,9},{14,12},{15,13},... | collective-permute-start | bytes 1376264 | tf_op jit(solution)/shard_map/ppermute | solution.py:79
  84.5 10.7 %collective-permute-start.25 = (bf16[64,3584]{1,0:T(8,128)(2,1)S(1)}, bf16[64,3584]{1,0:T(8,128)(2,1)S(1)}, u32[]{:S(2)}, u32[]{:S(2)}) collective-permute-start(bf16[64,3584]{1,0:T(8,128)(2,1)S(1)} %collective-permute-done.20.refs_1_), channel_id=1, source_target_pairs={{0,1},{1,0},{2,3},{3,2},{4,5},{5,4},{6,7},{7,6},{8,9},{9,8},{10,11... | collective-permute-start | bytes 1376264 | tf_op jit(solution)/shard_map/ppermute | solution.py:37
  84.5 11.2 %collective-permute-start.24 = (bf16[64,3584]{1,0:T(8,128)(2,1)S(1)}, bf16[64,3584]{1,0:T(8,128)(2,1)S(1)}, u32[]{:S(2)}, u32[]{:S(2)}) collective-permute-start(bf16[64,3584]{1,0:T(8,128)(2,1)S(1)} %collective-permute-done.18.refs_0_), channel_id=1, source_target_pairs={{0,1},{1,0},{2,3},{3,2},{4,5},{5,4},{6,7},{7,6},{8,9},{9,8},{10,11... | collective-permute-start | bytes 1376264 | tf_op jit(solution)/shard_map/ppermute | solution.py:37
  93.2 10.6 %collective-permute-start.22 = (bf16[64,3584]{1,0:T(8,128)(2,1)S(1)}, bf16[64,3584]{1,0:T(8,128)(2,1)S(1)}, u32[]{:S(2)}, u32[]{:S(2)}) collective-permute-start(bf16[64,3584]{1,0:T(8,128)(2,1)S(1)} %collective-permute-done.19.refs_0_), channel_id=1, source_target_pairs={{0,4},{1,5},{4,8},{5,9},{8,12},{9,13},{12,14},{13,15},{14,10},{15,... | collective-permute-start | bytes 1376264 | tf_op jit(solution)/shard_map/ppermute | solution.py:79
  93.5 10.6 %collective-permute-start.27 = (bf16[64,3584]{1,0:T(8,128)(2,1)S(1)}, bf16[64,3584]{1,0:T(8,128)(2,1)S(1)}, u32[]{:S(2)}, u32[]{:S(2)}) collective-permute-start(bf16[64,3584]{1,0:T(8,128)(2,1)S(1)} %collective-permute-done.23.refs_1_), channel_id=1, source_target_pairs={{0,2},{1,3},{4,0},{5,1},{8,4},{9,5},{12,8},{13,9},{14,12},{15,13},... | collective-permute-start | bytes 1376264 | tf_op jit(solution)/shard_map/ppermute | solution.py:79
  95.2 10.8 %collective-permute-start.31 = (bf16[64,3584]{1,0:T(8,128)(2,1)S(1)}, bf16[64,3584]{1,0:T(8,128)(2,1)S(1)}, u32[]{:S(2)}, u32[]{:S(2)}) collective-permute-start(bf16[64,3584]{1,0:T(8,128)(2,1)S(1)} %collective-permute-done.23.refs_1_), channel_id=1, source_target_pairs={{0,1},{1,0},{2,3},{3,2},{4,5},{5,4},{6,7},{7,6},{8,9},{9,8},{10,11... | collective-permute-start | bytes 1376264 | tf_op jit(solution)/shard_map/ppermute | solution.py:37
  95.2 11.3 %collective-permute-start.30 = (bf16[64,3584]{1,0:T(8,128)(2,1)S(1)}, bf16[64,3584]{1,0:T(8,128)(2,1)S(1)}, u32[]{:S(2)}, u32[]{:S(2)}) collective-permute-start(bf16[64,3584]{1,0:T(8,128)(2,1)S(1)} %collective-permute-done.19.refs_0_), channel_id=1, source_target_pairs={{0,1},{1,0},{2,3},{3,2},{4,5},{5,4},{6,7},{7,6},{8,9},{9,8},{10,11... | collective-permute-start | bytes 1376264 | tf_op jit(solution)/shard_map/ppermute | solution.py:37
  103.8 6.1 %collective-permute-start.29 = (bf16[64,1792]{1,0:T(8,128)(2,1)S(1)}, bf16[64,1792]{1,0:T(8,128)(2,1)S(1)}, u32[]{:S(2)}, u32[]{:S(2)}) collective-permute-start(bf16[64,1792]{1,0:T(8,128)(2,1)S(1)} %slice.126), channel_id=1, source_target_pairs={{0,4},{1,5},{4,8},{5,9},{8,12},{9,13},{12,14},{13,15},{14,10},{15,... | collective-permute-start | bytes 688136 | tf_op jit(solution)/shard_map/ppermute | solution.py:79
  104.2 6.1 %collective-permute-start.33 = (bf16[64,1792]{1,0:T(8,128)(2,1)S(1)}, bf16[64,1792]{1,0:T(8,128)(2,1)S(1)}, u32[]{:S(2)}, u32[]{:S(2)}) collective-permute-start(bf16[64,1792]{1,0:T(8,128)(2,1)S(1)} %slice.127), channel_id=1, source_target_pairs={{0,2},{1,3},{4,0},{5,1},{8,4},{9,5},{12,8},{13,9},{14,12},{15,13},... | collective-permute-start | bytes 688136 | tf_op jit(solution)/shard_map/ppermute | solution.py:79
  106.0 5.8 %collective-permute-start.28 = (bf16[64,3584]{1,0:T(8,128)(2,1)S(1)}, bf16[64,3584]{1,0:T(8,128)(2,1)S(1)}, u32[]{:S(2)}, u32[]{:S(2)}) collective-permute-start(bf16[64,3584]{1,0:T(8,128)(2,1)S(1)} %collective-permute-done.27.refs_1_), channel_id=1, source_target_pairs={{0,1},{1,0},{2,3},{3,2},{4,5},{5,4},{6,7},{7,6},{8,9},{9,8},{10,11... | collective-permute-start | bytes 1376264 | tf_op jit(solution)/shard_map/ppermute | solution.py:37
  106.0 5.8 %collective-permute-start.26 = (bf16[64,3584]{1,0:T(8,128)(2,1)S(1)}, bf16[64,3584]{1,0:T(8,128)(2,1)S(1)}, u32[]{:S(2)}, u32[]{:S(2)}) collective-permute-start(bf16[64,3584]{1,0:T(8,128)(2,1)S(1)} %collective-permute-done.22.refs_0_), channel_id=1, source_target_pairs={{0,1},{1,0},{2,3},{3,2},{4,5},{5,4},{6,7},{7,6},{8,9},{9,8},{10,11... | collective-permute-start | bytes 1376264 | tf_op jit(solution)/shard_map/ppermute | solution.py:37
  (15 other events, 236.2 us)

commit v12 on v11

--- a/solution.py
+++ b/solution.py
@@ -134,8 +134,9 @@
     return (code + jnp.where(code < 0, -0.5, 0.5)).astype(jnp.int32)
 
 
-def stream_kernel(size, rows, coef_ref, right_hbm, *refs):
-    outs, (right, by_latent, by_slot, stage, sems_in, sems_out) = refs[:4], refs[4:]
+def stream_kernel(size, rows, coef_hbm, right_hbm, *refs):
+    outs, near_left, refs = refs[:2], refs[2], refs[3:]
+    coef, right, by_latent, left, near_rows, stage, sems_left, sems_in, sems_out = refs
     tokens, width = right.shape
     part = outs[0].shape[0]
     pieces, cuts = sems_in.shape
@@ -154,49 +155,55 @@
         for group, out in enumerate(outs):
             source = stage.at[pl.ds(group * part, part), columns]
             writes.append(pltpu.make_async_copy(source, out.at[:, columns], sems_out.at[i, group]))
+    read_coef = pltpu.make_async_copy(coef_hbm, coef, sems_left.at[0])
+    write_near = pltpu.make_async_copy(near_rows, near_left, sems_left.at[1])
+    read_coef.start()
     for read in sum(reads, []):
         read.start()
-    by_latent[...] = coef_ref[...].T
-    far_rows = by_slot.shape[0] // 2
-    ordered_rows(
-        size, rows, by_latent, (by_slot.at[pl.ds(0, far_rows)], by_slot.at[pl.ds(far_rows, far_rows)])
-    )
+    read_coef.wait()
+    by_latent[...] = coef[...].T
+    ordered_rows(size, rows, by_latent, (left, near_rows))
+    write_near.start()
     for i in range(pieces):
         for read in reads[i]:
             read.wait()
         columns = slice(i * tile, (i + 1) * tile)
-        out = jnp.dot(by_slot[...], right[:, columns], preferred_element_type=jnp.float32)
+        out = jnp.dot(left[...], right[:, columns], preferred_element_type=jnp.float32)
         stage[:, columns] = out.astype(stage.dtype)
-        for write in writes[4 * i : 4 * i + 4]:
+        for write in writes[2 * i : 2 * i + 2]:
             write.start()
-    for write in writes:
+    for write in writes + [write_near]:
         write.wait()
 
 
-def stream_product(coef, right, size, rows):
+def stream_far_product(coef, right, size, rows):
     tokens, latents = coef.shape
     width = right.shape[1]
-    part = latents // 4
+    part, half = latents // 4, latents // 2
     pieces, cuts = 4, 4
     anywhere = pl.BlockSpec(memory_space=pl.ANY)
     return pl.pallas_call(
         functools.partial(stream_kernel, size, rows),
-        in_specs=[pl.BlockSpec(memory_space=pltpu.VMEM), anywhere],
-        out_specs=[anywhere] * 4,
-        out_shape=[jax.ShapeDtypeStruct((part, width), coef.dtype)] * 4,
+        in_specs=[anywhere] * 2,
+        out_specs=[anywhere] * 3,
+        out_shape=[jax.ShapeDtypeStruct((part, width), coef.dtype)] * 2
+        + [jax.ShapeDtypeStruct((half, tokens), coef.dtype)],
         scratch_shapes=[
+            pltpu.VMEM((tokens, latents), coef.dtype),
             pltpu.VMEM((tokens, width), coef.dtype),
             pltpu.VMEM((latents, tokens), coef.dtype),
-            pltpu.VMEM((latents, tokens), coef.dtype),
-            pltpu.VMEM((latents, width), coef.dtype),
+            pltpu.VMEM((half, tokens), coef.dtype),
+            pltpu.VMEM((half, tokens), coef.dtype),
+            pltpu.VMEM((half, width), coef.dtype),
+            pltpu.SemaphoreType.DMA((2,)),
             pltpu.SemaphoreType.DMA((pieces, cuts)),
-            pltpu.SemaphoreType.DMA((pieces, 4)),
+            pltpu.SemaphoreType.DMA((pieces, 2)),
         ],
-        compiler_params=params(50),
+        compiler_params=params(52),
         cost_estimate=cost(
-            2 * latents * tokens * width, 2 * (tokens * width + latents * (tokens + width))
+            latents * tokens * width, 2 * (tokens * width + latents * tokens) + latents * width
         ),
-        name="product",
+        name="stream_far_product",
     )(coef, right)
 
 
@@ -248,7 +255,7 @@
         scratch_shapes=scratch,
         compiler_params=params(20),
         cost_estimate=cost(
-            4 * part * tokens * width, 2 * (tokens * width + 2 * part * (tokens + width))
+            12 * part * tokens * width, 2 * (tokens * width + 2 * part * (tokens + width))
         ),
         name=name,
     )(left, right, *others)
@@ -414,12 +421,11 @@
     chips = size // 2
     stages = gather_table(jnp.concatenate([send_count, dead_order], axis=1), size)
     table = stages[-1]
-    dec = stream_product(latent_act, out_grad, size, rows)
-    dec_far = after(dec[0], *stages[0])
-    dec_kept = [dec[1], dec[3]]
-    dec_core = [swap(dec_far, 1, size), swap(after(dec[2], table[0]), 1, size)]
+    dec_sent, kept, dec_left = stream_far_product(latent_act, out_grad, size, rows)
+    dec_sent = after(dec_sent, *stages[0])
+    dec_kept, dec_core = [kept], [swap(dec_sent, 1, size)]
     enc_sent, kept, enc_left, code = far_product(
-        enc_coef, x_rows, size, rows, pick_rows[0].T, table
+        after(enc_coef, dec_sent), x_rows, size, rows, pick_rows[0].T, table
     )
     enc_kept, enc_core = [kept], [swap(enc_sent, 1, size)]
 
@@ -445,6 +451,10 @@
                 value = lax.pad(value, jnp.float32(0), pads)
             moving.append((value + both(2 * hop - side)).astype(jnp.bfloat16))
         came = travel(moving)
+        if hop == 1:
+            dec_sent, kept = near_product(after(dec_left, *moving), out_grad)
+            dec_kept.append(kept)
+            dec_core.append(swap(dec_sent, 1, size))
     states = (enc_w, enc_m, enc_v, dec_w, dec_m, dec_v)
     parts = ([enc_kept[1], enc_core[1]], [dec_kept[1], dec_core[1]], came)
     (blocks,) = update(code, states, *parts, True)

time: 113 us -> 113 us (level)
  waiting for transfers between devices: 55.4 us -> 51.6 us
  Pallas kernels: 27.7 us -> 30.6 us
    ppermute x16, waiting for transfers between devices: 48.9 us -> 44.8 us  [shift(): return lax.ppermute(value, 'latent', pairs)]
    pallas_call x2 -> x3, Pallas kernels: 8.71 us -> 12.4 us  [product(): pl.pallas_call(kernel, grid=(width // tile,), in_specs=in_specs + [pl.Blo...]
  transfers between devices with their start and end apart: 35 -> 35, of which waited for: 18 -> 19; matrix products, arithmetic and copies ran while one was open for 1% -> 1% of each run, Pallas kernels for 22% -> 25%
where the time goes in v12:
time: 113 us
  waiting for transfers between devices  51.6 us (46%)
  Pallas kernels  30.6 us (27%)
  starting transfers between devices  27.3 us (24%)
  other arithmetic  2.08 us (2%)
    ppermute x16, waiting for transfers between devices, shift(): return lax.ppermute(value, 'latent', pairs)  44.8 us
    ppermute x16, starting transfers between devices, shift(): return lax.ppermute(value, 'latent', pairs)  16.9 us
    pallas_call x3, Pallas kernels, product(): pl.pallas_call(kernel, grid=(width // tile,), in_specs=in_specs + [pl.Blo...  12.4 us
    ppermute x19, starting transfers between devices, swap(): return lax.ppermute(value, 'latent', [(i, i ^ bits) for i in range(size)])  10.3 us
    pallas_call x1, Pallas kernels, stream_far_product(): pl.pallas_call(functools.partial(stream_kernel, size, rows), in_specs=[an...  7.65 us
    ppermute x19, waiting for transfers between devices, swap(): return lax.ppermute(value, 'latent', [(i, i ^ bits) for i in range(size)])  6.79 us
    pallas_call x6, Pallas kernels, place(): pl.pallas_call(functools.partial(place_kernel, plan, size, rows, count),...  6.39 us
    pallas_call x2, Pallas kernels, update(): pl.pallas_call(blocks_kernel if blocks_only else states_kernel, grid=(row...  4.18 us
  transfers between devices with their start and end apart: 35, of which 19 were waited for; matrix products, arithmetic and copies ran while one was open for 1% of the time, Pallas kernels for 25%

profile of v12, /device:TPU:0, one launch (start us, length us, event | category | flops | bytes accessed | tf_op | source)
XLA Modules:
  0.0 112.6 jit_solution(1035644511423165085)
XLA Ops:
  1.4 2.5 %collective-permute-start.2 = (s32[1,48]{1,0:T(1,128)S(1)}, s32[1,48]{1,0:T(1,128)S(1)}, u32[]{:S(2)}, u32[]{:S(2)}) collective-permute-start(s32[1,48]{1,0:T(1,128)S(1)} %pad_add_fusion.1), channel_id=1, source_target_pairs={{0,3},{1,2},{2,1},{3,0},{4,7},{5,6},{6,5},{7,4},{8,11},{9,10},{10,... | collective-permute-start | bytes 584 | tf_op jit(solution)/shard_map/ppermute | solution.py:37
  4.6 7.6 %stream_far_product.1 = (bf16[128,3584]{1,0:T(8,128)(2,1)S(1)}, bf16[128,3584]{1,0:T(8,128)(2,1)}, bf16[256,1024]{1,0:T(8,128)(2,1)S(1)}) custom-call(bf16[1024,512]{1,0:T(8,128)(2,1)} %coef_hbm.1, bf16[1024,3584]{1,0:T(8,128)(2,1)} %right_ref.5), custom_call_target="tpu_custom_call" | custom-call | flops 1879048192 | bytes 10223616 | tf_op jit(solution)/shard_map/stream_far_product/pallas_call | solution.py:185
  12.9 3.9 %collective-permute-start.5 = (s32[4,48]{1,0:T(4,128)S(1)}, s32[4,48]{1,0:T(4,128)S(1)}, u32[]{:S(2)}, u32[]{:S(2)}) collective-permute-start(s32[4,48]{1,0:T(4,128)S(1)} %pad_add_fusion.refs_0_), channel_id=1, source_target_pairs={{0,12},{1,13},{2,14},{3,15},{4,8},{5,9},{6,10},{7,11},{8,4},{9,5},... | collective-permute-start | bytes 2312 | tf_op jit(solution)/shard_map/ppermute | solution.py:37
  18.3 2.9 %collective-permute-done.4.refs_2_ = s32[4,48]{1,0:T(4,128)S(1)} collective-permute-done((s32[4,48]{1,0:T(4,128)S(1)}, s32[4,48]{1,0:T(4,128)S(1)}, u32[]{:S(2)}, u32[]{:S(2)}) %collective-permute-start.4) | collective-permute-done | bytes 800 | tf_op jit(solution)/shard_map/ppermute | solution.py:37
  21.3 4.9 %far_product.1 = (bf16[128,3584]{1,0:T(8,128)(2,1)S(1)}, bf16[128,3584]{1,0:T(8,128)(2,1)S(1)}, bf16[256,1024]{1,0:T(8,128)(2,1)S(1)}, s32[32,1]{1,0:T(8,128)S(1)}) custom-call(bf16[1024,512]{1,0:T(8,128)(2,1)S(1)} %copy-done.7, bf16[1024,3584]{1,0:T(8,128)(2,1)S(1)} %copy-done.6, s32[2,16]{1,0:T(2,128)S(1)} %bitcast.10, s32[4,48]{1,0:T(4,128)S(1)} %pad_add_fusion.refs_0_, ...), custom_call_target="tpu_custom_call" | custom-call | flops 5637144576 | bytes 9699328 | tf_op jit(solution)/shard_map/far_product/pallas_call | solution.py:248
  26.5 2.2 %collective-permute-done.6 = bf16[128,3584]{1,0:T(8,128)(2,1)S(1)} collective-permute-done((bf16[128,3584]{1,0:T(8,128)(2,1)S(1)}, bf16[128,3584]{1,0:T(8,128)(2,1)S(1)}, u32[]{:S(2)}, u32[]{:S(2)}) %collective-permute-start.6) | collective-permute-done | bytes 917536 | tf_op jit(solution)/shard_map/ppermute | solution.py:37
  29.0 1.6 %collective-permute-start.9 = (bf16[64,1792]{1,0:T(8,128)(2,1)S(1)}, bf16[64,1792]{1,0:T(8,128)(2,1)S(1)}, u32[]{:S(2)}, u32[]{:S(2)}) collective-permute-start(bf16[64,1792]{1,0:T(8,128)(2,1)S(1)} %get-tuple-element.140), channel_id=1, source_target_pairs={{0,2},{1,3},{4,0},{5,1},{8,4},{9,5},{12,8},{13,9},{14,12},{15,13},... | collective-permute-start | bytes 688136 | tf_op jit(solution)/shard_map/ppermute | solution.py:79
  31.1 3.7 %near_product.2 = (bf16[128,3584]{1,0:T(8,128)(2,1)S(1)}, bf16[128,3584]{1,0:T(8,128)(2,1)S(1)}) custom-call(bf16[256,1024]{1,0:T(8,128)(2,1)S(1)} %get-tuple-element.75.left_ref, bf16[1024,3584]{1,0:T(8,128)(2,1)S(1)} %copy-done.6), custom_call_target="tpu_custom_call" | custom-call | flops 5637144576 | bytes 9699328 | tf_op jit(solution)/shard_map/near_product/pallas_call | solution.py:248
  34.8 1.9 %collective-permute-done.9 = bf16[64,1792]{1,0:T(8,128)(2,1)S(1)} collective-permute-done((bf16[64,1792]{1,0:T(8,128)(2,1)S(1)}, bf16[64,1792]{1,0:T(8,128)(2,1)S(1)}, u32[]{:S(2)}, u32[]{:S(2)}) %collective-permute-start.9) | collective-permute-done | bytes 229408 | tf_op jit(solution)/shard_map/ppermute | solution.py:79
  36.7 1.2 %collective-permute-done.8 = bf16[64,1792]{1,0:T(8,128)(2,1)S(1)} collective-permute-done((bf16[64,1792]{1,0:T(8,128)(2,1)S(1)}, bf16[64,1792]{1,0:T(8,128)(2,1)S(1)}, u32[]{:S(2)}, u32[]{:S(2)}) %collective-permute-start.8) | collective-permute-done | bytes 229408 | tf_op jit(solution)/shard_map/ppermute | solution.py:79
  38.7 1.6 %collective-permute-start.15 = (bf16[64,3584]{1,0:T(8,128)(2,1)S(1)}, bf16[64,3584]{1,0:T(8,128)(2,1)S(1)}, u32[]{:S(2)}, u32[]{:S(2)}) collective-permute-start(bf16[64,3584]{1,0:T(8,128)(2,1)S(1)} %fusion.1), channel_id=1, source_target_pairs={{0,2},{1,3},{4,0},{5,1},{8,4},{9,5},{12,8},{13,9},{14,12},{15,13},... | collective-permute-start | bytes 1376264 | tf_op jit(solution)/shard_map/ppermute | solution.py:79
  40.3 3.7 %near_product.3 = (bf16[128,3584]{1,0:T(8,128)(2,1)S(1)}, bf16[128,3584]{1,0:T(8,128)(2,1)S(1)}) custom-call(bf16[256,1024]{1,0:T(8,128)(2,1)S(1)} %get-tuple-element.82.left_ref, bf16[1024,3584]{1,0:T(8,128)(2,1)S(1)} %bitcast.5), custom_call_target="tpu_custom_call" | custom-call | flops 5637144576 | bytes 9699328 | tf_op jit(solution)/shard_map/near_product/pallas_call | solution.py:248
  44.5 5.3 %collective-permute-done.15 = bf16[64,3584]{1,0:T(8,128)(2,1)S(1)} collective-permute-done((bf16[64,3584]{1,0:T(8,128)(2,1)S(1)}, bf16[64,3584]{1,0:T(8,128)(2,1)S(1)}, u32[]{:S(2)}, u32[]{:S(2)}) %collective-permute-start.15) | collective-permute-done | bytes 458784 | tf_op jit(solution)/shard_map/ppermute | solution.py:79
  49.9 1.6 %collective-permute-start.16 = (bf16[64,3584]{1,0:T(8,128)(2,1)S(1)}, bf16[64,3584]{1,0:T(8,128)(2,1)S(1)}, u32[]{:S(2)}, u32[]{:S(2)}) collective-permute-start(bf16[64,3584]{1,0:T(8,128)(2,1)S(1)} %fusion.4), channel_id=1, source_target_pairs={{0,2},{1,3},{4,0},{5,1},{8,4},{9,5},{12,8},{13,9},{14,12},{15,13},... | collective-permute-start | bytes 1376264 | tf_op jit(solution)/shard_map/ppermute | solution.py:79
  52.6 7.8 %collective-permute-done.16 = bf16[64,3584]{1,0:T(8,128)(2,1)S(1)} collective-permute-done((bf16[64,3584]{1,0:T(8,128)(2,1)S(1)}, bf16[64,3584]{1,0:T(8,128)(2,1)S(1)}, u32[]{:S(2)}, u32[]{:S(2)}) %collective-permute-start.16) | collective-permute-done | bytes 458784 | tf_op jit(solution)/shard_map/ppermute | solution.py:79
  60.5 1.7 %collective-permute-start.17 = (bf16[64,3584]{1,0:T(8,128)(2,1)S(1)}, bf16[64,3584]{1,0:T(8,128)(2,1)S(1)}, u32[]{:S(2)}, u32[]{:S(2)}) collective-permute-start(bf16[64,3584]{1,0:T(8,128)(2,1)S(1)} %fusion.5), channel_id=1, source_target_pairs={{0,2},{1,3},{4,0},{5,1},{8,4},{9,5},{12,8},{13,9},{14,12},{15,13},... | collective-permute-start | bytes 1376264 | tf_op jit(solution)/shard_map/ppermute | solution.py:79
  63.3 6.8 %collective-permute-done.17.refs_10_.refs_14_ = bf16[64,3584]{1,0:T(8,128)(2,1)S(1)} collective-permute-done((bf16[64,3584]{1,0:T(8,128)(2,1)S(1)}, bf16[64,3584]{1,0:T(8,128)(2,1)S(1)}, u32[]{:S(2)}, u32[]{:S(2)}) %collective-permute-start.17) | collective-permute-done | bytes 458784 | tf_op jit(solution)/shard_map/ppermute | solution.py:79
  70.0 1.8 %collective-permute-done.14.refs_9_.refs_13_ = bf16[64,3584]{1,0:T(8,128)(2,1)S(1)} collective-permute-done((bf16[64,3584]{1,0:T(8,128)(2,1)S(1)}, bf16[64,3584]{1,0:T(8,128)(2,1)S(1)}, u32[]{:S(2)}, u32[]{:S(2)}) %collective-permute-start.14) | collective-permute-done | bytes 458784 | tf_op jit(solution)/shard_map/ppermute | solution.py:79
  71.9 1.6 %blocks.1 = bf16[2,32,3584]{2,1,0:T(8,128)(2,1)S(1)} custom-call(s32[32,1]{1,0:T(8,128)S(1)} %get-tuple-element.70.refs_0_, f32[32,3584]{1,0:T(8,128)S(1)} %copy-done, f32[32,3584]{1,0:T(8,128)S(1)} %copy-done.1, f32[32,3584]{1,0:T(8,128)S(1)} %copy-done.2, f32[32,3584]{1,0:T(8,128)S(1)} %copy-done.3, f32[32,3584]{1,0:T(8,128)S(1)} %copy-done.4, ...), custom_call_target="tpu_custom_call" | custom-call | flops 1146880 | bytes 1146880 | tf_op jit(solution)/shard_map/blocks/pallas_call | solution.py:333
  74.0 1.5 %collective-permute-start.20 = (bf16[64,3584]{1,0:T(8,128)(2,1)S(1)}, bf16[64,3584]{1,0:T(8,128)(2,1)S(1)}, u32[]{:S(2)}, u32[]{:S(2)}) collective-permute-start(bf16[64,3584]{1,0:T(8,128)(2,1)S(1)} %bitcast.7), channel_id=1, source_target_pairs={{0,2},{1,3},{4,0},{5,1},{8,4},{9,5},{12,8},{13,9},{14,12},{15,13},... | collective-permute-start | bytes 1376264 | tf_op jit(solution)/shard_map/ppermute | solution.py:79
  75.6 2.6 %states.1 = (f32[32,3584]{1,0:T(8,128)}, f32[32,3584]{1,0:T(8,128)}, f32[32,3584]{1,0:T(8,128)}, f32[32,3584]{1,0:T(8,128)}, f32[32,3584]{1,0:T(8,128)}, /*index=5*/f32[32,3584]{1,0:T(8,128)}) custom-call(s32[32,1]{1,0:T(8,128)S(1)} %get-tuple-element.70.refs_0_, f32[32,3584]{1,0:T(8,128)S(1)} %copy-done, f32[32,3584]{1,0:T(8,128)S(1)} %copy-done.1, ...), custom_call_target="tpu_custom_call" | custom-call | flops 1146880 | bytes 1146880 | tf_op jit(solution)/shard_map/states/pallas_call | solution.py:333
  78.9 3.1 %collective-permute-done.18.refs_0_ = bf16[64,3584]{1,0:T(8,128)(2,1)S(1)} collective-permute-done((bf16[64,3584]{1,0:T(8,128)(2,1)S(1)}, bf16[64,3584]{1,0:T(8,128)(2,1)S(1)}, u32[]{:S(2)}, u32[]{:S(2)}) %collective-permute-start.18) | collective-permute-done | bytes 458784 | tf_op jit(solution)/shard_map/ppermute | solution.py:79
  82.6 1.5 %collective-permute-start.23 = (bf16[64,3584]{1,0:T(8,128)(2,1)S(1)}, bf16[64,3584]{1,0:T(8,128)(2,1)S(1)}, u32[]{:S(2)}, u32[]{:S(2)}) collective-permute-start(bf16[64,3584]{1,0:T(8,128)(2,1)S(1)} %collective-permute-done.20.refs_1_), channel_id=1, source_target_pairs={{0,2},{1,3},{4,0},{5,1},{8,4},{9,5},{12,8},{13,9},{14,12},{15,13},... | collective-permute-start | bytes 1376264 | tf_op jit(solution)/shard_map/ppermute | solution.py:79
  84.7 1.1 place.7
  85.8 6.9 %collective-permute-done.19.refs_0_ = bf16[64,3584]{1,0:T(8,128)(2,1)S(1)} collective-permute-done((bf16[64,3584]{1,0:T(8,128)(2,1)S(1)}, bf16[64,3584]{1,0:T(8,128)(2,1)S(1)}, u32[]{:S(2)}, u32[]{:S(2)}) %collective-permute-start.19) | collective-permute-done | bytes 458784 | tf_op jit(solution)/shard_map/ppermute | solution.py:79
  93.3 1.5 %collective-permute-start.27 = (bf16[64,3584]{1,0:T(8,128)(2,1)S(1)}, bf16[64,3584]{1,0:T(8,128)(2,1)S(1)}, u32[]{:S(2)}, u32[]{:S(2)}) collective-permute-start(bf16[64,3584]{1,0:T(8,128)(2,1)S(1)} %collective-permute-done.23.refs_1_), channel_id=1, source_target_pairs={{0,2},{1,3},{4,0},{5,1},{8,4},{9,5},{12,8},{13,9},{14,12},{15,13},... | collective-permute-start | bytes 1376264 | tf_op jit(solution)/shard_map/ppermute | solution.py:79
  95.4 1.3 %place.8 = (bf16[512,3584]{1,0:T(8,128)(2,1)}, bf16[512,3584]{1,0:T(8,128)(2,1)}) custom-call(bf16[64,3584]{1,0:T(8,128)(2,1)S(1)} %collective-permute-done.19.refs_0_, bf16[64,3584]{1,0:T(8,128)(2,1)S(1)} %collective-permute-done.23.refs_1_, bf16[64,3584]{1,0:T(8,128)(2,1)S(1)} %collective-permute-done.24.refs_2_, ...), custom_call_target="tpu_custom_call", output_to_operand_aliasing={{0}: (4, {}), {1}: (5, {})} | custom-call | bytes 3670016 | tf_op jit(solution)/shard_map/place/pallas_call | solution.py:368
  96.7 6.7 %collective-permute-done.22.refs_0_ = bf16[64,3584]{1,0:T(8,128)(2,1)S(1)} collective-permute-done((bf16[64,3584]{1,0:T(8,128)(2,1)S(1)}, bf16[64,3584]{1,0:T(8,128)(2,1)S(1)}, u32[]{:S(2)}, u32[]{:S(2)}) %collective-permute-start.22) | collective-permute-done | bytes 458784 | tf_op jit(solution)/shard_map/ppermute | solution.py:79
  103.9 1.6 %collective-permute-start.33 = (bf16[64,1792]{1,0:T(8,128)(2,1)S(1)}, bf16[64,1792]{1,0:T(8,128)(2,1)S(1)}, u32[]{:S(2)}, u32[]{:S(2)}) collective-permute-start(bf16[64,1792]{1,0:T(8,128)(2,1)S(1)} %slice.127), channel_id=1, source_target_pairs={{0,2},{1,3},{4,0},{5,1},{8,4},{9,5},{12,8},{13,9},{14,12},{15,13},... | collective-permute-start | bytes 688136 | tf_op jit(solution)/shard_map/ppermute | solution.py:79
  106.0 1.3 %place.9 = (bf16[512,3584]{1,0:T(8,128)(2,1)}, bf16[512,3584]{1,0:T(8,128)(2,1)}) custom-call(bf16[64,3584]{1,0:T(8,128)(2,1)S(1)} %collective-permute-done.22.refs_0_, bf16[64,3584]{1,0:T(8,128)(2,1)S(1)} %collective-permute-done.27.refs_1_, bf16[64,3584]{1,0:T(8,128)(2,1)S(1)} %collective-permute-done.30.refs_2_, ...), custom_call_target="tpu_custom_call", output_to_operand_aliasing={{0}: (4, {}), {1}: (5, {})} | custom-call | bytes 3670016 | tf_op jit(solution)/shard_map/place/pallas_call | solution.py:368
  107.3 2.1 %collective-permute-done.29.refs_0_ = bf16[64,1792]{1,0:T(8,128)(2,1)S(1)} collective-permute-done((bf16[64,1792]{1,0:T(8,128)(2,1)S(1)}, bf16[64,1792]{1,0:T(8,128)(2,1)S(1)}, u32[]{:S(2)}, u32[]{:S(2)}) %collective-permute-start.29) | collective-permute-done | bytes 229408 | tf_op jit(solution)/shard_map/ppermute | solution.py:79
  111.5 1.1 %place.11 = (bf16[512,3584]{1,0:T(8,128)(2,1)}, bf16[512,3584]{1,0:T(8,128)(2,1)}) custom-call(bf16[64,3584]{1,0:T(8,128)(2,1)S(1)} %collective-permute-done.26.refs_0_, bf16[64,3584]{1,0:T(8,128)(2,1)S(1)} %collective-permute-done.28.refs_1_, bf16[64,1792]{1,0:T(8,128)(2,1)S(1)} %collective-permute-done.32.refs_2_, ...), custom_call_target="tpu_custom_call", output_to_operand_aliasing={{0}: (4, {}), {1}: (5, {})} | custom-call | bytes 3670016 | tf_op jit(solution)/shard_map/place/pallas_call | solution.py:368
  (94 shorter events, 15.0 us)
Async XLA Ops:
  1.4 10.8 %collective-permute-start.2 = (s32[1,48]{1,0:T(1,128)S(1)}, s32[1,48]{1,0:T(1,128)S(1)}, u32[]{:S(2)}, u32[]{:S(2)}) collective-permute-start(s32[1,48]{1,0:T(1,128)S(1)} %pad_add_fusion.1), channel_id=1, source_target_pairs={{0,3},{1,2},{2,1},{3,0},{4,7},{5,6},{6,5},{7,4},{8,11},{9,10},{10,... | collective-permute-start | bytes 584 | tf_op jit(solution)/shard_map/ppermute | solution.py:37
  3.9 8.3 %collective-permute-start.1 = (s32[1,48]{1,0:T(1,128)S(1)}, s32[1,48]{1,0:T(1,128)S(1)}, u32[]{:S(2)}, u32[]{:S(2)}) collective-permute-start(s32[1,48]{1,0:T(1,128)S(1)} %pad_add_fusion.1), channel_id=1, source_target_pairs={{0,2},{1,3},{2,0},{3,1},{4,6},{5,7},{6,4},{7,5},{8,10},{9,11},{10,... | collective-permute-start | bytes 584 | tf_op jit(solution)/shard_map/ppermute | solution.py:37
  4.6 7.7 %collective-permute-start = (s32[1,48]{1,0:T(1,128)S(1)}, s32[1,48]{1,0:T(1,128)S(1)}, u32[]{:S(2)}, u32[]{:S(2)}) collective-permute-start(s32[1,48]{1,0:T(1,128)S(1)} %pad_add_fusion.1), channel_id=1, source_target_pairs={{0,1},{1,0},{2,3},{3,2},{4,5},{5,4},{6,7},{7,6},{8,9},{9,8},{10,11... | collective-permute-start | bytes 584 | tf_op jit(solution)/shard_map/ppermute | solution.py:37
  12.3 14.0 %collective-permute-start.7 = (bf16[128,3584]{1,0:T(8,128)(2,1)S(1)}, bf16[128,3584]{1,0:T(8,128)(2,1)S(1)}, u32[]{:S(2)}, u32[]{:S(2)}) collective-permute-start(bf16[128,3584]{1,0:T(8,128)(2,1)S(1)} %get-tuple-element.68), channel_id=1, source_target_pairs={{0,1},{1,0},{2,3},{3,2},{4,5},{5,4},{6,7},{7,6},{8,9},{9,8},{10,11... | collective-permute-start | bytes 2752520 | tf_op jit(solution)/shard_map/ppermute | solution.py:37
  12.9 5.4 %collective-permute-start.5 = (s32[4,48]{1,0:T(4,128)S(1)}, s32[4,48]{1,0:T(4,128)S(1)}, u32[]{:S(2)}, u32[]{:S(2)}) collective-permute-start(s32[4,48]{1,0:T(4,128)S(1)} %pad_add_fusion.refs_0_), channel_id=1, source_target_pairs={{0,12},{1,13},{2,14},{3,15},{4,8},{5,9},{6,10},{7,11},{8,4},{9,5},... | collective-permute-start | bytes 2312 | tf_op jit(solution)/shard_map/ppermute | solution.py:37
  16.8 4.5 %collective-permute-start.4 = (s32[4,48]{1,0:T(4,128)S(1)}, s32[4,48]{1,0:T(4,128)S(1)}, u32[]{:S(2)}, u32[]{:S(2)}) collective-permute-start(s32[4,48]{1,0:T(4,128)S(1)} %pad_add_fusion.refs_0_), channel_id=1, source_target_pairs={{0,8},{1,9},{2,10},{3,11},{4,12},{5,13},{6,14},{7,15},{8,0},{9,1},... | collective-permute-start | bytes 2312 | tf_op jit(solution)/shard_map/ppermute | solution.py:37
  16.8 4.5 %collective-permute-start.3 = (s32[4,48]{1,0:T(4,128)S(1)}, s32[4,48]{1,0:T(4,128)S(1)}, u32[]{:S(2)}, u32[]{:S(2)}) collective-permute-start(s32[4,48]{1,0:T(4,128)S(1)} %pad_add_fusion.refs_0_), channel_id=1, source_target_pairs={{0,4},{1,5},{2,6},{3,7},{4,0},{5,1},{6,2},{7,3},{8,12},{9,13},{10,... | collective-permute-start | bytes 2312 | tf_op jit(solution)/shard_map/ppermute | solution.py:37
  29.0 7.7 %collective-permute-start.9 = (bf16[64,1792]{1,0:T(8,128)(2,1)S(1)}, bf16[64,1792]{1,0:T(8,128)(2,1)S(1)}, u32[]{:S(2)}, u32[]{:S(2)}) collective-permute-start(bf16[64,1792]{1,0:T(8,128)(2,1)S(1)} %get-tuple-element.140), channel_id=1, source_target_pairs={{0,2},{1,3},{4,0},{5,1},{8,4},{9,5},{12,8},{13,9},{14,12},{15,13},... | collective-permute-start | bytes 688136 | tf_op jit(solution)/shard_map/ppermute | solution.py:79
  30.6 7.4 %collective-permute-start.8 = (bf16[64,1792]{1,0:T(8,128)(2,1)S(1)}, bf16[64,1792]{1,0:T(8,128)(2,1)S(1)}, u32[]{:S(2)}, u32[]{:S(2)}) collective-permute-start(bf16[64,1792]{1,0:T(8,128)(2,1)S(1)} %get-tuple-element.141), channel_id=1, source_target_pairs={{0,4},{1,5},{4,8},{5,9},{8,12},{9,13},{12,14},{13,15},{14,10},{15,... | collective-permute-start | bytes 688136 | tf_op jit(solution)/shard_map/ppermute | solution.py:79
  38.0 13.9 %collective-permute-start.11 = (bf16[64,3584]{1,0:T(8,128)(2,1)S(1)}, bf16[64,3584]{1,0:T(8,128)(2,1)S(1)}, u32[]{:S(2)}, u32[]{:S(2)}) collective-permute-start(bf16[64,3584]{1,0:T(8,128)(2,1)S(1)} %fusion), channel_id=1, source_target_pairs={{0,4},{1,5},{4,8},{5,9},{8,12},{9,13},{12,14},{13,15},{14,10},{15,... | collective-permute-start | bytes 1376264 | tf_op jit(solution)/shard_map/ppermute | solution.py:79
  38.7 11.2 %collective-permute-start.15 = (bf16[64,3584]{1,0:T(8,128)(2,1)S(1)}, bf16[64,3584]{1,0:T(8,128)(2,1)S(1)}, u32[]{:S(2)}, u32[]{:S(2)}) collective-permute-start(bf16[64,3584]{1,0:T(8,128)(2,1)S(1)} %fusion.1), channel_id=1, source_target_pairs={{0,2},{1,3},{4,0},{5,1},{8,4},{9,5},{12,8},{13,9},{14,12},{15,13},... | collective-permute-start | bytes 1376264 | tf_op jit(solution)/shard_map/ppermute | solution.py:79
  40.2 11.4 %collective-permute-start.10 = (bf16[128,3584]{1,0:T(8,128)(2,1)S(1)}, bf16[128,3584]{1,0:T(8,128)(2,1)S(1)}, u32[]{:S(2)}, u32[]{:S(2)}) collective-permute-start(bf16[128,3584]{1,0:T(8,128)(2,1)S(1)} %get-tuple-element.78), channel_id=1, source_target_pairs={{0,1},{1,0},{2,3},{3,2},{4,5},{5,4},{6,7},{7,6},{8,9},{9,8},{10,11... | collective-permute-start | bytes 2752520 | tf_op jit(solution)/shard_map/ppermute | solution.py:37
  44.0 7.5 %collective-permute-start.12 = (bf16[128,3584]{1,0:T(8,128)(2,1)S(1)}, bf16[128,3584]{1,0:T(8,128)(2,1)S(1)}, u32[]{:S(2)}, u32[]{:S(2)}) collective-permute-start(bf16[128,3584]{1,0:T(8,128)(2,1)S(1)} %get-tuple-element.84), channel_id=1, source_target_pairs={{0,1},{1,0},{2,3},{3,2},{4,5},{5,4},{6,7},{7,6},{8,9},{9,8},{10,11... | collective-permute-start | bytes 2752520 | tf_op jit(solution)/shard_map/ppermute | solution.py:37
  49.9 10.5 %collective-permute-start.16 = (bf16[64,3584]{1,0:T(8,128)(2,1)S(1)}, bf16[64,3584]{1,0:T(8,128)(2,1)S(1)}, u32[]{:S(2)}, u32[]{:S(2)}) collective-permute-start(bf16[64,3584]{1,0:T(8,128)(2,1)S(1)} %fusion.4), channel_id=1, source_target_pairs={{0,2},{1,3},{4,0},{5,1},{8,4},{9,5},{12,8},{13,9},{14,12},{15,13},... | collective-permute-start | bytes 1376264 | tf_op jit(solution)/shard_map/ppermute | solution.py:79
  52.0 10.5 %collective-permute-start.13 = (bf16[64,3584]{1,0:T(8,128)(2,1)S(1)}, bf16[64,3584]{1,0:T(8,128)(2,1)S(1)}, u32[]{:S(2)}, u32[]{:S(2)}) collective-permute-start(bf16[64,3584]{1,0:T(8,128)(2,1)S(1)} %fusion.2), channel_id=1, source_target_pairs={{0,4},{1,5},{4,8},{5,9},{8,12},{9,13},{12,14},{13,15},{14,10},{15,... | collective-permute-start | bytes 1376264 | tf_op jit(solution)/shard_map/ppermute | solution.py:79
  60.5 9.5 %collective-permute-start.17 = (bf16[64,3584]{1,0:T(8,128)(2,1)S(1)}, bf16[64,3584]{1,0:T(8,128)(2,1)S(1)}, u32[]{:S(2)}, u32[]{:S(2)}) collective-permute-start(bf16[64,3584]{1,0:T(8,128)(2,1)S(1)} %fusion.5), channel_id=1, source_target_pairs={{0,2},{1,3},{4,0},{5,1},{8,4},{9,5},{12,8},{13,9},{14,12},{15,13},... | collective-permute-start | bytes 1376264 | tf_op jit(solution)/shard_map/ppermute | solution.py:79
  62.6 9.2 %collective-permute-start.14 = (bf16[64,3584]{1,0:T(8,128)(2,1)S(1)}, bf16[64,3584]{1,0:T(8,128)(2,1)S(1)}, u32[]{:S(2)}, u32[]{:S(2)}) collective-permute-start(bf16[64,3584]{1,0:T(8,128)(2,1)S(1)} %fusion.3), channel_id=1, source_target_pairs={{0,4},{1,5},{4,8},{5,9},{8,12},{9,13},{12,14},{13,15},{14,10},{15,... | collective-permute-start | bytes 1376264 | tf_op jit(solution)/shard_map/ppermute | solution.py:79
  73.5 8.5 %collective-permute-start.18 = (bf16[64,3584]{1,0:T(8,128)(2,1)S(1)}, bf16[64,3584]{1,0:T(8,128)(2,1)S(1)}, u32[]{:S(2)}, u32[]{:S(2)}) collective-permute-start(bf16[64,3584]{1,0:T(8,128)(2,1)S(1)} %bitcast.6), channel_id=1, source_target_pairs={{0,4},{1,5},{4,8},{5,9},{8,12},{9,13},{12,14},{13,15},{14,10},{15,... | collective-permute-start | bytes 1376264 | tf_op jit(solution)/shard_map/ppermute | solution.py:79
  74.0 8.6 %collective-permute-start.20 = (bf16[64,3584]{1,0:T(8,128)(2,1)S(1)}, bf16[64,3584]{1,0:T(8,128)(2,1)S(1)}, u32[]{:S(2)}, u32[]{:S(2)}) collective-permute-start(bf16[64,3584]{1,0:T(8,128)(2,1)S(1)} %bitcast.7), channel_id=1, source_target_pairs={{0,2},{1,3},{4,0},{5,1},{8,4},{9,5},{12,8},{13,9},{14,12},{15,13},... | collective-permute-start | bytes 1376264 | tf_op jit(solution)/shard_map/ppermute | solution.py:79
  78.1 6.5 %collective-permute-start.21 = (bf16[64,3584]{1,0:T(8,128)(2,1)S(1)}, bf16[64,3584]{1,0:T(8,128)(2,1)S(1)}, u32[]{:S(2)}, u32[]{:S(2)}) collective-permute-start(bf16[64,3584]{1,0:T(8,128)(2,1)S(1)} %bitcast.8), channel_id=1, source_target_pairs={{0,1},{1,0},{2,3},{3,2},{4,5},{5,4},{6,7},{7,6},{8,9},{9,8},{10,11... | collective-permute-start | bytes 1376264 | tf_op jit(solution)/shard_map/ppermute | solution.py:37
  82.0 10.7 %collective-permute-start.19 = (bf16[64,3584]{1,0:T(8,128)(2,1)S(1)}, bf16[64,3584]{1,0:T(8,128)(2,1)S(1)}, u32[]{:S(2)}, u32[]{:S(2)}) collective-permute-start(bf16[64,3584]{1,0:T(8,128)(2,1)S(1)} %collective-permute-done.18.refs_0_), channel_id=1, source_target_pairs={{0,4},{1,5},{4,8},{5,9},{8,12},{9,13},{12,14},{13,15},{14,10},{15,... | collective-permute-start | bytes 1376264 | tf_op jit(solution)/shard_map/ppermute | solution.py:79
  82.6 10.7 %collective-permute-start.23 = (bf16[64,3584]{1,0:T(8,128)(2,1)S(1)}, bf16[64,3584]{1,0:T(8,128)(2,1)S(1)}, u32[]{:S(2)}, u32[]{:S(2)}) collective-permute-start(bf16[64,3584]{1,0:T(8,128)(2,1)S(1)} %collective-permute-done.20.refs_1_), channel_id=1, source_target_pairs={{0,2},{1,3},{4,0},{5,1},{8,4},{9,5},{12,8},{13,9},{14,12},{15,13},... | collective-permute-start | bytes 1376264 | tf_op jit(solution)/shard_map/ppermute | solution.py:79
  84.2 10.7 %collective-permute-start.25 = (bf16[64,3584]{1,0:T(8,128)(2,1)S(1)}, bf16[64,3584]{1,0:T(8,128)(2,1)S(1)}, u32[]{:S(2)}, u32[]{:S(2)}) collective-permute-start(bf16[64,3584]{1,0:T(8,128)(2,1)S(1)} %collective-permute-done.20.refs_1_), channel_id=1, source_target_pairs={{0,1},{1,0},{2,3},{3,2},{4,5},{5,4},{6,7},{7,6},{8,9},{9,8},{10,11... | collective-permute-start | bytes 1376264 | tf_op jit(solution)/shard_map/ppermute | solution.py:37
  84.2 11.2 %collective-permute-start.24 = (bf16[64,3584]{1,0:T(8,128)(2,1)S(1)}, bf16[64,3584]{1,0:T(8,128)(2,1)S(1)}, u32[]{:S(2)}, u32[]{:S(2)}) collective-permute-start(bf16[64,3584]{1,0:T(8,128)(2,1)S(1)} %collective-permute-done.18.refs_0_), channel_id=1, source_target_pairs={{0,1},{1,0},{2,3},{3,2},{4,5},{5,4},{6,7},{7,6},{8,9},{9,8},{10,11... | collective-permute-start | bytes 1376264 | tf_op jit(solution)/shard_map/ppermute | solution.py:37
  92.7 10.6 %collective-permute-start.22 = (bf16[64,3584]{1,0:T(8,128)(2,1)S(1)}, bf16[64,3584]{1,0:T(8,128)(2,1)S(1)}, u32[]{:S(2)}, u32[]{:S(2)}) collective-permute-start(bf16[64,3584]{1,0:T(8,128)(2,1)S(1)} %collective-permute-done.19.refs_0_), channel_id=1, source_target_pairs={{0,4},{1,5},{4,8},{5,9},{8,12},{9,13},{12,14},{13,15},{14,10},{15,... | collective-permute-start | bytes 1376264 | tf_op jit(solution)/shard_map/ppermute | solution.py:79
  93.3 10.6 %collective-permute-start.27 = (bf16[64,3584]{1,0:T(8,128)(2,1)S(1)}, bf16[64,3584]{1,0:T(8,128)(2,1)S(1)}, u32[]{:S(2)}, u32[]{:S(2)}) collective-permute-start(bf16[64,3584]{1,0:T(8,128)(2,1)S(1)} %collective-permute-done.23.refs_1_), channel_id=1, source_target_pairs={{0,2},{1,3},{4,0},{5,1},{8,4},{9,5},{12,8},{13,9},{14,12},{15,13},... | collective-permute-start | bytes 1376264 | tf_op jit(solution)/shard_map/ppermute | solution.py:79
  94.8 10.6 %collective-permute-start.31 = (bf16[64,3584]{1,0:T(8,128)(2,1)S(1)}, bf16[64,3584]{1,0:T(8,128)(2,1)S(1)}, u32[]{:S(2)}, u32[]{:S(2)}) collective-permute-start(bf16[64,3584]{1,0:T(8,128)(2,1)S(1)} %collective-permute-done.23.refs_1_), channel_id=1, source_target_pairs={{0,1},{1,0},{2,3},{3,2},{4,5},{5,4},{6,7},{7,6},{8,9},{9,8},{10,11... | collective-permute-start | bytes 1376264 | tf_op jit(solution)/shard_map/ppermute | solution.py:37
  94.8 11.2 %collective-permute-start.30 = (bf16[64,3584]{1,0:T(8,128)(2,1)S(1)}, bf16[64,3584]{1,0:T(8,128)(2,1)S(1)}, u32[]{:S(2)}, u32[]{:S(2)}) collective-permute-start(bf16[64,3584]{1,0:T(8,128)(2,1)S(1)} %collective-permute-done.19.refs_0_), channel_id=1, source_target_pairs={{0,1},{1,0},{2,3},{3,2},{4,5},{5,4},{6,7},{7,6},{8,9},{9,8},{10,11... | collective-permute-start | bytes 1376264 | tf_op jit(solution)/shard_map/ppermute | solution.py:37
  103.3 6.1 %collective-permute-start.29 = (bf16[64,1792]{1,0:T(8,128)(2,1)S(1)}, bf16[64,1792]{1,0:T(8,128)(2,1)S(1)}, u32[]{:S(2)}, u32[]{:S(2)}) collective-permute-start(bf16[64,1792]{1,0:T(8,128)(2,1)S(1)} %slice.126), channel_id=1, source_target_pairs={{0,4},{1,5},{4,8},{5,9},{8,12},{9,13},{12,14},{13,15},{14,10},{15,... | collective-permute-start | bytes 688136 | tf_op jit(solution)/shard_map/ppermute | solution.py:79
  103.9 6.1 %collective-permute-start.33 = (bf16[64,1792]{1,0:T(8,128)(2,1)S(1)}, bf16[64,1792]{1,0:T(8,128)(2,1)S(1)}, u32[]{:S(2)}, u32[]{:S(2)}) collective-permute-start(bf16[64,1792]{1,0:T(8,128)(2,1)S(1)} %slice.127), channel_id=1, source_target_pairs={{0,2},{1,3},{4,0},{5,1},{8,4},{9,5},{12,8},{13,9},{14,12},{15,13},... | collective-permute-start | bytes 688136 | tf_op jit(solution)/shard_map/ppermute | solution.py:79
  105.5 6.0 %collective-permute-start.28 = (bf16[64,3584]{1,0:T(8,128)(2,1)S(1)}, bf16[64,3584]{1,0:T(8,128)(2,1)S(1)}, u32[]{:S(2)}, u32[]{:S(2)}) collective-permute-start(bf16[64,3584]{1,0:T(8,128)(2,1)S(1)} %collective-permute-done.27.refs_1_), channel_id=1, source_target_pairs={{0,1},{1,0},{2,3},{3,2},{4,5},{5,4},{6,7},{7,6},{8,9},{9,8},{10,11... | collective-permute-start | bytes 1376264 | tf_op jit(solution)/shard_map/ppermute | solution.py:37
  105.5 6.0 %collective-permute-start.26 = (bf16[64,3584]{1,0:T(8,128)(2,1)S(1)}, bf16[64,3584]{1,0:T(8,128)(2,1)S(1)}, u32[]{:S(2)}, u32[]{:S(2)}) collective-permute-start(bf16[64,3584]{1,0:T(8,128)(2,1)S(1)} %collective-permute-done.22.refs_0_), channel_id=1, source_target_pairs={{0,1},{1,0},{2,3},{3,2},{4,5},{5,4},{6,7},{7,6},{8,9},{9,8},{10,11... | collective-permute-start | bytes 1376264 | tf_op jit(solution)/shard_map/ppermute | solution.py:37
  (17 other events, 234.8 us)

commit v13 on v12

--- a/solution.py
+++ b/solution.py
@@ -136,42 +136,44 @@
 
 def stream_kernel(size, rows, coef_hbm, right_hbm, *refs):
     outs, near_left, refs = refs[:2], refs[2], refs[3:]
-    coef, right, by_latent, left, near_rows, stage, sems_left, sems_in, sems_out = refs
+    coef, right, by_latent, left, near_rows, total, stage, sems_left, sems_in, sems_out = refs
     tokens, width = right.shape
     part = outs[0].shape[0]
-    pieces, cuts = sems_in.shape
-    tile, height = width // pieces, tokens // cuts
+    cuts, pieces, passes = sems_in.shape[0], sems_out.shape[0], 2
+    tile, height, depth = width // pieces, tokens // cuts, tokens // passes
     reads, writes = [], []
+    for cut in range(cuts):
+        span = pl.ds(cut * height, height)
+        reads.append(pltpu.make_async_copy(right_hbm.at[span], right.at[span], sems_in.at[cut]))
     for i in range(pieces):
         columns = pl.ds(i * tile, tile)
-        reads.append([])
-        for cut in range(cuts):
-            span = pl.ds(cut * height, height)
-            reads[i].append(
-                pltpu.make_async_copy(
-                    right_hbm.at[span, columns], right.at[span, columns], sems_in.at[i, cut]
-                )
-            )
         for group, out in enumerate(outs):
             source = stage.at[pl.ds(group * part, part), columns]
             writes.append(pltpu.make_async_copy(source, out.at[:, columns], sems_out.at[i, group]))
     read_coef = pltpu.make_async_copy(coef_hbm, coef, sems_left.at[0])
     write_near = pltpu.make_async_copy(near_rows, near_left, sems_left.at[1])
     read_coef.start()
-    for read in sum(reads, []):
+    for read in reads:
         read.start()
     read_coef.wait()
     by_latent[...] = coef[...].T
     ordered_rows(size, rows, by_latent, (left, near_rows))
     write_near.start()
-    for i in range(pieces):
-        for read in reads[i]:
+    for step in range(passes):
+        for read in reads[step * cuts // passes : (step + 1) * cuts // passes]:
             read.wait()
-        columns = slice(i * tile, (i + 1) * tile)
-        out = jnp.dot(left[...], right[:, columns], preferred_element_type=jnp.float32)
-        stage[:, columns] = out.astype(stage.dtype)
-        for write in writes[2 * i : 2 * i + 2]:
-            write.start()
+        span = slice(step * depth, (step + 1) * depth)
+        for i in range(pieces):
+            columns = slice(i * tile, (i + 1) * tile)
+            out = jnp.dot(left[:, span], right[span, columns], preferred_element_type=jnp.float32)
+            if step > 0:
+                out = out + total[:, columns]
+            if step < passes - 1:
+                total[:, columns] = out
+            else:
+                stage[:, columns] = out.astype(stage.dtype)
+                for write in writes[2 * i : 2 * i + 2]:
+                    write.start()
     for write in writes + [write_near]:
         write.wait()
 
@@ -180,7 +182,7 @@
     tokens, latents = coef.shape
     width = right.shape[1]
     part, half = latents // 4, latents // 2
-    pieces, cuts = 4, 4
+    pieces, cuts = 4, 8
     anywhere = pl.BlockSpec(memory_space=pl.ANY)
     return pl.pallas_call(
         functools.partial(stream_kernel, size, rows),
@@ -194,9 +196,10 @@
             pltpu.VMEM((latents, tokens), coef.dtype),
             pltpu.VMEM((half, tokens), coef.dtype),
             pltpu.VMEM((half, tokens), coef.dtype),
+            pltpu.VMEM((half, width), jnp.float32),
             pltpu.VMEM((half, width), coef.dtype),
             pltpu.SemaphoreType.DMA((2,)),
-            pltpu.SemaphoreType.DMA((pieces, cuts)),
+            pltpu.SemaphoreType.DMA((cuts,)),
             pltpu.SemaphoreType.DMA((pieces, 2)),
         ],
         compiler_params=params(52),

time: 113 us -> 113 us (level)
  no operation moved by 1% of the time
where the time goes in v13:
time: 113 us
  waiting for transfers between devices  51.6 us (46%)
  Pallas kernels  30.5 us (27%)
  starting transfers between devices  27.3 us (24%)
  other arithmetic  2.08 us (2%)
    ppermute x16, waiting for transfers between devices, shift(): return lax.ppermute(value, 'latent', pairs)  44.8 us
    ppermute x16, starting transfers between devices, shift(): return lax.ppermute(value, 'latent', pairs)  16.9 us
    pallas_call x3, Pallas kernels, product(): pl.pallas_call(kernel, grid=(width // tile,), in_specs=in_specs + [pl.Blo...  12.4 us
    ppermute x19, starting transfers between devices, swap(): return lax.ppermute(value, 'latent', [(i, i ^ bits) for i in range(size)])  10.3 us
    pallas_call x1, Pallas kernels, stream_far_product(): pl.pallas_call(functools.partial(stream_kernel, size, rows), in_specs=[an...  7.57 us
    ppermute x19, waiting for transfers between devices, swap(): return lax.ppermute(value, 'latent', [(i, i ^ bits) for i in range(size)])  6.79 us
    pallas_call x6, Pallas kernels, place(): pl.pallas_call(functools.partial(place_kernel, plan, size, rows, count),...  6.39 us
    pallas_call x2, Pallas kernels, update(): pl.pallas_call(blocks_kernel if blocks_only else states_kernel, grid=(row...  4.18 us
  transfers between devices with their start and end apart: 35, of which 19 were waited for; matrix products, arithmetic and copies ran while one was open for 1% of the time, Pallas kernels for 25%

profile of v13, /device:TPU:0, one launch (start us, length us, event | category | flops | bytes accessed | tf_op | source)
XLA Modules:
  0.0 112.5 jit_solution(4293770035177840415)
XLA Ops:
  1.4 2.5 %collective-permute-start.2 = (s32[1,48]{1,0:T(1,128)S(1)}, s32[1,48]{1,0:T(1,128)S(1)}, u32[]{:S(2)}, u32[]{:S(2)}) collective-permute-start(s32[1,48]{1,0:T(1,128)S(1)} %pad_add_fusion.1), channel_id=1, source_target_pairs={{0,3},{1,2},{2,1},{3,0},{4,7},{5,6},{6,5},{7,4},{8,11},{9,10},{10,... | collective-permute-start | bytes 584 | tf_op jit(solution)/shard_map/ppermute | solution.py:37
  4.6 7.6 %stream_far_product.1 = (bf16[128,3584]{1,0:T(8,128)(2,1)S(1)}, bf16[128,3584]{1,0:T(8,128)(2,1)}, bf16[256,1024]{1,0:T(8,128)(2,1)S(1)}) custom-call(bf16[1024,512]{1,0:T(8,128)(2,1)} %coef_hbm.1, bf16[1024,3584]{1,0:T(8,128)(2,1)} %right_ref.5), custom_call_target="tpu_custom_call" | custom-call | flops 1879048192 | bytes 10223616 | tf_op jit(solution)/shard_map/stream_far_product/pallas_call | solution.py:187
  12.8 3.9 %collective-permute-start.5 = (s32[4,48]{1,0:T(4,128)S(1)}, s32[4,48]{1,0:T(4,128)S(1)}, u32[]{:S(2)}, u32[]{:S(2)}) collective-permute-start(s32[4,48]{1,0:T(4,128)S(1)} %pad_add_fusion.refs_0_), channel_id=1, source_target_pairs={{0,12},{1,13},{2,14},{3,15},{4,8},{5,9},{6,10},{7,11},{8,4},{9,5},... | collective-permute-start | bytes 2312 | tf_op jit(solution)/shard_map/ppermute | solution.py:37
  18.2 2.9 %collective-permute-done.4.refs_2_ = s32[4,48]{1,0:T(4,128)S(1)} collective-permute-done((s32[4,48]{1,0:T(4,128)S(1)}, s32[4,48]{1,0:T(4,128)S(1)}, u32[]{:S(2)}, u32[]{:S(2)}) %collective-permute-start.4) | collective-permute-done | bytes 800 | tf_op jit(solution)/shard_map/ppermute | solution.py:37
  21.2 4.9 %far_product.1 = (bf16[128,3584]{1,0:T(8,128)(2,1)S(1)}, bf16[128,3584]{1,0:T(8,128)(2,1)S(1)}, bf16[256,1024]{1,0:T(8,128)(2,1)S(1)}, s32[32,1]{1,0:T(8,128)S(1)}) custom-call(bf16[1024,512]{1,0:T(8,128)(2,1)S(1)} %copy-done.7, bf16[1024,3584]{1,0:T(8,128)(2,1)S(1)} %copy-done.6, s32[2,16]{1,0:T(2,128)S(1)} %bitcast.10, s32[4,48]{1,0:T(4,128)S(1)} %pad_add_fusion.refs_0_, ...), custom_call_target="tpu_custom_call" | custom-call | flops 5637144576 | bytes 9699328 | tf_op jit(solution)/shard_map/far_product/pallas_call | solution.py:251
  26.4 2.2 %collective-permute-done.6 = bf16[128,3584]{1,0:T(8,128)(2,1)S(1)} collective-permute-done((bf16[128,3584]{1,0:T(8,128)(2,1)S(1)}, bf16[128,3584]{1,0:T(8,128)(2,1)S(1)}, u32[]{:S(2)}, u32[]{:S(2)}) %collective-permute-start.6) | collective-permute-done | bytes 917536 | tf_op jit(solution)/shard_map/ppermute | solution.py:37
  29.0 1.6 %collective-permute-start.9 = (bf16[64,1792]{1,0:T(8,128)(2,1)S(1)}, bf16[64,1792]{1,0:T(8,128)(2,1)S(1)}, u32[]{:S(2)}, u32[]{:S(2)}) collective-permute-start(bf16[64,1792]{1,0:T(8,128)(2,1)S(1)} %get-tuple-element.140), channel_id=1, source_target_pairs={{0,2},{1,3},{4,0},{5,1},{8,4},{9,5},{12,8},{13,9},{14,12},{15,13},... | collective-permute-start | bytes 688136 | tf_op jit(solution)/shard_map/ppermute | solution.py:79
  31.0 3.7 %near_product.2 = (bf16[128,3584]{1,0:T(8,128)(2,1)S(1)}, bf16[128,3584]{1,0:T(8,128)(2,1)S(1)}) custom-call(bf16[256,1024]{1,0:T(8,128)(2,1)S(1)} %get-tuple-element.75.left_ref, bf16[1024,3584]{1,0:T(8,128)(2,1)S(1)} %copy-done.6), custom_call_target="tpu_custom_call" | custom-call | flops 5637144576 | bytes 9699328 | tf_op jit(solution)/shard_map/near_product/pallas_call | solution.py:251
  34.8 1.9 %collective-permute-done.9 = bf16[64,1792]{1,0:T(8,128)(2,1)S(1)} collective-permute-done((bf16[64,1792]{1,0:T(8,128)(2,1)S(1)}, bf16[64,1792]{1,0:T(8,128)(2,1)S(1)}, u32[]{:S(2)}, u32[]{:S(2)}) %collective-permute-start.9) | collective-permute-done | bytes 229408 | tf_op jit(solution)/shard_map/ppermute | solution.py:79
  36.7 1.2 %collective-permute-done.8 = bf16[64,1792]{1,0:T(8,128)(2,1)S(1)} collective-permute-done((bf16[64,1792]{1,0:T(8,128)(2,1)S(1)}, bf16[64,1792]{1,0:T(8,128)(2,1)S(1)}, u32[]{:S(2)}, u32[]{:S(2)}) %collective-permute-start.8) | collective-permute-done | bytes 229408 | tf_op jit(solution)/shard_map/ppermute | solution.py:79
  38.6 1.6 %collective-permute-start.15 = (bf16[64,3584]{1,0:T(8,128)(2,1)S(1)}, bf16[64,3584]{1,0:T(8,128)(2,1)S(1)}, u32[]{:S(2)}, u32[]{:S(2)}) collective-permute-start(bf16[64,3584]{1,0:T(8,128)(2,1)S(1)} %fusion.1), channel_id=1, source_target_pairs={{0,2},{1,3},{4,0},{5,1},{8,4},{9,5},{12,8},{13,9},{14,12},{15,13},... | collective-permute-start | bytes 1376264 | tf_op jit(solution)/shard_map/ppermute | solution.py:79
  40.2 3.7 %near_product.3 = (bf16[128,3584]{1,0:T(8,128)(2,1)S(1)}, bf16[128,3584]{1,0:T(8,128)(2,1)S(1)}) custom-call(bf16[256,1024]{1,0:T(8,128)(2,1)S(1)} %get-tuple-element.82.left_ref, bf16[1024,3584]{1,0:T(8,128)(2,1)S(1)} %bitcast.5), custom_call_target="tpu_custom_call" | custom-call | flops 5637144576 | bytes 9699328 | tf_op jit(solution)/shard_map/near_product/pallas_call | solution.py:251
  44.5 5.3 %collective-permute-done.15 = bf16[64,3584]{1,0:T(8,128)(2,1)S(1)} collective-permute-done((bf16[64,3584]{1,0:T(8,128)(2,1)S(1)}, bf16[64,3584]{1,0:T(8,128)(2,1)S(1)}, u32[]{:S(2)}, u32[]{:S(2)}) %collective-permute-start.15) | collective-permute-done | bytes 458784 | tf_op jit(solution)/shard_map/ppermute | solution.py:79
  49.9 1.6 %collective-permute-start.16 = (bf16[64,3584]{1,0:T(8,128)(2,1)S(1)}, bf16[64,3584]{1,0:T(8,128)(2,1)S(1)}, u32[]{:S(2)}, u32[]{:S(2)}) collective-permute-start(bf16[64,3584]{1,0:T(8,128)(2,1)S(1)} %fusion.4), channel_id=1, source_target_pairs={{0,2},{1,3},{4,0},{5,1},{8,4},{9,5},{12,8},{13,9},{14,12},{15,13},... | collective-permute-start | bytes 1376264 | tf_op jit(solution)/shard_map/ppermute | solution.py:79
  52.5 7.8 %collective-permute-done.16 = bf16[64,3584]{1,0:T(8,128)(2,1)S(1)} collective-permute-done((bf16[64,3584]{1,0:T(8,128)(2,1)S(1)}, bf16[64,3584]{1,0:T(8,128)(2,1)S(1)}, u32[]{:S(2)}, u32[]{:S(2)}) %collective-permute-start.16) | collective-permute-done | bytes 458784 | tf_op jit(solution)/shard_map/ppermute | solution.py:79
  60.4 1.7 %collective-permute-start.17 = (bf16[64,3584]{1,0:T(8,128)(2,1)S(1)}, bf16[64,3584]{1,0:T(8,128)(2,1)S(1)}, u32[]{:S(2)}, u32[]{:S(2)}) collective-permute-start(bf16[64,3584]{1,0:T(8,128)(2,1)S(1)} %fusion.5), channel_id=1, source_target_pairs={{0,2},{1,3},{4,0},{5,1},{8,4},{9,5},{12,8},{13,9},{14,12},{15,13},... | collective-permute-start | bytes 1376264 | tf_op jit(solution)/shard_map/ppermute | solution.py:79
  63.2 6.8 %collective-permute-done.17.refs_10_.refs_14_ = bf16[64,3584]{1,0:T(8,128)(2,1)S(1)} collective-permute-done((bf16[64,3584]{1,0:T(8,128)(2,1)S(1)}, bf16[64,3584]{1,0:T(8,128)(2,1)S(1)}, u32[]{:S(2)}, u32[]{:S(2)}) %collective-permute-start.17) | collective-permute-done | bytes 458784 | tf_op jit(solution)/shard_map/ppermute | solution.py:79
  69.9 1.8 %collective-permute-done.14.refs_9_.refs_13_ = bf16[64,3584]{1,0:T(8,128)(2,1)S(1)} collective-permute-done((bf16[64,3584]{1,0:T(8,128)(2,1)S(1)}, bf16[64,3584]{1,0:T(8,128)(2,1)S(1)}, u32[]{:S(2)}, u32[]{:S(2)}) %collective-permute-start.14) | collective-permute-done | bytes 458784 | tf_op jit(solution)/shard_map/ppermute | solution.py:79
  71.8 1.6 %blocks.1 = bf16[2,32,3584]{2,1,0:T(8,128)(2,1)S(1)} custom-call(s32[32,1]{1,0:T(8,128)S(1)} %get-tuple-element.70.refs_0_, f32[32,3584]{1,0:T(8,128)S(1)} %copy-done, f32[32,3584]{1,0:T(8,128)S(1)} %copy-done.1, f32[32,3584]{1,0:T(8,128)S(1)} %copy-done.2, f32[32,3584]{1,0:T(8,128)S(1)} %copy-done.3, f32[32,3584]{1,0:T(8,128)S(1)} %copy-done.4, ...), custom_call_target="tpu_custom_call" | custom-call | flops 1146880 | bytes 1146880 | tf_op jit(solution)/shard_map/blocks/pallas_call | solution.py:336
  74.0 1.5 %collective-permute-start.20 = (bf16[64,3584]{1,0:T(8,128)(2,1)S(1)}, bf16[64,3584]{1,0:T(8,128)(2,1)S(1)}, u32[]{:S(2)}, u32[]{:S(2)}) collective-permute-start(bf16[64,3584]{1,0:T(8,128)(2,1)S(1)} %bitcast.7), channel_id=1, source_target_pairs={{0,2},{1,3},{4,0},{5,1},{8,4},{9,5},{12,8},{13,9},{14,12},{15,13},... | collective-permute-start | bytes 1376264 | tf_op jit(solution)/shard_map/ppermute | solution.py:79
  75.5 2.6 %states.1 = (f32[32,3584]{1,0:T(8,128)}, f32[32,3584]{1,0:T(8,128)}, f32[32,3584]{1,0:T(8,128)}, f32[32,3584]{1,0:T(8,128)}, f32[32,3584]{1,0:T(8,128)}, /*index=5*/f32[32,3584]{1,0:T(8,128)}) custom-call(s32[32,1]{1,0:T(8,128)S(1)} %get-tuple-element.70.refs_0_, f32[32,3584]{1,0:T(8,128)S(1)} %copy-done, f32[32,3584]{1,0:T(8,128)S(1)} %copy-done.1, ...), custom_call_target="tpu_custom_call" | custom-call | flops 1146880 | bytes 1146880 | tf_op jit(solution)/shard_map/states/pallas_call | solution.py:336
  78.9 3.1 %collective-permute-done.18.refs_0_ = bf16[64,3584]{1,0:T(8,128)(2,1)S(1)} collective-permute-done((bf16[64,3584]{1,0:T(8,128)(2,1)S(1)}, bf16[64,3584]{1,0:T(8,128)(2,1)S(1)}, u32[]{:S(2)}, u32[]{:S(2)}) %collective-permute-start.18) | collective-permute-done | bytes 458784 | tf_op jit(solution)/shard_map/ppermute | solution.py:79
  82.6 1.5 %collective-permute-start.23 = (bf16[64,3584]{1,0:T(8,128)(2,1)S(1)}, bf16[64,3584]{1,0:T(8,128)(2,1)S(1)}, u32[]{:S(2)}, u32[]{:S(2)}) collective-permute-start(bf16[64,3584]{1,0:T(8,128)(2,1)S(1)} %collective-permute-done.20.refs_1_), channel_id=1, source_target_pairs={{0,2},{1,3},{4,0},{5,1},{8,4},{9,5},{12,8},{13,9},{14,12},{15,13},... | collective-permute-start | bytes 1376264 | tf_op jit(solution)/shard_map/ppermute | solution.py:79
  84.6 1.1 place.7
  85.7 6.9 %collective-permute-done.19.refs_0_ = bf16[64,3584]{1,0:T(8,128)(2,1)S(1)} collective-permute-done((bf16[64,3584]{1,0:T(8,128)(2,1)S(1)}, bf16[64,3584]{1,0:T(8,128)(2,1)S(1)}, u32[]{:S(2)}, u32[]{:S(2)}) %collective-permute-start.19) | collective-permute-done | bytes 458784 | tf_op jit(solution)/shard_map/ppermute | solution.py:79
  93.2 1.5 %collective-permute-start.27 = (bf16[64,3584]{1,0:T(8,128)(2,1)S(1)}, bf16[64,3584]{1,0:T(8,128)(2,1)S(1)}, u32[]{:S(2)}, u32[]{:S(2)}) collective-permute-start(bf16[64,3584]{1,0:T(8,128)(2,1)S(1)} %collective-permute-done.23.refs_1_), channel_id=1, source_target_pairs={{0,2},{1,3},{4,0},{5,1},{8,4},{9,5},{12,8},{13,9},{14,12},{15,13},... | collective-permute-start | bytes 1376264 | tf_op jit(solution)/shard_map/ppermute | solution.py:79
  95.3 1.3 %place.8 = (bf16[512,3584]{1,0:T(8,128)(2,1)}, bf16[512,3584]{1,0:T(8,128)(2,1)}) custom-call(bf16[64,3584]{1,0:T(8,128)(2,1)S(1)} %collective-permute-done.19.refs_0_, bf16[64,3584]{1,0:T(8,128)(2,1)S(1)} %collective-permute-done.23.refs_1_, bf16[64,3584]{1,0:T(8,128)(2,1)S(1)} %collective-permute-done.24.refs_2_, ...), custom_call_target="tpu_custom_call", output_to_operand_aliasing={{0}: (4, {}), {1}: (5, {})} | custom-call | bytes 3670016 | tf_op jit(solution)/shard_map/place/pallas_call | solution.py:371
  96.6 6.7 %collective-permute-done.22.refs_0_ = bf16[64,3584]{1,0:T(8,128)(2,1)S(1)} collective-permute-done((bf16[64,3584]{1,0:T(8,128)(2,1)S(1)}, bf16[64,3584]{1,0:T(8,128)(2,1)S(1)}, u32[]{:S(2)}, u32[]{:S(2)}) %collective-permute-start.22) | collective-permute-done | bytes 458784 | tf_op jit(solution)/shard_map/ppermute | solution.py:79
  103.8 1.6 %collective-permute-start.33 = (bf16[64,1792]{1,0:T(8,128)(2,1)S(1)}, bf16[64,1792]{1,0:T(8,128)(2,1)S(1)}, u32[]{:S(2)}, u32[]{:S(2)}) collective-permute-start(bf16[64,1792]{1,0:T(8,128)(2,1)S(1)} %slice.127), channel_id=1, source_target_pairs={{0,2},{1,3},{4,0},{5,1},{8,4},{9,5},{12,8},{13,9},{14,12},{15,13},... | collective-permute-start | bytes 688136 | tf_op jit(solution)/shard_map/ppermute | solution.py:79
  105.9 1.3 %place.9 = (bf16[512,3584]{1,0:T(8,128)(2,1)}, bf16[512,3584]{1,0:T(8,128)(2,1)}) custom-call(bf16[64,3584]{1,0:T(8,128)(2,1)S(1)} %collective-permute-done.22.refs_0_, bf16[64,3584]{1,0:T(8,128)(2,1)S(1)} %collective-permute-done.27.refs_1_, bf16[64,3584]{1,0:T(8,128)(2,1)S(1)} %collective-permute-done.30.refs_2_, ...), custom_call_target="tpu_custom_call", output_to_operand_aliasing={{0}: (4, {}), {1}: (5, {})} | custom-call | bytes 3670016 | tf_op jit(solution)/shard_map/place/pallas_call | solution.py:371
  107.2 2.1 %collective-permute-done.29.refs_0_ = bf16[64,1792]{1,0:T(8,128)(2,1)S(1)} collective-permute-done((bf16[64,1792]{1,0:T(8,128)(2,1)S(1)}, bf16[64,1792]{1,0:T(8,128)(2,1)S(1)}, u32[]{:S(2)}, u32[]{:S(2)}) %collective-permute-start.29) | collective-permute-done | bytes 229408 | tf_op jit(solution)/shard_map/ppermute | solution.py:79
  111.4 1.1 %place.11 = (bf16[512,3584]{1,0:T(8,128)(2,1)}, bf16[512,3584]{1,0:T(8,128)(2,1)}) custom-call(bf16[64,3584]{1,0:T(8,128)(2,1)S(1)} %collective-permute-done.26.refs_0_, bf16[64,3584]{1,0:T(8,128)(2,1)S(1)} %collective-permute-done.28.refs_1_, bf16[64,1792]{1,0:T(8,128)(2,1)S(1)} %collective-permute-done.32.refs_2_, ...), custom_call_target="tpu_custom_call", output_to_operand_aliasing={{0}: (4, {}), {1}: (5, {})} | custom-call | bytes 3670016 | tf_op jit(solution)/shard_map/place/pallas_call | solution.py:371
  (94 shorter events, 14.9 us)
Async XLA Ops:
  1.4 10.7 %collective-permute-start.2 = (s32[1,48]{1,0:T(1,128)S(1)}, s32[1,48]{1,0:T(1,128)S(1)}, u32[]{:S(2)}, u32[]{:S(2)}) collective-permute-start(s32[1,48]{1,0:T(1,128)S(1)} %pad_add_fusion.1), channel_id=1, source_target_pairs={{0,3},{1,2},{2,1},{3,0},{4,7},{5,6},{6,5},{7,4},{8,11},{9,10},{10,... | collective-permute-start | bytes 584 | tf_op jit(solution)/shard_map/ppermute | solution.py:37
  3.9 8.3 %collective-permute-start.1 = (s32[1,48]{1,0:T(1,128)S(1)}, s32[1,48]{1,0:T(1,128)S(1)}, u32[]{:S(2)}, u32[]{:S(2)}) collective-permute-start(s32[1,48]{1,0:T(1,128)S(1)} %pad_add_fusion.1), channel_id=1, source_target_pairs={{0,2},{1,3},{2,0},{3,1},{4,6},{5,7},{6,4},{7,5},{8,10},{9,11},{10,... | collective-permute-start | bytes 584 | tf_op jit(solution)/shard_map/ppermute | solution.py:37
  4.6 7.6 %collective-permute-start = (s32[1,48]{1,0:T(1,128)S(1)}, s32[1,48]{1,0:T(1,128)S(1)}, u32[]{:S(2)}, u32[]{:S(2)}) collective-permute-start(s32[1,48]{1,0:T(1,128)S(1)} %pad_add_fusion.1), channel_id=1, source_target_pairs={{0,1},{1,0},{2,3},{3,2},{4,5},{5,4},{6,7},{7,6},{8,9},{9,8},{10,11... | collective-permute-start | bytes 584 | tf_op jit(solution)/shard_map/ppermute | solution.py:37
  12.2 14.0 %collective-permute-start.7 = (bf16[128,3584]{1,0:T(8,128)(2,1)S(1)}, bf16[128,3584]{1,0:T(8,128)(2,1)S(1)}, u32[]{:S(2)}, u32[]{:S(2)}) collective-permute-start(bf16[128,3584]{1,0:T(8,128)(2,1)S(1)} %get-tuple-element.68), channel_id=1, source_target_pairs={{0,1},{1,0},{2,3},{3,2},{4,5},{5,4},{6,7},{7,6},{8,9},{9,8},{10,11... | collective-permute-start | bytes 2752520 | tf_op jit(solution)/shard_map/ppermute | solution.py:37
  12.8 5.4 %collective-permute-start.5 = (s32[4,48]{1,0:T(4,128)S(1)}, s32[4,48]{1,0:T(4,128)S(1)}, u32[]{:S(2)}, u32[]{:S(2)}) collective-permute-start(s32[4,48]{1,0:T(4,128)S(1)} %pad_add_fusion.refs_0_), channel_id=1, source_target_pairs={{0,12},{1,13},{2,14},{3,15},{4,8},{5,9},{6,10},{7,11},{8,4},{9,5},... | collective-permute-start | bytes 2312 | tf_op jit(solution)/shard_map/ppermute | solution.py:37
  16.7 4.5 %collective-permute-start.4 = (s32[4,48]{1,0:T(4,128)S(1)}, s32[4,48]{1,0:T(4,128)S(1)}, u32[]{:S(2)}, u32[]{:S(2)}) collective-permute-start(s32[4,48]{1,0:T(4,128)S(1)} %pad_add_fusion.refs_0_), channel_id=1, source_target_pairs={{0,8},{1,9},{2,10},{3,11},{4,12},{5,13},{6,14},{7,15},{8,0},{9,1},... | collective-permute-start | bytes 2312 | tf_op jit(solution)/shard_map/ppermute | solution.py:37
  16.7 4.5 %collective-permute-start.3 = (s32[4,48]{1,0:T(4,128)S(1)}, s32[4,48]{1,0:T(4,128)S(1)}, u32[]{:S(2)}, u32[]{:S(2)}) collective-permute-start(s32[4,48]{1,0:T(4,128)S(1)} %pad_add_fusion.refs_0_), channel_id=1, source_target_pairs={{0,4},{1,5},{2,6},{3,7},{4,0},{5,1},{6,2},{7,3},{8,12},{9,13},{10,... | collective-permute-start | bytes 2312 | tf_op jit(solution)/shard_map/ppermute | solution.py:37
  29.0 7.7 %collective-permute-start.9 = (bf16[64,1792]{1,0:T(8,128)(2,1)S(1)}, bf16[64,1792]{1,0:T(8,128)(2,1)S(1)}, u32[]{:S(2)}, u32[]{:S(2)}) collective-permute-start(bf16[64,1792]{1,0:T(8,128)(2,1)S(1)} %get-tuple-element.140), channel_id=1, source_target_pairs={{0,2},{1,3},{4,0},{5,1},{8,4},{9,5},{12,8},{13,9},{14,12},{15,13},... | collective-permute-start | bytes 688136 | tf_op jit(solution)/shard_map/ppermute | solution.py:79
  30.5 7.4 %collective-permute-start.8 = (bf16[64,1792]{1,0:T(8,128)(2,1)S(1)}, bf16[64,1792]{1,0:T(8,128)(2,1)S(1)}, u32[]{:S(2)}, u32[]{:S(2)}) collective-permute-start(bf16[64,1792]{1,0:T(8,128)(2,1)S(1)} %get-tuple-element.141), channel_id=1, source_target_pairs={{0,4},{1,5},{4,8},{5,9},{8,12},{9,13},{12,14},{13,15},{14,10},{15,... | collective-permute-start | bytes 688136 | tf_op jit(solution)/shard_map/ppermute | solution.py:79
  38.0 13.9 %collective-permute-start.11 = (bf16[64,3584]{1,0:T(8,128)(2,1)S(1)}, bf16[64,3584]{1,0:T(8,128)(2,1)S(1)}, u32[]{:S(2)}, u32[]{:S(2)}) collective-permute-start(bf16[64,3584]{1,0:T(8,128)(2,1)S(1)} %fusion), channel_id=1, source_target_pairs={{0,4},{1,5},{4,8},{5,9},{8,12},{9,13},{12,14},{13,15},{14,10},{15,... | collective-permute-start | bytes 1376264 | tf_op jit(solution)/shard_map/ppermute | solution.py:79
  38.6 11.2 %collective-permute-start.15 = (bf16[64,3584]{1,0:T(8,128)(2,1)S(1)}, bf16[64,3584]{1,0:T(8,128)(2,1)S(1)}, u32[]{:S(2)}, u32[]{:S(2)}) collective-permute-start(bf16[64,3584]{1,0:T(8,128)(2,1)S(1)} %fusion.1), channel_id=1, source_target_pairs={{0,2},{1,3},{4,0},{5,1},{8,4},{9,5},{12,8},{13,9},{14,12},{15,13},... | collective-permute-start | bytes 1376264 | tf_op jit(solution)/shard_map/ppermute | solution.py:79
  40.2 11.4 %collective-permute-start.10 = (bf16[128,3584]{1,0:T(8,128)(2,1)S(1)}, bf16[128,3584]{1,0:T(8,128)(2,1)S(1)}, u32[]{:S(2)}, u32[]{:S(2)}) collective-permute-start(bf16[128,3584]{1,0:T(8,128)(2,1)S(1)} %get-tuple-element.78), channel_id=1, source_target_pairs={{0,1},{1,0},{2,3},{3,2},{4,5},{5,4},{6,7},{7,6},{8,9},{9,8},{10,11... | collective-permute-start | bytes 2752520 | tf_op jit(solution)/shard_map/ppermute | solution.py:37
  43.9 7.5 %collective-permute-start.12 = (bf16[128,3584]{1,0:T(8,128)(2,1)S(1)}, bf16[128,3584]{1,0:T(8,128)(2,1)S(1)}, u32[]{:S(2)}, u32[]{:S(2)}) collective-permute-start(bf16[128,3584]{1,0:T(8,128)(2,1)S(1)} %get-tuple-element.84), channel_id=1, source_target_pairs={{0,1},{1,0},{2,3},{3,2},{4,5},{5,4},{6,7},{7,6},{8,9},{9,8},{10,11... | collective-permute-start | bytes 2752520 | tf_op jit(solution)/shard_map/ppermute | solution.py:37
  49.9 10.5 %collective-permute-start.16 = (bf16[64,3584]{1,0:T(8,128)(2,1)S(1)}, bf16[64,3584]{1,0:T(8,128)(2,1)S(1)}, u32[]{:S(2)}, u32[]{:S(2)}) collective-permute-start(bf16[64,3584]{1,0:T(8,128)(2,1)S(1)} %fusion.4), channel_id=1, source_target_pairs={{0,2},{1,3},{4,0},{5,1},{8,4},{9,5},{12,8},{13,9},{14,12},{15,13},... | collective-permute-start | bytes 1376264 | tf_op jit(solution)/shard_map/ppermute | solution.py:79
  51.9 10.5 %collective-permute-start.13 = (bf16[64,3584]{1,0:T(8,128)(2,1)S(1)}, bf16[64,3584]{1,0:T(8,128)(2,1)S(1)}, u32[]{:S(2)}, u32[]{:S(2)}) collective-permute-start(bf16[64,3584]{1,0:T(8,128)(2,1)S(1)} %fusion.2), channel_id=1, source_target_pairs={{0,4},{1,5},{4,8},{5,9},{8,12},{9,13},{12,14},{13,15},{14,10},{15,... | collective-permute-start | bytes 1376264 | tf_op jit(solution)/shard_map/ppermute | solution.py:79
  60.4 9.5 %collective-permute-start.17 = (bf16[64,3584]{1,0:T(8,128)(2,1)S(1)}, bf16[64,3584]{1,0:T(8,128)(2,1)S(1)}, u32[]{:S(2)}, u32[]{:S(2)}) collective-permute-start(bf16[64,3584]{1,0:T(8,128)(2,1)S(1)} %fusion.5), channel_id=1, source_target_pairs={{0,2},{1,3},{4,0},{5,1},{8,4},{9,5},{12,8},{13,9},{14,12},{15,13},... | collective-permute-start | bytes 1376264 | tf_op jit(solution)/shard_map/ppermute | solution.py:79
  62.6 9.2 %collective-permute-start.14 = (bf16[64,3584]{1,0:T(8,128)(2,1)S(1)}, bf16[64,3584]{1,0:T(8,128)(2,1)S(1)}, u32[]{:S(2)}, u32[]{:S(2)}) collective-permute-start(bf16[64,3584]{1,0:T(8,128)(2,1)S(1)} %fusion.3), channel_id=1, source_target_pairs={{0,4},{1,5},{4,8},{5,9},{8,12},{9,13},{12,14},{13,15},{14,10},{15,... | collective-permute-start | bytes 1376264 | tf_op jit(solution)/shard_map/ppermute | solution.py:79
  73.4 8.5 %collective-permute-start.18 = (bf16[64,3584]{1,0:T(8,128)(2,1)S(1)}, bf16[64,3584]{1,0:T(8,128)(2,1)S(1)}, u32[]{:S(2)}, u32[]{:S(2)}) collective-permute-start(bf16[64,3584]{1,0:T(8,128)(2,1)S(1)} %bitcast.6), channel_id=1, source_target_pairs={{0,4},{1,5},{4,8},{5,9},{8,12},{9,13},{12,14},{13,15},{14,10},{15,... | collective-permute-start | bytes 1376264 | tf_op jit(solution)/shard_map/ppermute | solution.py:79
  74.0 8.6 %collective-permute-start.20 = (bf16[64,3584]{1,0:T(8,128)(2,1)S(1)}, bf16[64,3584]{1,0:T(8,128)(2,1)S(1)}, u32[]{:S(2)}, u32[]{:S(2)}) collective-permute-start(bf16[64,3584]{1,0:T(8,128)(2,1)S(1)} %bitcast.7), channel_id=1, source_target_pairs={{0,2},{1,3},{4,0},{5,1},{8,4},{9,5},{12,8},{13,9},{14,12},{15,13},... | collective-permute-start | bytes 1376264 | tf_op jit(solution)/shard_map/ppermute | solution.py:79
  78.1 6.5 %collective-permute-start.21 = (bf16[64,3584]{1,0:T(8,128)(2,1)S(1)}, bf16[64,3584]{1,0:T(8,128)(2,1)S(1)}, u32[]{:S(2)}, u32[]{:S(2)}) collective-permute-start(bf16[64,3584]{1,0:T(8,128)(2,1)S(1)} %bitcast.8), channel_id=1, source_target_pairs={{0,1},{1,0},{2,3},{3,2},{4,5},{5,4},{6,7},{7,6},{8,9},{9,8},{10,11... | collective-permute-start | bytes 1376264 | tf_op jit(solution)/shard_map/ppermute | solution.py:37
  81.9 10.7 %collective-permute-start.19 = (bf16[64,3584]{1,0:T(8,128)(2,1)S(1)}, bf16[64,3584]{1,0:T(8,128)(2,1)S(1)}, u32[]{:S(2)}, u32[]{:S(2)}) collective-permute-start(bf16[64,3584]{1,0:T(8,128)(2,1)S(1)} %collective-permute-done.18.refs_0_), channel_id=1, source_target_pairs={{0,4},{1,5},{4,8},{5,9},{8,12},{9,13},{12,14},{13,15},{14,10},{15,... | collective-permute-start | bytes 1376264 | tf_op jit(solution)/shard_map/ppermute | solution.py:79
  82.6 10.7 %collective-permute-start.23 = (bf16[64,3584]{1,0:T(8,128)(2,1)S(1)}, bf16[64,3584]{1,0:T(8,128)(2,1)S(1)}, u32[]{:S(2)}, u32[]{:S(2)}) collective-permute-start(bf16[64,3584]{1,0:T(8,128)(2,1)S(1)} %collective-permute-done.20.refs_1_), channel_id=1, source_target_pairs={{0,2},{1,3},{4,0},{5,1},{8,4},{9,5},{12,8},{13,9},{14,12},{15,13},... | collective-permute-start | bytes 1376264 | tf_op jit(solution)/shard_map/ppermute | solution.py:79
  84.1 10.7 %collective-permute-start.25 = (bf16[64,3584]{1,0:T(8,128)(2,1)S(1)}, bf16[64,3584]{1,0:T(8,128)(2,1)S(1)}, u32[]{:S(2)}, u32[]{:S(2)}) collective-permute-start(bf16[64,3584]{1,0:T(8,128)(2,1)S(1)} %collective-permute-done.20.refs_1_), channel_id=1, source_target_pairs={{0,1},{1,0},{2,3},{3,2},{4,5},{5,4},{6,7},{7,6},{8,9},{9,8},{10,11... | collective-permute-start | bytes 1376264 | tf_op jit(solution)/shard_map/ppermute | solution.py:37
  84.1 11.2 %collective-permute-start.24 = (bf16[64,3584]{1,0:T(8,128)(2,1)S(1)}, bf16[64,3584]{1,0:T(8,128)(2,1)S(1)}, u32[]{:S(2)}, u32[]{:S(2)}) collective-permute-start(bf16[64,3584]{1,0:T(8,128)(2,1)S(1)} %collective-permute-done.18.refs_0_), channel_id=1, source_target_pairs={{0,1},{1,0},{2,3},{3,2},{4,5},{5,4},{6,7},{7,6},{8,9},{9,8},{10,11... | collective-permute-start | bytes 1376264 | tf_op jit(solution)/shard_map/ppermute | solution.py:37
  92.6 10.6 %collective-permute-start.22 = (bf16[64,3584]{1,0:T(8,128)(2,1)S(1)}, bf16[64,3584]{1,0:T(8,128)(2,1)S(1)}, u32[]{:S(2)}, u32[]{:S(2)}) collective-permute-start(bf16[64,3584]{1,0:T(8,128)(2,1)S(1)} %collective-permute-done.19.refs_0_), channel_id=1, source_target_pairs={{0,4},{1,5},{4,8},{5,9},{8,12},{9,13},{12,14},{13,15},{14,10},{15,... | collective-permute-start | bytes 1376264 | tf_op jit(solution)/shard_map/ppermute | solution.py:79
  93.2 10.6 %collective-permute-start.27 = (bf16[64,3584]{1,0:T(8,128)(2,1)S(1)}, bf16[64,3584]{1,0:T(8,128)(2,1)S(1)}, u32[]{:S(2)}, u32[]{:S(2)}) collective-permute-start(bf16[64,3584]{1,0:T(8,128)(2,1)S(1)} %collective-permute-done.23.refs_1_), channel_id=1, source_target_pairs={{0,2},{1,3},{4,0},{5,1},{8,4},{9,5},{12,8},{13,9},{14,12},{15,13},... | collective-permute-start | bytes 1376264 | tf_op jit(solution)/shard_map/ppermute | solution.py:79
  94.8 10.6 %collective-permute-start.31 = (bf16[64,3584]{1,0:T(8,128)(2,1)S(1)}, bf16[64,3584]{1,0:T(8,128)(2,1)S(1)}, u32[]{:S(2)}, u32[]{:S(2)}) collective-permute-start(bf16[64,3584]{1,0:T(8,128)(2,1)S(1)} %collective-permute-done.23.refs_1_), channel_id=1, source_target_pairs={{0,1},{1,0},{2,3},{3,2},{4,5},{5,4},{6,7},{7,6},{8,9},{9,8},{10,11... | collective-permute-start | bytes 1376264 | tf_op jit(solution)/shard_map/ppermute | solution.py:37
  94.8 11.2 %collective-permute-start.30 = (bf16[64,3584]{1,0:T(8,128)(2,1)S(1)}, bf16[64,3584]{1,0:T(8,128)(2,1)S(1)}, u32[]{:S(2)}, u32[]{:S(2)}) collective-permute-start(bf16[64,3584]{1,0:T(8,128)(2,1)S(1)} %collective-permute-done.19.refs_0_), channel_id=1, source_target_pairs={{0,1},{1,0},{2,3},{3,2},{4,5},{5,4},{6,7},{7,6},{8,9},{9,8},{10,11... | collective-permute-start | bytes 1376264 | tf_op jit(solution)/shard_map/ppermute | solution.py:37
  103.3 6.1 %collective-permute-start.29 = (bf16[64,1792]{1,0:T(8,128)(2,1)S(1)}, bf16[64,1792]{1,0:T(8,128)(2,1)S(1)}, u32[]{:S(2)}, u32[]{:S(2)}) collective-permute-start(bf16[64,1792]{1,0:T(8,128)(2,1)S(1)} %slice.126), channel_id=1, source_target_pairs={{0,4},{1,5},{4,8},{5,9},{8,12},{9,13},{12,14},{13,15},{14,10},{15,... | collective-permute-start | bytes 688136 | tf_op jit(solution)/shard_map/ppermute | solution.py:79
  103.8 6.1 %collective-permute-start.33 = (bf16[64,1792]{1,0:T(8,128)(2,1)S(1)}, bf16[64,1792]{1,0:T(8,128)(2,1)S(1)}, u32[]{:S(2)}, u32[]{:S(2)}) collective-permute-start(bf16[64,1792]{1,0:T(8,128)(2,1)S(1)} %slice.127), channel_id=1, source_target_pairs={{0,2},{1,3},{4,0},{5,1},{8,4},{9,5},{12,8},{13,9},{14,12},{15,13},... | collective-permute-start | bytes 688136 | tf_op jit(solution)/shard_map/ppermute | solution.py:79
  105.4 6.0 %collective-permute-start.28 = (bf16[64,3584]{1,0:T(8,128)(2,1)S(1)}, bf16[64,3584]{1,0:T(8,128)(2,1)S(1)}, u32[]{:S(2)}, u32[]{:S(2)}) collective-permute-start(bf16[64,3584]{1,0:T(8,128)(2,1)S(1)} %collective-permute-done.27.refs_1_), channel_id=1, source_target_pairs={{0,1},{1,0},{2,3},{3,2},{4,5},{5,4},{6,7},{7,6},{8,9},{9,8},{10,11... | collective-permute-start | bytes 1376264 | tf_op jit(solution)/shard_map/ppermute | solution.py:37
  105.4 6.0 %collective-permute-start.26 = (bf16[64,3584]{1,0:T(8,128)(2,1)S(1)}, bf16[64,3584]{1,0:T(8,128)(2,1)S(1)}, u32[]{:S(2)}, u32[]{:S(2)}) collective-permute-start(bf16[64,3584]{1,0:T(8,128)(2,1)S(1)} %collective-permute-done.22.refs_0_), channel_id=1, source_target_pairs={{0,1},{1,0},{2,3},{3,2},{4,5},{5,4},{6,7},{7,6},{8,9},{9,8},{10,11... | collective-permute-start | bytes 1376264 | tf_op jit(solution)/shard_map/ppermute | solution.py:37
  (17 other events, 234.4 us)

commit v14 on v13

--- a/solution.py
+++ b/solution.py
@@ -80,15 +80,13 @@
 
 
 def gather_table(row, size):
-    stages, step = [], 1
-    pieces = [row]
+    pieces, step = [row], 1
     while step < size:
         if step > 1:
             pieces = [jnp.concatenate(pieces, axis=0)]
         pieces += [swap(pieces[0], step * k, size) for k in range(1, min(4, size // step))]
-        stages.append(pieces)
         step *= len(pieces)
-    return stages
+    return pieces
 
 
 def ordered_rows(size, rows, by_latent, groups):
@@ -422,10 +420,11 @@
     half = width // 2
     size = lax.axis_size("latent")
     chips = size // 2
-    stages = gather_table(jnp.concatenate([send_count, dead_order], axis=1), size)
-    table = stages[-1]
-    dec_sent, kept, dec_left = stream_far_product(latent_act, out_grad, size, rows)
-    dec_sent = after(dec_sent, *stages[0])
+    table = gather_table(jnp.concatenate([send_count, dead_order], axis=1), size)
+    dec_sent, kept, dec_left = stream_far_product(
+        after(latent_act, table[0]), out_grad, size, rows
+    )
+    dec_sent = after(dec_sent, *table)
     dec_kept, dec_core = [kept], [swap(dec_sent, 1, size)]
     enc_sent, kept, enc_left, code = far_product(
         after(enc_coef, dec_sent), x_rows, size, rows, pick_rows[0].T, table

time: 113 us -> 114 us (level)
  waiting for transfers between devices: 51.6 us -> 52.8 us
    ppermute x16, waiting for transfers between devices: 44.8 us -> 47.3 us  [shift(): return lax.ppermute(value, 'latent', pairs)]
    ppermute x19, waiting for transfers between devices: 6.79 us -> 5.46 us  [swap(): return lax.ppermute(value, 'latent', [(i, i ^ bits) for i in range(size)])]
  transfers between devices with their start and end apart: 35 -> 35, of which waited for: 19 -> 16; matrix products, arithmetic and copies ran while one was open for 1% -> 1% of each run, Pallas kernels for 25% -> 24%
where the time goes in v14:
time: 114 us
  waiting for transfers between devices  52.8 us (46%)
  Pallas kernels  30.5 us (27%)
  starting transfers between devices  26.9 us (24%)
  other arithmetic  2.71 us (2%)
    ppermute x16, waiting for transfers between devices, shift(): return lax.ppermute(value, 'latent', pairs)  47.3 us
    ppermute x16, starting transfers between devices, shift(): return lax.ppermute(value, 'latent', pairs)  16.7 us
    pallas_call x3, Pallas kernels, product(): pl.pallas_call(kernel, grid=(width // tile,), in_specs=in_specs + [pl.Blo...  12.4 us
    ppermute x19, starting transfers between devices, swap(): return lax.ppermute(value, 'latent', [(i, i ^ bits) for i in range(size)])  10.2 us
    pallas_call x1, Pallas kernels, stream_far_product(): pl.pallas_call(functools.partial(stream_kernel, size, rows), in_specs=[an...  7.56 us
    pallas_call x6, Pallas kernels, place(): pl.pallas_call(functools.partial(place_kernel, plan, size, rows, count),...  6.39 us
    ppermute x19, waiting for transfers between devices, swap(): return lax.ppermute(value, 'latent', [(i, i ^ bits) for i in range(size)])  5.46 us
    pallas_call x2, Pallas kernels, update(): pl.pallas_call(blocks_kernel if blocks_only else states_kernel, grid=(row...  4.18 us
  transfers between devices with their start and end apart: 35, of which 16 were waited for; matrix products, arithmetic and copies ran while one was open for 1% of the time, Pallas kernels for 24%

profile of v14, /device:TPU:0, one launch (start us, length us, event | category | flops | bytes accessed | tf_op | source)
XLA Modules:
  0.0 114.0 jit_solution(7191694864116543023)
XLA Ops:
  1.4 2.4 %collective-permute-start.2 = (s32[1,48]{1,0:T(1,128)S(1)}, s32[1,48]{1,0:T(1,128)S(1)}, u32[]{:S(2)}, u32[]{:S(2)}) collective-permute-start(s32[1,48]{1,0:T(1,128)S(1)} %pad_add_fusion.1), channel_id=1, source_target_pairs={{0,3},{1,2},{2,1},{3,0},{4,7},{5,6},{6,5},{7,4},{8,11},{9,10},{10,... | collective-permute-start | bytes 584 | tf_op jit(solution)/shard_map/ppermute | solution.py:37
  5.1 2.2 %collective-permute-done.1 = s32[1,48]{1,0:T(1,128)S(1)} collective-permute-done((s32[1,48]{1,0:T(1,128)S(1)}, s32[1,48]{1,0:T(1,128)S(1)}, u32[]{:S(2)}, u32[]{:S(2)}) %collective-permute-start.1) | collective-permute-done | bytes 224 | tf_op jit(solution)/shard_map/ppermute | solution.py:37
  8.1 3.7 %collective-permute-start.5 = (s32[4,48]{1,0:T(4,128)S(1)}, s32[4,48]{1,0:T(4,128)S(1)}, u32[]{:S(2)}, u32[]{:S(2)}) collective-permute-start(s32[4,48]{1,0:T(4,128)S(1)} %pad_add_fusion.refs_0_), channel_id=1, source_target_pairs={{0,12},{1,13},{2,14},{3,15},{4,8},{5,9},{6,10},{7,11},{8,4},{9,5},... | collective-permute-start | bytes 2312 | tf_op jit(solution)/shard_map/ppermute | solution.py:37
  12.5 7.6 %stream_far_product.1 = (bf16[128,3584]{1,0:T(8,128)(2,1)S(1)}, bf16[128,3584]{1,0:T(8,128)(2,1)}, bf16[256,1024]{1,0:T(8,128)(2,1)S(1)}) custom-call(bf16[1024,512]{1,0:T(8,128)(2,1)} %coef_hbm, bf16[1024,3584]{1,0:T(8,128)(2,1)} %right_ref.5), custom_call_target="tpu_custom_call" | custom-call | flops 1879048192 | bytes 10223616 | tf_op jit(solution)/shard_map/stream_far_product/pallas_call | solution.py:185
  20.3 5.0 %far_product.1 = (bf16[128,3584]{1,0:T(8,128)(2,1)S(1)}, bf16[128,3584]{1,0:T(8,128)(2,1)S(1)}, bf16[256,1024]{1,0:T(8,128)(2,1)S(1)}, s32[32,1]{1,0:T(8,128)S(1)}) custom-call(bf16[1024,512]{1,0:T(8,128)(2,1)S(1)} %copy-done.7, bf16[1024,3584]{1,0:T(8,128)(2,1)S(1)} %copy-done.6, s32[2,16]{1,0:T(2,128)S(1)} %bitcast.10, s32[4,48]{1,0:T(4,128)S(1)} %pad_add_fusion.refs_0_, ...), custom_call_target="tpu_custom_call" | custom-call | flops 5637144576 | bytes 9699328 | tf_op jit(solution)/shard_map/far_product/pallas_call | solution.py:249
  26.0 1.9 %collective-permute-done.6 = bf16[128,3584]{1,0:T(8,128)(2,1)S(1)} collective-permute-done((bf16[128,3584]{1,0:T(8,128)(2,1)S(1)}, bf16[128,3584]{1,0:T(8,128)(2,1)S(1)}, u32[]{:S(2)}, u32[]{:S(2)}) %collective-permute-start.6) | collective-permute-done | bytes 917536 | tf_op jit(solution)/shard_map/ppermute | solution.py:37
  28.8 1.4 %collective-permute-start.8 = (bf16[64,1792]{1,0:T(8,128)(2,1)S(1)}, bf16[64,1792]{1,0:T(8,128)(2,1)S(1)}, u32[]{:S(2)}, u32[]{:S(2)}) collective-permute-start(bf16[64,1792]{1,0:T(8,128)(2,1)S(1)} %get-tuple-element.143), channel_id=1, source_target_pairs={{0,4},{1,5},{4,8},{5,9},{8,12},{9,13},{12,14},{13,15},{14,10},{15,... | collective-permute-start | bytes 688136 | tf_op jit(solution)/shard_map/ppermute | solution.py:79
  30.2 3.7 %near_product.2 = (bf16[128,3584]{1,0:T(8,128)(2,1)S(1)}, bf16[128,3584]{1,0:T(8,128)(2,1)S(1)}) custom-call(bf16[256,1024]{1,0:T(8,128)(2,1)S(1)} %get-tuple-element.77.left_ref, bf16[1024,3584]{1,0:T(8,128)(2,1)S(1)} %copy-done.6), custom_call_target="tpu_custom_call" | custom-call | flops 5637144576 | bytes 9699328 | tf_op jit(solution)/shard_map/near_product/pallas_call | solution.py:249
  33.9 2.1 %collective-permute-done.9 = bf16[64,1792]{1,0:T(8,128)(2,1)S(1)} collective-permute-done((bf16[64,1792]{1,0:T(8,128)(2,1)S(1)}, bf16[64,1792]{1,0:T(8,128)(2,1)S(1)}, u32[]{:S(2)}, u32[]{:S(2)}) %collective-permute-start.9) | collective-permute-done | bytes 229408 | tf_op jit(solution)/shard_map/ppermute | solution.py:79
  36.5 1.5 %collective-permute-start.11 = (bf16[64,3584]{1,0:T(8,128)(2,1)S(1)}, bf16[64,3584]{1,0:T(8,128)(2,1)S(1)}, u32[]{:S(2)}, u32[]{:S(2)}) collective-permute-start(bf16[64,3584]{1,0:T(8,128)(2,1)S(1)} %fusion), channel_id=1, source_target_pairs={{0,4},{1,5},{4,8},{5,9},{8,12},{9,13},{12,14},{13,15},{14,10},{15,... | collective-permute-start | bytes 1376264 | tf_op jit(solution)/shard_map/ppermute | solution.py:79
  38.7 3.7 %near_product.3 = (bf16[128,3584]{1,0:T(8,128)(2,1)S(1)}, bf16[128,3584]{1,0:T(8,128)(2,1)S(1)}) custom-call(bf16[256,1024]{1,0:T(8,128)(2,1)S(1)} %get-tuple-element.84.left_ref, bf16[1024,3584]{1,0:T(8,128)(2,1)S(1)} %bitcast.5), custom_call_target="tpu_custom_call" | custom-call | flops 5637144576 | bytes 9699328 | tf_op jit(solution)/shard_map/near_product/pallas_call | solution.py:249
  42.9 6.6 %collective-permute-done.15 = bf16[64,3584]{1,0:T(8,128)(2,1)S(1)} collective-permute-done((bf16[64,3584]{1,0:T(8,128)(2,1)S(1)}, bf16[64,3584]{1,0:T(8,128)(2,1)S(1)}, u32[]{:S(2)}, u32[]{:S(2)}) %collective-permute-start.15) | collective-permute-done | bytes 458784 | tf_op jit(solution)/shard_map/ppermute | solution.py:79
  50.7 1.5 %collective-permute-start.13 = (bf16[64,3584]{1,0:T(8,128)(2,1)S(1)}, bf16[64,3584]{1,0:T(8,128)(2,1)S(1)}, u32[]{:S(2)}, u32[]{:S(2)}) collective-permute-start(bf16[64,3584]{1,0:T(8,128)(2,1)S(1)} %fusion.2), channel_id=1, source_target_pairs={{0,4},{1,5},{4,8},{5,9},{8,12},{9,13},{12,14},{13,15},{14,10},{15,... | collective-permute-start | bytes 1376264 | tf_op jit(solution)/shard_map/ppermute | solution.py:79
  52.2 8.4 %collective-permute-done.16 = bf16[64,3584]{1,0:T(8,128)(2,1)S(1)} collective-permute-done((bf16[64,3584]{1,0:T(8,128)(2,1)S(1)}, bf16[64,3584]{1,0:T(8,128)(2,1)S(1)}, u32[]{:S(2)}, u32[]{:S(2)}) %collective-permute-start.16) | collective-permute-done | bytes 458784 | tf_op jit(solution)/shard_map/ppermute | solution.py:79
  61.1 2.0 %collective-permute-start.14 = (bf16[64,3584]{1,0:T(8,128)(2,1)S(1)}, bf16[64,3584]{1,0:T(8,128)(2,1)S(1)}, u32[]{:S(2)}, u32[]{:S(2)}) collective-permute-start(bf16[64,3584]{1,0:T(8,128)(2,1)S(1)} %fusion.3), channel_id=1, source_target_pairs={{0,4},{1,5},{4,8},{5,9},{8,12},{9,13},{12,14},{13,15},{14,10},{15,... | collective-permute-start | bytes 1376264 | tf_op jit(solution)/shard_map/ppermute | solution.py:79
  63.1 7.8 %collective-permute-done.17.refs_10_.refs_14_ = bf16[64,3584]{1,0:T(8,128)(2,1)S(1)} collective-permute-done((bf16[64,3584]{1,0:T(8,128)(2,1)S(1)}, bf16[64,3584]{1,0:T(8,128)(2,1)S(1)}, u32[]{:S(2)}, u32[]{:S(2)}) %collective-permute-start.17) | collective-permute-done | bytes 458784 | tf_op jit(solution)/shard_map/ppermute | solution.py:79
  71.1 1.6 %blocks.1 = bf16[2,32,3584]{2,1,0:T(8,128)(2,1)S(1)} custom-call(s32[32,1]{1,0:T(8,128)S(1)} %get-tuple-element.72.refs_0_, f32[32,3584]{1,0:T(8,128)S(1)} %copy-done, f32[32,3584]{1,0:T(8,128)S(1)} %copy-done.1, f32[32,3584]{1,0:T(8,128)S(1)} %copy-done.2, f32[32,3584]{1,0:T(8,128)S(1)} %copy-done.3, f32[32,3584]{1,0:T(8,128)S(1)} %copy-done.4, ...), custom_call_target="tpu_custom_call" | custom-call | flops 1146880 | bytes 1146880 | tf_op jit(solution)/shard_map/blocks/pallas_call | solution.py:334
  72.7 2.0 %collective-permute-start.18 = (bf16[64,3584]{1,0:T(8,128)(2,1)S(1)}, bf16[64,3584]{1,0:T(8,128)(2,1)S(1)}, u32[]{:S(2)}, u32[]{:S(2)}) collective-permute-start(bf16[64,3584]{1,0:T(8,128)(2,1)S(1)} %bitcast.6), channel_id=1, source_target_pairs={{0,4},{1,5},{4,8},{5,9},{8,12},{9,13},{12,14},{13,15},{14,10},{15,... | collective-permute-start | bytes 1376264 | tf_op jit(solution)/shard_map/ppermute | solution.py:79
  74.8 2.6 %states.1 = (f32[32,3584]{1,0:T(8,128)}, f32[32,3584]{1,0:T(8,128)}, f32[32,3584]{1,0:T(8,128)}, f32[32,3584]{1,0:T(8,128)}, f32[32,3584]{1,0:T(8,128)}, /*index=5*/f32[32,3584]{1,0:T(8,128)}) custom-call(s32[32,1]{1,0:T(8,128)S(1)} %get-tuple-element.72.refs_0_, f32[32,3584]{1,0:T(8,128)S(1)} %copy-done, f32[32,3584]{1,0:T(8,128)S(1)} %copy-done.1, ...), custom_call_target="tpu_custom_call" | custom-call | flops 1146880 | bytes 1146880 | tf_op jit(solution)/shard_map/states/pallas_call | solution.py:334
  78.2 4.0 %collective-permute-done.18.refs_0_ = bf16[64,3584]{1,0:T(8,128)(2,1)S(1)} collective-permute-done((bf16[64,3584]{1,0:T(8,128)(2,1)S(1)}, bf16[64,3584]{1,0:T(8,128)(2,1)S(1)}, u32[]{:S(2)}, u32[]{:S(2)}) %collective-permute-start.18) | collective-permute-done | bytes 458784 | tf_op jit(solution)/shard_map/ppermute | solution.py:79
  82.2 1.7 %collective-permute-start.19 = (bf16[64,3584]{1,0:T(8,128)(2,1)S(1)}, bf16[64,3584]{1,0:T(8,128)(2,1)S(1)}, u32[]{:S(2)}, u32[]{:S(2)}) collective-permute-start(bf16[64,3584]{1,0:T(8,128)(2,1)S(1)} %collective-permute-done.18.refs_0_), channel_id=1, source_target_pairs={{0,4},{1,5},{4,8},{5,9},{8,12},{9,13},{12,14},{13,15},{14,10},{15,... | collective-permute-start | bytes 1376264 | tf_op jit(solution)/shard_map/ppermute | solution.py:79
  84.7 1.1 place.7
  85.9 7.0 %collective-permute-done.19.refs_0_ = bf16[64,3584]{1,0:T(8,128)(2,1)S(1)} collective-permute-done((bf16[64,3584]{1,0:T(8,128)(2,1)S(1)}, bf16[64,3584]{1,0:T(8,128)(2,1)S(1)}, u32[]{:S(2)}, u32[]{:S(2)}) %collective-permute-start.19) | collective-permute-done | bytes 458784 | tf_op jit(solution)/shard_map/ppermute | solution.py:79
  92.9 1.7 %collective-permute-start.22 = (bf16[64,3584]{1,0:T(8,128)(2,1)S(1)}, bf16[64,3584]{1,0:T(8,128)(2,1)S(1)}, u32[]{:S(2)}, u32[]{:S(2)}) collective-permute-start(bf16[64,3584]{1,0:T(8,128)(2,1)S(1)} %collective-permute-done.19.refs_0_), channel_id=1, source_target_pairs={{0,4},{1,5},{4,8},{5,9},{8,12},{9,13},{12,14},{13,15},{14,10},{15,... | collective-permute-start | bytes 1376264 | tf_op jit(solution)/shard_map/ppermute | solution.py:79
  95.4 1.3 %place.8 = (bf16[512,3584]{1,0:T(8,128)(2,1)}, bf16[512,3584]{1,0:T(8,128)(2,1)}) custom-call(bf16[64,3584]{1,0:T(8,128)(2,1)S(1)} %collective-permute-done.19.refs_0_, bf16[64,3584]{1,0:T(8,128)(2,1)S(1)} %collective-permute-done.23.refs_1_, bf16[64,3584]{1,0:T(8,128)(2,1)S(1)} %collective-permute-done.24.refs_2_, ...), custom_call_target="tpu_custom_call", output_to_operand_aliasing={{0}: (4, {}), {1}: (5, {})} | custom-call | bytes 3670016 | tf_op jit(solution)/shard_map/place/pallas_call | solution.py:369
  96.7 6.7 %collective-permute-done.22.refs_0_ = bf16[64,3584]{1,0:T(8,128)(2,1)S(1)} collective-permute-done((bf16[64,3584]{1,0:T(8,128)(2,1)S(1)}, bf16[64,3584]{1,0:T(8,128)(2,1)S(1)}, u32[]{:S(2)}, u32[]{:S(2)}) %collective-permute-start.22) | collective-permute-done | bytes 458784 | tf_op jit(solution)/shard_map/ppermute | solution.py:79
  103.4 1.8 %collective-permute-start.29 = (bf16[64,1792]{1,0:T(8,128)(2,1)S(1)}, bf16[64,1792]{1,0:T(8,128)(2,1)S(1)}, u32[]{:S(2)}, u32[]{:S(2)}) collective-permute-start(bf16[64,1792]{1,0:T(8,128)(2,1)S(1)} %slice.126), channel_id=1, source_target_pairs={{0,4},{1,5},{4,8},{5,9},{8,12},{9,13},{12,14},{13,15},{14,10},{15,... | collective-permute-start | bytes 688136 | tf_op jit(solution)/shard_map/ppermute | solution.py:79
  106.1 1.3 %place.9 = (bf16[512,3584]{1,0:T(8,128)(2,1)}, bf16[512,3584]{1,0:T(8,128)(2,1)}) custom-call(bf16[64,3584]{1,0:T(8,128)(2,1)S(1)} %collective-permute-done.22.refs_0_, bf16[64,3584]{1,0:T(8,128)(2,1)S(1)} %collective-permute-done.27.refs_1_, bf16[64,3584]{1,0:T(8,128)(2,1)S(1)} %collective-permute-done.30.refs_2_, ...), custom_call_target="tpu_custom_call", output_to_operand_aliasing={{0}: (4, {}), {1}: (5, {})} | custom-call | bytes 3670016 | tf_op jit(solution)/shard_map/place/pallas_call | solution.py:369
  107.4 2.1 %collective-permute-done.29.refs_0_ = bf16[64,1792]{1,0:T(8,128)(2,1)S(1)} collective-permute-done((bf16[64,1792]{1,0:T(8,128)(2,1)S(1)}, bf16[64,1792]{1,0:T(8,128)(2,1)S(1)}, u32[]{:S(2)}, u32[]{:S(2)}) %collective-permute-start.29) | collective-permute-done | bytes 229408 | tf_op jit(solution)/shard_map/ppermute | solution.py:79
  109.5 1.9 %collective-permute-done.33.refs_1_ = bf16[64,1792]{1,0:T(8,128)(2,1)S(1)} collective-permute-done((bf16[64,1792]{1,0:T(8,128)(2,1)S(1)}, bf16[64,1792]{1,0:T(8,128)(2,1)S(1)}, u32[]{:S(2)}, u32[]{:S(2)}) %collective-permute-start.33) | collective-permute-done | bytes 229408 | tf_op jit(solution)/shard_map/ppermute | solution.py:79
  111.3 0.8 place.10
  112.8 1.1 place.11
  (90 shorter events, 12.8 us)
Async XLA Ops:
  1.4 3.7 %collective-permute-start.2 = (s32[1,48]{1,0:T(1,128)S(1)}, s32[1,48]{1,0:T(1,128)S(1)}, u32[]{:S(2)}, u32[]{:S(2)}) collective-permute-start(s32[1,48]{1,0:T(1,128)S(1)} %pad_add_fusion.1), channel_id=1, source_target_pairs={{0,3},{1,2},{2,1},{3,0},{4,7},{5,6},{6,5},{7,4},{8,11},{9,10},{10,... | collective-permute-start | bytes 584 | tf_op jit(solution)/shard_map/ppermute | solution.py:37
  3.8 3.5 %collective-permute-start.1 = (s32[1,48]{1,0:T(1,128)S(1)}, s32[1,48]{1,0:T(1,128)S(1)}, u32[]{:S(2)}, u32[]{:S(2)}) collective-permute-start(s32[1,48]{1,0:T(1,128)S(1)} %pad_add_fusion.1), channel_id=1, source_target_pairs={{0,2},{1,3},{2,0},{3,1},{4,6},{5,7},{6,4},{7,5},{8,10},{9,11},{10,... | collective-permute-start | bytes 584 | tf_op jit(solution)/shard_map/ppermute | solution.py:37
  4.4 2.9 %collective-permute-start = (s32[1,48]{1,0:T(1,128)S(1)}, s32[1,48]{1,0:T(1,128)S(1)}, u32[]{:S(2)}, u32[]{:S(2)}) collective-permute-start(s32[1,48]{1,0:T(1,128)S(1)} %pad_add_fusion.1), channel_id=1, source_target_pairs={{0,1},{1,0},{2,3},{3,2},{4,5},{5,4},{6,7},{7,6},{8,9},{9,8},{10,11... | collective-permute-start | bytes 584 | tf_op jit(solution)/shard_map/ppermute | solution.py:37
  8.1 12.0 %collective-permute-start.5 = (s32[4,48]{1,0:T(4,128)S(1)}, s32[4,48]{1,0:T(4,128)S(1)}, u32[]{:S(2)}, u32[]{:S(2)}) collective-permute-start(s32[4,48]{1,0:T(4,128)S(1)} %pad_add_fusion.refs_0_), channel_id=1, source_target_pairs={{0,12},{1,13},{2,14},{3,15},{4,8},{5,9},{6,10},{7,11},{8,4},{9,5},... | collective-permute-start | bytes 2312 | tf_op jit(solution)/shard_map/ppermute | solution.py:37
  11.8 8.4 %collective-permute-start.4 = (s32[4,48]{1,0:T(4,128)S(1)}, s32[4,48]{1,0:T(4,128)S(1)}, u32[]{:S(2)}, u32[]{:S(2)}) collective-permute-start(s32[4,48]{1,0:T(4,128)S(1)} %pad_add_fusion.refs_0_), channel_id=1, source_target_pairs={{0,8},{1,9},{2,10},{3,11},{4,12},{5,13},{6,14},{7,15},{8,0},{9,1},... | collective-permute-start | bytes 2312 | tf_op jit(solution)/shard_map/ppermute | solution.py:37
  11.8 8.4 %collective-permute-start.3 = (s32[4,48]{1,0:T(4,128)S(1)}, s32[4,48]{1,0:T(4,128)S(1)}, u32[]{:S(2)}, u32[]{:S(2)}) collective-permute-start(s32[4,48]{1,0:T(4,128)S(1)} %pad_add_fusion.refs_0_), channel_id=1, source_target_pairs={{0,4},{1,5},{2,6},{3,7},{4,0},{5,1},{6,2},{7,3},{8,12},{9,13},{10,... | collective-permute-start | bytes 2312 | tf_op jit(solution)/shard_map/ppermute | solution.py:37
  20.1 5.6 %collective-permute-start.7 = (bf16[128,3584]{1,0:T(8,128)(2,1)S(1)}, bf16[128,3584]{1,0:T(8,128)(2,1)S(1)}, u32[]{:S(2)}, u32[]{:S(2)}) collective-permute-start(bf16[128,3584]{1,0:T(8,128)(2,1)S(1)} %get-tuple-element.70), channel_id=1, source_target_pairs={{0,1},{1,0},{2,3},{3,2},{4,5},{5,4},{6,7},{7,6},{8,9},{9,8},{10,11... | collective-permute-start | bytes 2752520 | tf_op jit(solution)/shard_map/ppermute | solution.py:37
  28.1 7.9 %collective-permute-start.9 = (bf16[64,1792]{1,0:T(8,128)(2,1)S(1)}, bf16[64,1792]{1,0:T(8,128)(2,1)S(1)}, u32[]{:S(2)}, u32[]{:S(2)}) collective-permute-start(bf16[64,1792]{1,0:T(8,128)(2,1)S(1)} %get-tuple-element.142), channel_id=1, source_target_pairs={{0,2},{1,3},{4,0},{5,1},{8,4},{9,5},{12,8},{13,9},{14,12},{15,13},... | collective-permute-start | bytes 688136 | tf_op jit(solution)/shard_map/ppermute | solution.py:79
  28.8 7.6 %collective-permute-start.8 = (bf16[64,1792]{1,0:T(8,128)(2,1)S(1)}, bf16[64,1792]{1,0:T(8,128)(2,1)S(1)}, u32[]{:S(2)}, u32[]{:S(2)}) collective-permute-start(bf16[64,1792]{1,0:T(8,128)(2,1)S(1)} %get-tuple-element.143), channel_id=1, source_target_pairs={{0,4},{1,5},{4,8},{5,9},{8,12},{9,13},{12,14},{13,15},{14,10},{15,... | collective-permute-start | bytes 688136 | tf_op jit(solution)/shard_map/ppermute | solution.py:79
  36.5 14.1 %collective-permute-start.11 = (bf16[64,3584]{1,0:T(8,128)(2,1)S(1)}, bf16[64,3584]{1,0:T(8,128)(2,1)S(1)}, u32[]{:S(2)}, u32[]{:S(2)}) collective-permute-start(bf16[64,3584]{1,0:T(8,128)(2,1)S(1)} %fusion), channel_id=1, source_target_pairs={{0,4},{1,5},{4,8},{5,9},{8,12},{9,13},{12,14},{13,15},{14,10},{15,... | collective-permute-start | bytes 1376264 | tf_op jit(solution)/shard_map/ppermute | solution.py:79
  38.0 11.5 %collective-permute-start.15 = (bf16[64,3584]{1,0:T(8,128)(2,1)S(1)}, bf16[64,3584]{1,0:T(8,128)(2,1)S(1)}, u32[]{:S(2)}, u32[]{:S(2)}) collective-permute-start(bf16[64,3584]{1,0:T(8,128)(2,1)S(1)} %fusion.1), channel_id=1, source_target_pairs={{0,2},{1,3},{4,0},{5,1},{8,4},{9,5},{12,8},{13,9},{14,12},{15,13},... | collective-permute-start | bytes 1376264 | tf_op jit(solution)/shard_map/ppermute | solution.py:79
  38.6 11.7 %collective-permute-start.10 = (bf16[128,3584]{1,0:T(8,128)(2,1)S(1)}, bf16[128,3584]{1,0:T(8,128)(2,1)S(1)}, u32[]{:S(2)}, u32[]{:S(2)}) collective-permute-start(bf16[128,3584]{1,0:T(8,128)(2,1)S(1)} %get-tuple-element.80), channel_id=1, source_target_pairs={{0,1},{1,0},{2,3},{3,2},{4,5},{5,4},{6,7},{7,6},{8,9},{9,8},{10,11... | collective-permute-start | bytes 2752520 | tf_op jit(solution)/shard_map/ppermute | solution.py:37
  42.4 7.8 %collective-permute-start.12 = (bf16[128,3584]{1,0:T(8,128)(2,1)S(1)}, bf16[128,3584]{1,0:T(8,128)(2,1)S(1)}, u32[]{:S(2)}, u32[]{:S(2)}) collective-permute-start(bf16[128,3584]{1,0:T(8,128)(2,1)S(1)} %get-tuple-element.86), channel_id=1, source_target_pairs={{0,1},{1,0},{2,3},{3,2},{4,5},{5,4},{6,7},{7,6},{8,9},{9,8},{10,11... | collective-permute-start | bytes 2752520 | tf_op jit(solution)/shard_map/ppermute | solution.py:37
  49.6 11.1 %collective-permute-start.16 = (bf16[64,3584]{1,0:T(8,128)(2,1)S(1)}, bf16[64,3584]{1,0:T(8,128)(2,1)S(1)}, u32[]{:S(2)}, u32[]{:S(2)}) collective-permute-start(bf16[64,3584]{1,0:T(8,128)(2,1)S(1)} %fusion.4), channel_id=1, source_target_pairs={{0,2},{1,3},{4,0},{5,1},{8,4},{9,5},{12,8},{13,9},{14,12},{15,13},... | collective-permute-start | bytes 1376264 | tf_op jit(solution)/shard_map/ppermute | solution.py:79
  50.7 10.4 %collective-permute-start.13 = (bf16[64,3584]{1,0:T(8,128)(2,1)S(1)}, bf16[64,3584]{1,0:T(8,128)(2,1)S(1)}, u32[]{:S(2)}, u32[]{:S(2)}) collective-permute-start(bf16[64,3584]{1,0:T(8,128)(2,1)S(1)} %fusion.2), channel_id=1, source_target_pairs={{0,4},{1,5},{4,8},{5,9},{8,12},{9,13},{12,14},{13,15},{14,10},{15,... | collective-permute-start | bytes 1376264 | tf_op jit(solution)/shard_map/ppermute | solution.py:79
  60.7 10.2 %collective-permute-start.17 = (bf16[64,3584]{1,0:T(8,128)(2,1)S(1)}, bf16[64,3584]{1,0:T(8,128)(2,1)S(1)}, u32[]{:S(2)}, u32[]{:S(2)}) collective-permute-start(bf16[64,3584]{1,0:T(8,128)(2,1)S(1)} %fusion.5), channel_id=1, source_target_pairs={{0,2},{1,3},{4,0},{5,1},{8,4},{9,5},{12,8},{13,9},{14,12},{15,13},... | collective-permute-start | bytes 1376264 | tf_op jit(solution)/shard_map/ppermute | solution.py:79
  61.1 9.9 %collective-permute-start.14 = (bf16[64,3584]{1,0:T(8,128)(2,1)S(1)}, bf16[64,3584]{1,0:T(8,128)(2,1)S(1)}, u32[]{:S(2)}, u32[]{:S(2)}) collective-permute-start(bf16[64,3584]{1,0:T(8,128)(2,1)S(1)} %fusion.3), channel_id=1, source_target_pairs={{0,4},{1,5},{4,8},{5,9},{8,12},{9,13},{12,14},{13,15},{14,10},{15,... | collective-permute-start | bytes 1376264 | tf_op jit(solution)/shard_map/ppermute | solution.py:79
  72.7 9.5 %collective-permute-start.18 = (bf16[64,3584]{1,0:T(8,128)(2,1)S(1)}, bf16[64,3584]{1,0:T(8,128)(2,1)S(1)}, u32[]{:S(2)}, u32[]{:S(2)}) collective-permute-start(bf16[64,3584]{1,0:T(8,128)(2,1)S(1)} %bitcast.6), channel_id=1, source_target_pairs={{0,4},{1,5},{4,8},{5,9},{8,12},{9,13},{12,14},{13,15},{14,10},{15,... | collective-permute-start | bytes 1376264 | tf_op jit(solution)/shard_map/ppermute | solution.py:79
  74.7 9.2 %collective-permute-start.20 = (bf16[64,3584]{1,0:T(8,128)(2,1)S(1)}, bf16[64,3584]{1,0:T(8,128)(2,1)S(1)}, u32[]{:S(2)}, u32[]{:S(2)}) collective-permute-start(bf16[64,3584]{1,0:T(8,128)(2,1)S(1)} %bitcast.7), channel_id=1, source_target_pairs={{0,2},{1,3},{4,0},{5,1},{8,4},{9,5},{12,8},{13,9},{14,12},{15,13},... | collective-permute-start | bytes 1376264 | tf_op jit(solution)/shard_map/ppermute | solution.py:79
  77.4 7.4 %collective-permute-start.21 = (bf16[64,3584]{1,0:T(8,128)(2,1)S(1)}, bf16[64,3584]{1,0:T(8,128)(2,1)S(1)}, u32[]{:S(2)}, u32[]{:S(2)}) collective-permute-start(bf16[64,3584]{1,0:T(8,128)(2,1)S(1)} %bitcast.8), channel_id=1, source_target_pairs={{0,1},{1,0},{2,3},{3,2},{4,5},{5,4},{6,7},{7,6},{8,9},{9,8},{10,11... | collective-permute-start | bytes 1376264 | tf_op jit(solution)/shard_map/ppermute | solution.py:37
  82.2 10.7 %collective-permute-start.19 = (bf16[64,3584]{1,0:T(8,128)(2,1)S(1)}, bf16[64,3584]{1,0:T(8,128)(2,1)S(1)}, u32[]{:S(2)}, u32[]{:S(2)}) collective-permute-start(bf16[64,3584]{1,0:T(8,128)(2,1)S(1)} %collective-permute-done.18.refs_0_), channel_id=1, source_target_pairs={{0,4},{1,5},{4,8},{5,9},{8,12},{9,13},{12,14},{13,15},{14,10},{15,... | collective-permute-start | bytes 1376264 | tf_op jit(solution)/shard_map/ppermute | solution.py:79
  83.9 10.7 %collective-permute-start.23 = (bf16[64,3584]{1,0:T(8,128)(2,1)S(1)}, bf16[64,3584]{1,0:T(8,128)(2,1)S(1)}, u32[]{:S(2)}, u32[]{:S(2)}) collective-permute-start(bf16[64,3584]{1,0:T(8,128)(2,1)S(1)} %collective-permute-done.20.refs_1_), channel_id=1, source_target_pairs={{0,2},{1,3},{4,0},{5,1},{8,4},{9,5},{12,8},{13,9},{14,12},{15,13},... | collective-permute-start | bytes 1376264 | tf_op jit(solution)/shard_map/ppermute | solution.py:79
  84.2 10.7 %collective-permute-start.25 = (bf16[64,3584]{1,0:T(8,128)(2,1)S(1)}, bf16[64,3584]{1,0:T(8,128)(2,1)S(1)}, u32[]{:S(2)}, u32[]{:S(2)}) collective-permute-start(bf16[64,3584]{1,0:T(8,128)(2,1)S(1)} %collective-permute-done.20.refs_1_), channel_id=1, source_target_pairs={{0,1},{1,0},{2,3},{3,2},{4,5},{5,4},{6,7},{7,6},{8,9},{9,8},{10,11... | collective-permute-start | bytes 1376264 | tf_op jit(solution)/shard_map/ppermute | solution.py:37
  84.2 11.2 %collective-permute-start.24 = (bf16[64,3584]{1,0:T(8,128)(2,1)S(1)}, bf16[64,3584]{1,0:T(8,128)(2,1)S(1)}, u32[]{:S(2)}, u32[]{:S(2)}) collective-permute-start(bf16[64,3584]{1,0:T(8,128)(2,1)S(1)} %collective-permute-done.18.refs_0_), channel_id=1, source_target_pairs={{0,1},{1,0},{2,3},{3,2},{4,5},{5,4},{6,7},{7,6},{8,9},{9,8},{10,11... | collective-permute-start | bytes 1376264 | tf_op jit(solution)/shard_map/ppermute | solution.py:37
  92.9 10.5 %collective-permute-start.22 = (bf16[64,3584]{1,0:T(8,128)(2,1)S(1)}, bf16[64,3584]{1,0:T(8,128)(2,1)S(1)}, u32[]{:S(2)}, u32[]{:S(2)}) collective-permute-start(bf16[64,3584]{1,0:T(8,128)(2,1)S(1)} %collective-permute-done.19.refs_0_), channel_id=1, source_target_pairs={{0,4},{1,5},{4,8},{5,9},{8,12},{9,13},{12,14},{13,15},{14,10},{15,... | collective-permute-start | bytes 1376264 | tf_op jit(solution)/shard_map/ppermute | solution.py:79
  94.6 10.7 %collective-permute-start.27 = (bf16[64,3584]{1,0:T(8,128)(2,1)S(1)}, bf16[64,3584]{1,0:T(8,128)(2,1)S(1)}, u32[]{:S(2)}, u32[]{:S(2)}) collective-permute-start(bf16[64,3584]{1,0:T(8,128)(2,1)S(1)} %collective-permute-done.23.refs_1_), channel_id=1, source_target_pairs={{0,2},{1,3},{4,0},{5,1},{8,4},{9,5},{12,8},{13,9},{14,12},{15,13},... | collective-permute-start | bytes 1376264 | tf_op jit(solution)/shard_map/ppermute | solution.py:79
  94.9 10.7 %collective-permute-start.31 = (bf16[64,3584]{1,0:T(8,128)(2,1)S(1)}, bf16[64,3584]{1,0:T(8,128)(2,1)S(1)}, u32[]{:S(2)}, u32[]{:S(2)}) collective-permute-start(bf16[64,3584]{1,0:T(8,128)(2,1)S(1)} %collective-permute-done.23.refs_1_), channel_id=1, source_target_pairs={{0,1},{1,0},{2,3},{3,2},{4,5},{5,4},{6,7},{7,6},{8,9},{9,8},{10,11... | collective-permute-start | bytes 1376264 | tf_op jit(solution)/shard_map/ppermute | solution.py:37
  94.9 11.2 %collective-permute-start.30 = (bf16[64,3584]{1,0:T(8,128)(2,1)S(1)}, bf16[64,3584]{1,0:T(8,128)(2,1)S(1)}, u32[]{:S(2)}, u32[]{:S(2)}) collective-permute-start(bf16[64,3584]{1,0:T(8,128)(2,1)S(1)} %collective-permute-done.19.refs_0_), channel_id=1, source_target_pairs={{0,1},{1,0},{2,3},{3,2},{4,5},{5,4},{6,7},{7,6},{8,9},{9,8},{10,11... | collective-permute-start | bytes 1376264 | tf_op jit(solution)/shard_map/ppermute | solution.py:37
  103.4 6.1 %collective-permute-start.29 = (bf16[64,1792]{1,0:T(8,128)(2,1)S(1)}, bf16[64,1792]{1,0:T(8,128)(2,1)S(1)}, u32[]{:S(2)}, u32[]{:S(2)}) collective-permute-start(bf16[64,1792]{1,0:T(8,128)(2,1)S(1)} %slice.126), channel_id=1, source_target_pairs={{0,4},{1,5},{4,8},{5,9},{8,12},{9,13},{12,14},{13,15},{14,10},{15,... | collective-permute-start | bytes 688136 | tf_op jit(solution)/shard_map/ppermute | solution.py:79
  105.3 6.1 %collective-permute-start.33 = (bf16[64,1792]{1,0:T(8,128)(2,1)S(1)}, bf16[64,1792]{1,0:T(8,128)(2,1)S(1)}, u32[]{:S(2)}, u32[]{:S(2)}) collective-permute-start(bf16[64,1792]{1,0:T(8,128)(2,1)S(1)} %slice.127), channel_id=1, source_target_pairs={{0,2},{1,3},{4,0},{5,1},{8,4},{9,5},{12,8},{13,9},{14,12},{15,13},... | collective-permute-start | bytes 688136 | tf_op jit(solution)/shard_map/ppermute | solution.py:79
  105.6 7.3 %collective-permute-start.28 = (bf16[64,3584]{1,0:T(8,128)(2,1)S(1)}, bf16[64,3584]{1,0:T(8,128)(2,1)S(1)}, u32[]{:S(2)}, u32[]{:S(2)}) collective-permute-start(bf16[64,3584]{1,0:T(8,128)(2,1)S(1)} %collective-permute-done.27.refs_1_), channel_id=1, source_target_pairs={{0,1},{1,0},{2,3},{3,2},{4,5},{5,4},{6,7},{7,6},{8,9},{9,8},{10,11... | collective-permute-start | bytes 1376264 | tf_op jit(solution)/shard_map/ppermute | solution.py:37
  105.6 7.3 %collective-permute-start.26 = (bf16[64,3584]{1,0:T(8,128)(2,1)S(1)}, bf16[64,3584]{1,0:T(8,128)(2,1)S(1)}, u32[]{:S(2)}, u32[]{:S(2)}) collective-permute-start(bf16[64,3584]{1,0:T(8,128)(2,1)S(1)} %collective-permute-done.22.refs_0_), channel_id=1, source_target_pairs={{0,1},{1,0},{2,3},{3,2},{4,5},{5,4},{6,7},{7,6},{8,9},{9,8},{10,11... | collective-permute-start | bytes 1376264 | tf_op jit(solution)/shard_map/ppermute | solution.py:37
  (15 other events, 191.9 us)

commit v15 on v13

--- a/solution.py
+++ b/solution.py
@@ -316,7 +316,7 @@
         ref[...] = value
 
 
-def update(code, states, enc_parts, dec_parts, came, blocks_only):
+def update(code, states, enc_parts, dec_parts, blocks_only):
     rows, width = states[0].shape
     tile = 16
 
@@ -324,9 +324,7 @@
         return pl.BlockSpec((tile, value.shape[1]), lambda i: (i + skipped // tile, 0))
 
     operands = [(value, 0) for value in [code] + list(states)]
-    for parts, first in ((enc_parts, 0), (dec_parts, rows)):
-        operands += [(value, value.shape[0] - rows) for value in parts]
-        operands += [(value, first) for value in came]
+    operands += [(value, value.shape[0] - rows) for value in enc_parts + dec_parts]
     if blocks_only:
         out_shape = [jax.ShapeDtypeStruct((2, rows, width), jnp.bfloat16)]
         out_specs = [pl.BlockSpec((2, tile, width), lambda i: (0, i, 0))]
@@ -432,34 +430,44 @@
     )
     enc_kept, enc_core = [kept], [swap(enc_sent, 1, size)]
 
-    def both(slot):
-        terms = [term(*pair, slot, rows) for pair in ((enc_kept, enc_core), (dec_kept, dec_core))]
-        return jnp.concatenate(terms, axis=0)
+    def begin(kept, from_core):
+        far = term(kept, from_core, 0, rows).astype(jnp.bfloat16)
+        return [far[:, :half], far[:, half:]]
 
     def travel(moving):
         return [shift(moving[0], 1, size), shift(moving[1], -1, size)]
 
-    far = both(0).astype(jnp.bfloat16)
-    moving = [far[:, :half], far[:, half:]]
-    enc_sent, kept = near_product(after(enc_left, *moving), x_rows)
-    came, enc_sent = tied(travel(moving), enc_sent)
-    enc_kept.append(kept)
-    enc_core.append(swap(enc_sent, 1, size))
-    for hop in range(1, chips // 2):
+    def advance(came, kept, from_core, hop, order):
         moving = []
-        for side, value in enumerate(came):
+        for side, value in enumerate(after(came, order)):
             value = value.astype(jnp.float32)
             if value.shape[1] < width:
                 pads = ((0, 0, 0), (0, half, 0) if side == 0 else (half, 0, 0))
                 value = lax.pad(value, jnp.float32(0), pads)
-            moving.append((value + both(2 * hop - side)).astype(jnp.bfloat16))
-        came = travel(moving)
-        if hop == 1:
-            dec_sent, kept = near_product(after(dec_left, *moving), out_grad)
-            dec_kept.append(kept)
-            dec_core.append(swap(dec_sent, 1, size))
+            value = value + term(kept, from_core, 2 * hop - side, rows)
+            moving.append(value.astype(jnp.bfloat16))
+        return travel(moving), moving
+
+    dec_moving = begin(dec_kept, dec_core)
+    dec_came = travel(dec_moving)
+    enc_moving = begin(enc_kept, after(enc_core, *dec_moving))
+    enc_sent, kept = near_product(after(enc_left, *enc_moving), x_rows)
+    enc_came, enc_sent = tied(travel(enc_moving), enc_sent)
+    enc_kept.append(kept)
+    enc_core.append(swap(enc_sent, 1, size))
+    dec_came, order = advance(dec_came, dec_kept, dec_core, 1, enc_sent)
+    enc_came, order = advance(enc_came, enc_kept, enc_core, 1, order)
+    dec_sent, kept = near_product(after(dec_left, *order), out_grad)
+    dec_kept.append(kept)
+    dec_core.append(swap(dec_sent, 1, size))
+    order = dec_sent
+    for hop in range(2, chips // 2):
+        dec_came, order = advance(dec_came, dec_kept, dec_core, hop, order)
+        if hop == chips // 2 - 1:
+            order = (order, dec_came)
+        enc_came, order = advance(enc_came, enc_kept, enc_core, hop, order)
     states = (enc_w, enc_m, enc_v, dec_w, dec_m, dec_v)
-    parts = ([enc_kept[1], enc_core[1]], [dec_kept[1], dec_core[1]], came)
+    parts = ([enc_kept[1], enc_core[1]] + enc_came, [dec_kept[1], dec_core[1]] + dec_came)
     (blocks,) = update(code, states, *parts, True)
     results = update(code, after(states, blocks), *parts, False)
     enc_full, dec_full = gathered(blocks.reshape(2 * rows, width), results[0], size, rows)

time: 113 us -> 116 us (1.027)
  starting transfers between devices: 27.3 us -> 35.1 us
  waiting for transfers between devices: 51.6 us -> 46.8 us
    ppermute x16 -> x24, starting transfers between devices: 16.9 us -> 25.2 us  [shift(): return lax.ppermute(value, 'latent', pairs)]
    ppermute x16 -> x24, waiting for transfers between devices: 44.8 us -> 42 us  [shift(): return lax.ppermute(value, 'latent', pairs)]
    ppermute x19, waiting for transfers between devices: 6.79 us -> 4.83 us  [swap(): return lax.ppermute(value, 'latent', [(i, i ^ bits) for i in range(size)])]
  transfers between devices with their start and end apart: 35 -> 43, of which waited for: 19 -> 22; matrix products, arithmetic and copies ran while one was open for 1% -> 1% of each run, Pallas kernels for 25% -> 24%
where the time goes in v15:
time: 116 us; the launch traced here: 115 us
  waiting for transfers between devices  46.8 us (40%)
  starting transfers between devices  35.1 us (30%)
  Pallas kernels  30.5 us (26%)
  other arithmetic  1.94 us (2%)
    ppermute x24, waiting for transfers between devices, shift(): return lax.ppermute(value, 'latent', pairs)  42 us
    ppermute x24, starting transfers between devices, shift(): return lax.ppermute(value, 'latent', pairs)  25.2 us
    pallas_call x3, Pallas kernels, product(): pl.pallas_call(kernel, grid=(width // tile,), in_specs=in_specs + [pl.Blo...  12.3 us
    ppermute x19, starting transfers between devices, swap(): return lax.ppermute(value, 'latent', [(i, i ^ bits) for i in range(size)])  9.87 us
    pallas_call x1, Pallas kernels, stream_far_product(): pl.pallas_call(functools.partial(stream_kernel, size, rows), in_specs=[an...  7.57 us
    pallas_call x6, Pallas kernels, place(): pl.pallas_call(functools.partial(place_kernel, plan, size, rows, count),...  6.39 us
    ppermute x19, waiting for transfers between devices, swap(): return lax.ppermute(value, 'latent', [(i, i ^ bits) for i in range(size)])  4.83 us
    pallas_call x2, Pallas kernels, update(): pl.pallas_call(blocks_kernel if blocks_only else states_kernel, grid=(row...  4.19 us
  transfers between devices with their start and end apart: 43, of which 22 were waited for; matrix products, arithmetic and copies ran while one was open for 1% of the time, Pallas kernels for 24%

profile of v15, /device:TPU:0, one launch (start us, length us, event | category | flops | bytes accessed | tf_op | source)
XLA Modules:
  0.0 115.4 jit_solution(15557305865724655473)
XLA Ops:
  1.4 2.5 %collective-permute-start.2 = (s32[1,48]{1,0:T(1,128)S(1)}, s32[1,48]{1,0:T(1,128)S(1)}, u32[]{:S(2)}, u32[]{:S(2)}) collective-permute-start(s32[1,48]{1,0:T(1,128)S(1)} %pad_add_fusion.1), channel_id=1, source_target_pairs={{0,3},{1,2},{2,1},{3,0},{4,7},{5,6},{6,5},{7,4},{8,11},{9,10},{10,... | collective-permute-start | bytes 584 | tf_op jit(solution)/shard_map/ppermute | solution.py:37
  4.6 7.6 %stream_far_product.1 = (bf16[128,3584]{1,0:T(8,128)(2,1)S(1)}, bf16[128,3584]{1,0:T(8,128)(2,1)}, bf16[256,1024]{1,0:T(8,128)(2,1)S(1)}) custom-call(bf16[1024,512]{1,0:T(8,128)(2,1)} %coef_hbm.1, bf16[1024,3584]{1,0:T(8,128)(2,1)} %right_ref.5), custom_call_target="tpu_custom_call" | custom-call | flops 1879048192 | bytes 10223616 | tf_op jit(solution)/shard_map/stream_far_product/pallas_call | solution.py:187
  12.8 3.9 %collective-permute-start.5 = (s32[4,48]{1,0:T(4,128)S(1)}, s32[4,48]{1,0:T(4,128)S(1)}, u32[]{:S(2)}, u32[]{:S(2)}) collective-permute-start(s32[4,48]{1,0:T(4,128)S(1)} %pad_add_fusion.refs_0_), channel_id=1, source_target_pairs={{0,12},{1,13},{2,14},{3,15},{4,8},{5,9},{6,10},{7,11},{8,4},{9,5},... | collective-permute-start | bytes 2312 | tf_op jit(solution)/shard_map/ppermute | solution.py:37
  18.2 2.9 %collective-permute-done.4.refs_2_ = s32[4,48]{1,0:T(4,128)S(1)} collective-permute-done((s32[4,48]{1,0:T(4,128)S(1)}, s32[4,48]{1,0:T(4,128)S(1)}, u32[]{:S(2)}, u32[]{:S(2)}) %collective-permute-start.4) | collective-permute-done | bytes 800 | tf_op jit(solution)/shard_map/ppermute | solution.py:37
  21.2 4.9 %far_product.1 = (bf16[128,3584]{1,0:T(8,128)(2,1)S(1)}, bf16[128,3584]{1,0:T(8,128)(2,1)S(1)}, bf16[256,1024]{1,0:T(8,128)(2,1)S(1)}, s32[32,1]{1,0:T(8,128)S(1)}) custom-call(bf16[1024,512]{1,0:T(8,128)(2,1)S(1)} %copy-done.7, bf16[1024,3584]{1,0:T(8,128)(2,1)S(1)} %copy-done.6, s32[2,16]{1,0:T(2,128)S(1)} %bitcast.10, s32[4,48]{1,0:T(4,128)S(1)} %pad_add_fusion.refs_0_, ...), custom_call_target="tpu_custom_call" | custom-call | flops 5637144576 | bytes 9699328 | tf_op jit(solution)/shard_map/far_product/pallas_call | solution.py:251
  26.3 1.6 %collective-permute-start.12 = (bf16[32,1792]{1,0:T(8,128)(2,1)S(1)}, bf16[32,1792]{1,0:T(8,128)(2,1)S(1)}, u32[]{:S(2)}, u32[]{:S(2)}) collective-permute-start(bf16[32,1792]{1,0:T(8,128)(2,1)S(1)} %get-tuple-element.162), channel_id=1, source_target_pairs={{0,2},{1,3},{4,0},{5,1},{8,4},{9,5},{12,8},{13,9},{14,12},{15,13},... | collective-permute-start | bytes 344072 | tf_op jit(solution)/shard_map/ppermute | solution.py:79
  28.8 1.6 %collective-permute-start.9 = (bf16[32,1792]{1,0:T(8,128)(2,1)S(1)}, bf16[32,1792]{1,0:T(8,128)(2,1)S(1)}, u32[]{:S(2)}, u32[]{:S(2)}) collective-permute-start(bf16[32,1792]{1,0:T(8,128)(2,1)S(1)} %get-tuple-element.160), channel_id=1, source_target_pairs={{0,2},{1,3},{4,0},{5,1},{8,4},{9,5},{12,8},{13,9},{14,12},{15,13},... | collective-permute-start | bytes 344072 | tf_op jit(solution)/shard_map/ppermute | solution.py:79
  30.8 3.7 %near_product.2 = (bf16[128,3584]{1,0:T(8,128)(2,1)S(1)}, bf16[128,3584]{1,0:T(8,128)(2,1)S(1)}) custom-call(bf16[256,1024]{1,0:T(8,128)(2,1)S(1)} %get-tuple-element.89.left_ref, bf16[1024,3584]{1,0:T(8,128)(2,1)S(1)} %copy-done.6), custom_call_target="tpu_custom_call" | custom-call | flops 5637144576 | bytes 9699328 | tf_op jit(solution)/shard_map/near_product/pallas_call | solution.py:251
  40.1 3.7 %near_product.3 = (bf16[128,3584]{1,0:T(8,128)(2,1)S(1)}, bf16[128,3584]{1,0:T(8,128)(2,1)S(1)}) custom-call(bf16[256,1024]{1,0:T(8,128)(2,1)S(1)} %get-tuple-element.100.left_ref, bf16[1024,3584]{1,0:T(8,128)(2,1)S(1)} %bitcast.5), custom_call_target="tpu_custom_call" | custom-call | flops 5637144576 | bytes 9699328 | tf_op jit(solution)/shard_map/near_product/pallas_call | solution.py:251
  45.2 1.8 %collective-permute-start.21 = (bf16[32,3584]{1,0:T(8,128)(2,1)S(1)}, bf16[32,3584]{1,0:T(8,128)(2,1)S(1)}, u32[]{:S(2)}, u32[]{:S(2)}) collective-permute-start(bf16[32,3584]{1,0:T(8,128)(2,1)S(1)} %add_convert_fusion.6), channel_id=1, source_target_pairs={{0,2},{1,3},{4,0},{5,1},{8,4},{9,5},{12,8},{13,9},{14,12},{15,13},... | collective-permute-start | bytes 688136 | tf_op jit(solution)/shard_map/ppermute | solution.py:79
  47.4 1.7 %collective-permute-done.14 = bf16[32,3584]{1,0:T(8,128)(2,1)S(1)} collective-permute-done((bf16[32,3584]{1,0:T(8,128)(2,1)S(1)}, bf16[32,3584]{1,0:T(8,128)(2,1)S(1)}, u32[]{:S(2)}, u32[]{:S(2)}) %collective-permute-start.14) | collective-permute-done | bytes 229408 | tf_op jit(solution)/shard_map/ppermute | solution.py:79
  49.4 1.5 %collective-permute-start.18 = (bf16[32,3584]{1,0:T(8,128)(2,1)S(1)}, bf16[32,3584]{1,0:T(8,128)(2,1)S(1)}, u32[]{:S(2)}, u32[]{:S(2)}) collective-permute-start(bf16[32,3584]{1,0:T(8,128)(2,1)S(1)} %add_convert_fusion.5), channel_id=1, source_target_pairs={{0,4},{1,5},{4,8},{5,9},{8,12},{9,13},{12,14},{13,15},{14,10},{15,... | collective-permute-start | bytes 688136 | tf_op jit(solution)/shard_map/ppermute | solution.py:79
  51.8 2.2 %collective-permute-done.21 = bf16[32,3584]{1,0:T(8,128)(2,1)S(1)} collective-permute-done((bf16[32,3584]{1,0:T(8,128)(2,1)S(1)}, bf16[32,3584]{1,0:T(8,128)(2,1)S(1)}, u32[]{:S(2)}, u32[]{:S(2)}) %collective-permute-start.21) | collective-permute-done | bytes 229408 | tf_op jit(solution)/shard_map/ppermute | solution.py:79
  54.1 1.6 %collective-permute-done.20 = bf16[32,3584]{1,0:T(8,128)(2,1)S(1)} collective-permute-done((bf16[32,3584]{1,0:T(8,128)(2,1)S(1)}, bf16[32,3584]{1,0:T(8,128)(2,1)S(1)}, u32[]{:S(2)}, u32[]{:S(2)}) %collective-permute-start.20) | collective-permute-done | bytes 229408 | tf_op jit(solution)/shard_map/ppermute | solution.py:79
  56.7 1.2 %collective-permute-start.22 = (bf16[32,3584]{1,0:T(8,128)(2,1)S(1)}, bf16[32,3584]{1,0:T(8,128)(2,1)S(1)}, u32[]{:S(2)}, u32[]{:S(2)}) collective-permute-start(bf16[32,3584]{1,0:T(8,128)(2,1)S(1)} %get-tuple-element.155), channel_id=1, source_target_pairs={{0,4},{1,5},{4,8},{5,9},{8,12},{9,13},{12,14},{13,15},{14,10},{15,... | collective-permute-start | bytes 688136 | tf_op jit(solution)/shard_map/ppermute | solution.py:79
  57.9 2.7 %collective-permute-done.18 = bf16[32,3584]{1,0:T(8,128)(2,1)S(1)} collective-permute-done((bf16[32,3584]{1,0:T(8,128)(2,1)S(1)}, bf16[32,3584]{1,0:T(8,128)(2,1)S(1)}, u32[]{:S(2)}, u32[]{:S(2)}) %collective-permute-start.18) | collective-permute-done | bytes 229408 | tf_op jit(solution)/shard_map/ppermute | solution.py:79
  60.5 3.0 %collective-permute-done.23.refs_14_ = bf16[32,3584]{1,0:T(8,128)(2,1)S(1)} collective-permute-done((bf16[32,3584]{1,0:T(8,128)(2,1)S(1)}, bf16[32,3584]{1,0:T(8,128)(2,1)S(1)}, u32[]{:S(2)}, u32[]{:S(2)}) %collective-permute-start.23) | collective-permute-done | bytes 229408 | tf_op jit(solution)/shard_map/ppermute | solution.py:79
  64.6 1.4 %collective-permute-start.25 = (bf16[32,3584]{1,0:T(8,128)(2,1)S(1)}, bf16[32,3584]{1,0:T(8,128)(2,1)S(1)}, u32[]{:S(2)}, u32[]{:S(2)}) collective-permute-start(bf16[32,3584]{1,0:T(8,128)(2,1)S(1)} %get-tuple-element.152), channel_id=1, source_target_pairs={{0,2},{1,3},{4,0},{5,1},{8,4},{9,5},{12,8},{13,9},{14,12},{15,13},... | collective-permute-start | bytes 688136 | tf_op jit(solution)/shard_map/ppermute | solution.py:79
  66.7 4.6 %collective-permute-done.25.refs_10_ = bf16[32,3584]{1,0:T(8,128)(2,1)S(1)} collective-permute-done((bf16[32,3584]{1,0:T(8,128)(2,1)S(1)}, bf16[32,3584]{1,0:T(8,128)(2,1)S(1)}, u32[]{:S(2)}, u32[]{:S(2)}) %collective-permute-start.25) | collective-permute-done | bytes 229408 | tf_op jit(solution)/shard_map/ppermute | solution.py:79
  71.2 1.2 %collective-permute-done.24.refs_9_ = bf16[32,3584]{1,0:T(8,128)(2,1)S(1)} collective-permute-done((bf16[32,3584]{1,0:T(8,128)(2,1)S(1)}, bf16[32,3584]{1,0:T(8,128)(2,1)S(1)}, u32[]{:S(2)}, u32[]{:S(2)}) %collective-permute-start.24) | collective-permute-done | bytes 229408 | tf_op jit(solution)/shard_map/ppermute | solution.py:79
  72.5 1.6 %blocks.1 = bf16[2,32,3584]{2,1,0:T(8,128)(2,1)S(1)} custom-call(s32[32,1]{1,0:T(8,128)S(1)} %get-tuple-element.83.refs_0_, f32[32,3584]{1,0:T(8,128)S(1)} %copy-done, f32[32,3584]{1,0:T(8,128)S(1)} %copy-done.1, f32[32,3584]{1,0:T(8,128)S(1)} %copy-done.2, f32[32,3584]{1,0:T(8,128)S(1)} %copy-done.3, f32[32,3584]{1,0:T(8,128)S(1)} %copy-done.4, ...), custom_call_target="tpu_custom_call" | custom-call | flops 1146880 | bytes 1146880 | tf_op jit(solution)/shard_map/blocks/pallas_call | solution.py:334
  74.7 1.5 %collective-permute-start.28 = (bf16[64,3584]{1,0:T(8,128)(2,1)S(1)}, bf16[64,3584]{1,0:T(8,128)(2,1)S(1)}, u32[]{:S(2)}, u32[]{:S(2)}) collective-permute-start(bf16[64,3584]{1,0:T(8,128)(2,1)S(1)} %bitcast.7), channel_id=1, source_target_pairs={{0,2},{1,3},{4,0},{5,1},{8,4},{9,5},{12,8},{13,9},{14,12},{15,13},... | collective-permute-start | bytes 1376264 | tf_op jit(solution)/shard_map/ppermute | solution.py:79
  76.2 2.6 %states.1 = (f32[32,3584]{1,0:T(8,128)}, f32[32,3584]{1,0:T(8,128)}, f32[32,3584]{1,0:T(8,128)}, f32[32,3584]{1,0:T(8,128)}, f32[32,3584]{1,0:T(8,128)}, /*index=5*/f32[32,3584]{1,0:T(8,128)}) custom-call(s32[32,1]{1,0:T(8,128)S(1)} %get-tuple-element.83.refs_0_, f32[32,3584]{1,0:T(8,128)S(1)} %copy-done, f32[32,3584]{1,0:T(8,128)S(1)} %copy-done.1, ...), custom_call_target="tpu_custom_call" | custom-call | flops 1146880 | bytes 1146880 | tf_op jit(solution)/shard_map/states/pallas_call | solution.py:334
  79.5 5.3 %collective-permute-done.26.refs_0_ = bf16[64,3584]{1,0:T(8,128)(2,1)S(1)} collective-permute-done((bf16[64,3584]{1,0:T(8,128)(2,1)S(1)}, bf16[64,3584]{1,0:T(8,128)(2,1)S(1)}, u32[]{:S(2)}, u32[]{:S(2)}) %collective-permute-start.26) | collective-permute-done | bytes 458784 | tf_op jit(solution)/shard_map/ppermute | solution.py:79
  85.4 1.5 %collective-permute-start.31 = (bf16[64,3584]{1,0:T(8,128)(2,1)S(1)}, bf16[64,3584]{1,0:T(8,128)(2,1)S(1)}, u32[]{:S(2)}, u32[]{:S(2)}) collective-permute-start(bf16[64,3584]{1,0:T(8,128)(2,1)S(1)} %collective-permute-done.28.refs_1_), channel_id=1, source_target_pairs={{0,2},{1,3},{4,0},{5,1},{8,4},{9,5},{12,8},{13,9},{14,12},{15,13},... | collective-permute-start | bytes 1376264 | tf_op jit(solution)/shard_map/ppermute | solution.py:79
  88.5 7.0 %collective-permute-done.27.refs_0_ = bf16[64,3584]{1,0:T(8,128)(2,1)S(1)} collective-permute-done((bf16[64,3584]{1,0:T(8,128)(2,1)S(1)}, bf16[64,3584]{1,0:T(8,128)(2,1)S(1)}, u32[]{:S(2)}, u32[]{:S(2)}) %collective-permute-start.27) | collective-permute-done | bytes 458784 | tf_op jit(solution)/shard_map/ppermute | solution.py:79
  96.1 1.5 %collective-permute-start.35 = (bf16[64,3584]{1,0:T(8,128)(2,1)S(1)}, bf16[64,3584]{1,0:T(8,128)(2,1)S(1)}, u32[]{:S(2)}, u32[]{:S(2)}) collective-permute-start(bf16[64,3584]{1,0:T(8,128)(2,1)S(1)} %collective-permute-done.31.refs_1_), channel_id=1, source_target_pairs={{0,2},{1,3},{4,0},{5,1},{8,4},{9,5},{12,8},{13,9},{14,12},{15,13},... | collective-permute-start | bytes 1376264 | tf_op jit(solution)/shard_map/ppermute | solution.py:79
  98.1 1.3 %place.8 = (bf16[512,3584]{1,0:T(8,128)(2,1)}, bf16[512,3584]{1,0:T(8,128)(2,1)}) custom-call(bf16[64,3584]{1,0:T(8,128)(2,1)S(1)} %collective-permute-done.27.refs_0_, bf16[64,3584]{1,0:T(8,128)(2,1)S(1)} %collective-permute-done.31.refs_1_, bf16[64,3584]{1,0:T(8,128)(2,1)S(1)} %collective-permute-done.32.refs_2_, ...), custom_call_target="tpu_custom_call", output_to_operand_aliasing={{0}: (4, {}), {1}: (5, {})} | custom-call | bytes 3670016 | tf_op jit(solution)/shard_map/place/pallas_call | solution.py:369
  99.4 6.8 %collective-permute-done.30.refs_0_ = bf16[64,3584]{1,0:T(8,128)(2,1)S(1)} collective-permute-done((bf16[64,3584]{1,0:T(8,128)(2,1)S(1)}, bf16[64,3584]{1,0:T(8,128)(2,1)S(1)}, u32[]{:S(2)}, u32[]{:S(2)}) %collective-permute-start.30) | collective-permute-done | bytes 458784 | tf_op jit(solution)/shard_map/ppermute | solution.py:79
  106.7 1.6 %collective-permute-start.41 = (bf16[64,1792]{1,0:T(8,128)(2,1)S(1)}, bf16[64,1792]{1,0:T(8,128)(2,1)S(1)}, u32[]{:S(2)}, u32[]{:S(2)}) collective-permute-start(bf16[64,1792]{1,0:T(8,128)(2,1)S(1)} %slice.135), channel_id=1, source_target_pairs={{0,2},{1,3},{4,0},{5,1},{8,4},{9,5},{12,8},{13,9},{14,12},{15,13},... | collective-permute-start | bytes 688136 | tf_op jit(solution)/shard_map/ppermute | solution.py:79
  108.8 1.3 %place.9 = (bf16[512,3584]{1,0:T(8,128)(2,1)}, bf16[512,3584]{1,0:T(8,128)(2,1)}) custom-call(bf16[64,3584]{1,0:T(8,128)(2,1)S(1)} %collective-permute-done.30.refs_0_, bf16[64,3584]{1,0:T(8,128)(2,1)S(1)} %collective-permute-done.35.refs_1_, bf16[64,3584]{1,0:T(8,128)(2,1)S(1)} %collective-permute-done.38.refs_2_, ...), custom_call_target="tpu_custom_call", output_to_operand_aliasing={{0}: (4, {}), {1}: (5, {})} | custom-call | bytes 3670016 | tf_op jit(solution)/shard_map/place/pallas_call | solution.py:369
  110.1 2.1 %collective-permute-done.37.refs_0_ = bf16[64,1792]{1,0:T(8,128)(2,1)S(1)} collective-permute-done((bf16[64,1792]{1,0:T(8,128)(2,1)S(1)}, bf16[64,1792]{1,0:T(8,128)(2,1)S(1)}, u32[]{:S(2)}, u32[]{:S(2)}) %collective-permute-start.37) | collective-permute-done | bytes 229408 | tf_op jit(solution)/shard_map/ppermute | solution.py:79
  (111 shorter events, 25.4 us)
Async XLA Ops:
  1.4 10.7 %collective-permute-start.2 = (s32[1,48]{1,0:T(1,128)S(1)}, s32[1,48]{1,0:T(1,128)S(1)}, u32[]{:S(2)}, u32[]{:S(2)}) collective-permute-start(s32[1,48]{1,0:T(1,128)S(1)} %pad_add_fusion.1), channel_id=1, source_target_pairs={{0,3},{1,2},{2,1},{3,0},{4,7},{5,6},{6,5},{7,4},{8,11},{9,10},{10,... | collective-permute-start | bytes 584 | tf_op jit(solution)/shard_map/ppermute | solution.py:37
  3.9 8.3 %collective-permute-start.1 = (s32[1,48]{1,0:T(1,128)S(1)}, s32[1,48]{1,0:T(1,128)S(1)}, u32[]{:S(2)}, u32[]{:S(2)}) collective-permute-start(s32[1,48]{1,0:T(1,128)S(1)} %pad_add_fusion.1), channel_id=1, source_target_pairs={{0,2},{1,3},{2,0},{3,1},{4,6},{5,7},{6,4},{7,5},{8,10},{9,11},{10,... | collective-permute-start | bytes 584 | tf_op jit(solution)/shard_map/ppermute | solution.py:37
  4.6 7.6 %collective-permute-start = (s32[1,48]{1,0:T(1,128)S(1)}, s32[1,48]{1,0:T(1,128)S(1)}, u32[]{:S(2)}, u32[]{:S(2)}) collective-permute-start(s32[1,48]{1,0:T(1,128)S(1)} %pad_add_fusion.1), channel_id=1, source_target_pairs={{0,1},{1,0},{2,3},{3,2},{4,5},{5,4},{6,7},{7,6},{8,9},{9,8},{10,11... | collective-permute-start | bytes 584 | tf_op jit(solution)/shard_map/ppermute | solution.py:37
  12.2 14.0 %collective-permute-start.7 = (bf16[128,3584]{1,0:T(8,128)(2,1)S(1)}, bf16[128,3584]{1,0:T(8,128)(2,1)S(1)}, u32[]{:S(2)}, u32[]{:S(2)}) collective-permute-start(bf16[128,3584]{1,0:T(8,128)(2,1)S(1)} %get-tuple-element.81), channel_id=1, source_target_pairs={{0,1},{1,0},{2,3},{3,2},{4,5},{5,4},{6,7},{7,6},{8,9},{9,8},{10,11... | collective-permute-start | bytes 2752520 | tf_op jit(solution)/shard_map/ppermute | solution.py:37
  26.3 9.3 %collective-permute-start.12 = (bf16[32,1792]{1,0:T(8,128)(2,1)S(1)}, bf16[32,1792]{1,0:T(8,128)(2,1)S(1)}, u32[]{:S(2)}, u32[]{:S(2)}) collective-permute-start(bf16[32,1792]{1,0:T(8,128)(2,1)S(1)} %get-tuple-element.162), channel_id=1, source_target_pairs={{0,2},{1,3},{4,0},{5,1},{8,4},{9,5},{12,8},{13,9},{14,12},{15,13},... | collective-permute-start | bytes 344072 | tf_op jit(solution)/shard_map/ppermute | solution.py:79
  27.9 7.7 %collective-permute-start.11 = (bf16[32,1792]{1,0:T(8,128)(2,1)S(1)}, bf16[32,1792]{1,0:T(8,128)(2,1)S(1)}, u32[]{:S(2)}, u32[]{:S(2)}) collective-permute-start(bf16[32,1792]{1,0:T(8,128)(2,1)S(1)} %get-tuple-element.163), channel_id=1, source_target_pairs={{0,4},{1,5},{4,8},{5,9},{8,12},{9,13},{12,14},{13,15},{14,10},{15,... | collective-permute-start | bytes 344072 | tf_op jit(solution)/shard_map/ppermute | solution.py:79
  35.6 13.7 %collective-permute-start.10 = (bf16[128,3584]{1,0:T(8,128)(2,1)S(1)}, bf16[128,3584]{1,0:T(8,128)(2,1)S(1)}, u32[]{:S(2)}, u32[]{:S(2)}) collective-permute-start(bf16[128,3584]{1,0:T(8,128)(2,1)S(1)} %get-tuple-element.92), channel_id=1, source_target_pairs={{0,1},{1,0},{2,3},{3,2},{4,5},{5,4},{6,7},{7,6},{8,9},{9,8},{10,11... | collective-permute-start | bytes 2752520 | tf_op jit(solution)/shard_map/ppermute | solution.py:37
  35.8 8.5 %collective-permute-start.16 = (bf16[32,3584]{1,0:T(8,128)(2,1)S(1)}, bf16[32,3584]{1,0:T(8,128)(2,1)S(1)}, u32[]{:S(2)}, u32[]{:S(2)}) collective-permute-start(bf16[32,3584]{1,0:T(8,128)(2,1)S(1)} %get-tuple-element.158), channel_id=1, source_target_pairs={{0,2},{1,3},{4,0},{5,1},{8,4},{9,5},{12,8},{13,9},{14,12},{15,13},... | collective-permute-start | bytes 688136 | tf_op jit(solution)/shard_map/ppermute | solution.py:79
  36.7 8.4 %collective-permute-start.15 = (bf16[32,3584]{1,0:T(8,128)(2,1)S(1)}, bf16[32,3584]{1,0:T(8,128)(2,1)S(1)}, u32[]{:S(2)}, u32[]{:S(2)}) collective-permute-start(bf16[32,3584]{1,0:T(8,128)(2,1)S(1)} %get-tuple-element.159), channel_id=1, source_target_pairs={{0,4},{1,5},{4,8},{5,9},{8,12},{9,13},{12,14},{13,15},{14,10},{15,... | collective-permute-start | bytes 688136 | tf_op jit(solution)/shard_map/ppermute | solution.py:79
  38.0 11.1 %collective-permute-start.14 = (bf16[32,3584]{1,0:T(8,128)(2,1)S(1)}, bf16[32,3584]{1,0:T(8,128)(2,1)S(1)}, u32[]{:S(2)}, u32[]{:S(2)}) collective-permute-start(bf16[32,3584]{1,0:T(8,128)(2,1)S(1)} %get-tuple-element.156), channel_id=1, source_target_pairs={{0,2},{1,3},{4,0},{5,1},{8,4},{9,5},{12,8},{13,9},{14,12},{15,13},... | collective-permute-start | bytes 688136 | tf_op jit(solution)/shard_map/ppermute | solution.py:79
  38.9 10.4 %collective-permute-start.13 = (bf16[32,3584]{1,0:T(8,128)(2,1)S(1)}, bf16[32,3584]{1,0:T(8,128)(2,1)S(1)}, u32[]{:S(2)}, u32[]{:S(2)}) collective-permute-start(bf16[32,3584]{1,0:T(8,128)(2,1)S(1)} %get-tuple-element.157), channel_id=1, source_target_pairs={{0,4},{1,5},{4,8},{5,9},{8,12},{9,13},{12,14},{13,15},{14,10},{15,... | collective-permute-start | bytes 688136 | tf_op jit(solution)/shard_map/ppermute | solution.py:79
  45.2 8.9 %collective-permute-start.21 = (bf16[32,3584]{1,0:T(8,128)(2,1)S(1)}, bf16[32,3584]{1,0:T(8,128)(2,1)S(1)}, u32[]{:S(2)}, u32[]{:S(2)}) collective-permute-start(bf16[32,3584]{1,0:T(8,128)(2,1)S(1)} %add_convert_fusion.6), channel_id=1, source_target_pairs={{0,2},{1,3},{4,0},{5,1},{8,4},{9,5},{12,8},{13,9},{14,12},{15,13},... | collective-permute-start | bytes 688136 | tf_op jit(solution)/shard_map/ppermute | solution.py:79
  47.1 8.5 %collective-permute-start.20 = (bf16[32,3584]{1,0:T(8,128)(2,1)S(1)}, bf16[32,3584]{1,0:T(8,128)(2,1)S(1)}, u32[]{:S(2)}, u32[]{:S(2)}) collective-permute-start(bf16[32,3584]{1,0:T(8,128)(2,1)S(1)} %add_convert_fusion.7), channel_id=1, source_target_pairs={{0,4},{1,5},{4,8},{5,9},{8,12},{9,13},{12,14},{13,15},{14,10},{15,... | collective-permute-start | bytes 688136 | tf_op jit(solution)/shard_map/ppermute | solution.py:79
  49.4 11.1 %collective-permute-start.18 = (bf16[32,3584]{1,0:T(8,128)(2,1)S(1)}, bf16[32,3584]{1,0:T(8,128)(2,1)S(1)}, u32[]{:S(2)}, u32[]{:S(2)}) collective-permute-start(bf16[32,3584]{1,0:T(8,128)(2,1)S(1)} %add_convert_fusion.5), channel_id=1, source_target_pairs={{0,4},{1,5},{4,8},{5,9},{8,12},{9,13},{12,14},{13,15},{14,10},{15,... | collective-permute-start | bytes 688136 | tf_op jit(solution)/shard_map/ppermute | solution.py:79
  51.0 9.5 %collective-permute-start.19 = (bf16[32,3584]{1,0:T(8,128)(2,1)S(1)}, bf16[32,3584]{1,0:T(8,128)(2,1)S(1)}, u32[]{:S(2)}, u32[]{:S(2)}) collective-permute-start(bf16[32,3584]{1,0:T(8,128)(2,1)S(1)} %add_convert_fusion.4), channel_id=1, source_target_pairs={{0,2},{1,3},{4,0},{5,1},{8,4},{9,5},{12,8},{13,9},{14,12},{15,13},... | collective-permute-start | bytes 688136 | tf_op jit(solution)/shard_map/ppermute | solution.py:79
  55.8 7.7 %collective-permute-start.23 = (bf16[32,3584]{1,0:T(8,128)(2,1)S(1)}, bf16[32,3584]{1,0:T(8,128)(2,1)S(1)}, u32[]{:S(2)}, u32[]{:S(2)}) collective-permute-start(bf16[32,3584]{1,0:T(8,128)(2,1)S(1)} %get-tuple-element.154), channel_id=1, source_target_pairs={{0,2},{1,3},{4,0},{5,1},{8,4},{9,5},{12,8},{13,9},{14,12},{15,13},... | collective-permute-start | bytes 688136 | tf_op jit(solution)/shard_map/ppermute | solution.py:79
  56.7 7.8 %collective-permute-start.22 = (bf16[32,3584]{1,0:T(8,128)(2,1)S(1)}, bf16[32,3584]{1,0:T(8,128)(2,1)S(1)}, u32[]{:S(2)}, u32[]{:S(2)}) collective-permute-start(bf16[32,3584]{1,0:T(8,128)(2,1)S(1)} %get-tuple-element.155), channel_id=1, source_target_pairs={{0,4},{1,5},{4,8},{5,9},{8,12},{9,13},{12,14},{13,15},{14,10},{15,... | collective-permute-start | bytes 688136 | tf_op jit(solution)/shard_map/ppermute | solution.py:79
  64.6 6.7 %collective-permute-start.25 = (bf16[32,3584]{1,0:T(8,128)(2,1)S(1)}, bf16[32,3584]{1,0:T(8,128)(2,1)S(1)}, u32[]{:S(2)}, u32[]{:S(2)}) collective-permute-start(bf16[32,3584]{1,0:T(8,128)(2,1)S(1)} %get-tuple-element.152), channel_id=1, source_target_pairs={{0,2},{1,3},{4,0},{5,1},{8,4},{9,5},{12,8},{13,9},{14,12},{15,13},... | collective-permute-start | bytes 688136 | tf_op jit(solution)/shard_map/ppermute | solution.py:79
  66.0 6.4 %collective-permute-start.24 = (bf16[32,3584]{1,0:T(8,128)(2,1)S(1)}, bf16[32,3584]{1,0:T(8,128)(2,1)S(1)}, u32[]{:S(2)}, u32[]{:S(2)}) collective-permute-start(bf16[32,3584]{1,0:T(8,128)(2,1)S(1)} %get-tuple-element.153), channel_id=1, source_target_pairs={{0,4},{1,5},{4,8},{5,9},{8,12},{9,13},{12,14},{13,15},{14,10},{15,... | collective-permute-start | bytes 688136 | tf_op jit(solution)/shard_map/ppermute | solution.py:79
  74.1 10.7 %collective-permute-start.26 = (bf16[64,3584]{1,0:T(8,128)(2,1)S(1)}, bf16[64,3584]{1,0:T(8,128)(2,1)S(1)}, u32[]{:S(2)}, u32[]{:S(2)}) collective-permute-start(bf16[64,3584]{1,0:T(8,128)(2,1)S(1)} %bitcast.6), channel_id=1, source_target_pairs={{0,4},{1,5},{4,8},{5,9},{8,12},{9,13},{12,14},{13,15},{14,10},{15,... | collective-permute-start | bytes 1376264 | tf_op jit(solution)/shard_map/ppermute | solution.py:79
  74.7 10.7 %collective-permute-start.28 = (bf16[64,3584]{1,0:T(8,128)(2,1)S(1)}, bf16[64,3584]{1,0:T(8,128)(2,1)S(1)}, u32[]{:S(2)}, u32[]{:S(2)}) collective-permute-start(bf16[64,3584]{1,0:T(8,128)(2,1)S(1)} %bitcast.7), channel_id=1, source_target_pairs={{0,2},{1,3},{4,0},{5,1},{8,4},{9,5},{12,8},{13,9},{14,12},{15,13},... | collective-permute-start | bytes 1376264 | tf_op jit(solution)/shard_map/ppermute | solution.py:79
  78.8 8.6 %collective-permute-start.29 = (bf16[64,3584]{1,0:T(8,128)(2,1)S(1)}, bf16[64,3584]{1,0:T(8,128)(2,1)S(1)}, u32[]{:S(2)}, u32[]{:S(2)}) collective-permute-start(bf16[64,3584]{1,0:T(8,128)(2,1)S(1)} %bitcast.8), channel_id=1, source_target_pairs={{0,1},{1,0},{2,3},{3,2},{4,5},{5,4},{6,7},{7,6},{8,9},{9,8},{10,11... | collective-permute-start | bytes 1376264 | tf_op jit(solution)/shard_map/ppermute | solution.py:37
  84.8 10.7 %collective-permute-start.27 = (bf16[64,3584]{1,0:T(8,128)(2,1)S(1)}, bf16[64,3584]{1,0:T(8,128)(2,1)S(1)}, u32[]{:S(2)}, u32[]{:S(2)}) collective-permute-start(bf16[64,3584]{1,0:T(8,128)(2,1)S(1)} %collective-permute-done.26.refs_0_), channel_id=1, source_target_pairs={{0,4},{1,5},{4,8},{5,9},{8,12},{9,13},{12,14},{13,15},{14,10},{15,... | collective-permute-start | bytes 1376264 | tf_op jit(solution)/shard_map/ppermute | solution.py:79
  85.4 10.7 %collective-permute-start.31 = (bf16[64,3584]{1,0:T(8,128)(2,1)S(1)}, bf16[64,3584]{1,0:T(8,128)(2,1)S(1)}, u32[]{:S(2)}, u32[]{:S(2)}) collective-permute-start(bf16[64,3584]{1,0:T(8,128)(2,1)S(1)} %collective-permute-done.28.refs_1_), channel_id=1, source_target_pairs={{0,2},{1,3},{4,0},{5,1},{8,4},{9,5},{12,8},{13,9},{14,12},{15,13},... | collective-permute-start | bytes 1376264 | tf_op jit(solution)/shard_map/ppermute | solution.py:79
  86.9 10.7 %collective-permute-start.33 = (bf16[64,3584]{1,0:T(8,128)(2,1)S(1)}, bf16[64,3584]{1,0:T(8,128)(2,1)S(1)}, u32[]{:S(2)}, u32[]{:S(2)}) collective-permute-start(bf16[64,3584]{1,0:T(8,128)(2,1)S(1)} %collective-permute-done.28.refs_1_), channel_id=1, source_target_pairs={{0,1},{1,0},{2,3},{3,2},{4,5},{5,4},{6,7},{7,6},{8,9},{9,8},{10,11... | collective-permute-start | bytes 1376264 | tf_op jit(solution)/shard_map/ppermute | solution.py:37
  86.9 11.2 %collective-permute-start.32 = (bf16[64,3584]{1,0:T(8,128)(2,1)S(1)}, bf16[64,3584]{1,0:T(8,128)(2,1)S(1)}, u32[]{:S(2)}, u32[]{:S(2)}) collective-permute-start(bf16[64,3584]{1,0:T(8,128)(2,1)S(1)} %collective-permute-done.26.refs_0_), channel_id=1, source_target_pairs={{0,1},{1,0},{2,3},{3,2},{4,5},{5,4},{6,7},{7,6},{8,9},{9,8},{10,11... | collective-permute-start | bytes 1376264 | tf_op jit(solution)/shard_map/ppermute | solution.py:37
  95.5 10.6 %collective-permute-start.30 = (bf16[64,3584]{1,0:T(8,128)(2,1)S(1)}, bf16[64,3584]{1,0:T(8,128)(2,1)S(1)}, u32[]{:S(2)}, u32[]{:S(2)}) collective-permute-start(bf16[64,3584]{1,0:T(8,128)(2,1)S(1)} %collective-permute-done.27.refs_0_), channel_id=1, source_target_pairs={{0,4},{1,5},{4,8},{5,9},{8,12},{9,13},{12,14},{13,15},{14,10},{15,... | collective-permute-start | bytes 1376264 | tf_op jit(solution)/shard_map/ppermute | solution.py:79
  96.1 10.6 %collective-permute-start.35 = (bf16[64,3584]{1,0:T(8,128)(2,1)S(1)}, bf16[64,3584]{1,0:T(8,128)(2,1)S(1)}, u32[]{:S(2)}, u32[]{:S(2)}) collective-permute-start(bf16[64,3584]{1,0:T(8,128)(2,1)S(1)} %collective-permute-done.31.refs_1_), channel_id=1, source_target_pairs={{0,2},{1,3},{4,0},{5,1},{8,4},{9,5},{12,8},{13,9},{14,12},{15,13},... | collective-permute-start | bytes 1376264 | tf_op jit(solution)/shard_map/ppermute | solution.py:79
  97.6 10.8 %collective-permute-start.39 = (bf16[64,3584]{1,0:T(8,128)(2,1)S(1)}, bf16[64,3584]{1,0:T(8,128)(2,1)S(1)}, u32[]{:S(2)}, u32[]{:S(2)}) collective-permute-start(bf16[64,3584]{1,0:T(8,128)(2,1)S(1)} %collective-permute-done.31.refs_1_), channel_id=1, source_target_pairs={{0,1},{1,0},{2,3},{3,2},{4,5},{5,4},{6,7},{7,6},{8,9},{9,8},{10,11... | collective-permute-start | bytes 1376264 | tf_op jit(solution)/shard_map/ppermute | solution.py:37
  97.6 11.3 %collective-permute-start.38 = (bf16[64,3584]{1,0:T(8,128)(2,1)S(1)}, bf16[64,3584]{1,0:T(8,128)(2,1)S(1)}, u32[]{:S(2)}, u32[]{:S(2)}) collective-permute-start(bf16[64,3584]{1,0:T(8,128)(2,1)S(1)} %collective-permute-done.27.refs_0_), channel_id=1, source_target_pairs={{0,1},{1,0},{2,3},{3,2},{4,5},{5,4},{6,7},{7,6},{8,9},{9,8},{10,11... | collective-permute-start | bytes 1376264 | tf_op jit(solution)/shard_map/ppermute | solution.py:37
  106.2 6.1 %collective-permute-start.37 = (bf16[64,1792]{1,0:T(8,128)(2,1)S(1)}, bf16[64,1792]{1,0:T(8,128)(2,1)S(1)}, u32[]{:S(2)}, u32[]{:S(2)}) collective-permute-start(bf16[64,1792]{1,0:T(8,128)(2,1)S(1)} %slice.134), channel_id=1, source_target_pairs={{0,4},{1,5},{4,8},{5,9},{8,12},{9,13},{12,14},{13,15},{14,10},{15,... | collective-permute-start | bytes 688136 | tf_op jit(solution)/shard_map/ppermute | solution.py:79
  106.7 6.1 %collective-permute-start.41 = (bf16[64,1792]{1,0:T(8,128)(2,1)S(1)}, bf16[64,1792]{1,0:T(8,128)(2,1)S(1)}, u32[]{:S(2)}, u32[]{:S(2)}) collective-permute-start(bf16[64,1792]{1,0:T(8,128)(2,1)S(1)} %slice.135), channel_id=1, source_target_pairs={{0,2},{1,3},{4,0},{5,1},{8,4},{9,5},{12,8},{13,9},{14,12},{15,13},... | collective-permute-start | bytes 688136 | tf_op jit(solution)/shard_map/ppermute | solution.py:79
  (25 other events, 323.3 us)

commit v16 on v13

--- a/solution.py
+++ b/solution.py
@@ -80,15 +80,21 @@
 
 
 def gather_table(row, size):
-    stages, step = [], 1
+    stages, step = [], 4
     pieces = [row]
     while step < size:
-        if step > 1:
-            pieces = [jnp.concatenate(pieces, axis=0)]
+        pieces = [row if len(pieces) == 1 else jnp.concatenate(pieces, axis=0)]
         pieces += [swap(pieces[0], step * k, size) for k in range(1, min(4, size // step))]
         stages.append(pieces)
         step *= len(pieces)
+    table = jnp.concatenate(pieces, axis=0)
+    stages.append([table] + [swap(table, k, size) for k in range(1, 4)])
     return stages
+
+
+def table_key(row, size):
+    height = size // 4
+    return 4 * (row % height) + row // height
 
 
 def ordered_rows(size, rows, by_latent, groups):
@@ -107,7 +113,7 @@
     me = lax.axis_index("latent")
     counts = table[:, :size]
     order = table[:, size:]
-    source = me ^ lax.broadcasted_iota(jnp.int32, (size, 1), 0)
+    source = me ^ table_key(lax.broadcasted_iota(jnp.int32, (size, 1), 0), size)
     before = jnp.sum(jnp.where(source < me, counts, 0), axis=0, keepdims=True)
     total = jnp.sum(counts, axis=0, keepdims=True)
     owners = lax.broadcasted_iota(jnp.int32, (size, size), 1) == source
@@ -123,7 +129,7 @@
         token = jnp.where(own, by_key(picks_ref[c : c + 1]), token)
     token = jnp.where(place < by_key(total), token, KEPT)
     latent = lax.broadcasted_iota(jnp.int32, (size * rows, 1), 0)
-    keys = lax.broadcasted_iota(jnp.int32, (size * rows, size), 1)
+    keys = table_key(lax.broadcasted_iota(jnp.int32, (size * rows, size), 1), size)
     spread = (keys == (me ^ (latent // rows))).astype(jnp.float32)
 
     def by_row(values):

time: 113 us -> 113 us (level)
    ppermute x16, waiting for transfers between devices: 44.8 us -> 46.2 us  [shift(): return lax.ppermute(value, 'latent', pairs)]
  transfers between devices with their start and end apart: 35 -> 35, of which waited for: 19 -> 16; matrix products, arithmetic and copies ran while one was open for 1% -> 1% of each run, Pallas kernels for 25% -> 25%
where the time goes in v16:
time: 113 us
  waiting for transfers between devices  52.4 us (46%)
  Pallas kernels  30.5 us (27%)
  starting transfers between devices  26.8 us (24%)
  other arithmetic  2.08 us (2%)
    ppermute x16, waiting for transfers between devices, shift(): return lax.ppermute(value, 'latent', pairs)  46.2 us
    ppermute x16, starting transfers between devices, shift(): return lax.ppermute(value, 'latent', pairs)  16.7 us
    pallas_call x3, Pallas kernels, product(): pl.pallas_call(kernel, grid=(width // tile,), in_specs=in_specs + [pl.Blo...  12.4 us
    ppermute x19, starting transfers between devices, swap(): return lax.ppermute(value, 'latent', [(i, i ^ bits) for i in range(size)])  10.1 us
    pallas_call x1, Pallas kernels, stream_far_product(): pl.pallas_call(functools.partial(stream_kernel, size, rows), in_specs=[an...  7.57 us
    pallas_call x6, Pallas kernels, place(): pl.pallas_call(functools.partial(place_kernel, plan, size, rows, count),...  6.39 us
    ppermute x19, waiting for transfers between devices, swap(): return lax.ppermute(value, 'latent', [(i, i ^ bits) for i in range(size)])  6.16 us
    pallas_call x2, Pallas kernels, update(): pl.pallas_call(blocks_kernel if blocks_only else states_kernel, grid=(row...  4.18 us
  transfers between devices with their start and end apart: 35, of which 16 were waited for; matrix products, arithmetic and copies ran while one was open for 1% of the time, Pallas kernels for 25%

profile of v16, /device:TPU:0, one launch (start us, length us, event | category | flops | bytes accessed | tf_op | source)
XLA Modules:
  0.0 112.9 jit_solution(12869901864221887099)
XLA Ops:
  1.4 5.1 %collective-permute-start.2 = (s32[1,48]{1,0:T(1,128)S(1)}, s32[1,48]{1,0:T(1,128)S(1)}, u32[]{:S(2)}, u32[]{:S(2)}) collective-permute-start(s32[1,48]{1,0:T(1,128)S(1)} %pad_add_fusion.1), channel_id=1, source_target_pairs={{0,12},{1,13},{2,14},{3,15},{4,8},{5,9},{6,10},{7,11},{8,4},{9,5},... | collective-permute-start | bytes 584 | tf_op jit(solution)/shard_map/ppermute | solution.py:37
  7.2 7.6 %stream_far_product.1 = (bf16[128,3584]{1,0:T(8,128)(2,1)S(1)}, bf16[128,3584]{1,0:T(8,128)(2,1)}, bf16[256,1024]{1,0:T(8,128)(2,1)S(1)}) custom-call(bf16[1024,512]{1,0:T(8,128)(2,1)} %coef_hbm.1, bf16[1024,3584]{1,0:T(8,128)(2,1)} %right_ref.5), custom_call_target="tpu_custom_call" | custom-call | flops 1879048192 | bytes 10223616 | tf_op jit(solution)/shard_map/stream_far_product/pallas_call | solution.py:193
  15.0 1.7 %collective-permute-start.5 = (s32[4,48]{1,0:T(4,128)S(1)}, s32[4,48]{1,0:T(4,128)S(1)}, u32[]{:S(2)}, u32[]{:S(2)}) collective-permute-start(s32[4,48]{1,0:T(4,128)S(1)} %pad_add_fusion.refs_0_), channel_id=1, source_target_pairs={{0,3},{1,2},{2,1},{3,0},{4,7},{5,6},{6,5},{7,4},{8,11},{9,10},{10,... | collective-permute-start | bytes 2312 | tf_op jit(solution)/shard_map/ppermute | solution.py:37
  17.1 0.9 collective-permute-done.5.refs_3_
  18.1 2.3 %collective-permute-done.4.refs_2_ = s32[4,48]{1,0:T(4,128)S(1)} collective-permute-done((s32[4,48]{1,0:T(4,128)S(1)}, s32[4,48]{1,0:T(4,128)S(1)}, u32[]{:S(2)}, u32[]{:S(2)}) %collective-permute-start.4) | collective-permute-done | bytes 800 | tf_op jit(solution)/shard_map/ppermute | solution.py:37
  20.4 4.9 %far_product.1 = (bf16[128,3584]{1,0:T(8,128)(2,1)S(1)}, bf16[128,3584]{1,0:T(8,128)(2,1)S(1)}, bf16[256,1024]{1,0:T(8,128)(2,1)S(1)}, s32[32,1]{1,0:T(8,128)S(1)}) custom-call(bf16[1024,512]{1,0:T(8,128)(2,1)S(1)} %copy-done.7, bf16[1024,3584]{1,0:T(8,128)(2,1)S(1)} %copy-done.6, s32[2,16]{1,0:T(2,128)S(1)} %bitcast.10, s32[4,48]{1,0:T(4,128)S(1)} %pad_add_fusion.refs_0_, ...), custom_call_target="tpu_custom_call" | custom-call | flops 5637144576 | bytes 9699328 | tf_op jit(solution)/shard_map/far_product/pallas_call | solution.py:257
  25.6 2.2 %collective-permute-done.6 = bf16[128,3584]{1,0:T(8,128)(2,1)S(1)} collective-permute-done((bf16[128,3584]{1,0:T(8,128)(2,1)S(1)}, bf16[128,3584]{1,0:T(8,128)(2,1)S(1)}, u32[]{:S(2)}, u32[]{:S(2)}) %collective-permute-start.6) | collective-permute-done | bytes 917536 | tf_op jit(solution)/shard_map/ppermute | solution.py:37
  28.5 1.7 %collective-permute-start.8 = (bf16[64,1792]{1,0:T(8,128)(2,1)S(1)}, bf16[64,1792]{1,0:T(8,128)(2,1)S(1)}, u32[]{:S(2)}, u32[]{:S(2)}) collective-permute-start(bf16[64,1792]{1,0:T(8,128)(2,1)S(1)} %get-tuple-element.141), channel_id=1, source_target_pairs={{0,4},{1,5},{4,8},{5,9},{8,12},{9,13},{12,14},{13,15},{14,10},{15,... | collective-permute-start | bytes 688136 | tf_op jit(solution)/shard_map/ppermute | solution.py:79
  30.2 3.7 %near_product.2 = (bf16[128,3584]{1,0:T(8,128)(2,1)S(1)}, bf16[128,3584]{1,0:T(8,128)(2,1)S(1)}) custom-call(bf16[256,1024]{1,0:T(8,128)(2,1)S(1)} %get-tuple-element.75.left_ref, bf16[1024,3584]{1,0:T(8,128)(2,1)S(1)} %copy-done.6), custom_call_target="tpu_custom_call" | custom-call | flops 5637144576 | bytes 9699328 | tf_op jit(solution)/shard_map/near_product/pallas_call | solution.py:257
  33.9 1.9 %collective-permute-done.9 = bf16[64,1792]{1,0:T(8,128)(2,1)S(1)} collective-permute-done((bf16[64,1792]{1,0:T(8,128)(2,1)S(1)}, bf16[64,1792]{1,0:T(8,128)(2,1)S(1)}, u32[]{:S(2)}, u32[]{:S(2)}) %collective-permute-start.9) | collective-permute-done | bytes 229408 | tf_op jit(solution)/shard_map/ppermute | solution.py:79
  36.0 1.7 %collective-permute-start.11 = (bf16[64,3584]{1,0:T(8,128)(2,1)S(1)}, bf16[64,3584]{1,0:T(8,128)(2,1)S(1)}, u32[]{:S(2)}, u32[]{:S(2)}) collective-permute-start(bf16[64,3584]{1,0:T(8,128)(2,1)S(1)} %fusion), channel_id=1, source_target_pairs={{0,4},{1,5},{4,8},{5,9},{8,12},{9,13},{12,14},{13,15},{14,10},{15,... | collective-permute-start | bytes 1376264 | tf_op jit(solution)/shard_map/ppermute | solution.py:79
  38.2 3.7 %near_product.3 = (bf16[128,3584]{1,0:T(8,128)(2,1)S(1)}, bf16[128,3584]{1,0:T(8,128)(2,1)S(1)}) custom-call(bf16[256,1024]{1,0:T(8,128)(2,1)S(1)} %get-tuple-element.82.left_ref, bf16[1024,3584]{1,0:T(8,128)(2,1)S(1)} %bitcast.5), custom_call_target="tpu_custom_call" | custom-call | flops 5637144576 | bytes 9699328 | tf_op jit(solution)/shard_map/near_product/pallas_call | solution.py:257
  42.5 6.6 %collective-permute-done.15 = bf16[64,3584]{1,0:T(8,128)(2,1)S(1)} collective-permute-done((bf16[64,3584]{1,0:T(8,128)(2,1)S(1)}, bf16[64,3584]{1,0:T(8,128)(2,1)S(1)}, u32[]{:S(2)}, u32[]{:S(2)}) %collective-permute-start.15) | collective-permute-done | bytes 458784 | tf_op jit(solution)/shard_map/ppermute | solution.py:79
  50.2 1.6 %collective-permute-start.13 = (bf16[64,3584]{1,0:T(8,128)(2,1)S(1)}, bf16[64,3584]{1,0:T(8,128)(2,1)S(1)}, u32[]{:S(2)}, u32[]{:S(2)}) collective-permute-start(bf16[64,3584]{1,0:T(8,128)(2,1)S(1)} %fusion.2), channel_id=1, source_target_pairs={{0,4},{1,5},{4,8},{5,9},{8,12},{9,13},{12,14},{13,15},{14,10},{15,... | collective-permute-start | bytes 1376264 | tf_op jit(solution)/shard_map/ppermute | solution.py:79
  51.8 8.2 %collective-permute-done.16 = bf16[64,3584]{1,0:T(8,128)(2,1)S(1)} collective-permute-done((bf16[64,3584]{1,0:T(8,128)(2,1)S(1)}, bf16[64,3584]{1,0:T(8,128)(2,1)S(1)}, u32[]{:S(2)}, u32[]{:S(2)}) %collective-permute-start.16) | collective-permute-done | bytes 458784 | tf_op jit(solution)/shard_map/ppermute | solution.py:79
  60.5 2.0 %collective-permute-start.14 = (bf16[64,3584]{1,0:T(8,128)(2,1)S(1)}, bf16[64,3584]{1,0:T(8,128)(2,1)S(1)}, u32[]{:S(2)}, u32[]{:S(2)}) collective-permute-start(bf16[64,3584]{1,0:T(8,128)(2,1)S(1)} %fusion.3), channel_id=1, source_target_pairs={{0,4},{1,5},{4,8},{5,9},{8,12},{9,13},{12,14},{13,15},{14,10},{15,... | collective-permute-start | bytes 1376264 | tf_op jit(solution)/shard_map/ppermute | solution.py:79
  62.5 7.6 %collective-permute-done.17.refs_10_.refs_14_ = bf16[64,3584]{1,0:T(8,128)(2,1)S(1)} collective-permute-done((bf16[64,3584]{1,0:T(8,128)(2,1)S(1)}, bf16[64,3584]{1,0:T(8,128)(2,1)S(1)}, u32[]{:S(2)}, u32[]{:S(2)}) %collective-permute-start.17) | collective-permute-done | bytes 458784 | tf_op jit(solution)/shard_map/ppermute | solution.py:79
  70.3 1.6 %blocks.1 = bf16[2,32,3584]{2,1,0:T(8,128)(2,1)S(1)} custom-call(s32[32,1]{1,0:T(8,128)S(1)} %get-tuple-element.70.refs_0_, f32[32,3584]{1,0:T(8,128)S(1)} %copy-done, f32[32,3584]{1,0:T(8,128)S(1)} %copy-done.1, f32[32,3584]{1,0:T(8,128)S(1)} %copy-done.2, f32[32,3584]{1,0:T(8,128)S(1)} %copy-done.3, f32[32,3584]{1,0:T(8,128)S(1)} %copy-done.4, ...), custom_call_target="tpu_custom_call" | custom-call | flops 1146880 | bytes 1146880 | tf_op jit(solution)/shard_map/blocks/pallas_call | solution.py:342
  71.9 2.0 %collective-permute-start.18 = (bf16[64,3584]{1,0:T(8,128)(2,1)S(1)}, bf16[64,3584]{1,0:T(8,128)(2,1)S(1)}, u32[]{:S(2)}, u32[]{:S(2)}) collective-permute-start(bf16[64,3584]{1,0:T(8,128)(2,1)S(1)} %bitcast.6), channel_id=1, source_target_pairs={{0,4},{1,5},{4,8},{5,9},{8,12},{9,13},{12,14},{13,15},{14,10},{15,... | collective-permute-start | bytes 1376264 | tf_op jit(solution)/shard_map/ppermute | solution.py:79
  74.0 2.6 %states.1 = (f32[32,3584]{1,0:T(8,128)}, f32[32,3584]{1,0:T(8,128)}, f32[32,3584]{1,0:T(8,128)}, f32[32,3584]{1,0:T(8,128)}, f32[32,3584]{1,0:T(8,128)}, /*index=5*/f32[32,3584]{1,0:T(8,128)}) custom-call(s32[32,1]{1,0:T(8,128)S(1)} %get-tuple-element.70.refs_0_, f32[32,3584]{1,0:T(8,128)S(1)} %copy-done, f32[32,3584]{1,0:T(8,128)S(1)} %copy-done.1, ...), custom_call_target="tpu_custom_call" | custom-call | flops 1146880 | bytes 1146880 | tf_op jit(solution)/shard_map/states/pallas_call | solution.py:342
  77.3 3.6 %collective-permute-done.18.refs_0_ = bf16[64,3584]{1,0:T(8,128)(2,1)S(1)} collective-permute-done((bf16[64,3584]{1,0:T(8,128)(2,1)S(1)}, bf16[64,3584]{1,0:T(8,128)(2,1)S(1)}, u32[]{:S(2)}, u32[]{:S(2)}) %collective-permute-start.18) | collective-permute-done | bytes 458784 | tf_op jit(solution)/shard_map/ppermute | solution.py:79
  81.0 1.9 %collective-permute-start.19 = (bf16[64,3584]{1,0:T(8,128)(2,1)S(1)}, bf16[64,3584]{1,0:T(8,128)(2,1)S(1)}, u32[]{:S(2)}, u32[]{:S(2)}) collective-permute-start(bf16[64,3584]{1,0:T(8,128)(2,1)S(1)} %collective-permute-done.18.refs_0_), channel_id=1, source_target_pairs={{0,4},{1,5},{4,8},{5,9},{8,12},{9,13},{12,14},{13,15},{14,10},{15,... | collective-permute-start | bytes 1376264 | tf_op jit(solution)/shard_map/ppermute | solution.py:79
  83.5 1.1 place.7
  84.6 7.0 %collective-permute-done.19.refs_0_ = bf16[64,3584]{1,0:T(8,128)(2,1)S(1)} collective-permute-done((bf16[64,3584]{1,0:T(8,128)(2,1)S(1)}, bf16[64,3584]{1,0:T(8,128)(2,1)S(1)}, u32[]{:S(2)}, u32[]{:S(2)}) %collective-permute-start.19) | collective-permute-done | bytes 458784 | tf_op jit(solution)/shard_map/ppermute | solution.py:79
  91.6 1.9 %collective-permute-start.22 = (bf16[64,3584]{1,0:T(8,128)(2,1)S(1)}, bf16[64,3584]{1,0:T(8,128)(2,1)S(1)}, u32[]{:S(2)}, u32[]{:S(2)}) collective-permute-start(bf16[64,3584]{1,0:T(8,128)(2,1)S(1)} %collective-permute-done.19.refs_0_), channel_id=1, source_target_pairs={{0,4},{1,5},{4,8},{5,9},{8,12},{9,13},{12,14},{13,15},{14,10},{15,... | collective-permute-start | bytes 1376264 | tf_op jit(solution)/shard_map/ppermute | solution.py:79
  94.2 1.3 %place.8 = (bf16[512,3584]{1,0:T(8,128)(2,1)}, bf16[512,3584]{1,0:T(8,128)(2,1)}) custom-call(bf16[64,3584]{1,0:T(8,128)(2,1)S(1)} %collective-permute-done.19.refs_0_, bf16[64,3584]{1,0:T(8,128)(2,1)S(1)} %collective-permute-done.23.refs_1_, bf16[64,3584]{1,0:T(8,128)(2,1)S(1)} %collective-permute-done.24.refs_2_, ...), custom_call_target="tpu_custom_call", output_to_operand_aliasing={{0}: (4, {}), {1}: (5, {})} | custom-call | bytes 3670016 | tf_op jit(solution)/shard_map/place/pallas_call | solution.py:377
  95.5 6.8 %collective-permute-done.22.refs_0_ = bf16[64,3584]{1,0:T(8,128)(2,1)S(1)} collective-permute-done((bf16[64,3584]{1,0:T(8,128)(2,1)S(1)}, bf16[64,3584]{1,0:T(8,128)(2,1)S(1)}, u32[]{:S(2)}, u32[]{:S(2)}) %collective-permute-start.22) | collective-permute-done | bytes 458784 | tf_op jit(solution)/shard_map/ppermute | solution.py:79
  102.3 1.9 %collective-permute-start.29 = (bf16[64,1792]{1,0:T(8,128)(2,1)S(1)}, bf16[64,1792]{1,0:T(8,128)(2,1)S(1)}, u32[]{:S(2)}, u32[]{:S(2)}) collective-permute-start(bf16[64,1792]{1,0:T(8,128)(2,1)S(1)} %slice.126), channel_id=1, source_target_pairs={{0,4},{1,5},{4,8},{5,9},{8,12},{9,13},{12,14},{13,15},{14,10},{15,... | collective-permute-start | bytes 688136 | tf_op jit(solution)/shard_map/ppermute | solution.py:79
  104.9 1.3 %place.9 = (bf16[512,3584]{1,0:T(8,128)(2,1)}, bf16[512,3584]{1,0:T(8,128)(2,1)}) custom-call(bf16[64,3584]{1,0:T(8,128)(2,1)S(1)} %collective-permute-done.22.refs_0_, bf16[64,3584]{1,0:T(8,128)(2,1)S(1)} %collective-permute-done.27.refs_1_, bf16[64,3584]{1,0:T(8,128)(2,1)S(1)} %collective-permute-done.30.refs_2_, ...), custom_call_target="tpu_custom_call", output_to_operand_aliasing={{0}: (4, {}), {1}: (5, {})} | custom-call | bytes 3670016 | tf_op jit(solution)/shard_map/place/pallas_call | solution.py:377
  106.2 2.1 %collective-permute-done.29.refs_0_ = bf16[64,1792]{1,0:T(8,128)(2,1)S(1)} collective-permute-done((bf16[64,1792]{1,0:T(8,128)(2,1)S(1)}, bf16[64,1792]{1,0:T(8,128)(2,1)S(1)}, u32[]{:S(2)}, u32[]{:S(2)}) %collective-permute-start.29) | collective-permute-done | bytes 229408 | tf_op jit(solution)/shard_map/ppermute | solution.py:79
  108.4 1.9 %collective-permute-done.33.refs_1_ = bf16[64,1792]{1,0:T(8,128)(2,1)S(1)} collective-permute-done((bf16[64,1792]{1,0:T(8,128)(2,1)S(1)}, bf16[64,1792]{1,0:T(8,128)(2,1)S(1)}, u32[]{:S(2)}, u32[]{:S(2)}) %collective-permute-start.33) | collective-permute-done | bytes 229408 | tf_op jit(solution)/shard_map/ppermute | solution.py:79
  111.8 1.1 %place.11 = (bf16[512,3584]{1,0:T(8,128)(2,1)}, bf16[512,3584]{1,0:T(8,128)(2,1)}) custom-call(bf16[64,3584]{1,0:T(8,128)(2,1)S(1)} %collective-permute-done.26.refs_0_, bf16[64,3584]{1,0:T(8,128)(2,1)S(1)} %collective-permute-done.28.refs_1_, bf16[64,1792]{1,0:T(8,128)(2,1)S(1)} %collective-permute-done.32.refs_2_, ...), custom_call_target="tpu_custom_call", output_to_operand_aliasing={{0}: (4, {}), {1}: (5, {})} | custom-call | bytes 3670016 | tf_op jit(solution)/shard_map/place/pallas_call | solution.py:377
  (94 shorter events, 10.3 us)
Async XLA Ops:
  1.4 13.3 %collective-permute-start.2 = (s32[1,48]{1,0:T(1,128)S(1)}, s32[1,48]{1,0:T(1,128)S(1)}, u32[]{:S(2)}, u32[]{:S(2)}) collective-permute-start(s32[1,48]{1,0:T(1,128)S(1)} %pad_add_fusion.1), channel_id=1, source_target_pairs={{0,12},{1,13},{2,14},{3,15},{4,8},{5,9},{6,10},{7,11},{8,4},{9,5},... | collective-permute-start | bytes 584 | tf_op jit(solution)/shard_map/ppermute | solution.py:37
  6.6 8.2 %collective-permute-start.1 = (s32[1,48]{1,0:T(1,128)S(1)}, s32[1,48]{1,0:T(1,128)S(1)}, u32[]{:S(2)}, u32[]{:S(2)}) collective-permute-start(s32[1,48]{1,0:T(1,128)S(1)} %pad_add_fusion.1), channel_id=1, source_target_pairs={{0,8},{1,9},{2,10},{3,11},{4,12},{5,13},{6,14},{7,15},{8,0},{9,1},... | collective-permute-start | bytes 584 | tf_op jit(solution)/shard_map/ppermute | solution.py:37
  6.6 8.2 %collective-permute-start = (s32[1,48]{1,0:T(1,128)S(1)}, s32[1,48]{1,0:T(1,128)S(1)}, u32[]{:S(2)}, u32[]{:S(2)}) collective-permute-start(s32[1,48]{1,0:T(1,128)S(1)} %pad_add_fusion.1), channel_id=1, source_target_pairs={{0,4},{1,5},{2,6},{3,7},{4,0},{5,1},{6,2},{7,3},{8,12},{9,13},{10,... | collective-permute-start | bytes 584 | tf_op jit(solution)/shard_map/ppermute | solution.py:37
  14.8 10.6 %collective-permute-start.7 = (bf16[128,3584]{1,0:T(8,128)(2,1)S(1)}, bf16[128,3584]{1,0:T(8,128)(2,1)S(1)}, u32[]{:S(2)}, u32[]{:S(2)}) collective-permute-start(bf16[128,3584]{1,0:T(8,128)(2,1)S(1)} %get-tuple-element.68), channel_id=1, source_target_pairs={{0,1},{1,0},{2,3},{3,2},{4,5},{5,4},{6,7},{7,6},{8,9},{9,8},{10,11... | collective-permute-start | bytes 2752520 | tf_op jit(solution)/shard_map/ppermute | solution.py:37
  15.0 3.1 %collective-permute-start.5 = (s32[4,48]{1,0:T(4,128)S(1)}, s32[4,48]{1,0:T(4,128)S(1)}, u32[]{:S(2)}, u32[]{:S(2)}) collective-permute-start(s32[4,48]{1,0:T(4,128)S(1)} %pad_add_fusion.refs_0_), channel_id=1, source_target_pairs={{0,3},{1,2},{2,1},{3,0},{4,7},{5,6},{6,5},{7,4},{8,11},{9,10},{10,... | collective-permute-start | bytes 2312 | tf_op jit(solution)/shard_map/ppermute | solution.py:37
  16.7 3.6 %collective-permute-start.4 = (s32[4,48]{1,0:T(4,128)S(1)}, s32[4,48]{1,0:T(4,128)S(1)}, u32[]{:S(2)}, u32[]{:S(2)}) collective-permute-start(s32[4,48]{1,0:T(4,128)S(1)} %pad_add_fusion.refs_0_), channel_id=1, source_target_pairs={{0,2},{1,3},{2,0},{3,1},{4,6},{5,7},{6,4},{7,5},{8,10},{9,11},{10,... | collective-permute-start | bytes 2312 | tf_op jit(solution)/shard_map/ppermute | solution.py:37
  17.1 3.2 %collective-permute-start.3 = (s32[4,48]{1,0:T(4,128)S(1)}, s32[4,48]{1,0:T(4,128)S(1)}, u32[]{:S(2)}, u32[]{:S(2)}) collective-permute-start(s32[4,48]{1,0:T(4,128)S(1)} %pad_add_fusion.refs_0_), channel_id=1, source_target_pairs={{0,1},{1,0},{2,3},{3,2},{4,5},{5,4},{6,7},{7,6},{8,9},{9,8},{10,11... | collective-permute-start | bytes 2312 | tf_op jit(solution)/shard_map/ppermute | solution.py:37
  28.1 7.7 %collective-permute-start.9 = (bf16[64,1792]{1,0:T(8,128)(2,1)S(1)}, bf16[64,1792]{1,0:T(8,128)(2,1)S(1)}, u32[]{:S(2)}, u32[]{:S(2)}) collective-permute-start(bf16[64,1792]{1,0:T(8,128)(2,1)S(1)} %get-tuple-element.140), channel_id=1, source_target_pairs={{0,2},{1,3},{4,0},{5,1},{8,4},{9,5},{12,8},{13,9},{14,12},{15,13},... | collective-permute-start | bytes 688136 | tf_op jit(solution)/shard_map/ppermute | solution.py:79
  28.5 7.4 %collective-permute-start.8 = (bf16[64,1792]{1,0:T(8,128)(2,1)S(1)}, bf16[64,1792]{1,0:T(8,128)(2,1)S(1)}, u32[]{:S(2)}, u32[]{:S(2)}) collective-permute-start(bf16[64,1792]{1,0:T(8,128)(2,1)S(1)} %get-tuple-element.141), channel_id=1, source_target_pairs={{0,4},{1,5},{4,8},{5,9},{8,12},{9,13},{12,14},{13,15},{14,10},{15,... | collective-permute-start | bytes 688136 | tf_op jit(solution)/shard_map/ppermute | solution.py:79
  36.0 14.1 %collective-permute-start.11 = (bf16[64,3584]{1,0:T(8,128)(2,1)S(1)}, bf16[64,3584]{1,0:T(8,128)(2,1)S(1)}, u32[]{:S(2)}, u32[]{:S(2)}) collective-permute-start(bf16[64,3584]{1,0:T(8,128)(2,1)S(1)} %fusion), channel_id=1, source_target_pairs={{0,4},{1,5},{4,8},{5,9},{8,12},{9,13},{12,14},{13,15},{14,10},{15,... | collective-permute-start | bytes 1376264 | tf_op jit(solution)/shard_map/ppermute | solution.py:79
  37.7 11.3 %collective-permute-start.15 = (bf16[64,3584]{1,0:T(8,128)(2,1)S(1)}, bf16[64,3584]{1,0:T(8,128)(2,1)S(1)}, u32[]{:S(2)}, u32[]{:S(2)}) collective-permute-start(bf16[64,3584]{1,0:T(8,128)(2,1)S(1)} %fusion.1), channel_id=1, source_target_pairs={{0,2},{1,3},{4,0},{5,1},{8,4},{9,5},{12,8},{13,9},{14,12},{15,13},... | collective-permute-start | bytes 1376264 | tf_op jit(solution)/shard_map/ppermute | solution.py:79
  38.2 11.7 %collective-permute-start.10 = (bf16[128,3584]{1,0:T(8,128)(2,1)S(1)}, bf16[128,3584]{1,0:T(8,128)(2,1)S(1)}, u32[]{:S(2)}, u32[]{:S(2)}) collective-permute-start(bf16[128,3584]{1,0:T(8,128)(2,1)S(1)} %get-tuple-element.78), channel_id=1, source_target_pairs={{0,1},{1,0},{2,3},{3,2},{4,5},{5,4},{6,7},{7,6},{8,9},{9,8},{10,11... | collective-permute-start | bytes 2752520 | tf_op jit(solution)/shard_map/ppermute | solution.py:37
  41.9 7.8 %collective-permute-start.12 = (bf16[128,3584]{1,0:T(8,128)(2,1)S(1)}, bf16[128,3584]{1,0:T(8,128)(2,1)S(1)}, u32[]{:S(2)}, u32[]{:S(2)}) collective-permute-start(bf16[128,3584]{1,0:T(8,128)(2,1)S(1)} %get-tuple-element.84), channel_id=1, source_target_pairs={{0,1},{1,0},{2,3},{3,2},{4,5},{5,4},{6,7},{7,6},{8,9},{9,8},{10,11... | collective-permute-start | bytes 2752520 | tf_op jit(solution)/shard_map/ppermute | solution.py:37
  49.1 10.9 %collective-permute-start.16 = (bf16[64,3584]{1,0:T(8,128)(2,1)S(1)}, bf16[64,3584]{1,0:T(8,128)(2,1)S(1)}, u32[]{:S(2)}, u32[]{:S(2)}) collective-permute-start(bf16[64,3584]{1,0:T(8,128)(2,1)S(1)} %fusion.4), channel_id=1, source_target_pairs={{0,2},{1,3},{4,0},{5,1},{8,4},{9,5},{12,8},{13,9},{14,12},{15,13},... | collective-permute-start | bytes 1376264 | tf_op jit(solution)/shard_map/ppermute | solution.py:79
  50.2 10.2 %collective-permute-start.13 = (bf16[64,3584]{1,0:T(8,128)(2,1)S(1)}, bf16[64,3584]{1,0:T(8,128)(2,1)S(1)}, u32[]{:S(2)}, u32[]{:S(2)}) collective-permute-start(bf16[64,3584]{1,0:T(8,128)(2,1)S(1)} %fusion.2), channel_id=1, source_target_pairs={{0,4},{1,5},{4,8},{5,9},{8,12},{9,13},{12,14},{13,15},{14,10},{15,... | collective-permute-start | bytes 1376264 | tf_op jit(solution)/shard_map/ppermute | solution.py:79
  60.1 10.0 %collective-permute-start.17 = (bf16[64,3584]{1,0:T(8,128)(2,1)S(1)}, bf16[64,3584]{1,0:T(8,128)(2,1)S(1)}, u32[]{:S(2)}, u32[]{:S(2)}) collective-permute-start(bf16[64,3584]{1,0:T(8,128)(2,1)S(1)} %fusion.5), channel_id=1, source_target_pairs={{0,2},{1,3},{4,0},{5,1},{8,4},{9,5},{12,8},{13,9},{14,12},{15,13},... | collective-permute-start | bytes 1376264 | tf_op jit(solution)/shard_map/ppermute | solution.py:79
  60.5 9.8 %collective-permute-start.14 = (bf16[64,3584]{1,0:T(8,128)(2,1)S(1)}, bf16[64,3584]{1,0:T(8,128)(2,1)S(1)}, u32[]{:S(2)}, u32[]{:S(2)}) collective-permute-start(bf16[64,3584]{1,0:T(8,128)(2,1)S(1)} %fusion.3), channel_id=1, source_target_pairs={{0,4},{1,5},{4,8},{5,9},{8,12},{9,13},{12,14},{13,15},{14,10},{15,... | collective-permute-start | bytes 1376264 | tf_op jit(solution)/shard_map/ppermute | solution.py:79
  71.9 9.1 %collective-permute-start.18 = (bf16[64,3584]{1,0:T(8,128)(2,1)S(1)}, bf16[64,3584]{1,0:T(8,128)(2,1)S(1)}, u32[]{:S(2)}, u32[]{:S(2)}) collective-permute-start(bf16[64,3584]{1,0:T(8,128)(2,1)S(1)} %bitcast.6), channel_id=1, source_target_pairs={{0,4},{1,5},{4,8},{5,9},{8,12},{9,13},{12,14},{13,15},{14,10},{15,... | collective-permute-start | bytes 1376264 | tf_op jit(solution)/shard_map/ppermute | solution.py:79
  73.9 8.9 %collective-permute-start.20 = (bf16[64,3584]{1,0:T(8,128)(2,1)S(1)}, bf16[64,3584]{1,0:T(8,128)(2,1)S(1)}, u32[]{:S(2)}, u32[]{:S(2)}) collective-permute-start(bf16[64,3584]{1,0:T(8,128)(2,1)S(1)} %bitcast.7), channel_id=1, source_target_pairs={{0,2},{1,3},{4,0},{5,1},{8,4},{9,5},{12,8},{13,9},{14,12},{15,13},... | collective-permute-start | bytes 1376264 | tf_op jit(solution)/shard_map/ppermute | solution.py:79
  76.5 7.0 %collective-permute-start.21 = (bf16[64,3584]{1,0:T(8,128)(2,1)S(1)}, bf16[64,3584]{1,0:T(8,128)(2,1)S(1)}, u32[]{:S(2)}, u32[]{:S(2)}) collective-permute-start(bf16[64,3584]{1,0:T(8,128)(2,1)S(1)} %bitcast.8), channel_id=1, source_target_pairs={{0,1},{1,0},{2,3},{3,2},{4,5},{5,4},{6,7},{7,6},{8,9},{9,8},{10,11... | collective-permute-start | bytes 1376264 | tf_op jit(solution)/shard_map/ppermute | solution.py:37
  81.0 10.7 %collective-permute-start.19 = (bf16[64,3584]{1,0:T(8,128)(2,1)S(1)}, bf16[64,3584]{1,0:T(8,128)(2,1)S(1)}, u32[]{:S(2)}, u32[]{:S(2)}) collective-permute-start(bf16[64,3584]{1,0:T(8,128)(2,1)S(1)} %collective-permute-done.18.refs_0_), channel_id=1, source_target_pairs={{0,4},{1,5},{4,8},{5,9},{8,12},{9,13},{12,14},{13,15},{14,10},{15,... | collective-permute-start | bytes 1376264 | tf_op jit(solution)/shard_map/ppermute | solution.py:79
  82.8 10.7 %collective-permute-start.23 = (bf16[64,3584]{1,0:T(8,128)(2,1)S(1)}, bf16[64,3584]{1,0:T(8,128)(2,1)S(1)}, u32[]{:S(2)}, u32[]{:S(2)}) collective-permute-start(bf16[64,3584]{1,0:T(8,128)(2,1)S(1)} %collective-permute-done.20.refs_1_), channel_id=1, source_target_pairs={{0,2},{1,3},{4,0},{5,1},{8,4},{9,5},{12,8},{13,9},{14,12},{15,13},... | collective-permute-start | bytes 1376264 | tf_op jit(solution)/shard_map/ppermute | solution.py:79
  83.0 10.7 %collective-permute-start.25 = (bf16[64,3584]{1,0:T(8,128)(2,1)S(1)}, bf16[64,3584]{1,0:T(8,128)(2,1)S(1)}, u32[]{:S(2)}, u32[]{:S(2)}) collective-permute-start(bf16[64,3584]{1,0:T(8,128)(2,1)S(1)} %collective-permute-done.20.refs_1_), channel_id=1, source_target_pairs={{0,1},{1,0},{2,3},{3,2},{4,5},{5,4},{6,7},{7,6},{8,9},{9,8},{10,11... | collective-permute-start | bytes 1376264 | tf_op jit(solution)/shard_map/ppermute | solution.py:37
  83.0 11.2 %collective-permute-start.24 = (bf16[64,3584]{1,0:T(8,128)(2,1)S(1)}, bf16[64,3584]{1,0:T(8,128)(2,1)S(1)}, u32[]{:S(2)}, u32[]{:S(2)}) collective-permute-start(bf16[64,3584]{1,0:T(8,128)(2,1)S(1)} %collective-permute-done.18.refs_0_), channel_id=1, source_target_pairs={{0,1},{1,0},{2,3},{3,2},{4,5},{5,4},{6,7},{7,6},{8,9},{9,8},{10,11... | collective-permute-start | bytes 1376264 | tf_op jit(solution)/shard_map/ppermute | solution.py:37
  91.6 10.6 %collective-permute-start.22 = (bf16[64,3584]{1,0:T(8,128)(2,1)S(1)}, bf16[64,3584]{1,0:T(8,128)(2,1)S(1)}, u32[]{:S(2)}, u32[]{:S(2)}) collective-permute-start(bf16[64,3584]{1,0:T(8,128)(2,1)S(1)} %collective-permute-done.19.refs_0_), channel_id=1, source_target_pairs={{0,4},{1,5},{4,8},{5,9},{8,12},{9,13},{12,14},{13,15},{14,10},{15,... | collective-permute-start | bytes 1376264 | tf_op jit(solution)/shard_map/ppermute | solution.py:79
  93.5 10.7 %collective-permute-start.27 = (bf16[64,3584]{1,0:T(8,128)(2,1)S(1)}, bf16[64,3584]{1,0:T(8,128)(2,1)S(1)}, u32[]{:S(2)}, u32[]{:S(2)}) collective-permute-start(bf16[64,3584]{1,0:T(8,128)(2,1)S(1)} %collective-permute-done.23.refs_1_), channel_id=1, source_target_pairs={{0,2},{1,3},{4,0},{5,1},{8,4},{9,5},{12,8},{13,9},{14,12},{15,13},... | collective-permute-start | bytes 1376264 | tf_op jit(solution)/shard_map/ppermute | solution.py:79
  93.7 10.8 %collective-permute-start.31 = (bf16[64,3584]{1,0:T(8,128)(2,1)S(1)}, bf16[64,3584]{1,0:T(8,128)(2,1)S(1)}, u32[]{:S(2)}, u32[]{:S(2)}) collective-permute-start(bf16[64,3584]{1,0:T(8,128)(2,1)S(1)} %collective-permute-done.23.refs_1_), channel_id=1, source_target_pairs={{0,1},{1,0},{2,3},{3,2},{4,5},{5,4},{6,7},{7,6},{8,9},{9,8},{10,11... | collective-permute-start | bytes 1376264 | tf_op jit(solution)/shard_map/ppermute | solution.py:37
  93.7 11.3 %collective-permute-start.30 = (bf16[64,3584]{1,0:T(8,128)(2,1)S(1)}, bf16[64,3584]{1,0:T(8,128)(2,1)S(1)}, u32[]{:S(2)}, u32[]{:S(2)}) collective-permute-start(bf16[64,3584]{1,0:T(8,128)(2,1)S(1)} %collective-permute-done.19.refs_0_), channel_id=1, source_target_pairs={{0,1},{1,0},{2,3},{3,2},{4,5},{5,4},{6,7},{7,6},{8,9},{9,8},{10,11... | collective-permute-start | bytes 1376264 | tf_op jit(solution)/shard_map/ppermute | solution.py:37
  102.3 6.1 %collective-permute-start.29 = (bf16[64,1792]{1,0:T(8,128)(2,1)S(1)}, bf16[64,1792]{1,0:T(8,128)(2,1)S(1)}, u32[]{:S(2)}, u32[]{:S(2)}) collective-permute-start(bf16[64,1792]{1,0:T(8,128)(2,1)S(1)} %slice.126), channel_id=1, source_target_pairs={{0,4},{1,5},{4,8},{5,9},{8,12},{9,13},{12,14},{13,15},{14,10},{15,... | collective-permute-start | bytes 688136 | tf_op jit(solution)/shard_map/ppermute | solution.py:79
  104.2 6.1 %collective-permute-start.33 = (bf16[64,1792]{1,0:T(8,128)(2,1)S(1)}, bf16[64,1792]{1,0:T(8,128)(2,1)S(1)}, u32[]{:S(2)}, u32[]{:S(2)}) collective-permute-start(bf16[64,1792]{1,0:T(8,128)(2,1)S(1)} %slice.127), channel_id=1, source_target_pairs={{0,2},{1,3},{4,0},{5,1},{8,4},{9,5},{12,8},{13,9},{14,12},{15,13},... | collective-permute-start | bytes 688136 | tf_op jit(solution)/shard_map/ppermute | solution.py:79
  104.4 7.4 %collective-permute-start.28 = (bf16[64,3584]{1,0:T(8,128)(2,1)S(1)}, bf16[64,3584]{1,0:T(8,128)(2,1)S(1)}, u32[]{:S(2)}, u32[]{:S(2)}) collective-permute-start(bf16[64,3584]{1,0:T(8,128)(2,1)S(1)} %collective-permute-done.27.refs_1_), channel_id=1, source_target_pairs={{0,1},{1,0},{2,3},{3,2},{4,5},{5,4},{6,7},{7,6},{8,9},{9,8},{10,11... | collective-permute-start | bytes 1376264 | tf_op jit(solution)/shard_map/ppermute | solution.py:37
  104.4 7.4 %collective-permute-start.26 = (bf16[64,3584]{1,0:T(8,128)(2,1)S(1)}, bf16[64,3584]{1,0:T(8,128)(2,1)S(1)}, u32[]{:S(2)}, u32[]{:S(2)}) collective-permute-start(bf16[64,3584]{1,0:T(8,128)(2,1)S(1)} %collective-permute-done.22.refs_0_), channel_id=1, source_target_pairs={{0,1},{1,0},{2,3},{3,2},{4,5},{5,4},{6,7},{7,6},{8,9},{9,8},{10,11... | collective-permute-start | bytes 1376264 | tf_op jit(solution)/shard_map/ppermute | solution.py:37
  (17 other events, 236.6 us)

commit v17 on v11

--- a/solution.py
+++ b/solution.py
@@ -418,32 +418,44 @@
     dec_far = after(dec[0], *stages[0])
     dec_kept = [dec[1], dec[3]]
     dec_core = [swap(dec_far, 1, size), swap(after(dec[2], table[0]), 1, size)]
-    enc_sent, kept, enc_left, code = far_product(
-        enc_coef, x_rows, size, rows, pick_rows[0].T, table
-    )
-    enc_kept, enc_core = [kept], [swap(enc_sent, 1, size)]
-
-    def both(slot):
-        terms = [term(*pair, slot, rows) for pair in ((enc_kept, enc_core), (dec_kept, dec_core))]
-        return jnp.concatenate(terms, axis=0)
 
     def travel(moving):
         return [shift(moving[0], 1, size), shift(moving[1], -1, size)]
 
-    far = both(0).astype(jnp.bfloat16)
-    moving = [far[:, :half], far[:, half:]]
-    enc_sent, kept = near_product(after(enc_left, *moving), x_rows)
-    came, enc_sent = tied(travel(moving), enc_sent)
+    def begin(kept, from_core):
+        far = term(kept, from_core, 0, rows).astype(jnp.bfloat16)
+        return [far[:, :half], far[:, half:]]
+
+    def second(came, kept, from_core, order):
+        moving = []
+        for side, value in enumerate(after(came, order)):
+            pads = ((0, 0, 0), (0, half, 0) if side == 0 else (half, 0, 0))
+            value = lax.pad(value.astype(jnp.float32), jnp.float32(0), pads)
+            value = value + term(kept, from_core, 2 - side, rows)
+            moving.append(value.astype(jnp.bfloat16))
+        return moving
+
+    dec_moving = begin(dec_kept, after(dec_core, table[0]))
+    enc_sent, kept, enc_left, code = far_product(
+        after(enc_coef, *dec_moving), x_rows, size, rows, pick_rows[0].T, table
+    )
+    dec_came, enc_sent = tied(travel(dec_moving), enc_sent)
+    enc_kept, enc_core = [kept], [swap(enc_sent, 1, size)]
+    dec_moving = second(dec_came, dec_kept, dec_core, enc_sent)
+    enc_moving = begin(enc_kept, after(enc_core, *dec_moving))
+    enc_sent, kept = near_product(after(enc_left, *enc_moving), x_rows)
+    enc_came, dec_came, enc_sent = tied(travel(enc_moving), travel(dec_moving), enc_sent)
     enc_kept.append(kept)
     enc_core.append(swap(enc_sent, 1, size))
-    for hop in range(1, chips // 2):
+    enc_came = travel(second(enc_came, enc_kept, enc_core, enc_sent))
+    came = [jnp.concatenate(pair, axis=0) for pair in zip(enc_came, dec_came)]
+    for hop in range(2, chips // 2):
         moving = []
         for side, value in enumerate(came):
-            value = value.astype(jnp.float32)
-            if value.shape[1] < width:
-                pads = ((0, 0, 0), (0, half, 0) if side == 0 else (half, 0, 0))
-                value = lax.pad(value, jnp.float32(0), pads)
-            moving.append((value + both(2 * hop - side)).astype(jnp.bfloat16))
+            slot = 2 * hop - side
+            terms = [term(*pair, slot, rows) for pair in ((enc_kept, enc_core), (dec_kept, dec_core))]
+            value = value.astype(jnp.float32) + jnp.concatenate(terms, axis=0)
+            moving.append(value.astype(jnp.bfloat16))
         came = travel(moving)
     states = (enc_w, enc_m, enc_v, dec_w, dec_m, dec_v)
     parts = ([enc_kept[1], enc_core[1]], [dec_kept[1], dec_core[1]], came)

time: 113 us -> 115 us (1.018)
  starting transfers between devices: 26.6 us -> 30.6 us
  waiting for transfers between devices: 55.4 us -> 53.9 us
    ppermute x16 -> x20, starting transfers between devices: 16.7 us -> 20.9 us  [shift(): return lax.ppermute(value, 'latent', pairs)]
    ppermute x19, waiting for transfers between devices: 6.48 us -> 2.72 us  [swap(): return lax.ppermute(value, 'latent', [(i, i ^ bits) for i in range(size)])]
    ppermute x16 -> x20, waiting for transfers between devices: 48.9 us -> 51.2 us  [shift(): return lax.ppermute(value, 'latent', pairs)]
  transfers between devices with their start and end apart: 35 -> 39, of which waited for: 18 -> 17; matrix products, arithmetic and copies ran while one was open for 1% -> 1% of each run, Pallas kernels for 22% -> 22%
where the time goes in v17:
time: 115 us
  waiting for transfers between devices  53.9 us (47%)
  starting transfers between devices  30.6 us (27%)
  Pallas kernels  27.6 us (24%)
  other arithmetic  2.09 us (2%)
    ppermute x20, waiting for transfers between devices, shift(): return lax.ppermute(value, 'latent', pairs)  51.2 us
    ppermute x20, starting transfers between devices, shift(): return lax.ppermute(value, 'latent', pairs)  20.9 us
    ppermute x19, starting transfers between devices, swap(): return lax.ppermute(value, 'latent', [(i, i ^ bits) for i in range(size)])  9.7 us
    pallas_call x2, Pallas kernels, product(): pl.pallas_call(kernel, grid=(width // tile,), in_specs=in_specs + [pl.Blo...  8.7 us
    pallas_call x1, Pallas kernels, stream_product(): pl.pallas_call(functools.partial(stream_kernel, size, rows), in_specs=[pl...  8.36 us
    pallas_call x6, Pallas kernels, place(): pl.pallas_call(functools.partial(place_kernel, plan, size, rows, count),...  6.39 us
    pallas_call x2, Pallas kernels, update(): pl.pallas_call(blocks_kernel if blocks_only else states_kernel, grid=(row...  4.19 us
    ppermute x19, waiting for transfers between devices, swap(): return lax.ppermute(value, 'latent', [(i, i ^ bits) for i in range(size)])  2.72 us
  transfers between devices with their start and end apart: 39, of which 17 were waited for; matrix products, arithmetic and copies ran while one was open for 1% of the time, Pallas kernels for 22%

profile of v17, /device:TPU:0, one launch (start us, length us, event | category | flops | bytes accessed | tf_op | source)
XLA Modules:
  0.0 115.3 jit_solution(6455186700523929918)
XLA Ops:
  1.6 2.5 %collective-permute-start.2 = (s32[1,48]{1,0:T(1,128)S(1)}, s32[1,48]{1,0:T(1,128)S(1)}, u32[]{:S(2)}, u32[]{:S(2)}) collective-permute-start(s32[1,48]{1,0:T(1,128)S(1)} %pad_add_fusion.1), channel_id=1, source_target_pairs={{0,3},{1,2},{2,1},{3,0},{4,7},{5,6},{6,5},{7,4},{8,11},{9,10},{10,... | collective-permute-start | bytes 584 | tf_op jit(solution)/shard_map/ppermute | solution.py:37
  4.7 8.4 %product.1 = (bf16[128,3584]{1,0:T(8,128)(2,1)S(1)}, bf16[128,3584]{1,0:T(8,128)(2,1)S(1)}, bf16[128,3584]{1,0:T(8,128)(2,1)S(1)}, bf16[128,3584]{1,0:T(8,128)(2,1)S(1)}) custom-call(bf16[1024,512]{1,0:T(8,128)(2,1)} %coef_ref.1, bf16[1024,3584]{1,0:T(8,128)(2,1)} %right_hbm.1), custom_call_target="tpu_custom_call" | custom-call | flops 3758096384 | bytes 12058624 | tf_op jit(solution)/shard_map/product/pallas_call | solution.py:182
  13.8 3.8 %collective-permute-start.7 = (s32[4,48]{1,0:T(4,128)S(1)}, s32[4,48]{1,0:T(4,128)S(1)}, u32[]{:S(2)}, u32[]{:S(2)}) collective-permute-start(s32[4,48]{1,0:T(4,128)S(1)} %pad_add_fusion.refs_0_), channel_id=1, source_target_pairs={{0,12},{1,13},{2,14},{3,15},{4,8},{5,9},{6,10},{7,11},{8,4},{9,5},... | collective-permute-start | bytes 2312 | tf_op jit(solution)/shard_map/ppermute | solution.py:37
  18.3 1.8 %collective-permute-start.9 = (bf16[32,1792]{1,0:T(8,128)(2,1)S(1)}, bf16[32,1792]{1,0:T(8,128)(2,1)S(1)}, u32[]{:S(2)}, u32[]{:S(2)}) collective-permute-start(bf16[32,1792]{1,0:T(8,128)(2,1)S(1)} %get-tuple-element.162), channel_id=1, source_target_pairs={{0,2},{1,3},{4,0},{5,1},{8,4},{9,5},{12,8},{13,9},{14,12},{15,13},... | collective-permute-start | bytes 344072 | tf_op jit(solution)/shard_map/ppermute | solution.py:79
  20.3 1.8 %collective-permute-done.6.refs_2_ = s32[4,48]{1,0:T(4,128)S(1)} collective-permute-done((s32[4,48]{1,0:T(4,128)S(1)}, s32[4,48]{1,0:T(4,128)S(1)}, u32[]{:S(2)}, u32[]{:S(2)}) %collective-permute-start.6) | collective-permute-done | bytes 800 | tf_op jit(solution)/shard_map/ppermute | solution.py:37
  22.2 4.9 %far_product.1 = (bf16[128,3584]{1,0:T(8,128)(2,1)S(1)}, bf16[128,3584]{1,0:T(8,128)(2,1)S(1)}, bf16[256,1024]{1,0:T(8,128)(2,1)S(1)}, s32[32,1]{1,0:T(8,128)S(1)}) custom-call(bf16[1024,512]{1,0:T(8,128)(2,1)S(1)} %copy-done.6, bf16[1024,3584]{1,0:T(8,128)(2,1)S(1)} %bitcast.5, s32[2,16]{1,0:T(2,128)S(1)} %bitcast.10, s32[4,48]{1,0:T(4,128)S(1)} %pad_add_fusion.refs_0_, ...), custom_call_target="tpu_custom_call" | custom-call | flops 1879048192 | bytes 9699328 | tf_op jit(solution)/shard_map/far_product/pallas_call | solution.py:241
  27.4 1.6 %collective-permute-start.14 = (bf16[32,3584]{1,0:T(8,128)(2,1)S(1)}, bf16[32,3584]{1,0:T(8,128)(2,1)S(1)}, u32[]{:S(2)}, u32[]{:S(2)}) collective-permute-start(bf16[32,3584]{1,0:T(8,128)(2,1)S(1)} %get-tuple-element.152), channel_id=1, source_target_pairs={{0,2},{1,3},{4,0},{5,1},{8,4},{9,5},{12,8},{13,9},{14,12},{15,13},... | collective-permute-start | bytes 688136 | tf_op jit(solution)/shard_map/ppermute | solution.py:79
  29.8 1.6 %collective-permute-start.12 = (bf16[32,1792]{1,0:T(8,128)(2,1)S(1)}, bf16[32,1792]{1,0:T(8,128)(2,1)S(1)}, u32[]{:S(2)}, u32[]{:S(2)}) collective-permute-start(bf16[32,1792]{1,0:T(8,128)(2,1)S(1)} %get-tuple-element.160), channel_id=1, source_target_pairs={{0,2},{1,3},{4,0},{5,1},{8,4},{9,5},{12,8},{13,9},{14,12},{15,13},... | collective-permute-start | bytes 344072 | tf_op jit(solution)/shard_map/ppermute | solution.py:79
  31.9 3.8 %near_product.1 = (bf16[128,3584]{1,0:T(8,128)(2,1)S(1)}, bf16[128,3584]{1,0:T(8,128)(2,1)S(1)}) custom-call(bf16[256,1024]{1,0:T(8,128)(2,1)S(1)} %get-tuple-element.96.left_ref, bf16[1024,3584]{1,0:T(8,128)(2,1)S(1)} %bitcast.5), custom_call_target="tpu_custom_call" | custom-call | flops 1879048192 | bytes 9699328 | tf_op jit(solution)/shard_map/near_product/pallas_call | solution.py:241
  35.9 1.5 %collective-permute-done.13 = bf16[32,3584]{1,0:T(8,128)(2,1)S(1)} collective-permute-done((bf16[32,3584]{1,0:T(8,128)(2,1)S(1)}, bf16[32,3584]{1,0:T(8,128)(2,1)S(1)}, u32[]{:S(2)}, u32[]{:S(2)}) %collective-permute-start.13) | collective-permute-done | bytes 229408 | tf_op jit(solution)/shard_map/ppermute | solution.py:79
  37.9 1.2 %collective-permute-done.11 = bf16[32,1792]{1,0:T(8,128)(2,1)S(1)} collective-permute-done((bf16[32,1792]{1,0:T(8,128)(2,1)S(1)}, bf16[32,1792]{1,0:T(8,128)(2,1)S(1)}, u32[]{:S(2)}, u32[]{:S(2)}) %collective-permute-start.11) | collective-permute-done | bytes 114720 | tf_op jit(solution)/shard_map/ppermute | solution.py:79
  40.3 1.3 %collective-permute-start.16 = (bf16[32,3584]{1,0:T(8,128)(2,1)S(1)}, bf16[32,3584]{1,0:T(8,128)(2,1)S(1)}, u32[]{:S(2)}, u32[]{:S(2)}) collective-permute-start(bf16[32,3584]{1,0:T(8,128)(2,1)S(1)} %get-tuple-element.150), channel_id=1, source_target_pairs={{0,4},{1,5},{4,8},{5,9},{8,12},{9,13},{12,14},{13,15},{14,10},{15,... | collective-permute-start | bytes 688136 | tf_op jit(solution)/shard_map/ppermute | solution.py:79
  41.7 5.8 %collective-permute-done.19 = bf16[32,3584]{1,0:T(8,128)(2,1)S(1)} collective-permute-done((bf16[32,3584]{1,0:T(8,128)(2,1)S(1)}, bf16[32,3584]{1,0:T(8,128)(2,1)S(1)}, u32[]{:S(2)}, u32[]{:S(2)}) %collective-permute-start.19) | collective-permute-done | bytes 229408 | tf_op jit(solution)/shard_map/ppermute | solution.py:79
  48.6 1.3 %collective-permute-start.17 = (bf16[64,3584]{1,0:T(8,128)(2,1)S(1)}, bf16[64,3584]{1,0:T(8,128)(2,1)S(1)}, u32[]{:S(2)}, u32[]{:S(2)}) collective-permute-start(bf16[64,3584]{1,0:T(8,128)(2,1)S(1)} %fusion), channel_id=1, source_target_pairs={{0,4},{1,5},{4,8},{5,9},{8,12},{9,13},{12,14},{13,15},{14,10},{15,... | collective-permute-start | bytes 1376264 | tf_op jit(solution)/shard_map/ppermute | solution.py:79
  50.0 9.8 %collective-permute-done.20 = bf16[64,3584]{1,0:T(8,128)(2,1)S(1)} collective-permute-done((bf16[64,3584]{1,0:T(8,128)(2,1)S(1)}, bf16[64,3584]{1,0:T(8,128)(2,1)S(1)}, u32[]{:S(2)}, u32[]{:S(2)}) %collective-permute-start.20) | collective-permute-done | bytes 458784 | tf_op jit(solution)/shard_map/ppermute | solution.py:79
  60.7 1.3 %collective-permute-start.18 = (bf16[64,3584]{1,0:T(8,128)(2,1)S(1)}, bf16[64,3584]{1,0:T(8,128)(2,1)S(1)}, u32[]{:S(2)}, u32[]{:S(2)}) collective-permute-start(bf16[64,3584]{1,0:T(8,128)(2,1)S(1)} %fusion.1), channel_id=1, source_target_pairs={{0,4},{1,5},{4,8},{5,9},{8,12},{9,13},{12,14},{13,15},{14,10},{15,... | collective-permute-start | bytes 1376264 | tf_op jit(solution)/shard_map/ppermute | solution.py:79
  62.0 9.1 %collective-permute-done.21.refs_10_.refs_14_ = bf16[64,3584]{1,0:T(8,128)(2,1)S(1)} collective-permute-done((bf16[64,3584]{1,0:T(8,128)(2,1)S(1)}, bf16[64,3584]{1,0:T(8,128)(2,1)S(1)}, u32[]{:S(2)}, u32[]{:S(2)}) %collective-permute-start.21) | collective-permute-done | bytes 458784 | tf_op jit(solution)/shard_map/ppermute | solution.py:79
  71.7 1.6 %blocks.1 = bf16[2,32,3584]{2,1,0:T(8,128)(2,1)S(1)} custom-call(s32[32,1]{1,0:T(8,128)S(1)} %get-tuple-element.86.refs_0_, f32[32,3584]{1,0:T(8,128)S(1)} %copy-done, f32[32,3584]{1,0:T(8,128)S(1)} %copy-done.1, f32[32,3584]{1,0:T(8,128)S(1)} %copy-done.2, f32[32,3584]{1,0:T(8,128)S(1)} %copy-done.3, f32[32,3584]{1,0:T(8,128)S(1)} %copy-done.4, ...), custom_call_target="tpu_custom_call" | custom-call | flops 1146880 | bytes 1146880 | tf_op jit(solution)/shard_map/blocks/pallas_call | solution.py:326
  73.4 1.3 %collective-permute-start.22 = (bf16[64,3584]{1,0:T(8,128)(2,1)S(1)}, bf16[64,3584]{1,0:T(8,128)(2,1)S(1)}, u32[]{:S(2)}, u32[]{:S(2)}) collective-permute-start(bf16[64,3584]{1,0:T(8,128)(2,1)S(1)} %bitcast.6), channel_id=1, source_target_pairs={{0,4},{1,5},{4,8},{5,9},{8,12},{9,13},{12,14},{13,15},{14,10},{15,... | collective-permute-start | bytes 1376264 | tf_op jit(solution)/shard_map/ppermute | solution.py:79
  75.4 2.6 %states.1 = (f32[32,3584]{1,0:T(8,128)}, f32[32,3584]{1,0:T(8,128)}, f32[32,3584]{1,0:T(8,128)}, f32[32,3584]{1,0:T(8,128)}, f32[32,3584]{1,0:T(8,128)}, /*index=5*/f32[32,3584]{1,0:T(8,128)}) custom-call(s32[32,1]{1,0:T(8,128)S(1)} %get-tuple-element.86.refs_0_, f32[32,3584]{1,0:T(8,128)S(1)} %copy-done, f32[32,3584]{1,0:T(8,128)S(1)} %copy-done.1, ...), custom_call_target="tpu_custom_call" | custom-call | flops 1146880 | bytes 1146880 | tf_op jit(solution)/shard_map/states/pallas_call | solution.py:326
  78.8 5.3 %collective-permute-done.22.refs_0_ = bf16[64,3584]{1,0:T(8,128)(2,1)S(1)} collective-permute-done((bf16[64,3584]{1,0:T(8,128)(2,1)S(1)}, bf16[64,3584]{1,0:T(8,128)(2,1)S(1)}, u32[]{:S(2)}, u32[]{:S(2)}) %collective-permute-start.22) | collective-permute-done | bytes 458784 | tf_op jit(solution)/shard_map/ppermute | solution.py:79
  84.1 1.3 %collective-permute-start.23 = (bf16[64,3584]{1,0:T(8,128)(2,1)S(1)}, bf16[64,3584]{1,0:T(8,128)(2,1)S(1)}, u32[]{:S(2)}, u32[]{:S(2)}) collective-permute-start(bf16[64,3584]{1,0:T(8,128)(2,1)S(1)} %collective-permute-done.22.refs_0_), channel_id=1, source_target_pairs={{0,4},{1,5},{4,8},{5,9},{8,12},{9,13},{12,14},{13,15},{14,10},{15,... | collective-permute-start | bytes 1376264 | tf_op jit(solution)/shard_map/ppermute | solution.py:79
  86.6 1.1 place.7
  87.8 7.0 %collective-permute-done.23.refs_0_ = bf16[64,3584]{1,0:T(8,128)(2,1)S(1)} collective-permute-done((bf16[64,3584]{1,0:T(8,128)(2,1)S(1)}, bf16[64,3584]{1,0:T(8,128)(2,1)S(1)}, u32[]{:S(2)}, u32[]{:S(2)}) %collective-permute-start.23) | collective-permute-done | bytes 458784 | tf_op jit(solution)/shard_map/ppermute | solution.py:79
  94.8 1.3 %collective-permute-start.26 = (bf16[64,3584]{1,0:T(8,128)(2,1)S(1)}, bf16[64,3584]{1,0:T(8,128)(2,1)S(1)}, u32[]{:S(2)}, u32[]{:S(2)}) collective-permute-start(bf16[64,3584]{1,0:T(8,128)(2,1)S(1)} %collective-permute-done.23.refs_0_), channel_id=1, source_target_pairs={{0,4},{1,5},{4,8},{5,9},{8,12},{9,13},{12,14},{13,15},{14,10},{15,... | collective-permute-start | bytes 1376264 | tf_op jit(solution)/shard_map/ppermute | solution.py:79
  97.3 1.3 %place.8 = (bf16[512,3584]{1,0:T(8,128)(2,1)}, bf16[512,3584]{1,0:T(8,128)(2,1)}) custom-call(bf16[64,3584]{1,0:T(8,128)(2,1)S(1)} %collective-permute-done.23.refs_0_, bf16[64,3584]{1,0:T(8,128)(2,1)S(1)} %collective-permute-done.27.refs_1_, bf16[64,3584]{1,0:T(8,128)(2,1)S(1)} %collective-permute-done.28.refs_2_, ...), custom_call_target="tpu_custom_call", output_to_operand_aliasing={{0}: (4, {}), {1}: (5, {})} | custom-call | bytes 3670016 | tf_op jit(solution)/shard_map/place/pallas_call | solution.py:361
  98.6 6.5 %collective-permute-done.26.refs_0_ = bf16[64,3584]{1,0:T(8,128)(2,1)S(1)} collective-permute-done((bf16[64,3584]{1,0:T(8,128)(2,1)S(1)}, bf16[64,3584]{1,0:T(8,128)(2,1)S(1)}, u32[]{:S(2)}, u32[]{:S(2)}) %collective-permute-start.26) | collective-permute-done | bytes 458784 | tf_op jit(solution)/shard_map/ppermute | solution.py:79
  105.1 1.3 %collective-permute-start.33 = (bf16[64,1792]{1,0:T(8,128)(2,1)S(1)}, bf16[64,1792]{1,0:T(8,128)(2,1)S(1)}, u32[]{:S(2)}, u32[]{:S(2)}) collective-permute-start(bf16[64,1792]{1,0:T(8,128)(2,1)S(1)} %slice.134), channel_id=1, source_target_pairs={{0,4},{1,5},{4,8},{5,9},{8,12},{9,13},{12,14},{13,15},{14,10},{15,... | collective-permute-start | bytes 688136 | tf_op jit(solution)/shard_map/ppermute | solution.py:79
  107.9 1.3 %place.9 = (bf16[512,3584]{1,0:T(8,128)(2,1)}, bf16[512,3584]{1,0:T(8,128)(2,1)}) custom-call(bf16[64,3584]{1,0:T(8,128)(2,1)S(1)} %collective-permute-done.26.refs_0_, bf16[64,3584]{1,0:T(8,128)(2,1)S(1)} %collective-permute-done.31.refs_1_, bf16[64,3584]{1,0:T(8,128)(2,1)S(1)} %collective-permute-done.34.refs_2_, ...), custom_call_target="tpu_custom_call", output_to_operand_aliasing={{0}: (4, {}), {1}: (5, {})} | custom-call | bytes 3670016 | tf_op jit(solution)/shard_map/place/pallas_call | solution.py:361
  109.2 2.0 %collective-permute-done.33.refs_0_ = bf16[64,1792]{1,0:T(8,128)(2,1)S(1)} collective-permute-done((bf16[64,1792]{1,0:T(8,128)(2,1)S(1)}, bf16[64,1792]{1,0:T(8,128)(2,1)S(1)}, u32[]{:S(2)}, u32[]{:S(2)}) %collective-permute-start.33) | collective-permute-done | bytes 229408 | tf_op jit(solution)/shard_map/ppermute | solution.py:79
  111.2 1.5 %collective-permute-done.37.refs_1_ = bf16[64,1792]{1,0:T(8,128)(2,1)S(1)} collective-permute-done((bf16[64,1792]{1,0:T(8,128)(2,1)S(1)}, bf16[64,1792]{1,0:T(8,128)(2,1)S(1)}, u32[]{:S(2)}, u32[]{:S(2)}) %collective-permute-start.37) | collective-permute-done | bytes 229408 | tf_op jit(solution)/shard_map/ppermute | solution.py:79
  114.2 1.1 place.11
  (98 shorter events, 16.4 us)
Async XLA Ops:
  1.6 11.5 %collective-permute-start.2 = (s32[1,48]{1,0:T(1,128)S(1)}, s32[1,48]{1,0:T(1,128)S(1)}, u32[]{:S(2)}, u32[]{:S(2)}) collective-permute-start(s32[1,48]{1,0:T(1,128)S(1)} %pad_add_fusion.1), channel_id=1, source_target_pairs={{0,3},{1,2},{2,1},{3,0},{4,7},{5,6},{6,5},{7,4},{8,11},{9,10},{10,... | collective-permute-start | bytes 584 | tf_op jit(solution)/shard_map/ppermute | solution.py:37
  4.0 9.1 %collective-permute-start.1 = (s32[1,48]{1,0:T(1,128)S(1)}, s32[1,48]{1,0:T(1,128)S(1)}, u32[]{:S(2)}, u32[]{:S(2)}) collective-permute-start(s32[1,48]{1,0:T(1,128)S(1)} %pad_add_fusion.1), channel_id=1, source_target_pairs={{0,2},{1,3},{2,0},{3,1},{4,6},{5,7},{6,4},{7,5},{8,10},{9,11},{10,... | collective-permute-start | bytes 584 | tf_op jit(solution)/shard_map/ppermute | solution.py:37
  4.7 8.4 %collective-permute-start = (s32[1,48]{1,0:T(1,128)S(1)}, s32[1,48]{1,0:T(1,128)S(1)}, u32[]{:S(2)}, u32[]{:S(2)}) collective-permute-start(s32[1,48]{1,0:T(1,128)S(1)} %pad_add_fusion.1), channel_id=1, source_target_pairs={{0,1},{1,0},{2,3},{3,2},{4,5},{5,4},{6,7},{7,6},{8,9},{9,8},{10,11... | collective-permute-start | bytes 584 | tf_op jit(solution)/shard_map/ppermute | solution.py:37
  13.8 6.6 %collective-permute-start.7 = (s32[4,48]{1,0:T(4,128)S(1)}, s32[4,48]{1,0:T(4,128)S(1)}, u32[]{:S(2)}, u32[]{:S(2)}) collective-permute-start(s32[4,48]{1,0:T(4,128)S(1)} %pad_add_fusion.refs_0_), channel_id=1, source_target_pairs={{0,12},{1,13},{2,14},{3,15},{4,8},{5,9},{6,10},{7,11},{8,4},{9,5},... | collective-permute-start | bytes 2312 | tf_op jit(solution)/shard_map/ppermute | solution.py:37
  18.3 8.9 %collective-permute-start.9 = (bf16[32,1792]{1,0:T(8,128)(2,1)S(1)}, bf16[32,1792]{1,0:T(8,128)(2,1)S(1)}, u32[]{:S(2)}, u32[]{:S(2)}) collective-permute-start(bf16[32,1792]{1,0:T(8,128)(2,1)S(1)} %get-tuple-element.162), channel_id=1, source_target_pairs={{0,2},{1,3},{4,0},{5,1},{8,4},{9,5},{12,8},{13,9},{14,12},{15,13},... | collective-permute-start | bytes 344072 | tf_op jit(solution)/shard_map/ppermute | solution.py:79
  20.0 7.1 %collective-permute-start.8 = (bf16[32,1792]{1,0:T(8,128)(2,1)S(1)}, bf16[32,1792]{1,0:T(8,128)(2,1)S(1)}, u32[]{:S(2)}, u32[]{:S(2)}) collective-permute-start(bf16[32,1792]{1,0:T(8,128)(2,1)S(1)} %get-tuple-element.163), channel_id=1, source_target_pairs={{0,4},{1,5},{4,8},{5,9},{8,12},{9,13},{12,14},{13,15},{14,10},{15,... | collective-permute-start | bytes 344072 | tf_op jit(solution)/shard_map/ppermute | solution.py:79
  27.4 8.4 %collective-permute-start.14 = (bf16[32,3584]{1,0:T(8,128)(2,1)S(1)}, bf16[32,3584]{1,0:T(8,128)(2,1)S(1)}, u32[]{:S(2)}, u32[]{:S(2)}) collective-permute-start(bf16[32,3584]{1,0:T(8,128)(2,1)S(1)} %get-tuple-element.152), channel_id=1, source_target_pairs={{0,2},{1,3},{4,0},{5,1},{8,4},{9,5},{12,8},{13,9},{14,12},{15,13},... | collective-permute-start | bytes 688136 | tf_op jit(solution)/shard_map/ppermute | solution.py:79
  29.0 8.4 %collective-permute-start.13 = (bf16[32,3584]{1,0:T(8,128)(2,1)S(1)}, bf16[32,3584]{1,0:T(8,128)(2,1)S(1)}, u32[]{:S(2)}, u32[]{:S(2)}) collective-permute-start(bf16[32,3584]{1,0:T(8,128)(2,1)S(1)} %get-tuple-element.153), channel_id=1, source_target_pairs={{0,4},{1,5},{4,8},{5,9},{8,12},{9,13},{12,14},{13,15},{14,10},{15,... | collective-permute-start | bytes 688136 | tf_op jit(solution)/shard_map/ppermute | solution.py:79
  29.8 8.2 %collective-permute-start.12 = (bf16[32,1792]{1,0:T(8,128)(2,1)S(1)}, bf16[32,1792]{1,0:T(8,128)(2,1)S(1)}, u32[]{:S(2)}, u32[]{:S(2)}) collective-permute-start(bf16[32,1792]{1,0:T(8,128)(2,1)S(1)} %get-tuple-element.160), channel_id=1, source_target_pairs={{0,2},{1,3},{4,0},{5,1},{8,4},{9,5},{12,8},{13,9},{14,12},{15,13},... | collective-permute-start | bytes 344072 | tf_op jit(solution)/shard_map/ppermute | solution.py:79
  31.3 7.8 %collective-permute-start.11 = (bf16[32,1792]{1,0:T(8,128)(2,1)S(1)}, bf16[32,1792]{1,0:T(8,128)(2,1)S(1)}, u32[]{:S(2)}, u32[]{:S(2)}) collective-permute-start(bf16[32,1792]{1,0:T(8,128)(2,1)S(1)} %get-tuple-element.161), channel_id=1, source_target_pairs={{0,4},{1,5},{4,8},{5,9},{8,12},{9,13},{12,14},{13,15},{14,10},{15,... | collective-permute-start | bytes 344072 | tf_op jit(solution)/shard_map/ppermute | solution.py:79
  39.2 9.1 %collective-permute-start.15 = (bf16[128,3584]{1,0:T(8,128)(2,1)S(1)}, bf16[128,3584]{1,0:T(8,128)(2,1)S(1)}, u32[]{:S(2)}, u32[]{:S(2)}) collective-permute-start(bf16[128,3584]{1,0:T(8,128)(2,1)S(1)} %get-tuple-element.99), channel_id=1, source_target_pairs={{0,1},{1,0},{2,3},{3,2},{4,5},{5,4},{6,7},{7,6},{8,9},{9,8},{10,11... | collective-permute-start | bytes 2752520 | tf_op jit(solution)/shard_map/ppermute | solution.py:37
  39.4 8.1 %collective-permute-start.19 = (bf16[32,3584]{1,0:T(8,128)(2,1)S(1)}, bf16[32,3584]{1,0:T(8,128)(2,1)S(1)}, u32[]{:S(2)}, u32[]{:S(2)}) collective-permute-start(bf16[32,3584]{1,0:T(8,128)(2,1)S(1)} %get-tuple-element.148), channel_id=1, source_target_pairs={{0,2},{1,3},{4,0},{5,1},{8,4},{9,5},{12,8},{13,9},{14,12},{15,13},... | collective-permute-start | bytes 688136 | tf_op jit(solution)/shard_map/ppermute | solution.py:79
  40.3 8.2 %collective-permute-start.16 = (bf16[32,3584]{1,0:T(8,128)(2,1)S(1)}, bf16[32,3584]{1,0:T(8,128)(2,1)S(1)}, u32[]{:S(2)}, u32[]{:S(2)}) collective-permute-start(bf16[32,3584]{1,0:T(8,128)(2,1)S(1)} %get-tuple-element.150), channel_id=1, source_target_pairs={{0,4},{1,5},{4,8},{5,9},{8,12},{9,13},{12,14},{13,15},{14,10},{15,... | collective-permute-start | bytes 688136 | tf_op jit(solution)/shard_map/ppermute | solution.py:79
  47.5 12.2 %collective-permute-start.20 = (bf16[64,3584]{1,0:T(8,128)(2,1)S(1)}, bf16[64,3584]{1,0:T(8,128)(2,1)S(1)}, u32[]{:S(2)}, u32[]{:S(2)}) collective-permute-start(bf16[64,3584]{1,0:T(8,128)(2,1)S(1)} %fusion.2), channel_id=1, source_target_pairs={{0,2},{1,3},{4,0},{5,1},{8,4},{9,5},{12,8},{13,9},{14,12},{15,13},... | collective-permute-start | bytes 1376264 | tf_op jit(solution)/shard_map/ppermute | solution.py:79
  48.6 12.0 %collective-permute-start.17 = (bf16[64,3584]{1,0:T(8,128)(2,1)S(1)}, bf16[64,3584]{1,0:T(8,128)(2,1)S(1)}, u32[]{:S(2)}, u32[]{:S(2)}) collective-permute-start(bf16[64,3584]{1,0:T(8,128)(2,1)S(1)} %fusion), channel_id=1, source_target_pairs={{0,4},{1,5},{4,8},{5,9},{8,12},{9,13},{12,14},{13,15},{14,10},{15,... | collective-permute-start | bytes 1376264 | tf_op jit(solution)/shard_map/ppermute | solution.py:79
  59.8 11.3 %collective-permute-start.21 = (bf16[64,3584]{1,0:T(8,128)(2,1)S(1)}, bf16[64,3584]{1,0:T(8,128)(2,1)S(1)}, u32[]{:S(2)}, u32[]{:S(2)}) collective-permute-start(bf16[64,3584]{1,0:T(8,128)(2,1)S(1)} %fusion.3), channel_id=1, source_target_pairs={{0,2},{1,3},{4,0},{5,1},{8,4},{9,5},{12,8},{13,9},{14,12},{15,13},... | collective-permute-start | bytes 1376264 | tf_op jit(solution)/shard_map/ppermute | solution.py:79
  60.7 11.0 %collective-permute-start.18 = (bf16[64,3584]{1,0:T(8,128)(2,1)S(1)}, bf16[64,3584]{1,0:T(8,128)(2,1)S(1)}, u32[]{:S(2)}, u32[]{:S(2)}) collective-permute-start(bf16[64,3584]{1,0:T(8,128)(2,1)S(1)} %fusion.1), channel_id=1, source_target_pairs={{0,4},{1,5},{4,8},{5,9},{8,12},{9,13},{12,14},{13,15},{14,10},{15,... | collective-permute-start | bytes 1376264 | tf_op jit(solution)/shard_map/ppermute | solution.py:79
  73.4 10.7 %collective-permute-start.22 = (bf16[64,3584]{1,0:T(8,128)(2,1)S(1)}, bf16[64,3584]{1,0:T(8,128)(2,1)S(1)}, u32[]{:S(2)}, u32[]{:S(2)}) collective-permute-start(bf16[64,3584]{1,0:T(8,128)(2,1)S(1)} %bitcast.6), channel_id=1, source_target_pairs={{0,4},{1,5},{4,8},{5,9},{8,12},{9,13},{12,14},{13,15},{14,10},{15,... | collective-permute-start | bytes 1376264 | tf_op jit(solution)/shard_map/ppermute | solution.py:79
  74.7 10.7 %collective-permute-start.24 = (bf16[64,3584]{1,0:T(8,128)(2,1)S(1)}, bf16[64,3584]{1,0:T(8,128)(2,1)S(1)}, u32[]{:S(2)}, u32[]{:S(2)}) collective-permute-start(bf16[64,3584]{1,0:T(8,128)(2,1)S(1)} %bitcast.7), channel_id=1, source_target_pairs={{0,2},{1,3},{4,0},{5,1},{8,4},{9,5},{12,8},{13,9},{14,12},{15,13},... | collective-permute-start | bytes 1376264 | tf_op jit(solution)/shard_map/ppermute | solution.py:79
  78.0 8.6 %collective-permute-start.25 = (bf16[64,3584]{1,0:T(8,128)(2,1)S(1)}, bf16[64,3584]{1,0:T(8,128)(2,1)S(1)}, u32[]{:S(2)}, u32[]{:S(2)}) collective-permute-start(bf16[64,3584]{1,0:T(8,128)(2,1)S(1)} %bitcast.8), channel_id=1, source_target_pairs={{0,1},{1,0},{2,3},{3,2},{4,5},{5,4},{6,7},{7,6},{8,9},{9,8},{10,11... | collective-permute-start | bytes 1376264 | tf_op jit(solution)/shard_map/ppermute | solution.py:37
  84.1 10.7 %collective-permute-start.23 = (bf16[64,3584]{1,0:T(8,128)(2,1)S(1)}, bf16[64,3584]{1,0:T(8,128)(2,1)S(1)}, u32[]{:S(2)}, u32[]{:S(2)}) collective-permute-start(bf16[64,3584]{1,0:T(8,128)(2,1)S(1)} %collective-permute-done.22.refs_0_), channel_id=1, source_target_pairs={{0,4},{1,5},{4,8},{5,9},{8,12},{9,13},{12,14},{13,15},{14,10},{15,... | collective-permute-start | bytes 1376264 | tf_op jit(solution)/shard_map/ppermute | solution.py:79
  85.4 10.7 %collective-permute-start.27 = (bf16[64,3584]{1,0:T(8,128)(2,1)S(1)}, bf16[64,3584]{1,0:T(8,128)(2,1)S(1)}, u32[]{:S(2)}, u32[]{:S(2)}) collective-permute-start(bf16[64,3584]{1,0:T(8,128)(2,1)S(1)} %collective-permute-done.24.refs_1_), channel_id=1, source_target_pairs={{0,2},{1,3},{4,0},{5,1},{8,4},{9,5},{12,8},{13,9},{14,12},{15,13},... | collective-permute-start | bytes 1376264 | tf_op jit(solution)/shard_map/ppermute | solution.py:79
  86.1 10.7 %collective-permute-start.29 = (bf16[64,3584]{1,0:T(8,128)(2,1)S(1)}, bf16[64,3584]{1,0:T(8,128)(2,1)S(1)}, u32[]{:S(2)}, u32[]{:S(2)}) collective-permute-start(bf16[64,3584]{1,0:T(8,128)(2,1)S(1)} %collective-permute-done.24.refs_1_), channel_id=1, source_target_pairs={{0,1},{1,0},{2,3},{3,2},{4,5},{5,4},{6,7},{7,6},{8,9},{9,8},{10,11... | collective-permute-start | bytes 1376264 | tf_op jit(solution)/shard_map/ppermute | solution.py:37
  86.1 11.2 %collective-permute-start.28 = (bf16[64,3584]{1,0:T(8,128)(2,1)S(1)}, bf16[64,3584]{1,0:T(8,128)(2,1)S(1)}, u32[]{:S(2)}, u32[]{:S(2)}) collective-permute-start(bf16[64,3584]{1,0:T(8,128)(2,1)S(1)} %collective-permute-done.22.refs_0_), channel_id=1, source_target_pairs={{0,1},{1,0},{2,3},{3,2},{4,5},{5,4},{6,7},{7,6},{8,9},{9,8},{10,11... | collective-permute-start | bytes 1376264 | tf_op jit(solution)/shard_map/ppermute | solution.py:37
  94.8 10.3 %collective-permute-start.26 = (bf16[64,3584]{1,0:T(8,128)(2,1)S(1)}, bf16[64,3584]{1,0:T(8,128)(2,1)S(1)}, u32[]{:S(2)}, u32[]{:S(2)}) collective-permute-start(bf16[64,3584]{1,0:T(8,128)(2,1)S(1)} %collective-permute-done.23.refs_0_), channel_id=1, source_target_pairs={{0,4},{1,5},{4,8},{5,9},{8,12},{9,13},{12,14},{13,15},{14,10},{15,... | collective-permute-start | bytes 1376264 | tf_op jit(solution)/shard_map/ppermute | solution.py:79
  96.1 10.5 %collective-permute-start.31 = (bf16[64,3584]{1,0:T(8,128)(2,1)S(1)}, bf16[64,3584]{1,0:T(8,128)(2,1)S(1)}, u32[]{:S(2)}, u32[]{:S(2)}) collective-permute-start(bf16[64,3584]{1,0:T(8,128)(2,1)S(1)} %collective-permute-done.27.refs_1_), channel_id=1, source_target_pairs={{0,2},{1,3},{4,0},{5,1},{8,4},{9,5},{12,8},{13,9},{14,12},{15,13},... | collective-permute-start | bytes 1376264 | tf_op jit(solution)/shard_map/ppermute | solution.py:79
  96.8 10.6 %collective-permute-start.35 = (bf16[64,3584]{1,0:T(8,128)(2,1)S(1)}, bf16[64,3584]{1,0:T(8,128)(2,1)S(1)}, u32[]{:S(2)}, u32[]{:S(2)}) collective-permute-start(bf16[64,3584]{1,0:T(8,128)(2,1)S(1)} %collective-permute-done.27.refs_1_), channel_id=1, source_target_pairs={{0,1},{1,0},{2,3},{3,2},{4,5},{5,4},{6,7},{7,6},{8,9},{9,8},{10,11... | collective-permute-start | bytes 1376264 | tf_op jit(solution)/shard_map/ppermute | solution.py:37
  96.8 11.1 %collective-permute-start.34 = (bf16[64,3584]{1,0:T(8,128)(2,1)S(1)}, bf16[64,3584]{1,0:T(8,128)(2,1)S(1)}, u32[]{:S(2)}, u32[]{:S(2)}) collective-permute-start(bf16[64,3584]{1,0:T(8,128)(2,1)S(1)} %collective-permute-done.23.refs_0_), channel_id=1, source_target_pairs={{0,1},{1,0},{2,3},{3,2},{4,5},{5,4},{6,7},{7,6},{8,9},{9,8},{10,11... | collective-permute-start | bytes 1376264 | tf_op jit(solution)/shard_map/ppermute | solution.py:37
  105.1 6.1 %collective-permute-start.33 = (bf16[64,1792]{1,0:T(8,128)(2,1)S(1)}, bf16[64,1792]{1,0:T(8,128)(2,1)S(1)}, u32[]{:S(2)}, u32[]{:S(2)}) collective-permute-start(bf16[64,1792]{1,0:T(8,128)(2,1)S(1)} %slice.134), channel_id=1, source_target_pairs={{0,4},{1,5},{4,8},{5,9},{8,12},{9,13},{12,14},{13,15},{14,10},{15,... | collective-permute-start | bytes 688136 | tf_op jit(solution)/shard_map/ppermute | solution.py:79
  106.6 6.1 %collective-permute-start.37 = (bf16[64,1792]{1,0:T(8,128)(2,1)S(1)}, bf16[64,1792]{1,0:T(8,128)(2,1)S(1)}, u32[]{:S(2)}, u32[]{:S(2)}) collective-permute-start(bf16[64,1792]{1,0:T(8,128)(2,1)S(1)} %slice.135), channel_id=1, source_target_pairs={{0,2},{1,3},{4,0},{5,1},{8,4},{9,5},{12,8},{13,9},{14,12},{15,13},... | collective-permute-start | bytes 688136 | tf_op jit(solution)/shard_map/ppermute | solution.py:79
  107.4 6.8 %collective-permute-start.32 = (bf16[64,3584]{1,0:T(8,128)(2,1)S(1)}, bf16[64,3584]{1,0:T(8,128)(2,1)S(1)}, u32[]{:S(2)}, u32[]{:S(2)}) collective-permute-start(bf16[64,3584]{1,0:T(8,128)(2,1)S(1)} %collective-permute-done.31.refs_1_), channel_id=1, source_target_pairs={{0,1},{1,0},{2,3},{3,2},{4,5},{5,4},{6,7},{7,6},{8,9},{9,8},{10,11... | collective-permute-start | bytes 1376264 | tf_op jit(solution)/shard_map/ppermute | solution.py:37
  107.4 6.8 %collective-permute-start.30 = (bf16[64,3584]{1,0:T(8,128)(2,1)S(1)}, bf16[64,3584]{1,0:T(8,128)(2,1)S(1)}, u32[]{:S(2)}, u32[]{:S(2)}) collective-permute-start(bf16[64,3584]{1,0:T(8,128)(2,1)S(1)} %collective-permute-done.26.refs_0_), channel_id=1, source_target_pairs={{0,1},{1,0},{2,3},{3,2},{4,5},{5,4},{6,7},{7,6},{8,9},{9,8},{10,11... | collective-permute-start | bytes 1376264 | tf_op jit(solution)/shard_map/ppermute | solution.py:37
  (19 other events, 271.9 us)

commit v18 on v8

--- a/solution.py
+++ b/solution.py
@@ -196,7 +196,7 @@
             pltpu.SemaphoreType.DMA((pieces, cuts)),
             pltpu.SemaphoreType.DMA((pieces, 4)),
         ],
-        compiler_params=params(56),
+        compiler_params=params(50),
         cost_estimate=cost(
             2 * latents * tokens * width, 2 * (tokens * width + latents * (tokens + width))
         ),
@@ -263,63 +263,57 @@
     return sum(value[begin : begin + rows].astype(jnp.float32) for value in pair)
 
 
-def read_gradient(refs):
-    return sum(ref[...].astype(jnp.float32) for ref in refs)
-
-
-def enc_kernel(code_ref, w_ref, m_ref, v_ref, *refs):
-    parts, (w_out, m_out, v_out, block, fresh) = refs[:-5], refs[-5:]
-    gradient = read_gradient(parts)
-    reset = code_ref[...] != KEPT
-    w, m, v = adam_update(w_ref[...], m_ref[...], v_ref[...], gradient)
-    w = jnp.where(reset, reset_gain * gradient * inverse_rms(gradient), w)
-    w_out[...] = w
-    m_out[...] = jnp.where(reset, 0.0, m)
-    v_out[...] = jnp.where(reset, 0.0, v)
-    block[...] = w.astype(block.dtype)
-    fresh[...] = gradient.astype(fresh.dtype)
-
-
-def dec_kernel(code_ref, w_ref, m_ref, v_ref, fresh_ref, enc_block, *refs):
-    parts, (w_out, m_out, v_out, blocks) = refs[:-4], refs[-4:]
-    reset = code_ref[...] != KEPT
-    w, m, v = adam_update(w_ref[...], m_ref[...], v_ref[...], read_gradient(parts))
-    w = jnp.where(reset, fresh_ref[...].astype(jnp.float32), w)
-    w = w * inverse_rms(w)
-    w_out[...] = w
-    m_out[...] = jnp.where(reset, 0.0, m)
-    v_out[...] = jnp.where(reset, 0.0, v)
-    blocks[0] = enc_block[...]
-    blocks[1] = w.astype(blocks.dtype)
-
-
-def update(kernel, code, states, others, parts, last_shapes, name):
+def updated(refs):
+    code, states, terms = refs[0], refs[1:7], refs[7:15]
+    reset = code[...] != KEPT
+    enc_grad, dec_grad = (
+        sum(ref[...].astype(jnp.float32) for ref in half) for half in (terms[:4], terms[4:])
+    )
+    enc = adam_update(*(ref[...] for ref in states[:3]), enc_grad)
+    dec = adam_update(*(ref[...] for ref in states[3:]), dec_grad)
+    enc_w = jnp.where(reset, reset_gain * enc_grad * inverse_rms(enc_grad), enc[0])
+    dec_w = jnp.where(reset, enc_grad, dec[0])
+    dec_w = dec_w * inverse_rms(dec_w)
+    moments = [jnp.where(reset, 0.0, value) for value in enc[1:] + dec[1:]]
+    return [enc_w] + moments[:2] + [dec_w] + moments[2:]
+
+
+def blocks_kernel(*refs):
+    results, blocks = updated(refs), refs[-1]
+    blocks[0] = results[0].astype(blocks.dtype)
+    blocks[1] = results[3].astype(blocks.dtype)
+
+
+def states_kernel(*refs):
+    for ref, value in zip(refs[-6:], updated(refs)):
+        ref[...] = value
+
+
+def update(code, states, enc_parts, dec_parts, blocks_only):
     rows, width = states[0].shape
     tile = 16
 
-    def last_rows(value):
-        skipped = (value.shape[0] - rows) // tile
-        return pl.BlockSpec((tile, value.shape[1]), lambda i: (i + skipped, 0))
-
-    operands = [code] + list(states) + list(others) + list(parts)
-    out_shape = [jax.ShapeDtypeStruct((rows, width), jnp.float32)] * 3
-    out_specs = [pl.BlockSpec((tile, width), lambda i: (i, 0))] * 3
-    for pair in last_shapes:
-        lead = (2,) if pair else ()
-        out_shape.append(jax.ShapeDtypeStruct(lead + (rows, width), jnp.bfloat16))
-        out_specs.append(
-            pl.BlockSpec(lead + (tile, width), lambda i, pair=pair: (0, i, 0) if pair else (i, 0))
-        )
+    def row_tile(value, skipped):
+        return pl.BlockSpec((tile, value.shape[1]), lambda i: (i + skipped // tile, 0))
+
+    operands = [(value, 0) for value in [code] + list(states)]
+    operands += [(value, value.shape[0] - rows) for value in enc_parts + dec_parts]
+    if blocks_only:
+        out_shape = [jax.ShapeDtypeStruct((2, rows, width), jnp.bfloat16)]
+        out_specs = [pl.BlockSpec((2, tile, width), lambda i: (0, i, 0))]
+    else:
+        out_shape = [jax.ShapeDtypeStruct((rows, width), jnp.float32)] * 6
+        out_specs = [pl.BlockSpec((tile, width), lambda i: (i, 0))] * 6
     return pl.pallas_call(
-        kernel,
+        blocks_kernel if blocks_only else states_kernel,
         grid=(rows // tile,),
-        in_specs=[last_rows(value) for value in operands],
+        in_specs=[row_tile(*operand) for operand in operands],
         out_specs=out_specs,
         out_shape=out_shape,
-        cost_estimate=cost(40 * rows * width, 40 * rows * width),
-        compiler_params=params(12),
-        name=name,
-    )(*operands)
+        cost_estimate=cost(10 * rows * width, 10 * rows * width),
+        compiler_params=params(20),
+        name="blocks" if blocks_only else "states",
+    )(*(value for value, _ in operands))
 
 
 def place_kernel(plan, size, rows, count, *refs):
@@ -358,13 +352,13 @@
     )(*operands)
 
 
-def gathered(block, size, rows):
+def gathered(block, order, size, rows):
     chips = size // 2
     width = block.shape[1]
     half = width // 2
     hops = chips // 2
     right = left = block
-    near, far, wholes = [(0, 0, 0, block)], [], None
+    near, far, wholes = [(0, 0, 0, after(block, order))], [], None
     for hop in range(1, hops + 1):
         if hop == hops:
             right, left = right[:, :half], left[:, half:]
@@ -372,11 +366,12 @@
         sent = [(offset, 1, column, swap(value, 1, size)) for offset, _, column, value in near]
         wholes = place(near + far, wholes, size, rows, width)
         far = sent
-        right, left, wholes = lax.optimization_barrier((right, left, wholes))
+        right, wholes = tied(right, wholes)
+        left = after(left, right)
         near = [(-hop, 0, 0, right), (hop, 0, half if hop == hops else 0, left)]
     sent = [(offset, 1, column, swap(value, 1, size)) for offset, _, column, value in near]
-    wholes = place(near + far, wholes, size, rows, width)
-    return place(sent, wholes, size, rows, width)
+    wholes = place(near, wholes, size, rows, width)
+    return place(far + sent, wholes, size, rows, width)
 
 
 def shards(
@@ -440,26 +435,12 @@
         enc_moving = advance(enc_came, enc_kept, enc_core, hop)
         enc_came = travel(enc_moving)
         dec_came = after(dec_came, *enc_moving)
-    enc_out, enc_mo, enc_vo, enc_block, fresh = update(
-        enc_kernel,
-        code,
-        (enc_w, enc_m, enc_v),
-        (),
-        [enc_kept[1], enc_core[1]] + enc_came,
-        (False, False),
-        "enc_update",
-    )
-    dec_out, dec_mo, dec_vo, blocks = update(
-        dec_kernel,
-        code,
-        (dec_w, dec_m, dec_v),
-        (fresh, enc_block),
-        [dec_kept[1], dec_core[1]] + dec_came,
-        (True,),
-        "dec_update",
-    )
-    enc_full, dec_full = gathered(blocks.reshape(2 * rows, width), size, rows)
-    return (enc_out, enc_mo, enc_vo, dec_out, dec_mo, dec_vo, enc_full, dec_full)
+    states = (enc_w, enc_m, enc_v, dec_w, dec_m, dec_v)
+    parts = ([enc_kept[1], enc_core[1]] + enc_came, [dec_kept[1], dec_core[1]] + dec_came)
+    (blocks,) = update(code, states, *parts, True)
+    results = update(code, after(states, blocks), *parts, False)
+    enc_full, dec_full = gathered(blocks.reshape(2 * rows, width), results[0], size, rows)
+    return (*results, enc_full, dec_full)
 
 
 def solution(mesh):

time: 119 us -> 110 us (0.924)
  waiting for transfers between devices: 52.4 us -> 45.5 us
  local copies, waits for them, and re-layouts: 1.35 us -> 0.13 us
    ppermute x24, waiting for transfers between devices: 50.3 us -> 41.9 us  [shift(): return lax.ppermute(value, 'latent', pairs)]
    ppermute x19, waiting for transfers between devices: 2.1 us -> 3.57 us  [swap(): return lax.ppermute(value, 'latent', [(i, i ^ bits) for i in range(size)])]
    unnamed x28 -> x24, local copies, waits for them, and re-layouts: 1.28 us -> 0.07 us
  transfers between devices with their start and end apart: 43 -> 43, of which waited for: 21 -> 20; matrix products, arithmetic and copies ran while one was open for 2% -> 1% of each run, Pallas kernels for 18% -> 21%
where the time goes in v18:
time: 110 us
  waiting for transfers between devices  45.5 us (41%)
  starting transfers between devices  35.1 us (32%)
  Pallas kernels  26 us (24%)
  other arithmetic  2.04 us (2%)
    ppermute x24, waiting for transfers between devices, shift(): return lax.ppermute(value, 'latent', pairs)  41.9 us
    ppermute x24, starting transfers between devices, shift(): return lax.ppermute(value, 'latent', pairs)  24.9 us
    ppermute x19, starting transfers between devices, swap(): return lax.ppermute(value, 'latent', [(i, i ^ bits) for i in range(size)])  10.2 us
    pallas_call x1, Pallas kernels, stream_product(): pl.pallas_call(functools.partial(stream_kernel, size, rows), in_specs=[pl...  8.36 us
    pallas_call x1, Pallas kernels, select_product(): pl.pallas_call(functools.partial(select_kernel, size, rows, len(table)),...  7.01 us
    pallas_call x6, Pallas kernels, place(): pl.pallas_call(functools.partial(place_kernel, plan, size, rows, count),...  6.39 us
    pallas_call x2, Pallas kernels, update(): pl.pallas_call(blocks_kernel if blocks_only else states_kernel, grid=(row...  4.2 us
    ppermute x19, waiting for transfers between devices, swap(): return lax.ppermute(value, 'latent', [(i, i ^ bits) for i in range(size)])  3.57 us
  transfers between devices with their start and end apart: 43, of which 20 were waited for; matrix products, arithmetic and copies ran while one was open for 1% of the time, Pallas kernels for 21%

profile of v18, /device:TPU:0, one launch (start us, length us, event | category | flops | bytes accessed | tf_op | source)
XLA Modules:
  0.0 109.7 jit_solution(10289291498743036727)
XLA Ops:
  1.6 2.5 %collective-permute-start.2 = (s32[1,48]{1,0:T(1,128)S(1)}, s32[1,48]{1,0:T(1,128)S(1)}, u32[]{:S(2)}, u32[]{:S(2)}) collective-permute-start(s32[1,48]{1,0:T(1,128)S(1)} %pad_add_fusion.1), channel_id=1, source_target_pairs={{0,3},{1,2},{2,1},{3,0},{4,7},{5,6},{6,5},{7,4},{8,11},{9,10},{10,... | collective-permute-start | bytes 584 | tf_op jit(solution)/shard_map/ppermute | solution.py:37
  4.7 8.4 %product.1 = (bf16[128,3584]{1,0:T(8,128)(2,1)S(1)}, bf16[128,3584]{1,0:T(8,128)(2,1)S(1)}, bf16[128,3584]{1,0:T(8,128)(2,1)S(1)}, bf16[128,3584]{1,0:T(8,128)(2,1)S(1)}) custom-call(bf16[1024,512]{1,0:T(8,128)(2,1)} %coef_ref.1, bf16[1024,3584]{1,0:T(8,128)(2,1)} %right_hbm.1), custom_call_target="tpu_custom_call" | custom-call | flops 3758096384 | bytes 12058624 | tf_op jit(solution)/shard_map/product/pallas_call | solution.py:186
  13.8 3.8 %collective-permute-start.7 = (s32[4,48]{1,0:T(4,128)S(1)}, s32[4,48]{1,0:T(4,128)S(1)}, u32[]{:S(2)}, u32[]{:S(2)}) collective-permute-start(s32[4,48]{1,0:T(4,128)S(1)} %pad_add_fusion.refs_0_), channel_id=1, source_target_pairs={{0,12},{1,13},{2,14},{3,15},{4,8},{5,9},{6,10},{7,11},{8,4},{9,5},... | collective-permute-start | bytes 2312 | tf_op jit(solution)/shard_map/ppermute | solution.py:37
  18.3 1.8 %collective-permute-start.10 = (bf16[32,1792]{1,0:T(8,128)(2,1)S(1)}, bf16[32,1792]{1,0:T(8,128)(2,1)S(1)}, u32[]{:S(2)}, u32[]{:S(2)}) collective-permute-start(bf16[32,1792]{1,0:T(8,128)(2,1)S(1)} %get-tuple-element.158), channel_id=1, source_target_pairs={{0,2},{1,3},{4,0},{5,1},{8,4},{9,5},{12,8},{13,9},{14,12},{15,13},... | collective-permute-start | bytes 344072 | tf_op jit(solution)/shard_map/ppermute | solution.py:79
  20.3 1.8 %collective-permute-done.6.refs_2_ = s32[4,48]{1,0:T(4,128)S(1)} collective-permute-done((s32[4,48]{1,0:T(4,128)S(1)}, s32[4,48]{1,0:T(4,128)S(1)}, u32[]{:S(2)}, u32[]{:S(2)}) %collective-permute-start.6) | collective-permute-done | bytes 800 | tf_op jit(solution)/shard_map/ppermute | solution.py:37
  22.2 7.0 %select_product.1 = (bf16[128,3584]{1,0:T(8,128)(2,1)S(1)}, bf16[128,3584]{1,0:T(8,128)(2,1)S(1)}, bf16[128,3584]{1,0:T(8,128)(2,1)S(1)}, bf16[128,3584]{1,0:T(8,128)(2,1)S(1)}, s32[32,1]{1,0:T(8,128)S(1)}) custom-call(bf16[1024,512]{1,0:T(8,128)(2,1)S(1)} %copy-done.6, bf16[1024,3584]{1,0:T(8,128)(2,1)S(1)} %bitcast.9, s32[2,16]{1,0:T(2,128)S(1)} %bitcast.10, ...), custom_call_target="tpu_custom_call" | custom-call | flops 3758096384 | bytes 12058624 | tf_op jit(solution)/shard_map/select_product/pallas_call | solution.py:237
  29.9 1.6 %collective-permute-start.15 = (bf16[32,3584]{1,0:T(8,128)(2,1)S(1)}, bf16[32,3584]{1,0:T(8,128)(2,1)S(1)}, u32[]{:S(2)}, u32[]{:S(2)}) collective-permute-start(bf16[32,3584]{1,0:T(8,128)(2,1)S(1)} %get-tuple-element.154), channel_id=1, source_target_pairs={{0,2},{1,3},{4,0},{5,1},{8,4},{9,5},{12,8},{13,9},{14,12},{15,13},... | collective-permute-start | bytes 688136 | tf_op jit(solution)/shard_map/ppermute | solution.py:79
  33.1 1.6 %collective-permute-start.13 = (bf16[32,1792]{1,0:T(8,128)(2,1)S(1)}, bf16[32,1792]{1,0:T(8,128)(2,1)S(1)}, u32[]{:S(2)}, u32[]{:S(2)}) collective-permute-start(bf16[32,1792]{1,0:T(8,128)(2,1)S(1)} %get-tuple-element.156), channel_id=1, source_target_pairs={{0,2},{1,3},{4,0},{5,1},{8,4},{9,5},{12,8},{13,9},{14,12},{15,13},... | collective-permute-start | bytes 344072 | tf_op jit(solution)/shard_map/ppermute | solution.py:79
  35.2 3.2 %collective-permute-done.15 = bf16[32,3584]{1,0:T(8,128)(2,1)S(1)} collective-permute-done((bf16[32,3584]{1,0:T(8,128)(2,1)S(1)}, bf16[32,3584]{1,0:T(8,128)(2,1)S(1)}, u32[]{:S(2)}, u32[]{:S(2)}) %collective-permute-start.15) | collective-permute-done | bytes 229408 | tf_op jit(solution)/shard_map/ppermute | solution.py:79
  38.4 1.6 %collective-permute-done.14 = bf16[32,3584]{1,0:T(8,128)(2,1)S(1)} collective-permute-done((bf16[32,3584]{1,0:T(8,128)(2,1)S(1)}, bf16[32,3584]{1,0:T(8,128)(2,1)S(1)}, u32[]{:S(2)}, u32[]{:S(2)}) %collective-permute-start.14) | collective-permute-done | bytes 229408 | tf_op jit(solution)/shard_map/ppermute | solution.py:79
  40.8 1.6 %collective-permute-start.19 = (bf16[32,3584]{1,0:T(8,128)(2,1)S(1)}, bf16[32,3584]{1,0:T(8,128)(2,1)S(1)}, u32[]{:S(2)}, u32[]{:S(2)}) collective-permute-start(bf16[32,3584]{1,0:T(8,128)(2,1)S(1)} %add_convert_fusion.8), channel_id=1, source_target_pairs={{0,2},{1,3},{4,0},{5,1},{8,4},{9,5},{12,8},{13,9},{14,12},{15,13},... | collective-permute-start | bytes 688136 | tf_op jit(solution)/shard_map/ppermute | solution.py:79
  43.1 1.6 %collective-permute-start.16 = (bf16[32,3584]{1,0:T(8,128)(2,1)S(1)}, bf16[32,3584]{1,0:T(8,128)(2,1)S(1)}, u32[]{:S(2)}, u32[]{:S(2)}) collective-permute-start(bf16[32,3584]{1,0:T(8,128)(2,1)S(1)} %get-tuple-element.153), channel_id=1, source_target_pairs={{0,4},{1,5},{4,8},{5,9},{8,12},{9,13},{12,14},{13,15},{14,10},{15,... | collective-permute-start | bytes 688136 | tf_op jit(solution)/shard_map/ppermute | solution.py:79
  44.6 4.0 %collective-permute-done.18 = bf16[32,3584]{1,0:T(8,128)(2,1)S(1)} collective-permute-done((bf16[32,3584]{1,0:T(8,128)(2,1)S(1)}, bf16[32,3584]{1,0:T(8,128)(2,1)S(1)}, u32[]{:S(2)}, u32[]{:S(2)}) %collective-permute-start.18) | collective-permute-done | bytes 229408 | tf_op jit(solution)/shard_map/ppermute | solution.py:79
  48.8 2.0 %collective-permute-done.17 = bf16[32,3584]{1,0:T(8,128)(2,1)S(1)} collective-permute-done((bf16[32,3584]{1,0:T(8,128)(2,1)S(1)}, bf16[32,3584]{1,0:T(8,128)(2,1)S(1)}, u32[]{:S(2)}, u32[]{:S(2)}) %collective-permute-start.17) | collective-permute-done | bytes 229408 | tf_op jit(solution)/shard_map/ppermute | solution.py:79
  52.2 1.3 %collective-permute-start.22 = (bf16[32,3584]{1,0:T(8,128)(2,1)S(1)}, bf16[32,3584]{1,0:T(8,128)(2,1)S(1)}, u32[]{:S(2)}, u32[]{:S(2)}) collective-permute-start(bf16[32,3584]{1,0:T(8,128)(2,1)S(1)} %add_convert_fusion.1), channel_id=1, source_target_pairs={{0,2},{1,3},{4,0},{5,1},{8,4},{9,5},{12,8},{13,9},{14,12},{15,13},... | collective-permute-start | bytes 688136 | tf_op jit(solution)/shard_map/ppermute | solution.py:79
  53.4 1.2 %collective-permute-start.25 = (bf16[32,3584]{1,0:T(8,128)(2,1)S(1)}, bf16[32,3584]{1,0:T(8,128)(2,1)S(1)}, u32[]{:S(2)}, u32[]{:S(2)}) collective-permute-start(bf16[32,3584]{1,0:T(8,128)(2,1)S(1)} %get-tuple-element.150), channel_id=1, source_target_pairs={{0,2},{1,3},{4,0},{5,1},{8,4},{9,5},{12,8},{13,9},{14,12},{15,13},... | collective-permute-start | bytes 688136 | tf_op jit(solution)/shard_map/ppermute | solution.py:79
  55.5 4.2 %collective-permute-done.20 = bf16[32,3584]{1,0:T(8,128)(2,1)S(1)} collective-permute-done((bf16[32,3584]{1,0:T(8,128)(2,1)S(1)}, bf16[32,3584]{1,0:T(8,128)(2,1)S(1)}, u32[]{:S(2)}, u32[]{:S(2)}) %collective-permute-start.20) | collective-permute-done | bytes 229408 | tf_op jit(solution)/shard_map/ppermute | solution.py:79
  60.9 1.3 %collective-permute-start.23 = (bf16[32,3584]{1,0:T(8,128)(2,1)S(1)}, bf16[32,3584]{1,0:T(8,128)(2,1)S(1)}, u32[]{:S(2)}, u32[]{:S(2)}) collective-permute-start(bf16[32,3584]{1,0:T(8,128)(2,1)S(1)} %get-tuple-element.148), channel_id=1, source_target_pairs={{0,2},{1,3},{4,0},{5,1},{8,4},{9,5},{12,8},{13,9},{14,12},{15,13},... | collective-permute-start | bytes 688136 | tf_op jit(solution)/shard_map/ppermute | solution.py:79
  63.0 1.6 %collective-permute-done.25.refs_14_ = bf16[32,3584]{1,0:T(8,128)(2,1)S(1)} collective-permute-done((bf16[32,3584]{1,0:T(8,128)(2,1)S(1)}, bf16[32,3584]{1,0:T(8,128)(2,1)S(1)}, u32[]{:S(2)}, u32[]{:S(2)}) %collective-permute-start.25) | collective-permute-done | bytes 229408 | tf_op jit(solution)/shard_map/ppermute | solution.py:79
  64.6 2.5 %collective-permute-done.23.refs_10_ = bf16[32,3584]{1,0:T(8,128)(2,1)S(1)} collective-permute-done((bf16[32,3584]{1,0:T(8,128)(2,1)S(1)}, bf16[32,3584]{1,0:T(8,128)(2,1)S(1)}, u32[]{:S(2)}, u32[]{:S(2)}) %collective-permute-start.23) | collective-permute-done | bytes 229408 | tf_op jit(solution)/shard_map/ppermute | solution.py:79
  67.1 1.2 %collective-permute-done.21.refs_9_ = bf16[32,3584]{1,0:T(8,128)(2,1)S(1)} collective-permute-done((bf16[32,3584]{1,0:T(8,128)(2,1)S(1)}, bf16[32,3584]{1,0:T(8,128)(2,1)S(1)}, u32[]{:S(2)}, u32[]{:S(2)}) %collective-permute-start.21) | collective-permute-done | bytes 229408 | tf_op jit(solution)/shard_map/ppermute | solution.py:79
  68.3 1.6 %blocks.1 = bf16[2,32,3584]{2,1,0:T(8,128)(2,1)S(1)} custom-call(s32[32,1]{1,0:T(8,128)S(1)} %get-tuple-element.85.refs_0_, f32[32,3584]{1,0:T(8,128)S(1)} %copy-done, f32[32,3584]{1,0:T(8,128)S(1)} %copy-done.1, f32[32,3584]{1,0:T(8,128)S(1)} %copy-done.2, f32[32,3584]{1,0:T(8,128)S(1)} %copy-done.3, f32[32,3584]{1,0:T(8,128)S(1)} %copy-done.4, ...), custom_call_target="tpu_custom_call" | custom-call | flops 1146880 | bytes 1146880 | tf_op jit(solution)/shard_map/blocks/pallas_call | solution.py:307
  69.9 1.2 %collective-permute-start.26 = (bf16[64,3584]{1,0:T(8,128)(2,1)S(1)}, bf16[64,3584]{1,0:T(8,128)(2,1)S(1)}, u32[]{:S(2)}, u32[]{:S(2)}) collective-permute-start(bf16[64,3584]{1,0:T(8,128)(2,1)S(1)} %bitcast.4), channel_id=1, source_target_pairs={{0,4},{1,5},{4,8},{5,9},{8,12},{9,13},{12,14},{13,15},{14,10},{15,... | collective-permute-start | bytes 1376264 | tf_op jit(solution)/shard_map/ppermute | solution.py:79
  72.0 2.6 %states.1 = (f32[32,3584]{1,0:T(8,128)}, f32[32,3584]{1,0:T(8,128)}, f32[32,3584]{1,0:T(8,128)}, f32[32,3584]{1,0:T(8,128)}, f32[32,3584]{1,0:T(8,128)}, /*index=5*/f32[32,3584]{1,0:T(8,128)}) custom-call(s32[32,1]{1,0:T(8,128)S(1)} %get-tuple-element.85.refs_0_, f32[32,3584]{1,0:T(8,128)S(1)} %copy-done, f32[32,3584]{1,0:T(8,128)S(1)} %copy-done.1, ...), custom_call_target="tpu_custom_call" | custom-call | flops 1146880 | bytes 1146880 | tf_op jit(solution)/shard_map/states/pallas_call | solution.py:307
  75.4 3.1 %collective-permute-done.26.refs_0_ = bf16[64,3584]{1,0:T(8,128)(2,1)S(1)} collective-permute-done((bf16[64,3584]{1,0:T(8,128)(2,1)S(1)}, bf16[64,3584]{1,0:T(8,128)(2,1)S(1)}, u32[]{:S(2)}, u32[]{:S(2)}) %collective-permute-start.26) | collective-permute-done | bytes 458784 | tf_op jit(solution)/shard_map/ppermute | solution.py:79
  82.3 6.9 %collective-permute-done.27.refs_0_ = bf16[64,3584]{1,0:T(8,128)(2,1)S(1)} collective-permute-done((bf16[64,3584]{1,0:T(8,128)(2,1)S(1)}, bf16[64,3584]{1,0:T(8,128)(2,1)S(1)}, u32[]{:S(2)}, u32[]{:S(2)}) %collective-permute-start.27) | collective-permute-done | bytes 458784 | tf_op jit(solution)/shard_map/ppermute | solution.py:79
  91.8 1.3 %place.8 = (bf16[512,3584]{1,0:T(8,128)(2,1)}, bf16[512,3584]{1,0:T(8,128)(2,1)}) custom-call(bf16[64,3584]{1,0:T(8,128)(2,1)S(1)} %collective-permute-done.27.refs_0_, bf16[64,3584]{1,0:T(8,128)(2,1)S(1)} %collective-permute-done.31.refs_1_, bf16[64,3584]{1,0:T(8,128)(2,1)S(1)} %collective-permute-done.32.refs_2_, ...), custom_call_target="tpu_custom_call", output_to_operand_aliasing={{0}: (4, {}), {1}: (5, {})} | custom-call | bytes 3670016 | tf_op jit(solution)/shard_map/place/pallas_call | solution.py:342
  93.1 6.7 %collective-permute-done.30.refs_0_ = bf16[64,3584]{1,0:T(8,128)(2,1)S(1)} collective-permute-done((bf16[64,3584]{1,0:T(8,128)(2,1)S(1)}, bf16[64,3584]{1,0:T(8,128)(2,1)S(1)}, u32[]{:S(2)}, u32[]{:S(2)}) %collective-permute-start.30) | collective-permute-done | bytes 458784 | tf_op jit(solution)/shard_map/ppermute | solution.py:79
  99.8 1.2 %collective-permute-start.37 = (bf16[64,1792]{1,0:T(8,128)(2,1)S(1)}, bf16[64,1792]{1,0:T(8,128)(2,1)S(1)}, u32[]{:S(2)}, u32[]{:S(2)}) collective-permute-start(bf16[64,1792]{1,0:T(8,128)(2,1)S(1)} %slice.134), channel_id=1, source_target_pairs={{0,4},{1,5},{4,8},{5,9},{8,12},{9,13},{12,14},{13,15},{14,10},{15,... | collective-permute-start | bytes 688136 | tf_op jit(solution)/shard_map/ppermute | solution.py:79
  102.5 1.3 %place.9 = (bf16[512,3584]{1,0:T(8,128)(2,1)}, bf16[512,3584]{1,0:T(8,128)(2,1)}) custom-call(bf16[64,3584]{1,0:T(8,128)(2,1)S(1)} %collective-permute-done.30.refs_0_, bf16[64,3584]{1,0:T(8,128)(2,1)S(1)} %collective-permute-done.35.refs_1_, bf16[64,3584]{1,0:T(8,128)(2,1)S(1)} %collective-permute-done.38.refs_2_, ...), custom_call_target="tpu_custom_call", output_to_operand_aliasing={{0}: (4, {}), {1}: (5, {})} | custom-call | bytes 3670016 | tf_op jit(solution)/shard_map/place/pallas_call | solution.py:342
  103.8 2.1 %collective-permute-done.37.refs_0_ = bf16[64,1792]{1,0:T(8,128)(2,1)S(1)} collective-permute-done((bf16[64,1792]{1,0:T(8,128)(2,1)S(1)}, bf16[64,1792]{1,0:T(8,128)(2,1)S(1)}, u32[]{:S(2)}, u32[]{:S(2)}) %collective-permute-start.37) | collective-permute-done | bytes 229408 | tf_op jit(solution)/shard_map/ppermute | solution.py:79
  105.9 1.2 %collective-permute-done.41.refs_1_ = bf16[64,1792]{1,0:T(8,128)(2,1)S(1)} collective-permute-done((bf16[64,1792]{1,0:T(8,128)(2,1)S(1)}, bf16[64,1792]{1,0:T(8,128)(2,1)S(1)}, u32[]{:S(2)}, u32[]{:S(2)}) %collective-permute-start.41) | collective-permute-done | bytes 229408 | tf_op jit(solution)/shard_map/ppermute | solution.py:79
  (105 shorter events, 24.2 us)
Async XLA Ops:
  1.6 11.5 %collective-permute-start.2 = (s32[1,48]{1,0:T(1,128)S(1)}, s32[1,48]{1,0:T(1,128)S(1)}, u32[]{:S(2)}, u32[]{:S(2)}) collective-permute-start(s32[1,48]{1,0:T(1,128)S(1)} %pad_add_fusion.1), channel_id=1, source_target_pairs={{0,3},{1,2},{2,1},{3,0},{4,7},{5,6},{6,5},{7,4},{8,11},{9,10},{10,... | collective-permute-start | bytes 584 | tf_op jit(solution)/shard_map/ppermute | solution.py:37
  4.0 9.1 %collective-permute-start.1 = (s32[1,48]{1,0:T(1,128)S(1)}, s32[1,48]{1,0:T(1,128)S(1)}, u32[]{:S(2)}, u32[]{:S(2)}) collective-permute-start(s32[1,48]{1,0:T(1,128)S(1)} %pad_add_fusion.1), channel_id=1, source_target_pairs={{0,2},{1,3},{2,0},{3,1},{4,6},{5,7},{6,4},{7,5},{8,10},{9,11},{10,... | collective-permute-start | bytes 584 | tf_op jit(solution)/shard_map/ppermute | solution.py:37
  4.7 8.4 %collective-permute-start = (s32[1,48]{1,0:T(1,128)S(1)}, s32[1,48]{1,0:T(1,128)S(1)}, u32[]{:S(2)}, u32[]{:S(2)}) collective-permute-start(s32[1,48]{1,0:T(1,128)S(1)} %pad_add_fusion.1), channel_id=1, source_target_pairs={{0,1},{1,0},{2,3},{3,2},{4,5},{5,4},{6,7},{7,6},{8,9},{9,8},{10,11... | collective-permute-start | bytes 584 | tf_op jit(solution)/shard_map/ppermute | solution.py:37
  13.8 6.6 %collective-permute-start.7 = (s32[4,48]{1,0:T(4,128)S(1)}, s32[4,48]{1,0:T(4,128)S(1)}, u32[]{:S(2)}, u32[]{:S(2)}) collective-permute-start(s32[4,48]{1,0:T(4,128)S(1)} %pad_add_fusion.refs_0_), channel_id=1, source_target_pairs={{0,12},{1,13},{2,14},{3,15},{4,8},{5,9},{6,10},{7,11},{8,4},{9,5},... | collective-permute-start | bytes 2312 | tf_op jit(solution)/shard_map/ppermute | solution.py:37
  18.3 11.0 %collective-permute-start.10 = (bf16[32,1792]{1,0:T(8,128)(2,1)S(1)}, bf16[32,1792]{1,0:T(8,128)(2,1)S(1)}, u32[]{:S(2)}, u32[]{:S(2)}) collective-permute-start(bf16[32,1792]{1,0:T(8,128)(2,1)S(1)} %get-tuple-element.158), channel_id=1, source_target_pairs={{0,2},{1,3},{4,0},{5,1},{8,4},{9,5},{12,8},{13,9},{14,12},{15,13},... | collective-permute-start | bytes 344072 | tf_op jit(solution)/shard_map/ppermute | solution.py:79
  20.0 9.3 %collective-permute-start.9 = (bf16[32,1792]{1,0:T(8,128)(2,1)S(1)}, bf16[32,1792]{1,0:T(8,128)(2,1)S(1)}, u32[]{:S(2)}, u32[]{:S(2)}) collective-permute-start(bf16[32,1792]{1,0:T(8,128)(2,1)S(1)} %get-tuple-element.159), channel_id=1, source_target_pairs={{0,4},{1,5},{4,8},{5,9},{8,12},{9,13},{12,14},{13,15},{14,10},{15,... | collective-permute-start | bytes 344072 | tf_op jit(solution)/shard_map/ppermute | solution.py:79
  29.9 8.5 %collective-permute-start.15 = (bf16[32,3584]{1,0:T(8,128)(2,1)S(1)}, bf16[32,3584]{1,0:T(8,128)(2,1)S(1)}, u32[]{:S(2)}, u32[]{:S(2)}) collective-permute-start(bf16[32,3584]{1,0:T(8,128)(2,1)S(1)} %get-tuple-element.154), channel_id=1, source_target_pairs={{0,2},{1,3},{4,0},{5,1},{8,4},{9,5},{12,8},{13,9},{14,12},{15,13},... | collective-permute-start | bytes 688136 | tf_op jit(solution)/shard_map/ppermute | solution.py:79
  31.5 8.5 %collective-permute-start.14 = (bf16[32,3584]{1,0:T(8,128)(2,1)S(1)}, bf16[32,3584]{1,0:T(8,128)(2,1)S(1)}, u32[]{:S(2)}, u32[]{:S(2)}) collective-permute-start(bf16[32,3584]{1,0:T(8,128)(2,1)S(1)} %get-tuple-element.155), channel_id=1, source_target_pairs={{0,4},{1,5},{4,8},{5,9},{8,12},{9,13},{12,14},{13,15},{14,10},{15,... | collective-permute-start | bytes 688136 | tf_op jit(solution)/shard_map/ppermute | solution.py:79
  33.1 9.2 %collective-permute-start.13 = (bf16[32,1792]{1,0:T(8,128)(2,1)S(1)}, bf16[32,1792]{1,0:T(8,128)(2,1)S(1)}, u32[]{:S(2)}, u32[]{:S(2)}) collective-permute-start(bf16[32,1792]{1,0:T(8,128)(2,1)S(1)} %get-tuple-element.156), channel_id=1, source_target_pairs={{0,2},{1,3},{4,0},{5,1},{8,4},{9,5},{12,8},{13,9},{14,12},{15,13},... | collective-permute-start | bytes 344072 | tf_op jit(solution)/shard_map/ppermute | solution.py:79
  34.7 7.7 %collective-permute-start.12 = (bf16[32,1792]{1,0:T(8,128)(2,1)S(1)}, bf16[32,1792]{1,0:T(8,128)(2,1)S(1)}, u32[]{:S(2)}, u32[]{:S(2)}) collective-permute-start(bf16[32,1792]{1,0:T(8,128)(2,1)S(1)} %get-tuple-element.157), channel_id=1, source_target_pairs={{0,4},{1,5},{4,8},{5,9},{8,12},{9,13},{12,14},{13,15},{14,10},{15,... | collective-permute-start | bytes 344072 | tf_op jit(solution)/shard_map/ppermute | solution.py:79
  40.1 8.5 %collective-permute-start.18 = (bf16[32,3584]{1,0:T(8,128)(2,1)S(1)}, bf16[32,3584]{1,0:T(8,128)(2,1)S(1)}, u32[]{:S(2)}, u32[]{:S(2)}) collective-permute-start(bf16[32,3584]{1,0:T(8,128)(2,1)S(1)} %add_convert_fusion.9), channel_id=1, source_target_pairs={{0,4},{1,5},{4,8},{5,9},{8,12},{9,13},{12,14},{13,15},{14,10},{15,... | collective-permute-start | bytes 688136 | tf_op jit(solution)/shard_map/ppermute | solution.py:79
  40.8 7.8 %collective-permute-start.19 = (bf16[32,3584]{1,0:T(8,128)(2,1)S(1)}, bf16[32,3584]{1,0:T(8,128)(2,1)S(1)}, u32[]{:S(2)}, u32[]{:S(2)}) collective-permute-start(bf16[32,3584]{1,0:T(8,128)(2,1)S(1)} %add_convert_fusion.8), channel_id=1, source_target_pairs={{0,2},{1,3},{4,0},{5,1},{8,4},{9,5},{12,8},{13,9},{14,12},{15,13},... | collective-permute-start | bytes 688136 | tf_op jit(solution)/shard_map/ppermute | solution.py:79
  42.5 8.2 %collective-permute-start.17 = (bf16[32,3584]{1,0:T(8,128)(2,1)S(1)}, bf16[32,3584]{1,0:T(8,128)(2,1)S(1)}, u32[]{:S(2)}, u32[]{:S(2)}) collective-permute-start(bf16[32,3584]{1,0:T(8,128)(2,1)S(1)} %get-tuple-element.152), channel_id=1, source_target_pairs={{0,2},{1,3},{4,0},{5,1},{8,4},{9,5},{12,8},{13,9},{14,12},{15,13},... | collective-permute-start | bytes 688136 | tf_op jit(solution)/shard_map/ppermute | solution.py:79
  43.1 8.1 %collective-permute-start.16 = (bf16[32,3584]{1,0:T(8,128)(2,1)S(1)}, bf16[32,3584]{1,0:T(8,128)(2,1)S(1)}, u32[]{:S(2)}, u32[]{:S(2)}) collective-permute-start(bf16[32,3584]{1,0:T(8,128)(2,1)S(1)} %get-tuple-element.153), channel_id=1, source_target_pairs={{0,4},{1,5},{4,8},{5,9},{8,12},{9,13},{12,14},{13,15},{14,10},{15,... | collective-permute-start | bytes 688136 | tf_op jit(solution)/shard_map/ppermute | solution.py:79
  51.2 8.5 %collective-permute-start.20 = (bf16[32,3584]{1,0:T(8,128)(2,1)S(1)}, bf16[32,3584]{1,0:T(8,128)(2,1)S(1)}, u32[]{:S(2)}, u32[]{:S(2)}) collective-permute-start(bf16[32,3584]{1,0:T(8,128)(2,1)S(1)} %add_convert_fusion.3), channel_id=1, source_target_pairs={{0,4},{1,5},{4,8},{5,9},{8,12},{9,13},{12,14},{13,15},{14,10},{15,... | collective-permute-start | bytes 688136 | tf_op jit(solution)/shard_map/ppermute | solution.py:79
  52.2 8.6 %collective-permute-start.22 = (bf16[32,3584]{1,0:T(8,128)(2,1)S(1)}, bf16[32,3584]{1,0:T(8,128)(2,1)S(1)}, u32[]{:S(2)}, u32[]{:S(2)}) collective-permute-start(bf16[32,3584]{1,0:T(8,128)(2,1)S(1)} %add_convert_fusion.1), channel_id=1, source_target_pairs={{0,2},{1,3},{4,0},{5,1},{8,4},{9,5},{12,8},{13,9},{14,12},{15,13},... | collective-permute-start | bytes 688136 | tf_op jit(solution)/shard_map/ppermute | solution.py:79
  53.4 11.2 %collective-permute-start.25 = (bf16[32,3584]{1,0:T(8,128)(2,1)S(1)}, bf16[32,3584]{1,0:T(8,128)(2,1)S(1)}, u32[]{:S(2)}, u32[]{:S(2)}) collective-permute-start(bf16[32,3584]{1,0:T(8,128)(2,1)S(1)} %get-tuple-element.150), channel_id=1, source_target_pairs={{0,2},{1,3},{4,0},{5,1},{8,4},{9,5},{12,8},{13,9},{14,12},{15,13},... | collective-permute-start | bytes 688136 | tf_op jit(solution)/shard_map/ppermute | solution.py:79
  54.6 10.0 %collective-permute-start.24 = (bf16[32,3584]{1,0:T(8,128)(2,1)S(1)}, bf16[32,3584]{1,0:T(8,128)(2,1)S(1)}, u32[]{:S(2)}, u32[]{:S(2)}) collective-permute-start(bf16[32,3584]{1,0:T(8,128)(2,1)S(1)} %get-tuple-element.151), channel_id=1, source_target_pairs={{0,4},{1,5},{4,8},{5,9},{8,12},{9,13},{12,14},{13,15},{14,10},{15,... | collective-permute-start | bytes 688136 | tf_op jit(solution)/shard_map/ppermute | solution.py:79
  60.9 6.1 %collective-permute-start.23 = (bf16[32,3584]{1,0:T(8,128)(2,1)S(1)}, bf16[32,3584]{1,0:T(8,128)(2,1)S(1)}, u32[]{:S(2)}, u32[]{:S(2)}) collective-permute-start(bf16[32,3584]{1,0:T(8,128)(2,1)S(1)} %get-tuple-element.148), channel_id=1, source_target_pairs={{0,2},{1,3},{4,0},{5,1},{8,4},{9,5},{12,8},{13,9},{14,12},{15,13},... | collective-permute-start | bytes 688136 | tf_op jit(solution)/shard_map/ppermute | solution.py:79
  69.9 8.5 %collective-permute-start.26 = (bf16[64,3584]{1,0:T(8,128)(2,1)S(1)}, bf16[64,3584]{1,0:T(8,128)(2,1)S(1)}, u32[]{:S(2)}, u32[]{:S(2)}) collective-permute-start(bf16[64,3584]{1,0:T(8,128)(2,1)S(1)} %bitcast.4), channel_id=1, source_target_pairs={{0,4},{1,5},{4,8},{5,9},{8,12},{9,13},{12,14},{13,15},{14,10},{15,... | collective-permute-start | bytes 1376264 | tf_op jit(solution)/shard_map/ppermute | solution.py:79
  71.1 8.6 %collective-permute-start.28 = (bf16[64,3584]{1,0:T(8,128)(2,1)S(1)}, bf16[64,3584]{1,0:T(8,128)(2,1)S(1)}, u32[]{:S(2)}, u32[]{:S(2)}) collective-permute-start(bf16[64,3584]{1,0:T(8,128)(2,1)S(1)} %bitcast.5), channel_id=1, source_target_pairs={{0,2},{1,3},{4,0},{5,1},{8,4},{9,5},{12,8},{13,9},{14,12},{15,13},... | collective-permute-start | bytes 1376264 | tf_op jit(solution)/shard_map/ppermute | solution.py:79
  74.6 6.5 %collective-permute-start.29 = (bf16[64,3584]{1,0:T(8,128)(2,1)S(1)}, bf16[64,3584]{1,0:T(8,128)(2,1)S(1)}, u32[]{:S(2)}, u32[]{:S(2)}) collective-permute-start(bf16[64,3584]{1,0:T(8,128)(2,1)S(1)} %bitcast.6), channel_id=1, source_target_pairs={{0,1},{1,0},{2,3},{3,2},{4,5},{5,4},{6,7},{7,6},{8,9},{9,8},{10,11... | collective-permute-start | bytes 1376264 | tf_op jit(solution)/shard_map/ppermute | solution.py:37
  78.5 10.7 %collective-permute-start.27 = (bf16[64,3584]{1,0:T(8,128)(2,1)S(1)}, bf16[64,3584]{1,0:T(8,128)(2,1)S(1)}, u32[]{:S(2)}, u32[]{:S(2)}) collective-permute-start(bf16[64,3584]{1,0:T(8,128)(2,1)S(1)} %collective-permute-done.26.refs_0_), channel_id=1, source_target_pairs={{0,4},{1,5},{4,8},{5,9},{8,12},{9,13},{12,14},{13,15},{14,10},{15,... | collective-permute-start | bytes 1376264 | tf_op jit(solution)/shard_map/ppermute | solution.py:79
  79.7 10.7 %collective-permute-start.31 = (bf16[64,3584]{1,0:T(8,128)(2,1)S(1)}, bf16[64,3584]{1,0:T(8,128)(2,1)S(1)}, u32[]{:S(2)}, u32[]{:S(2)}) collective-permute-start(bf16[64,3584]{1,0:T(8,128)(2,1)S(1)} %collective-permute-done.28.refs_1_), channel_id=1, source_target_pairs={{0,2},{1,3},{4,0},{5,1},{8,4},{9,5},{12,8},{13,9},{14,12},{15,13},... | collective-permute-start | bytes 1376264 | tf_op jit(solution)/shard_map/ppermute | solution.py:79
  80.6 10.7 %collective-permute-start.33 = (bf16[64,3584]{1,0:T(8,128)(2,1)S(1)}, bf16[64,3584]{1,0:T(8,128)(2,1)S(1)}, u32[]{:S(2)}, u32[]{:S(2)}) collective-permute-start(bf16[64,3584]{1,0:T(8,128)(2,1)S(1)} %collective-permute-done.28.refs_1_), channel_id=1, source_target_pairs={{0,1},{1,0},{2,3},{3,2},{4,5},{5,4},{6,7},{7,6},{8,9},{9,8},{10,11... | collective-permute-start | bytes 1376264 | tf_op jit(solution)/shard_map/ppermute | solution.py:37
  80.6 11.2 %collective-permute-start.32 = (bf16[64,3584]{1,0:T(8,128)(2,1)S(1)}, bf16[64,3584]{1,0:T(8,128)(2,1)S(1)}, u32[]{:S(2)}, u32[]{:S(2)}) collective-permute-start(bf16[64,3584]{1,0:T(8,128)(2,1)S(1)} %collective-permute-done.26.refs_0_), channel_id=1, source_target_pairs={{0,1},{1,0},{2,3},{3,2},{4,5},{5,4},{6,7},{7,6},{8,9},{9,8},{10,11... | collective-permute-start | bytes 1376264 | tf_op jit(solution)/shard_map/ppermute | solution.py:37
  89.2 10.6 %collective-permute-start.30 = (bf16[64,3584]{1,0:T(8,128)(2,1)S(1)}, bf16[64,3584]{1,0:T(8,128)(2,1)S(1)}, u32[]{:S(2)}, u32[]{:S(2)}) collective-permute-start(bf16[64,3584]{1,0:T(8,128)(2,1)S(1)} %collective-permute-done.27.refs_0_), channel_id=1, source_target_pairs={{0,4},{1,5},{4,8},{5,9},{8,12},{9,13},{12,14},{13,15},{14,10},{15,... | collective-permute-start | bytes 1376264 | tf_op jit(solution)/shard_map/ppermute | solution.py:79
  90.4 10.6 %collective-permute-start.35 = (bf16[64,3584]{1,0:T(8,128)(2,1)S(1)}, bf16[64,3584]{1,0:T(8,128)(2,1)S(1)}, u32[]{:S(2)}, u32[]{:S(2)}) collective-permute-start(bf16[64,3584]{1,0:T(8,128)(2,1)S(1)} %collective-permute-done.31.refs_1_), channel_id=1, source_target_pairs={{0,2},{1,3},{4,0},{5,1},{8,4},{9,5},{12,8},{13,9},{14,12},{15,13},... | collective-permute-start | bytes 1376264 | tf_op jit(solution)/shard_map/ppermute | solution.py:79
  91.3 10.7 %collective-permute-start.39 = (bf16[64,3584]{1,0:T(8,128)(2,1)S(1)}, bf16[64,3584]{1,0:T(8,128)(2,1)S(1)}, u32[]{:S(2)}, u32[]{:S(2)}) collective-permute-start(bf16[64,3584]{1,0:T(8,128)(2,1)S(1)} %collective-permute-done.31.refs_1_), channel_id=1, source_target_pairs={{0,1},{1,0},{2,3},{3,2},{4,5},{5,4},{6,7},{7,6},{8,9},{9,8},{10,11... | collective-permute-start | bytes 1376264 | tf_op jit(solution)/shard_map/ppermute | solution.py:37
  91.3 11.2 %collective-permute-start.38 = (bf16[64,3584]{1,0:T(8,128)(2,1)S(1)}, bf16[64,3584]{1,0:T(8,128)(2,1)S(1)}, u32[]{:S(2)}, u32[]{:S(2)}) collective-permute-start(bf16[64,3584]{1,0:T(8,128)(2,1)S(1)} %collective-permute-done.27.refs_0_), channel_id=1, source_target_pairs={{0,1},{1,0},{2,3},{3,2},{4,5},{5,4},{6,7},{7,6},{8,9},{9,8},{10,11... | collective-permute-start | bytes 1376264 | tf_op jit(solution)/shard_map/ppermute | solution.py:37
  101.9 6.6 %collective-permute-start.36 = (bf16[64,3584]{1,0:T(8,128)(2,1)S(1)}, bf16[64,3584]{1,0:T(8,128)(2,1)S(1)}, u32[]{:S(2)}, u32[]{:S(2)}) collective-permute-start(bf16[64,3584]{1,0:T(8,128)(2,1)S(1)} %collective-permute-done.35.refs_1_), channel_id=1, source_target_pairs={{0,1},{1,0},{2,3},{3,2},{4,5},{5,4},{6,7},{7,6},{8,9},{9,8},{10,11... | collective-permute-start | bytes 1376264 | tf_op jit(solution)/shard_map/ppermute | solution.py:37
  102.0 6.6 %collective-permute-start.34 = (bf16[64,3584]{1,0:T(8,128)(2,1)S(1)}, bf16[64,3584]{1,0:T(8,128)(2,1)S(1)}, u32[]{:S(2)}, u32[]{:S(2)}) collective-permute-start(bf16[64,3584]{1,0:T(8,128)(2,1)S(1)} %collective-permute-done.30.refs_0_), channel_id=1, source_target_pairs={{0,1},{1,0},{2,3},{3,2},{4,5},{5,4},{6,7},{7,6},{8,9},{9,8},{10,11... | collective-permute-start | bytes 1376264 | tf_op jit(solution)/shard_map/ppermute | solution.py:37
  (23 other events, 318.5 us)

commit v19 on v18

--- a/solution.py
+++ b/solution.py
@@ -430,8 +430,10 @@
     for hop in range(1, chips // 2):
         if hop + 1 < chips // 2:
             dec_moving = advance(dec_came, dec_kept, dec_core, hop + 1)
-            dec_came = travel(dec_moving)
+            dec_came = dec_arrived = travel(dec_moving)
             enc_came = after(enc_came, *dec_moving)
+        else:
+            enc_came = after(enc_came, *dec_arrived)
         enc_moving = advance(enc_came, enc_kept, enc_core, hop)
         enc_came = travel(enc_moving)
         dec_came = after(dec_came, *enc_moving)

time: 110 us -> 114 us (1.036)
  waiting for transfers between devices: 45.5 us -> 48.8 us
    ppermute x24, waiting for transfers between devices: 41.9 us -> 45.2 us  [shift(): return lax.ppermute(value, 'latent', pairs)]
  transfers between devices with their start and end apart: 43 -> 43, of which waited for: 20 -> 22; matrix products, arithmetic and copies ran while one was open for 1% -> 1% of each run, Pallas kernels for 21% -> 20%
where the time goes in v19:
time: 114 us; the launch traced here: 113 us
  waiting for transfers between devices  48.8 us (43%)
  starting transfers between devices  35.6 us (31%)
  Pallas kernels  26 us (23%)
  other arithmetic  2.05 us (2%)
    ppermute x24, waiting for transfers between devices, shift(): return lax.ppermute(value, 'latent', pairs)  45.2 us
    ppermute x24, starting transfers between devices, shift(): return lax.ppermute(value, 'latent', pairs)  25.4 us
    ppermute x19, starting transfers between devices, swap(): return lax.ppermute(value, 'latent', [(i, i ^ bits) for i in range(size)])  10.2 us
    pallas_call x1, Pallas kernels, stream_product(): pl.pallas_call(functools.partial(stream_kernel, size, rows), in_specs=[pl...  8.36 us
    pallas_call x1, Pallas kernels, select_product(): pl.pallas_call(functools.partial(select_kernel, size, rows, len(table)),...  7.01 us
    pallas_call x6, Pallas kernels, place(): pl.pallas_call(functools.partial(place_kernel, plan, size, rows, count),...  6.39 us
    pallas_call x2, Pallas kernels, update(): pl.pallas_call(blocks_kernel if blocks_only else states_kernel, grid=(row...  4.2 us
    ppermute x19, waiting for transfers between devices, swap(): return lax.ppermute(value, 'latent', [(i, i ^ bits) for i in range(size)])  3.57 us
  transfers between devices with their start and end apart: 43, of which 22 were waited for; matrix products, arithmetic and copies ran while one was open for 1% of the time, Pallas kernels for 20%

profile of v19, /device:TPU:0, one launch (start us, length us, event | category | flops | bytes accessed | tf_op | source)
XLA Modules:
  0.0 113.5 jit_solution(13469963349238607127)
XLA Ops:
  1.6 2.5 %collective-permute-start.2 = (s32[1,48]{1,0:T(1,128)S(1)}, s32[1,48]{1,0:T(1,128)S(1)}, u32[]{:S(2)}, u32[]{:S(2)}) collective-permute-start(s32[1,48]{1,0:T(1,128)S(1)} %pad_add_fusion.1), channel_id=1, source_target_pairs={{0,3},{1,2},{2,1},{3,0},{4,7},{5,6},{6,5},{7,4},{8,11},{9,10},{10,... | collective-permute-start | bytes 584 | tf_op jit(solution)/shard_map/ppermute | solution.py:37
  4.7 8.4 %product.1 = (bf16[128,3584]{1,0:T(8,128)(2,1)S(1)}, bf16[128,3584]{1,0:T(8,128)(2,1)S(1)}, bf16[128,3584]{1,0:T(8,128)(2,1)S(1)}, bf16[128,3584]{1,0:T(8,128)(2,1)S(1)}) custom-call(bf16[1024,512]{1,0:T(8,128)(2,1)} %coef_ref.1, bf16[1024,3584]{1,0:T(8,128)(2,1)} %right_hbm.1), custom_call_target="tpu_custom_call" | custom-call | flops 3758096384 | bytes 12058624 | tf_op jit(solution)/shard_map/product/pallas_call | solution.py:186
  13.8 3.8 %collective-permute-start.7 = (s32[4,48]{1,0:T(4,128)S(1)}, s32[4,48]{1,0:T(4,128)S(1)}, u32[]{:S(2)}, u32[]{:S(2)}) collective-permute-start(s32[4,48]{1,0:T(4,128)S(1)} %pad_add_fusion.refs_0_), channel_id=1, source_target_pairs={{0,12},{1,13},{2,14},{3,15},{4,8},{5,9},{6,10},{7,11},{8,4},{9,5},... | collective-permute-start | bytes 2312 | tf_op jit(solution)/shard_map/ppermute | solution.py:37
  18.3 1.8 %collective-permute-start.10 = (bf16[32,1792]{1,0:T(8,128)(2,1)S(1)}, bf16[32,1792]{1,0:T(8,128)(2,1)S(1)}, u32[]{:S(2)}, u32[]{:S(2)}) collective-permute-start(bf16[32,1792]{1,0:T(8,128)(2,1)S(1)} %get-tuple-element.162), channel_id=1, source_target_pairs={{0,2},{1,3},{4,0},{5,1},{8,4},{9,5},{12,8},{13,9},{14,12},{15,13},... | collective-permute-start | bytes 344072 | tf_op jit(solution)/shard_map/ppermute | solution.py:79
  20.3 1.8 %collective-permute-done.6.refs_2_ = s32[4,48]{1,0:T(4,128)S(1)} collective-permute-done((s32[4,48]{1,0:T(4,128)S(1)}, s32[4,48]{1,0:T(4,128)S(1)}, u32[]{:S(2)}, u32[]{:S(2)}) %collective-permute-start.6) | collective-permute-done | bytes 800 | tf_op jit(solution)/shard_map/ppermute | solution.py:37
  22.2 7.0 %select_product.1 = (bf16[128,3584]{1,0:T(8,128)(2,1)S(1)}, bf16[128,3584]{1,0:T(8,128)(2,1)S(1)}, bf16[128,3584]{1,0:T(8,128)(2,1)S(1)}, bf16[128,3584]{1,0:T(8,128)(2,1)S(1)}, s32[32,1]{1,0:T(8,128)S(1)}) custom-call(bf16[1024,512]{1,0:T(8,128)(2,1)S(1)} %copy-done.6, bf16[1024,3584]{1,0:T(8,128)(2,1)S(1)} %bitcast.9, s32[2,16]{1,0:T(2,128)S(1)} %bitcast.10, ...), custom_call_target="tpu_custom_call" | custom-call | flops 3758096384 | bytes 12058624 | tf_op jit(solution)/shard_map/select_product/pallas_call | solution.py:237
  29.9 1.6 %collective-permute-start.15 = (bf16[32,3584]{1,0:T(8,128)(2,1)S(1)}, bf16[32,3584]{1,0:T(8,128)(2,1)S(1)}, u32[]{:S(2)}, u32[]{:S(2)}) collective-permute-start(bf16[32,3584]{1,0:T(8,128)(2,1)S(1)} %get-tuple-element.158), channel_id=1, source_target_pairs={{0,2},{1,3},{4,0},{5,1},{8,4},{9,5},{12,8},{13,9},{14,12},{15,13},... | collective-permute-start | bytes 688136 | tf_op jit(solution)/shard_map/ppermute | solution.py:79
  33.1 1.6 %collective-permute-start.13 = (bf16[32,1792]{1,0:T(8,128)(2,1)S(1)}, bf16[32,1792]{1,0:T(8,128)(2,1)S(1)}, u32[]{:S(2)}, u32[]{:S(2)}) collective-permute-start(bf16[32,1792]{1,0:T(8,128)(2,1)S(1)} %get-tuple-element.160), channel_id=1, source_target_pairs={{0,2},{1,3},{4,0},{5,1},{8,4},{9,5},{12,8},{13,9},{14,12},{15,13},... | collective-permute-start | bytes 344072 | tf_op jit(solution)/shard_map/ppermute | solution.py:79
  35.2 3.2 %collective-permute-done.15 = bf16[32,3584]{1,0:T(8,128)(2,1)S(1)} collective-permute-done((bf16[32,3584]{1,0:T(8,128)(2,1)S(1)}, bf16[32,3584]{1,0:T(8,128)(2,1)S(1)}, u32[]{:S(2)}, u32[]{:S(2)}) %collective-permute-start.15) | collective-permute-done | bytes 229408 | tf_op jit(solution)/shard_map/ppermute | solution.py:79
  38.4 1.6 %collective-permute-done.14 = bf16[32,3584]{1,0:T(8,128)(2,1)S(1)} collective-permute-done((bf16[32,3584]{1,0:T(8,128)(2,1)S(1)}, bf16[32,3584]{1,0:T(8,128)(2,1)S(1)}, u32[]{:S(2)}, u32[]{:S(2)}) %collective-permute-start.14) | collective-permute-done | bytes 229408 | tf_op jit(solution)/shard_map/ppermute | solution.py:79
  40.8 1.6 %collective-permute-start.19 = (bf16[32,3584]{1,0:T(8,128)(2,1)S(1)}, bf16[32,3584]{1,0:T(8,128)(2,1)S(1)}, u32[]{:S(2)}, u32[]{:S(2)}) collective-permute-start(bf16[32,3584]{1,0:T(8,128)(2,1)S(1)} %add_convert_fusion.8), channel_id=1, source_target_pairs={{0,2},{1,3},{4,0},{5,1},{8,4},{9,5},{12,8},{13,9},{14,12},{15,13},... | collective-permute-start | bytes 688136 | tf_op jit(solution)/shard_map/ppermute | solution.py:79
  43.1 1.6 %collective-permute-start.16 = (bf16[32,3584]{1,0:T(8,128)(2,1)S(1)}, bf16[32,3584]{1,0:T(8,128)(2,1)S(1)}, u32[]{:S(2)}, u32[]{:S(2)}) collective-permute-start(bf16[32,3584]{1,0:T(8,128)(2,1)S(1)} %get-tuple-element.157), channel_id=1, source_target_pairs={{0,4},{1,5},{4,8},{5,9},{8,12},{9,13},{12,14},{13,15},{14,10},{15,... | collective-permute-start | bytes 688136 | tf_op jit(solution)/shard_map/ppermute | solution.py:79
  44.6 4.0 %collective-permute-done.18 = bf16[32,3584]{1,0:T(8,128)(2,1)S(1)} collective-permute-done((bf16[32,3584]{1,0:T(8,128)(2,1)S(1)}, bf16[32,3584]{1,0:T(8,128)(2,1)S(1)}, u32[]{:S(2)}, u32[]{:S(2)}) %collective-permute-start.18) | collective-permute-done | bytes 229408 | tf_op jit(solution)/shard_map/ppermute | solution.py:79
  49.6 1.6 %collective-permute-start.23 = (bf16[32,3584]{1,0:T(8,128)(2,1)S(1)}, bf16[32,3584]{1,0:T(8,128)(2,1)S(1)}, u32[]{:S(2)}, u32[]{:S(2)}) collective-permute-start(bf16[32,3584]{1,0:T(8,128)(2,1)S(1)} %get-tuple-element.154), channel_id=1, source_target_pairs={{0,2},{1,3},{4,0},{5,1},{8,4},{9,5},{12,8},{13,9},{14,12},{15,13},... | collective-permute-start | bytes 688136 | tf_op jit(solution)/shard_map/ppermute | solution.py:79
  51.7 2.4 %collective-permute-done.17 = bf16[32,3584]{1,0:T(8,128)(2,1)S(1)} collective-permute-done((bf16[32,3584]{1,0:T(8,128)(2,1)S(1)}, bf16[32,3584]{1,0:T(8,128)(2,1)S(1)}, u32[]{:S(2)}, u32[]{:S(2)}) %collective-permute-start.17) | collective-permute-done | bytes 229408 | tf_op jit(solution)/shard_map/ppermute | solution.py:79
  55.1 1.3 %collective-permute-start.21 = (bf16[32,3584]{1,0:T(8,128)(2,1)S(1)}, bf16[32,3584]{1,0:T(8,128)(2,1)S(1)}, u32[]{:S(2)}, u32[]{:S(2)}) collective-permute-start(bf16[32,3584]{1,0:T(8,128)(2,1)S(1)} %add_convert_fusion.2), channel_id=1, source_target_pairs={{0,2},{1,3},{4,0},{5,1},{8,4},{9,5},{12,8},{13,9},{14,12},{15,13},... | collective-permute-start | bytes 688136 | tf_op jit(solution)/shard_map/ppermute | solution.py:79
  56.4 1.8 %collective-permute-done.23.refs_14_ = bf16[32,3584]{1,0:T(8,128)(2,1)S(1)} collective-permute-done((bf16[32,3584]{1,0:T(8,128)(2,1)S(1)}, bf16[32,3584]{1,0:T(8,128)(2,1)S(1)}, u32[]{:S(2)}, u32[]{:S(2)}) %collective-permute-start.23) | collective-permute-done | bytes 229408 | tf_op jit(solution)/shard_map/ppermute | solution.py:79
  58.5 2.5 %collective-permute-done.20 = bf16[32,3584]{1,0:T(8,128)(2,1)S(1)} collective-permute-done((bf16[32,3584]{1,0:T(8,128)(2,1)S(1)}, bf16[32,3584]{1,0:T(8,128)(2,1)S(1)}, u32[]{:S(2)}, u32[]{:S(2)}) %collective-permute-start.20) | collective-permute-done | bytes 229408 | tf_op jit(solution)/shard_map/ppermute | solution.py:79
  62.2 1.3 %collective-permute-start.25 = (bf16[32,3584]{1,0:T(8,128)(2,1)S(1)}, bf16[32,3584]{1,0:T(8,128)(2,1)S(1)}, u32[]{:S(2)}, u32[]{:S(2)}) collective-permute-start(bf16[32,3584]{1,0:T(8,128)(2,1)S(1)} %get-tuple-element.152), channel_id=1, source_target_pairs={{0,2},{1,3},{4,0},{5,1},{8,4},{9,5},{12,8},{13,9},{14,12},{15,13},... | collective-permute-start | bytes 688136 | tf_op jit(solution)/shard_map/ppermute | solution.py:79
  63.5 1.3 %collective-permute-start.24 = (bf16[32,3584]{1,0:T(8,128)(2,1)S(1)}, bf16[32,3584]{1,0:T(8,128)(2,1)S(1)}, u32[]{:S(2)}, u32[]{:S(2)}) collective-permute-start(bf16[32,3584]{1,0:T(8,128)(2,1)S(1)} %get-tuple-element.153), channel_id=1, source_target_pairs={{0,4},{1,5},{4,8},{5,9},{8,12},{9,13},{12,14},{13,15},{14,10},{15,... | collective-permute-start | bytes 688136 | tf_op jit(solution)/shard_map/ppermute | solution.py:79
  64.8 3.9 %collective-permute-done.25.refs_10_ = bf16[32,3584]{1,0:T(8,128)(2,1)S(1)} collective-permute-done((bf16[32,3584]{1,0:T(8,128)(2,1)S(1)}, bf16[32,3584]{1,0:T(8,128)(2,1)S(1)}, u32[]{:S(2)}, u32[]{:S(2)}) %collective-permute-start.25) | collective-permute-done | bytes 229408 | tf_op jit(solution)/shard_map/ppermute | solution.py:79
  68.7 2.5 %collective-permute-done.24.refs_9_ = bf16[32,3584]{1,0:T(8,128)(2,1)S(1)} collective-permute-done((bf16[32,3584]{1,0:T(8,128)(2,1)S(1)}, bf16[32,3584]{1,0:T(8,128)(2,1)S(1)}, u32[]{:S(2)}, u32[]{:S(2)}) %collective-permute-start.24) | collective-permute-done | bytes 229408 | tf_op jit(solution)/shard_map/ppermute | solution.py:79
  71.3 1.6 %blocks.1 = bf16[2,32,3584]{2,1,0:T(8,128)(2,1)S(1)} custom-call(s32[32,1]{1,0:T(8,128)S(1)} %get-tuple-element.87.refs_0_, f32[32,3584]{1,0:T(8,128)S(1)} %copy-done, f32[32,3584]{1,0:T(8,128)S(1)} %copy-done.1, f32[32,3584]{1,0:T(8,128)S(1)} %copy-done.2, f32[32,3584]{1,0:T(8,128)S(1)} %copy-done.3, f32[32,3584]{1,0:T(8,128)S(1)} %copy-done.4, ...), custom_call_target="tpu_custom_call" | custom-call | flops 1146880 | bytes 1146880 | tf_op jit(solution)/shard_map/blocks/pallas_call | solution.py:307
  72.9 1.5 %collective-permute-start.26 = (bf16[64,3584]{1,0:T(8,128)(2,1)S(1)}, bf16[64,3584]{1,0:T(8,128)(2,1)S(1)}, u32[]{:S(2)}, u32[]{:S(2)}) collective-permute-start(bf16[64,3584]{1,0:T(8,128)(2,1)S(1)} %bitcast.4), channel_id=1, source_target_pairs={{0,4},{1,5},{4,8},{5,9},{8,12},{9,13},{12,14},{13,15},{14,10},{15,... | collective-permute-start | bytes 1376264 | tf_op jit(solution)/shard_map/ppermute | solution.py:79
  75.3 2.6 %states.1 = (f32[32,3584]{1,0:T(8,128)}, f32[32,3584]{1,0:T(8,128)}, f32[32,3584]{1,0:T(8,128)}, f32[32,3584]{1,0:T(8,128)}, f32[32,3584]{1,0:T(8,128)}, /*index=5*/f32[32,3584]{1,0:T(8,128)}) custom-call(s32[32,1]{1,0:T(8,128)S(1)} %get-tuple-element.87.refs_0_, f32[32,3584]{1,0:T(8,128)S(1)} %copy-done, f32[32,3584]{1,0:T(8,128)S(1)} %copy-done.1, ...), custom_call_target="tpu_custom_call" | custom-call | flops 1146880 | bytes 1146880 | tf_op jit(solution)/shard_map/states/pallas_call | solution.py:307
  78.6 3.0 %collective-permute-done.26.refs_0_ = bf16[64,3584]{1,0:T(8,128)(2,1)S(1)} collective-permute-done((bf16[64,3584]{1,0:T(8,128)(2,1)S(1)}, bf16[64,3584]{1,0:T(8,128)(2,1)S(1)}, u32[]{:S(2)}, u32[]{:S(2)}) %collective-permute-start.26) | collective-permute-done | bytes 458784 | tf_op jit(solution)/shard_map/ppermute | solution.py:79
  85.4 6.6 %collective-permute-done.27.refs_0_ = bf16[64,3584]{1,0:T(8,128)(2,1)S(1)} collective-permute-done((bf16[64,3584]{1,0:T(8,128)(2,1)S(1)}, bf16[64,3584]{1,0:T(8,128)(2,1)S(1)}, u32[]{:S(2)}, u32[]{:S(2)}) %collective-permute-start.27) | collective-permute-done | bytes 458784 | tf_op jit(solution)/shard_map/ppermute | solution.py:79
  92.0 1.6 %collective-permute-start.30 = (bf16[64,3584]{1,0:T(8,128)(2,1)S(1)}, bf16[64,3584]{1,0:T(8,128)(2,1)S(1)}, u32[]{:S(2)}, u32[]{:S(2)}) collective-permute-start(bf16[64,3584]{1,0:T(8,128)(2,1)S(1)} %collective-permute-done.27.refs_0_), channel_id=1, source_target_pairs={{0,4},{1,5},{4,8},{5,9},{8,12},{9,13},{12,14},{13,15},{14,10},{15,... | collective-permute-start | bytes 1376264 | tf_op jit(solution)/shard_map/ppermute | solution.py:79
  96.0 6.6 %collective-permute-done.30.refs_0_ = bf16[64,3584]{1,0:T(8,128)(2,1)S(1)} collective-permute-done((bf16[64,3584]{1,0:T(8,128)(2,1)S(1)}, bf16[64,3584]{1,0:T(8,128)(2,1)S(1)}, u32[]{:S(2)}, u32[]{:S(2)}) %collective-permute-start.30) | collective-permute-done | bytes 458784 | tf_op jit(solution)/shard_map/ppermute | solution.py:79
  102.6 1.7 %collective-permute-start.37 = (bf16[64,1792]{1,0:T(8,128)(2,1)S(1)}, bf16[64,1792]{1,0:T(8,128)(2,1)S(1)}, u32[]{:S(2)}, u32[]{:S(2)}) collective-permute-start(bf16[64,1792]{1,0:T(8,128)(2,1)S(1)} %slice.134), channel_id=1, source_target_pairs={{0,4},{1,5},{4,8},{5,9},{8,12},{9,13},{12,14},{13,15},{14,10},{15,... | collective-permute-start | bytes 688136 | tf_op jit(solution)/shard_map/ppermute | solution.py:79
  106.8 2.1 %collective-permute-done.37.refs_0_ = bf16[64,1792]{1,0:T(8,128)(2,1)S(1)} collective-permute-done((bf16[64,1792]{1,0:T(8,128)(2,1)S(1)}, bf16[64,1792]{1,0:T(8,128)(2,1)S(1)}, u32[]{:S(2)}, u32[]{:S(2)}) %collective-permute-start.37) | collective-permute-done | bytes 229408 | tf_op jit(solution)/shard_map/ppermute | solution.py:79
  108.9 2.0 %collective-permute-done.41.refs_1_ = bf16[64,1792]{1,0:T(8,128)(2,1)S(1)} collective-permute-done((bf16[64,1792]{1,0:T(8,128)(2,1)S(1)}, bf16[64,1792]{1,0:T(8,128)(2,1)S(1)}, u32[]{:S(2)}, u32[]{:S(2)}) %collective-permute-start.41) | collective-permute-done | bytes 229408 | tf_op jit(solution)/shard_map/ppermute | solution.py:79
  (105 shorter events, 24.3 us)
Async XLA Ops:
  1.6 11.5 %collective-permute-start.2 = (s32[1,48]{1,0:T(1,128)S(1)}, s32[1,48]{1,0:T(1,128)S(1)}, u32[]{:S(2)}, u32[]{:S(2)}) collective-permute-start(s32[1,48]{1,0:T(1,128)S(1)} %pad_add_fusion.1), channel_id=1, source_target_pairs={{0,3},{1,2},{2,1},{3,0},{4,7},{5,6},{6,5},{7,4},{8,11},{9,10},{10,... | collective-permute-start | bytes 584 | tf_op jit(solution)/shard_map/ppermute | solution.py:37
  4.0 9.1 %collective-permute-start.1 = (s32[1,48]{1,0:T(1,128)S(1)}, s32[1,48]{1,0:T(1,128)S(1)}, u32[]{:S(2)}, u32[]{:S(2)}) collective-permute-start(s32[1,48]{1,0:T(1,128)S(1)} %pad_add_fusion.1), channel_id=1, source_target_pairs={{0,2},{1,3},{2,0},{3,1},{4,6},{5,7},{6,4},{7,5},{8,10},{9,11},{10,... | collective-permute-start | bytes 584 | tf_op jit(solution)/shard_map/ppermute | solution.py:37
  4.7 8.4 %collective-permute-start = (s32[1,48]{1,0:T(1,128)S(1)}, s32[1,48]{1,0:T(1,128)S(1)}, u32[]{:S(2)}, u32[]{:S(2)}) collective-permute-start(s32[1,48]{1,0:T(1,128)S(1)} %pad_add_fusion.1), channel_id=1, source_target_pairs={{0,1},{1,0},{2,3},{3,2},{4,5},{5,4},{6,7},{7,6},{8,9},{9,8},{10,11... | collective-permute-start | bytes 584 | tf_op jit(solution)/shard_map/ppermute | solution.py:37
  13.8 6.6 %collective-permute-start.7 = (s32[4,48]{1,0:T(4,128)S(1)}, s32[4,48]{1,0:T(4,128)S(1)}, u32[]{:S(2)}, u32[]{:S(2)}) collective-permute-start(s32[4,48]{1,0:T(4,128)S(1)} %pad_add_fusion.refs_0_), channel_id=1, source_target_pairs={{0,12},{1,13},{2,14},{3,15},{4,8},{5,9},{6,10},{7,11},{8,4},{9,5},... | collective-permute-start | bytes 2312 | tf_op jit(solution)/shard_map/ppermute | solution.py:37
  18.3 11.0 %collective-permute-start.10 = (bf16[32,1792]{1,0:T(8,128)(2,1)S(1)}, bf16[32,1792]{1,0:T(8,128)(2,1)S(1)}, u32[]{:S(2)}, u32[]{:S(2)}) collective-permute-start(bf16[32,1792]{1,0:T(8,128)(2,1)S(1)} %get-tuple-element.162), channel_id=1, source_target_pairs={{0,2},{1,3},{4,0},{5,1},{8,4},{9,5},{12,8},{13,9},{14,12},{15,13},... | collective-permute-start | bytes 344072 | tf_op jit(solution)/shard_map/ppermute | solution.py:79
  20.0 9.3 %collective-permute-start.9 = (bf16[32,1792]{1,0:T(8,128)(2,1)S(1)}, bf16[32,1792]{1,0:T(8,128)(2,1)S(1)}, u32[]{:S(2)}, u32[]{:S(2)}) collective-permute-start(bf16[32,1792]{1,0:T(8,128)(2,1)S(1)} %get-tuple-element.163), channel_id=1, source_target_pairs={{0,4},{1,5},{4,8},{5,9},{8,12},{9,13},{12,14},{13,15},{14,10},{15,... | collective-permute-start | bytes 344072 | tf_op jit(solution)/shard_map/ppermute | solution.py:79
  29.9 8.5 %collective-permute-start.15 = (bf16[32,3584]{1,0:T(8,128)(2,1)S(1)}, bf16[32,3584]{1,0:T(8,128)(2,1)S(1)}, u32[]{:S(2)}, u32[]{:S(2)}) collective-permute-start(bf16[32,3584]{1,0:T(8,128)(2,1)S(1)} %get-tuple-element.158), channel_id=1, source_target_pairs={{0,2},{1,3},{4,0},{5,1},{8,4},{9,5},{12,8},{13,9},{14,12},{15,13},... | collective-permute-start | bytes 688136 | tf_op jit(solution)/shard_map/ppermute | solution.py:79
  31.5 8.5 %collective-permute-start.14 = (bf16[32,3584]{1,0:T(8,128)(2,1)S(1)}, bf16[32,3584]{1,0:T(8,128)(2,1)S(1)}, u32[]{:S(2)}, u32[]{:S(2)}) collective-permute-start(bf16[32,3584]{1,0:T(8,128)(2,1)S(1)} %get-tuple-element.159), channel_id=1, source_target_pairs={{0,4},{1,5},{4,8},{5,9},{8,12},{9,13},{12,14},{13,15},{14,10},{15,... | collective-permute-start | bytes 688136 | tf_op jit(solution)/shard_map/ppermute | solution.py:79
  33.1 9.2 %collective-permute-start.13 = (bf16[32,1792]{1,0:T(8,128)(2,1)S(1)}, bf16[32,1792]{1,0:T(8,128)(2,1)S(1)}, u32[]{:S(2)}, u32[]{:S(2)}) collective-permute-start(bf16[32,1792]{1,0:T(8,128)(2,1)S(1)} %get-tuple-element.160), channel_id=1, source_target_pairs={{0,2},{1,3},{4,0},{5,1},{8,4},{9,5},{12,8},{13,9},{14,12},{15,13},... | collective-permute-start | bytes 344072 | tf_op jit(solution)/shard_map/ppermute | solution.py:79
  34.7 7.7 %collective-permute-start.12 = (bf16[32,1792]{1,0:T(8,128)(2,1)S(1)}, bf16[32,1792]{1,0:T(8,128)(2,1)S(1)}, u32[]{:S(2)}, u32[]{:S(2)}) collective-permute-start(bf16[32,1792]{1,0:T(8,128)(2,1)S(1)} %get-tuple-element.161), channel_id=1, source_target_pairs={{0,4},{1,5},{4,8},{5,9},{8,12},{9,13},{12,14},{13,15},{14,10},{15,... | collective-permute-start | bytes 344072 | tf_op jit(solution)/shard_map/ppermute | solution.py:79
  40.1 8.5 %collective-permute-start.18 = (bf16[32,3584]{1,0:T(8,128)(2,1)S(1)}, bf16[32,3584]{1,0:T(8,128)(2,1)S(1)}, u32[]{:S(2)}, u32[]{:S(2)}) collective-permute-start(bf16[32,3584]{1,0:T(8,128)(2,1)S(1)} %add_convert_fusion.9), channel_id=1, source_target_pairs={{0,4},{1,5},{4,8},{5,9},{8,12},{9,13},{12,14},{13,15},{14,10},{15,... | collective-permute-start | bytes 688136 | tf_op jit(solution)/shard_map/ppermute | solution.py:79
  40.8 8.6 %collective-permute-start.19 = (bf16[32,3584]{1,0:T(8,128)(2,1)S(1)}, bf16[32,3584]{1,0:T(8,128)(2,1)S(1)}, u32[]{:S(2)}, u32[]{:S(2)}) collective-permute-start(bf16[32,3584]{1,0:T(8,128)(2,1)S(1)} %add_convert_fusion.8), channel_id=1, source_target_pairs={{0,2},{1,3},{4,0},{5,1},{8,4},{9,5},{12,8},{13,9},{14,12},{15,13},... | collective-permute-start | bytes 688136 | tf_op jit(solution)/shard_map/ppermute | solution.py:79
  42.5 11.5 %collective-permute-start.17 = (bf16[32,3584]{1,0:T(8,128)(2,1)S(1)}, bf16[32,3584]{1,0:T(8,128)(2,1)S(1)}, u32[]{:S(2)}, u32[]{:S(2)}) collective-permute-start(bf16[32,3584]{1,0:T(8,128)(2,1)S(1)} %get-tuple-element.156), channel_id=1, source_target_pairs={{0,2},{1,3},{4,0},{5,1},{8,4},{9,5},{12,8},{13,9},{14,12},{15,13},... | collective-permute-start | bytes 688136 | tf_op jit(solution)/shard_map/ppermute | solution.py:79
  43.1 11.0 %collective-permute-start.16 = (bf16[32,3584]{1,0:T(8,128)(2,1)S(1)}, bf16[32,3584]{1,0:T(8,128)(2,1)S(1)}, u32[]{:S(2)}, u32[]{:S(2)}) collective-permute-start(bf16[32,3584]{1,0:T(8,128)(2,1)S(1)} %get-tuple-element.157), channel_id=1, source_target_pairs={{0,4},{1,5},{4,8},{5,9},{8,12},{9,13},{12,14},{13,15},{14,10},{15,... | collective-permute-start | bytes 688136 | tf_op jit(solution)/shard_map/ppermute | solution.py:79
  49.6 8.6 %collective-permute-start.23 = (bf16[32,3584]{1,0:T(8,128)(2,1)S(1)}, bf16[32,3584]{1,0:T(8,128)(2,1)S(1)}, u32[]{:S(2)}, u32[]{:S(2)}) collective-permute-start(bf16[32,3584]{1,0:T(8,128)(2,1)S(1)} %get-tuple-element.154), channel_id=1, source_target_pairs={{0,2},{1,3},{4,0},{5,1},{8,4},{9,5},{12,8},{13,9},{14,12},{15,13},... | collective-permute-start | bytes 688136 | tf_op jit(solution)/shard_map/ppermute | solution.py:79
  51.2 7.3 %collective-permute-start.22 = (bf16[32,3584]{1,0:T(8,128)(2,1)S(1)}, bf16[32,3584]{1,0:T(8,128)(2,1)S(1)}, u32[]{:S(2)}, u32[]{:S(2)}) collective-permute-start(bf16[32,3584]{1,0:T(8,128)(2,1)S(1)} %get-tuple-element.155), channel_id=1, source_target_pairs={{0,4},{1,5},{4,8},{5,9},{8,12},{9,13},{12,14},{13,15},{14,10},{15,... | collective-permute-start | bytes 688136 | tf_op jit(solution)/shard_map/ppermute | solution.py:79
  54.2 6.8 %collective-permute-start.20 = (bf16[32,3584]{1,0:T(8,128)(2,1)S(1)}, bf16[32,3584]{1,0:T(8,128)(2,1)S(1)}, u32[]{:S(2)}, u32[]{:S(2)}) collective-permute-start(bf16[32,3584]{1,0:T(8,128)(2,1)S(1)} %add_convert_fusion.3), channel_id=1, source_target_pairs={{0,4},{1,5},{4,8},{5,9},{8,12},{9,13},{12,14},{13,15},{14,10},{15,... | collective-permute-start | bytes 688136 | tf_op jit(solution)/shard_map/ppermute | solution.py:79
  55.1 6.9 %collective-permute-start.21 = (bf16[32,3584]{1,0:T(8,128)(2,1)S(1)}, bf16[32,3584]{1,0:T(8,128)(2,1)S(1)}, u32[]{:S(2)}, u32[]{:S(2)}) collective-permute-start(bf16[32,3584]{1,0:T(8,128)(2,1)S(1)} %add_convert_fusion.2), channel_id=1, source_target_pairs={{0,2},{1,3},{4,0},{5,1},{8,4},{9,5},{12,8},{13,9},{14,12},{15,13},... | collective-permute-start | bytes 688136 | tf_op jit(solution)/shard_map/ppermute | solution.py:79
  62.2 6.6 %collective-permute-start.25 = (bf16[32,3584]{1,0:T(8,128)(2,1)S(1)}, bf16[32,3584]{1,0:T(8,128)(2,1)S(1)}, u32[]{:S(2)}, u32[]{:S(2)}) collective-permute-start(bf16[32,3584]{1,0:T(8,128)(2,1)S(1)} %get-tuple-element.152), channel_id=1, source_target_pairs={{0,2},{1,3},{4,0},{5,1},{8,4},{9,5},{12,8},{13,9},{14,12},{15,13},... | collective-permute-start | bytes 688136 | tf_op jit(solution)/shard_map/ppermute | solution.py:79
  63.5 7.8 %collective-permute-start.24 = (bf16[32,3584]{1,0:T(8,128)(2,1)S(1)}, bf16[32,3584]{1,0:T(8,128)(2,1)S(1)}, u32[]{:S(2)}, u32[]{:S(2)}) collective-permute-start(bf16[32,3584]{1,0:T(8,128)(2,1)S(1)} %get-tuple-element.153), channel_id=1, source_target_pairs={{0,4},{1,5},{4,8},{5,9},{8,12},{9,13},{12,14},{13,15},{14,10},{15,... | collective-permute-start | bytes 688136 | tf_op jit(solution)/shard_map/ppermute | solution.py:79
  72.9 8.7 %collective-permute-start.26 = (bf16[64,3584]{1,0:T(8,128)(2,1)S(1)}, bf16[64,3584]{1,0:T(8,128)(2,1)S(1)}, u32[]{:S(2)}, u32[]{:S(2)}) collective-permute-start(bf16[64,3584]{1,0:T(8,128)(2,1)S(1)} %bitcast.4), channel_id=1, source_target_pairs={{0,4},{1,5},{4,8},{5,9},{8,12},{9,13},{12,14},{13,15},{14,10},{15,... | collective-permute-start | bytes 1376264 | tf_op jit(solution)/shard_map/ppermute | solution.py:79
  74.5 8.9 %collective-permute-start.28 = (bf16[64,3584]{1,0:T(8,128)(2,1)S(1)}, bf16[64,3584]{1,0:T(8,128)(2,1)S(1)}, u32[]{:S(2)}, u32[]{:S(2)}) collective-permute-start(bf16[64,3584]{1,0:T(8,128)(2,1)S(1)} %bitcast.5), channel_id=1, source_target_pairs={{0,2},{1,3},{4,0},{5,1},{8,4},{9,5},{12,8},{13,9},{14,12},{15,13},... | collective-permute-start | bytes 1376264 | tf_op jit(solution)/shard_map/ppermute | solution.py:79
  81.7 10.3 %collective-permute-start.27 = (bf16[64,3584]{1,0:T(8,128)(2,1)S(1)}, bf16[64,3584]{1,0:T(8,128)(2,1)S(1)}, u32[]{:S(2)}, u32[]{:S(2)}) collective-permute-start(bf16[64,3584]{1,0:T(8,128)(2,1)S(1)} %collective-permute-done.26.refs_0_), channel_id=1, source_target_pairs={{0,4},{1,5},{4,8},{5,9},{8,12},{9,13},{12,14},{13,15},{14,10},{15,... | collective-permute-start | bytes 1376264 | tf_op jit(solution)/shard_map/ppermute | solution.py:79
  83.4 10.5 %collective-permute-start.31 = (bf16[64,3584]{1,0:T(8,128)(2,1)S(1)}, bf16[64,3584]{1,0:T(8,128)(2,1)S(1)}, u32[]{:S(2)}, u32[]{:S(2)}) collective-permute-start(bf16[64,3584]{1,0:T(8,128)(2,1)S(1)} %collective-permute-done.28.refs_1_), channel_id=1, source_target_pairs={{0,2},{1,3},{4,0},{5,1},{8,4},{9,5},{12,8},{13,9},{14,12},{15,13},... | collective-permute-start | bytes 1376264 | tf_op jit(solution)/shard_map/ppermute | solution.py:79
  83.7 10.4 %collective-permute-start.33 = (bf16[64,3584]{1,0:T(8,128)(2,1)S(1)}, bf16[64,3584]{1,0:T(8,128)(2,1)S(1)}, u32[]{:S(2)}, u32[]{:S(2)}) collective-permute-start(bf16[64,3584]{1,0:T(8,128)(2,1)S(1)} %collective-permute-done.28.refs_1_), channel_id=1, source_target_pairs={{0,1},{1,0},{2,3},{3,2},{4,5},{5,4},{6,7},{7,6},{8,9},{9,8},{10,11... | collective-permute-start | bytes 1376264 | tf_op jit(solution)/shard_map/ppermute | solution.py:37
  83.8 11.0 %collective-permute-start.32 = (bf16[64,3584]{1,0:T(8,128)(2,1)S(1)}, bf16[64,3584]{1,0:T(8,128)(2,1)S(1)}, u32[]{:S(2)}, u32[]{:S(2)}) collective-permute-start(bf16[64,3584]{1,0:T(8,128)(2,1)S(1)} %collective-permute-done.26.refs_0_), channel_id=1, source_target_pairs={{0,1},{1,0},{2,3},{3,2},{4,5},{5,4},{6,7},{7,6},{8,9},{9,8},{10,11... | collective-permute-start | bytes 1376264 | tf_op jit(solution)/shard_map/ppermute | solution.py:37
  92.0 10.6 %collective-permute-start.30 = (bf16[64,3584]{1,0:T(8,128)(2,1)S(1)}, bf16[64,3584]{1,0:T(8,128)(2,1)S(1)}, u32[]{:S(2)}, u32[]{:S(2)}) collective-permute-start(bf16[64,3584]{1,0:T(8,128)(2,1)S(1)} %collective-permute-done.27.refs_0_), channel_id=1, source_target_pairs={{0,4},{1,5},{4,8},{5,9},{8,12},{9,13},{12,14},{13,15},{14,10},{15,... | collective-permute-start | bytes 1376264 | tf_op jit(solution)/shard_map/ppermute | solution.py:79
  93.9 10.5 %collective-permute-start.35 = (bf16[64,3584]{1,0:T(8,128)(2,1)S(1)}, bf16[64,3584]{1,0:T(8,128)(2,1)S(1)}, u32[]{:S(2)}, u32[]{:S(2)}) collective-permute-start(bf16[64,3584]{1,0:T(8,128)(2,1)S(1)} %collective-permute-done.31.refs_1_), channel_id=1, source_target_pairs={{0,2},{1,3},{4,0},{5,1},{8,4},{9,5},{12,8},{13,9},{14,12},{15,13},... | collective-permute-start | bytes 1376264 | tf_op jit(solution)/shard_map/ppermute | solution.py:79
  94.2 10.8 %collective-permute-start.39 = (bf16[64,3584]{1,0:T(8,128)(2,1)S(1)}, bf16[64,3584]{1,0:T(8,128)(2,1)S(1)}, u32[]{:S(2)}, u32[]{:S(2)}) collective-permute-start(bf16[64,3584]{1,0:T(8,128)(2,1)S(1)} %collective-permute-done.31.refs_1_), channel_id=1, source_target_pairs={{0,1},{1,0},{2,3},{3,2},{4,5},{5,4},{6,7},{7,6},{8,9},{9,8},{10,11... | collective-permute-start | bytes 1376264 | tf_op jit(solution)/shard_map/ppermute | solution.py:37
  94.2 11.3 %collective-permute-start.38 = (bf16[64,3584]{1,0:T(8,128)(2,1)S(1)}, bf16[64,3584]{1,0:T(8,128)(2,1)S(1)}, u32[]{:S(2)}, u32[]{:S(2)}) collective-permute-start(bf16[64,3584]{1,0:T(8,128)(2,1)S(1)} %collective-permute-done.27.refs_0_), channel_id=1, source_target_pairs={{0,1},{1,0},{2,3},{3,2},{4,5},{5,4},{6,7},{7,6},{8,9},{9,8},{10,11... | collective-permute-start | bytes 1376264 | tf_op jit(solution)/shard_map/ppermute | solution.py:37
  105.0 7.4 %collective-permute-start.36 = (bf16[64,3584]{1,0:T(8,128)(2,1)S(1)}, bf16[64,3584]{1,0:T(8,128)(2,1)S(1)}, u32[]{:S(2)}, u32[]{:S(2)}) collective-permute-start(bf16[64,3584]{1,0:T(8,128)(2,1)S(1)} %collective-permute-done.35.refs_1_), channel_id=1, source_target_pairs={{0,1},{1,0},{2,3},{3,2},{4,5},{5,4},{6,7},{7,6},{8,9},{9,8},{10,11... | collective-permute-start | bytes 1376264 | tf_op jit(solution)/shard_map/ppermute | solution.py:37
  105.0 7.4 %collective-permute-start.34 = (bf16[64,3584]{1,0:T(8,128)(2,1)S(1)}, bf16[64,3584]{1,0:T(8,128)(2,1)S(1)}, u32[]{:S(2)}, u32[]{:S(2)}) collective-permute-start(bf16[64,3584]{1,0:T(8,128)(2,1)S(1)} %collective-permute-done.30.refs_0_), channel_id=1, source_target_pairs={{0,1},{1,0},{2,3},{3,2},{4,5},{5,4},{6,7},{7,6},{8,9},{9,8},{10,11... | collective-permute-start | bytes 1376264 | tf_op jit(solution)/shard_map/ppermute | solution.py:37
  (23 other events, 338.0 us)

commit v20 on v18

--- a/solution.py
+++ b/solution.py
@@ -181,7 +181,7 @@
     tokens, latents = coef.shape
     width = right.shape[1]
     part = latents // 4
-    pieces, cuts = 4, 4
+    pieces, cuts = 2, 8
     anywhere = pl.BlockSpec(memory_space=pl.ANY)
     return pl.pallas_call(
         functools.partial(stream_kernel, size, rows),

time: 110 us -> 110 us (level)
  no operation moved by 1% of the time
where the time goes in v20:
time: 110 us
  waiting for transfers between devices  45.5 us (41%)
  starting transfers between devices  35.1 us (32%)
  Pallas kernels  26 us (24%)
  other arithmetic  2.04 us (2%)
    ppermute x24, waiting for transfers between devices, shift(): return lax.ppermute(value, 'latent', pairs)  41.9 us
    ppermute x24, starting transfers between devices, shift(): return lax.ppermute(value, 'latent', pairs)  24.9 us
    ppermute x19, starting transfers between devices, swap(): return lax.ppermute(value, 'latent', [(i, i ^ bits) for i in range(size)])  10.2 us
    pallas_call x1, Pallas kernels, stream_product(): pl.pallas_call(functools.partial(stream_kernel, size, rows), in_specs=[pl...  8.38 us
    pallas_call x1, Pallas kernels, select_product(): pl.pallas_call(functools.partial(select_kernel, size, rows, len(table)),...  7.01 us
    pallas_call x6, Pallas kernels, place(): pl.pallas_call(functools.partial(place_kernel, plan, size, rows, count),...  6.39 us
    pallas_call x2, Pallas kernels, update(): pl.pallas_call(blocks_kernel if blocks_only else states_kernel, grid=(row...  4.2 us
    ppermute x19, waiting for transfers between devices, swap(): return lax.ppermute(value, 'latent', [(i, i ^ bits) for i in range(size)])  3.57 us
  transfers between devices with their start and end apart: 43, of which 20 were waited for; matrix products, arithmetic and copies ran while one was open for 1% of the time, Pallas kernels for 21%

profile of v20, /device:TPU:0, one launch (start us, length us, event | category | flops | bytes accessed | tf_op | source)
XLA Modules:
  0.0 109.8 jit_solution(4911736727288029945)
XLA Ops:
  1.6 2.5 %collective-permute-start.2 = (s32[1,48]{1,0:T(1,128)S(1)}, s32[1,48]{1,0:T(1,128)S(1)}, u32[]{:S(2)}, u32[]{:S(2)}) collective-permute-start(s32[1,48]{1,0:T(1,128)S(1)} %pad_add_fusion.1), channel_id=1, source_target_pairs={{0,3},{1,2},{2,1},{3,0},{4,7},{5,6},{6,5},{7,4},{8,11},{9,10},{10,... | collective-permute-start | bytes 584 | tf_op jit(solution)/shard_map/ppermute | solution.py:37
  4.7 8.4 %product.1 = (bf16[128,3584]{1,0:T(8,128)(2,1)S(1)}, bf16[128,3584]{1,0:T(8,128)(2,1)S(1)}, bf16[128,3584]{1,0:T(8,128)(2,1)S(1)}, bf16[128,3584]{1,0:T(8,128)(2,1)S(1)}) custom-call(bf16[1024,512]{1,0:T(8,128)(2,1)} %coef_ref.1, bf16[1024,3584]{1,0:T(8,128)(2,1)} %right_hbm.1), custom_call_target="tpu_custom_call" | custom-call | flops 3758096384 | bytes 12058624 | tf_op jit(solution)/shard_map/product/pallas_call | solution.py:186
  13.8 3.8 %collective-permute-start.7 = (s32[4,48]{1,0:T(4,128)S(1)}, s32[4,48]{1,0:T(4,128)S(1)}, u32[]{:S(2)}, u32[]{:S(2)}) collective-permute-start(s32[4,48]{1,0:T(4,128)S(1)} %pad_add_fusion.refs_0_), channel_id=1, source_target_pairs={{0,12},{1,13},{2,14},{3,15},{4,8},{5,9},{6,10},{7,11},{8,4},{9,5},... | collective-permute-start | bytes 2312 | tf_op jit(solution)/shard_map/ppermute | solution.py:37
  18.3 1.8 %collective-permute-start.10 = (bf16[32,1792]{1,0:T(8,128)(2,1)S(1)}, bf16[32,1792]{1,0:T(8,128)(2,1)S(1)}, u32[]{:S(2)}, u32[]{:S(2)}) collective-permute-start(bf16[32,1792]{1,0:T(8,128)(2,1)S(1)} %get-tuple-element.158), channel_id=1, source_target_pairs={{0,2},{1,3},{4,0},{5,1},{8,4},{9,5},{12,8},{13,9},{14,12},{15,13},... | collective-permute-start | bytes 344072 | tf_op jit(solution)/shard_map/ppermute | solution.py:79
  20.4 1.8 %collective-permute-done.6.refs_2_ = s32[4,48]{1,0:T(4,128)S(1)} collective-permute-done((s32[4,48]{1,0:T(4,128)S(1)}, s32[4,48]{1,0:T(4,128)S(1)}, u32[]{:S(2)}, u32[]{:S(2)}) %collective-permute-start.6) | collective-permute-done | bytes 800 | tf_op jit(solution)/shard_map/ppermute | solution.py:37
  22.2 7.0 %select_product.1 = (bf16[128,3584]{1,0:T(8,128)(2,1)S(1)}, bf16[128,3584]{1,0:T(8,128)(2,1)S(1)}, bf16[128,3584]{1,0:T(8,128)(2,1)S(1)}, bf16[128,3584]{1,0:T(8,128)(2,1)S(1)}, s32[32,1]{1,0:T(8,128)S(1)}) custom-call(bf16[1024,512]{1,0:T(8,128)(2,1)S(1)} %copy-done.6, bf16[1024,3584]{1,0:T(8,128)(2,1)S(1)} %bitcast.9, s32[2,16]{1,0:T(2,128)S(1)} %bitcast.10, ...), custom_call_target="tpu_custom_call" | custom-call | flops 3758096384 | bytes 12058624 | tf_op jit(solution)/shard_map/select_product/pallas_call | solution.py:237
  30.0 1.6 %collective-permute-start.15 = (bf16[32,3584]{1,0:T(8,128)(2,1)S(1)}, bf16[32,3584]{1,0:T(8,128)(2,1)S(1)}, u32[]{:S(2)}, u32[]{:S(2)}) collective-permute-start(bf16[32,3584]{1,0:T(8,128)(2,1)S(1)} %get-tuple-element.154), channel_id=1, source_target_pairs={{0,2},{1,3},{4,0},{5,1},{8,4},{9,5},{12,8},{13,9},{14,12},{15,13},... | collective-permute-start | bytes 688136 | tf_op jit(solution)/shard_map/ppermute | solution.py:79
  33.2 1.6 %collective-permute-start.13 = (bf16[32,1792]{1,0:T(8,128)(2,1)S(1)}, bf16[32,1792]{1,0:T(8,128)(2,1)S(1)}, u32[]{:S(2)}, u32[]{:S(2)}) collective-permute-start(bf16[32,1792]{1,0:T(8,128)(2,1)S(1)} %get-tuple-element.156), channel_id=1, source_target_pairs={{0,2},{1,3},{4,0},{5,1},{8,4},{9,5},{12,8},{13,9},{14,12},{15,13},... | collective-permute-start | bytes 344072 | tf_op jit(solution)/shard_map/ppermute | solution.py:79
  35.2 3.2 %collective-permute-done.15 = bf16[32,3584]{1,0:T(8,128)(2,1)S(1)} collective-permute-done((bf16[32,3584]{1,0:T(8,128)(2,1)S(1)}, bf16[32,3584]{1,0:T(8,128)(2,1)S(1)}, u32[]{:S(2)}, u32[]{:S(2)}) %collective-permute-start.15) | collective-permute-done | bytes 229408 | tf_op jit(solution)/shard_map/ppermute | solution.py:79
  38.5 1.6 %collective-permute-done.14 = bf16[32,3584]{1,0:T(8,128)(2,1)S(1)} collective-permute-done((bf16[32,3584]{1,0:T(8,128)(2,1)S(1)}, bf16[32,3584]{1,0:T(8,128)(2,1)S(1)}, u32[]{:S(2)}, u32[]{:S(2)}) %collective-permute-start.14) | collective-permute-done | bytes 229408 | tf_op jit(solution)/shard_map/ppermute | solution.py:79
  40.8 1.6 %collective-permute-start.19 = (bf16[32,3584]{1,0:T(8,128)(2,1)S(1)}, bf16[32,3584]{1,0:T(8,128)(2,1)S(1)}, u32[]{:S(2)}, u32[]{:S(2)}) collective-permute-start(bf16[32,3584]{1,0:T(8,128)(2,1)S(1)} %add_convert_fusion.8), channel_id=1, source_target_pairs={{0,2},{1,3},{4,0},{5,1},{8,4},{9,5},{12,8},{13,9},{14,12},{15,13},... | collective-permute-start | bytes 688136 | tf_op jit(solution)/shard_map/ppermute | solution.py:79
  43.1 1.6 %collective-permute-start.16 = (bf16[32,3584]{1,0:T(8,128)(2,1)S(1)}, bf16[32,3584]{1,0:T(8,128)(2,1)S(1)}, u32[]{:S(2)}, u32[]{:S(2)}) collective-permute-start(bf16[32,3584]{1,0:T(8,128)(2,1)S(1)} %get-tuple-element.153), channel_id=1, source_target_pairs={{0,4},{1,5},{4,8},{5,9},{8,12},{9,13},{12,14},{13,15},{14,10},{15,... | collective-permute-start | bytes 688136 | tf_op jit(solution)/shard_map/ppermute | solution.py:79
  44.6 4.0 %collective-permute-done.18 = bf16[32,3584]{1,0:T(8,128)(2,1)S(1)} collective-permute-done((bf16[32,3584]{1,0:T(8,128)(2,1)S(1)}, bf16[32,3584]{1,0:T(8,128)(2,1)S(1)}, u32[]{:S(2)}, u32[]{:S(2)}) %collective-permute-start.18) | collective-permute-done | bytes 229408 | tf_op jit(solution)/shard_map/ppermute | solution.py:79
  48.8 2.0 %collective-permute-done.17 = bf16[32,3584]{1,0:T(8,128)(2,1)S(1)} collective-permute-done((bf16[32,3584]{1,0:T(8,128)(2,1)S(1)}, bf16[32,3584]{1,0:T(8,128)(2,1)S(1)}, u32[]{:S(2)}, u32[]{:S(2)}) %collective-permute-start.17) | collective-permute-done | bytes 229408 | tf_op jit(solution)/shard_map/ppermute | solution.py:79
  52.2 1.3 %collective-permute-start.22 = (bf16[32,3584]{1,0:T(8,128)(2,1)S(1)}, bf16[32,3584]{1,0:T(8,128)(2,1)S(1)}, u32[]{:S(2)}, u32[]{:S(2)}) collective-permute-start(bf16[32,3584]{1,0:T(8,128)(2,1)S(1)} %add_convert_fusion.1), channel_id=1, source_target_pairs={{0,2},{1,3},{4,0},{5,1},{8,4},{9,5},{12,8},{13,9},{14,12},{15,13},... | collective-permute-start | bytes 688136 | tf_op jit(solution)/shard_map/ppermute | solution.py:79
  55.5 4.2 %collective-permute-done.20 = bf16[32,3584]{1,0:T(8,128)(2,1)S(1)} collective-permute-done((bf16[32,3584]{1,0:T(8,128)(2,1)S(1)}, bf16[32,3584]{1,0:T(8,128)(2,1)S(1)}, u32[]{:S(2)}, u32[]{:S(2)}) %collective-permute-start.20) | collective-permute-done | bytes 229408 | tf_op jit(solution)/shard_map/ppermute | solution.py:79
  60.9 1.3 %collective-permute-start.23 = (bf16[32,3584]{1,0:T(8,128)(2,1)S(1)}, bf16[32,3584]{1,0:T(8,128)(2,1)S(1)}, u32[]{:S(2)}, u32[]{:S(2)}) collective-permute-start(bf16[32,3584]{1,0:T(8,128)(2,1)S(1)} %get-tuple-element.148), channel_id=1, source_target_pairs={{0,2},{1,3},{4,0},{5,1},{8,4},{9,5},{12,8},{13,9},{14,12},{15,13},... | collective-permute-start | bytes 688136 | tf_op jit(solution)/shard_map/ppermute | solution.py:79
  63.0 1.6 %collective-permute-done.25.refs_14_ = bf16[32,3584]{1,0:T(8,128)(2,1)S(1)} collective-permute-done((bf16[32,3584]{1,0:T(8,128)(2,1)S(1)}, bf16[32,3584]{1,0:T(8,128)(2,1)S(1)}, u32[]{:S(2)}, u32[]{:S(2)}) %collective-permute-start.25) | collective-permute-done | bytes 229408 | tf_op jit(solution)/shard_map/ppermute | solution.py:79
  64.6 2.5 %collective-permute-done.23.refs_10_ = bf16[32,3584]{1,0:T(8,128)(2,1)S(1)} collective-permute-done((bf16[32,3584]{1,0:T(8,128)(2,1)S(1)}, bf16[32,3584]{1,0:T(8,128)(2,1)S(1)}, u32[]{:S(2)}, u32[]{:S(2)}) %collective-permute-start.23) | collective-permute-done | bytes 229408 | tf_op jit(solution)/shard_map/ppermute | solution.py:79
  68.3 1.6 %blocks.1 = bf16[2,32,3584]{2,1,0:T(8,128)(2,1)S(1)} custom-call(s32[32,1]{1,0:T(8,128)S(1)} %get-tuple-element.85.refs_0_, f32[32,3584]{1,0:T(8,128)S(1)} %copy-done, f32[32,3584]{1,0:T(8,128)S(1)} %copy-done.1, f32[32,3584]{1,0:T(8,128)S(1)} %copy-done.2, f32[32,3584]{1,0:T(8,128)S(1)} %copy-done.3, f32[32,3584]{1,0:T(8,128)S(1)} %copy-done.4, ...), custom_call_target="tpu_custom_call" | custom-call | flops 1146880 | bytes 1146880 | tf_op jit(solution)/shard_map/blocks/pallas_call | solution.py:307
  69.9 1.2 %collective-permute-start.26 = (bf16[64,3584]{1,0:T(8,128)(2,1)S(1)}, bf16[64,3584]{1,0:T(8,128)(2,1)S(1)}, u32[]{:S(2)}, u32[]{:S(2)}) collective-permute-start(bf16[64,3584]{1,0:T(8,128)(2,1)S(1)} %bitcast.4), channel_id=1, source_target_pairs={{0,4},{1,5},{4,8},{5,9},{8,12},{9,13},{12,14},{13,15},{14,10},{15,... | collective-permute-start | bytes 1376264 | tf_op jit(solution)/shard_map/ppermute | solution.py:79
  72.0 2.6 %states.1 = (f32[32,3584]{1,0:T(8,128)}, f32[32,3584]{1,0:T(8,128)}, f32[32,3584]{1,0:T(8,128)}, f32[32,3584]{1,0:T(8,128)}, f32[32,3584]{1,0:T(8,128)}, /*index=5*/f32[32,3584]{1,0:T(8,128)}) custom-call(s32[32,1]{1,0:T(8,128)S(1)} %get-tuple-element.85.refs_0_, f32[32,3584]{1,0:T(8,128)S(1)} %copy-done, f32[32,3584]{1,0:T(8,128)S(1)} %copy-done.1, ...), custom_call_target="tpu_custom_call" | custom-call | flops 1146880 | bytes 1146880 | tf_op jit(solution)/shard_map/states/pallas_call | solution.py:307
  75.4 3.1 %collective-permute-done.26.refs_0_ = bf16[64,3584]{1,0:T(8,128)(2,1)S(1)} collective-permute-done((bf16[64,3584]{1,0:T(8,128)(2,1)S(1)}, bf16[64,3584]{1,0:T(8,128)(2,1)S(1)}, u32[]{:S(2)}, u32[]{:S(2)}) %collective-permute-start.26) | collective-permute-done | bytes 458784 | tf_op jit(solution)/shard_map/ppermute | solution.py:79
  78.5 1.2 %collective-permute-start.27 = (bf16[64,3584]{1,0:T(8,128)(2,1)S(1)}, bf16[64,3584]{1,0:T(8,128)(2,1)S(1)}, u32[]{:S(2)}, u32[]{:S(2)}) collective-permute-start(bf16[64,3584]{1,0:T(8,128)(2,1)S(1)} %collective-permute-done.26.refs_0_), channel_id=1, source_target_pairs={{0,4},{1,5},{4,8},{5,9},{8,12},{9,13},{12,14},{13,15},{14,10},{15,... | collective-permute-start | bytes 1376264 | tf_op jit(solution)/shard_map/ppermute | solution.py:79
  82.2 6.9 %collective-permute-done.27.refs_0_ = bf16[64,3584]{1,0:T(8,128)(2,1)S(1)} collective-permute-done((bf16[64,3584]{1,0:T(8,128)(2,1)S(1)}, bf16[64,3584]{1,0:T(8,128)(2,1)S(1)}, u32[]{:S(2)}, u32[]{:S(2)}) %collective-permute-start.27) | collective-permute-done | bytes 458784 | tf_op jit(solution)/shard_map/ppermute | solution.py:79
  89.1 1.2 %collective-permute-start.30 = (bf16[64,3584]{1,0:T(8,128)(2,1)S(1)}, bf16[64,3584]{1,0:T(8,128)(2,1)S(1)}, u32[]{:S(2)}, u32[]{:S(2)}) collective-permute-start(bf16[64,3584]{1,0:T(8,128)(2,1)S(1)} %collective-permute-done.27.refs_0_), channel_id=1, source_target_pairs={{0,4},{1,5},{4,8},{5,9},{8,12},{9,13},{12,14},{13,15},{14,10},{15,... | collective-permute-start | bytes 1376264 | tf_op jit(solution)/shard_map/ppermute | solution.py:79
  91.8 1.3 %place.8 = (bf16[512,3584]{1,0:T(8,128)(2,1)}, bf16[512,3584]{1,0:T(8,128)(2,1)}) custom-call(bf16[64,3584]{1,0:T(8,128)(2,1)S(1)} %collective-permute-done.27.refs_0_, bf16[64,3584]{1,0:T(8,128)(2,1)S(1)} %collective-permute-done.31.refs_1_, bf16[64,3584]{1,0:T(8,128)(2,1)S(1)} %collective-permute-done.32.refs_2_, ...), custom_call_target="tpu_custom_call", output_to_operand_aliasing={{0}: (4, {}), {1}: (5, {})} | custom-call | bytes 3670016 | tf_op jit(solution)/shard_map/place/pallas_call | solution.py:342
  93.1 6.7 %collective-permute-done.30.refs_0_ = bf16[64,3584]{1,0:T(8,128)(2,1)S(1)} collective-permute-done((bf16[64,3584]{1,0:T(8,128)(2,1)S(1)}, bf16[64,3584]{1,0:T(8,128)(2,1)S(1)}, u32[]{:S(2)}, u32[]{:S(2)}) %collective-permute-start.30) | collective-permute-done | bytes 458784 | tf_op jit(solution)/shard_map/ppermute | solution.py:79
  99.8 1.2 %collective-permute-start.37 = (bf16[64,1792]{1,0:T(8,128)(2,1)S(1)}, bf16[64,1792]{1,0:T(8,128)(2,1)S(1)}, u32[]{:S(2)}, u32[]{:S(2)}) collective-permute-start(bf16[64,1792]{1,0:T(8,128)(2,1)S(1)} %slice.134), channel_id=1, source_target_pairs={{0,4},{1,5},{4,8},{5,9},{8,12},{9,13},{12,14},{13,15},{14,10},{15,... | collective-permute-start | bytes 688136 | tf_op jit(solution)/shard_map/ppermute | solution.py:79
  102.5 1.3 %place.9 = (bf16[512,3584]{1,0:T(8,128)(2,1)}, bf16[512,3584]{1,0:T(8,128)(2,1)}) custom-call(bf16[64,3584]{1,0:T(8,128)(2,1)S(1)} %collective-permute-done.30.refs_0_, bf16[64,3584]{1,0:T(8,128)(2,1)S(1)} %collective-permute-done.35.refs_1_, bf16[64,3584]{1,0:T(8,128)(2,1)S(1)} %collective-permute-done.38.refs_2_, ...), custom_call_target="tpu_custom_call", output_to_operand_aliasing={{0}: (4, {}), {1}: (5, {})} | custom-call | bytes 3670016 | tf_op jit(solution)/shard_map/place/pallas_call | solution.py:342
  103.7 2.1 %collective-permute-done.37.refs_0_ = bf16[64,1792]{1,0:T(8,128)(2,1)S(1)} collective-permute-done((bf16[64,1792]{1,0:T(8,128)(2,1)S(1)}, bf16[64,1792]{1,0:T(8,128)(2,1)S(1)}, u32[]{:S(2)}, u32[]{:S(2)}) %collective-permute-start.37) | collective-permute-done | bytes 229408 | tf_op jit(solution)/shard_map/ppermute | solution.py:79
  105.9 1.3 %collective-permute-done.41.refs_1_ = bf16[64,1792]{1,0:T(8,128)(2,1)S(1)} collective-permute-done((bf16[64,1792]{1,0:T(8,128)(2,1)S(1)}, bf16[64,1792]{1,0:T(8,128)(2,1)S(1)}, u32[]{:S(2)}, u32[]{:S(2)}) %collective-permute-start.41) | collective-permute-done | bytes 229408 | tf_op jit(solution)/shard_map/ppermute | solution.py:79
  (105 shorter events, 24.1 us)
Async XLA Ops:
  1.6 11.5 %collective-permute-start.2 = (s32[1,48]{1,0:T(1,128)S(1)}, s32[1,48]{1,0:T(1,128)S(1)}, u32[]{:S(2)}, u32[]{:S(2)}) collective-permute-start(s32[1,48]{1,0:T(1,128)S(1)} %pad_add_fusion.1), channel_id=1, source_target_pairs={{0,3},{1,2},{2,1},{3,0},{4,7},{5,6},{6,5},{7,4},{8,11},{9,10},{10,... | collective-permute-start | bytes 584 | tf_op jit(solution)/shard_map/ppermute | solution.py:37
  4.0 9.1 %collective-permute-start.1 = (s32[1,48]{1,0:T(1,128)S(1)}, s32[1,48]{1,0:T(1,128)S(1)}, u32[]{:S(2)}, u32[]{:S(2)}) collective-permute-start(s32[1,48]{1,0:T(1,128)S(1)} %pad_add_fusion.1), channel_id=1, source_target_pairs={{0,2},{1,3},{2,0},{3,1},{4,6},{5,7},{6,4},{7,5},{8,10},{9,11},{10,... | collective-permute-start | bytes 584 | tf_op jit(solution)/shard_map/ppermute | solution.py:37
  4.7 8.5 %collective-permute-start = (s32[1,48]{1,0:T(1,128)S(1)}, s32[1,48]{1,0:T(1,128)S(1)}, u32[]{:S(2)}, u32[]{:S(2)}) collective-permute-start(s32[1,48]{1,0:T(1,128)S(1)} %pad_add_fusion.1), channel_id=1, source_target_pairs={{0,1},{1,0},{2,3},{3,2},{4,5},{5,4},{6,7},{7,6},{8,9},{9,8},{10,11... | collective-permute-start | bytes 584 | tf_op jit(solution)/shard_map/ppermute | solution.py:37
  13.8 6.6 %collective-permute-start.7 = (s32[4,48]{1,0:T(4,128)S(1)}, s32[4,48]{1,0:T(4,128)S(1)}, u32[]{:S(2)}, u32[]{:S(2)}) collective-permute-start(s32[4,48]{1,0:T(4,128)S(1)} %pad_add_fusion.refs_0_), channel_id=1, source_target_pairs={{0,12},{1,13},{2,14},{3,15},{4,8},{5,9},{6,10},{7,11},{8,4},{9,5},... | collective-permute-start | bytes 2312 | tf_op jit(solution)/shard_map/ppermute | solution.py:37
  18.3 11.0 %collective-permute-start.10 = (bf16[32,1792]{1,0:T(8,128)(2,1)S(1)}, bf16[32,1792]{1,0:T(8,128)(2,1)S(1)}, u32[]{:S(2)}, u32[]{:S(2)}) collective-permute-start(bf16[32,1792]{1,0:T(8,128)(2,1)S(1)} %get-tuple-element.158), channel_id=1, source_target_pairs={{0,2},{1,3},{4,0},{5,1},{8,4},{9,5},{12,8},{13,9},{14,12},{15,13},... | collective-permute-start | bytes 344072 | tf_op jit(solution)/shard_map/ppermute | solution.py:79
  20.0 9.3 %collective-permute-start.9 = (bf16[32,1792]{1,0:T(8,128)(2,1)S(1)}, bf16[32,1792]{1,0:T(8,128)(2,1)S(1)}, u32[]{:S(2)}, u32[]{:S(2)}) collective-permute-start(bf16[32,1792]{1,0:T(8,128)(2,1)S(1)} %get-tuple-element.159), channel_id=1, source_target_pairs={{0,4},{1,5},{4,8},{5,9},{8,12},{9,13},{12,14},{13,15},{14,10},{15,... | collective-permute-start | bytes 344072 | tf_op jit(solution)/shard_map/ppermute | solution.py:79
  30.0 8.5 %collective-permute-start.15 = (bf16[32,3584]{1,0:T(8,128)(2,1)S(1)}, bf16[32,3584]{1,0:T(8,128)(2,1)S(1)}, u32[]{:S(2)}, u32[]{:S(2)}) collective-permute-start(bf16[32,3584]{1,0:T(8,128)(2,1)S(1)} %get-tuple-element.154), channel_id=1, source_target_pairs={{0,2},{1,3},{4,0},{5,1},{8,4},{9,5},{12,8},{13,9},{14,12},{15,13},... | collective-permute-start | bytes 688136 | tf_op jit(solution)/shard_map/ppermute | solution.py:79
  31.5 8.5 %collective-permute-start.14 = (bf16[32,3584]{1,0:T(8,128)(2,1)S(1)}, bf16[32,3584]{1,0:T(8,128)(2,1)S(1)}, u32[]{:S(2)}, u32[]{:S(2)}) collective-permute-start(bf16[32,3584]{1,0:T(8,128)(2,1)S(1)} %get-tuple-element.155), channel_id=1, source_target_pairs={{0,4},{1,5},{4,8},{5,9},{8,12},{9,13},{12,14},{13,15},{14,10},{15,... | collective-permute-start | bytes 688136 | tf_op jit(solution)/shard_map/ppermute | solution.py:79
  33.2 9.2 %collective-permute-start.13 = (bf16[32,1792]{1,0:T(8,128)(2,1)S(1)}, bf16[32,1792]{1,0:T(8,128)(2,1)S(1)}, u32[]{:S(2)}, u32[]{:S(2)}) collective-permute-start(bf16[32,1792]{1,0:T(8,128)(2,1)S(1)} %get-tuple-element.156), channel_id=1, source_target_pairs={{0,2},{1,3},{4,0},{5,1},{8,4},{9,5},{12,8},{13,9},{14,12},{15,13},... | collective-permute-start | bytes 344072 | tf_op jit(solution)/shard_map/ppermute | solution.py:79
  34.7 7.7 %collective-permute-start.12 = (bf16[32,1792]{1,0:T(8,128)(2,1)S(1)}, bf16[32,1792]{1,0:T(8,128)(2,1)S(1)}, u32[]{:S(2)}, u32[]{:S(2)}) collective-permute-start(bf16[32,1792]{1,0:T(8,128)(2,1)S(1)} %get-tuple-element.157), channel_id=1, source_target_pairs={{0,4},{1,5},{4,8},{5,9},{8,12},{9,13},{12,14},{13,15},{14,10},{15,... | collective-permute-start | bytes 344072 | tf_op jit(solution)/shard_map/ppermute | solution.py:79
  40.1 8.5 %collective-permute-start.18 = (bf16[32,3584]{1,0:T(8,128)(2,1)S(1)}, bf16[32,3584]{1,0:T(8,128)(2,1)S(1)}, u32[]{:S(2)}, u32[]{:S(2)}) collective-permute-start(bf16[32,3584]{1,0:T(8,128)(2,1)S(1)} %add_convert_fusion.9), channel_id=1, source_target_pairs={{0,4},{1,5},{4,8},{5,9},{8,12},{9,13},{12,14},{13,15},{14,10},{15,... | collective-permute-start | bytes 688136 | tf_op jit(solution)/shard_map/ppermute | solution.py:79
  40.8 7.8 %collective-permute-start.19 = (bf16[32,3584]{1,0:T(8,128)(2,1)S(1)}, bf16[32,3584]{1,0:T(8,128)(2,1)S(1)}, u32[]{:S(2)}, u32[]{:S(2)}) collective-permute-start(bf16[32,3584]{1,0:T(8,128)(2,1)S(1)} %add_convert_fusion.8), channel_id=1, source_target_pairs={{0,2},{1,3},{4,0},{5,1},{8,4},{9,5},{12,8},{13,9},{14,12},{15,13},... | collective-permute-start | bytes 688136 | tf_op jit(solution)/shard_map/ppermute | solution.py:79
  42.6 8.2 %collective-permute-start.17 = (bf16[32,3584]{1,0:T(8,128)(2,1)S(1)}, bf16[32,3584]{1,0:T(8,128)(2,1)S(1)}, u32[]{:S(2)}, u32[]{:S(2)}) collective-permute-start(bf16[32,3584]{1,0:T(8,128)(2,1)S(1)} %get-tuple-element.152), channel_id=1, source_target_pairs={{0,2},{1,3},{4,0},{5,1},{8,4},{9,5},{12,8},{13,9},{14,12},{15,13},... | collective-permute-start | bytes 688136 | tf_op jit(solution)/shard_map/ppermute | solution.py:79
  43.1 8.0 %collective-permute-start.16 = (bf16[32,3584]{1,0:T(8,128)(2,1)S(1)}, bf16[32,3584]{1,0:T(8,128)(2,1)S(1)}, u32[]{:S(2)}, u32[]{:S(2)}) collective-permute-start(bf16[32,3584]{1,0:T(8,128)(2,1)S(1)} %get-tuple-element.153), channel_id=1, source_target_pairs={{0,4},{1,5},{4,8},{5,9},{8,12},{9,13},{12,14},{13,15},{14,10},{15,... | collective-permute-start | bytes 688136 | tf_op jit(solution)/shard_map/ppermute | solution.py:79
  51.2 8.5 %collective-permute-start.20 = (bf16[32,3584]{1,0:T(8,128)(2,1)S(1)}, bf16[32,3584]{1,0:T(8,128)(2,1)S(1)}, u32[]{:S(2)}, u32[]{:S(2)}) collective-permute-start(bf16[32,3584]{1,0:T(8,128)(2,1)S(1)} %add_convert_fusion.3), channel_id=1, source_target_pairs={{0,4},{1,5},{4,8},{5,9},{8,12},{9,13},{12,14},{13,15},{14,10},{15,... | collective-permute-start | bytes 688136 | tf_op jit(solution)/shard_map/ppermute | solution.py:79
  52.2 8.6 %collective-permute-start.22 = (bf16[32,3584]{1,0:T(8,128)(2,1)S(1)}, bf16[32,3584]{1,0:T(8,128)(2,1)S(1)}, u32[]{:S(2)}, u32[]{:S(2)}) collective-permute-start(bf16[32,3584]{1,0:T(8,128)(2,1)S(1)} %add_convert_fusion.1), channel_id=1, source_target_pairs={{0,2},{1,3},{4,0},{5,1},{8,4},{9,5},{12,8},{13,9},{14,12},{15,13},... | collective-permute-start | bytes 688136 | tf_op jit(solution)/shard_map/ppermute | solution.py:79
  53.4 11.2 %collective-permute-start.25 = (bf16[32,3584]{1,0:T(8,128)(2,1)S(1)}, bf16[32,3584]{1,0:T(8,128)(2,1)S(1)}, u32[]{:S(2)}, u32[]{:S(2)}) collective-permute-start(bf16[32,3584]{1,0:T(8,128)(2,1)S(1)} %get-tuple-element.150), channel_id=1, source_target_pairs={{0,2},{1,3},{4,0},{5,1},{8,4},{9,5},{12,8},{13,9},{14,12},{15,13},... | collective-permute-start | bytes 688136 | tf_op jit(solution)/shard_map/ppermute | solution.py:79
  54.6 10.0 %collective-permute-start.24 = (bf16[32,3584]{1,0:T(8,128)(2,1)S(1)}, bf16[32,3584]{1,0:T(8,128)(2,1)S(1)}, u32[]{:S(2)}, u32[]{:S(2)}) collective-permute-start(bf16[32,3584]{1,0:T(8,128)(2,1)S(1)} %get-tuple-element.151), channel_id=1, source_target_pairs={{0,4},{1,5},{4,8},{5,9},{8,12},{9,13},{12,14},{13,15},{14,10},{15,... | collective-permute-start | bytes 688136 | tf_op jit(solution)/shard_map/ppermute | solution.py:79
  60.9 6.1 %collective-permute-start.23 = (bf16[32,3584]{1,0:T(8,128)(2,1)S(1)}, bf16[32,3584]{1,0:T(8,128)(2,1)S(1)}, u32[]{:S(2)}, u32[]{:S(2)}) collective-permute-start(bf16[32,3584]{1,0:T(8,128)(2,1)S(1)} %get-tuple-element.148), channel_id=1, source_target_pairs={{0,2},{1,3},{4,0},{5,1},{8,4},{9,5},{12,8},{13,9},{14,12},{15,13},... | collective-permute-start | bytes 688136 | tf_op jit(solution)/shard_map/ppermute | solution.py:79
  69.9 8.5 %collective-permute-start.26 = (bf16[64,3584]{1,0:T(8,128)(2,1)S(1)}, bf16[64,3584]{1,0:T(8,128)(2,1)S(1)}, u32[]{:S(2)}, u32[]{:S(2)}) collective-permute-start(bf16[64,3584]{1,0:T(8,128)(2,1)S(1)} %bitcast.4), channel_id=1, source_target_pairs={{0,4},{1,5},{4,8},{5,9},{8,12},{9,13},{12,14},{13,15},{14,10},{15,... | collective-permute-start | bytes 1376264 | tf_op jit(solution)/shard_map/ppermute | solution.py:79
  71.2 8.6 %collective-permute-start.28 = (bf16[64,3584]{1,0:T(8,128)(2,1)S(1)}, bf16[64,3584]{1,0:T(8,128)(2,1)S(1)}, u32[]{:S(2)}, u32[]{:S(2)}) collective-permute-start(bf16[64,3584]{1,0:T(8,128)(2,1)S(1)} %bitcast.5), channel_id=1, source_target_pairs={{0,2},{1,3},{4,0},{5,1},{8,4},{9,5},{12,8},{13,9},{14,12},{15,13},... | collective-permute-start | bytes 1376264 | tf_op jit(solution)/shard_map/ppermute | solution.py:79
  74.6 6.5 %collective-permute-start.29 = (bf16[64,3584]{1,0:T(8,128)(2,1)S(1)}, bf16[64,3584]{1,0:T(8,128)(2,1)S(1)}, u32[]{:S(2)}, u32[]{:S(2)}) collective-permute-start(bf16[64,3584]{1,0:T(8,128)(2,1)S(1)} %bitcast.6), channel_id=1, source_target_pairs={{0,1},{1,0},{2,3},{3,2},{4,5},{5,4},{6,7},{7,6},{8,9},{9,8},{10,11... | collective-permute-start | bytes 1376264 | tf_op jit(solution)/shard_map/ppermute | solution.py:37
  78.5 10.7 %collective-permute-start.27 = (bf16[64,3584]{1,0:T(8,128)(2,1)S(1)}, bf16[64,3584]{1,0:T(8,128)(2,1)S(1)}, u32[]{:S(2)}, u32[]{:S(2)}) collective-permute-start(bf16[64,3584]{1,0:T(8,128)(2,1)S(1)} %collective-permute-done.26.refs_0_), channel_id=1, source_target_pairs={{0,4},{1,5},{4,8},{5,9},{8,12},{9,13},{12,14},{13,15},{14,10},{15,... | collective-permute-start | bytes 1376264 | tf_op jit(solution)/shard_map/ppermute | solution.py:79
  79.8 10.7 %collective-permute-start.31 = (bf16[64,3584]{1,0:T(8,128)(2,1)S(1)}, bf16[64,3584]{1,0:T(8,128)(2,1)S(1)}, u32[]{:S(2)}, u32[]{:S(2)}) collective-permute-start(bf16[64,3584]{1,0:T(8,128)(2,1)S(1)} %collective-permute-done.28.refs_1_), channel_id=1, source_target_pairs={{0,2},{1,3},{4,0},{5,1},{8,4},{9,5},{12,8},{13,9},{14,12},{15,13},... | collective-permute-start | bytes 1376264 | tf_op jit(solution)/shard_map/ppermute | solution.py:79
  80.6 10.7 %collective-permute-start.33 = (bf16[64,3584]{1,0:T(8,128)(2,1)S(1)}, bf16[64,3584]{1,0:T(8,128)(2,1)S(1)}, u32[]{:S(2)}, u32[]{:S(2)}) collective-permute-start(bf16[64,3584]{1,0:T(8,128)(2,1)S(1)} %collective-permute-done.28.refs_1_), channel_id=1, source_target_pairs={{0,1},{1,0},{2,3},{3,2},{4,5},{5,4},{6,7},{7,6},{8,9},{9,8},{10,11... | collective-permute-start | bytes 1376264 | tf_op jit(solution)/shard_map/ppermute | solution.py:37
  80.6 11.2 %collective-permute-start.32 = (bf16[64,3584]{1,0:T(8,128)(2,1)S(1)}, bf16[64,3584]{1,0:T(8,128)(2,1)S(1)}, u32[]{:S(2)}, u32[]{:S(2)}) collective-permute-start(bf16[64,3584]{1,0:T(8,128)(2,1)S(1)} %collective-permute-done.26.refs_0_), channel_id=1, source_target_pairs={{0,1},{1,0},{2,3},{3,2},{4,5},{5,4},{6,7},{7,6},{8,9},{9,8},{10,11... | collective-permute-start | bytes 1376264 | tf_op jit(solution)/shard_map/ppermute | solution.py:37
  89.1 10.6 %collective-permute-start.30 = (bf16[64,3584]{1,0:T(8,128)(2,1)S(1)}, bf16[64,3584]{1,0:T(8,128)(2,1)S(1)}, u32[]{:S(2)}, u32[]{:S(2)}) collective-permute-start(bf16[64,3584]{1,0:T(8,128)(2,1)S(1)} %collective-permute-done.27.refs_0_), channel_id=1, source_target_pairs={{0,4},{1,5},{4,8},{5,9},{8,12},{9,13},{12,14},{13,15},{14,10},{15,... | collective-permute-start | bytes 1376264 | tf_op jit(solution)/shard_map/ppermute | solution.py:79
  90.5 10.6 %collective-permute-start.35 = (bf16[64,3584]{1,0:T(8,128)(2,1)S(1)}, bf16[64,3584]{1,0:T(8,128)(2,1)S(1)}, u32[]{:S(2)}, u32[]{:S(2)}) collective-permute-start(bf16[64,3584]{1,0:T(8,128)(2,1)S(1)} %collective-permute-done.31.refs_1_), channel_id=1, source_target_pairs={{0,2},{1,3},{4,0},{5,1},{8,4},{9,5},{12,8},{13,9},{14,12},{15,13},... | collective-permute-start | bytes 1376264 | tf_op jit(solution)/shard_map/ppermute | solution.py:79
  91.3 10.7 %collective-permute-start.39 = (bf16[64,3584]{1,0:T(8,128)(2,1)S(1)}, bf16[64,3584]{1,0:T(8,128)(2,1)S(1)}, u32[]{:S(2)}, u32[]{:S(2)}) collective-permute-start(bf16[64,3584]{1,0:T(8,128)(2,1)S(1)} %collective-permute-done.31.refs_1_), channel_id=1, source_target_pairs={{0,1},{1,0},{2,3},{3,2},{4,5},{5,4},{6,7},{7,6},{8,9},{9,8},{10,11... | collective-permute-start | bytes 1376264 | tf_op jit(solution)/shard_map/ppermute | solution.py:37
  91.3 11.2 %collective-permute-start.38 = (bf16[64,3584]{1,0:T(8,128)(2,1)S(1)}, bf16[64,3584]{1,0:T(8,128)(2,1)S(1)}, u32[]{:S(2)}, u32[]{:S(2)}) collective-permute-start(bf16[64,3584]{1,0:T(8,128)(2,1)S(1)} %collective-permute-done.27.refs_0_), channel_id=1, source_target_pairs={{0,1},{1,0},{2,3},{3,2},{4,5},{5,4},{6,7},{7,6},{8,9},{9,8},{10,11... | collective-permute-start | bytes 1376264 | tf_op jit(solution)/shard_map/ppermute | solution.py:37
  101.9 6.7 %collective-permute-start.36 = (bf16[64,3584]{1,0:T(8,128)(2,1)S(1)}, bf16[64,3584]{1,0:T(8,128)(2,1)S(1)}, u32[]{:S(2)}, u32[]{:S(2)}) collective-permute-start(bf16[64,3584]{1,0:T(8,128)(2,1)S(1)} %collective-permute-done.35.refs_1_), channel_id=1, source_target_pairs={{0,1},{1,0},{2,3},{3,2},{4,5},{5,4},{6,7},{7,6},{8,9},{9,8},{10,11... | collective-permute-start | bytes 1376264 | tf_op jit(solution)/shard_map/ppermute | solution.py:37
  101.9 6.7 %collective-permute-start.34 = (bf16[64,3584]{1,0:T(8,128)(2,1)S(1)}, bf16[64,3584]{1,0:T(8,128)(2,1)S(1)}, u32[]{:S(2)}, u32[]{:S(2)}) collective-permute-start(bf16[64,3584]{1,0:T(8,128)(2,1)S(1)} %collective-permute-done.30.refs_0_), channel_id=1, source_target_pairs={{0,1},{1,0},{2,3},{3,2},{4,5},{5,4},{6,7},{7,6},{8,9},{9,8},{10,11... | collective-permute-start | bytes 1376264 | tf_op jit(solution)/shard_map/ppermute | solution.py:37
  (23 other events, 318.4 us)
